TPU v7x, 32 devices: a whole 2x2x4 slice. The times are simulated.
32 devices in a mesh: groups: 2 (over y), expert: 8 (over z, x), dp: 2 (over core).
Axes of the slice: x: 2, y: 2, z: 4, core: 2. Of those that a mesh axis runs over, the one named last changes fastest.
Arguments:
- cotangent: bfloat16 [4096, 3584], P(('groups', 'expert', 'dp')), parts along dimension 0, may hold values from -6 to 6
- hidden: bfloat16 [4096, 8, 128], P(('groups', 'expert', 'dp')), parts along dimension 0, may hold values from -1.5 to 1.5
- probs: bfloat16 [4096, 8], P(('groups', 'expert', 'dp')), parts along dimension 0, may hold values from 0.049804688 to 0.5
- expert_ids: int32 [4096, 8], P(('groups', 'expert', 'dp')), parts along dimension 0, may hold values from 0 to 15, as said below
- send_counts: int32 [32, 8], P(('groups', 'expert', 'dp')), parts along dimension 0, may hold values from 0 to 3
- replica_of: int32 [16], P('groups'), parts along dimension 0, may hold values from 0 to 15, as said below
- weights: bfloat16 [16, 128, 3584], P('expert'), may hold values from -0.09375 to 0.09375
Outputs:
- hidden_gradient: bfloat16 [4096, 8, 128], P(('groups', 'expert', 'dp')), parts along dimension 0
- grad_probs: bfloat16 [4096, 8], P(('groups', 'expert', 'dp')), parts along dimension 0
- grad_weights: bfloat16 [32, 128, 3584], P(('groups', 'expert'), None, 'dp'), parts along dimension 0
There are 2 independent parts, one for each index of `groups`. A program takes and returns all parts, laid end to end along the dimension named above; an argument that names none is the same for every part. Nothing has to cross between parts.
Inputs may be any that keep to these rules, and one draw needn't show every extreme that they name: `expert_ids`: each row names 8 different experts. `replica_of`: entry d is never one of the experts homed on device d, d * 2 to d * 2 + 1.
All inputs are finite; a program needn't handle non-finite values.
Results may differ from a plain program's by a relative error of at most 0.0058.
Values may be sent and summed in bfloat16 or wider, within the bound.
No kernel may reach another device: no remote copies, remote signals or barrier semaphores. Data moves between devices by JAX's collectives and lax.ppermute only.
A program may use at most 128 MiB of HBM per device.

v0:
```python
import jax
import jax.numpy as jnp
from jax import lax
from jax.sharding import PartitionSpec as P

CAPH = 3
CAPR = 3


def ranks_within(keys):
    total_rows = keys.shape[0]
    sort_order = jnp.argsort(keys * total_rows + jnp.arange(total_rows, dtype=jnp.int32))
    sorted_keys = keys[sort_order]
    first_seen = jnp.searchsorted(sorted_keys, sorted_keys, side="left")
    ranked = jnp.arange(total_rows, dtype=jnp.int32) - first_seen
    return jnp.zeros((total_rows,), jnp.int32).at[sort_order].set(ranked)


def route_rows(ids_block, counts_row, replica_of, local_count, cap_home, cap_copy):
    dev_count = replica_of.shape[0]
    experts = ids_block.reshape(-1)
    rank_expert = ranks_within(experts)
    devices = jnp.arange(dev_count, dtype=jnp.int32)
    same_copy = (replica_of[:, None] == replica_of[None, :]) & (devices[None, :] < devices[:, None])
    lower_rank = jnp.sum(jnp.where(same_copy, counts_row[None, :], 0), axis=1)
    upper_rank = lower_rank + counts_row
    hit_table = (
        (replica_of[None, :] == experts[:, None])
        & (lower_rank[None, :] <= rank_expert[:, None])
        & (rank_expert[:, None] < upper_rank[None, :])
    )
    copied = jnp.any(hit_table, axis=1)
    copy_dev = jnp.sum(jnp.where(hit_table, devices[None, :], 0), axis=1)
    dest_dev = jnp.where(copied, copy_dev, experts // local_count)
    index_of_slot = jnp.where(copied, local_count, experts % local_count)
    rank_bucket = ranks_within(dest_dev * (local_count + 1) + index_of_slot)
    keep_row = rank_bucket < jnp.where(copied, cap_copy, cap_home)
    per_dev = local_count * cap_home + cap_copy
    target = dest_dev * per_dev + index_of_slot * cap_home + rank_bucket
    return jnp.where(keep_row, target, dev_count * per_dev)


def body(cotangent, hidden, probs, expert_ids, send_counts, replica_of, weights):
    tok_rows, d_model = cotangent.shape
    top_count = expert_ids.shape[1]
    hidden_width = hidden.shape[2]
    local_count = weights.shape[0]
    dev_count = lax.axis_size("expert")
    data_count = lax.axis_size("dp")
    per_dev = local_count * CAPH + CAPR
    row_count = tok_rows * top_count
    recv_count = dev_count * per_dev
    target = route_rows(expert_ids, send_counts[0], replica_of, local_count, CAPH, CAPR)
    inverse = (
        jnp.full((recv_count,), row_count, jnp.int32)
        .at[target]
        .set(jnp.arange(row_count, dtype=jnp.int32), mode="drop")
    )
    dy_pad = jnp.concatenate([cotangent, jnp.zeros((1, d_model), cotangent.dtype)], axis=0)
    h_pad = jnp.concatenate(
        [hidden.reshape(row_count, hidden_width), jnp.zeros((1, hidden_width), hidden.dtype)],
        axis=0,
    )
    p_pad = jnp.concatenate([probs.reshape(row_count), jnp.zeros((1,), probs.dtype)], axis=0)
    send_dy = dy_pad[inverse // top_count]
    send_h = h_pad[inverse]
    send_p = p_pad[inverse]
    recv_dy, recv_h, recv_p = (
        lax.all_to_all(send_dy, "expert", split_axis=0, concat_axis=0, tiled=True),
        lax.all_to_all(send_h, "expert", split_axis=0, concat_axis=0, tiled=True),
        lax.all_to_all(send_p, "expert", split_axis=0, concat_axis=0, tiled=True),
    )
    flat_size = hidden_width * d_model
    flat_w = weights.reshape(local_count, flat_size)
    pieces = lax.all_to_all(flat_w, "expert", split_axis=1, concat_axis=0, tiled=True)
    chosen = pieces[replica_of]
    copy_weight = lax.all_to_all(chosen, "expert", split_axis=0, concat_axis=0, tiled=True).reshape(
        hidden_width, d_model
    )
    slot_total = local_count + 1
    home_rows = local_count * CAPH
    row_pos = jnp.arange(recv_count, dtype=jnp.int32) % per_dev
    row_slot = jnp.where(row_pos < home_rows, row_pos // CAPH, local_count)
    all_weights = jnp.concatenate(
        [weights.reshape(local_count * hidden_width, d_model), copy_weight], axis=0
    )
    all_in = lax.dot_general(
        recv_dy, all_weights, (((1,), (1,)), ((), ())), preferred_element_type=jnp.float32
    )
    grad_in = jnp.zeros((recv_count, hidden_width), jnp.float32)
    for slot_num in range(slot_total):
        grad_in = grad_in + jnp.where(
            (row_slot == slot_num)[:, None],
            all_in[:, slot_num * hidden_width : (slot_num + 1) * hidden_width],
            0.0,
        )
    p_wide = recv_p.astype(jnp.float32)[:, None]
    h_wide = recv_h.astype(jnp.float32)
    grad_h_buf = (p_wide * grad_in).astype(jnp.bfloat16)
    grad_p_buf = jnp.sum(h_wide * grad_in, axis=1).astype(jnp.bfloat16)
    scaled = (p_wide * h_wide).astype(jnp.bfloat16)
    zero_rows = jnp.zeros_like(scaled)
    scaled_wide = jnp.concatenate(
        [
            jnp.where((row_slot == slot_num)[:, None], scaled, zero_rows)
            for slot_num in range(slot_total)
        ],
        axis=1,
    )
    parts = lax.dot_general(
        scaled_wide, recv_dy, (((0,), (0,)), ((), ())), preferred_element_type=jnp.float32
    ).astype(jnp.bfloat16)
    home_part = parts[: local_count * hidden_width].reshape(local_count, hidden_width, d_model)
    copy_part = parts[local_count * hidden_width :]
    back_h, back_p = (
        lax.all_to_all(grad_h_buf, "expert", split_axis=0, concat_axis=0, tiled=True),
        lax.all_to_all(grad_p_buf, "expert", split_axis=0, concat_axis=0, tiled=True),
    )
    flat_h = jnp.concatenate([back_h, jnp.zeros((1, hidden_width), back_h.dtype)], axis=0)
    flat_p = jnp.concatenate([back_p, jnp.zeros((1,), back_p.dtype)], axis=0)
    hidden_gradient = flat_h[target].reshape(tok_rows, top_count, hidden_width)
    grad_probs = flat_p[target].reshape(tok_rows, top_count)
    expert_total = dev_count * local_count
    cover = replica_of[None, :] == jnp.arange(expert_total, dtype=jnp.int32)[:, None]
    half_width = d_model // data_count
    halves = lax.all_to_all(copy_part, "dp", split_axis=1, concat_axis=0, tiled=True)
    copy_half = jnp.sum(
        halves.reshape(data_count, hidden_width, half_width).astype(jnp.float32), axis=0
    )
    piece_len = hidden_width * half_width // dev_count
    slabs = copy_half.reshape(dev_count, piece_len)
    arrived = lax.all_to_all(slabs, "expert", split_axis=0, concat_axis=0, tiled=True)
    sums = jnp.dot(cover.astype(jnp.float32), arrived, precision=lax.Precision.HIGHEST)
    homed = lax.all_to_all(
        sums.reshape(dev_count, local_count * piece_len),
        "expert",
        split_axis=0,
        concat_axis=0,
        tiled=True,
    )
    homed = (
        homed.reshape(dev_count, local_count, piece_len)
        .transpose(1, 0, 2)
        .reshape(local_count, hidden_width, half_width)
    )
    home_half = lax.psum_scatter(
        home_part.astype(jnp.float32).astype(jnp.bfloat16), "dp", scatter_dimension=2, tiled=True
    ).astype(jnp.float32)
    grad_weights = (home_half + homed).astype(jnp.bfloat16)
    return (hidden_gradient, grad_probs, grad_weights)


def solution(mesh):
    in_specs = (
        P(("groups", "expert", "dp"), None),
        P(("groups", "expert", "dp"), None, None),
        P(("groups", "expert", "dp"), None),
        P(("groups", "expert", "dp"), None),
        P(("groups", "expert", "dp"), None),
        P("groups"),
        P("expert", None, None),
    )
    out_specs = (
        P(("groups", "expert", "dp"), None, None),
        P(("groups", "expert", "dp"), None),
        P(("groups", "expert"), None, "dp"),
    )
    return jax.shard_map(body, mesh=mesh, in_specs=in_specs, out_specs=out_specs, check_vma=False)
```

profile of v0, /device:TPU:0, one launch (start us, length us, event | category | flops | bytes accessed | tf_op | source)
XLA Modules:
  0.0 393.1 jit_solution(14757840275772128985)
XLA Ops:
  10.6 4.4 %sort.31 = (s32[1024]{0:T(1024)}, s32[1024]{0:T(1024)S(1)}) sort(s32[1024]{0:T(1024)S(1)} %iota_add_fusion.1, s32[1024]{0:T(1024)S(1)} %iota.54), dimensions={0}, to_apply=%region_1.2 | sort | flops 10240 | bytes 16384 | tf_op jit(solution)/shard_map/jit(argsort)/sort | solution.py:12
  15.0 4.5 %gather_fusion.2 = s32[1024]{0:T(1024)S(1)} fusion(s32[1024]{0:T(1024)S(1)} %eq.76, s32[1024]{0:T(1024)S(1)} %get-tuple-element.223), kind=kCustom, calls=%fused_computation.2 | custom fusion | bytes 12288 | tf_op jit(solution)/shard_map/gather | solution.py:13
  19.5 50.7 %while.39 = (s32[]{:T(128)}, u32[1024]{0:T(1024)S(1)}, u32[1024]{0:T(1024)S(1)}, s32[1024]{0:T(1024)S(1)}, s32[]{:T(128)}, /*index=5*/s32[]{:T(128)}, s32[]{}) while((s32[]{:T(128)}, u32[1024]{0:T(1024)S(1)}, u32[1024]{0:T(1024)S(1)}, s32[1024]{0:T(1024)S(1)}, s32[]{:T(128)}, /*index=5*/s32[]{:T(128)}, s32[]{}) %tuple.85), condition=%wide.region_3.4_spmd.clone, body=%wide.region_2.3_spmd.clone.sunk | while | flops 19460 | bytes 67685 | solution.py:14
  19.5 4.5 %gather_fusion = s32[1024]{0:T(1024)S(1)} fusion(s32[1024]{0:T(1024)S(1)} %get-tuple-element.306, u32[1024]{0:T(1024)S(1)} %broadcast_clamp_fusion.6), kind=kCustom, calls=%fused_computation.clone.clone.1 | custom fusion | bytes 12288 | tf_op jit(solution)/shard_map/jit(searchsorted)/jit(_searchsorted_scan_impl)/vmap(jit(_searchsorted_scan_impl))/while/body/eval_jaxpr/gather | solution.py:14
  24.1 4.5 %gather_fusion = s32[1024]{0:T(1024)S(1)} fusion(s32[1024]{0:T(1024)S(1)} %get-tuple-element.306, u32[1024]{0:T(1024)S(1)} %broadcast_clamp_fusion.6), kind=kCustom, calls=%fused_computation.clone.clone.1 | custom fusion | bytes 12288 | tf_op jit(solution)/shard_map/jit(searchsorted)/jit(_searchsorted_scan_impl)/vmap(jit(_searchsorted_scan_impl))/while/body/eval_jaxpr/gather | solution.py:14
  28.7 4.5 %gather_fusion = s32[1024]{0:T(1024)S(1)} fusion(s32[1024]{0:T(1024)S(1)} %get-tuple-element.306, u32[1024]{0:T(1024)S(1)} %broadcast_clamp_fusion.6), kind=kCustom, calls=%fused_computation.clone.clone.1 | custom fusion | bytes 12288 | tf_op jit(solution)/shard_map/jit(searchsorted)/jit(_searchsorted_scan_impl)/vmap(jit(_searchsorted_scan_impl))/while/body/eval_jaxpr/gather | solution.py:14
  33.4 4.5 %gather_fusion = s32[1024]{0:T(1024)S(1)} fusion(s32[1024]{0:T(1024)S(1)} %get-tuple-element.306, u32[1024]{0:T(1024)S(1)} %broadcast_clamp_fusion.6), kind=kCustom, calls=%fused_computation.clone.clone.1 | custom fusion | bytes 12288 | tf_op jit(solution)/shard_map/jit(searchsorted)/jit(_searchsorted_scan_impl)/vmap(jit(_searchsorted_scan_impl))/while/body/eval_jaxpr/gather | solution.py:14
  38.0 4.5 %gather_fusion = s32[1024]{0:T(1024)S(1)} fusion(s32[1024]{0:T(1024)S(1)} %get-tuple-element.306, u32[1024]{0:T(1024)S(1)} %broadcast_clamp_fusion.6), kind=kCustom, calls=%fused_computation.clone.clone.1 | custom fusion | bytes 12288 | tf_op jit(solution)/shard_map/jit(searchsorted)/jit(_searchsorted_scan_impl)/vmap(jit(_searchsorted_scan_impl))/while/body/eval_jaxpr/gather | solution.py:14
  42.6 4.5 %gather_fusion = s32[1024]{0:T(1024)S(1)} fusion(s32[1024]{0:T(1024)S(1)} %get-tuple-element.306, u32[1024]{0:T(1024)S(1)} %broadcast_clamp_fusion.6), kind=kCustom, calls=%fused_computation.clone.clone.1 | custom fusion | bytes 12288 | tf_op jit(solution)/shard_map/jit(searchsorted)/jit(_searchsorted_scan_impl)/vmap(jit(_searchsorted_scan_impl))/while/body/eval_jaxpr/gather | solution.py:14
  47.2 4.5 %gather_fusion = s32[1024]{0:T(1024)S(1)} fusion(s32[1024]{0:T(1024)S(1)} %get-tuple-element.306, u32[1024]{0:T(1024)S(1)} %broadcast_clamp_fusion.6), kind=kCustom, calls=%fused_computation.clone.clone.1 | custom fusion | bytes 12288 | tf_op jit(solution)/shard_map/jit(searchsorted)/jit(_searchsorted_scan_impl)/vmap(jit(_searchsorted_scan_impl))/while/body/eval_jaxpr/gather | solution.py:14
  51.8 4.5 %gather_fusion = s32[1024]{0:T(1024)S(1)} fusion(s32[1024]{0:T(1024)S(1)} %get-tuple-element.306, u32[1024]{0:T(1024)S(1)} %broadcast_clamp_fusion.6), kind=kCustom, calls=%fused_computation.clone.clone.1 | custom fusion | bytes 12288 | tf_op jit(solution)/shard_map/jit(searchsorted)/jit(_searchsorted_scan_impl)/vmap(jit(_searchsorted_scan_impl))/while/body/eval_jaxpr/gather | solution.py:14
  56.4 4.5 %gather_fusion = s32[1024]{0:T(1024)S(1)} fusion(s32[1024]{0:T(1024)S(1)} %get-tuple-element.306, u32[1024]{0:T(1024)S(1)} %broadcast_clamp_fusion.6), kind=kCustom, calls=%fused_computation.clone.clone.1 | custom fusion | bytes 12288 | tf_op jit(solution)/shard_map/jit(searchsorted)/jit(_searchsorted_scan_impl)/vmap(jit(_searchsorted_scan_impl))/while/body/eval_jaxpr/gather | solution.py:14
  61.0 4.5 %gather_fusion = s32[1024]{0:T(1024)S(1)} fusion(s32[1024]{0:T(1024)S(1)} %get-tuple-element.306, u32[1024]{0:T(1024)S(1)} %broadcast_clamp_fusion.6), kind=kCustom, calls=%fused_computation.clone.clone.1 | custom fusion | bytes 12288 | tf_op jit(solution)/shard_map/jit(searchsorted)/jit(_searchsorted_scan_impl)/vmap(jit(_searchsorted_scan_impl))/while/body/eval_jaxpr/gather | solution.py:14
  65.6 4.5 %gather_fusion = s32[1024]{0:T(1024)S(1)} fusion(s32[1024]{0:T(1024)S(1)} %get-tuple-element.306, u32[1024]{0:T(1024)S(1)} %broadcast_clamp_fusion.6), kind=kCustom, calls=%fused_computation.clone.clone.1 | custom fusion | bytes 12288 | tf_op jit(solution)/shard_map/jit(searchsorted)/jit(_searchsorted_scan_impl)/vmap(jit(_searchsorted_scan_impl))/while/body/eval_jaxpr/gather | solution.py:14
  70.2 4.3 %scatter_custom_fusion = s32[1024]{0:T(1024)S(1)} fusion(s32[1024]{0:T(1024)S(1)} %get-tuple-element.224, s32[1024]{0:T(1024)S(1)} %convert_subtract_fusion.1, s32[]{:T(128)} %constant.123.clone.1), kind=kCustom, calls=%fused_computation.87 | custom fusion | bytes 4100 | tf_op jit(solution)/shard_map/scatter | solution.py:16
  74.7 4.4 %sort.32 = (s32[1024]{0:T(1024)}, s32[1024]{0:T(1024)S(1)}) sort(s32[1024]{0:T(1024)S(1)} %get-tuple-element.215, s32[1024]{0:T(1024)S(1)} %iota.57), dimensions={0}, to_apply=%region_7.8 | sort | flops 10240 | bytes 16384 | tf_op jit(solution)/shard_map/jit(argsort)/sort | solution.py:12
  79.1 4.5 %gather_fusion.3 = s32[1024]{0:T(1024)S(1)} fusion(s32[1024]{0:T(1024)S(1)} %get-tuple-element.216, s32[1024]{0:T(1024)S(1)} %get-tuple-element.221), kind=kCustom, calls=%fused_computation.3 | custom fusion | bytes 12288 | tf_op jit(solution)/shard_map/gather | solution.py:13
  83.6 50.7 %while.40 = (s32[]{:T(128)}, u32[1024]{0:T(1024)S(1)}, u32[1024]{0:T(1024)S(1)}, s32[1024]{0:T(1024)S(1)}, s32[]{:T(128)}, /*index=5*/s32[]{:T(128)}, s32[]{}) while((s32[]{:T(128)}, u32[1024]{0:T(1024)S(1)}, u32[1024]{0:T(1024)S(1)}, s32[1024]{0:T(1024)S(1)}, s32[]{:T(128)}, /*index=5*/s32[]{:T(128)}, s32[]{}) %tuple.88), condition=%wide.region_9.10_spmd.clone, body=%wide.region_8.9_spmd.clone.sunk | while | flops 19460 | bytes 67685 | solution.py:14
  83.7 4.5 %gather_fusion.1 = s32[1024]{0:T(1024)S(1)} fusion(s32[1024]{0:T(1024)S(1)} %get-tuple-element.327, u32[1024]{0:T(1024)S(1)} %broadcast_clamp_fusion.7), kind=kCustom, calls=%fused_computation.1.clone.clone.1 | custom fusion | bytes 12288 | tf_op jit(solution)/shard_map/jit(searchsorted)/jit(_searchsorted_scan_impl)/vmap(jit(_searchsorted_scan_impl))/while/body/eval_jaxpr/gather | solution.py:14
  88.3 4.5 %gather_fusion.1 = s32[1024]{0:T(1024)S(1)} fusion(s32[1024]{0:T(1024)S(1)} %get-tuple-element.327, u32[1024]{0:T(1024)S(1)} %broadcast_clamp_fusion.7), kind=kCustom, calls=%fused_computation.1.clone.clone.1 | custom fusion | bytes 12288 | tf_op jit(solution)/shard_map/jit(searchsorted)/jit(_searchsorted_scan_impl)/vmap(jit(_searchsorted_scan_impl))/while/body/eval_jaxpr/gather | solution.py:14
  92.9 4.5 %gather_fusion.1 = s32[1024]{0:T(1024)S(1)} fusion(s32[1024]{0:T(1024)S(1)} %get-tuple-element.327, u32[1024]{0:T(1024)S(1)} %broadcast_clamp_fusion.7), kind=kCustom, calls=%fused_computation.1.clone.clone.1 | custom fusion | bytes 12288 | tf_op jit(solution)/shard_map/jit(searchsorted)/jit(_searchsorted_scan_impl)/vmap(jit(_searchsorted_scan_impl))/while/body/eval_jaxpr/gather | solution.py:14
  97.5 4.5 %gather_fusion.1 = s32[1024]{0:T(1024)S(1)} fusion(s32[1024]{0:T(1024)S(1)} %get-tuple-element.327, u32[1024]{0:T(1024)S(1)} %broadcast_clamp_fusion.7), kind=kCustom, calls=%fused_computation.1.clone.clone.1 | custom fusion | bytes 12288 | tf_op jit(solution)/shard_map/jit(searchsorted)/jit(_searchsorted_scan_impl)/vmap(jit(_searchsorted_scan_impl))/while/body/eval_jaxpr/gather | solution.py:14
  102.1 4.5 %gather_fusion.1 = s32[1024]{0:T(1024)S(1)} fusion(s32[1024]{0:T(1024)S(1)} %get-tuple-element.327, u32[1024]{0:T(1024)S(1)} %broadcast_clamp_fusion.7), kind=kCustom, calls=%fused_computation.1.clone.clone.1 | custom fusion | bytes 12288 | tf_op jit(solution)/shard_map/jit(searchsorted)/jit(_searchsorted_scan_impl)/vmap(jit(_searchsorted_scan_impl))/while/body/eval_jaxpr/gather | solution.py:14
  106.7 4.5 %gather_fusion.1 = s32[1024]{0:T(1024)S(1)} fusion(s32[1024]{0:T(1024)S(1)} %get-tuple-element.327, u32[1024]{0:T(1024)S(1)} %broadcast_clamp_fusion.7), kind=kCustom, calls=%fused_computation.1.clone.clone.1 | custom fusion | bytes 12288 | tf_op jit(solution)/shard_map/jit(searchsorted)/jit(_searchsorted_scan_impl)/vmap(jit(_searchsorted_scan_impl))/while/body/eval_jaxpr/gather | solution.py:14
  111.3 4.5 %gather_fusion.1 = s32[1024]{0:T(1024)S(1)} fusion(s32[1024]{0:T(1024)S(1)} %get-tuple-element.327, u32[1024]{0:T(1024)S(1)} %broadcast_clamp_fusion.7), kind=kCustom, calls=%fused_computation.1.clone.clone.1 | custom fusion | bytes 12288 | tf_op jit(solution)/shard_map/jit(searchsorted)/jit(_searchsorted_scan_impl)/vmap(jit(_searchsorted_scan_impl))/while/body/eval_jaxpr/gather | solution.py:14
  116.0 4.5 %gather_fusion.1 = s32[1024]{0:T(1024)S(1)} fusion(s32[1024]{0:T(1024)S(1)} %get-tuple-element.327, u32[1024]{0:T(1024)S(1)} %broadcast_clamp_fusion.7), kind=kCustom, calls=%fused_computation.1.clone.clone.1 | custom fusion | bytes 12288 | tf_op jit(solution)/shard_map/jit(searchsorted)/jit(_searchsorted_scan_impl)/vmap(jit(_searchsorted_scan_impl))/while/body/eval_jaxpr/gather | solution.py:14
  120.6 4.5 %gather_fusion.1 = s32[1024]{0:T(1024)S(1)} fusion(s32[1024]{0:T(1024)S(1)} %get-tuple-element.327, u32[1024]{0:T(1024)S(1)} %broadcast_clamp_fusion.7), kind=kCustom, calls=%fused_computation.1.clone.clone.1 | custom fusion | bytes 12288 | tf_op jit(solution)/shard_map/jit(searchsorted)/jit(_searchsorted_scan_impl)/vmap(jit(_searchsorted_scan_impl))/while/body/eval_jaxpr/gather | solution.py:14
  125.2 4.5 %gather_fusion.1 = s32[1024]{0:T(1024)S(1)} fusion(s32[1024]{0:T(1024)S(1)} %get-tuple-element.327, u32[1024]{0:T(1024)S(1)} %broadcast_clamp_fusion.7), kind=kCustom, calls=%fused_computation.1.clone.clone.1 | custom fusion | bytes 12288 | tf_op jit(solution)/shard_map/jit(searchsorted)/jit(_searchsorted_scan_impl)/vmap(jit(_searchsorted_scan_impl))/while/body/eval_jaxpr/gather | solution.py:14
  129.8 4.5 %gather_fusion.1 = s32[1024]{0:T(1024)S(1)} fusion(s32[1024]{0:T(1024)S(1)} %get-tuple-element.327, u32[1024]{0:T(1024)S(1)} %broadcast_clamp_fusion.7), kind=kCustom, calls=%fused_computation.1.clone.clone.1 | custom fusion | bytes 12288 | tf_op jit(solution)/shard_map/jit(searchsorted)/jit(_searchsorted_scan_impl)/vmap(jit(_searchsorted_scan_impl))/while/body/eval_jaxpr/gather | solution.py:14
  134.4 4.3 %scatter_custom_fusion.1 = s32[1024]{0:T(1024)S(1)} fusion(s32[1024]{0:T(1024)S(1)} %get-tuple-element.222, s32[1024]{0:T(1024)S(1)} %convert_subtract_fusion, s32[]{:T(128)} %constant.123.clone.1), kind=kCustom, calls=%fused_computation.85 | custom fusion | bytes 4100 | tf_op jit(solution)/shard_map/scatter | solution.py:16
  138.8 4.3 %scatter_custom_fusion.2 = s32[72]{0:T(128)S(1)} fusion(s32[1024]{0:T(1024)S(1)} %compare_select_fusion.1, s32[1024]{0:T(1024)S(1)} %iota.59, s32[]{:T(128)} %constant.122.clone.1), kind=kCustom, calls=%fused_computation.103 | custom fusion | bytes 292 | tf_op jit(solution)/shard_map/scatter | solution.py:57
  145.1 7.3 %all-to-all-start = ((bf16[8,9,1]{1,2,0:T(2,128)(2,1)}), bf16[8,9,1]{1,2,0:T(2,128)(2,1)S(1)}, u32[]{:S(2)}, u32[]{:S(2)}) async-start(bf16[8,9,1]{1,2,0:T(2,128)(2,1)} %all_to_all.103), calls=%async_computation | async-start | bytes 8192 | tf_op jit(solution)/shard_map/all_to_all | solution.py:71
  153.6 5.1 %all-to-all-done = bf16[8,9,1]{1,2,0:T(2,128)(2,1)S(1)} async-done(((bf16[8,9,1]{1,2,0:T(2,128)(2,1)}), bf16[8,9,1]{1,2,0:T(2,128)(2,1)S(1)}, u32[]{:S(2)}, u32[]{:S(2)}) %all-to-all-start) | async-done | bytes 176 | tf_op jit(solution)/shard_map/all_to_all | solution.py:71
  158.7 3.3 all-to-all-start.5
  164.2 4.5 %all-to-all-done.5 = bf16[8,9,128]{2,1,0:T(8,128)(2,1)S(1)} async-done(((bf16[8,9,128]{2,1,0:T(8,128)(2,1)}), bf16[8,9,128]{2,1,0:T(8,128)(2,1)S(1)}, u32[]{:S(2)}, u32[]{:S(2)}) %all-to-all-start.5) | async-done | bytes 18464 | tf_op jit(solution)/shard_map/all_to_all | solution.py:70
  168.7 3.6 all-to-all-start.1
  172.3 2.0 all_to_all.83
  174.3 3.1 copy.38
  177.4 15.6 %all-to-all-done.1 = bf16[8,9,3584]{2,1,0:T(8,128)(2,1)S(1)} async-done(((bf16[8,9,3584]{2,1,0:T(8,128)(2,1)}), bf16[8,9,3584]{2,1,0:T(8,128)(2,1)S(1)}, u32[]{:S(2)}, u32[]{:S(2)}) %all-to-all-start.1) | async-done | bytes 516128 | tf_op jit(solution)/shard_map/all_to_all | solution.py:69
  193.0 3.6 all-to-all-start.2
  200.8 37.3 %all-to-all-done.2 = bf16[2,8,57344]{2,0,1:T(2,128)(2,1)S(1)} async-done(((bf16[2,8,57344]{2,0,1:T(2,128)(2,1)}), bf16[2,8,57344]{2,0,1:T(2,128)(2,1)S(1)}, u32[]{:S(2)}, u32[]{:S(2)}) %all-to-all-start.2) | async-done | bytes 1835040 | tf_op jit(solution)/shard_map/all_to_all | solution.py:75
  238.1 4.5 %all-to-all-start.7 = ((bf16[128,2,1792]{2,0,1:T(8,128)(2,1)}), bf16[128,2,1792]{2,0,1:T(8,128)(2,1)}, u32[]{:S(2)}, u32[]{:S(2)}) async-start(bf16[128,2,1792]{2,0,1:T(8,128)(2,1)} %bitcast.22), calls=%async_computation.8 | async-start | bytes 1835008 | tf_op jit(solution)/shard_map/all_to_all | solution.py:126
  249.3 4.2 %all-to-all-start.3 = ((bf16[8,2,28672]{2,1,0:T(2,128)(2,1)}), bf16[8,2,28672]{2,1,0:T(2,128)(2,1)}, u32[]{:S(2)}, u32[]{:S(2)}) async-start(bf16[8,2,28672]{2,1,0:T(2,128)(2,1)} %reshape.268), calls=%async_computation.3 | async-start | bytes 1835008 | tf_op jit(solution)/shard_map/all_to_all | solution.py:77
  253.5 2.3 convert_reduce_fusion
  255.8 3.2 all_to_all.98
  259.0 18.2 %all-to-all-done.3 = bf16[8,2,28672]{2,1,0:T(2,128)(2,1)} async-done(((bf16[8,2,28672]{2,1,0:T(2,128)(2,1)}), bf16[8,2,28672]{2,1,0:T(2,128)(2,1)}, u32[]{:S(2)}, u32[]{:S(2)}) %all-to-all-start.3) | async-done | bytes 917536 | tf_op jit(solution)/shard_map/all_to_all | solution.py:77
  277.2 4.2 %all-to-all-start.8 = ((f32[8,1,28672]{2,1,0:T(1,128)}), f32[8,1,28672]{2,1,0:T(1,128)}, u32[]{:S(2)}, u32[]{:S(2)}) async-start(f32[8,1,28672]{2,1,0:T(1,128)} %all_to_all.98), calls=%async_computation.9 | async-start | bytes 1835008 | tf_op jit(solution)/shard_map/all_to_all | solution.py:132
  282.9 4.2 %reshape.269 = bf16[8,1,57344]{2,1,0:T(2,128)(2,1)S(1)} reshape(bf16[8,2,28672]{2,1,0:T(2,128)(2,1)} %all-to-all-done.3) | data formatting | bytes 1835008
  287.1 5.6 %reduce.2 = bf16[8,57344]{1,0:T(8,128)(2,1)S(1)} reduce(bf16[8,1,57344]{2,1,0:T(2,128)(2,1)S(1)} %reshape.269, bf16[]{:T(256)} %constant.150), dimensions={1}, to_apply=%all_to_all.88.reduce_sub_computation | reduce | bytes 1835010 | tf_op jit(solution)/shard_map/all_to_all | solution.py:77
  294.6 2.2 fusion
  297.7 6.8 %all-to-all-done.8 = f32[8,1,28672]{2,1,0:T(1,128)} async-done(((f32[8,1,28672]{2,1,0:T(1,128)}), f32[8,1,28672]{2,1,0:T(1,128)}, u32[]{:S(2)}, u32[]{:S(2)}) %all-to-all-start.8) | async-done | bytes 917536 | tf_op jit(solution)/shard_map/all_to_all | solution.py:132
  304.4 3.5 all-to-all-start.6
  308.6 5.7 %all-to-all-done.6 = bf16[8,9,1]{1,2,0:T(2,128)(2,1)S(1)} async-done(((bf16[8,9,1]{1,2,0:T(2,128)(2,1)}), bf16[8,9,1]{1,2,0:T(2,128)(2,1)S(1)}, u32[]{:S(2)}, u32[]{:S(2)}) %all-to-all-start.6) | async-done | bytes 176 | tf_op jit(solution)/shard_map/all_to_all | solution.py:117
  314.3 3.6 all-to-all-start.4
  317.9 2.4 fusion.4
  320.3 3.2 all_to_all.104
  324.3 4.9 %all-to-all-start.9 = ((f32[8,1,57344]{2,1,0:T(1,128)}), f32[8,1,57344]{2,1,0:T(1,128)S(1)}, u32[]{:S(2)}, u32[]{:S(2)}) async-start(f32[8,1,57344]{2,1,0:T(1,128)} %all_to_all.104), calls=%async_computation.10 | async-start | bytes 3670016 | tf_op jit(solution)/shard_map/all_to_all | solution.py:134
  329.4 6.5 %gather_fusion.9 = bf16[1024]{0:T(1024)(128)(2,1)S(1)} fusion(bf16[73]{0:T(256)(128)(2,1)S(1)} %pad_maximum_fusion.1, s32[1024]{0:T(1024)S(1)} %get-tuple-element.213), kind=kCustom, calls=%fused_computation.9 | custom fusion | bytes 8192 | tf_op jit(solution)/shard_map/gather | solution.py:122
  336.7 4.3 %gather_fusion.7 = bf16[1024,128]{1,0:T(8,128)(2,1)} fusion(bf16[73,128]{1,0:T(8,128)(2,1)S(1)} %concatenate.24, s32[1024]{0:T(1024)S(1)} %get-tuple-element.213), kind=kCustom, calls=%fused_computation.7 | custom fusion | bytes 528384 | tf_op jit(solution)/shard_map/gather | solution.py:121
  341.0 29.5 %all-to-all-done.9 = f32[8,1,57344]{2,1,0:T(1,128)S(1)} async-done(((f32[8,1,57344]{2,1,0:T(1,128)}), f32[8,1,57344]{2,1,0:T(1,128)S(1)}, u32[]{:S(2)}, u32[]{:S(2)}) %all-to-all-start.9) | async-done | bytes 1835040 | tf_op jit(solution)/shard_map/all_to_all | solution.py:134
  370.5 6.3 %reduce.4 = f32[8,57344]{1,0:T(8,128)} reduce(f32[8,1,57344]{2,1,0:T(1,128)S(1)} %all-to-all-done.9, f32[]{:T(128)} %constant.152), dimensions={1}, to_apply=%all_to_all.102.reduce_sub_computation | reduce | bytes 3670020 | tf_op jit(solution)/shard_map/all_to_all | solution.py:134
  376.9 3.1 reshape.125
  379.9 2.3 copy.43
  384.0 2.3 add_convert_fusion
  (173 shorter events, 28.8 us)
Async XLA Ops:
  19.5 55.1 %copy-start.6 = (s32[8]{0:T(128)S(1)}, s32[8]{0:T(128)}, u32[]{:S(2)}) copy-start(s32[8]{0:T(128)} %param.16) | copy-start | bytes 100
  83.6 68.7 %copy-start.5 = (bf16[128,8,128]{2,1,0:T(8,128)(2,1)S(1)}, bf16[128,8,128]{2,1,0:T(8,128)(2,1)}, u32[]{:S(2)}) copy-start(bf16[128,8,128]{2,1,0:T(8,128)(2,1)} %param.12) | copy-start | bytes 786436
  134.4 27.7 %copy-start.4 = (bf16[128,3584]{1,0:T(8,128)(2,1)S(1)}, bf16[128,3584]{1,0:T(8,128)(2,1)}, u32[]{:S(2)}) copy-start(bf16[128,3584]{1,0:T(8,128)(2,1)} %param.11) | copy-start | bytes 2752516
  145.1 13.6 %all-to-all-start = ((bf16[8,9,1]{1,2,0:T(2,128)(2,1)}), bf16[8,9,1]{1,2,0:T(2,128)(2,1)S(1)}, u32[]{:S(2)}, u32[]{:S(2)}) async-start(bf16[8,9,1]{1,2,0:T(2,128)(2,1)} %all_to_all.103), calls=%async_computation | async-start | bytes 8192 | tf_op jit(solution)/shard_map/all_to_all | solution.py:71
  158.7 10.0 %all-to-all-start.5 = ((bf16[8,9,128]{2,1,0:T(8,128)(2,1)}), bf16[8,9,128]{2,1,0:T(8,128)(2,1)S(1)}, u32[]{:S(2)}, u32[]{:S(2)}) async-start(bf16[8,9,128]{2,1,0:T(8,128)(2,1)} %all_to_all.92), calls=%async_computation.5 | async-start | bytes 65536 | tf_op jit(solution)/shard_map/all_to_all | solution.py:70
  168.7 24.3 %all-to-all-start.1 = ((bf16[8,9,3584]{2,1,0:T(8,128)(2,1)}), bf16[8,9,3584]{2,1,0:T(8,128)(2,1)S(1)}, u32[]{:S(2)}, u32[]{:S(2)}) async-start(bf16[8,9,3584]{2,1,0:T(8,128)(2,1)} %all_to_all.80), calls=%async_computation.1 | async-start | bytes 1835008 | tf_op jit(solution)/shard_map/all_to_all | solution.py:69
  193.0 45.1 %all-to-all-start.2 = ((bf16[2,8,57344]{2,0,1:T(2,128)(2,1)}), bf16[2,8,57344]{2,0,1:T(2,128)(2,1)S(1)}, u32[]{:S(2)}, u32[]{:S(2)}) async-start(bf16[2,8,57344]{2,0,1:T(2,128)(2,1)} %copy.38), calls=%async_computation.2 | async-start | bytes 3670016 | tf_op jit(solution)/shard_map/all_to_all | solution.py:75
  198.2 1.6 copy-start
  238.1 4.5 %copy-start.2 = (bf16[2,8,57344]{2,0,1:T(2,128)(2,1)}, bf16[2,8,57344]{2,0,1:T(2,128)(2,1)S(1)}, u32[]{:S(2)}) copy-start(bf16[2,8,57344]{2,0,1:T(2,128)(2,1)S(1)} %all-to-all-done.2) | copy-start | bytes 5505028
  238.1 11.2 %all-to-all-start.7 = ((bf16[128,2,1792]{2,0,1:T(8,128)(2,1)}), bf16[128,2,1792]{2,0,1:T(8,128)(2,1)}, u32[]{:S(2)}, u32[]{:S(2)}) async-start(bf16[128,2,1792]{2,0,1:T(8,128)(2,1)} %bitcast.22), calls=%async_computation.8 | async-start | bytes 1835008 | tf_op jit(solution)/shard_map/all_to_all | solution.py:126
  249.3 27.9 %all-to-all-start.3 = ((bf16[8,2,28672]{2,1,0:T(2,128)(2,1)}), bf16[8,2,28672]{2,1,0:T(2,128)(2,1)}, u32[]{:S(2)}, u32[]{:S(2)}) async-start(bf16[8,2,28672]{2,1,0:T(2,128)(2,1)} %reshape.268), calls=%async_computation.3 | async-start | bytes 1835008 | tf_op jit(solution)/shard_map/all_to_all | solution.py:77
  255.8 25.7 %copy-start.1 = (bf16[384,3584]{1,0:T(8,128)(2,1)S(1)}, bf16[384,3584]{1,0:T(8,128)(2,1)}, u32[]{:S(2)}) copy-start(bf16[384,3584]{1,0:T(8,128)(2,1)} %copy-done) | copy-start | bytes 8257540
  277.2 27.2 %all-to-all-start.8 = ((f32[8,1,28672]{2,1,0:T(1,128)}), f32[8,1,28672]{2,1,0:T(1,128)}, u32[]{:S(2)}, u32[]{:S(2)}) async-start(f32[8,1,28672]{2,1,0:T(1,128)} %all_to_all.98), calls=%async_computation.9 | async-start | bytes 1835008 | tf_op jit(solution)/shard_map/all_to_all | solution.py:132
  281.5 102.6 %reduce-scatter.2.cloned.1.call-start = ((), (), s32[]{:S(2)}) async-start(), calls=%async_computation.11 | async-start | bytes 2752512 | tf_op jit(solution)/shard_map/reduce_scatter | solution.py:146
  292.7 1.9 copy-start.3
  304.4 9.9 %all-to-all-start.6 = ((bf16[8,9,1]{1,2,0:T(2,128)(2,1)}), bf16[8,9,1]{1,2,0:T(2,128)(2,1)S(1)}, u32[]{:S(2)}, u32[]{:S(2)}) async-start(bf16[8,9,1]{1,2,0:T(2,128)(2,1)} %convert_element_type.82), calls=%async_computation.6 | async-start | bytes 8192 | tf_op jit(solution)/shard_map/all_to_all | solution.py:117
  314.3 10.0 %all-to-all-start.4 = ((bf16[8,9,128]{2,1,0:T(8,128)(2,1)}), bf16[8,9,128]{2,1,0:T(8,128)(2,1)S(1)}, u32[]{:S(2)}, u32[]{:S(2)}) async-start(bf16[8,9,128]{2,1,0:T(8,128)(2,1)} %all_to_all.89), calls=%async_computation.4 | async-start | bytes 65536 | tf_op jit(solution)/shard_map/all_to_all | solution.py:116
  324.3 46.2 %all-to-all-start.9 = ((f32[8,1,57344]{2,1,0:T(1,128)}), f32[8,1,57344]{2,1,0:T(1,128)S(1)}, u32[]{:S(2)}, u32[]{:S(2)}) async-start(f32[8,1,57344]{2,1,0:T(1,128)} %all_to_all.104), calls=%async_computation.10 | async-start | bytes 3670016 | tf_op jit(solution)/shard_map/all_to_all | solution.py:134
Sparse Core Ops, SparseCore 0:
  284.5 10.6 reduce-scatter.1
where the time goes:
time: 394 us; the launch traced here: 393 us
  local copies, waits for them, and re-layouts  176 us (45%)
  waiting for transfers between devices  123 us (31%)
  starting transfers between devices  42.8 us (11%)
  other arithmetic  29.6 us (8%)
  between operations  14.5 us (4%)
  matrix products  5.53 us (1%)
    gather x22, local copies, waits for them, and re-layouts, ranks_within(): first_seen = jnp.searchsorted(sorted_keys, sorted_keys, side='left')  99.6 us
    all_to_all x1, waiting for transfers between devices, body(): lax.all_to_all(flat_w, 'expert', split_axis=1, concat_axis=0, tiled=True)  37.3 us
    all_to_all x1, waiting for transfers between devices, body(): lax.all_to_all(sums.reshape(dev_count, local_count * piece_len), 'expert'...  29.5 us
    all_to_all x1, waiting for transfers between devices, body(): lax.all_to_all(chosen, 'expert', split_axis=0, concat_axis=0, tiled=True)  18.2 us
    all_to_all x1, waiting for transfers between devices, body(): lax.all_to_all(send_dy, 'expert', split_axis=0, concat_axis=0, tiled=True)  15.6 us
    unnamed x19, local copies, waits for them, and re-layouts  10.2 us
    gather x2, local copies, waits for them, and re-layouts, ranks_within(): sorted_keys = keys[sort_order]  9.04 us
    sort x2, other arithmetic, ranks_within(): jnp.argsort(keys * total_rows + jnp.arange(total_rows, dtype=jnp.int32))  8.73 us
  transfers between devices with their start and end apart: 11, of which 9 were waited for; matrix products, arithmetic and copies ran while one was open for 15% of the time, Pallas kernels for 0%

commit v1 on v0

--- a/solution.py
+++ b/solution.py
@@ -1,6 +1,10 @@
+import functools
+
 import jax
 import jax.numpy as jnp
 from jax import lax
+from jax.experimental import pallas as pl
+from jax.experimental.pallas import tpu as pltpu
 from jax.sharding import PartitionSpec as P
 
 CAPH = 3
@@ -40,7 +44,7 @@
     return jnp.where(keep_row, target, dev_count * per_dev)
 
 
-def body(cotangent, hidden, probs, expert_ids, send_counts, replica_of, weights):
+def replica_body(cotangent, hidden, probs, expert_ids, send_counts, replica_of, weights):
     tok_rows, d_model = cotangent.shape
     top_count = expert_ids.shape[1]
     hidden_width = hidden.shape[2]
@@ -150,6 +154,234 @@
     return (hidden_gradient, grad_probs, grad_weights)
 
 
+SLOT = 4
+F32 = jnp.float32
+BF16 = jnp.bfloat16
+NT = (((1,), (1,)), ((), ()))
+TN = (((0,), (0,)), ((), ()))
+
+
+def iota(shape, dim):
+    return lax.broadcasted_iota(jnp.int32, shape, dim)
+
+
+def dispatch_kernel(local_count, dev_count, replica_ref, counts_ref, ids_ref, probs_ref, cot_ref, hid_ref,
+                    home_ref, copy_ref, pick_ref, expert_ref, hs_ref, ps_ref, wide):
+    top, toks = ids_ref.shape
+    d_model = cot_ref.shape[1]
+    homes = dev_count * local_count * SLOT
+    slots = homes + dev_count * CAPR
+    row = iota((slots, toks), 0)
+    expert = row // SLOT
+    within = row % SLOT
+    allowed = jnp.where(within < CAPH, 1, 0)
+    for d in range(dev_count):
+        first = homes + d * CAPR
+        mine = (row >= first) & (row < first + CAPR)
+        expert = jnp.where(mine, replica_ref[d], expert)
+        within = jnp.where(mine, row - first, within)
+        allowed = jnp.where(mine, jnp.where(row - first < counts_ref[0, d], 1, 0), allowed)
+    lower = jnp.zeros((slots, toks), jnp.int32)
+    for d in range(dev_count):
+        earlier = (row < homes) | (row >= homes + (d + 1) * CAPR)
+        lower = lower + jnp.where(earlier & (expert == replica_ref[d]), counts_ref[0, d], 0)
+    ids = ids_ref[...]
+    named = jnp.zeros((slots, toks), F32)
+    for k in range(top):
+        named = named + jnp.where(ids[k:k + 1, :] == expert, 1.0, 0.0)
+    before = jnp.where(iota((toks, toks), 0) < iota((toks, toks), 1), 1.0, 0.0).astype(BF16)
+    rank = jnp.dot(named.astype(BF16), before, preferred_element_type=F32)
+    wanted = (lower + within).astype(F32)
+    pick = jnp.where((rank == wanted) & (allowed > 0), named, 0.0)
+    pick_ref[...] = pick
+    expert_ref[...] = expert
+    wide[...] = hid_ref[...].astype(F32)
+    h_slot = jnp.zeros((slots, hid_ref.shape[1]), F32)
+    p_slot = jnp.zeros((slots, toks), F32)
+    probs = probs_ref[...].astype(F32)
+    for k in range(top):
+        sel = jnp.where(ids[k:k + 1, :] == expert, pick, 0.0)
+        h_k = wide[pl.ds(k, toks, stride=top), :].astype(BF16)
+        h_slot = h_slot + jnp.dot(sel.astype(BF16), h_k, preferred_element_type=F32)
+        p_slot = p_slot + sel * probs[k:k + 1, :]
+    p_slot = jnp.sum(p_slot, axis=1, keepdims=True)
+    hs_ref[...] = h_slot
+    ps_ref[...] = jnp.broadcast_to(p_slot, ps_ref.shape)
+    scaled = p_slot * h_slot
+    rows = jnp.dot(pick.astype(BF16), cot_ref[...], preferred_element_type=F32)
+    home_ref[:, :d_model] = rows[:homes].astype(BF16)
+    home_ref[:, d_model:] = scaled[:homes].astype(BF16)
+    copy_ref[:, :d_model] = rows[homes:].astype(BF16)
+    copy_ref[:, d_model:] = scaled[homes:].astype(BF16)
+
+
+def local_slots(local_count, dev_count, width, replica_ref):
+    first = lax.axis_index("expert") * local_count
+    home = (iota((dev_count * local_count * SLOT, width), 0) // SLOT) % local_count
+    row = iota((dev_count * CAPR, width), 0)
+    copy = jnp.full((dev_count * CAPR, width), -1, jnp.int32)
+    for d in range(dev_count):
+        mine = (row >= d * CAPR) & (row < (d + 1) * CAPR)
+        copy = jnp.where(mine, replica_ref[d] - first, copy)
+    copy = jnp.broadcast_to(copy[None], (dev_count, dev_count * CAPR, width))
+    return home, copy.reshape(dev_count * dev_count * CAPR, width)
+
+
+def grad_in_kernel(local_count, dev_count, replica_ref, home_ref, copy_ref, w_ref, out_ref):
+    d_model = w_ref.shape[1]
+    width = w_ref.shape[0] // local_count
+    per_home, per_copy = local_count * SLOT, dev_count * CAPR
+    results = []
+    for ref, slot in zip((home_ref, copy_ref), local_slots(local_count, dev_count, width, replica_ref)):
+        every = lax.dot_general(ref[:, :d_model], w_ref[...], NT, preferred_element_type=F32)
+        own = jnp.zeros((ref.shape[0], width), F32)
+        for e in range(local_count):
+            own = jnp.where(slot == e, every[:, e * width:(e + 1) * width], own)
+        results.append(own)
+    home, copy = results
+    both = jnp.concatenate(
+        [home.reshape(dev_count, per_home, width), copy.reshape(dev_count, per_copy, width)], axis=1)
+    out_ref[...] = both.reshape(dev_count * (per_home + per_copy), width).astype(out_ref.dtype)
+
+
+def grad_weights_half(local_count, dev_count, half, replica_ref, home_ref, copy_ref, columns):
+    width = home_ref.shape[1] - 2 * columns
+    start = pl.multiple_of(half * columns, 128)
+    total = None
+    for ref, slot in zip((home_ref, copy_ref), local_slots(local_count, dev_count, width, replica_ref)):
+        scaled = ref[:, 2 * columns:].astype(F32)
+        spread = jnp.concatenate([jnp.where(slot == e, scaled, 0.0) for e in range(local_count)], axis=1)
+        part = lax.dot_general(spread.astype(BF16), ref[:, pl.ds(start, columns)], TN, preferred_element_type=F32)
+        total = part if total is None else total + part
+    return total
+
+
+def other_half_kernel(local_count, dev_count, replica_ref, home_ref, copy_ref, out_ref):
+    half = 1 - lax.axis_index("dp")
+    out_ref[...] = grad_weights_half(
+        local_count, dev_count, half, replica_ref, home_ref, copy_ref, out_ref.shape[1]).astype(out_ref.dtype)
+
+
+def own_half_kernel(local_count, dev_count, replica_ref, home_ref, copy_ref, arrived_ref, out_ref):
+    half = lax.axis_index("dp")
+    total = grad_weights_half(
+        local_count, dev_count, half, replica_ref, home_ref, copy_ref, out_ref.shape[1])
+    out_ref[...] = (total + arrived_ref[...].astype(F32)).astype(out_ref.dtype)
+
+
+def combine_kernel(local_count, dev_count, back_ref, pick_ref, expert_ref, hs_ref, ps_ref, ids_ref,
+                   grad_h_ref, grad_p_ref, wide):
+    top, toks = ids_ref.shape
+    width = back_ref.shape[1]
+    per_home, per_copy = local_count * SLOT, dev_count * CAPR
+    back = back_ref[...].astype(F32).reshape(dev_count, per_home + per_copy, width)
+    home = back[:, :per_home].reshape(dev_count * per_home, width)
+    copy = jnp.sum(back[:, per_home:], axis=0)
+    grad_in = jnp.concatenate([home, copy], axis=0)
+    h_rows = (ps_ref[...] * grad_in).astype(BF16)
+    p_rows = jnp.sum(hs_ref[...] * grad_in, axis=1, keepdims=True)
+    ids = ids_ref[...]
+    pick = pick_ref[...]
+    expert = expert_ref[...]
+    for k in range(top):
+        sel = jnp.where(ids[k:k + 1, :] == expert, pick, 0.0)
+        wide[pl.ds(k, toks, stride=top), :] = lax.dot_general(
+            sel.astype(BF16), h_rows, TN, preferred_element_type=F32)
+        grad_p_ref[k:k + 1, :] = jnp.sum(sel * p_rows, axis=0, keepdims=True)
+    grad_h_ref[...] = wide[...].astype(grad_h_ref.dtype)
+
+
+def call(kernel, out_shape, smem, operands, scratch=(), flops=0):
+    vmem = pl.BlockSpec(memory_space=pltpu.VMEM)
+    shapes = jax.tree.leaves(out_shape)
+    moved = sum(a.size * a.dtype.itemsize for a in (*operands, *shapes))
+    return pl.pallas_call(
+        kernel,
+        out_shape=out_shape,
+        in_specs=[pl.BlockSpec(memory_space=pltpu.SMEM)] * len(smem) + [vmem] * len(operands),
+        out_specs=jax.tree.map(lambda _: vmem, out_shape),
+        scratch_shapes=list(scratch),
+        compiler_params=pltpu.CompilerParams(vmem_limit_bytes=24 << 20),
+        cost_estimate=pl.CostEstimate(flops=flops, bytes_accessed=moved, transcendentals=0),
+    )(*smem, *operands)
+
+
+def gather_body(cotangent, hidden, probs, expert_ids, send_counts, replica_of, weights):
+    toks, d_model = cotangent.shape
+    top = expert_ids.shape[1]
+    width = hidden.shape[2]
+    local_count = weights.shape[0]
+    dev_count = lax.axis_size("expert")
+    homes = dev_count * local_count * SLOT
+    copies = dev_count * CAPR
+    slots = homes + copies
+    sizes = (local_count, dev_count)
+    ids = expert_ids.T
+    shape = jax.ShapeDtypeStruct
+    home_rows, copy_rows, pick, expert, h_slot, p_slot = call(
+        functools.partial(dispatch_kernel, *sizes),
+        (shape((homes, d_model + width), BF16), shape((copies, d_model + width), BF16), shape((slots, toks), F32),
+         shape((slots, toks), jnp.int32), shape((slots, width), F32), shape((slots, width), F32)),
+        (replica_of, send_counts),
+        (ids, probs.T, cotangent, hidden.reshape(toks * top, width)),
+        [pltpu.VMEM((toks * top, width), F32)],
+        flops=2 * slots * toks * d_model,
+    )
+    home_in = lax.all_to_all(home_rows, "expert", split_axis=0, concat_axis=0, tiled=True)
+    copy_in = lax.all_gather(copy_rows, "expert", axis=0, tiled=True)
+    rows = homes + dev_count * copies
+    w_flat = weights.reshape(local_count * width, d_model)
+    back = call(
+        functools.partial(grad_in_kernel, *sizes),
+        shape((rows, width), BF16),
+        (replica_of,),
+        (home_in, copy_in, w_flat),
+        flops=2 * rows * d_model * local_count * width,
+    )
+    back = lax.all_to_all(back, "expert", split_axis=0, concat_axis=0, tiled=True)
+    columns = d_model // 2
+    half_flops = 2 * rows * columns * local_count * width
+    other = call(
+        functools.partial(other_half_kernel, *sizes),
+        shape((local_count * width, columns), BF16),
+        (replica_of,),
+        (home_in, copy_in),
+        flops=half_flops,
+    )
+    arrived = lax.ppermute(other, "dp", [(0, 1), (1, 0)])
+    grad_h, grad_p = call(
+        functools.partial(combine_kernel, *sizes),
+        (shape((toks * top, width), BF16), shape((top, toks), F32)),
+        (),
+        (back, pick, expert, h_slot, p_slot, ids),
+        [pltpu.VMEM((toks * top, width), F32)],
+        flops=2 * slots * toks * width * top,
+    )
+    grad_w = call(
+        functools.partial(own_half_kernel, *sizes),
+        shape((local_count * width, columns), BF16),
+        (replica_of,),
+        (home_in, copy_in, arrived),
+        flops=half_flops,
+    )
+    return (
+        grad_h.reshape(toks, top, width),
+        grad_p.T.astype(BF16),
+        grad_w.reshape(local_count, width, columns),
+    )
+
+
+def body(cotangent, hidden, probs, expert_ids, send_counts, replica_of, weights):
+    dev_count = lax.axis_size("expert")
+    local_count, width, _ = weights.shape
+    gathered = dev_count * dev_count * CAPR
+    if gathered <= (local_count + 3) * width and lax.axis_size("dp") == 2:
+        run = gather_body
+    else:
+        run = replica_body
+    return run(cotangent, hidden, probs, expert_ids, send_counts, replica_of, weights)
+
+
 def solution(mesh):
     in_specs = (
         P(("groups", "expert", "dp"), None),

time: 394 us -> 88.1 us (0.22)
  local copies, waits for them, and re-layouts: 176 us -> 6.37 us
  waiting for transfers between devices: 123 us -> 22.8 us
  starting transfers between devices: 42.8 us -> 0.11 us
  blocking collectives: 0 us -> 35.8 us
  other arithmetic: 29.6 us -> 0.58 us
  Pallas kernels: 0 us -> 7.9 us
  matrix products: 5.53 us -> 0 us
    all_to_all x10 -> x0, waiting for transfers between devices: 123 us -> none  [the longest x1 37.3 us: body(): lax.all_to_all(flat_w, 'expert', split_axis=1, concat_axis=0, tiled=True)]
    gather x30 -> x0, local copies, waits for them, and re-layouts: 123 us -> none  [the longest x22 99.6 us: ranks_within(): first_seen = jnp.searchsorted(sorted_keys, sorted_keys, side='left')]
    all_to_all x10 -> x0, starting transfers between devices: 42.7 us -> none  [the longest x1 7.25 us: body(): lax.all_to_all(send_p, 'expert', split_axis=0, concat_axis=0, tiled=True)]
    all_to_all x0 -> x2, blocking collectives: none -> 35.8 us  [the longest x1 26.1 us: gather_body(): lax.all_to_all(home_rows, 'expert', split_axis=0, concat_axis=0, tiled=True)]
    all_gather x0 -> x1, waiting for transfers between devices: none -> 22.8 us  [gather_body(): copy_in = lax.all_gather(copy_rows, 'expert', axis=0, tiled=True)]
    all_to_all x14 -> x0, local copies, waits for them, and re-layouts: 18.4 us -> none  [the longest x3 7.06 us: body(): lax.all_to_all(flat_w, 'expert', split_axis=1, concat_axis=0, tiled=True)]
    all_to_all x4 -> x0, other arithmetic: 13.3 us -> none  [the longest x2 6.92 us: body(): lax.all_to_all(chosen, 'expert', split_axis=0, concat_axis=0, tiled=True)]
    scatter x3 -> x0, local copies, waits for them, and re-layouts: 12.9 us -> none  [the longest x2 8.62 us: ranks_within(): return jnp.zeros((total_rows,), jnp.int32).at[sort_order].set(ranked)]
  transfers between devices with their start and end apart: 11 -> 2, of which waited for: 9 -> 1; matrix products, arithmetic and copies ran while one was open for 15% -> 1% of each run, Pallas kernels for 0% -> 3%
where the time goes in v1:
time: 88.1 us; the launch traced here: 87.7 us
  blocking collectives  35.8 us (41%)
  waiting for transfers between devices  22.8 us (26%)
  between operations  14.1 us (16%)
  Pallas kernels  7.9 us (9%)
  local copies, waits for them, and re-layouts  6.37 us (7%)
    all_to_all x1, blocking collectives, gather_body(): lax.all_to_all(home_rows, 'expert', split_axis=0, concat_axis=0, tiled=True)  26.1 us
    all_gather x1, waiting for transfers between devices, gather_body(): copy_in = lax.all_gather(copy_rows, 'expert', axis=0, tiled=True)  22.8 us
    all_to_all x1, blocking collectives, gather_body(): lax.all_to_all(back, 'expert', split_axis=0, concat_axis=0, tiled=True)  9.71 us
    pallas_call x5, Pallas kernels, call(): pl.pallas_call(kernel, out_shape=out_shape, in_specs=[pl.BlockSpec(memory...  7.9 us
    unnamed x20, local copies, waits for them, and re-layouts  6.37 us
  transfers between devices with their start and end apart: 2, of which 1 were waited for; matrix products, arithmetic and copies ran while one was open for 1% of the time, Pallas kernels for 3%

profile of v1, /device:TPU:0, one launch (start us, length us, event | category | flops | bytes accessed | tf_op | source)
XLA Modules:
  0.0 87.7 jit_solution(14822154048540836256)
XLA Ops:
  7.2 0.0 copy-start.7
  7.2 0.0 all-gather.2.cloned.1.call-start
  7.2 0.0 copy-start.2
  7.2 1.2 %copy-done.2 = bf16[128,3584]{1,0:T(8,128)(2,1)S(1)} copy-done((bf16[128,3584]{1,0:T(8,128)(2,1)S(1)}, bf16[128,3584]{1,0:T(8,128)(2,1)}, u32[]{:S(2)}) %copy-start.2) | copy-done | bytes 917528
  8.4 0.0 copy-start.3
  8.4 0.9 %copy-done.3 = bf16[128,8,128]{2,1,0:T(8,128)(2,1)S(1)} copy-done((bf16[128,8,128]{2,1,0:T(8,128)(2,1)S(1)}, bf16[128,8,128]{2,1,0:T(8,128)(2,1)}, u32[]{:S(2)}) %copy-start.3) | copy-done | bytes 262168
  9.4 0.0 copy-start.4
  9.4 0.7 copy-done.4
  10.0 0.0 copy-start.6
  10.0 0.7 copy-done.6
  10.7 0.0 copy-start.8
  10.7 0.7 copy-done.8
  11.4 0.0 copy-start.9
  11.4 0.7 copy-done.9
  12.0 1.8 %shard_map.94 = (bf16[64,3712]{1,0:T(8,128)(2,1)S(1)}, bf16[24,3712]{1,0:T(8,128)(2,1)}, f32[88,128]{1,0:T(8,128)S(1)}, s32[88,128]{1,0:T(8,128)S(1)}, f32[88,128]{1,0:T(8,128)S(1)}, /*index=5*/f32[88,128]{1,0:T(8,128)S(1)}) custom-call(s32[8]{0:T(128)S(1)} %copy-done.6, s32[1,8]{1,0:T(1,128)S(1)} %copy-done.9, s32[8,128]{1,0:T(8,128)S(1)} %bitcast.20, ...), custom_call_target="tpu_custom_call" | custom-call | flops 80740352 | bytes 2019328 | tf_op jit(solution)/shard_map/pallas_call | solution.py:298
  13.8 0.0 all-gather.2.cloned.1.call-update
  13.8 26.1 %all_to_all.22 = bf16[8,8,3712]{2,1,0:T(8,128)(2,1)S(1)} all-to-all(bf16[8,8,3712]{2,1,0:T(8,128)(2,1)S(1)} %bitcast.16), channel_id=1, replica_groups=mesh['groups'=2,'expert'=8,'dp'=2] {'expert'}, dimensions={0} | all-to-all | bytes 950272 | tf_op jit(solution)/shard_map/all_to_all | solution.py:330
  40.0 22.8 %all-gather.2.cloned.1.call-done.copy_ref = bf16[192,3712]{1,0:T(8,128)(2,1)} async-done(((bf16[24,3712]{1,0:T(8,128)(2,1)}), bf16[192,3712]{1,0:T(8,128)(2,1)}) %all-gather.2.cloned.1.call-update) | async-done | bytes 1425424 | tf_op jit(solution)/shard_map/all_gather | solution.py:331
  62.8 0.0 copy-done.7
  62.8 0.0 copy-start
  62.8 1.4 %copy-done = bf16[192,3712]{1,0:T(8,128)(2,1)S(1)} copy-done((bf16[192,3712]{1,0:T(8,128)(2,1)S(1)}, bf16[192,3712]{1,0:T(8,128)(2,1)}, u32[]{:S(2)}) %copy-start) | copy-done | bytes 1425432
  64.1 0.0 copy-start.1
  64.2 1.2 %shard_map.97 = bf16[256,1792]{1,0:T(8,128)(2,1)S(1)} custom-call(s32[8]{0:T(128)S(1)} %copy-done.7, bf16[64,3712]{1,0:T(8,128)(2,1)S(1)} %bitcast.12, bf16[192,3712]{1,0:T(8,128)(2,1)S(1)} %copy-done), custom_call_target="tpu_custom_call" | custom-call | flops 234881024 | bytes 2818048 | tf_op jit(solution)/shard_map/pallas_call | solution.py:298
  65.4 0.1 collective-permute-start
  65.4 0.2 copy-done.1
  65.6 0.0 copy-start.5
  65.7 1.8 %shard_map.95 = bf16[256,128]{1,0:T(8,128)(2,1)S(1)} custom-call(s32[8]{0:T(128)S(1)} %copy-done.7, bf16[64,3712]{1,0:T(8,128)(2,1)S(1)} %bitcast.13, bf16[192,3712]{1,0:T(8,128)(2,1)S(1)} %copy-done, bf16[256,3584]{1,0:T(8,128)(2,1)S(1)} %bitcast.15), custom_call_target="tpu_custom_call" | custom-call | flops 469762048 | bytes 3801088 | tf_op jit(solution)/shard_map/pallas_call | solution.py:298
  67.4 9.7 %all_to_all.23 = bf16[8,32,128]{2,1,0:T(8,128)(2,1)S(1)} all-to-all(bf16[8,32,128]{2,1,0:T(8,128)(2,1)S(1)} %bitcast.17), channel_id=1, replica_groups=mesh['groups'=2,'expert'=8,'dp'=2] {'expert'}, dimensions={0} | all-to-all | bytes 131072 | tf_op jit(solution)/shard_map/all_to_all | solution.py:341
  77.1 0.0 copy-done.5
  77.1 1.0 %shard_map.96 = (bf16[1024,128]{1,0:T(8,128)(2,1)}, f32[8,128]{1,0:T(8,128)S(1)}) custom-call(bf16[256,128]{1,0:T(8,128)(2,1)S(1)} %bitcast.18, f32[88,128]{1,0:T(8,128)S(1)} %get-tuple-element.13.pick_ref, s32[88,128]{1,0:T(8,128)S(1)} %get-tuple-element.14.expert_ref, f32[88,128]{1,0:T(8,128)S(1)} %get-tuple-element.15.hs_ref, ...), custom_call_target="tpu_custom_call" | custom-call | flops 23068672 | bytes 516096 | tf_op jit(solution)/shard_map/pallas_call | solution.py:298
  78.1 0.6 convert_bitcast_fusion
  78.7 0.0 collective-permute-done.arrived_ref
  78.7 2.1 %shard_map.98 = bf16[256,1792]{1,0:T(8,128)(2,1)} custom-call(s32[8]{0:T(128)S(1)} %copy-done.7, bf16[64,3712]{1,0:T(8,128)(2,1)S(1)} %bitcast.14, bf16[192,3712]{1,0:T(8,128)(2,1)S(1)} %copy-done, bf16[256,1792]{1,0:T(8,128)(2,1)S(1)} %collective-permute-done.arrived_ref), custom_call_target="tpu_custom_call" | custom-call | flops 234881024 | bytes 3735552 | tf_op jit(solution)/shard_map/pallas_call | solution.py:298
Async XLA Ops:
  7.2 55.6 %copy-start.7 = (s32[8]{0:T(128)S(1)}, s32[8]{0:T(128)}, u32[]{:S(2)}) copy-start(s32[8]{0:T(128)} %replica_ref.7) | copy-start | bytes 100
  7.2 55.6 %all-gather.2.cloned.1.call-start = ((), (), s32[]{:S(2)}) async-start(), calls=%async_computation.2 | async-start | bytes 1603584 | tf_op jit(solution)/shard_map/all_gather | solution.py:331
  7.2 1.2 %copy-start.2 = (bf16[128,3584]{1,0:T(8,128)(2,1)S(1)}, bf16[128,3584]{1,0:T(8,128)(2,1)}, u32[]{:S(2)}) copy-start(bf16[128,3584]{1,0:T(8,128)(2,1)} %cot_ref.1) | copy-start | bytes 2752516
  8.4 0.9 %copy-start.3 = (bf16[128,8,128]{2,1,0:T(8,128)(2,1)S(1)}, bf16[128,8,128]{2,1,0:T(8,128)(2,1)}, u32[]{:S(2)}) copy-start(bf16[128,8,128]{2,1,0:T(8,128)(2,1)} %param.8) | copy-start | bytes 786436
  9.4 0.7 copy-start.4
  10.0 0.7 copy-start.6
  10.7 0.7 copy-start.8
  11.4 0.7 copy-start.9
  62.8 1.4 %copy-start = (bf16[192,3712]{1,0:T(8,128)(2,1)S(1)}, bf16[192,3712]{1,0:T(8,128)(2,1)}, u32[]{:S(2)}) copy-start(bf16[192,3712]{1,0:T(8,128)(2,1)} %all-gather.2.cloned.1.call-done.copy_ref) | copy-start | bytes 4276228
  64.1 1.5 %copy-start.1 = (bf16[2,128,3584]{2,1,0:T(8,128)(2,1)S(1)}, bf16[2,128,3584]{2,1,0:T(8,128)(2,1)}, u32[]{:S(2)}) copy-start(bf16[2,128,3584]{2,1,0:T(8,128)(2,1)} %param.13) | copy-start | bytes 5505028
  65.4 13.4 %collective-permute-start = (bf16[256,1792]{1,0:T(8,128)(2,1)S(1)}, bf16[256,1792]{1,0:T(8,128)(2,1)S(1)}, u32[]{:S(2)}, u32[]{:S(2)}) collective-permute-start(bf16[256,1792]{1,0:T(8,128)(2,1)S(1)} %shard_map.97), channel_id=1, source_target_pairs={{0,1},{1,0},{2,3},{3,2},{4,5},{5,4},{6,7},{7,6},{8,9},{9,8},{10,11... | collective-permute-start | bytes 2752520 | tf_op jit(solution)/shard_map/ppermute | solution.py:351
  65.6 11.5 %copy-start.5 = (s32[128,8]{0,1:T(8,128)S(1)}, s32[128,8]{0,1:T(8,128)}, u32[]{:S(2)}) copy-start(s32[128,8]{0,1:T(8,128)} %param.10) | copy-start | bytes 12292
Sparse Core Ops, SparseCore 0:
  14.0 48.7 all-gather.1

commit v2 on v1

--- a/solution.py
+++ b/solution.py
@@ -165,14 +165,25 @@
     return lax.broadcasted_iota(jnp.int32, shape, dim)
 
 
-def dispatch_kernel(local_count, dev_count, replica_ref, counts_ref, ids_ref, probs_ref, cot_ref, hid_ref,
-                    home_ref, copy_ref, pick_ref, expert_ref, hs_ref, ps_ref, wide):
+def dispatch_kernel(local_count, dev_count, *refs):
+    sources, refs = refs[:6], refs[6:]
+    copy_ref, home_refs, refs = refs[0], refs[1:1 + dev_count], refs[1 + dev_count:]
+    pick_ref, expert_ref, hs_ref, ps_ref = refs[:4]
+    held, wide, sems = refs[4:10], refs[10], refs[11]
+    moves = [pltpu.make_async_copy(s, h, sems.at[n]) for n, (s, h) in enumerate(zip(sources, held))]
+    for move in moves:
+        move.start()
+    replica_ref, counts_ref, ids_ref, probs_ref, hid_ref, cot_ref = held
     top, toks = ids_ref.shape
     d_model = cot_ref.shape[1]
-    homes = dev_count * local_count * SLOT
+    per_home = local_count * SLOT
+    homes = dev_count * per_home
     slots = homes + dev_count * CAPR
+    me = lax.axis_index("expert")
+    for move in moves[:3]:
+        move.wait()
     row = iota((slots, toks), 0)
-    expert = row // SLOT
+    expert = ((row // per_home) ^ me) * local_count + (row % per_home) // SLOT
     within = row % SLOT
     allowed = jnp.where(within < CAPH, 1, 0)
     for d in range(dev_count):
@@ -195,6 +206,8 @@
     pick = jnp.where((rank == wanted) & (allowed > 0), named, 0.0)
     pick_ref[...] = pick
     expert_ref[...] = expert
+    for move in moves[3:5]:
+        move.wait()
     wide[...] = hid_ref[...].astype(F32)
     h_slot = jnp.zeros((slots, hid_ref.shape[1]), F32)
     p_slot = jnp.zeros((slots, toks), F32)
@@ -208,11 +221,13 @@
     hs_ref[...] = h_slot
     ps_ref[...] = jnp.broadcast_to(p_slot, ps_ref.shape)
     scaled = p_slot * h_slot
+    moves[5].wait()
     rows = jnp.dot(pick.astype(BF16), cot_ref[...], preferred_element_type=F32)
-    home_ref[:, :d_model] = rows[:homes].astype(BF16)
-    home_ref[:, d_model:] = scaled[:homes].astype(BF16)
     copy_ref[:, :d_model] = rows[homes:].astype(BF16)
     copy_ref[:, d_model:] = scaled[homes:].astype(BF16)
+    for m, home_ref in enumerate(home_refs):
+        home_ref[:, :d_model] = rows[m * per_home:(m + 1) * per_home].astype(BF16)
+        home_ref[:, d_model:] = scaled[m * per_home:(m + 1) * per_home].astype(BF16)
 
 
 def local_slots(local_count, dev_count, width, replica_ref):
@@ -223,61 +238,60 @@
     for d in range(dev_count):
         mine = (row >= d * CAPR) & (row < (d + 1) * CAPR)
         copy = jnp.where(mine, replica_ref[d] - first, copy)
-    copy = jnp.broadcast_to(copy[None], (dev_count, dev_count * CAPR, width))
-    return home, copy.reshape(dev_count * dev_count * CAPR, width)
-
-
-def grad_in_kernel(local_count, dev_count, replica_ref, home_ref, copy_ref, w_ref, out_ref):
+    return jnp.concatenate([home] + [copy] * dev_count, axis=0)
+
+
+def grad_in_kernel(local_count, dev_count, replica_ref, w_ref, *refs):
+    home_refs, copy_refs, refs = refs[:dev_count], refs[dev_count:2 * dev_count], refs[2 * dev_count:]
+    rows_ref, back_refs = refs[0], refs[1:]
     d_model = w_ref.shape[1]
     width = w_ref.shape[0] // local_count
     per_home, per_copy = local_count * SLOT, dev_count * CAPR
-    results = []
-    for ref, slot in zip((home_ref, copy_ref), local_slots(local_count, dev_count, width, replica_ref)):
-        every = lax.dot_general(ref[:, :d_model], w_ref[...], NT, preferred_element_type=F32)
-        own = jnp.zeros((ref.shape[0], width), F32)
-        for e in range(local_count):
-            own = jnp.where(slot == e, every[:, e * width:(e + 1) * width], own)
-        results.append(own)
-    home, copy = results
-    both = jnp.concatenate(
-        [home.reshape(dev_count, per_home, width), copy.reshape(dev_count, per_copy, width)], axis=1)
-    out_ref[...] = both.reshape(dev_count * (per_home + per_copy), width).astype(out_ref.dtype)
-
-
-def grad_weights_half(local_count, dev_count, half, replica_ref, home_ref, copy_ref, columns):
-    width = home_ref.shape[1] - 2 * columns
+    homes = dev_count * per_home
+    rows_ref[:homes] = jnp.concatenate([r[...].astype(F32) for r in home_refs], axis=0).astype(BF16)
+    rows_ref[homes:] = jnp.concatenate([r[...].astype(F32) for r in copy_refs], axis=0).astype(BF16)
+    every = lax.dot_general(rows_ref[:, :d_model], w_ref[...], NT, preferred_element_type=F32)
+    slot = local_slots(local_count, dev_count, width, replica_ref)
+    own = jnp.zeros((rows_ref.shape[0], width), F32)
+    for e in range(local_count):
+        own = jnp.where(slot == e, every[:, e * width:(e + 1) * width], own)
+    for m, back_ref in enumerate(back_refs):
+        home = own[m * per_home:(m + 1) * per_home]
+        copy = own[homes + m * per_copy:homes + (m + 1) * per_copy]
+        back_ref[...] = jnp.concatenate([home, copy], axis=0).astype(back_ref.dtype)
+
+
+def grad_weights_half(local_count, dev_count, half, replica_ref, rows_ref, columns):
+    width = rows_ref.shape[1] - 2 * columns
     start = pl.multiple_of(half * columns, 128)
-    total = None
-    for ref, slot in zip((home_ref, copy_ref), local_slots(local_count, dev_count, width, replica_ref)):
-        scaled = ref[:, 2 * columns:].astype(F32)
-        spread = jnp.concatenate([jnp.where(slot == e, scaled, 0.0) for e in range(local_count)], axis=1)
-        part = lax.dot_general(spread.astype(BF16), ref[:, pl.ds(start, columns)], TN, preferred_element_type=F32)
-        total = part if total is None else total + part
-    return total
-
-
-def other_half_kernel(local_count, dev_count, replica_ref, home_ref, copy_ref, out_ref):
+    slot = local_slots(local_count, dev_count, width, replica_ref)
+    scaled = rows_ref[:, 2 * columns:].astype(F32)
+    spread = jnp.concatenate([jnp.where(slot == e, scaled, 0.0) for e in range(local_count)], axis=1)
+    return lax.dot_general(spread.astype(BF16), rows_ref[:, pl.ds(start, columns)], TN, preferred_element_type=F32)
+
+
+def other_half_kernel(local_count, dev_count, replica_ref, rows_ref, out_ref):
     half = 1 - lax.axis_index("dp")
     out_ref[...] = grad_weights_half(
-        local_count, dev_count, half, replica_ref, home_ref, copy_ref, out_ref.shape[1]).astype(out_ref.dtype)
-
-
-def own_half_kernel(local_count, dev_count, replica_ref, home_ref, copy_ref, arrived_ref, out_ref):
+        local_count, dev_count, half, replica_ref, rows_ref, out_ref.shape[1]).astype(out_ref.dtype)
+
+
+def own_half_kernel(local_count, dev_count, replica_ref, rows_ref, arrived_ref, out_ref):
     half = lax.axis_index("dp")
-    total = grad_weights_half(
-        local_count, dev_count, half, replica_ref, home_ref, copy_ref, out_ref.shape[1])
+    total = grad_weights_half(local_count, dev_count, half, replica_ref, rows_ref, out_ref.shape[1])
     out_ref[...] = (total + arrived_ref[...].astype(F32)).astype(out_ref.dtype)
 
 
-def combine_kernel(local_count, dev_count, back_ref, pick_ref, expert_ref, hs_ref, ps_ref, ids_ref,
-                   grad_h_ref, grad_p_ref, wide):
+def combine_kernel(local_count, dev_count, *refs):
+    back_refs, refs = refs[:dev_count], refs[dev_count:]
+    pick_ref, expert_ref, hs_ref, ps_ref, ids_ref, grad_h_ref, grad_p_ref, wide, narrow = refs
     top, toks = ids_ref.shape
-    width = back_ref.shape[1]
-    per_home, per_copy = local_count * SLOT, dev_count * CAPR
-    back = back_ref[...].astype(F32).reshape(dev_count, per_home + per_copy, width)
-    home = back[:, :per_home].reshape(dev_count * per_home, width)
-    copy = jnp.sum(back[:, per_home:], axis=0)
-    grad_in = jnp.concatenate([home, copy], axis=0)
+    per_home = local_count * SLOT
+    back = [r[...].astype(F32) for r in back_refs]
+    copy = back[0][per_home:]
+    for b in back[1:]:
+        copy = copy + b[per_home:]
+    grad_in = jnp.concatenate([b[:per_home] for b in back] + [copy], axis=0)
     h_rows = (ps_ref[...] * grad_in).astype(BF16)
     p_rows = jnp.sum(hs_ref[...] * grad_in, axis=1, keepdims=True)
     ids = ids_ref[...]
@@ -287,23 +301,28 @@
         sel = jnp.where(ids[k:k + 1, :] == expert, pick, 0.0)
         wide[pl.ds(k, toks, stride=top), :] = lax.dot_general(
             sel.astype(BF16), h_rows, TN, preferred_element_type=F32)
-        grad_p_ref[k:k + 1, :] = jnp.sum(sel * p_rows, axis=0, keepdims=True)
+        narrow[k:k + 1, :] = jnp.sum(sel * p_rows, axis=0, keepdims=True)
     grad_h_ref[...] = wide[...].astype(grad_h_ref.dtype)
-
-
-def call(kernel, out_shape, smem, operands, scratch=(), flops=0):
-    vmem = pl.BlockSpec(memory_space=pltpu.VMEM)
+    grad_p_ref[...] = narrow[...].astype(grad_p_ref.dtype)
+
+
+def call(kernel, out_shape, smem, operands, scratch=(), flops=0, limit=24, space=pltpu.VMEM):
     shapes = jax.tree.leaves(out_shape)
     moved = sum(a.size * a.dtype.itemsize for a in (*operands, *shapes))
     return pl.pallas_call(
         kernel,
         out_shape=out_shape,
-        in_specs=[pl.BlockSpec(memory_space=pltpu.SMEM)] * len(smem) + [vmem] * len(operands),
-        out_specs=jax.tree.map(lambda _: vmem, out_shape),
+        in_specs=[pl.BlockSpec(memory_space=pltpu.SMEM)] * len(smem)
+        + [pl.BlockSpec(memory_space=space)] * len(operands),
+        out_specs=jax.tree.map(lambda _: pl.BlockSpec(memory_space=pltpu.VMEM), out_shape),
         scratch_shapes=list(scratch),
-        compiler_params=pltpu.CompilerParams(vmem_limit_bytes=24 << 20),
+        compiler_params=pltpu.CompilerParams(vmem_limit_bytes=limit << 20),
         cost_estimate=pl.CostEstimate(flops=flops, bytes_accessed=moved, transcendentals=0),
     )(*smem, *operands)
+
+
+def swap(x, bits, count):
+    return lax.ppermute(x, "expert", [(i, i ^ bits) for i in range(count)])
 
 
 def gather_body(cotangent, hidden, probs, expert_ids, send_counts, replica_of, weights):
@@ -312,61 +331,72 @@
     width = hidden.shape[2]
     local_count = weights.shape[0]
     dev_count = lax.axis_size("expert")
-    homes = dev_count * local_count * SLOT
+    per_home = local_count * SLOT
+    homes = dev_count * per_home
     copies = dev_count * CAPR
     slots = homes + copies
     sizes = (local_count, dev_count)
     ids = expert_ids.T
     shape = jax.ShapeDtypeStruct
-    home_rows, copy_rows, pick, expert, h_slot, p_slot = call(
+    sources = (replica_of, send_counts, ids, probs.T, hidden.reshape(toks * top, width), cotangent)
+    copy_rows, *rest = call(
         functools.partial(dispatch_kernel, *sizes),
-        (shape((homes, d_model + width), BF16), shape((copies, d_model + width), BF16), shape((slots, toks), F32),
-         shape((slots, toks), jnp.int32), shape((slots, width), F32), shape((slots, width), F32)),
-        (replica_of, send_counts),
-        (ids, probs.T, cotangent, hidden.reshape(toks * top, width)),
-        [pltpu.VMEM((toks * top, width), F32)],
+        [shape((copies, d_model + width), BF16)]
+        + [shape((per_home, d_model + width), BF16)] * dev_count
+        + [shape((slots, toks), F32), shape((slots, toks), jnp.int32),
+           shape((slots, width), F32), shape((slots, width), F32)],
+        (),
+        sources,
+        [(pltpu.SMEM if n < 2 else pltpu.VMEM)(a.shape, a.dtype) for n, a in enumerate(sources)]
+        + [pltpu.VMEM((toks * top, width), F32), pltpu.SemaphoreType.DMA((len(sources),))],
         flops=2 * slots * toks * d_model,
-    )
-    home_in = lax.all_to_all(home_rows, "expert", split_axis=0, concat_axis=0, tiled=True)
-    copy_in = lax.all_gather(copy_rows, "expert", axis=0, tiled=True)
+        limit=48,
+        space=pl.ANY,
+    )
+    home_rows, (pick, expert, h_slot, p_slot) = rest[:dev_count], rest[dev_count:]
+    copy_in = [copy_rows] + [None] * (dev_count - 1)
+    for m in sorted(range(1, dev_count), key=lambda m: (m.bit_count(), -m)):
+        low = m & -m
+        copy_in[m] = swap(copy_in[m ^ low], low, dev_count)
+    home_in = [home_rows[0]] + [swap(home_rows[m], m, dev_count) for m in range(1, dev_count)]
     rows = homes + dev_count * copies
     w_flat = weights.reshape(local_count * width, d_model)
-    back = call(
+    all_rows, *back = call(
         functools.partial(grad_in_kernel, *sizes),
-        shape((rows, width), BF16),
+        [shape((rows, d_model + width), BF16)] + [shape((per_home + copies, width), BF16)] * dev_count,
         (replica_of,),
-        (home_in, copy_in, w_flat),
+        (w_flat, *home_in, *copy_in),
         flops=2 * rows * d_model * local_count * width,
     )
-    back = lax.all_to_all(back, "expert", split_axis=0, concat_axis=0, tiled=True)
+    back = [back[0]] + [swap(back[m], m, dev_count) for m in range(1, dev_count)]
     columns = d_model // 2
     half_flops = 2 * rows * columns * local_count * width
     other = call(
         functools.partial(other_half_kernel, *sizes),
         shape((local_count * width, columns), BF16),
         (replica_of,),
-        (home_in, copy_in),
+        (all_rows,),
         flops=half_flops,
     )
     arrived = lax.ppermute(other, "dp", [(0, 1), (1, 0)])
     grad_h, grad_p = call(
         functools.partial(combine_kernel, *sizes),
-        (shape((toks * top, width), BF16), shape((top, toks), F32)),
+        (shape((toks * top, width), BF16), shape((top, toks), BF16)),
         (),
-        (back, pick, expert, h_slot, p_slot, ids),
-        [pltpu.VMEM((toks * top, width), F32)],
+        (*back, pick, expert, h_slot, p_slot, ids),
+        [pltpu.VMEM((toks * top, width), F32), pltpu.VMEM((top, toks), F32)],
         flops=2 * slots * toks * width * top,
     )
     grad_w = call(
         functools.partial(own_half_kernel, *sizes),
         shape((local_count * width, columns), BF16),
         (replica_of,),
-        (home_in, copy_in, arrived),
+        (all_rows, arrived),
         flops=half_flops,
     )
     return (
         grad_h.reshape(toks, top, width),
-        grad_p.T.astype(BF16),
+        grad_p.T,
         grad_w.reshape(local_count, width, columns),
     )
 
@@ -375,7 +405,7 @@
     dev_count = lax.axis_size("expert")
     local_count, width, _ = weights.shape
     gathered = dev_count * dev_count * CAPR
-    if gathered <= (local_count + 3) * width and lax.axis_size("dp") == 2:
+    if gathered <= (local_count + 3) * width and dev_count.bit_count() == 1 and lax.axis_size("dp") == 2:
         run = gather_body
     else:
         run = replica_body

time: 88.1 us -> 73.1 us (0.83)
  starting transfers between devices: 0.11 us -> 40.1 us
  blocking collectives: 35.8 us -> 0 us
  between operations: 14.1 us -> 0.7 us
  waiting for transfers between devices: 22.8 us -> 19 us
  Pallas kernels: 7.9 us -> 6.66 us
    ppermute x0 -> x21, starting transfers between devices: none -> 40.1 us  [swap(): return lax.ppermute(x, 'expert', [(i, i ^ bits) for i in range(count)])]
    all_to_all x2 -> x0, blocking collectives: 35.8 us -> none  [the longest x1 26.1 us: gather_body(): lax.all_to_all(home_rows, 'expert', split_axis=0, concat_axis=0, tiled=True)]
    all_gather x1 -> x0, waiting for transfers between devices: 22.8 us -> none  [gather_body(): copy_in = lax.all_gather(copy_rows, 'expert', axis=0, tiled=True)]
    ppermute x0 -> x21, waiting for transfers between devices: none -> 19 us  [swap(): return lax.ppermute(x, 'expert', [(i, i ^ bits) for i in range(count)])]
    pallas_call x5, Pallas kernels: 7.9 us -> 6.66 us  [call(): pl.pallas_call(kernel, out_shape=out_shape, in_specs=[pl.BlockSpec(memory...]
    unnamed x20 -> x14, local copies, waits for them, and re-layouts: 6.37 us -> 6.3 us
  transfers between devices with their start and end apart: 2 -> 22, of which waited for: 1 -> 7; matrix products, arithmetic and copies ran while one was open for 1% -> 0% of each run, Pallas kernels for 3% -> 1%
where the time goes in v2:
time: 73.1 us; the launch traced here: 72.8 us
  starting transfers between devices  40.1 us (55%)
  waiting for transfers between devices  19 us (26%)
  Pallas kernels  6.66 us (9%)
  local copies, waits for them, and re-layouts  6.3 us (9%)
    ppermute x21, starting transfers between devices, swap(): return lax.ppermute(x, 'expert', [(i, i ^ bits) for i in range(count)])  40.1 us
    ppermute x21, waiting for transfers between devices, swap(): return lax.ppermute(x, 'expert', [(i, i ^ bits) for i in range(count)])  19 us
    pallas_call x5, Pallas kernels, call(): pl.pallas_call(kernel, out_shape=out_shape, in_specs=[pl.BlockSpec(memory...  6.66 us
    unnamed x14, local copies, waits for them, and re-layouts  6.3 us
  transfers between devices with their start and end apart: 22, of which 7 were waited for; matrix products, arithmetic and copies ran while one was open for 0% of the time, Pallas kernels for 1%

profile of v2, /device:TPU:0, one launch (start us, length us, event | category | flops | bytes accessed | tf_op | source)
XLA Modules:
  0.0 72.8 jit_solution(15269769222099551533)
XLA Ops:
  0.6 0.0 copy-start.1
  0.6 1.2 %copy-done.1 = bf16[128,3584]{1,0:T(8,128)(2,1)S(1)} copy-done((bf16[128,3584]{1,0:T(8,128)(2,1)S(1)}, bf16[128,3584]{1,0:T(8,128)(2,1)}, u32[]{:S(2)}) %copy-start.1) | copy-done | bytes 917528
  1.8 0.0 copy-start.2
  1.8 0.9 %copy-done.2 = bf16[128,8,128]{2,1,0:T(8,128)(2,1)S(1)} copy-done((bf16[128,8,128]{2,1,0:T(8,128)(2,1)S(1)}, bf16[128,8,128]{2,1,0:T(8,128)(2,1)}, u32[]{:S(2)}) %copy-start.2) | copy-done | bytes 262168
  2.8 0.0 copy-start.3
  2.8 0.7 copy-done.3
  3.5 0.0 copy-start.4
  3.5 0.7 copy-done.4
  4.1 0.0 copy-start.5
  4.1 0.7 copy-done.5
  4.8 0.0 copy-start.6
  4.8 0.7 copy-done.6
  5.4 1.5 %shard_map.94 = (bf16[24,3712]{1,0:T(8,128)(2,1)S(1)}, bf16[8,3712]{1,0:T(8,128)(2,1)S(1)}, bf16[8,3712]{1,0:T(8,128)(2,1)S(1)}, bf16[8,3712]{1,0:T(8,128)(2,1)S...) custom-call(s32[8]{0:T(128)S(1)} %copy-done.4, ...), custom_call_target="tpu_custom_call" | custom-call | flops 80740352 | bytes 2019392 | tf_op jit(solution)/shard_map/pallas_call | solution.py:312
  6.9 4.1 %collective-permute-start.10 = (bf16[24,3712]{1,0:T(8,128)(2,1)S(1)}, bf16[24,3712]{1,0:T(8,128)(2,1)S(1)}, u32[]{:S(2)}, u32[]{:S(2)}) collective-permute-start(bf16[24,3712]{1,0:T(8,128)(2,1)S(1)} %get-tuple-element.35.refs_8_), channel_id=1, source_target_pairs={{0,8},{2,10},{4,12},{6,14},{8,0},{10,2},{12,4},{14,6},{1,9},{3,11}... | collective-permute-start | bytes 534536 | tf_op jit(solution)/shard_map/ppermute | solution.py:325
  11.0 1.6 %collective-permute-start.8 = (bf16[24,3712]{1,0:T(8,128)(2,1)S(1)}, bf16[24,3712]{1,0:T(8,128)(2,1)S(1)}, u32[]{:S(2)}, u32[]{:S(2)}) collective-permute-start(bf16[24,3712]{1,0:T(8,128)(2,1)S(1)} %get-tuple-element.35.refs_8_), channel_id=1, source_target_pairs={{0,4},{2,6},{4,0},{6,2},{8,12},{10,14},{12,8},{14,10},{1,5},{3,7},... | collective-permute-start | bytes 534536 | tf_op jit(solution)/shard_map/ppermute | solution.py:325
  12.6 6.9 %collective-permute-done.10.refs_12_ = bf16[24,3712]{1,0:T(8,128)(2,1)S(1)} collective-permute-done((bf16[24,3712]{1,0:T(8,128)(2,1)S(1)}, bf16[24,3712]{1,0:T(8,128)(2,1)S(1)}, u32[]{:S(2)}, u32[]{:S(2)}) %collective-permute-start.10) | collective-permute-done | bytes 178208 | tf_op jit(solution)/shard_map/ppermute | solution.py:325
  19.5 0.6 collective-permute-start.12
  20.1 1.5 %collective-permute-start = (bf16[8,3712]{1,0:T(8,128)(2,1)S(1)}, bf16[8,3712]{1,0:T(8,128)(2,1)S(1)}, u32[]{:S(2)}, u32[]{:S(2)}) collective-permute-start(bf16[8,3712]{1,0:T(8,128)(2,1)S(1)} %get-tuple-element.28), channel_id=1, source_target_pairs={{0,2},{2,0},{4,6},{6,4},{8,10},{10,8},{12,14},{14,12},{1,3},{3,1},... | collective-permute-start | bytes 178184 | tf_op jit(solution)/shard_map/ppermute | solution.py:325
  21.6 1.5 %collective-permute-start.1 = (bf16[8,3712]{1,0:T(8,128)(2,1)S(1)}, bf16[8,3712]{1,0:T(8,128)(2,1)S(1)}, u32[]{:S(2)}, u32[]{:S(2)}) collective-permute-start(bf16[8,3712]{1,0:T(8,128)(2,1)S(1)} %get-tuple-element.29), channel_id=1, source_target_pairs={{0,4},{2,6},{4,0},{6,2},{8,12},{10,14},{12,8},{14,10},{1,5},{3,7},... | collective-permute-start | bytes 178184 | tf_op jit(solution)/shard_map/ppermute | solution.py:325
  23.0 0.5 collective-permute-start.2
  23.6 0.7 collective-permute-done.refs_1_
  24.3 3.4 %collective-permute-start.3 = (bf16[8,3712]{1,0:T(8,128)(2,1)S(1)}, bf16[8,3712]{1,0:T(8,128)(2,1)S(1)}, u32[]{:S(2)}, u32[]{:S(2)}) collective-permute-start(bf16[8,3712]{1,0:T(8,128)(2,1)S(1)} %get-tuple-element.31), channel_id=1, source_target_pairs={{0,8},{2,10},{4,12},{6,14},{8,0},{10,2},{12,4},{14,6},{1,9},{3,11}... | collective-permute-start | bytes 178184 | tf_op jit(solution)/shard_map/ppermute | solution.py:325
  27.7 0.0 collective-permute-done.1.refs_2_
  27.7 3.9 %collective-permute-start.4 = (bf16[8,3712]{1,0:T(8,128)(2,1)S(1)}, bf16[8,3712]{1,0:T(8,128)(2,1)S(1)}, u32[]{:S(2)}, u32[]{:S(2)}) collective-permute-start(bf16[8,3712]{1,0:T(8,128)(2,1)S(1)} %get-tuple-element.32), channel_id=1, source_target_pairs={{0,10},{2,8},{4,14},{6,12},{8,2},{10,0},{12,6},{14,4},{1,11},{3,9}... | collective-permute-start | bytes 178184 | tf_op jit(solution)/shard_map/ppermute | solution.py:325
  31.6 0.0 collective-permute-done.2.refs_3_
  31.6 0.5 collective-permute-start.7
  32.1 0.0 collective-permute-done.3.refs_4_
  32.1 1.5 %collective-permute-start.11 = (bf16[24,3712]{1,0:T(8,128)(2,1)S(1)}, bf16[24,3712]{1,0:T(8,128)(2,1)S(1)}, u32[]{:S(2)}, u32[]{:S(2)}) collective-permute-start(bf16[24,3712]{1,0:T(8,128)(2,1)S(1)} %collective-permute-done.10.refs_12_), channel_id=1, source_target_pairs={{0,2},{2,0},{4,6},{6,4},{8,10},{10,8},{12,14},{14,12},{1,3},{3,1},... | collective-permute-start | bytes 534536 | tf_op jit(solution)/shard_map/ppermute | solution.py:325
  33.6 0.0 collective-permute-done.8.refs_10_
  33.6 0.5 collective-permute-start.9
  34.1 0.0 collective-permute-done.12.refs_14_
  34.1 1.5 %collective-permute-start.13 = (bf16[24,3712]{1,0:T(8,128)(2,1)S(1)}, bf16[24,3712]{1,0:T(8,128)(2,1)S(1)}, u32[]{:S(2)}, u32[]{:S(2)}) collective-permute-start(bf16[24,3712]{1,0:T(8,128)(2,1)S(1)} %collective-permute-done.12.refs_14_), channel_id=1, source_target_pairs={{0,2},{2,0},{4,6},{6,4},{8,10},{10,8},{12,14},{14,12},{1,3},{3,1},... | collective-permute-start | bytes 534536 | tf_op jit(solution)/shard_map/ppermute | solution.py:325
  35.6 0.0 collective-permute-done.4.refs_5_
  35.6 3.2 %collective-permute-start.5 = (bf16[8,3712]{1,0:T(8,128)(2,1)S(1)}, bf16[8,3712]{1,0:T(8,128)(2,1)S(1)}, u32[]{:S(2)}, u32[]{:S(2)}) collective-permute-start(bf16[8,3712]{1,0:T(8,128)(2,1)S(1)} %get-tuple-element.33), channel_id=1, source_target_pairs={{0,12},{2,14},{4,8},{6,10},{8,4},{10,6},{12,0},{14,2},{1,13},{3,15... | collective-permute-start | bytes 178184 | tf_op jit(solution)/shard_map/ppermute | solution.py:325
  38.8 2.9 %collective-permute-done.5.refs_6_ = bf16[8,3712]{1,0:T(8,128)(2,1)S(1)} collective-permute-done((bf16[8,3712]{1,0:T(8,128)(2,1)S(1)}, bf16[8,3712]{1,0:T(8,128)(2,1)S(1)}, u32[]{:S(2)}, u32[]{:S(2)}) %collective-permute-start.5) | collective-permute-done | bytes 59424 | tf_op jit(solution)/shard_map/ppermute | solution.py:325
  41.7 4.6 %collective-permute-start.6 = (bf16[8,3712]{1,0:T(8,128)(2,1)S(1)}, bf16[8,3712]{1,0:T(8,128)(2,1)S(1)}, u32[]{:S(2)}, u32[]{:S(2)}) collective-permute-start(bf16[8,3712]{1,0:T(8,128)(2,1)S(1)} %get-tuple-element.34), channel_id=1, source_target_pairs={{0,14},{2,12},{4,10},{6,8},{8,6},{10,4},{12,2},{14,0},{1,15},{3,13... | collective-permute-start | bytes 178184 | tf_op jit(solution)/shard_map/ppermute | solution.py:325
  46.3 2.4 %collective-permute-done.6.refs_7_ = bf16[8,3712]{1,0:T(8,128)(2,1)S(1)} collective-permute-done((bf16[8,3712]{1,0:T(8,128)(2,1)S(1)}, bf16[8,3712]{1,0:T(8,128)(2,1)S(1)}, u32[]{:S(2)}, u32[]{:S(2)}) %collective-permute-start.6) | collective-permute-done | bytes 59424 | tf_op jit(solution)/shard_map/ppermute | solution.py:325
  48.7 0.0 collective-permute-done.7.refs_9_
  48.7 0.0 collective-permute-done.11.refs_13_
  48.7 0.0 collective-permute-done.9.refs_11_
  48.7 0.9 %collective-permute-done.13.refs_15_ = bf16[24,3712]{1,0:T(8,128)(2,1)S(1)} collective-permute-done((bf16[24,3712]{1,0:T(8,128)(2,1)S(1)}, bf16[24,3712]{1,0:T(8,128)(2,1)S(1)}, u32[]{:S(2)}, u32[]{:S(2)}) %collective-permute-start.13) | collective-permute-done | bytes 178208 | tf_op jit(solution)/shard_map/ppermute | solution.py:325
  49.6 0.0 copy-start
  49.6 1.5 %copy-done = bf16[2,128,3584]{2,1,0:T(8,128)(2,1)S(1)} copy-done((bf16[2,128,3584]{2,1,0:T(8,128)(2,1)S(1)}, bf16[2,128,3584]{2,1,0:T(8,128)(2,1)}, u32[]{:S(2)}) %copy-start) | copy-done | bytes 1835032
  51.1 1.2 %shard_map.95 = (bf16[256,3712]{1,0:T(8,128)(2,1)S(1)}, bf16[32,128]{1,0:T(8,128)(2,1)S(1)}, bf16[32,128]{1,0:T(8,128)(2,1)S(1)}, bf16[32,128]{1,0:T(8,128)(2,1)...) custom-call(s32[8]{0:T(128)S(1)} %copy-done.4, ...), custom_call_target="tpu_custom_call" | custom-call | flops 469762048 | bytes 5701632 | tf_op jit(solution)/shard_map/pallas_call | solution.py:312
  52.3 1.0 %shard_map.97 = bf16[256,1792]{1,0:T(8,128)(2,1)S(1)} custom-call(s32[8]{0:T(128)S(1)} %copy-done.4, bf16[256,3712]{1,0:T(8,128)(2,1)S(1)} %get-tuple-element.50.rows_ref), custom_call_target="tpu_custom_call" | custom-call | flops 234881024 | bytes 2818048 | tf_op jit(solution)/shard_map/pallas_call | solution.py:312
  53.3 0.1 collective-permute-start.21
  53.4 0.9 %collective-permute-start.14 = (bf16[32,128]{1,0:T(8,128)(2,1)S(1)}, bf16[32,128]{1,0:T(8,128)(2,1)S(1)}, u32[]{:S(2)}, u32[]{:S(2)}) collective-permute-start(bf16[32,128]{1,0:T(8,128)(2,1)S(1)} %get-tuple-element.37), channel_id=1, source_target_pairs={{0,2},{2,0},{4,6},{6,4},{8,10},{10,8},{12,14},{14,12},{1,3},{3,1},... | collective-permute-start | bytes 24584 | tf_op jit(solution)/shard_map/ppermute | solution.py:325
  54.3 1.6 %collective-permute-start.15 = (bf16[32,128]{1,0:T(8,128)(2,1)S(1)}, bf16[32,128]{1,0:T(8,128)(2,1)S(1)}, u32[]{:S(2)}, u32[]{:S(2)}) collective-permute-start(bf16[32,128]{1,0:T(8,128)(2,1)S(1)} %get-tuple-element.38), channel_id=1, source_target_pairs={{0,4},{2,6},{4,0},{6,2},{8,12},{10,14},{12,8},{14,10},{1,5},{3,7},... | collective-permute-start | bytes 24584 | tf_op jit(solution)/shard_map/ppermute | solution.py:325
  55.8 1.1 %collective-permute-start.16 = (bf16[32,128]{1,0:T(8,128)(2,1)S(1)}, bf16[32,128]{1,0:T(8,128)(2,1)S(1)}, u32[]{:S(2)}, u32[]{:S(2)}) collective-permute-start(bf16[32,128]{1,0:T(8,128)(2,1)S(1)} %get-tuple-element.39), channel_id=1, source_target_pairs={{0,6},{2,4},{4,2},{6,0},{8,14},{10,12},{12,10},{14,8},{1,7},{3,5},... | collective-permute-start | bytes 24584 | tf_op jit(solution)/shard_map/ppermute | solution.py:325
  57.0 1.7 %collective-permute-start.17 = (bf16[32,128]{1,0:T(8,128)(2,1)S(1)}, bf16[32,128]{1,0:T(8,128)(2,1)S(1)}, u32[]{:S(2)}, u32[]{:S(2)}) collective-permute-start(bf16[32,128]{1,0:T(8,128)(2,1)S(1)} %get-tuple-element.40), channel_id=1, source_target_pairs={{0,8},{2,10},{4,12},{6,14},{8,0},{10,2},{12,4},{14,6},{1,9},{3,11}... | collective-permute-start | bytes 24584 | tf_op jit(solution)/shard_map/ppermute | solution.py:325
  58.7 0.0 collective-permute-done.14.refs_1_
  58.7 1.4 %collective-permute-start.18 = (bf16[32,128]{1,0:T(8,128)(2,1)S(1)}, bf16[32,128]{1,0:T(8,128)(2,1)S(1)}, u32[]{:S(2)}, u32[]{:S(2)}) collective-permute-start(bf16[32,128]{1,0:T(8,128)(2,1)S(1)} %get-tuple-element.41), channel_id=1, source_target_pairs={{0,10},{2,8},{4,14},{6,12},{8,2},{10,0},{12,6},{14,4},{1,11},{3,9}... | collective-permute-start | bytes 24584 | tf_op jit(solution)/shard_map/ppermute | solution.py:325
  60.1 0.0 collective-permute-done.15.refs_2_
  60.1 3.4 %collective-permute-start.19 = (bf16[32,128]{1,0:T(8,128)(2,1)S(1)}, bf16[32,128]{1,0:T(8,128)(2,1)S(1)}, u32[]{:S(2)}, u32[]{:S(2)}) collective-permute-start(bf16[32,128]{1,0:T(8,128)(2,1)S(1)} %get-tuple-element.42), channel_id=1, source_target_pairs={{0,12},{2,14},{4,8},{6,10},{8,4},{10,6},{12,0},{14,2},{1,13},{3,15... | collective-permute-start | bytes 24584 | tf_op jit(solution)/shard_map/ppermute | solution.py:325
  63.5 0.0 collective-permute-done.16.refs_3_
  63.5 1.1 %collective-permute-start.20 = (bf16[32,128]{1,0:T(8,128)(2,1)S(1)}, bf16[32,128]{1,0:T(8,128)(2,1)S(1)}, u32[]{:S(2)}, u32[]{:S(2)}) collective-permute-start(bf16[32,128]{1,0:T(8,128)(2,1)S(1)} %get-tuple-element.43), channel_id=1, source_target_pairs={{0,14},{2,12},{4,10},{6,8},{8,6},{10,4},{12,2},{14,0},{1,15},{3,13... | collective-permute-start | bytes 24584 | tf_op jit(solution)/shard_map/ppermute | solution.py:325
  64.6 0.0 collective-permute-done.17.refs_4_
  64.6 0.0 collective-permute-done.18.refs_5_
  64.6 0.9 %collective-permute-done.19.refs_6_ = bf16[32,128]{1,0:T(8,128)(2,1)S(1)} collective-permute-done((bf16[32,128]{1,0:T(8,128)(2,1)S(1)}, bf16[32,128]{1,0:T(8,128)(2,1)S(1)}, u32[]{:S(2)}, u32[]{:S(2)}) %collective-permute-start.19) | collective-permute-done | bytes 8224 | tf_op jit(solution)/shard_map/ppermute | solution.py:325
  65.6 4.3 %collective-permute-done.20.refs_7_ = bf16[32,128]{1,0:T(8,128)(2,1)S(1)} collective-permute-done((bf16[32,128]{1,0:T(8,128)(2,1)S(1)}, bf16[32,128]{1,0:T(8,128)(2,1)S(1)}, u32[]{:S(2)}, u32[]{:S(2)}) %collective-permute-start.20) | collective-permute-done | bytes 8224 | tf_op jit(solution)/shard_map/ppermute | solution.py:325
  69.9 1.0 %shard_map.96 = (bf16[1024,128]{1,0:T(8,128)(2,1)}, bf16[8,128]{1,0:T(8,128)(2,1)}) custom-call(bf16[32,128]{1,0:T(8,128)(2,1)S(1)} %get-tuple-element.36.refs_0_, bf16[32,128]{1,0:T(8,128)(2,1)S(1)} %collective-permute-done.14.refs_1_, bf16[32,128]{1,0:T(8,128)(2,1)S(1)} %collective-permute-done.15.refs_2_, ...), custom_call_target="tpu_custom_call" | custom-call | flops 23068672 | bytes 514048 | tf_op jit(solution)/shard_map/pallas_call | solution.py:312
  70.9 0.0 collective-permute-done.21.arrived_ref
  70.9 1.9 %shard_map.98 = bf16[256,1792]{1,0:T(8,128)(2,1)} custom-call(s32[8]{0:T(128)S(1)} %copy-done.4, bf16[256,3712]{1,0:T(8,128)(2,1)S(1)} %get-tuple-element.50.rows_ref, bf16[256,1792]{1,0:T(8,128)(2,1)S(1)} %collective-permute-done.21.arrived_ref), custom_call_target="tpu_custom_call" | custom-call | flops 234881024 | bytes 3735552 | tf_op jit(solution)/shard_map/pallas_call | solution.py:312
Async XLA Ops:
  0.6 1.2 %copy-start.1 = (bf16[128,3584]{1,0:T(8,128)(2,1)S(1)}, bf16[128,3584]{1,0:T(8,128)(2,1)}, u32[]{:S(2)}) copy-start(bf16[128,3584]{1,0:T(8,128)(2,1)} %refs_5_.1) | copy-start | bytes 2752516
  1.8 0.9 %copy-start.2 = (bf16[128,8,128]{2,1,0:T(8,128)(2,1)S(1)}, bf16[128,8,128]{2,1,0:T(8,128)(2,1)}, u32[]{:S(2)}) copy-start(bf16[128,8,128]{2,1,0:T(8,128)(2,1)} %param.8) | copy-start | bytes 786436
  2.8 0.7 copy-start.3
  3.5 0.7 copy-start.4
  4.1 0.7 copy-start.5
  4.8 0.7 copy-start.6
  6.9 12.5 %collective-permute-start.10 = (bf16[24,3712]{1,0:T(8,128)(2,1)S(1)}, bf16[24,3712]{1,0:T(8,128)(2,1)S(1)}, u32[]{:S(2)}, u32[]{:S(2)}) collective-permute-start(bf16[24,3712]{1,0:T(8,128)(2,1)S(1)} %get-tuple-element.35.refs_8_), channel_id=1, source_target_pairs={{0,8},{2,10},{4,12},{6,14},{8,0},{10,2},{12,4},{14,6},{1,9},{3,11}... | collective-permute-start | bytes 534536 | tf_op jit(solution)/shard_map/ppermute | solution.py:325
  11.0 22.6 %collective-permute-start.8 = (bf16[24,3712]{1,0:T(8,128)(2,1)S(1)}, bf16[24,3712]{1,0:T(8,128)(2,1)S(1)}, u32[]{:S(2)}, u32[]{:S(2)}) collective-permute-start(bf16[24,3712]{1,0:T(8,128)(2,1)S(1)} %get-tuple-element.35.refs_8_), channel_id=1, source_target_pairs={{0,4},{2,6},{4,0},{6,2},{8,12},{10,14},{12,8},{14,10},{1,5},{3,7},... | collective-permute-start | bytes 534536 | tf_op jit(solution)/shard_map/ppermute | solution.py:325
  19.5 14.7 %collective-permute-start.12 = (bf16[24,3712]{1,0:T(8,128)(2,1)S(1)}, bf16[24,3712]{1,0:T(8,128)(2,1)S(1)}, u32[]{:S(2)}, u32[]{:S(2)}) collective-permute-start(bf16[24,3712]{1,0:T(8,128)(2,1)S(1)} %collective-permute-done.10.refs_12_), channel_id=1, source_target_pairs={{0,4},{2,6},{4,0},{6,2},{8,12},{10,14},{12,8},{14,10},{1,5},{3,7},... | collective-permute-start | bytes 534536 | tf_op jit(solution)/shard_map/ppermute | solution.py:325
  20.1 4.2 %collective-permute-start = (bf16[8,3712]{1,0:T(8,128)(2,1)S(1)}, bf16[8,3712]{1,0:T(8,128)(2,1)S(1)}, u32[]{:S(2)}, u32[]{:S(2)}) collective-permute-start(bf16[8,3712]{1,0:T(8,128)(2,1)S(1)} %get-tuple-element.28), channel_id=1, source_target_pairs={{0,2},{2,0},{4,6},{6,4},{8,10},{10,8},{12,14},{14,12},{1,3},{3,1},... | collective-permute-start | bytes 178184 | tf_op jit(solution)/shard_map/ppermute | solution.py:325
  21.6 6.1 %collective-permute-start.1 = (bf16[8,3712]{1,0:T(8,128)(2,1)S(1)}, bf16[8,3712]{1,0:T(8,128)(2,1)S(1)}, u32[]{:S(2)}, u32[]{:S(2)}) collective-permute-start(bf16[8,3712]{1,0:T(8,128)(2,1)S(1)} %get-tuple-element.29), channel_id=1, source_target_pairs={{0,4},{2,6},{4,0},{6,2},{8,12},{10,14},{12,8},{14,10},{1,5},{3,7},... | collective-permute-start | bytes 178184 | tf_op jit(solution)/shard_map/ppermute | solution.py:325
  23.0 8.5 %collective-permute-start.2 = (bf16[8,3712]{1,0:T(8,128)(2,1)S(1)}, bf16[8,3712]{1,0:T(8,128)(2,1)S(1)}, u32[]{:S(2)}, u32[]{:S(2)}) collective-permute-start(bf16[8,3712]{1,0:T(8,128)(2,1)S(1)} %get-tuple-element.30), channel_id=1, source_target_pairs={{0,6},{2,4},{4,2},{6,0},{8,14},{10,12},{12,10},{14,8},{1,7},{3,5},... | collective-permute-start | bytes 178184 | tf_op jit(solution)/shard_map/ppermute | solution.py:325
  24.3 7.8 %collective-permute-start.3 = (bf16[8,3712]{1,0:T(8,128)(2,1)S(1)}, bf16[8,3712]{1,0:T(8,128)(2,1)S(1)}, u32[]{:S(2)}, u32[]{:S(2)}) collective-permute-start(bf16[8,3712]{1,0:T(8,128)(2,1)S(1)} %get-tuple-element.31), channel_id=1, source_target_pairs={{0,8},{2,10},{4,12},{6,14},{8,0},{10,2},{12,4},{14,6},{1,9},{3,11}... | collective-permute-start | bytes 178184 | tf_op jit(solution)/shard_map/ppermute | solution.py:325
  27.7 8.0 %collective-permute-start.4 = (bf16[8,3712]{1,0:T(8,128)(2,1)S(1)}, bf16[8,3712]{1,0:T(8,128)(2,1)S(1)}, u32[]{:S(2)}, u32[]{:S(2)}) collective-permute-start(bf16[8,3712]{1,0:T(8,128)(2,1)S(1)} %get-tuple-element.32), channel_id=1, source_target_pairs={{0,10},{2,8},{4,14},{6,12},{8,2},{10,0},{12,6},{14,4},{1,11},{3,9}... | collective-permute-start | bytes 178184 | tf_op jit(solution)/shard_map/ppermute | solution.py:325
  31.6 17.1 %collective-permute-start.7 = (bf16[24,3712]{1,0:T(8,128)(2,1)S(1)}, bf16[24,3712]{1,0:T(8,128)(2,1)S(1)}, u32[]{:S(2)}, u32[]{:S(2)}) collective-permute-start(bf16[24,3712]{1,0:T(8,128)(2,1)S(1)} %get-tuple-element.35.refs_8_), channel_id=1, source_target_pairs={{0,2},{2,0},{4,6},{6,4},{8,10},{10,8},{12,14},{14,12},{1,3},{3,1},... | collective-permute-start | bytes 534536 | tf_op jit(solution)/shard_map/ppermute | solution.py:325
  32.1 16.6 %collective-permute-start.11 = (bf16[24,3712]{1,0:T(8,128)(2,1)S(1)}, bf16[24,3712]{1,0:T(8,128)(2,1)S(1)}, u32[]{:S(2)}, u32[]{:S(2)}) collective-permute-start(bf16[24,3712]{1,0:T(8,128)(2,1)S(1)} %collective-permute-done.10.refs_12_), channel_id=1, source_target_pairs={{0,2},{2,0},{4,6},{6,4},{8,10},{10,8},{12,14},{14,12},{1,3},{3,1},... | collective-permute-start | bytes 534536 | tf_op jit(solution)/shard_map/ppermute | solution.py:325
  33.6 15.1 %collective-permute-start.9 = (bf16[24,3712]{1,0:T(8,128)(2,1)S(1)}, bf16[24,3712]{1,0:T(8,128)(2,1)S(1)}, u32[]{:S(2)}, u32[]{:S(2)}) collective-permute-start(bf16[24,3712]{1,0:T(8,128)(2,1)S(1)} %collective-permute-done.8.refs_10_), channel_id=1, source_target_pairs={{0,2},{2,0},{4,6},{6,4},{8,10},{10,8},{12,14},{14,12},{1,3},{3,1},... | collective-permute-start | bytes 534536 | tf_op jit(solution)/shard_map/ppermute | solution.py:325
  34.1 15.5 %collective-permute-start.13 = (bf16[24,3712]{1,0:T(8,128)(2,1)S(1)}, bf16[24,3712]{1,0:T(8,128)(2,1)S(1)}, u32[]{:S(2)}, u32[]{:S(2)}) collective-permute-start(bf16[24,3712]{1,0:T(8,128)(2,1)S(1)} %collective-permute-done.12.refs_14_), channel_id=1, source_target_pairs={{0,2},{2,0},{4,6},{6,4},{8,10},{10,8},{12,14},{14,12},{1,3},{3,1},... | collective-permute-start | bytes 534536 | tf_op jit(solution)/shard_map/ppermute | solution.py:325
  35.6 6.1 %collective-permute-start.5 = (bf16[8,3712]{1,0:T(8,128)(2,1)S(1)}, bf16[8,3712]{1,0:T(8,128)(2,1)S(1)}, u32[]{:S(2)}, u32[]{:S(2)}) collective-permute-start(bf16[8,3712]{1,0:T(8,128)(2,1)S(1)} %get-tuple-element.33), channel_id=1, source_target_pairs={{0,12},{2,14},{4,8},{6,10},{8,4},{10,6},{12,0},{14,2},{1,13},{3,15... | collective-permute-start | bytes 178184 | tf_op jit(solution)/shard_map/ppermute | solution.py:325
  41.7 7.0 %collective-permute-start.6 = (bf16[8,3712]{1,0:T(8,128)(2,1)S(1)}, bf16[8,3712]{1,0:T(8,128)(2,1)S(1)}, u32[]{:S(2)}, u32[]{:S(2)}) collective-permute-start(bf16[8,3712]{1,0:T(8,128)(2,1)S(1)} %get-tuple-element.34), channel_id=1, source_target_pairs={{0,14},{2,12},{4,10},{6,8},{8,6},{10,4},{12,2},{14,0},{1,15},{3,13... | collective-permute-start | bytes 178184 | tf_op jit(solution)/shard_map/ppermute | solution.py:325
  49.6 1.5 %copy-start = (bf16[2,128,3584]{2,1,0:T(8,128)(2,1)S(1)}, bf16[2,128,3584]{2,1,0:T(8,128)(2,1)}, u32[]{:S(2)}) copy-start(bf16[2,128,3584]{2,1,0:T(8,128)(2,1)} %param.13) | copy-start | bytes 5505028
  53.3 17.5 %collective-permute-start.21 = (bf16[256,1792]{1,0:T(8,128)(2,1)S(1)}, bf16[256,1792]{1,0:T(8,128)(2,1)S(1)}, u32[]{:S(2)}, u32[]{:S(2)}) collective-permute-start(bf16[256,1792]{1,0:T(8,128)(2,1)S(1)} %shard_map.97), channel_id=1, source_target_pairs={{0,1},{1,0},{2,3},{3,2},{4,5},{5,4},{6,7},{7,6},{8,9},{9,8},{10,11... | collective-permute-start | bytes 2752520 | tf_op jit(solution)/shard_map/ppermute | solution.py:381
  53.4 5.3 %collective-permute-start.14 = (bf16[32,128]{1,0:T(8,128)(2,1)S(1)}, bf16[32,128]{1,0:T(8,128)(2,1)S(1)}, u32[]{:S(2)}, u32[]{:S(2)}) collective-permute-start(bf16[32,128]{1,0:T(8,128)(2,1)S(1)} %get-tuple-element.37), channel_id=1, source_target_pairs={{0,2},{2,0},{4,6},{6,4},{8,10},{10,8},{12,14},{14,12},{1,3},{3,1},... | collective-permute-start | bytes 24584 | tf_op jit(solution)/shard_map/ppermute | solution.py:325
  54.3 5.9 %collective-permute-start.15 = (bf16[32,128]{1,0:T(8,128)(2,1)S(1)}, bf16[32,128]{1,0:T(8,128)(2,1)S(1)}, u32[]{:S(2)}, u32[]{:S(2)}) collective-permute-start(bf16[32,128]{1,0:T(8,128)(2,1)S(1)} %get-tuple-element.38), channel_id=1, source_target_pairs={{0,4},{2,6},{4,0},{6,2},{8,12},{10,14},{12,8},{14,10},{1,5},{3,7},... | collective-permute-start | bytes 24584 | tf_op jit(solution)/shard_map/ppermute | solution.py:325
  55.8 7.7 %collective-permute-start.16 = (bf16[32,128]{1,0:T(8,128)(2,1)S(1)}, bf16[32,128]{1,0:T(8,128)(2,1)S(1)}, u32[]{:S(2)}, u32[]{:S(2)}) collective-permute-start(bf16[32,128]{1,0:T(8,128)(2,1)S(1)} %get-tuple-element.39), channel_id=1, source_target_pairs={{0,6},{2,4},{4,2},{6,0},{8,14},{10,12},{12,10},{14,8},{1,7},{3,5},... | collective-permute-start | bytes 24584 | tf_op jit(solution)/shard_map/ppermute | solution.py:325
  57.0 7.7 %collective-permute-start.17 = (bf16[32,128]{1,0:T(8,128)(2,1)S(1)}, bf16[32,128]{1,0:T(8,128)(2,1)S(1)}, u32[]{:S(2)}, u32[]{:S(2)}) collective-permute-start(bf16[32,128]{1,0:T(8,128)(2,1)S(1)} %get-tuple-element.40), channel_id=1, source_target_pairs={{0,8},{2,10},{4,12},{6,14},{8,0},{10,2},{12,4},{14,6},{1,9},{3,11}... | collective-permute-start | bytes 24584 | tf_op jit(solution)/shard_map/ppermute | solution.py:325
  58.7 5.9 %collective-permute-start.18 = (bf16[32,128]{1,0:T(8,128)(2,1)S(1)}, bf16[32,128]{1,0:T(8,128)(2,1)S(1)}, u32[]{:S(2)}, u32[]{:S(2)}) collective-permute-start(bf16[32,128]{1,0:T(8,128)(2,1)S(1)} %get-tuple-element.41), channel_id=1, source_target_pairs={{0,10},{2,8},{4,14},{6,12},{8,2},{10,0},{12,6},{14,4},{1,11},{3,9}... | collective-permute-start | bytes 24584 | tf_op jit(solution)/shard_map/ppermute | solution.py:325
  60.1 5.4 %collective-permute-start.19 = (bf16[32,128]{1,0:T(8,128)(2,1)S(1)}, bf16[32,128]{1,0:T(8,128)(2,1)S(1)}, u32[]{:S(2)}, u32[]{:S(2)}) collective-permute-start(bf16[32,128]{1,0:T(8,128)(2,1)S(1)} %get-tuple-element.42), channel_id=1, source_target_pairs={{0,12},{2,14},{4,8},{6,10},{8,4},{10,6},{12,0},{14,2},{1,13},{3,15... | collective-permute-start | bytes 24584 | tf_op jit(solution)/shard_map/ppermute | solution.py:325
  63.5 6.3 %collective-permute-start.20 = (bf16[32,128]{1,0:T(8,128)(2,1)S(1)}, bf16[32,128]{1,0:T(8,128)(2,1)S(1)}, u32[]{:S(2)}, u32[]{:S(2)}) collective-permute-start(bf16[32,128]{1,0:T(8,128)(2,1)S(1)} %get-tuple-element.43), channel_id=1, source_target_pairs={{0,14},{2,12},{4,10},{6,8},{8,6},{10,4},{12,2},{14,0},{1,15},{3,13... | collective-permute-start | bytes 24584 | tf_op jit(solution)/shard_map/ppermute | solution.py:325

commit v3 on v2

--- a/solution.py
+++ b/solution.py
@@ -167,23 +167,20 @@
 
 def dispatch_kernel(local_count, dev_count, *refs):
     sources, refs = refs[:6], refs[6:]
-    copy_ref, home_refs, refs = refs[0], refs[1:1 + dev_count], refs[1 + dev_count:]
-    pick_ref, expert_ref, hs_ref, ps_ref = refs[:4]
-    held, wide, sems = refs[4:10], refs[10], refs[11]
+    copy_ref, home_ref, pick_ref, expert_ref, hs_ref, ps_ref = refs[:6]
+    held, wide, sems = refs[6:12], refs[12], refs[13]
     moves = [pltpu.make_async_copy(s, h, sems.at[n]) for n, (s, h) in enumerate(zip(sources, held))]
     for move in moves:
         move.start()
     replica_ref, counts_ref, ids_ref, probs_ref, hid_ref, cot_ref = held
     top, toks = ids_ref.shape
     d_model = cot_ref.shape[1]
-    per_home = local_count * SLOT
-    homes = dev_count * per_home
+    homes = dev_count * local_count * SLOT
     slots = homes + dev_count * CAPR
-    me = lax.axis_index("expert")
     for move in moves[:3]:
         move.wait()
     row = iota((slots, toks), 0)
-    expert = ((row // per_home) ^ me) * local_count + (row % per_home) // SLOT
+    expert = row // SLOT
     within = row % SLOT
     allowed = jnp.where(within < CAPH, 1, 0)
     for d in range(dev_count):
@@ -225,9 +222,8 @@
     rows = jnp.dot(pick.astype(BF16), cot_ref[...], preferred_element_type=F32)
     copy_ref[:, :d_model] = rows[homes:].astype(BF16)
     copy_ref[:, d_model:] = scaled[homes:].astype(BF16)
-    for m, home_ref in enumerate(home_refs):
-        home_ref[:, :d_model] = rows[m * per_home:(m + 1) * per_home].astype(BF16)
-        home_ref[:, d_model:] = scaled[m * per_home:(m + 1) * per_home].astype(BF16)
+    home_ref[:, :d_model] = rows[:homes].astype(BF16)
+    home_ref[:, d_model:] = scaled[:homes].astype(BF16)
 
 
 def local_slots(local_count, dev_count, width, replica_ref):
@@ -241,24 +237,28 @@
     return jnp.concatenate([home] + [copy] * dev_count, axis=0)
 
 
-def grad_in_kernel(local_count, dev_count, replica_ref, w_ref, *refs):
-    home_refs, copy_refs, refs = refs[:dev_count], refs[dev_count:2 * dev_count], refs[2 * dev_count:]
-    rows_ref, back_refs = refs[0], refs[1:]
+def grad_in_kernel(local_count, dev_count, replica_ref, w_hbm, home_ref, *refs):
+    copy_refs, (rows_ref, back_ref, w_ref, passed, sem) = refs[:dev_count], refs[dev_count:]
+    fetch = pltpu.make_async_copy(w_hbm, w_ref, sem)
+    fetch.start()
     d_model = w_ref.shape[1]
     width = w_ref.shape[0] // local_count
     per_home, per_copy = local_count * SLOT, dev_count * CAPR
     homes = dev_count * per_home
-    rows_ref[:homes] = jnp.concatenate([r[...].astype(F32) for r in home_refs], axis=0).astype(BF16)
+    rows_ref[:homes] = home_ref[...]
     rows_ref[homes:] = jnp.concatenate([r[...].astype(F32) for r in copy_refs], axis=0).astype(BF16)
+    slot = local_slots(local_count, dev_count, width, replica_ref)
+    fetch.wait()
     every = lax.dot_general(rows_ref[:, :d_model], w_ref[...], NT, preferred_element_type=F32)
-    slot = local_slots(local_count, dev_count, width, replica_ref)
     own = jnp.zeros((rows_ref.shape[0], width), F32)
     for e in range(local_count):
         own = jnp.where(slot == e, every[:, e * width:(e + 1) * width], own)
-    for m, back_ref in enumerate(back_refs):
-        home = own[m * per_home:(m + 1) * per_home]
-        copy = own[homes + m * per_copy:homes + (m + 1) * per_copy]
-        back_ref[...] = jnp.concatenate([home, copy], axis=0).astype(back_ref.dtype)
+    passed[...] = own[homes:].reshape(passed.shape)
+    me = lax.axis_index("expert")
+    blocks = []
+    for source in range(dev_count):
+        blocks += [own[source * per_home:(source + 1) * per_home], passed[me ^ source]]
+    back_ref[...] = jnp.concatenate(blocks, axis=0).astype(back_ref.dtype)
 
 
 def grad_weights_half(local_count, dev_count, half, replica_ref, rows_ref, columns):
@@ -282,16 +282,14 @@
     out_ref[...] = (total + arrived_ref[...].astype(F32)).astype(out_ref.dtype)
 
 
-def combine_kernel(local_count, dev_count, *refs):
-    back_refs, refs = refs[:dev_count], refs[dev_count:]
-    pick_ref, expert_ref, hs_ref, ps_ref, ids_ref, grad_h_ref, grad_p_ref, wide, narrow = refs
+def combine_kernel(local_count, dev_count, back_ref, pick_ref, expert_ref, hs_ref, ps_ref, ids_ref,
+                   grad_h_ref, grad_p_ref, wide, narrow):
     top, toks = ids_ref.shape
-    per_home = local_count * SLOT
-    back = [r[...].astype(F32) for r in back_refs]
-    copy = back[0][per_home:]
-    for b in back[1:]:
-        copy = copy + b[per_home:]
-    grad_in = jnp.concatenate([b[:per_home] for b in back] + [copy], axis=0)
+    width = back_ref.shape[1]
+    per_home, per_copy = local_count * SLOT, dev_count * CAPR
+    back = back_ref[...].astype(F32).reshape(dev_count, per_home + per_copy, width)
+    home = back[:, :per_home].reshape(dev_count * per_home, width)
+    grad_in = jnp.concatenate([home, jnp.sum(back[:, per_home:], axis=0)], axis=0)
     h_rows = (ps_ref[...] * grad_in).astype(BF16)
     p_rows = jnp.sum(hs_ref[...] * grad_in, axis=1, keepdims=True)
     ids = ids_ref[...]
@@ -306,19 +304,18 @@
     grad_p_ref[...] = narrow[...].astype(grad_p_ref.dtype)
 
 
-def call(kernel, out_shape, smem, operands, scratch=(), flops=0, limit=24, space=pltpu.VMEM):
+def call(kernel, out_shape, operands, scratch=(), flops=0, limit=24):
     shapes = jax.tree.leaves(out_shape)
-    moved = sum(a.size * a.dtype.itemsize for a in (*operands, *shapes))
+    moved = sum(a.size * a.dtype.itemsize for a in (*(a for _, a in operands), *shapes))
     return pl.pallas_call(
         kernel,
         out_shape=out_shape,
-        in_specs=[pl.BlockSpec(memory_space=pltpu.SMEM)] * len(smem)
-        + [pl.BlockSpec(memory_space=space)] * len(operands),
+        in_specs=[pl.BlockSpec(memory_space=space) for space, _ in operands],
         out_specs=jax.tree.map(lambda _: pl.BlockSpec(memory_space=pltpu.VMEM), out_shape),
         scratch_shapes=list(scratch),
         compiler_params=pltpu.CompilerParams(vmem_limit_bytes=limit << 20),
         cost_estimate=pl.CostEstimate(flops=flops, bytes_accessed=moved, transcendentals=0),
-    )(*smem, *operands)
+    )(*(a for _, a in operands))
 
 
 def swap(x, bits, count):
@@ -331,67 +328,60 @@
     width = hidden.shape[2]
     local_count = weights.shape[0]
     dev_count = lax.axis_size("expert")
-    per_home = local_count * SLOT
-    homes = dev_count * per_home
+    homes = dev_count * local_count * SLOT
     copies = dev_count * CAPR
     slots = homes + copies
+    rows = homes + dev_count * copies
+    columns = d_model // 2
     sizes = (local_count, dev_count)
     ids = expert_ids.T
     shape = jax.ShapeDtypeStruct
+    hbm, vmem, smem = pltpu.HBM, pltpu.VMEM, pltpu.SMEM
     sources = (replica_of, send_counts, ids, probs.T, hidden.reshape(toks * top, width), cotangent)
-    copy_rows, *rest = call(
+    copy_rows, home_rows, pick, expert, h_slot, p_slot = call(
         functools.partial(dispatch_kernel, *sizes),
-        [shape((copies, d_model + width), BF16)]
-        + [shape((per_home, d_model + width), BF16)] * dev_count
-        + [shape((slots, toks), F32), shape((slots, toks), jnp.int32),
-           shape((slots, width), F32), shape((slots, width), F32)],
-        (),
-        sources,
-        [(pltpu.SMEM if n < 2 else pltpu.VMEM)(a.shape, a.dtype) for n, a in enumerate(sources)]
-        + [pltpu.VMEM((toks * top, width), F32), pltpu.SemaphoreType.DMA((len(sources),))],
+        (shape((copies, d_model + width), BF16), shape((homes, d_model + width), BF16), shape((slots, toks), F32),
+         shape((slots, toks), jnp.int32), shape((slots, width), F32), shape((slots, width), F32)),
+        [(hbm, a) for a in sources],
+        [(smem if n < 2 else vmem)(a.shape, a.dtype) for n, a in enumerate(sources)]
+        + [vmem((toks * top, width), F32), pltpu.SemaphoreType.DMA((len(sources),))],
         flops=2 * slots * toks * d_model,
-        limit=48,
-        space=pl.ANY,
-    )
-    home_rows, (pick, expert, h_slot, p_slot) = rest[:dev_count], rest[dev_count:]
+        limit=60,
+    )
     copy_in = [copy_rows] + [None] * (dev_count - 1)
     for m in sorted(range(1, dev_count), key=lambda m: (m.bit_count(), -m)):
         low = m & -m
         copy_in[m] = swap(copy_in[m ^ low], low, dev_count)
-    home_in = [home_rows[0]] + [swap(home_rows[m], m, dev_count) for m in range(1, dev_count)]
-    rows = homes + dev_count * copies
-    w_flat = weights.reshape(local_count * width, d_model)
-    all_rows, *back = call(
+    home_in = lax.all_to_all(home_rows, "expert", split_axis=0, concat_axis=0, tiled=True)
+    all_rows, back = call(
         functools.partial(grad_in_kernel, *sizes),
-        [shape((rows, d_model + width), BF16)] + [shape((per_home + copies, width), BF16)] * dev_count,
-        (replica_of,),
-        (w_flat, *home_in, *copy_in),
+        (shape((rows, d_model + width), BF16), shape((rows, width), BF16)),
+        [(smem, replica_of), (hbm, weights.reshape(local_count * width, d_model)), (vmem, home_in)]
+        + [(vmem, a) for a in copy_in],
+        [vmem((local_count * width, d_model), BF16), vmem((dev_count, copies, width), F32),
+         pltpu.SemaphoreType.DMA(())],
         flops=2 * rows * d_model * local_count * width,
     )
-    back = [back[0]] + [swap(back[m], m, dev_count) for m in range(1, dev_count)]
-    columns = d_model // 2
+    back = lax.all_to_all(back, "expert", split_axis=0, concat_axis=0, tiled=True)
     half_flops = 2 * rows * columns * local_count * width
     other = call(
         functools.partial(other_half_kernel, *sizes),
         shape((local_count * width, columns), BF16),
-        (replica_of,),
-        (all_rows,),
+        [(smem, replica_of), (vmem, all_rows)],
         flops=half_flops,
     )
     arrived = lax.ppermute(other, "dp", [(0, 1), (1, 0)])
     grad_h, grad_p = call(
         functools.partial(combine_kernel, *sizes),
         (shape((toks * top, width), BF16), shape((top, toks), BF16)),
-        (),
-        (*back, pick, expert, h_slot, p_slot, ids),
-        [pltpu.VMEM((toks * top, width), F32), pltpu.VMEM((top, toks), F32)],
+        [(vmem, a) for a in (back, pick, expert, h_slot, p_slot, ids)],
+        [vmem((toks * top, width), F32), vmem((top, toks), F32)],
         flops=2 * slots * toks * width * top,
     )
     grad_w = call(
         functools.partial(own_half_kernel, *sizes),
         shape((local_count * width, columns), BF16),
-        (replica_of,),
-        (all_rows, arrived),
+        [(smem, replica_of), (vmem, all_rows), (vmem, arrived)],
         flops=half_flops,
     )
     return (

time: 73.1 us -> 68.8 us (0.941)
  starting transfers between devices: 40.1 us -> 16.7 us
  blocking collectives: 0 us -> 11.8 us
  waiting for transfers between devices: 19 us -> 28.6 us
  local copies, waits for them, and re-layouts: 6.3 us -> 2.53 us
  Pallas kernels: 6.66 us -> 8.1 us
    ppermute x21 -> x7, starting transfers between devices: 40.1 us -> 9.34 us  [swap(): return lax.ppermute(x, 'expert', [(i, i ^ bits) for i in range(count)])]
    all_to_all x0 -> x1, blocking collectives: none -> 11.8 us  [gather_body(): lax.all_to_all(back, 'expert', split_axis=0, concat_axis=0, tiled=True)]
    ppermute x21 -> x7, waiting for transfers between devices: 19 us -> 28.6 us  [swap(): return lax.ppermute(x, 'expert', [(i, i ^ bits) for i in range(count)])]
    all_to_all x0 -> x1, starting transfers between devices: none -> 7.26 us  [gather_body(): lax.all_to_all(home_rows, 'expert', split_axis=0, concat_axis=0, tiled=True)]
    unnamed x14 -> x20, local copies, waits for them, and re-layouts: 6.3 us -> 2.53 us
    pallas_call x5, Pallas kernels: 6.66 us -> 8.1 us  [call(): pl.pallas_call(kernel, out_shape=out_shape, in_specs=[pl.BlockSpec(memory...]
  transfers between devices with their start and end apart: 22 -> 9, of which waited for: 7 -> 6; matrix products, arithmetic and copies ran while one was open for 0% -> 0% of each run, Pallas kernels for 1% -> 1%
where the time goes in v3:
time: 68.8 us; the launch traced here: 68.5 us
  waiting for transfers between devices  28.6 us (42%)
  starting transfers between devices  16.7 us (24%)
  blocking collectives  11.8 us (17%)
  Pallas kernels  8.1 us (12%)
  local copies, waits for them, and re-layouts  2.53 us (4%)
  between operations  0.76 us (1%)
    ppermute x7, waiting for transfers between devices, swap(): return lax.ppermute(x, 'expert', [(i, i ^ bits) for i in range(count)])  28.6 us
    all_to_all x1, blocking collectives, gather_body(): lax.all_to_all(back, 'expert', split_axis=0, concat_axis=0, tiled=True)  11.8 us
    ppermute x7, starting transfers between devices, swap(): return lax.ppermute(x, 'expert', [(i, i ^ bits) for i in range(count)])  9.34 us
    pallas_call x5, Pallas kernels, call(): pl.pallas_call(kernel, out_shape=out_shape, in_specs=[pl.BlockSpec(memory...  8.1 us
    all_to_all x1, starting transfers between devices, gather_body(): lax.all_to_all(home_rows, 'expert', split_axis=0, concat_axis=0, tiled=True)  7.26 us
    unnamed x20, local copies, waits for them, and re-layouts  2.53 us
  transfers between devices with their start and end apart: 9, of which 6 were waited for; matrix products, arithmetic and copies ran while one was open for 0% of the time, Pallas kernels for 1%

profile of v3, /device:TPU:0, one launch (start us, length us, event | category | flops | bytes accessed | tf_op | source)
XLA Modules:
  0.0 68.5 jit_solution(4768589191925862062)
XLA Ops:
  0.6 0.0 copy-start.9
  0.6 0.0 copy-start
  0.7 2.7 %shard_map.94 = (bf16[24,3712]{1,0:T(8,128)(2,1)}, bf16[64,3712]{1,0:T(8,128)(2,1)}, f32[88,128]{1,0:T(8,128)}, s32[88,128]{1,0:T(8,128)}, f32[88,128]{1,0:T(8,128)}, /*index=5*/f32[88,128]{1,0:T(8,128)}) custom-call(s32[8]{0:T(128)} %replica_ref.5, s32[1,8]{1,0:T(1,128)} %refs_1_.1, s32[8,128]{1,0:T(8,128)} %bitcast.15, bf16[8,128]{1,0:T(8,128)(2,1)} %bitcast.20, ...), custom_call_target="tpu_custom_call" | custom-call | flops 80740352 | bytes 2019392 | tf_op jit(solution)/shard_map/pallas_call | solution.py:310
  3.3 7.3 %all-to-all-start = ((bf16[8,8,3712]{2,1,0:T(8,128)(2,1)}), bf16[8,8,3712]{2,1,0:T(8,128)(2,1)S(1)}, u32[]{:S(2)}, u32[]{:S(2)}) async-start(bf16[8,8,3712]{2,1,0:T(8,128)(2,1)} %bitcast.18), calls=%async_computation | async-start | bytes 950272 | tf_op jit(solution)/shard_map/all_to_all | solution.py:355
  10.6 2.9 %collective-permute-start.3 = (bf16[24,3712]{1,0:T(8,128)(2,1)}, bf16[24,3712]{1,0:T(8,128)(2,1)S(1)}, u32[]{:S(2)}, u32[]{:S(2)}) collective-permute-start(bf16[24,3712]{1,0:T(8,128)(2,1)} %get-tuple-element.14.refs_0_), channel_id=1, source_target_pairs={{0,8},{2,10},{4,12},{6,14},{8,0},{10,2},{12,4},{14,6},{1,9},{3,11}... | collective-permute-start | bytes 534536 | tf_op jit(solution)/shard_map/ppermute | solution.py:322
  13.5 1.5 %collective-permute-start.1 = (bf16[24,3712]{1,0:T(8,128)(2,1)}, bf16[24,3712]{1,0:T(8,128)(2,1)S(1)}, u32[]{:S(2)}, u32[]{:S(2)}) collective-permute-start(bf16[24,3712]{1,0:T(8,128)(2,1)} %get-tuple-element.14.refs_0_), channel_id=1, source_target_pairs={{0,4},{2,6},{4,0},{6,2},{8,12},{10,14},{12,8},{14,10},{1,5},{3,7},... | collective-permute-start | bytes 534536 | tf_op jit(solution)/shard_map/ppermute | solution.py:322
  15.0 16.7 %collective-permute-done.3.refs_4_ = bf16[24,3712]{1,0:T(8,128)(2,1)S(1)} collective-permute-done((bf16[24,3712]{1,0:T(8,128)(2,1)}, bf16[24,3712]{1,0:T(8,128)(2,1)S(1)}, u32[]{:S(2)}, u32[]{:S(2)}) %collective-permute-start.3) | collective-permute-done | bytes 178208 | tf_op jit(solution)/shard_map/ppermute | solution.py:322
  31.7 0.0 collective-permute-start.5
  31.7 1.5 %collective-permute-start = (bf16[24,3712]{1,0:T(8,128)(2,1)}, bf16[24,3712]{1,0:T(8,128)(2,1)S(1)}, u32[]{:S(2)}, u32[]{:S(2)}) collective-permute-start(bf16[24,3712]{1,0:T(8,128)(2,1)} %get-tuple-element.14.refs_0_), channel_id=1, source_target_pairs={{0,2},{2,0},{4,6},{6,4},{8,10},{10,8},{12,14},{14,12},{1,3},{3,1},... | collective-permute-start | bytes 534536 | tf_op jit(solution)/shard_map/ppermute | solution.py:322
  33.1 0.6 collective-permute-start.4
  33.7 0.0 collective-permute-done.1.refs_2_
  33.7 1.5 %collective-permute-start.2 = (bf16[24,3712]{1,0:T(8,128)(2,1)S(1)}, bf16[24,3712]{1,0:T(8,128)(2,1)S(1)}, u32[]{:S(2)}, u32[]{:S(2)}) collective-permute-start(bf16[24,3712]{1,0:T(8,128)(2,1)S(1)} %collective-permute-done.1.refs_2_), channel_id=1, source_target_pairs={{0,2},{2,0},{4,6},{6,4},{8,10},{10,8},{12,14},{14,12},{1,3},{3,1},... | collective-permute-start | bytes 534536 | tf_op jit(solution)/shard_map/ppermute | solution.py:322
  35.2 2.0 %collective-permute-done.5.refs_6_ = bf16[24,3712]{1,0:T(8,128)(2,1)S(1)} collective-permute-done((bf16[24,3712]{1,0:T(8,128)(2,1)S(1)}, bf16[24,3712]{1,0:T(8,128)(2,1)S(1)}, u32[]{:S(2)}, u32[]{:S(2)}) %collective-permute-start.5) | collective-permute-done | bytes 178208 | tf_op jit(solution)/shard_map/ppermute | solution.py:322
  37.2 1.5 %collective-permute-start.6 = (bf16[24,3712]{1,0:T(8,128)(2,1)S(1)}, bf16[24,3712]{1,0:T(8,128)(2,1)S(1)}, u32[]{:S(2)}, u32[]{:S(2)}) collective-permute-start(bf16[24,3712]{1,0:T(8,128)(2,1)S(1)} %collective-permute-done.5.refs_6_), channel_id=1, source_target_pairs={{0,2},{2,0},{4,6},{6,4},{8,10},{10,8},{12,14},{14,12},{1,3},{3,1},... | collective-permute-start | bytes 534536 | tf_op jit(solution)/shard_map/ppermute | solution.py:322
  38.6 0.7 %collective-permute-done.refs_1_ = bf16[24,3712]{1,0:T(8,128)(2,1)S(1)} collective-permute-done((bf16[24,3712]{1,0:T(8,128)(2,1)}, bf16[24,3712]{1,0:T(8,128)(2,1)S(1)}, u32[]{:S(2)}, u32[]{:S(2)}) %collective-permute-start) | collective-permute-done | bytes 178208 | tf_op jit(solution)/shard_map/ppermute | solution.py:322
  39.3 3.8 %collective-permute-done.4.refs_5_ = bf16[24,3712]{1,0:T(8,128)(2,1)S(1)} collective-permute-done((bf16[24,3712]{1,0:T(8,128)(2,1)S(1)}, bf16[24,3712]{1,0:T(8,128)(2,1)S(1)}, u32[]{:S(2)}, u32[]{:S(2)}) %collective-permute-start.4) | collective-permute-done | bytes 178208 | tf_op jit(solution)/shard_map/ppermute | solution.py:322
  43.2 3.5 %collective-permute-done.2.refs_3_ = bf16[24,3712]{1,0:T(8,128)(2,1)S(1)} collective-permute-done((bf16[24,3712]{1,0:T(8,128)(2,1)S(1)}, bf16[24,3712]{1,0:T(8,128)(2,1)S(1)}, u32[]{:S(2)}, u32[]{:S(2)}) %collective-permute-start.2) | collective-permute-done | bytes 178208 | tf_op jit(solution)/shard_map/ppermute | solution.py:322
  46.6 1.9 %collective-permute-done.6.refs_7_ = bf16[24,3712]{1,0:T(8,128)(2,1)S(1)} collective-permute-done((bf16[24,3712]{1,0:T(8,128)(2,1)S(1)}, bf16[24,3712]{1,0:T(8,128)(2,1)S(1)}, u32[]{:S(2)}, u32[]{:S(2)}) %collective-permute-start.6) | collective-permute-done | bytes 178208 | tf_op jit(solution)/shard_map/ppermute | solution.py:322
  48.5 0.0 copy-start.2
  48.5 0.7 copy-done.2
  49.2 0.0 all-to-all-done
  49.2 0.0 copy-done.9
  49.2 0.0 copy-done
  49.2 0.0 copy-start.1
  49.2 0.9 %copy-done.1 = bf16[24,3712]{1,0:T(8,128)(2,1)S(1)} copy-done((bf16[24,3712]{1,0:T(8,128)(2,1)S(1)}, bf16[24,3712]{1,0:T(8,128)(2,1)}, u32[]{:S(2)}) %copy-start.1) | copy-done | bytes 178200
  50.1 0.0 copy-start.3
  50.1 0.9 %copy-done.3 = bf16[24,3712]{1,0:T(8,128)(2,1)S(1)} copy-done((bf16[24,3712]{1,0:T(8,128)(2,1)S(1)}, bf16[24,3712]{1,0:T(8,128)(2,1)}, u32[]{:S(2)}) %copy-start.3) | copy-done | bytes 178200
  51.1 1.5 %shard_map.95 = (bf16[256,3712]{1,0:T(8,128)(2,1)S(1)}, bf16[256,128]{1,0:T(8,128)(2,1)S(1)}) custom-call(s32[8]{0:T(128)S(1)} %copy-done.9, bf16[256,3584]{1,0:T(8,128)(2,1)S(1)} %bitcast.12, bf16[64,3712]{1,0:T(8,128)(2,1)S(1)} %bitcast.11, bf16[24,3712]{1,0:T(8,128)(2,1)S(1)} %copy-done.1, bf16[24,3712]{1,0:T(8,128)(2,1)S(1)} %collective-permute-done.refs_1_, ...), custom_call_target="tpu_custom_call" | custom-call | flops 469762048 | bytes 5701664 | tf_op jit(solution)/shard_map/pallas_call | solution.py:310
  52.5 0.0 copy-start.4
  52.5 0.0 copy-start.5
  52.6 0.0 copy-start.6
  52.6 0.0 copy-start.7
  52.6 0.0 copy-start.8
  52.6 1.0 %shard_map.97 = bf16[256,1792]{1,0:T(8,128)(2,1)S(1)} custom-call(s32[8]{0:T(128)S(1)} %copy-done.9, bf16[256,3712]{1,0:T(8,128)(2,1)S(1)} %get-tuple-element.22.rows_ref), custom_call_target="tpu_custom_call" | custom-call | flops 234881024 | bytes 2818080 | tf_op jit(solution)/shard_map/pallas_call | solution.py:310
  53.6 0.1 collective-permute-start.7
  53.7 11.8 %all_to_all.22 = bf16[8,32,128]{2,1,0:T(8,128)(2,1)S(1)} all-to-all(bf16[8,32,128]{2,1,0:T(8,128)(2,1)S(1)} %bitcast.14), channel_id=1, replica_groups=mesh['groups'=2,'expert'=8,'dp'=2] {'expert'}, dimensions={0} | all-to-all | bytes 131072 | tf_op jit(solution)/shard_map/all_to_all | solution.py:365
  65.5 0.0 copy-done.4
  65.5 0.0 copy-done.5
  65.5 0.0 copy-done.6
  65.5 0.0 copy-done.7
  65.5 0.0 copy-done.8
  65.5 1.0 %shard_map.96 = (bf16[1024,128]{1,0:T(8,128)(2,1)}, bf16[8,128]{1,0:T(8,128)(2,1)}) custom-call(bf16[256,128]{1,0:T(8,128)(2,1)S(1)} %bitcast.13, f32[88,128]{1,0:T(8,128)S(1)} %copy-done.4, s32[88,128]{1,0:T(8,128)S(1)} %copy-done.5, f32[88,128]{1,0:T(8,128)S(1)} %copy-done.6, f32[88,128]{1,0:T(8,128)S(1)} %copy-done.7, s32[8,128]{1,0:T(8,128)S(1)} %bitcast.16), custom_call_target="tpu_custom_call" | custom-call | flops 23068672 | bytes 514048 | tf_op jit(solution)/shard_map/pallas_call | solution.py:310
  66.5 0.0 collective-permute-done.7.arrived_ref
  66.5 1.9 %shard_map.98 = bf16[256,1792]{1,0:T(8,128)(2,1)} custom-call(s32[8]{0:T(128)S(1)} %copy-done.9, bf16[256,3712]{1,0:T(8,128)(2,1)S(1)} %get-tuple-element.22.rows_ref, bf16[256,1792]{1,0:T(8,128)(2,1)S(1)} %collective-permute-done.7.arrived_ref), custom_call_target="tpu_custom_call" | custom-call | flops 234881024 | bytes 3735584 | tf_op jit(solution)/shard_map/pallas_call | solution.py:310
Async XLA Ops:
  0.6 48.6 %copy-start.9 = (s32[8]{0:T(128)S(1)}, s32[8]{0:T(128)}, u32[]{:S(2)}) copy-start(s32[8]{0:T(128)} %replica_ref.5) | copy-start | bytes 100
  0.6 48.6 %copy-start = (bf16[2,128,3584]{2,1,0:T(8,128)(2,1)S(1)}, bf16[2,128,3584]{2,1,0:T(8,128)(2,1)}, u32[]{:S(2)}) copy-start(bf16[2,128,3584]{2,1,0:T(8,128)(2,1)} %param.13) | copy-start | bytes 5505028
  3.3 45.9 %all-to-all-start = ((bf16[8,8,3712]{2,1,0:T(8,128)(2,1)}), bf16[8,8,3712]{2,1,0:T(8,128)(2,1)S(1)}, u32[]{:S(2)}, u32[]{:S(2)}) async-start(bf16[8,8,3712]{2,1,0:T(8,128)(2,1)} %bitcast.18), calls=%async_computation | async-start | bytes 950272 | tf_op jit(solution)/shard_map/all_to_all | solution.py:355
  10.6 21.1 %collective-permute-start.3 = (bf16[24,3712]{1,0:T(8,128)(2,1)}, bf16[24,3712]{1,0:T(8,128)(2,1)S(1)}, u32[]{:S(2)}, u32[]{:S(2)}) collective-permute-start(bf16[24,3712]{1,0:T(8,128)(2,1)} %get-tuple-element.14.refs_0_), channel_id=1, source_target_pairs={{0,8},{2,10},{4,12},{6,14},{8,0},{10,2},{12,4},{14,6},{1,9},{3,11}... | collective-permute-start | bytes 534536 | tf_op jit(solution)/shard_map/ppermute | solution.py:322
  13.5 20.2 %collective-permute-start.1 = (bf16[24,3712]{1,0:T(8,128)(2,1)}, bf16[24,3712]{1,0:T(8,128)(2,1)S(1)}, u32[]{:S(2)}, u32[]{:S(2)}) collective-permute-start(bf16[24,3712]{1,0:T(8,128)(2,1)} %get-tuple-element.14.refs_0_), channel_id=1, source_target_pairs={{0,4},{2,6},{4,0},{6,2},{8,12},{10,14},{12,8},{14,10},{1,5},{3,7},... | collective-permute-start | bytes 534536 | tf_op jit(solution)/shard_map/ppermute | solution.py:322
  31.7 5.5 %collective-permute-start.5 = (bf16[24,3712]{1,0:T(8,128)(2,1)S(1)}, bf16[24,3712]{1,0:T(8,128)(2,1)S(1)}, u32[]{:S(2)}, u32[]{:S(2)}) collective-permute-start(bf16[24,3712]{1,0:T(8,128)(2,1)S(1)} %collective-permute-done.3.refs_4_), channel_id=1, source_target_pairs={{0,4},{2,6},{4,0},{6,2},{8,12},{10,14},{12,8},{14,10},{1,5},{3,7},... | collective-permute-start | bytes 534536 | tf_op jit(solution)/shard_map/ppermute | solution.py:322
  31.7 7.7 %collective-permute-start = (bf16[24,3712]{1,0:T(8,128)(2,1)}, bf16[24,3712]{1,0:T(8,128)(2,1)S(1)}, u32[]{:S(2)}, u32[]{:S(2)}) collective-permute-start(bf16[24,3712]{1,0:T(8,128)(2,1)} %get-tuple-element.14.refs_0_), channel_id=1, source_target_pairs={{0,2},{2,0},{4,6},{6,4},{8,10},{10,8},{12,14},{14,12},{1,3},{3,1},... | collective-permute-start | bytes 534536 | tf_op jit(solution)/shard_map/ppermute | solution.py:322
  33.1 10.0 %collective-permute-start.4 = (bf16[24,3712]{1,0:T(8,128)(2,1)S(1)}, bf16[24,3712]{1,0:T(8,128)(2,1)S(1)}, u32[]{:S(2)}, u32[]{:S(2)}) collective-permute-start(bf16[24,3712]{1,0:T(8,128)(2,1)S(1)} %collective-permute-done.3.refs_4_), channel_id=1, source_target_pairs={{0,2},{2,0},{4,6},{6,4},{8,10},{10,8},{12,14},{14,12},{1,3},{3,1},... | collective-permute-start | bytes 534536 | tf_op jit(solution)/shard_map/ppermute | solution.py:322
  33.7 12.9 %collective-permute-start.2 = (bf16[24,3712]{1,0:T(8,128)(2,1)S(1)}, bf16[24,3712]{1,0:T(8,128)(2,1)S(1)}, u32[]{:S(2)}, u32[]{:S(2)}) collective-permute-start(bf16[24,3712]{1,0:T(8,128)(2,1)S(1)} %collective-permute-done.1.refs_2_), channel_id=1, source_target_pairs={{0,2},{2,0},{4,6},{6,4},{8,10},{10,8},{12,14},{14,12},{1,3},{3,1},... | collective-permute-start | bytes 534536 | tf_op jit(solution)/shard_map/ppermute | solution.py:322
  37.2 11.4 %collective-permute-start.6 = (bf16[24,3712]{1,0:T(8,128)(2,1)S(1)}, bf16[24,3712]{1,0:T(8,128)(2,1)S(1)}, u32[]{:S(2)}, u32[]{:S(2)}) collective-permute-start(bf16[24,3712]{1,0:T(8,128)(2,1)S(1)} %collective-permute-done.5.refs_6_), channel_id=1, source_target_pairs={{0,2},{2,0},{4,6},{6,4},{8,10},{10,8},{12,14},{14,12},{1,3},{3,1},... | collective-permute-start | bytes 534536 | tf_op jit(solution)/shard_map/ppermute | solution.py:322
  48.5 0.7 copy-start.2
  49.2 0.9 %copy-start.1 = (bf16[24,3712]{1,0:T(8,128)(2,1)S(1)}, bf16[24,3712]{1,0:T(8,128)(2,1)}, u32[]{:S(2)}) copy-start(bf16[24,3712]{1,0:T(8,128)(2,1)} %get-tuple-element.14.refs_0_) | copy-start | bytes 534532
  50.1 0.9 %copy-start.3 = (bf16[24,3712]{1,0:T(8,128)(2,1)S(1)}, bf16[24,3712]{1,0:T(8,128)(2,1)}, u32[]{:S(2)}) copy-start(bf16[24,3712]{1,0:T(8,128)(2,1)} %copy-done.2) | copy-start | bytes 534532
  52.5 13.0 %copy-start.4 = (f32[88,128]{1,0:T(8,128)S(1)}, f32[88,128]{1,0:T(8,128)}, u32[]{:S(2)}) copy-start(f32[88,128]{1,0:T(8,128)} %get-tuple-element.16.pick_ref) | copy-start | bytes 135172
  52.5 13.0 %copy-start.5 = (s32[88,128]{1,0:T(8,128)S(1)}, s32[88,128]{1,0:T(8,128)}, u32[]{:S(2)}) copy-start(s32[88,128]{1,0:T(8,128)} %get-tuple-element.17.expert_ref) | copy-start | bytes 135172
  52.6 13.0 %copy-start.6 = (f32[88,128]{1,0:T(8,128)S(1)}, f32[88,128]{1,0:T(8,128)}, u32[]{:S(2)}) copy-start(f32[88,128]{1,0:T(8,128)} %get-tuple-element.18.hs_ref) | copy-start | bytes 135172
  52.6 13.0 %copy-start.7 = (f32[88,128]{1,0:T(8,128)S(1)}, f32[88,128]{1,0:T(8,128)}, u32[]{:S(2)}) copy-start(f32[88,128]{1,0:T(8,128)} %get-tuple-element.19.ps_ref) | copy-start | bytes 135172
  52.6 13.0 %copy-start.8 = (s32[128,8]{0,1:T(8,128)S(1)}, s32[128,8]{0,1:T(8,128)}, u32[]{:S(2)}) copy-start(s32[128,8]{0,1:T(8,128)} %param.10) | copy-start | bytes 12292
  53.6 12.9 %collective-permute-start.7 = (bf16[256,1792]{1,0:T(8,128)(2,1)S(1)}, bf16[256,1792]{1,0:T(8,128)(2,1)S(1)}, u32[]{:S(2)}, u32[]{:S(2)}) collective-permute-start(bf16[256,1792]{1,0:T(8,128)(2,1)S(1)} %shard_map.97), channel_id=1, source_target_pairs={{0,1},{1,0},{2,3},{3,2},{4,5},{5,4},{6,7},{7,6},{8,9},{9,8},{10,11... | collective-permute-start | bytes 2752520 | tf_op jit(solution)/shard_map/ppermute | solution.py:373

commit v4 on v3

--- a/solution.py
+++ b/solution.py
@@ -348,16 +348,20 @@
         flops=2 * slots * toks * d_model,
         limit=60,
     )
-    copy_in = [copy_rows] + [None] * (dev_count - 1)
+    copy_in = {0: copy_rows}
+    for bits in reversed(range(dev_count.bit_length() - 1)):
+        copy_in[1 << bits] = swap(copy_rows, 1 << bits, dev_count)
+    copy_in, home_rows = lax.optimization_barrier((copy_in, home_rows))
     for m in sorted(range(1, dev_count), key=lambda m: (m.bit_count(), -m)):
         low = m & -m
-        copy_in[m] = swap(copy_in[m ^ low], low, dev_count)
+        if m != low:
+            copy_in[m] = swap(copy_in[m ^ low], low, dev_count)
     home_in = lax.all_to_all(home_rows, "expert", split_axis=0, concat_axis=0, tiled=True)
     all_rows, back = call(
         functools.partial(grad_in_kernel, *sizes),
         (shape((rows, d_model + width), BF16), shape((rows, width), BF16)),
         [(smem, replica_of), (hbm, weights.reshape(local_count * width, d_model)), (vmem, home_in)]
-        + [(vmem, a) for a in copy_in],
+        + [(vmem, copy_in[m]) for m in range(dev_count)],
         [vmem((local_count * width, d_model), BF16), vmem((dev_count, copies, width), F32),
          pltpu.SemaphoreType.DMA(())],
         flops=2 * rows * d_model * local_count * width,

time: 68.8 us -> 61.1 us (0.89)
  waiting for transfers between devices: 28.6 us -> 19.9 us
  starting transfers between devices: 16.7 us -> 18.2 us
    ppermute x7, waiting for transfers between devices: 28.6 us -> 19.9 us  [swap(): return lax.ppermute(x, 'expert', [(i, i ^ bits) for i in range(count)])]
    ppermute x7, starting transfers between devices: 9.34 us -> 12.7 us  [swap(): return lax.ppermute(x, 'expert', [(i, i ^ bits) for i in range(count)])]
    all_to_all x1, starting transfers between devices: 7.26 us -> 5.44 us  [gather_body(): lax.all_to_all(home_rows, 'expert', split_axis=0, concat_axis=0, tiled=True)]
  transfers between devices with their start and end apart: 9 -> 9, of which waited for: 6 -> 5; matrix products, arithmetic and copies ran while one was open for 0% -> 0% of each run, Pallas kernels for 1% -> 2%
where the time goes in v4:
time: 61.1 us; the launch traced here: 60.8 us
  waiting for transfers between devices  19.9 us (33%)
  starting transfers between devices  18.2 us (30%)
  blocking collectives  11.3 us (18%)
  Pallas kernels  8.1 us (13%)
  local copies, waits for them, and re-layouts  2.53 us (4%)
  between operations  0.76 us (1%)
    ppermute x7, waiting for transfers between devices, swap(): return lax.ppermute(x, 'expert', [(i, i ^ bits) for i in range(count)])  19.9 us
    ppermute x7, starting transfers between devices, swap(): return lax.ppermute(x, 'expert', [(i, i ^ bits) for i in range(count)])  12.7 us
    all_to_all x1, blocking collectives, gather_body(): lax.all_to_all(back, 'expert', split_axis=0, concat_axis=0, tiled=True)  11.3 us
    pallas_call x5, Pallas kernels, call(): pl.pallas_call(kernel, out_shape=out_shape, in_specs=[pl.BlockSpec(memory...  8.1 us
    all_to_all x1, starting transfers between devices, gather_body(): lax.all_to_all(home_rows, 'expert', split_axis=0, concat_axis=0, tiled=True)  5.44 us
    unnamed x20, local copies, waits for them, and re-layouts  2.53 us
  transfers between devices with their start and end apart: 9, of which 5 were waited for; matrix products, arithmetic and copies ran while one was open for 0% of the time, Pallas kernels for 2%

profile of v4, /device:TPU:0, one launch (start us, length us, event | category | flops | bytes accessed | tf_op | source)
XLA Modules:
  0.0 60.8 jit_solution(2752063817200676409)
XLA Ops:
  0.6 0.0 copy-start.9
  0.6 0.0 copy-start
  0.7 2.7 %shard_map.94 = (bf16[24,3712]{1,0:T(8,128)(2,1)}, bf16[64,3712]{1,0:T(8,128)(2,1)}, f32[88,128]{1,0:T(8,128)}, s32[88,128]{1,0:T(8,128)}, f32[88,128]{1,0:T(8,128)}, /*index=5*/f32[88,128]{1,0:T(8,128)}) custom-call(s32[8]{0:T(128)} %replica_ref.5, s32[1,8]{1,0:T(1,128)} %refs_1_.1, s32[8,128]{1,0:T(8,128)} %bitcast.15, bf16[8,128]{1,0:T(8,128)(2,1)} %bitcast.20, ...), custom_call_target="tpu_custom_call" | custom-call | flops 80740352 | bytes 2019392 | tf_op jit(solution)/shard_map/pallas_call | solution.py:310
  3.3 4.1 %collective-permute-start.2 = (bf16[24,3712]{1,0:T(8,128)(2,1)}, bf16[24,3712]{1,0:T(8,128)(2,1)S(1)}, u32[]{:S(2)}, u32[]{:S(2)}) collective-permute-start(bf16[24,3712]{1,0:T(8,128)(2,1)} %get-tuple-element.21.refs_0_), channel_id=1, source_target_pairs={{0,8},{2,10},{4,12},{6,14},{8,0},{10,2},{12,4},{14,6},{1,9},{3,11}... | collective-permute-start | bytes 534536 | tf_op jit(solution)/shard_map/ppermute | solution.py:322
  7.4 1.6 %collective-permute-start.1 = (bf16[24,3712]{1,0:T(8,128)(2,1)}, bf16[24,3712]{1,0:T(8,128)(2,1)S(1)}, u32[]{:S(2)}, u32[]{:S(2)}) collective-permute-start(bf16[24,3712]{1,0:T(8,128)(2,1)} %get-tuple-element.21.refs_0_), channel_id=1, source_target_pairs={{0,4},{2,6},{4,0},{6,2},{8,12},{10,14},{12,8},{14,10},{1,5},{3,7},... | collective-permute-start | bytes 534536 | tf_op jit(solution)/shard_map/ppermute | solution.py:322
  9.0 1.5 %collective-permute-start = (bf16[24,3712]{1,0:T(8,128)(2,1)}, bf16[24,3712]{1,0:T(8,128)(2,1)S(1)}, u32[]{:S(2)}, u32[]{:S(2)}) collective-permute-start(bf16[24,3712]{1,0:T(8,128)(2,1)} %get-tuple-element.21.refs_0_), channel_id=1, source_target_pairs={{0,2},{2,0},{4,6},{6,4},{8,10},{10,8},{12,14},{14,12},{1,3},{3,1},... | collective-permute-start | bytes 534536 | tf_op jit(solution)/shard_map/ppermute | solution.py:322
  10.5 5.6 %collective-permute-done.2.refs_4_ = bf16[24,3712]{1,0:T(8,128)(2,1)S(1)} collective-permute-done((bf16[24,3712]{1,0:T(8,128)(2,1)}, bf16[24,3712]{1,0:T(8,128)(2,1)S(1)}, u32[]{:S(2)}, u32[]{:S(2)}) %collective-permute-start.2) | collective-permute-done | bytes 178208 | tf_op jit(solution)/shard_map/ppermute | solution.py:322
  16.1 0.2 collective-permute-done.1.refs_2_
  16.3 0.0 collective-permute-done.refs_1_
  16.3 5.4 %all-to-all-start = ((bf16[8,8,3712]{2,1,0:T(8,128)(2,1)}), bf16[8,8,3712]{2,1,0:T(8,128)(2,1)S(1)}, u32[]{:S(2)}, u32[]{:S(2)}) async-start(bf16[8,8,3712]{2,1,0:T(8,128)(2,1)} %bitcast.18), calls=%async_computation | async-start | bytes 950272 | tf_op jit(solution)/shard_map/all_to_all | solution.py:359
  21.7 2.0 %collective-permute-start.5 = (bf16[24,3712]{1,0:T(8,128)(2,1)S(1)}, bf16[24,3712]{1,0:T(8,128)(2,1)S(1)}, u32[]{:S(2)}, u32[]{:S(2)}) collective-permute-start(bf16[24,3712]{1,0:T(8,128)(2,1)S(1)} %collective-permute-done.2.refs_4_), channel_id=1, source_target_pairs={{0,4},{2,6},{4,0},{6,2},{8,12},{10,14},{12,8},{14,10},{1,5},{3,7},... | collective-permute-start | bytes 534536 | tf_op jit(solution)/shard_map/ppermute | solution.py:322
  23.8 1.5 %collective-permute-start.4 = (bf16[24,3712]{1,0:T(8,128)(2,1)S(1)}, bf16[24,3712]{1,0:T(8,128)(2,1)S(1)}, u32[]{:S(2)}, u32[]{:S(2)}) collective-permute-start(bf16[24,3712]{1,0:T(8,128)(2,1)S(1)} %collective-permute-done.2.refs_4_), channel_id=1, source_target_pairs={{0,2},{2,0},{4,6},{6,4},{8,10},{10,8},{12,14},{14,12},{1,3},{3,1},... | collective-permute-start | bytes 534536 | tf_op jit(solution)/shard_map/ppermute | solution.py:322
  25.2 0.6 collective-permute-start.3
  25.8 9.9 %collective-permute-done.5.refs_6_ = bf16[24,3712]{1,0:T(8,128)(2,1)S(1)} collective-permute-done((bf16[24,3712]{1,0:T(8,128)(2,1)S(1)}, bf16[24,3712]{1,0:T(8,128)(2,1)S(1)}, u32[]{:S(2)}, u32[]{:S(2)}) %collective-permute-start.5) | collective-permute-done | bytes 178208 | tf_op jit(solution)/shard_map/ppermute | solution.py:322
  35.7 1.5 %collective-permute-start.6 = (bf16[24,3712]{1,0:T(8,128)(2,1)S(1)}, bf16[24,3712]{1,0:T(8,128)(2,1)S(1)}, u32[]{:S(2)}, u32[]{:S(2)}) collective-permute-start(bf16[24,3712]{1,0:T(8,128)(2,1)S(1)} %collective-permute-done.5.refs_6_), channel_id=1, source_target_pairs={{0,2},{2,0},{4,6},{6,4},{8,10},{10,8},{12,14},{14,12},{1,3},{3,1},... | collective-permute-start | bytes 534536 | tf_op jit(solution)/shard_map/ppermute | solution.py:322
  37.2 1.0 %collective-permute-done.3.refs_3_ = bf16[24,3712]{1,0:T(8,128)(2,1)S(1)} collective-permute-done((bf16[24,3712]{1,0:T(8,128)(2,1)S(1)}, bf16[24,3712]{1,0:T(8,128)(2,1)S(1)}, u32[]{:S(2)}, u32[]{:S(2)}) %collective-permute-start.3) | collective-permute-done | bytes 178208 | tf_op jit(solution)/shard_map/ppermute | solution.py:322
  38.2 0.0 collective-permute-done.4.refs_5_
  38.2 3.2 %collective-permute-done.6.refs_7_ = bf16[24,3712]{1,0:T(8,128)(2,1)S(1)} collective-permute-done((bf16[24,3712]{1,0:T(8,128)(2,1)S(1)}, bf16[24,3712]{1,0:T(8,128)(2,1)S(1)}, u32[]{:S(2)}, u32[]{:S(2)}) %collective-permute-start.6) | collective-permute-done | bytes 178208 | tf_op jit(solution)/shard_map/ppermute | solution.py:322
  41.4 0.0 copy-start.2
  41.4 0.7 %copy-done.2 = bf16[24,3712]{1,0:T(8,128)(2,1)} copy-done((bf16[24,3712]{1,0:T(8,128)(2,1)}, bf16[24,3712]{1,0:T(8,128)(2,1)S(1)}, u32[]{:S(2)}) %copy-start.2) | copy-done | bytes 178200
  42.1 0.0 all-to-all-done
  42.1 0.0 copy-done.9
  42.1 0.0 copy-done
  42.1 0.0 copy-start.1
  42.1 0.9 %copy-done.1 = bf16[24,3712]{1,0:T(8,128)(2,1)S(1)} copy-done((bf16[24,3712]{1,0:T(8,128)(2,1)S(1)}, bf16[24,3712]{1,0:T(8,128)(2,1)}, u32[]{:S(2)}) %copy-start.1) | copy-done | bytes 178200
  43.0 0.0 copy-start.3
  43.0 0.9 %copy-done.3 = bf16[24,3712]{1,0:T(8,128)(2,1)S(1)} copy-done((bf16[24,3712]{1,0:T(8,128)(2,1)S(1)}, bf16[24,3712]{1,0:T(8,128)(2,1)}, u32[]{:S(2)}) %copy-start.3) | copy-done | bytes 178200
  43.9 1.5 %shard_map.95 = (bf16[256,3712]{1,0:T(8,128)(2,1)S(1)}, bf16[256,128]{1,0:T(8,128)(2,1)S(1)}) custom-call(s32[8]{0:T(128)S(1)} %copy-done.9, bf16[256,3584]{1,0:T(8,128)(2,1)S(1)} %bitcast.12, bf16[64,3712]{1,0:T(8,128)(2,1)S(1)} %bitcast.11, bf16[24,3712]{1,0:T(8,128)(2,1)S(1)} %copy-done.1, bf16[24,3712]{1,0:T(8,128)(2,1)S(1)} %collective-permute-done.refs_1_, ...), custom_call_target="tpu_custom_call" | custom-call | flops 469762048 | bytes 5701664 | tf_op jit(solution)/shard_map/pallas_call | solution.py:310
  45.4 0.0 copy-start.4
  45.4 0.0 copy-start.5
  45.4 0.0 copy-start.6
  45.4 0.0 copy-start.7
  45.4 0.0 copy-start.8
  45.5 1.0 %shard_map.97 = bf16[256,1792]{1,0:T(8,128)(2,1)S(1)} custom-call(s32[8]{0:T(128)S(1)} %copy-done.9, bf16[256,3712]{1,0:T(8,128)(2,1)S(1)} %get-tuple-element.32.rows_ref), custom_call_target="tpu_custom_call" | custom-call | flops 234881024 | bytes 2818080 | tf_op jit(solution)/shard_map/pallas_call | solution.py:310
  46.5 0.1 collective-permute-start.7
  46.5 11.3 %all_to_all.22 = bf16[8,32,128]{2,1,0:T(8,128)(2,1)S(1)} all-to-all(bf16[8,32,128]{2,1,0:T(8,128)(2,1)S(1)} %bitcast.14), channel_id=1, replica_groups=mesh['groups'=2,'expert'=8,'dp'=2] {'expert'}, dimensions={0} | all-to-all | bytes 131072 | tf_op jit(solution)/shard_map/all_to_all | solution.py:369
  57.9 0.0 copy-done.4
  57.9 0.0 copy-done.5
  57.9 0.0 copy-done.6
  57.9 0.0 copy-done.7
  57.9 0.0 copy-done.8
  57.9 1.0 %shard_map.96 = (bf16[1024,128]{1,0:T(8,128)(2,1)}, bf16[8,128]{1,0:T(8,128)(2,1)}) custom-call(bf16[256,128]{1,0:T(8,128)(2,1)S(1)} %bitcast.13, f32[88,128]{1,0:T(8,128)S(1)} %copy-done.4, s32[88,128]{1,0:T(8,128)S(1)} %copy-done.5, f32[88,128]{1,0:T(8,128)S(1)} %copy-done.6, f32[88,128]{1,0:T(8,128)S(1)} %copy-done.7, s32[8,128]{1,0:T(8,128)S(1)} %bitcast.16), custom_call_target="tpu_custom_call" | custom-call | flops 23068672 | bytes 514048 | tf_op jit(solution)/shard_map/pallas_call | solution.py:310
  58.9 0.0 collective-permute-done.7.arrived_ref
  58.9 1.9 %shard_map.98 = bf16[256,1792]{1,0:T(8,128)(2,1)} custom-call(s32[8]{0:T(128)S(1)} %copy-done.9, bf16[256,3712]{1,0:T(8,128)(2,1)S(1)} %get-tuple-element.32.rows_ref, bf16[256,1792]{1,0:T(8,128)(2,1)S(1)} %collective-permute-done.7.arrived_ref), custom_call_target="tpu_custom_call" | custom-call | flops 234881024 | bytes 3735584 | tf_op jit(solution)/shard_map/pallas_call | solution.py:310
Async XLA Ops:
  0.6 41.4 %copy-start.9 = (s32[8]{0:T(128)S(1)}, s32[8]{0:T(128)}, u32[]{:S(2)}) copy-start(s32[8]{0:T(128)} %replica_ref.5) | copy-start | bytes 100
  0.6 41.4 %copy-start = (bf16[2,128,3584]{2,1,0:T(8,128)(2,1)S(1)}, bf16[2,128,3584]{2,1,0:T(8,128)(2,1)}, u32[]{:S(2)}) copy-start(bf16[2,128,3584]{2,1,0:T(8,128)(2,1)} %param.13) | copy-start | bytes 5505028
  3.3 12.7 %collective-permute-start.2 = (bf16[24,3712]{1,0:T(8,128)(2,1)}, bf16[24,3712]{1,0:T(8,128)(2,1)S(1)}, u32[]{:S(2)}, u32[]{:S(2)}) collective-permute-start(bf16[24,3712]{1,0:T(8,128)(2,1)} %get-tuple-element.21.refs_0_), channel_id=1, source_target_pairs={{0,8},{2,10},{4,12},{6,14},{8,0},{10,2},{12,4},{14,6},{1,9},{3,11}... | collective-permute-start | bytes 534536 | tf_op jit(solution)/shard_map/ppermute | solution.py:322
  7.4 8.8 %collective-permute-start.1 = (bf16[24,3712]{1,0:T(8,128)(2,1)}, bf16[24,3712]{1,0:T(8,128)(2,1)S(1)}, u32[]{:S(2)}, u32[]{:S(2)}) collective-permute-start(bf16[24,3712]{1,0:T(8,128)(2,1)} %get-tuple-element.21.refs_0_), channel_id=1, source_target_pairs={{0,4},{2,6},{4,0},{6,2},{8,12},{10,14},{12,8},{14,10},{1,5},{3,7},... | collective-permute-start | bytes 534536 | tf_op jit(solution)/shard_map/ppermute | solution.py:322
  9.0 7.3 %collective-permute-start = (bf16[24,3712]{1,0:T(8,128)(2,1)}, bf16[24,3712]{1,0:T(8,128)(2,1)S(1)}, u32[]{:S(2)}, u32[]{:S(2)}) collective-permute-start(bf16[24,3712]{1,0:T(8,128)(2,1)} %get-tuple-element.21.refs_0_), channel_id=1, source_target_pairs={{0,2},{2,0},{4,6},{6,4},{8,10},{10,8},{12,14},{14,12},{1,3},{3,1},... | collective-permute-start | bytes 534536 | tf_op jit(solution)/shard_map/ppermute | solution.py:322
  16.3 25.8 %all-to-all-start = ((bf16[8,8,3712]{2,1,0:T(8,128)(2,1)}), bf16[8,8,3712]{2,1,0:T(8,128)(2,1)S(1)}, u32[]{:S(2)}, u32[]{:S(2)}) async-start(bf16[8,8,3712]{2,1,0:T(8,128)(2,1)} %bitcast.18), calls=%async_computation | async-start | bytes 950272 | tf_op jit(solution)/shard_map/all_to_all | solution.py:359
  21.7 14.0 %collective-permute-start.5 = (bf16[24,3712]{1,0:T(8,128)(2,1)S(1)}, bf16[24,3712]{1,0:T(8,128)(2,1)S(1)}, u32[]{:S(2)}, u32[]{:S(2)}) collective-permute-start(bf16[24,3712]{1,0:T(8,128)(2,1)S(1)} %collective-permute-done.2.refs_4_), channel_id=1, source_target_pairs={{0,4},{2,6},{4,0},{6,2},{8,12},{10,14},{12,8},{14,10},{1,5},{3,7},... | collective-permute-start | bytes 534536 | tf_op jit(solution)/shard_map/ppermute | solution.py:322
  23.8 14.4 %collective-permute-start.4 = (bf16[24,3712]{1,0:T(8,128)(2,1)S(1)}, bf16[24,3712]{1,0:T(8,128)(2,1)S(1)}, u32[]{:S(2)}, u32[]{:S(2)}) collective-permute-start(bf16[24,3712]{1,0:T(8,128)(2,1)S(1)} %collective-permute-done.2.refs_4_), channel_id=1, source_target_pairs={{0,2},{2,0},{4,6},{6,4},{8,10},{10,8},{12,14},{14,12},{1,3},{3,1},... | collective-permute-start | bytes 534536 | tf_op jit(solution)/shard_map/ppermute | solution.py:322
  25.2 13.0 %collective-permute-start.3 = (bf16[24,3712]{1,0:T(8,128)(2,1)S(1)}, bf16[24,3712]{1,0:T(8,128)(2,1)S(1)}, u32[]{:S(2)}, u32[]{:S(2)}) collective-permute-start(bf16[24,3712]{1,0:T(8,128)(2,1)S(1)} %collective-permute-done.1.refs_2_), channel_id=1, source_target_pairs={{0,2},{2,0},{4,6},{6,4},{8,10},{10,8},{12,14},{14,12},{1,3},{3,1},... | collective-permute-start | bytes 534536 | tf_op jit(solution)/shard_map/ppermute | solution.py:322
  35.7 5.7 %collective-permute-start.6 = (bf16[24,3712]{1,0:T(8,128)(2,1)S(1)}, bf16[24,3712]{1,0:T(8,128)(2,1)S(1)}, u32[]{:S(2)}, u32[]{:S(2)}) collective-permute-start(bf16[24,3712]{1,0:T(8,128)(2,1)S(1)} %collective-permute-done.5.refs_6_), channel_id=1, source_target_pairs={{0,2},{2,0},{4,6},{6,4},{8,10},{10,8},{12,14},{14,12},{1,3},{3,1},... | collective-permute-start | bytes 534536 | tf_op jit(solution)/shard_map/ppermute | solution.py:322
  41.4 0.7 %copy-start.2 = (bf16[24,3712]{1,0:T(8,128)(2,1)}, bf16[24,3712]{1,0:T(8,128)(2,1)S(1)}, u32[]{:S(2)}) copy-start(bf16[24,3712]{1,0:T(8,128)(2,1)S(1)} %collective-permute-done.6.refs_7_) | copy-start | bytes 534532
  42.1 0.9 %copy-start.1 = (bf16[24,3712]{1,0:T(8,128)(2,1)S(1)}, bf16[24,3712]{1,0:T(8,128)(2,1)}, u32[]{:S(2)}) copy-start(bf16[24,3712]{1,0:T(8,128)(2,1)} %get-tuple-element.21.refs_0_) | copy-start | bytes 534532
  43.0 0.9 %copy-start.3 = (bf16[24,3712]{1,0:T(8,128)(2,1)S(1)}, bf16[24,3712]{1,0:T(8,128)(2,1)}, u32[]{:S(2)}) copy-start(bf16[24,3712]{1,0:T(8,128)(2,1)} %copy-done.2) | copy-start | bytes 534532
  45.4 12.5 %copy-start.4 = (f32[88,128]{1,0:T(8,128)S(1)}, f32[88,128]{1,0:T(8,128)}, u32[]{:S(2)}) copy-start(f32[88,128]{1,0:T(8,128)} %get-tuple-element.26.pick_ref) | copy-start | bytes 135172
  45.4 12.5 %copy-start.5 = (s32[88,128]{1,0:T(8,128)S(1)}, s32[88,128]{1,0:T(8,128)}, u32[]{:S(2)}) copy-start(s32[88,128]{1,0:T(8,128)} %get-tuple-element.27.expert_ref) | copy-start | bytes 135172
  45.4 12.4 %copy-start.6 = (f32[88,128]{1,0:T(8,128)S(1)}, f32[88,128]{1,0:T(8,128)}, u32[]{:S(2)}) copy-start(f32[88,128]{1,0:T(8,128)} %get-tuple-element.28.hs_ref) | copy-start | bytes 135172
  45.4 12.4 %copy-start.7 = (f32[88,128]{1,0:T(8,128)S(1)}, f32[88,128]{1,0:T(8,128)}, u32[]{:S(2)}) copy-start(f32[88,128]{1,0:T(8,128)} %get-tuple-element.29.ps_ref) | copy-start | bytes 135172
  45.4 12.4 %copy-start.8 = (s32[128,8]{0,1:T(8,128)S(1)}, s32[128,8]{0,1:T(8,128)}, u32[]{:S(2)}) copy-start(s32[128,8]{0,1:T(8,128)} %param.10) | copy-start | bytes 12292
  46.5 12.4 %collective-permute-start.7 = (bf16[256,1792]{1,0:T(8,128)(2,1)S(1)}, bf16[256,1792]{1,0:T(8,128)(2,1)S(1)}, u32[]{:S(2)}, u32[]{:S(2)}) collective-permute-start(bf16[256,1792]{1,0:T(8,128)(2,1)S(1)} %shard_map.97), channel_id=1, source_target_pairs={{0,1},{1,0},{2,3},{3,2},{4,5},{5,4},{6,7},{7,6},{8,9},{9,8},{10,11... | collective-permute-start | bytes 2752520 | tf_op jit(solution)/shard_map/ppermute | solution.py:377

commit v5 on v3

--- a/solution.py
+++ b/solution.py
@@ -155,6 +155,7 @@
 
 
 SLOT = 4
+HOME, COPIES = "home", "copies"
 F32 = jnp.float32
 BF16 = jnp.bfloat16
 NT = (((1,), (1,)), ((), ()))
@@ -165,22 +166,24 @@
     return lax.broadcasted_iota(jnp.int32, shape, dim)
 
 
-def dispatch_kernel(local_count, dev_count, *refs):
+def dispatch_kernel(local_count, dev_count, packing, *refs):
     sources, refs = refs[:6], refs[6:]
-    copy_ref, home_ref, pick_ref, expert_ref, hs_ref, ps_ref = refs[:6]
-    held, wide, sems = refs[6:12], refs[12], refs[13]
+    pick_ref, expert_ref, hs_ref, ps_ref = refs[:4]
+    packed, (held, wide, sems) = refs[4:4 + len(packing)], (refs[-8:-2], refs[-2], refs[-1])
     moves = [pltpu.make_async_copy(s, h, sems.at[n]) for n, (s, h) in enumerate(zip(sources, held))]
     for move in moves:
         move.start()
     replica_ref, counts_ref, ids_ref, probs_ref, hid_ref, cot_ref = held
     top, toks = ids_ref.shape
     d_model = cot_ref.shape[1]
-    homes = dev_count * local_count * SLOT
+    per_home = local_count * SLOT
+    homes = dev_count * per_home
     slots = homes + dev_count * CAPR
+    me = lax.axis_index("expert")
     for move in moves[:3]:
         move.wait()
     row = iota((slots, toks), 0)
-    expert = row // SLOT
+    expert = ((row // per_home) ^ me) * local_count + (row % per_home) // SLOT
     within = row % SLOT
     allowed = jnp.where(within < CAPH, 1, 0)
     for d in range(dev_count):
@@ -220,76 +223,117 @@
     scaled = p_slot * h_slot
     moves[5].wait()
     rows = jnp.dot(pick.astype(BF16), cot_ref[...], preferred_element_type=F32)
-    copy_ref[:, :d_model] = rows[homes:].astype(BF16)
-    copy_ref[:, d_model:] = scaled[homes:].astype(BF16)
-    home_ref[:, :d_model] = rows[:homes].astype(BF16)
-    home_ref[:, d_model:] = scaled[:homes].astype(BF16)
-
-
-def local_slots(local_count, dev_count, width, replica_ref):
-    first = lax.axis_index("expert") * local_count
-    home = (iota((dev_count * local_count * SLOT, width), 0) // SLOT) % local_count
-    row = iota((dev_count * CAPR, width), 0)
-    copy = jnp.full((dev_count * CAPR, width), -1, jnp.int32)
-    for d in range(dev_count):
-        mine = (row >= d * CAPR) & (row < (d + 1) * CAPR)
-        copy = jnp.where(mine, replica_ref[d] - first, copy)
-    return jnp.concatenate([home] + [copy] * dev_count, axis=0)
-
-
-def grad_in_kernel(local_count, dev_count, replica_ref, w_hbm, home_ref, *refs):
-    copy_refs, (rows_ref, back_ref, w_ref, passed, sem) = refs[:dev_count], refs[dev_count:]
-    fetch = pltpu.make_async_copy(w_hbm, w_ref, sem)
-    fetch.start()
+    for out_ref, blocks in zip(packed, packing):
+        spans = [(homes, slots) if b == COPIES else (b * per_home, (b + 1) * per_home) for b in blocks]
+        out_ref[:, :d_model] = jnp.concatenate([rows[i:j] for i, j in spans], axis=0).astype(BF16)
+        out_ref[:, d_model:] = jnp.concatenate([scaled[i:j] for i, j in spans], axis=0).astype(BF16)
+
+
+def padded(rows):
+    return -(-rows // 16) * 16
+
+
+def stack(order, blocks, height):
+    values = [blocks[key] for key in order]
+    missing = height - sum(v.shape[0] for v in values)
+    if missing:
+        values.append(jnp.zeros((missing, values[0].shape[1]), values[0].dtype))
+    return jnp.concatenate(values, axis=0)
+
+
+def slots_of(order, slot_ref, per_home, height):
+    kinds = {HOME: slot_ref[:per_home], COPIES: slot_ref[per_home:]}
+    return stack(order, {key: kinds[key[1]] for key in order}, height)
+
+
+def fill_rows(order, pieces, per_home, per_copy, piece_refs, rows_ref):
+    values = [r[...].astype(F32) for r in piece_refs]
+    blocks = {}
+    for key in order:
+        n, start = pieces[key]
+        blocks[key] = values[n][start:start + (per_home if key[1] == HOME else per_copy)]
+    rows_ref[...] = stack(order, blocks, rows_ref.shape[0]).astype(BF16)
+
+
+def own_columns(rows_ref, w_ref, slot, local_count):
     d_model = w_ref.shape[1]
     width = w_ref.shape[0] // local_count
-    per_home, per_copy = local_count * SLOT, dev_count * CAPR
-    homes = dev_count * per_home
-    rows_ref[:homes] = home_ref[...]
-    rows_ref[homes:] = jnp.concatenate([r[...].astype(F32) for r in copy_refs], axis=0).astype(BF16)
-    slot = local_slots(local_count, dev_count, width, replica_ref)
-    fetch.wait()
     every = lax.dot_general(rows_ref[:, :d_model], w_ref[...], NT, preferred_element_type=F32)
     own = jnp.zeros((rows_ref.shape[0], width), F32)
     for e in range(local_count):
         own = jnp.where(slot == e, every[:, e * width:(e + 1) * width], own)
-    passed[...] = own[homes:].reshape(passed.shape)
+    return own
+
+
+def early_kernel(local_count, dev_count, order, pieces, replica_ref, w_hbm, *refs):
+    piece_refs, (rows_ref, w_ref, slot_ref, own_ref, sem) = refs[:-5], refs[-5:]
+    fetch = pltpu.make_async_copy(w_hbm, w_ref, sem)
+    fetch.start()
+    per_home, per_copy = local_count * SLOT, dev_count * CAPR
+    first = lax.axis_index("expert") * local_count
+    width = slot_ref.shape[1]
+    slot_ref[:per_home] = iota((per_home, width), 0) // SLOT
+    row = iota((per_copy, width), 0)
+    copy = jnp.full((per_copy, width), -1, jnp.int32)
+    for d in range(dev_count):
+        mine = (row >= d * CAPR) & (row < (d + 1) * CAPR)
+        copy = jnp.where(mine, replica_ref[d] - first, copy)
+    slot_ref[per_home:] = copy
+    fill_rows(order, pieces, per_home, per_copy, piece_refs, rows_ref)
+    fetch.wait()
+    slot = slots_of(order, slot_ref, per_home, rows_ref.shape[0])
+    own_ref[...] = own_columns(rows_ref, w_ref, slot, local_count)
+
+
+def late_kernel(local_count, dev_count, early, order, pieces, own_ref, w_ref, slot_ref, *refs):
+    piece_refs, (rows_ref, back_ref, passed) = refs[:-3], refs[-3:]
+    per_home, per_copy = local_count * SLOT, dev_count * CAPR
+    fill_rows(order, pieces, per_home, per_copy, piece_refs, rows_ref)
+    own = own_columns(rows_ref, w_ref, slots_of(order, slot_ref, per_home, rows_ref.shape[0]), local_count)
+    for keys, value in ((early, own_ref[...]), (order, own)):
+        start = 0
+        for m, kind in keys:
+            lower, size = (0, per_home) if kind == HOME else (per_home, per_copy)
+            passed[m, lower:lower + size] = value[start:start + size]
+            start += size
     me = lax.axis_index("expert")
-    blocks = []
-    for source in range(dev_count):
-        blocks += [own[source * per_home:(source + 1) * per_home], passed[me ^ source]]
-    back_ref[...] = jnp.concatenate(blocks, axis=0).astype(back_ref.dtype)
-
-
-def grad_weights_half(local_count, dev_count, half, replica_ref, rows_ref, columns):
-    width = rows_ref.shape[1] - 2 * columns
+    back = jnp.concatenate([passed[me ^ source] for source in range(dev_count)], axis=0)
+    back_ref[...] = back.astype(back_ref.dtype)
+
+
+def grad_weights_half(local_count, dev_count, orders, half, slot_ref, rows_refs, columns):
     start = pl.multiple_of(half * columns, 128)
-    slot = local_slots(local_count, dev_count, width, replica_ref)
-    scaled = rows_ref[:, 2 * columns:].astype(F32)
-    spread = jnp.concatenate([jnp.where(slot == e, scaled, 0.0) for e in range(local_count)], axis=1)
-    return lax.dot_general(spread.astype(BF16), rows_ref[:, pl.ds(start, columns)], TN, preferred_element_type=F32)
-
-
-def other_half_kernel(local_count, dev_count, replica_ref, rows_ref, out_ref):
+    total = None
+    for order, ref in zip(orders, rows_refs):
+        slot = slots_of(order, slot_ref, local_count * SLOT, ref.shape[0])
+        scaled = ref[:, 2 * columns:].astype(F32)
+        spread = jnp.concatenate([jnp.where(slot == e, scaled, 0.0) for e in range(local_count)], axis=1)
+        part = lax.dot_general(spread.astype(BF16), ref[:, pl.ds(start, columns)], TN, preferred_element_type=F32)
+        total = part if total is None else total + part
+    return total
+
+
+def other_half_kernel(local_count, dev_count, orders, slot_ref, early_ref, late_ref, out_ref):
     half = 1 - lax.axis_index("dp")
     out_ref[...] = grad_weights_half(
-        local_count, dev_count, half, replica_ref, rows_ref, out_ref.shape[1]).astype(out_ref.dtype)
-
-
-def own_half_kernel(local_count, dev_count, replica_ref, rows_ref, arrived_ref, out_ref):
+        local_count, dev_count, orders, half, slot_ref, (early_ref, late_ref), out_ref.shape[1]).astype(out_ref.dtype)
+
+
+def own_half_kernel(local_count, dev_count, orders, slot_ref, early_ref, late_ref, arrived_ref, out_ref):
     half = lax.axis_index("dp")
-    total = grad_weights_half(local_count, dev_count, half, replica_ref, rows_ref, out_ref.shape[1])
+    total = grad_weights_half(
+        local_count, dev_count, orders, half, slot_ref, (early_ref, late_ref), out_ref.shape[1])
     out_ref[...] = (total + arrived_ref[...].astype(F32)).astype(out_ref.dtype)
 
 
 def combine_kernel(local_count, dev_count, back_ref, pick_ref, expert_ref, hs_ref, ps_ref, ids_ref,
                    grad_h_ref, grad_p_ref, wide, narrow):
     top, toks = ids_ref.shape
-    width = back_ref.shape[1]
-    per_home, per_copy = local_count * SLOT, dev_count * CAPR
-    back = back_ref[...].astype(F32).reshape(dev_count, per_home + per_copy, width)
-    home = back[:, :per_home].reshape(dev_count * per_home, width)
-    grad_in = jnp.concatenate([home, jnp.sum(back[:, per_home:], axis=0)], axis=0)
+    per_home = local_count * SLOT
+    me = lax.axis_index("expert")
+    back = [back_ref[me ^ m].astype(F32) for m in range(dev_count)]
+    copy = functools.reduce(jnp.add, [b[per_home:] for b in back])
+    grad_in = jnp.concatenate([b[:per_home] for b in back] + [copy], axis=0)
     h_rows = (ps_ref[...] * grad_in).astype(BF16)
     p_rows = jnp.sum(hs_ref[...] * grad_in, axis=1, keepdims=True)
     ids = ids_ref[...]
@@ -338,51 +382,88 @@
     shape = jax.ShapeDtypeStruct
     hbm, vmem, smem = pltpu.HBM, pltpu.VMEM, pltpu.SMEM
     sources = (replica_of, send_counts, ids, probs.T, hidden.reshape(toks * top, width), cotangent)
-    copy_rows, home_rows, pick, expert, h_slot, p_slot = call(
-        functools.partial(dispatch_kernel, *sizes),
-        (shape((copies, d_model + width), BF16), shape((homes, d_model + width), BF16), shape((slots, toks), F32),
-         shape((slots, toks), jnp.int32), shape((slots, width), F32), shape((slots, width), F32)),
+    per_home = local_count * SLOT
+    firsts = [1 << n for n in reversed(range(dev_count.bit_length() - 1))]
+    riders = {low: [low] + [low + 1] * (low == 2) for low in firsts if low < firsts[0]}
+    packing = [[COPIES] + riders.get(low, [])[::-1] for low in firsts]
+    direct = [m for m in range(1, dev_count) if not any(m in ride for ride in riders.values())]
+    packing += [[0], [COPIES]] + [[m] for m in direct]
+    sized = [sum(copies if b == COPIES else per_home for b in blocks) for blocks in packing]
+    pick, expert, h_slot, p_slot, *packed = call(
+        functools.partial(dispatch_kernel, *sizes, packing),
+        [shape((slots, toks), F32), shape((slots, toks), jnp.int32), shape((slots, width), F32),
+         shape((slots, width), F32)] + [shape((n, d_model + width), BF16) for n in sized],
         [(hbm, a) for a in sources],
         [(smem if n < 2 else vmem)(a.shape, a.dtype) for n, a in enumerate(sources)]
         + [vmem((toks * top, width), F32), pltpu.SemaphoreType.DMA((len(sources),))],
         flops=2 * slots * toks * d_model,
         limit=60,
     )
-    copy_in = [copy_rows] + [None] * (dev_count - 1)
+    pieces, arrays = {(0, HOME): (0, 0), (0, COPIES): (1, 0)}, packed[len(firsts):len(firsts) + 2]
+    arrived = [swap(a, low, dev_count) for a, low in zip(packed, firsts)]
+    arrived, packed, arrays = lax.optimization_barrier((arrived, packed, arrays))
+    passing = {}
+    for low, a in zip(firsts, arrived):
+        pieces[low, COPIES] = (len(arrays), 0)
+        if low in riders:
+            pieces[low, HOME] = (len(arrays), a.shape[0] - per_home)
+        passing[low] = a[:a.shape[0] - per_home] if low in riders else a
+        arrays.append(a)
+    flat_w = weights.reshape(local_count * width, d_model)
+    orders = [list(pieces)]
+    height = padded(sum(per_home if kind == HOME else copies for _, kind in pieces))
+    early_rows, w_held, slot, own = call(
+        functools.partial(early_kernel, *sizes, orders[0], pieces),
+        (shape((height, d_model + width), BF16), shape(flat_w.shape, BF16),
+         shape((per_home + copies, width), jnp.int32), shape((height, width), F32)),
+        [(smem, replica_of), (hbm, flat_w)] + [(vmem, a) for a in arrays],
+        [pltpu.SemaphoreType.DMA(())],
+        flops=2 * height * d_model * local_count * width,
+    )
+    pieces, arrays = {}, []
     for m in sorted(range(1, dev_count), key=lambda m: (m.bit_count(), -m)):
         low = m & -m
-        copy_in[m] = swap(copy_in[m ^ low], low, dev_count)
-    home_in = lax.all_to_all(home_rows, "expert", split_axis=0, concat_axis=0, tiled=True)
-    all_rows, back = call(
-        functools.partial(grad_in_kernel, *sizes),
-        (shape((rows, d_model + width), BF16), shape((rows, width), BF16)),
-        [(smem, replica_of), (hbm, weights.reshape(local_count * width, d_model)), (vmem, home_in)]
-        + [(vmem, a) for a in copy_in],
-        [vmem((local_count * width, d_model), BF16), vmem((dev_count, copies, width), F32),
-         pltpu.SemaphoreType.DMA(())],
-        flops=2 * rows * d_model * local_count * width,
+        if m != low:
+            passing[m] = swap(passing[m ^ low], low, dev_count)
+            pieces[m, COPIES] = (len(arrays), 0)
+            if passing[m].shape[0] > copies:
+                pieces[m, HOME] = (len(arrays), copies)
+            arrays.append(passing[m])
+    for m, a in zip(direct, packed[len(firsts) + 2:]):
+        pieces[m, HOME] = (len(arrays), 0)
+        arrays.append(swap(a, m, dev_count))
+    orders.append(list(pieces))
+    height = padded(sum(per_home if kind == HOME else copies for _, kind in pieces))
+    late_rows, back = call(
+        functools.partial(late_kernel, *sizes, *orders, pieces),
+        (shape((height, d_model + width), BF16), shape((dev_count * (per_home + copies), width), BF16)),
+        [(vmem, a) for a in (own, w_held, slot, *arrays)],
+        [vmem((dev_count, per_home + copies, width), F32)],
+        flops=2 * height * d_model * local_count * width,
     )
     back = lax.all_to_all(back, "expert", split_axis=0, concat_axis=0, tiled=True)
     half_flops = 2 * rows * columns * local_count * width
+    halves = (slot, early_rows, late_rows)
     other = call(
-        functools.partial(other_half_kernel, *sizes),
+        functools.partial(other_half_kernel, *sizes, orders),
         shape((local_count * width, columns), BF16),
-        [(smem, replica_of), (vmem, all_rows)],
+        [(vmem, a) for a in halves],
         flops=half_flops,
     )
     arrived = lax.ppermute(other, "dp", [(0, 1), (1, 0)])
+    grad_w = call(
+        functools.partial(own_half_kernel, *sizes, orders),
+        shape((local_count * width, columns), BF16),
+        [(vmem, a) for a in (*halves, arrived)],
+        flops=half_flops,
+    )
+    grad_w, pick = lax.optimization_barrier((grad_w, pick))
     grad_h, grad_p = call(
         functools.partial(combine_kernel, *sizes),
         (shape((toks * top, width), BF16), shape((top, toks), BF16)),
-        [(vmem, a) for a in (back, pick, expert, h_slot, p_slot, ids)],
+        [(vmem, a) for a in (back.reshape(dev_count, per_home + copies, width), pick, expert, h_slot, p_slot, ids)],
         [vmem((toks * top, width), F32), vmem((top, toks), F32)],
         flops=2 * slots * toks * width * top,
-    )
-    grad_w = call(
-        functools.partial(own_half_kernel, *sizes),
-        shape((local_count * width, columns), BF16),
-        [(smem, replica_of), (vmem, all_rows), (vmem, arrived)],
-        flops=half_flops,
     )
     return (
         grad_h.reshape(toks, top, width),

time: 68.8 us -> 58.5 us (0.85)
  waiting for transfers between devices: 28.6 us -> 16.2 us
  blocking collectives: 11.8 us -> 0 us
  starting transfers between devices: 16.7 us -> 27.5 us
  Pallas kernels: 8.1 us -> 9.77 us
  local copies, waits for them, and re-layouts: 2.53 us -> 3.94 us
    ppermute x7 -> x11, waiting for transfers between devices: 28.6 us -> 10.9 us  [swap(): return lax.ppermute(x, 'expert', [(i, i ^ bits) for i in range(count)])]
    ppermute x7 -> x11, starting transfers between devices: 9.34 us -> 23.6 us  [swap(): return lax.ppermute(x, 'expert', [(i, i ^ bits) for i in range(count)])]
    all_to_all x1 -> x0, blocking collectives: 11.8 us -> none  [gather_body(): lax.all_to_all(back, 'expert', split_axis=0, concat_axis=0, tiled=True)]
    all_to_all x1, waiting for transfers between devices: 0.01 us -> 5.24 us  [gather_body(): lax.all_to_all(back, 'expert', split_axis=0, concat_axis=0, tiled=True)]
    all_to_all x1, starting transfers between devices: 7.26 us -> 3.92 us  [gather_body(): lax.all_to_all(back, 'expert', split_axis=0, concat_axis=0, tiled=True)]
    pallas_call x5 -> x6, Pallas kernels: 8.1 us -> 9.77 us  [call(): pl.pallas_call(kernel, out_shape=out_shape, in_specs=[pl.BlockSpec(memory...]
    unnamed x20 -> x18, local copies, waits for them, and re-layouts: 2.53 us -> 3.92 us
  transfers between devices with their start and end apart: 9 -> 13, of which waited for: 6 -> 5; matrix products, arithmetic and copies ran while one was open for 0% -> 0% of each run, Pallas kernels for 1% -> 5%
where the time goes in v5:
time: 58.5 us; the launch traced here: 58.2 us
  starting transfers between devices  27.5 us (47%)
  waiting for transfers between devices  16.2 us (28%)
  Pallas kernels  9.77 us (17%)
  local copies, waits for them, and re-layouts  3.94 us (7%)
  between operations  0.77 us (1%)
    ppermute x11, starting transfers between devices, swap(): return lax.ppermute(x, 'expert', [(i, i ^ bits) for i in range(count)])  23.6 us
    ppermute x11, waiting for transfers between devices, swap(): return lax.ppermute(x, 'expert', [(i, i ^ bits) for i in range(count)])  10.9 us
    pallas_call x6, Pallas kernels, call(): pl.pallas_call(kernel, out_shape=out_shape, in_specs=[pl.BlockSpec(memory...  9.77 us
    all_to_all x1, waiting for transfers between devices, gather_body(): lax.all_to_all(back, 'expert', split_axis=0, concat_axis=0, tiled=True)  5.24 us
    all_to_all x1, starting transfers between devices, gather_body(): lax.all_to_all(back, 'expert', split_axis=0, concat_axis=0, tiled=True)  3.92 us
    unnamed x18, local copies, waits for them, and re-layouts  3.92 us
  transfers between devices with their start and end apart: 13, of which 5 were waited for; matrix products, arithmetic and copies ran while one was open for 0% of the time, Pallas kernels for 5%

profile of v5, /device:TPU:0, one launch (start us, length us, event | category | flops | bytes accessed | tf_op | source)
XLA Modules:
  0.0 58.2 jit_solution(2830302061569406020)
XLA Ops:
  0.6 2.7 %shard_map.94 = (f32[88,128]{1,0:T(8,128)}, s32[88,128]{1,0:T(8,128)}, f32[88,128]{1,0:T(8,128)}, f32[88,128]{1,0:T(8,128)}, bf16[24,3712]{1,0:T(8,128)(2,1)}, /...) custom-call(s32[8]{0:T(128)} %replica_ref.1, ...), custom_call_target="tpu_custom_call" | custom-call | flops 80740352 | bytes 2553920 | tf_op jit(solution)/shard_map/pallas_call | solution.py:354
  3.4 3.1 %collective-permute-start.1 = (bf16[40,3712]{1,0:T(8,128)(2,1)}, bf16[40,3712]{1,0:T(8,128)(2,1)S(1)}, u32[]{:S(2)}, u32[]{:S(2)}) collective-permute-start(bf16[40,3712]{1,0:T(8,128)(2,1)} %get-tuple-element.36), channel_id=1, source_target_pairs={{0,4},{2,6},{4,0},{6,2},{8,12},{10,14},{12,8},{14,10},{1,5},{3,7},... | collective-permute-start | bytes 890888 | tf_op jit(solution)/shard_map/ppermute | solution.py:366
  6.4 1.5 %collective-permute-start.2 = (bf16[32,3712]{1,0:T(8,128)(2,1)}, bf16[32,3712]{1,0:T(8,128)(2,1)S(1)}, u32[]{:S(2)}, u32[]{:S(2)}) collective-permute-start(bf16[32,3712]{1,0:T(8,128)(2,1)} %get-tuple-element.37), channel_id=1, source_target_pairs={{0,2},{2,0},{4,6},{6,4},{8,10},{10,8},{12,14},{14,12},{1,3},{3,1},... | collective-permute-start | bytes 712712 | tf_op jit(solution)/shard_map/ppermute | solution.py:366
  7.9 2.6 %collective-permute-start = (bf16[24,3712]{1,0:T(8,128)(2,1)}, bf16[24,3712]{1,0:T(8,128)(2,1)S(1)}, u32[]{:S(2)}, u32[]{:S(2)}) collective-permute-start(bf16[24,3712]{1,0:T(8,128)(2,1)} %get-tuple-element.35), channel_id=1, source_target_pairs={{0,8},{2,10},{4,12},{6,14},{8,0},{10,2},{12,4},{14,6},{1,9},{3,11}... | collective-permute-start | bytes 534536 | tf_op jit(solution)/shard_map/ppermute | solution.py:366
  10.5 6.4 %collective-permute-done.refs_2_ = bf16[24,3712]{1,0:T(8,128)(2,1)S(1)} collective-permute-done((bf16[24,3712]{1,0:T(8,128)(2,1)}, bf16[24,3712]{1,0:T(8,128)(2,1)S(1)}, u32[]{:S(2)}, u32[]{:S(2)}) %collective-permute-start) | collective-permute-done | bytes 178208 | tf_op jit(solution)/shard_map/ppermute | solution.py:366
  16.9 0.0 collective-permute-done.2.refs_4_
  16.9 0.6 %collective-permute-done.1.refs_3_ = bf16[40,3712]{1,0:T(8,128)(2,1)S(1)} collective-permute-done((bf16[40,3712]{1,0:T(8,128)(2,1)}, bf16[40,3712]{1,0:T(8,128)(2,1)S(1)}, u32[]{:S(2)}, u32[]{:S(2)}) %collective-permute-start.1) | collective-permute-done | bytes 296992 | tf_op jit(solution)/shard_map/ppermute | solution.py:366
  17.5 2.8 %collective-permute-start.3 = (bf16[24,3712]{1,0:T(8,128)(2,1)S(1)}, bf16[24,3712]{1,0:T(8,128)(2,1)S(1)}, u32[]{:S(2)}, u32[]{:S(2)}) collective-permute-start(bf16[24,3712]{1,0:T(8,128)(2,1)S(1)} %collective-permute-done.refs_2_), channel_id=1, source_target_pairs={{0,4},{2,6},{4,0},{6,2},{8,12},{10,14},{12,8},{14,10},{1,5},{3,7},... | collective-permute-start | bytes 534536 | tf_op jit(solution)/shard_map/ppermute | solution.py:366
  20.3 1.6 %collective-permute-start.5 = (bf16[32,3712]{1,0:T(8,128)(2,1)S(1)}, bf16[32,3712]{1,0:T(8,128)(2,1)S(1)}, u32[]{:S(2)}, u32[]{:S(2)}) collective-permute-start(bf16[32,3712]{1,0:T(8,128)(2,1)S(1)} %slice.3), channel_id=1, source_target_pairs={{0,2},{2,0},{4,6},{6,4},{8,10},{10,8},{12,14},{14,12},{1,3},{3,1},... | collective-permute-start | bytes 712712 | tf_op jit(solution)/shard_map/ppermute | solution.py:366
  21.9 0.5 collective-permute-start.4
  22.4 1.5 %collective-permute-done.3.refs_0_ = bf16[24,3712]{1,0:T(8,128)(2,1)S(1)} collective-permute-done((bf16[24,3712]{1,0:T(8,128)(2,1)S(1)}, bf16[24,3712]{1,0:T(8,128)(2,1)S(1)}, u32[]{:S(2)}, u32[]{:S(2)}) %collective-permute-start.3) | collective-permute-done | bytes 178208 | tf_op jit(solution)/shard_map/ppermute | solution.py:366
  23.9 1.5 %collective-permute-start.6 = (bf16[24,3712]{1,0:T(8,128)(2,1)S(1)}, bf16[24,3712]{1,0:T(8,128)(2,1)S(1)}, u32[]{:S(2)}, u32[]{:S(2)}) collective-permute-start(bf16[24,3712]{1,0:T(8,128)(2,1)S(1)} %collective-permute-done.3.refs_0_), channel_id=1, source_target_pairs={{0,2},{2,0},{4,6},{6,4},{8,10},{10,8},{12,14},{14,12},{1,3},{3,1},... | collective-permute-start | bytes 534536 | tf_op jit(solution)/shard_map/ppermute | solution.py:366
  25.4 1.7 %collective-permute-start.7 = (bf16[8,3712]{1,0:T(8,128)(2,1)}, bf16[8,3712]{1,0:T(8,128)(2,1)S(1)}, u32[]{:S(2)}, u32[]{:S(2)}) collective-permute-start(bf16[8,3712]{1,0:T(8,128)(2,1)} %get-tuple-element.52), channel_id=1, source_target_pairs={{0,8},{2,10},{4,12},{6,14},{8,0},{10,2},{12,4},{14,6},{1,9},{3,11}... | collective-permute-start | bytes 178184 | tf_op jit(solution)/shard_map/ppermute | solution.py:366
  27.1 1.2 %collective-permute-start.8 = (bf16[8,3712]{1,0:T(8,128)(2,1)}, bf16[8,3712]{1,0:T(8,128)(2,1)S(1)}, u32[]{:S(2)}, u32[]{:S(2)}) collective-permute-start(bf16[8,3712]{1,0:T(8,128)(2,1)} %get-tuple-element.53), channel_id=1, source_target_pairs={{0,10},{2,8},{4,14},{6,12},{8,2},{10,0},{12,6},{14,4},{1,11},{3,9}... | collective-permute-start | bytes 178184 | tf_op jit(solution)/shard_map/ppermute | solution.py:366
  28.3 2.4 %collective-permute-done.7.refs_4_ = bf16[8,3712]{1,0:T(8,128)(2,1)S(1)} collective-permute-done((bf16[8,3712]{1,0:T(8,128)(2,1)}, bf16[8,3712]{1,0:T(8,128)(2,1)S(1)}, u32[]{:S(2)}, u32[]{:S(2)}) %collective-permute-start.7) | collective-permute-done | bytes 59424 | tf_op jit(solution)/shard_map/ppermute | solution.py:366
  30.7 5.1 %collective-permute-start.9 = (bf16[8,3712]{1,0:T(8,128)(2,1)}, bf16[8,3712]{1,0:T(8,128)(2,1)S(1)}, u32[]{:S(2)}, u32[]{:S(2)}) collective-permute-start(bf16[8,3712]{1,0:T(8,128)(2,1)} %get-tuple-element.54), channel_id=1, source_target_pairs={{0,12},{2,14},{4,8},{6,10},{8,4},{10,6},{12,0},{14,2},{1,13},{3,15... | collective-permute-start | bytes 178184 | tf_op jit(solution)/shard_map/ppermute | solution.py:366
  35.8 0.0 collective-permute-done.8.refs_5_
  35.8 2.1 %collective-permute-start.10 = (bf16[8,3712]{1,0:T(8,128)(2,1)}, bf16[8,3712]{1,0:T(8,128)(2,1)S(1)}, u32[]{:S(2)}, u32[]{:S(2)}) collective-permute-start(bf16[8,3712]{1,0:T(8,128)(2,1)} %get-tuple-element.55), channel_id=1, source_target_pairs={{0,14},{2,12},{4,10},{6,8},{8,6},{10,4},{12,2},{14,0},{1,15},{3,13... | collective-permute-start | bytes 178184 | tf_op jit(solution)/shard_map/ppermute | solution.py:366
  37.9 0.0 copy-start
  37.9 1.5 %copy-done = bf16[2,128,3584]{2,1,0:T(8,128)(2,1)S(1)} copy-done((bf16[2,128,3584]{2,1,0:T(8,128)(2,1)S(1)}, bf16[2,128,3584]{2,1,0:T(8,128)(2,1)}, u32[]{:S(2)}) %copy-start) | copy-done | bytes 1835032
  39.4 0.0 copy-start.1
  39.4 0.9 %copy-done.1 = bf16[24,3712]{1,0:T(8,128)(2,1)S(1)} copy-done((bf16[24,3712]{1,0:T(8,128)(2,1)S(1)}, bf16[24,3712]{1,0:T(8,128)(2,1)}, u32[]{:S(2)}) %copy-start.1) | copy-done | bytes 178200
  40.3 0.0 copy-start.2
  40.3 0.8 %copy-done.2 = bf16[8,3712]{1,0:T(8,128)(2,1)S(1)} copy-done((bf16[8,3712]{1,0:T(8,128)(2,1)S(1)}, bf16[8,3712]{1,0:T(8,128)(2,1)}, u32[]{:S(2)}) %copy-start.2) | copy-done | bytes 59416
  41.2 0.0 copy-start.8
  41.2 0.7 %copy-done.8 = s32[8]{0:T(128)S(1)} copy-done((s32[8]{0:T(128)S(1)}, s32[8]{0:T(128)}, u32[]{:S(2)}) %copy-start.8) | copy-done | bytes 56
  41.8 1.4 %shard_map.95 = (bf16[128,3712]{1,0:T(8,128)(2,1)S(1)}, bf16[256,3584]{1,0:T(8,128)(2,1)S(1)}, s32[32,128]{1,0:T(8,128)S(1)}, f32[128,128]{1,0:T(8,128)S(1)}) custom-call(s32[8]{0:T(128)S(1)} %copy-done.8, bf16[256,3584]{1,0:T(8,128)(2,1)S(1)} %bitcast.8, bf16[8,3712]{1,0:T(8,128)(2,1)S(1)} %copy-done.2, bf16[24,3712]{1,0:T(8,128)(2,1)S(1)} %copy-done.1, ...), custom_call_target="tpu_custom_call" | custom-call | flops 234881024 | bytes 5652512 | tf_op jit(solution)/shard_map/pallas_call | solution.py:354
  43.3 0.0 collective-permute-done.9.refs_6_
  43.3 0.0 collective-permute-done.10.refs_7_
  43.3 0.0 collective-permute-done.4.refs_1_
  43.3 0.0 collective-permute-done.5.refs_2_
  43.3 0.0 collective-permute-done.6.refs_3_
  43.3 1.4 %shard_map.96 = (bf16[144,3712]{1,0:T(8,128)(2,1)S(1)}, bf16[256,128]{1,0:T(8,128)(2,1)}) custom-call(f32[128,128]{1,0:T(8,128)S(1)} %get-tuple-element.49.own_ref, bf16[256,3584]{1,0:T(8,128)(2,1)S(1)} %get-tuple-element.50.w_ref, s32[32,128]{1,0:T(8,128)S(1)} %get-tuple-element.51.slot_ref, bf16[24,3712]{1,0:T(8,128)(2,1)S(1)} %collective-permute-done.3.refs_0_, ...), custom_call_target="tpu_custom_call" | custom-call | flops 264241152 | bytes 4061184 | tf_op jit(solution)/shard_map/pallas_call | solution.py:354
  44.7 1.6 %shard_map.97 = bf16[256,1792]{1,0:T(8,128)(2,1)} custom-call(s32[32,128]{1,0:T(8,128)S(1)} %get-tuple-element.51.slot_ref, bf16[128,3712]{1,0:T(8,128)(2,1)S(1)} %get-tuple-element.57.early_ref, bf16[144,3712]{1,0:T(8,128)(2,1)S(1)} %get-tuple-element.58.late_ref), custom_call_target="tpu_custom_call" | custom-call | flops 234881024 | bytes 2953216 | tf_op jit(solution)/shard_map/pallas_call | solution.py:354
  46.3 0.0 collective-permute-start.11
  46.3 3.9 %all-to-all-start = ((bf16[8,32,128]{2,1,0:T(8,128)(2,1)}), bf16[8,32,128]{2,1,0:T(8,128)(2,1)S(1)}, u32[]{:S(2)}, u32[]{:S(2)}) async-start(bf16[8,32,128]{2,1,0:T(8,128)(2,1)} %bitcast.4), calls=%async_computation | async-start | bytes 131072 | tf_op jit(solution)/shard_map/all_to_all | solution.py:444
  50.2 0.0 copy-start.3
  50.2 0.0 copy-start.4
  50.3 0.0 copy-start.5
  50.3 0.0 copy-start.6
  50.3 0.0 copy-start.7
  50.3 0.0 collective-permute-done.11.arrived_ref
  50.3 1.6 %shard_map.98 = bf16[256,1792]{1,0:T(8,128)(2,1)} custom-call(s32[32,128]{1,0:T(8,128)S(1)} %get-tuple-element.51.slot_ref, bf16[128,3712]{1,0:T(8,128)(2,1)S(1)} %get-tuple-element.57.early_ref, bf16[144,3712]{1,0:T(8,128)(2,1)S(1)} %get-tuple-element.58.late_ref, bf16[256,1792]{1,0:T(8,128)(2,1)S(1)} %collective-permute-done.11.arrived_ref), custom_call_target="tpu_custom_call" | custom-call | flops 234881024 | bytes 3870720 | tf_op jit(solution)/shard_map/pallas_call | solution.py:354
  51.9 5.2 %all-to-all-done.back_ref = bf16[8,32,128]{2,1,0:T(8,128)(2,1)S(1)} async-done(((bf16[8,32,128]{2,1,0:T(8,128)(2,1)}), bf16[8,32,128]{2,1,0:T(8,128)(2,1)S(1)}, u32[]{:S(2)}, u32[]{:S(2)}) %all-to-all-start) | async-done | bytes 65568 | tf_op jit(solution)/shard_map/all_to_all | solution.py:444
  57.1 0.0 copy-done.3
  57.2 0.0 copy-done.4
  57.2 0.0 copy-done.5
  57.2 0.0 copy-done.6
  57.2 0.0 copy-done.7
  57.2 1.0 %shard_map.99 = (bf16[1024,128]{1,0:T(8,128)(2,1)}, bf16[8,128]{1,0:T(8,128)(2,1)}) custom-call(bf16[8,32,128]{2,1,0:T(8,128)(2,1)S(1)} %all-to-all-done.back_ref, f32[88,128]{1,0:T(8,128)S(1)} %copy-done.3, s32[88,128]{1,0:T(8,128)S(1)} %copy-done.4, f32[88,128]{1,0:T(8,128)S(1)} %copy-done.5, f32[88,128]{1,0:T(8,128)S(1)} %copy-done.6, s32[8,128]{1,0:T(8,128)S(1)} %bitcast.10), custom_call_target="tpu_custom_call" | custom-call | flops 23068672 | bytes 514048 | tf_op jit(solution)/shard_map/pallas_call | solution.py:354
  (1 shorter events, 0.0 us)
Async XLA Ops:
  3.4 14.2 %collective-permute-start.1 = (bf16[40,3712]{1,0:T(8,128)(2,1)}, bf16[40,3712]{1,0:T(8,128)(2,1)S(1)}, u32[]{:S(2)}, u32[]{:S(2)}) collective-permute-start(bf16[40,3712]{1,0:T(8,128)(2,1)} %get-tuple-element.36), channel_id=1, source_target_pairs={{0,4},{2,6},{4,0},{6,2},{8,12},{10,14},{12,8},{14,10},{1,5},{3,7},... | collective-permute-start | bytes 890888 | tf_op jit(solution)/shard_map/ppermute | solution.py:366
  6.4 10.5 %collective-permute-start.2 = (bf16[32,3712]{1,0:T(8,128)(2,1)}, bf16[32,3712]{1,0:T(8,128)(2,1)S(1)}, u32[]{:S(2)}, u32[]{:S(2)}) collective-permute-start(bf16[32,3712]{1,0:T(8,128)(2,1)} %get-tuple-element.37), channel_id=1, source_target_pairs={{0,2},{2,0},{4,6},{6,4},{8,10},{10,8},{12,14},{14,12},{1,3},{3,1},... | collective-permute-start | bytes 712712 | tf_op jit(solution)/shard_map/ppermute | solution.py:366
  7.9 8.9 %collective-permute-start = (bf16[24,3712]{1,0:T(8,128)(2,1)}, bf16[24,3712]{1,0:T(8,128)(2,1)S(1)}, u32[]{:S(2)}, u32[]{:S(2)}) collective-permute-start(bf16[24,3712]{1,0:T(8,128)(2,1)} %get-tuple-element.35), channel_id=1, source_target_pairs={{0,8},{2,10},{4,12},{6,14},{8,0},{10,2},{12,4},{14,6},{1,9},{3,11}... | collective-permute-start | bytes 534536 | tf_op jit(solution)/shard_map/ppermute | solution.py:366
  17.5 6.4 %collective-permute-start.3 = (bf16[24,3712]{1,0:T(8,128)(2,1)S(1)}, bf16[24,3712]{1,0:T(8,128)(2,1)S(1)}, u32[]{:S(2)}, u32[]{:S(2)}) collective-permute-start(bf16[24,3712]{1,0:T(8,128)(2,1)S(1)} %collective-permute-done.refs_2_), channel_id=1, source_target_pairs={{0,4},{2,6},{4,0},{6,2},{8,12},{10,14},{12,8},{14,10},{1,5},{3,7},... | collective-permute-start | bytes 534536 | tf_op jit(solution)/shard_map/ppermute | solution.py:366
  20.3 23.0 %collective-permute-start.5 = (bf16[32,3712]{1,0:T(8,128)(2,1)S(1)}, bf16[32,3712]{1,0:T(8,128)(2,1)S(1)}, u32[]{:S(2)}, u32[]{:S(2)}) collective-permute-start(bf16[32,3712]{1,0:T(8,128)(2,1)S(1)} %slice.3), channel_id=1, source_target_pairs={{0,2},{2,0},{4,6},{6,4},{8,10},{10,8},{12,14},{14,12},{1,3},{3,1},... | collective-permute-start | bytes 712712 | tf_op jit(solution)/shard_map/ppermute | solution.py:366
  21.9 21.4 %collective-permute-start.4 = (bf16[24,3712]{1,0:T(8,128)(2,1)S(1)}, bf16[24,3712]{1,0:T(8,128)(2,1)S(1)}, u32[]{:S(2)}, u32[]{:S(2)}) collective-permute-start(bf16[24,3712]{1,0:T(8,128)(2,1)S(1)} %collective-permute-done.refs_2_), channel_id=1, source_target_pairs={{0,2},{2,0},{4,6},{6,4},{8,10},{10,8},{12,14},{14,12},{1,3},{3,1},... | collective-permute-start | bytes 534536 | tf_op jit(solution)/shard_map/ppermute | solution.py:366
  23.9 19.4 %collective-permute-start.6 = (bf16[24,3712]{1,0:T(8,128)(2,1)S(1)}, bf16[24,3712]{1,0:T(8,128)(2,1)S(1)}, u32[]{:S(2)}, u32[]{:S(2)}) collective-permute-start(bf16[24,3712]{1,0:T(8,128)(2,1)S(1)} %collective-permute-done.3.refs_0_), channel_id=1, source_target_pairs={{0,2},{2,0},{4,6},{6,4},{8,10},{10,8},{12,14},{14,12},{1,3},{3,1},... | collective-permute-start | bytes 534536 | tf_op jit(solution)/shard_map/ppermute | solution.py:366
  25.4 5.3 %collective-permute-start.7 = (bf16[8,3712]{1,0:T(8,128)(2,1)}, bf16[8,3712]{1,0:T(8,128)(2,1)S(1)}, u32[]{:S(2)}, u32[]{:S(2)}) collective-permute-start(bf16[8,3712]{1,0:T(8,128)(2,1)} %get-tuple-element.52), channel_id=1, source_target_pairs={{0,8},{2,10},{4,12},{6,14},{8,0},{10,2},{12,4},{14,6},{1,9},{3,11}... | collective-permute-start | bytes 178184 | tf_op jit(solution)/shard_map/ppermute | solution.py:366
  27.1 8.7 %collective-permute-start.8 = (bf16[8,3712]{1,0:T(8,128)(2,1)}, bf16[8,3712]{1,0:T(8,128)(2,1)S(1)}, u32[]{:S(2)}, u32[]{:S(2)}) collective-permute-start(bf16[8,3712]{1,0:T(8,128)(2,1)} %get-tuple-element.53), channel_id=1, source_target_pairs={{0,10},{2,8},{4,14},{6,12},{8,2},{10,0},{12,6},{14,4},{1,11},{3,9}... | collective-permute-start | bytes 178184 | tf_op jit(solution)/shard_map/ppermute | solution.py:366
  30.7 12.6 %collective-permute-start.9 = (bf16[8,3712]{1,0:T(8,128)(2,1)}, bf16[8,3712]{1,0:T(8,128)(2,1)S(1)}, u32[]{:S(2)}, u32[]{:S(2)}) collective-permute-start(bf16[8,3712]{1,0:T(8,128)(2,1)} %get-tuple-element.54), channel_id=1, source_target_pairs={{0,12},{2,14},{4,8},{6,10},{8,4},{10,6},{12,0},{14,2},{1,13},{3,15... | collective-permute-start | bytes 178184 | tf_op jit(solution)/shard_map/ppermute | solution.py:366
  35.8 7.5 %collective-permute-start.10 = (bf16[8,3712]{1,0:T(8,128)(2,1)}, bf16[8,3712]{1,0:T(8,128)(2,1)S(1)}, u32[]{:S(2)}, u32[]{:S(2)}) collective-permute-start(bf16[8,3712]{1,0:T(8,128)(2,1)} %get-tuple-element.55), channel_id=1, source_target_pairs={{0,14},{2,12},{4,10},{6,8},{8,6},{10,4},{12,2},{14,0},{1,15},{3,13... | collective-permute-start | bytes 178184 | tf_op jit(solution)/shard_map/ppermute | solution.py:366
  37.9 1.5 %copy-start = (bf16[2,128,3584]{2,1,0:T(8,128)(2,1)S(1)}, bf16[2,128,3584]{2,1,0:T(8,128)(2,1)}, u32[]{:S(2)}) copy-start(bf16[2,128,3584]{2,1,0:T(8,128)(2,1)} %param.13) | copy-start | bytes 5505028
  39.4 0.9 %copy-start.1 = (bf16[24,3712]{1,0:T(8,128)(2,1)S(1)}, bf16[24,3712]{1,0:T(8,128)(2,1)}, u32[]{:S(2)}) copy-start(bf16[24,3712]{1,0:T(8,128)(2,1)} %get-tuple-element.45.refs_1_) | copy-start | bytes 534532
  40.3 0.8 %copy-start.2 = (bf16[8,3712]{1,0:T(8,128)(2,1)S(1)}, bf16[8,3712]{1,0:T(8,128)(2,1)}, u32[]{:S(2)}) copy-start(bf16[8,3712]{1,0:T(8,128)(2,1)} %get-tuple-element.44.refs_0_) | copy-start | bytes 178180
  41.2 0.7 %copy-start.8 = (s32[8]{0:T(128)S(1)}, s32[8]{0:T(128)}, u32[]{:S(2)}) copy-start(s32[8]{0:T(128)} %replica_ref.1) | copy-start | bytes 100
  46.3 4.0 %collective-permute-start.11 = (bf16[256,1792]{1,0:T(8,128)(2,1)}, bf16[256,1792]{1,0:T(8,128)(2,1)S(1)}, u32[]{:S(2)}, u32[]{:S(2)}) collective-permute-start(bf16[256,1792]{1,0:T(8,128)(2,1)} %shard_map.97), channel_id=1, source_target_pairs={{0,1},{1,0},{2,3},{3,2},{4,5},{5,4},{6,7},{7,6},{8,9},{9,8},{10,11... | collective-permute-start | bytes 2752520 | tf_op jit(solution)/shard_map/ppermute | solution.py:453
  46.3 10.8 %all-to-all-start = ((bf16[8,32,128]{2,1,0:T(8,128)(2,1)}), bf16[8,32,128]{2,1,0:T(8,128)(2,1)S(1)}, u32[]{:S(2)}, u32[]{:S(2)}) async-start(bf16[8,32,128]{2,1,0:T(8,128)(2,1)} %bitcast.4), calls=%async_computation | async-start | bytes 131072 | tf_op jit(solution)/shard_map/all_to_all | solution.py:444
  50.2 6.9 %copy-start.3 = (f32[88,128]{1,0:T(8,128)S(1)}, f32[88,128]{1,0:T(8,128)}, u32[]{:S(2)}) copy-start(f32[88,128]{1,0:T(8,128)} %get-tuple-element.60.pick_ref) | copy-start | bytes 135172
  50.2 6.9 %copy-start.4 = (s32[88,128]{1,0:T(8,128)S(1)}, s32[88,128]{1,0:T(8,128)}, u32[]{:S(2)}) copy-start(s32[88,128]{1,0:T(8,128)} %get-tuple-element.61.expert_ref) | copy-start | bytes 135172
  50.3 6.9 %copy-start.5 = (f32[88,128]{1,0:T(8,128)S(1)}, f32[88,128]{1,0:T(8,128)}, u32[]{:S(2)}) copy-start(f32[88,128]{1,0:T(8,128)} %get-tuple-element.62.hs_ref) | copy-start | bytes 135172
  50.3 6.9 %copy-start.6 = (f32[88,128]{1,0:T(8,128)S(1)}, f32[88,128]{1,0:T(8,128)}, u32[]{:S(2)}) copy-start(f32[88,128]{1,0:T(8,128)} %get-tuple-element.63.ps_ref) | copy-start | bytes 135172
  50.3 6.9 %copy-start.7 = (s32[128,8]{0,1:T(8,128)S(1)}, s32[128,8]{0,1:T(8,128)}, u32[]{:S(2)}) copy-start(s32[128,8]{0,1:T(8,128)} %param.10) | copy-start | bytes 12292

commit v6 on v5

--- a/solution.py
+++ b/solution.py
@@ -175,7 +175,6 @@
         move.start()
     replica_ref, counts_ref, ids_ref, probs_ref, hid_ref, cot_ref = held
     top, toks = ids_ref.shape
-    d_model = cot_ref.shape[1]
     per_home = local_count * SLOT
     homes = dev_count * per_home
     slots = homes + dev_count * CAPR
@@ -222,9 +221,27 @@
     ps_ref[...] = jnp.broadcast_to(p_slot, ps_ref.shape)
     scaled = p_slot * h_slot
     moves[5].wait()
+    pack_rows(homes, per_home, packing, pick, scaled, cot_ref, packed)
+
+
+def pack_rows(homes, per_home, packing, pick, scaled, cot_ref, packed):
+    d_model = cot_ref.shape[1]
+    for out_ref, blocks in zip(packed, packing):
+        spans = [(homes, pick.shape[0]) if b == COPIES else (b * per_home, (b + 1) * per_home) for b in blocks]
+        chosen, extra = (jnp.concatenate([v[i:j] for i, j in spans], axis=0) for v in (pick, scaled))
+        rows = jnp.dot(chosen.astype(BF16), cot_ref[...], preferred_element_type=F32)
+        out_ref[:, :d_model] = rows.astype(BF16)
+        out_ref[:, d_model:] = extra.astype(BF16)
+
+
+def pack_kernel(local_count, dev_count, packing, pick_ref, hs_ref, ps_ref, cot_ref, *packed):
+    d_model = cot_ref.shape[1]
+    per_home = local_count * SLOT
+    homes = dev_count * per_home
+    pick, scaled = pick_ref[...], ps_ref[...] * hs_ref[...]
     rows = jnp.dot(pick.astype(BF16), cot_ref[...], preferred_element_type=F32)
     for out_ref, blocks in zip(packed, packing):
-        spans = [(homes, slots) if b == COPIES else (b * per_home, (b + 1) * per_home) for b in blocks]
+        spans = [(homes, pick.shape[0]) if b == COPIES else (b * per_home, (b + 1) * per_home) for b in blocks]
         out_ref[:, :d_model] = jnp.concatenate([rows[i:j] for i, j in spans], axis=0).astype(BF16)
         out_ref[:, d_model:] = jnp.concatenate([scaled[i:j] for i, j in spans], axis=0).astype(BF16)
 
@@ -265,11 +282,11 @@
     return own
 
 
-def early_kernel(local_count, dev_count, order, pieces, replica_ref, w_hbm, *refs):
-    piece_refs, (rows_ref, w_ref, slot_ref, own_ref, sem) = refs[:-5], refs[-5:]
+def hold_kernel(local_count, dev_count, replica_ref, w_hbm, home_ref, copy_ref, rows_ref, w_ref, slot_ref, sem):
     fetch = pltpu.make_async_copy(w_hbm, w_ref, sem)
     fetch.start()
     per_home, per_copy = local_count * SLOT, dev_count * CAPR
+    rows_ref[...] = jnp.concatenate([home_ref[...].astype(F32), copy_ref[...].astype(F32)], axis=0).astype(BF16)
     first = lax.axis_index("expert") * local_count
     width = slot_ref.shape[1]
     slot_ref[:per_home] = iota((per_home, width), 0) // SLOT
@@ -279,8 +296,13 @@
         mine = (row >= d * CAPR) & (row < (d + 1) * CAPR)
         copy = jnp.where(mine, replica_ref[d] - first, copy)
     slot_ref[per_home:] = copy
+    fetch.wait()
+
+
+def early_kernel(local_count, dev_count, order, pieces, w_ref, slot_ref, *refs):
+    piece_refs, (rows_ref, own_ref) = refs[:-2], refs[-2:]
+    per_home, per_copy = local_count * SLOT, dev_count * CAPR
     fill_rows(order, pieces, per_home, per_copy, piece_refs, rows_ref)
-    fetch.wait()
     slot = slots_of(order, slot_ref, per_home, rows_ref.shape[0])
     own_ref[...] = own_columns(rows_ref, w_ref, slot, local_count)
 
@@ -384,54 +406,69 @@
     sources = (replica_of, send_counts, ids, probs.T, hidden.reshape(toks * top, width), cotangent)
     per_home = local_count * SLOT
     firsts = [1 << n for n in reversed(range(dev_count.bit_length() - 1))]
-    riders = {low: [low] + [low + 1] * (low == 2) for low in firsts if low < firsts[0]}
-    packing = [[COPIES] + riders.get(low, [])[::-1] for low in firsts]
-    direct = [m for m in range(1, dev_count) if not any(m in ride for ride in riders.values())]
+    packing = [[COPIES, low | 1] for low in firsts]
+    direct = [m for m in reversed(range(1, dev_count)) if m not in [low | 1 for low in firsts]]
     packing += [[0], [COPIES]] + [[m] for m in direct]
     sized = [sum(copies if b == COPIES else per_home for b in blocks) for blocks in packing]
     pick, expert, h_slot, p_slot, *packed = call(
-        functools.partial(dispatch_kernel, *sizes, packing),
+        functools.partial(dispatch_kernel, *sizes, packing[:1]),
         [shape((slots, toks), F32), shape((slots, toks), jnp.int32), shape((slots, width), F32),
-         shape((slots, width), F32)] + [shape((n, d_model + width), BF16) for n in sized],
+         shape((slots, width), F32)] + [shape((n, d_model + width), BF16) for n in sized[:1]],
         [(hbm, a) for a in sources],
         [(smem if n < 2 else vmem)(a.shape, a.dtype) for n, a in enumerate(sources)]
         + [vmem((toks * top, width), F32), pltpu.SemaphoreType.DMA((len(sources),))],
         flops=2 * slots * toks * d_model,
         limit=60,
     )
-    pieces, arrays = {(0, HOME): (0, 0), (0, COPIES): (1, 0)}, packed[len(firsts):len(firsts) + 2]
-    arrived = [swap(a, low, dev_count) for a, low in zip(packed, firsts)]
-    arrived, packed, arrays = lax.optimization_barrier((arrived, packed, arrays))
-    passing = {}
-    for low, a in zip(firsts, arrived):
-        pieces[low, COPIES] = (len(arrays), 0)
-        if low in riders:
-            pieces[low, HOME] = (len(arrays), a.shape[0] - per_home)
-        passing[low] = a[:a.shape[0] - per_home] if low in riders else a
-        arrays.append(a)
+    packed += call(
+        functools.partial(pack_kernel, *sizes, packing[1:]),
+        [shape((n, d_model + width), BF16) for n in sized[1:]],
+        [(vmem, a) for a in (pick, h_slot, p_slot, cotangent)],
+        flops=2 * slots * toks * d_model,
+        limit=60,
+    )
     flat_w = weights.reshape(local_count * width, d_model)
+    own_rows, w_held, slot = call(
+        functools.partial(hold_kernel, *sizes),
+        (shape((per_home + copies, d_model + width), BF16), shape(flat_w.shape, BF16),
+         shape((per_home + copies, width), jnp.int32)),
+        [(smem, replica_of), (hbm, flat_w)] + [(vmem, a) for a in packed[len(firsts):len(firsts) + 2]],
+        [pltpu.SemaphoreType.DMA(())],
+    )
+    direct = dict(zip(direct, packed[len(firsts) + 2:]))
+    first_in = {low: swap(a, low, dev_count) for a, low in zip(packed, firsts)}
+    passing = {low: swap(a, 1, dev_count) for low, a in first_in.items() if 1 < low < firsts[0]}
+    first_in, direct, own_rows, w_held, slot = lax.optimization_barrier((first_in, direct, own_rows, w_held, slot))
+    far = first_in[firsts[0]]
+    low_three = [low for low in firsts[1:] if low > 1]
+    onward = {firsts[0] | low: swap(far[:copies], low, dev_count) for low in low_three}
+    if firsts[0] > 1:
+        passing[firsts[0]] = swap(far, 1, dev_count)
+    direct_in = {m: swap(direct[m], m, dev_count) for m in direct if m > firsts[0]}
+    pieces = {(0, HOME): (0, 0), (0, COPIES): (0, per_home), (1, COPIES): (len(firsts), 0), (1, HOME): (len(firsts), copies)}
+    pieces.update({(low, COPIES): (1 + n, 0) for n, low in enumerate(firsts)})
     orders = [list(pieces)]
     height = padded(sum(per_home if kind == HOME else copies for _, kind in pieces))
-    early_rows, w_held, slot, own = call(
+    early_rows, own = call(
         functools.partial(early_kernel, *sizes, orders[0], pieces),
-        (shape((height, d_model + width), BF16), shape(flat_w.shape, BF16),
-         shape((per_home + copies, width), jnp.int32), shape((height, width), F32)),
-        [(smem, replica_of), (hbm, flat_w)] + [(vmem, a) for a in arrays],
-        [pltpu.SemaphoreType.DMA(())],
+        (shape((height, d_model + width), BF16), shape((height, width), F32)),
+        [(vmem, a) for a in (w_held, slot, own_rows, *(first_in[low] for low in firsts))],
         flops=2 * height * d_model * local_count * width,
     )
+    passing[firsts[0]], direct_in, direct, early_rows, own = lax.optimization_barrier(
+        (passing[firsts[0]], direct_in, direct, early_rows, own))
+    last = {m | 1: swap(passing[firsts[0]][:copies], m ^ firsts[0], dev_count) for m in onward}
+    direct_in.update({m: swap(direct[m], m, dev_count) for m in direct if m < firsts[0] or m == firsts[0]})
     pieces, arrays = {}, []
-    for m in sorted(range(1, dev_count), key=lambda m: (m.bit_count(), -m)):
-        low = m & -m
-        if m != low:
-            passing[m] = swap(passing[m ^ low], low, dev_count)
-            pieces[m, COPIES] = (len(arrays), 0)
-            if passing[m].shape[0] > copies:
-                pieces[m, HOME] = (len(arrays), copies)
-            arrays.append(passing[m])
-    for m, a in zip(direct, packed[len(firsts) + 2:]):
-        pieces[m, HOME] = (len(arrays), 0)
-        arrays.append(swap(a, m, dev_count))
+    for blocks in (passing, onward, last, direct_in):
+        for m, a in blocks.items():
+            if blocks is direct_in:
+                pieces[m, HOME] = (len(arrays), 0)
+            elif blocks is passing:
+                pieces[m | 1, COPIES], pieces[m | 1, HOME] = (len(arrays), 0), (len(arrays), copies)
+            else:
+                pieces[m, COPIES] = (len(arrays), 0)
+            arrays.append(a)
     orders.append(list(pieces))
     height = padded(sum(per_home if kind == HOME else copies for _, kind in pieces))
     late_rows, back = call(
@@ -476,7 +513,7 @@
     dev_count = lax.axis_size("expert")
     local_count, width, _ = weights.shape
     gathered = dev_count * dev_count * CAPR
-    if gathered <= (local_count + 3) * width and dev_count.bit_count() == 1 and lax.axis_size("dp") == 2:
+    if gathered <= (local_count + 3) * width and dev_count == 8 and lax.axis_size("dp") == 2:
         run = gather_body
     else:
         run = replica_body

time: 58.5 us -> 56 us (0.957)
  starting transfers between devices: 27.5 us -> 19.8 us
  waiting for transfers between devices: 16.2 us -> 21.2 us
  Pallas kernels: 9.77 us -> 12 us
  local copies, waits for them, and re-layouts: 3.94 us -> 1.82 us
    ppermute x11, starting transfers between devices: 23.6 us -> 15.6 us  [swap(): return lax.ppermute(x, 'expert', [(i, i ^ bits) for i in range(count)])]
    ppermute x11, waiting for transfers between devices: 10.9 us -> 16 us  [swap(): return lax.ppermute(x, 'expert', [(i, i ^ bits) for i in range(count)])]
    pallas_call x6 -> x8, Pallas kernels: 9.77 us -> 12 us  [call(): pl.pallas_call(kernel, out_shape=out_shape, in_specs=[pl.BlockSpec(memory...]
    unnamed x18 -> x26, local copies, waits for them, and re-layouts: 3.92 us -> 1.79 us
  transfers between devices with their start and end apart: 13 -> 13, of which waited for: 5 -> 7; matrix products, arithmetic and copies ran while one was open for 0% -> 0% of each run, Pallas kernels for 5% -> 10%
where the time goes in v6:
time: 56 us; the launch traced here: 55.6 us
  waiting for transfers between devices  21.2 us (38%)
  starting transfers between devices  19.8 us (35%)
  Pallas kernels  12 us (21%)
  local copies, waits for them, and re-layouts  1.82 us (3%)
  between operations  0.8 us (1%)
    ppermute x11, waiting for transfers between devices, swap(): return lax.ppermute(x, 'expert', [(i, i ^ bits) for i in range(count)])  16 us
    ppermute x11, starting transfers between devices, swap(): return lax.ppermute(x, 'expert', [(i, i ^ bits) for i in range(count)])  15.6 us
    pallas_call x8, Pallas kernels, call(): pl.pallas_call(kernel, out_shape=out_shape, in_specs=[pl.BlockSpec(memory...  12 us
    all_to_all x1, waiting for transfers between devices, gather_body(): lax.all_to_all(back, 'expert', split_axis=0, concat_axis=0, tiled=True)  5.24 us
    all_to_all x1, starting transfers between devices, gather_body(): lax.all_to_all(back, 'expert', split_axis=0, concat_axis=0, tiled=True)  4.21 us
    unnamed x26, local copies, waits for them, and re-layouts  1.79 us
  transfers between devices with their start and end apart: 13, of which 7 were waited for; matrix products, arithmetic and copies ran while one was open for 0% of the time, Pallas kernels for 10%

profile of v6, /device:TPU:0, one launch (start us, length us, event | category | flops | bytes accessed | tf_op | source)
XLA Modules:
  0.0 55.6 jit_solution(11245264721467934003)
XLA Ops:
  0.6 0.0 copy-start.8
  0.6 0.0 copy-start
  0.7 2.5 %shard_map.94 = (f32[88,128]{1,0:T(8,128)}, s32[88,128]{1,0:T(8,128)}, f32[88,128]{1,0:T(8,128)}, f32[88,128]{1,0:T(8,128)}, bf16[32,3712]{1,0:T(8,128)(2,1)}) custom-call(s32[8]{0:T(128)} %replica_ref.1, s32[1,8]{1,0:T(1,128)} %refs_1_.1, s32[8,128]{1,0:T(8,128)} %bitcast.9, bf16[8,128]{1,0:T(8,128)(2,1)} %bitcast.13, bf16[1024,128]{1,0:T(8,128)(2,1)} %bitcast.12, ...), custom_call_target="tpu_custom_call" | custom-call | flops 80740352 | bytes 1603648 | tf_op jit(solution)/shard_map/pallas_call | solution.py:376
  3.1 4.1 %collective-permute-start.2 = (bf16[32,3712]{1,0:T(8,128)(2,1)}, bf16[32,3712]{1,0:T(8,128)(2,1)S(1)}, u32[]{:S(2)}, u32[]{:S(2)}) collective-permute-start(bf16[32,3712]{1,0:T(8,128)(2,1)} %get-tuple-element.49), channel_id=1, source_target_pairs={{0,8},{2,10},{4,12},{6,14},{8,0},{10,2},{12,4},{14,6},{1,9},{3,11}... | collective-permute-start | bytes 712712 | tf_op jit(solution)/shard_map/ppermute | solution.py:388
  7.2 2.5 %shard_map.95 = (bf16[32,3712]{1,0:T(8,128)(2,1)}, bf16[32,3712]{1,0:T(8,128)(2,1)}, bf16[8,3712]{1,0:T(8,128)(2,1)}, bf16[24,3712]{1,0:T(8,128)(2,1)}, bf16[8,3...) custom-call(f32[88,128]{1,0:T(8,128)} %get-tuple-element.80.pick_ref, ...), custom_call_target="tpu_custom_call" | custom-call | flops 80740352 | bytes 2002944 | tf_op jit(solution)/shard_map/pallas_call | solution.py:376
  9.7 1.5 %collective-permute-start = (bf16[32,3712]{1,0:T(8,128)(2,1)}, bf16[32,3712]{1,0:T(8,128)(2,1)S(1)}, u32[]{:S(2)}, u32[]{:S(2)}) collective-permute-start(bf16[32,3712]{1,0:T(8,128)(2,1)} %get-tuple-element.47), channel_id=1, source_target_pairs={{0,2},{2,0},{4,6},{6,4},{8,10},{10,8},{12,14},{14,12},{1,3},{3,1},... | collective-permute-start | bytes 712712 | tf_op jit(solution)/shard_map/ppermute | solution.py:388
  11.2 1.6 %collective-permute-start.1 = (bf16[32,3712]{1,0:T(8,128)(2,1)}, bf16[32,3712]{1,0:T(8,128)(2,1)S(1)}, u32[]{:S(2)}, u32[]{:S(2)}) collective-permute-start(bf16[32,3712]{1,0:T(8,128)(2,1)} %get-tuple-element.48), channel_id=1, source_target_pairs={{0,4},{2,6},{4,0},{6,2},{8,12},{10,14},{12,8},{14,10},{1,5},{3,7},... | collective-permute-start | bytes 712712 | tf_op jit(solution)/shard_map/ppermute | solution.py:388
  12.8 0.0 copy-done.8
  12.8 0.0 copy-done
  12.8 0.0 copy-start.4
  12.8 0.9 %copy-done.4 = bf16[24,3712]{1,0:T(8,128)(2,1)S(1)} copy-done((bf16[24,3712]{1,0:T(8,128)(2,1)S(1)}, bf16[24,3712]{1,0:T(8,128)(2,1)}, u32[]{:S(2)}) %copy-start.4) | copy-done | bytes 178200
  13.7 0.0 copy-start.5
  13.7 0.8 %copy-done.5 = bf16[8,3712]{1,0:T(8,128)(2,1)S(1)} copy-done((bf16[8,3712]{1,0:T(8,128)(2,1)S(1)}, bf16[8,3712]{1,0:T(8,128)(2,1)}, u32[]{:S(2)}) %copy-start.5) | copy-done | bytes 59416
  14.6 0.0 copy-start.12
  14.6 0.0 copy-start.11
  14.6 0.7 %shard_map.96 = (bf16[32,3712]{1,0:T(8,128)(2,1)S(1)}, bf16[256,3584]{1,0:T(8,128)(2,1)S(1)}, s32[32,128]{1,0:T(8,128)S(1)}) custom-call(s32[8]{0:T(128)S(1)} %copy-done.8, bf16[256,3584]{1,0:T(8,128)(2,1)S(1)} %bitcast.8, bf16[8,3712]{1,0:T(8,128)(2,1)S(1)} %copy-done.5, bf16[24,3712]{1,0:T(8,128)(2,1)S(1)} %copy-done.4), custom_call_target="tpu_custom_call" | custom-call | bytes 4161568 | tf_op jit(solution)/shard_map/pallas_call | solution.py:376
  15.3 0.0 copy-start.10
  15.3 0.0 copy-start.9
  15.3 3.1 %collective-permute-done.2.refs_1_ = bf16[32,3712]{1,0:T(8,128)(2,1)S(1)} collective-permute-done((bf16[32,3712]{1,0:T(8,128)(2,1)}, bf16[32,3712]{1,0:T(8,128)(2,1)S(1)}, u32[]{:S(2)}, u32[]{:S(2)}) %collective-permute-start.2) | collective-permute-done | bytes 237600 | tf_op jit(solution)/shard_map/ppermute | solution.py:388
  18.4 0.0 collective-permute-done.refs_3_
  18.4 3.9 %collective-permute-done.1.refs_2_ = bf16[32,3712]{1,0:T(8,128)(2,1)S(1)} collective-permute-done((bf16[32,3712]{1,0:T(8,128)(2,1)}, bf16[32,3712]{1,0:T(8,128)(2,1)S(1)}, u32[]{:S(2)}, u32[]{:S(2)}) %collective-permute-start.1) | collective-permute-done | bytes 237600 | tf_op jit(solution)/shard_map/ppermute | solution.py:388
  22.3 0.6 %collective-permute-start.3 = (bf16[32,3712]{1,0:T(8,128)(2,1)S(1)}, bf16[32,3712]{1,0:T(8,128)(2,1)S(1)}, u32[]{:S(2)}, u32[]{:S(2)}) collective-permute-start(bf16[32,3712]{1,0:T(8,128)(2,1)S(1)} %collective-permute-done.2.refs_1_), channel_id=1, source_target_pairs={{0,2},{2,0},{4,6},{6,4},{8,10},{10,8},{12,14},{14,12},{1,3},{3,1},... | collective-permute-start | bytes 712712 | tf_op jit(solution)/shard_map/ppermute | solution.py:388
  22.9 0.0 copy-done.12
  22.9 2.4 %collective-permute-start.4 = (bf16[8,3712]{1,0:T(8,128)(2,1)S(1)}, bf16[8,3712]{1,0:T(8,128)(2,1)S(1)}, u32[]{:S(2)}, u32[]{:S(2)}) collective-permute-start(bf16[8,3712]{1,0:T(8,128)(2,1)S(1)} %copy-done.12), channel_id=1, source_target_pairs={{0,12},{2,14},{4,8},{6,10},{8,4},{10,6},{12,0},{14,2},{1,13},{3,15... | collective-permute-start | bytes 178184 | tf_op jit(solution)/shard_map/ppermute | solution.py:388
  25.3 0.0 copy-done.11
  25.3 2.3 %collective-permute-start.5 = (bf16[8,3712]{1,0:T(8,128)(2,1)S(1)}, bf16[8,3712]{1,0:T(8,128)(2,1)S(1)}, u32[]{:S(2)}, u32[]{:S(2)}) collective-permute-start(bf16[8,3712]{1,0:T(8,128)(2,1)S(1)} %copy-done.11), channel_id=1, source_target_pairs={{0,14},{2,12},{4,10},{6,8},{8,6},{10,4},{12,2},{14,0},{1,15},{3,13... | collective-permute-start | bytes 178184 | tf_op jit(solution)/shard_map/ppermute | solution.py:388
  27.6 0.6 %collective-permute-start.6 = (bf16[32,3712]{1,0:T(8,128)(2,1)S(1)}, bf16[32,3712]{1,0:T(8,128)(2,1)S(1)}, u32[]{:S(2)}, u32[]{:S(2)}) collective-permute-start(bf16[32,3712]{1,0:T(8,128)(2,1)S(1)} %collective-permute-done.1.refs_2_), channel_id=1, source_target_pairs={{0,2},{2,0},{4,6},{6,4},{8,10},{10,8},{12,14},{14,12},{1,3},{3,1},... | collective-permute-start | bytes 712712 | tf_op jit(solution)/shard_map/ppermute | solution.py:388
  28.2 0.1 collective-permute-start.7
  28.3 0.7 %shard_map.97 = (bf16[112,3712]{1,0:T(8,128)(2,1)S(1)}, f32[112,128]{1,0:T(8,128)S(1)}) custom-call(bf16[256,3584]{1,0:T(8,128)(2,1)S(1)} %get-tuple-element.64.w_ref, s32[32,128]{1,0:T(8,128)S(1)} %get-tuple-element.65.slot_ref, bf16[32,3712]{1,0:T(8,128)(2,1)S(1)} %get-tuple-element.66.refs_0_, bf16[32,3712]{1,0:T(8,128)(2,1)S(1)} %collective-permute-done.2.refs_1_, ...), custom_call_target="tpu_custom_call" | custom-call | flops 205520896 | bytes 3690496 | tf_op jit(solution)/shard_map/pallas_call | solution.py:376
  29.0 0.6 %collective-permute-done.4.refs_4_ = bf16[8,3712]{1,0:T(8,128)(2,1)S(1)} collective-permute-done((bf16[8,3712]{1,0:T(8,128)(2,1)S(1)}, bf16[8,3712]{1,0:T(8,128)(2,1)S(1)}, u32[]{:S(2)}, u32[]{:S(2)}) %collective-permute-start.4) | collective-permute-done | bytes 59424 | tf_op jit(solution)/shard_map/ppermute | solution.py:388
  29.6 2.9 %collective-permute-done.5.refs_5_ = bf16[8,3712]{1,0:T(8,128)(2,1)S(1)} collective-permute-done((bf16[8,3712]{1,0:T(8,128)(2,1)S(1)}, bf16[8,3712]{1,0:T(8,128)(2,1)S(1)}, u32[]{:S(2)}, u32[]{:S(2)}) %collective-permute-start.5) | collective-permute-done | bytes 59424 | tf_op jit(solution)/shard_map/ppermute | solution.py:388
  32.5 0.0 collective-permute-done.3.refs_1_
  32.5 0.1 collective-permute-start.8
  32.6 0.0 copy-done.10
  32.6 2.0 %collective-permute-start.9 = (bf16[8,3712]{1,0:T(8,128)(2,1)S(1)}, bf16[8,3712]{1,0:T(8,128)(2,1)S(1)}, u32[]{:S(2)}, u32[]{:S(2)}) collective-permute-start(bf16[8,3712]{1,0:T(8,128)(2,1)S(1)} %copy-done.10), channel_id=1, source_target_pairs={{0,4},{2,6},{4,0},{6,2},{8,12},{10,14},{12,8},{14,10},{1,5},{3,7},... | collective-permute-start | bytes 178184 | tf_op jit(solution)/shard_map/ppermute | solution.py:388
  34.6 0.0 copy-done.9
  34.6 0.4 collective-permute-start.10
  35.0 1.6 %collective-permute-done.7.refs_2_ = bf16[24,3712]{1,0:T(8,128)(2,1)S(1)} collective-permute-done((bf16[24,3712]{1,0:T(8,128)(2,1)S(1)}, bf16[24,3712]{1,0:T(8,128)(2,1)S(1)}, u32[]{:S(2)}, u32[]{:S(2)}) %collective-permute-start.7) | collective-permute-done | bytes 178208 | tf_op jit(solution)/shard_map/ppermute | solution.py:388
  36.7 0.0 collective-permute-done.6.refs_0_
  36.7 3.8 %collective-permute-done.9.refs_6_ = bf16[8,3712]{1,0:T(8,128)(2,1)S(1)} collective-permute-done((bf16[8,3712]{1,0:T(8,128)(2,1)S(1)}, bf16[8,3712]{1,0:T(8,128)(2,1)S(1)}, u32[]{:S(2)}, u32[]{:S(2)}) %collective-permute-start.9) | collective-permute-done | bytes 59424 | tf_op jit(solution)/shard_map/ppermute | solution.py:388
  40.5 0.0 collective-permute-done.10.refs_7_
  40.5 0.0 collective-permute-done.8.refs_3_
  40.5 1.4 %shard_map.98 = (bf16[144,3712]{1,0:T(8,128)(2,1)S(1)}, bf16[256,128]{1,0:T(8,128)(2,1)}) custom-call(f32[112,128]{1,0:T(8,128)S(1)} %get-tuple-element.71.own_ref, bf16[256,3584]{1,0:T(8,128)(2,1)S(1)} %get-tuple-element.64.w_ref, s32[32,128]{1,0:T(8,128)S(1)} %get-tuple-element.65.slot_ref, bf16[32,3712]{1,0:T(8,128)(2,1)S(1)} %collective-permute-done.6.refs_0_, ...), custom_call_target="tpu_custom_call" | custom-call | flops 264241152 | bytes 4112384 | tf_op jit(solution)/shard_map/pallas_call | solution.py:376
  41.9 1.6 %shard_map.99 = bf16[256,1792]{1,0:T(8,128)(2,1)} custom-call(s32[32,128]{1,0:T(8,128)S(1)} %get-tuple-element.65.slot_ref, bf16[112,3712]{1,0:T(8,128)(2,1)S(1)} %get-tuple-element.78.early_ref, bf16[144,3712]{1,0:T(8,128)(2,1)S(1)} %get-tuple-element.79.late_ref), custom_call_target="tpu_custom_call" | custom-call | flops 234881024 | bytes 2834432 | tf_op jit(solution)/shard_map/pallas_call | solution.py:376
  43.5 0.0 collective-permute-start.11
  43.5 4.2 %all-to-all-start = ((bf16[8,32,128]{2,1,0:T(8,128)(2,1)}), bf16[8,32,128]{2,1,0:T(8,128)(2,1)S(1)}, u32[]{:S(2)}, u32[]{:S(2)}) async-start(bf16[8,32,128]{2,1,0:T(8,128)(2,1)} %bitcast.4), calls=%async_computation | async-start | bytes 131072 | tf_op jit(solution)/shard_map/all_to_all | solution.py:481
  47.7 0.0 copy-start.1
  47.7 0.0 copy-start.2
  47.7 0.0 copy-start.3
  47.7 0.0 copy-start.6
  47.7 0.0 copy-start.7
  47.7 0.0 collective-permute-done.11.arrived_ref
  47.8 1.6 %shard_map.100 = bf16[256,1792]{1,0:T(8,128)(2,1)} custom-call(s32[32,128]{1,0:T(8,128)S(1)} %get-tuple-element.65.slot_ref, bf16[112,3712]{1,0:T(8,128)(2,1)S(1)} %get-tuple-element.78.early_ref, bf16[144,3712]{1,0:T(8,128)(2,1)S(1)} %get-tuple-element.79.late_ref, bf16[256,1792]{1,0:T(8,128)(2,1)S(1)} %collective-permute-done.11.arrived_ref), custom_call_target="tpu_custom_call" | custom-call | flops 234881024 | bytes 3751936 | tf_op jit(solution)/shard_map/pallas_call | solution.py:376
  49.4 5.2 %all-to-all-done.back_ref = bf16[8,32,128]{2,1,0:T(8,128)(2,1)S(1)} async-done(((bf16[8,32,128]{2,1,0:T(8,128)(2,1)}), bf16[8,32,128]{2,1,0:T(8,128)(2,1)S(1)}, u32[]{:S(2)}, u32[]{:S(2)}) %all-to-all-start) | async-done | bytes 65568 | tf_op jit(solution)/shard_map/all_to_all | solution.py:481
  54.6 0.0 copy-done.1
  54.6 0.0 copy-done.2
  54.6 0.0 copy-done.3
  54.6 0.0 copy-done.6
  54.6 0.0 copy-done.7
  54.6 1.0 %shard_map.101 = (bf16[1024,128]{1,0:T(8,128)(2,1)}, bf16[8,128]{1,0:T(8,128)(2,1)}) custom-call(bf16[8,32,128]{2,1,0:T(8,128)(2,1)S(1)} %all-to-all-done.back_ref, f32[88,128]{1,0:T(8,128)S(1)} %copy-done.1, s32[88,128]{1,0:T(8,128)S(1)} %copy-done.6, f32[88,128]{1,0:T(8,128)S(1)} %copy-done.2, f32[88,128]{1,0:T(8,128)S(1)} %copy-done.3, s32[8,128]{1,0:T(8,128)S(1)} %bitcast.10), custom_call_target="tpu_custom_call" | custom-call | flops 23068672 | bytes 514048 | tf_op jit(solution)/shard_map/pallas_call | solution.py:376
  (2 shorter events, 0.0 us)
Async XLA Ops:
  0.6 12.2 %copy-start.8 = (s32[8]{0:T(128)S(1)}, s32[8]{0:T(128)}, u32[]{:S(2)}) copy-start(s32[8]{0:T(128)} %replica_ref.1) | copy-start | bytes 100
  0.6 12.2 %copy-start = (bf16[2,128,3584]{2,1,0:T(8,128)(2,1)S(1)}, bf16[2,128,3584]{2,1,0:T(8,128)(2,1)}, u32[]{:S(2)}) copy-start(bf16[2,128,3584]{2,1,0:T(8,128)(2,1)} %param.13) | copy-start | bytes 5505028
  3.1 15.3 %collective-permute-start.2 = (bf16[32,3712]{1,0:T(8,128)(2,1)}, bf16[32,3712]{1,0:T(8,128)(2,1)S(1)}, u32[]{:S(2)}, u32[]{:S(2)}) collective-permute-start(bf16[32,3712]{1,0:T(8,128)(2,1)} %get-tuple-element.49), channel_id=1, source_target_pairs={{0,8},{2,10},{4,12},{6,14},{8,0},{10,2},{12,4},{14,6},{1,9},{3,11}... | collective-permute-start | bytes 712712 | tf_op jit(solution)/shard_map/ppermute | solution.py:388
  9.7 8.7 %collective-permute-start = (bf16[32,3712]{1,0:T(8,128)(2,1)}, bf16[32,3712]{1,0:T(8,128)(2,1)S(1)}, u32[]{:S(2)}, u32[]{:S(2)}) collective-permute-start(bf16[32,3712]{1,0:T(8,128)(2,1)} %get-tuple-element.47), channel_id=1, source_target_pairs={{0,2},{2,0},{4,6},{6,4},{8,10},{10,8},{12,14},{14,12},{1,3},{3,1},... | collective-permute-start | bytes 712712 | tf_op jit(solution)/shard_map/ppermute | solution.py:388
  11.2 11.1 %collective-permute-start.1 = (bf16[32,3712]{1,0:T(8,128)(2,1)}, bf16[32,3712]{1,0:T(8,128)(2,1)S(1)}, u32[]{:S(2)}, u32[]{:S(2)}) collective-permute-start(bf16[32,3712]{1,0:T(8,128)(2,1)} %get-tuple-element.48), channel_id=1, source_target_pairs={{0,4},{2,6},{4,0},{6,2},{8,12},{10,14},{12,8},{14,10},{1,5},{3,7},... | collective-permute-start | bytes 712712 | tf_op jit(solution)/shard_map/ppermute | solution.py:388
  12.8 0.9 %copy-start.4 = (bf16[24,3712]{1,0:T(8,128)(2,1)S(1)}, bf16[24,3712]{1,0:T(8,128)(2,1)}, u32[]{:S(2)}) copy-start(bf16[24,3712]{1,0:T(8,128)(2,1)} %get-tuple-element.55.copy_ref) | copy-start | bytes 534532
  13.7 0.8 %copy-start.5 = (bf16[8,3712]{1,0:T(8,128)(2,1)S(1)}, bf16[8,3712]{1,0:T(8,128)(2,1)}, u32[]{:S(2)}) copy-start(bf16[8,3712]{1,0:T(8,128)(2,1)} %get-tuple-element.54.home_ref) | copy-start | bytes 178180
  14.6 8.3 %copy-start.12 = (bf16[8,3712]{1,0:T(8,128)(2,1)S(1)}, bf16[8,3712]{1,0:T(8,128)(2,1)}, u32[]{:S(2)}) copy-start(bf16[8,3712]{1,0:T(8,128)(2,1)} %get-tuple-element.60) | copy-start | bytes 178180
  14.6 10.7 %copy-start.11 = (bf16[8,3712]{1,0:T(8,128)(2,1)S(1)}, bf16[8,3712]{1,0:T(8,128)(2,1)}, u32[]{:S(2)}) copy-start(bf16[8,3712]{1,0:T(8,128)(2,1)} %get-tuple-element.61) | copy-start | bytes 178180
  15.3 17.3 %copy-start.10 = (bf16[8,3712]{1,0:T(8,128)(2,1)S(1)}, bf16[8,3712]{1,0:T(8,128)(2,1)}, u32[]{:S(2)}) copy-start(bf16[8,3712]{1,0:T(8,128)(2,1)} %get-tuple-element.75) | copy-start | bytes 178180
  15.3 19.3 %copy-start.9 = (bf16[8,3712]{1,0:T(8,128)(2,1)S(1)}, bf16[8,3712]{1,0:T(8,128)(2,1)}, u32[]{:S(2)}) copy-start(bf16[8,3712]{1,0:T(8,128)(2,1)} %get-tuple-element.76) | copy-start | bytes 178180
  22.3 10.2 %collective-permute-start.3 = (bf16[32,3712]{1,0:T(8,128)(2,1)S(1)}, bf16[32,3712]{1,0:T(8,128)(2,1)S(1)}, u32[]{:S(2)}, u32[]{:S(2)}) collective-permute-start(bf16[32,3712]{1,0:T(8,128)(2,1)S(1)} %collective-permute-done.2.refs_1_), channel_id=1, source_target_pairs={{0,2},{2,0},{4,6},{6,4},{8,10},{10,8},{12,14},{14,12},{1,3},{3,1},... | collective-permute-start | bytes 712712 | tf_op jit(solution)/shard_map/ppermute | solution.py:388
  22.9 6.7 %collective-permute-start.4 = (bf16[8,3712]{1,0:T(8,128)(2,1)S(1)}, bf16[8,3712]{1,0:T(8,128)(2,1)S(1)}, u32[]{:S(2)}, u32[]{:S(2)}) collective-permute-start(bf16[8,3712]{1,0:T(8,128)(2,1)S(1)} %copy-done.12), channel_id=1, source_target_pairs={{0,12},{2,14},{4,8},{6,10},{8,4},{10,6},{12,0},{14,2},{1,13},{3,15... | collective-permute-start | bytes 178184 | tf_op jit(solution)/shard_map/ppermute | solution.py:388
  25.3 7.2 %collective-permute-start.5 = (bf16[8,3712]{1,0:T(8,128)(2,1)S(1)}, bf16[8,3712]{1,0:T(8,128)(2,1)S(1)}, u32[]{:S(2)}, u32[]{:S(2)}) collective-permute-start(bf16[8,3712]{1,0:T(8,128)(2,1)S(1)} %copy-done.11), channel_id=1, source_target_pairs={{0,14},{2,12},{4,10},{6,8},{8,6},{10,4},{12,2},{14,0},{1,15},{3,13... | collective-permute-start | bytes 178184 | tf_op jit(solution)/shard_map/ppermute | solution.py:388
  27.6 9.1 %collective-permute-start.6 = (bf16[32,3712]{1,0:T(8,128)(2,1)S(1)}, bf16[32,3712]{1,0:T(8,128)(2,1)S(1)}, u32[]{:S(2)}, u32[]{:S(2)}) collective-permute-start(bf16[32,3712]{1,0:T(8,128)(2,1)S(1)} %collective-permute-done.1.refs_2_), channel_id=1, source_target_pairs={{0,2},{2,0},{4,6},{6,4},{8,10},{10,8},{12,14},{14,12},{1,3},{3,1},... | collective-permute-start | bytes 712712 | tf_op jit(solution)/shard_map/ppermute | solution.py:388
  28.2 8.5 %collective-permute-start.7 = (bf16[24,3712]{1,0:T(8,128)(2,1)S(1)}, bf16[24,3712]{1,0:T(8,128)(2,1)S(1)}, u32[]{:S(2)}, u32[]{:S(2)}) collective-permute-start(bf16[24,3712]{1,0:T(8,128)(2,1)S(1)} %slice.6), channel_id=1, source_target_pairs={{0,4},{2,6},{4,0},{6,2},{8,12},{10,14},{12,8},{14,10},{1,5},{3,7},... | collective-permute-start | bytes 534536 | tf_op jit(solution)/shard_map/ppermute | solution.py:388
  32.5 8.0 %collective-permute-start.8 = (bf16[24,3712]{1,0:T(8,128)(2,1)S(1)}, bf16[24,3712]{1,0:T(8,128)(2,1)S(1)}, u32[]{:S(2)}, u32[]{:S(2)}) collective-permute-start(bf16[24,3712]{1,0:T(8,128)(2,1)S(1)} %slice.7), channel_id=1, source_target_pairs={{0,4},{2,6},{4,0},{6,2},{8,12},{10,14},{12,8},{14,10},{1,5},{3,7},... | collective-permute-start | bytes 534536 | tf_op jit(solution)/shard_map/ppermute | solution.py:388
  32.6 7.9 %collective-permute-start.9 = (bf16[8,3712]{1,0:T(8,128)(2,1)S(1)}, bf16[8,3712]{1,0:T(8,128)(2,1)S(1)}, u32[]{:S(2)}, u32[]{:S(2)}) collective-permute-start(bf16[8,3712]{1,0:T(8,128)(2,1)S(1)} %copy-done.10), channel_id=1, source_target_pairs={{0,4},{2,6},{4,0},{6,2},{8,12},{10,14},{12,8},{14,10},{1,5},{3,7},... | collective-permute-start | bytes 178184 | tf_op jit(solution)/shard_map/ppermute | solution.py:388
  34.6 5.9 %collective-permute-start.10 = (bf16[8,3712]{1,0:T(8,128)(2,1)S(1)}, bf16[8,3712]{1,0:T(8,128)(2,1)S(1)}, u32[]{:S(2)}, u32[]{:S(2)}) collective-permute-start(bf16[8,3712]{1,0:T(8,128)(2,1)S(1)} %copy-done.9), channel_id=1, source_target_pairs={{0,8},{2,10},{4,12},{6,14},{8,0},{10,2},{12,4},{14,6},{1,9},{3,11}... | collective-permute-start | bytes 178184 | tf_op jit(solution)/shard_map/ppermute | solution.py:388
  43.5 4.3 %collective-permute-start.11 = (bf16[256,1792]{1,0:T(8,128)(2,1)}, bf16[256,1792]{1,0:T(8,128)(2,1)S(1)}, u32[]{:S(2)}, u32[]{:S(2)}) collective-permute-start(bf16[256,1792]{1,0:T(8,128)(2,1)} %shard_map.99), channel_id=1, source_target_pairs={{0,1},{1,0},{2,3},{3,2},{4,5},{5,4},{6,7},{7,6},{8,9},{9,8},{10,11... | collective-permute-start | bytes 2752520 | tf_op jit(solution)/shard_map/ppermute | solution.py:490
  43.5 11.1 %all-to-all-start = ((bf16[8,32,128]{2,1,0:T(8,128)(2,1)}), bf16[8,32,128]{2,1,0:T(8,128)(2,1)S(1)}, u32[]{:S(2)}, u32[]{:S(2)}) async-start(bf16[8,32,128]{2,1,0:T(8,128)(2,1)} %bitcast.4), calls=%async_computation | async-start | bytes 131072 | tf_op jit(solution)/shard_map/all_to_all | solution.py:481
  47.7 6.9 %copy-start.1 = (f32[88,128]{1,0:T(8,128)S(1)}, f32[88,128]{1,0:T(8,128)}, u32[]{:S(2)}) copy-start(f32[88,128]{1,0:T(8,128)} %get-tuple-element.80.pick_ref) | copy-start | bytes 135172
  47.7 6.9 %copy-start.2 = (f32[88,128]{1,0:T(8,128)S(1)}, f32[88,128]{1,0:T(8,128)}, u32[]{:S(2)}) copy-start(f32[88,128]{1,0:T(8,128)} %get-tuple-element.45.hs_ref) | copy-start | bytes 135172
  47.7 6.9 %copy-start.3 = (f32[88,128]{1,0:T(8,128)S(1)}, f32[88,128]{1,0:T(8,128)}, u32[]{:S(2)}) copy-start(f32[88,128]{1,0:T(8,128)} %get-tuple-element.46.ps_ref) | copy-start | bytes 135172
  47.7 6.9 %copy-start.6 = (s32[88,128]{1,0:T(8,128)S(1)}, s32[88,128]{1,0:T(8,128)}, u32[]{:S(2)}) copy-start(s32[88,128]{1,0:T(8,128)} %get-tuple-element.81.expert_ref) | copy-start | bytes 135172
  47.7 6.9 %copy-start.7 = (s32[128,8]{0,1:T(8,128)S(1)}, s32[128,8]{0,1:T(8,128)}, u32[]{:S(2)}) copy-start(s32[128,8]{0,1:T(8,128)} %param.10) | copy-start | bytes 12292

commit v7 on v5

--- a/solution.py
+++ b/solution.py
@@ -175,7 +175,6 @@
         move.start()
     replica_ref, counts_ref, ids_ref, probs_ref, hid_ref, cot_ref = held
     top, toks = ids_ref.shape
-    d_model = cot_ref.shape[1]
     per_home = local_count * SLOT
     homes = dev_count * per_home
     slots = homes + dev_count * CAPR
@@ -223,6 +222,7 @@
     scaled = p_slot * h_slot
     moves[5].wait()
     rows = jnp.dot(pick.astype(BF16), cot_ref[...], preferred_element_type=F32)
+    d_model = cot_ref.shape[1]
     for out_ref, blocks in zip(packed, packing):
         spans = [(homes, slots) if b == COPIES else (b * per_home, (b + 1) * per_home) for b in blocks]
         out_ref[:, :d_model] = jnp.concatenate([rows[i:j] for i, j in spans], axis=0).astype(BF16)
@@ -265,10 +265,12 @@
     return own
 
 
-def early_kernel(local_count, dev_count, order, pieces, replica_ref, w_hbm, *refs):
-    piece_refs, (rows_ref, w_ref, slot_ref, own_ref, sem) = refs[:-5], refs[-5:]
-    fetch = pltpu.make_async_copy(w_hbm, w_ref, sem)
-    fetch.start()
+def hold_kernel(local_count, dev_count, replica_ref, w_hbm, own_hbm, even_hbm,
+                own_ref, even_ref, w_ref, slot_ref, sems):
+    moves = [pltpu.make_async_copy(a, b, sems.at[n]) for n, (a, b) in enumerate(
+        ((w_hbm, w_ref), (own_hbm, own_ref), (even_hbm, even_ref)))]
+    for move in moves:
+        move.start()
     per_home, per_copy = local_count * SLOT, dev_count * CAPR
     first = lax.axis_index("expert") * local_count
     width = slot_ref.shape[1]
@@ -279,8 +281,24 @@
         mine = (row >= d * CAPR) & (row < (d + 1) * CAPR)
         copy = jnp.where(mine, replica_ref[d] - first, copy)
     slot_ref[per_home:] = copy
+    for move in moves:
+        move.wait()
+
+
+def turn_kernel(local_count, dev_count, beside_ref, far_ref, even_ref, *out_refs):
+    per_home, per_copy = local_count * SLOT, dev_count * CAPR
+    beside = beside_ref[per_copy + per_home:].astype(F32)
+    even = even_ref[...].astype(F32)
+    for n, out_ref in enumerate(out_refs):
+        span = slice(n * per_home, (n + 1) * per_home)
+        blocks = [far_ref[...].astype(F32)] * (n == 0) + [even[span], beside[span]]
+        out_ref[...] = jnp.concatenate(blocks, axis=0).astype(BF16)
+
+
+def early_kernel(local_count, dev_count, order, pieces, w_ref, slot_ref, *refs):
+    piece_refs, (rows_ref, own_ref) = refs[:-2], refs[-2:]
+    per_home, per_copy = local_count * SLOT, dev_count * CAPR
     fill_rows(order, pieces, per_home, per_copy, piece_refs, rows_ref)
-    fetch.wait()
     slot = slots_of(order, slot_ref, per_home, rows_ref.shape[0])
     own_ref[...] = own_columns(rows_ref, w_ref, slot, local_count)
 
@@ -303,14 +321,14 @@
 
 def grad_weights_half(local_count, dev_count, orders, half, slot_ref, rows_refs, columns):
     start = pl.multiple_of(half * columns, 128)
-    total = None
+    spread = []
     for order, ref in zip(orders, rows_refs):
         slot = slots_of(order, slot_ref, local_count * SLOT, ref.shape[0])
         scaled = ref[:, 2 * columns:].astype(F32)
-        spread = jnp.concatenate([jnp.where(slot == e, scaled, 0.0) for e in range(local_count)], axis=1)
-        part = lax.dot_general(spread.astype(BF16), ref[:, pl.ds(start, columns)], TN, preferred_element_type=F32)
-        total = part if total is None else total + part
-    return total
+        spread.append(jnp.concatenate([jnp.where(slot == e, scaled, 0.0) for e in range(local_count)], axis=1))
+    rows = jnp.concatenate([ref[:, pl.ds(start, columns)] for ref in rows_refs], axis=0)
+    return lax.dot_general(
+        jnp.concatenate(spread, axis=0).astype(BF16), rows, TN, preferred_element_type=F32)
 
 
 def other_half_kernel(local_count, dev_count, orders, slot_ref, early_ref, late_ref, out_ref):
@@ -383,13 +401,10 @@
     hbm, vmem, smem = pltpu.HBM, pltpu.VMEM, pltpu.SMEM
     sources = (replica_of, send_counts, ids, probs.T, hidden.reshape(toks * top, width), cotangent)
     per_home = local_count * SLOT
-    firsts = [1 << n for n in reversed(range(dev_count.bit_length() - 1))]
-    riders = {low: [low] + [low + 1] * (low == 2) for low in firsts if low < firsts[0]}
-    packing = [[COPIES] + riders.get(low, [])[::-1] for low in firsts]
-    direct = [m for m in range(1, dev_count) if not any(m in ride for ride in riders.values())]
-    packing += [[0], [COPIES]] + [[m] for m in direct]
+    odd, even = range(1, dev_count, 2), range(2, dev_count, 2)
+    packing = [[COPIES, *odd], [COPIES], [0, COPIES], [*even]]
     sized = [sum(copies if b == COPIES else per_home for b in blocks) for blocks in packing]
-    pick, expert, h_slot, p_slot, *packed = call(
+    pick, expert, h_slot, p_slot, to_beside, copy_rows, own_rows, even_rows = call(
         functools.partial(dispatch_kernel, *sizes, packing),
         [shape((slots, toks), F32), shape((slots, toks), jnp.int32), shape((slots, width), F32),
          shape((slots, width), F32)] + [shape((n, d_model + width), BF16) for n in sized],
@@ -399,39 +414,42 @@
         flops=2 * slots * toks * d_model,
         limit=60,
     )
-    pieces, arrays = {(0, HOME): (0, 0), (0, COPIES): (1, 0)}, packed[len(firsts):len(firsts) + 2]
-    arrived = [swap(a, low, dev_count) for a, low in zip(packed, firsts)]
-    arrived, packed, arrays = lax.optimization_barrier((arrived, packed, arrays))
-    passing = {}
-    for low, a in zip(firsts, arrived):
-        pieces[low, COPIES] = (len(arrays), 0)
-        if low in riders:
-            pieces[low, HOME] = (len(arrays), a.shape[0] - per_home)
-        passing[low] = a[:a.shape[0] - per_home] if low in riders else a
-        arrays.append(a)
+    beside = swap(to_beside, 1, dev_count)
+    far = swap(copy_rows, 4, dev_count)
+    near = swap(copy_rows, 2, dev_count)
     flat_w = weights.reshape(local_count * width, d_model)
+    own_rows, even_rows, w_held, slot = call(
+        functools.partial(hold_kernel, *sizes),
+        [shape(a.shape, BF16) for a in (own_rows, even_rows, flat_w)] + [shape((per_home + copies, width), jnp.int32)],
+        [(smem, replica_of)] + [(hbm, a) for a in (flat_w, own_rows, even_rows)],
+        [pltpu.SemaphoreType.DMA((3,))],
+    )
+    beside, far, near, own_rows, even_rows, w_held, slot = lax.optimization_barrier(
+        (beside, far, near, own_rows, even_rows, w_held, slot))
+    far_beside = swap(far, 1, dev_count)
+    turned = call(
+        functools.partial(turn_kernel, *sizes),
+        [shape((copies * (m == 2) + 2 * per_home, d_model + width), BF16) for m in even],
+        [(vmem, a) for a in (beside, far, even_rows)],
+    )
+    turned = [swap(a, m, dev_count) for a, m in zip(turned, even)]
+    near_beside = swap(near, 1, dev_count)
+    pieces = {(0, HOME): (0, 0), (0, COPIES): (0, per_home), (1, COPIES): (1, 0), (1, HOME): (1, copies),
+              (2, COPIES): (2, 0), (4, COPIES): (3, 0)}
     orders = [list(pieces)]
     height = padded(sum(per_home if kind == HOME else copies for _, kind in pieces))
-    early_rows, w_held, slot, own = call(
+    early_rows, own = call(
         functools.partial(early_kernel, *sizes, orders[0], pieces),
-        (shape((height, d_model + width), BF16), shape(flat_w.shape, BF16),
-         shape((per_home + copies, width), jnp.int32), shape((height, width), F32)),
-        [(smem, replica_of), (hbm, flat_w)] + [(vmem, a) for a in arrays],
-        [pltpu.SemaphoreType.DMA(())],
+        (shape((height, d_model + width), BF16), shape((height, width), F32)),
+        [(vmem, a) for a in (w_held, slot, own_rows, beside, near, far)],
         flops=2 * height * d_model * local_count * width,
     )
-    pieces, arrays = {}, []
-    for m in sorted(range(1, dev_count), key=lambda m: (m.bit_count(), -m)):
-        low = m & -m
-        if m != low:
-            passing[m] = swap(passing[m ^ low], low, dev_count)
-            pieces[m, COPIES] = (len(arrays), 0)
-            if passing[m].shape[0] > copies:
-                pieces[m, HOME] = (len(arrays), copies)
-            arrays.append(passing[m])
-    for m, a in zip(direct, packed[len(firsts) + 2:]):
-        pieces[m, HOME] = (len(arrays), 0)
-        arrays.append(swap(a, m, dev_count))
+    far_beside, early_rows, own, turned[2] = lax.optimization_barrier((far_beside, early_rows, own, turned[2]))
+    far_across = swap(far_beside, 2, dev_count)
+    arrays = [far_beside, near_beside, far_across, *turned]
+    pieces = {(5, COPIES): (0, 0), (3, COPIES): (1, 0), (7, COPIES): (2, 0), (6, COPIES): (3, 0)}
+    for n, m in enumerate(even):
+        pieces[m, HOME], pieces[m + 1, HOME] = ((3 + n, copies * (m == 2) + k * per_home) for k in range(2))
     orders.append(list(pieces))
     height = padded(sum(per_home if kind == HOME else copies for _, kind in pieces))
     late_rows, back = call(
@@ -476,7 +494,7 @@
     dev_count = lax.axis_size("expert")
     local_count, width, _ = weights.shape
     gathered = dev_count * dev_count * CAPR
-    if gathered <= (local_count + 3) * width and dev_count.bit_count() == 1 and lax.axis_size("dp") == 2:
+    if gathered <= (local_count + 3) * width and dev_count == 8 and lax.axis_size("dp") == 2:
         run = gather_body
     else:
         run = replica_body

time: 58.5 us -> 51.4 us (0.88)
  starting transfers between devices: 27.5 us -> 18.8 us
  waiting for transfers between devices: 16.2 us -> 17.7 us
    ppermute x11 -> x9, starting transfers between devices: 23.6 us -> 15 us  [swap(): return lax.ppermute(x, 'expert', [(i, i ^ bits) for i in range(count)])]
    ppermute x11 -> x9, waiting for transfers between devices: 10.9 us -> 12.2 us  [swap(): return lax.ppermute(x, 'expert', [(i, i ^ bits) for i in range(count)])]
    pallas_call x6 -> x8, Pallas kernels: 9.77 us -> 9.8 us  [call(): pl.pallas_call(kernel, out_shape=out_shape, in_specs=[pl.BlockSpec(memory...]
  transfers between devices with their start and end apart: 13 -> 11, of which waited for: 5 -> 6; matrix products, arithmetic and copies ran while one was open for 0% -> 0% of each run, Pallas kernels for 5% -> 7%
where the time goes in v7:
time: 51.4 us; the launch traced here: 51 us
  starting transfers between devices  18.8 us (37%)
  waiting for transfers between devices  17.7 us (34%)
  Pallas kernels  9.8 us (19%)
  local copies, waits for them, and re-layouts  4.04 us (8%)
  between operations  0.74 us (1%)
    ppermute x9, starting transfers between devices, swap(): return lax.ppermute(x, 'expert', [(i, i ^ bits) for i in range(count)])  15 us
    ppermute x9, waiting for transfers between devices, swap(): return lax.ppermute(x, 'expert', [(i, i ^ bits) for i in range(count)])  12.2 us
    pallas_call x8, Pallas kernels, call(): pl.pallas_call(kernel, out_shape=out_shape, in_specs=[pl.BlockSpec(memory...  9.8 us
    all_to_all x1, waiting for transfers between devices, gather_body(): lax.all_to_all(back, 'expert', split_axis=0, concat_axis=0, tiled=True)  5.47 us
    unnamed x18, local copies, waits for them, and re-layouts  4.04 us
    all_to_all x1, starting transfers between devices, gather_body(): lax.all_to_all(back, 'expert', split_axis=0, concat_axis=0, tiled=True)  3.75 us
  transfers between devices with their start and end apart: 11, of which 6 were waited for; matrix products, arithmetic and copies ran while one was open for 0% of the time, Pallas kernels for 7%

profile of v7, /device:TPU:0, one launch (start us, length us, event | category | flops | bytes accessed | tf_op | source)
XLA Modules:
  0.0 51.0 jit_solution(14309199923006602281)
XLA Ops:
  0.6 2.7 %shard_map.94 = (f32[88,128]{1,0:T(8,128)}, s32[88,128]{1,0:T(8,128)}, f32[88,128]{1,0:T(8,128)}, f32[88,128]{1,0:T(8,128)}, bf16[56,3712]{1,0:T(8,128)(2,1)}, /...) custom-call(s32[8]{0:T(128)} %replica_ref.1, s32[1,8]{1,0:T(1,128)} %refs_1_.1, ...), custom_call_target="tpu_custom_call" | custom-call | flops 80740352 | bytes 2375744 | tf_op jit(solution)/shard_map/pallas_call | solution.py:372
  3.3 3.0 %collective-permute-start = (bf16[56,3712]{1,0:T(8,128)(2,1)}, bf16[56,3712]{1,0:T(8,128)(2,1)S(1)}, u32[]{:S(2)}, u32[]{:S(2)}) collective-permute-start(bf16[56,3712]{1,0:T(8,128)(2,1)} %get-tuple-element.37), channel_id=1, source_target_pairs={{0,2},{2,0},{4,6},{6,4},{8,10},{10,8},{12,14},{14,12},{1,3},{3,1},... | collective-permute-start | bytes 1247240 | tf_op jit(solution)/shard_map/ppermute | solution.py:384
  6.3 1.6 %collective-permute-start.2 = (bf16[24,3712]{1,0:T(8,128)(2,1)}, bf16[24,3712]{1,0:T(8,128)(2,1)S(1)}, u32[]{:S(2)}, u32[]{:S(2)}) collective-permute-start(bf16[24,3712]{1,0:T(8,128)(2,1)} %get-tuple-element.38), channel_id=1, source_target_pairs={{0,4},{2,6},{4,0},{6,2},{8,12},{10,14},{12,8},{14,10},{1,5},{3,7},... | collective-permute-start | bytes 534536 | tf_op jit(solution)/shard_map/ppermute | solution.py:384
  7.9 2.6 %collective-permute-start.1 = (bf16[24,3712]{1,0:T(8,128)(2,1)}, bf16[24,3712]{1,0:T(8,128)(2,1)S(1)}, u32[]{:S(2)}, u32[]{:S(2)}) collective-permute-start(bf16[24,3712]{1,0:T(8,128)(2,1)} %get-tuple-element.38), channel_id=1, source_target_pairs={{0,8},{2,10},{4,12},{6,14},{8,0},{10,2},{12,4},{14,6},{1,9},{3,11}... | collective-permute-start | bytes 534536 | tf_op jit(solution)/shard_map/ppermute | solution.py:384
  10.5 0.0 copy-start
  10.5 1.5 %copy-done = bf16[2,128,3584]{2,1,0:T(8,128)(2,1)S(1)} copy-done((bf16[2,128,3584]{2,1,0:T(8,128)(2,1)S(1)}, bf16[2,128,3584]{2,1,0:T(8,128)(2,1)}, u32[]{:S(2)}) %copy-start) | copy-done | bytes 1835032
  12.0 0.0 copy-start.1
  12.0 0.9 %copy-done.1 = bf16[32,3712]{1,0:T(8,128)(2,1)S(1)} copy-done((bf16[32,3712]{1,0:T(8,128)(2,1)S(1)}, bf16[32,3712]{1,0:T(8,128)(2,1)}, u32[]{:S(2)}) %copy-start.1) | copy-done | bytes 237592
  12.9 0.0 copy-start.2
  12.9 0.9 %copy-done.2 = bf16[24,3712]{1,0:T(8,128)(2,1)S(1)} copy-done((bf16[24,3712]{1,0:T(8,128)(2,1)S(1)}, bf16[24,3712]{1,0:T(8,128)(2,1)}, u32[]{:S(2)}) %copy-start.2) | copy-done | bytes 178200
  13.8 0.0 copy-start.8
  13.8 0.7 %copy-done.8 = s32[8]{0:T(128)S(1)} copy-done((s32[8]{0:T(128)S(1)}, s32[8]{0:T(128)}, u32[]{:S(2)}) %copy-start.8) | copy-done | bytes 56
  14.5 1.2 %shard_map.95 = (bf16[32,3712]{1,0:T(8,128)(2,1)S(1)}, bf16[24,3712]{1,0:T(8,128)(2,1)S(1)}, bf16[256,3584]{1,0:T(8,128)(2,1)S(1)}, s32[32,128]{1,0:T(8,128)S(1)}) custom-call(s32[8]{0:T(128)S(1)} %copy-done.8, bf16[256,3584]{1,0:T(8,128)(2,1)S(1)} %bitcast.8, bf16[32,3712]{1,0:T(8,128)(2,1)S(1)} %copy-done.1, bf16[24,3712]{1,0:T(8,128)(2,1)S(1)} %copy-done.2), custom_call_target="tpu_custom_call" | custom-call | bytes 4517920 | tf_op jit(solution)/shard_map/pallas_call | solution.py:372
  15.7 0.4 collective-permute-done.2.refs_2_
  16.2 2.4 %collective-permute-done.1.refs_3_.far_ref = bf16[24,3712]{1,0:T(8,128)(2,1)S(1)} collective-permute-done((bf16[24,3712]{1,0:T(8,128)(2,1)}, bf16[24,3712]{1,0:T(8,128)(2,1)S(1)}, u32[]{:S(2)}, u32[]{:S(2)}) %collective-permute-start.1) | collective-permute-done | bytes 178208 | tf_op jit(solution)/shard_map/ppermute | solution.py:384
  18.6 0.0 collective-permute-done.refs_1_.beside_ref
  18.6 0.5 %collective-permute-start.3 = (bf16[24,3712]{1,0:T(8,128)(2,1)S(1)}, bf16[24,3712]{1,0:T(8,128)(2,1)S(1)}, u32[]{:S(2)}, u32[]{:S(2)}) collective-permute-start(bf16[24,3712]{1,0:T(8,128)(2,1)S(1)} %collective-permute-done.1.refs_3_.far_ref), channel_id=1, source_target_pairs={{0,2},{2,0},{4,6},{6,4},{8,10},{10,8},{12,14},{14,12},{1,3},{3,1},... | collective-permute-start | bytes 534536 | tf_op jit(solution)/shard_map/ppermute | solution.py:384
  19.2 2.5 %collective-permute-start.4 = (bf16[16,3712]{1,0:T(8,128)(2,1)S(1)}, bf16[16,3712]{1,0:T(8,128)(2,1)S(1)}, u32[]{:S(2)}, u32[]{:S(2)}) collective-permute-start(bf16[16,3712]{1,0:T(8,128)(2,1)S(1)} %get-tuple-element.54), channel_id=1, source_target_pairs={{0,12},{2,14},{4,8},{6,10},{8,4},{10,6},{12,0},{14,2},{1,13},{3,15... | collective-permute-start | bytes 356360 | tf_op jit(solution)/shard_map/ppermute | solution.py:384
  21.7 0.0 collective-permute-start.7
  21.7 1.5 %collective-permute-start.5 = (bf16[24,3712]{1,0:T(8,128)(2,1)S(1)}, bf16[24,3712]{1,0:T(8,128)(2,1)S(1)}, u32[]{:S(2)}, u32[]{:S(2)}) collective-permute-start(bf16[24,3712]{1,0:T(8,128)(2,1)S(1)} %collective-permute-done.2.refs_2_), channel_id=1, source_target_pairs={{0,2},{2,0},{4,6},{6,4},{8,10},{10,8},{12,14},{14,12},{1,3},{3,1},... | collective-permute-start | bytes 534536 | tf_op jit(solution)/shard_map/ppermute | solution.py:384
  23.2 0.7 %shard_map.96 = (bf16[112,3712]{1,0:T(8,128)(2,1)S(1)}, f32[112,128]{1,0:T(8,128)S(1)}) custom-call(bf16[256,3584]{1,0:T(8,128)(2,1)S(1)} %get-tuple-element.46.w_ref, s32[32,128]{1,0:T(8,128)S(1)} %get-tuple-element.47.slot_ref, bf16[32,3712]{1,0:T(8,128)(2,1)S(1)} %get-tuple-element.48.refs_0_, ...), custom_call_target="tpu_custom_call" | custom-call | flops 205520896 | bytes 3749888 | tf_op jit(solution)/shard_map/pallas_call | solution.py:372
  23.9 3.1 %collective-permute-done.4.refs_5_ = bf16[16,3712]{1,0:T(8,128)(2,1)S(1)} collective-permute-done((bf16[16,3712]{1,0:T(8,128)(2,1)S(1)}, bf16[16,3712]{1,0:T(8,128)(2,1)S(1)}, u32[]{:S(2)}, u32[]{:S(2)}) %collective-permute-start.4) | collective-permute-done | bytes 118816 | tf_op jit(solution)/shard_map/ppermute | solution.py:384
  27.0 0.0 collective-permute-done.3.refs_0_
  27.0 0.0 collective-permute-start.6
  27.0 3.3 %collective-permute-start.8 = (bf16[16,3712]{1,0:T(8,128)(2,1)S(1)}, bf16[16,3712]{1,0:T(8,128)(2,1)S(1)}, u32[]{:S(2)}, u32[]{:S(2)}) collective-permute-start(bf16[16,3712]{1,0:T(8,128)(2,1)S(1)} %get-tuple-element.58), channel_id=1, source_target_pairs={{0,8},{2,10},{4,12},{6,14},{8,0},{10,2},{12,4},{14,6},{1,9},{3,11}... | collective-permute-start | bytes 356360 | tf_op jit(solution)/shard_map/ppermute | solution.py:384
  30.3 5.3 %collective-permute-done.8.refs_4_ = bf16[16,3712]{1,0:T(8,128)(2,1)S(1)} collective-permute-done((bf16[16,3712]{1,0:T(8,128)(2,1)S(1)}, bf16[16,3712]{1,0:T(8,128)(2,1)S(1)}, u32[]{:S(2)}, u32[]{:S(2)}) %collective-permute-start.8) | collective-permute-done | bytes 118816 | tf_op jit(solution)/shard_map/ppermute | solution.py:384
  35.6 0.0 collective-permute-done.5.refs_1_
  35.6 0.0 collective-permute-done.7.refs_3_
  35.6 0.9 %collective-permute-done.6.refs_2_ = bf16[24,3712]{1,0:T(8,128)(2,1)S(1)} collective-permute-done((bf16[24,3712]{1,0:T(8,128)(2,1)S(1)}, bf16[24,3712]{1,0:T(8,128)(2,1)S(1)}, u32[]{:S(2)}, u32[]{:S(2)}) %collective-permute-start.6) | collective-permute-done | bytes 178208 | tf_op jit(solution)/shard_map/ppermute | solution.py:384
  36.6 1.4 %shard_map.98 = (bf16[144,3712]{1,0:T(8,128)(2,1)S(1)}, bf16[256,128]{1,0:T(8,128)(2,1)}) custom-call(f32[112,128]{1,0:T(8,128)S(1)} %get-tuple-element.55.own_ref, bf16[256,3584]{1,0:T(8,128)(2,1)S(1)} %get-tuple-element.46.w_ref, s32[32,128]{1,0:T(8,128)S(1)} %get-tuple-element.47.slot_ref, bf16[24,3712]{1,0:T(8,128)(2,1)S(1)} %collective-permute-done.3.refs_0_, ...), custom_call_target="tpu_custom_call" | custom-call | flops 264241152 | bytes 4112384 | tf_op jit(solution)/shard_map/pallas_call | solution.py:372
  38.0 1.4 %shard_map.99 = bf16[256,1792]{1,0:T(8,128)(2,1)} custom-call(s32[32,128]{1,0:T(8,128)S(1)} %get-tuple-element.47.slot_ref, bf16[112,3712]{1,0:T(8,128)(2,1)S(1)} %get-tuple-element.61.early_ref, bf16[144,3712]{1,0:T(8,128)(2,1)S(1)} %get-tuple-element.62.late_ref), custom_call_target="tpu_custom_call" | custom-call | flops 234881024 | bytes 2834432 | tf_op jit(solution)/shard_map/pallas_call | solution.py:372
  39.3 0.0 collective-permute-start.9
  39.3 3.7 %all-to-all-start = ((bf16[8,32,128]{2,1,0:T(8,128)(2,1)}), bf16[8,32,128]{2,1,0:T(8,128)(2,1)S(1)}, u32[]{:S(2)}, u32[]{:S(2)}) async-start(bf16[8,32,128]{2,1,0:T(8,128)(2,1)} %bitcast.4), calls=%async_computation | async-start | bytes 131072 | tf_op jit(solution)/shard_map/all_to_all | solution.py:462
  43.1 0.0 copy-start.3
  43.1 0.0 copy-start.4
  43.1 0.0 copy-start.5
  43.1 0.0 copy-start.6
  43.1 0.0 copy-start.7
  43.1 0.0 collective-permute-done.9.arrived_ref
  43.2 1.4 %shard_map.100 = bf16[256,1792]{1,0:T(8,128)(2,1)} custom-call(s32[32,128]{1,0:T(8,128)S(1)} %get-tuple-element.47.slot_ref, bf16[112,3712]{1,0:T(8,128)(2,1)S(1)} %get-tuple-element.61.early_ref, bf16[144,3712]{1,0:T(8,128)(2,1)S(1)} %get-tuple-element.62.late_ref, bf16[256,1792]{1,0:T(8,128)(2,1)S(1)} %collective-permute-done.9.arrived_ref), custom_call_target="tpu_custom_call" | custom-call | flops 234881024 | bytes 3751936 | tf_op jit(solution)/shard_map/pallas_call | solution.py:372
  44.5 5.5 %all-to-all-done.back_ref = bf16[8,32,128]{2,1,0:T(8,128)(2,1)S(1)} async-done(((bf16[8,32,128]{2,1,0:T(8,128)(2,1)}), bf16[8,32,128]{2,1,0:T(8,128)(2,1)S(1)}, u32[]{:S(2)}, u32[]{:S(2)}) %all-to-all-start) | async-done | bytes 65568 | tf_op jit(solution)/shard_map/all_to_all | solution.py:462
  50.0 0.0 copy-done.3
  50.0 0.0 copy-done.4
  50.0 0.0 copy-done.5
  50.0 0.0 copy-done.6
  50.0 0.0 copy-done.7
  50.0 1.0 %shard_map.101 = (bf16[1024,128]{1,0:T(8,128)(2,1)}, bf16[8,128]{1,0:T(8,128)(2,1)}) custom-call(bf16[8,32,128]{2,1,0:T(8,128)(2,1)S(1)} %all-to-all-done.back_ref, f32[88,128]{1,0:T(8,128)S(1)} %copy-done.3, s32[88,128]{1,0:T(8,128)S(1)} %copy-done.4, f32[88,128]{1,0:T(8,128)S(1)} %copy-done.5, f32[88,128]{1,0:T(8,128)S(1)} %copy-done.6, s32[8,128]{1,0:T(8,128)S(1)} %bitcast.10), custom_call_target="tpu_custom_call" | custom-call | flops 23068672 | bytes 514048 | tf_op jit(solution)/shard_map/pallas_call | solution.py:372
  (1 shorter events, 0.0 us)
Async XLA Ops:
  3.3 15.3 %collective-permute-start = (bf16[56,3712]{1,0:T(8,128)(2,1)}, bf16[56,3712]{1,0:T(8,128)(2,1)S(1)}, u32[]{:S(2)}, u32[]{:S(2)}) collective-permute-start(bf16[56,3712]{1,0:T(8,128)(2,1)} %get-tuple-element.37), channel_id=1, source_target_pairs={{0,2},{2,0},{4,6},{6,4},{8,10},{10,8},{12,14},{14,12},{1,3},{3,1},... | collective-permute-start | bytes 1247240 | tf_op jit(solution)/shard_map/ppermute | solution.py:384
  6.3 9.9 %collective-permute-start.2 = (bf16[24,3712]{1,0:T(8,128)(2,1)}, bf16[24,3712]{1,0:T(8,128)(2,1)S(1)}, u32[]{:S(2)}, u32[]{:S(2)}) collective-permute-start(bf16[24,3712]{1,0:T(8,128)(2,1)} %get-tuple-element.38), channel_id=1, source_target_pairs={{0,4},{2,6},{4,0},{6,2},{8,12},{10,14},{12,8},{14,10},{1,5},{3,7},... | collective-permute-start | bytes 534536 | tf_op jit(solution)/shard_map/ppermute | solution.py:384
  7.9 10.7 %collective-permute-start.1 = (bf16[24,3712]{1,0:T(8,128)(2,1)}, bf16[24,3712]{1,0:T(8,128)(2,1)S(1)}, u32[]{:S(2)}, u32[]{:S(2)}) collective-permute-start(bf16[24,3712]{1,0:T(8,128)(2,1)} %get-tuple-element.38), channel_id=1, source_target_pairs={{0,8},{2,10},{4,12},{6,14},{8,0},{10,2},{12,4},{14,6},{1,9},{3,11}... | collective-permute-start | bytes 534536 | tf_op jit(solution)/shard_map/ppermute | solution.py:384
  10.5 1.5 %copy-start = (bf16[2,128,3584]{2,1,0:T(8,128)(2,1)S(1)}, bf16[2,128,3584]{2,1,0:T(8,128)(2,1)}, u32[]{:S(2)}) copy-start(bf16[2,128,3584]{2,1,0:T(8,128)(2,1)} %param.13) | copy-start | bytes 5505028
  12.0 0.9 %copy-start.1 = (bf16[32,3712]{1,0:T(8,128)(2,1)S(1)}, bf16[32,3712]{1,0:T(8,128)(2,1)}, u32[]{:S(2)}) copy-start(bf16[32,3712]{1,0:T(8,128)(2,1)} %get-tuple-element.39.own_hbm) | copy-start | bytes 712708
  12.9 0.9 %copy-start.2 = (bf16[24,3712]{1,0:T(8,128)(2,1)S(1)}, bf16[24,3712]{1,0:T(8,128)(2,1)}, u32[]{:S(2)}) copy-start(bf16[24,3712]{1,0:T(8,128)(2,1)} %get-tuple-element.40.even_hbm) | copy-start | bytes 534532
  13.8 0.7 %copy-start.8 = (s32[8]{0:T(128)S(1)}, s32[8]{0:T(128)}, u32[]{:S(2)}) copy-start(s32[8]{0:T(128)} %replica_ref.1) | copy-start | bytes 100
  18.6 8.4 %collective-permute-start.3 = (bf16[24,3712]{1,0:T(8,128)(2,1)S(1)}, bf16[24,3712]{1,0:T(8,128)(2,1)S(1)}, u32[]{:S(2)}, u32[]{:S(2)}) collective-permute-start(bf16[24,3712]{1,0:T(8,128)(2,1)S(1)} %collective-permute-done.1.refs_3_.far_ref), channel_id=1, source_target_pairs={{0,2},{2,0},{4,6},{6,4},{8,10},{10,8},{12,14},{14,12},{1,3},{3,1},... | collective-permute-start | bytes 534536 | tf_op jit(solution)/shard_map/ppermute | solution.py:384
  19.2 7.8 %collective-permute-start.4 = (bf16[16,3712]{1,0:T(8,128)(2,1)S(1)}, bf16[16,3712]{1,0:T(8,128)(2,1)S(1)}, u32[]{:S(2)}, u32[]{:S(2)}) collective-permute-start(bf16[16,3712]{1,0:T(8,128)(2,1)S(1)} %get-tuple-element.54), channel_id=1, source_target_pairs={{0,12},{2,14},{4,8},{6,10},{8,4},{10,6},{12,0},{14,2},{1,13},{3,15... | collective-permute-start | bytes 356360 | tf_op jit(solution)/shard_map/ppermute | solution.py:384
  21.7 14.0 %collective-permute-start.7 = (bf16[40,3712]{1,0:T(8,128)(2,1)S(1)}, bf16[40,3712]{1,0:T(8,128)(2,1)S(1)}, u32[]{:S(2)}, u32[]{:S(2)}) collective-permute-start(bf16[40,3712]{1,0:T(8,128)(2,1)S(1)} %get-tuple-element.57), channel_id=1, source_target_pairs={{0,4},{2,6},{4,0},{6,2},{8,12},{10,14},{12,8},{14,10},{1,5},{3,7},... | collective-permute-start | bytes 890888 | tf_op jit(solution)/shard_map/ppermute | solution.py:384
  21.7 14.0 %collective-permute-start.5 = (bf16[24,3712]{1,0:T(8,128)(2,1)S(1)}, bf16[24,3712]{1,0:T(8,128)(2,1)S(1)}, u32[]{:S(2)}, u32[]{:S(2)}) collective-permute-start(bf16[24,3712]{1,0:T(8,128)(2,1)S(1)} %collective-permute-done.2.refs_2_), channel_id=1, source_target_pairs={{0,2},{2,0},{4,6},{6,4},{8,10},{10,8},{12,14},{14,12},{1,3},{3,1},... | collective-permute-start | bytes 534536 | tf_op jit(solution)/shard_map/ppermute | solution.py:384
  27.0 9.6 %collective-permute-start.6 = (bf16[24,3712]{1,0:T(8,128)(2,1)S(1)}, bf16[24,3712]{1,0:T(8,128)(2,1)S(1)}, u32[]{:S(2)}, u32[]{:S(2)}) collective-permute-start(bf16[24,3712]{1,0:T(8,128)(2,1)S(1)} %collective-permute-done.3.refs_0_), channel_id=1, source_target_pairs={{0,4},{2,6},{4,0},{6,2},{8,12},{10,14},{12,8},{14,10},{1,5},{3,7},... | collective-permute-start | bytes 534536 | tf_op jit(solution)/shard_map/ppermute | solution.py:384
  27.0 8.6 %collective-permute-start.8 = (bf16[16,3712]{1,0:T(8,128)(2,1)S(1)}, bf16[16,3712]{1,0:T(8,128)(2,1)S(1)}, u32[]{:S(2)}, u32[]{:S(2)}) collective-permute-start(bf16[16,3712]{1,0:T(8,128)(2,1)S(1)} %get-tuple-element.58), channel_id=1, source_target_pairs={{0,8},{2,10},{4,12},{6,14},{8,0},{10,2},{12,4},{14,6},{1,9},{3,11}... | collective-permute-start | bytes 356360 | tf_op jit(solution)/shard_map/ppermute | solution.py:384
  39.3 3.8 %collective-permute-start.9 = (bf16[256,1792]{1,0:T(8,128)(2,1)}, bf16[256,1792]{1,0:T(8,128)(2,1)S(1)}, u32[]{:S(2)}, u32[]{:S(2)}) collective-permute-start(bf16[256,1792]{1,0:T(8,128)(2,1)} %shard_map.99), channel_id=1, source_target_pairs={{0,1},{1,0},{2,3},{3,2},{4,5},{5,4},{6,7},{7,6},{8,9},{9,8},{10,11... | collective-permute-start | bytes 2752520 | tf_op jit(solution)/shard_map/ppermute | solution.py:471
  39.3 10.7 %all-to-all-start = ((bf16[8,32,128]{2,1,0:T(8,128)(2,1)}), bf16[8,32,128]{2,1,0:T(8,128)(2,1)S(1)}, u32[]{:S(2)}, u32[]{:S(2)}) async-start(bf16[8,32,128]{2,1,0:T(8,128)(2,1)} %bitcast.4), calls=%async_computation | async-start | bytes 131072 | tf_op jit(solution)/shard_map/all_to_all | solution.py:462
  43.1 6.9 %copy-start.3 = (f32[88,128]{1,0:T(8,128)S(1)}, f32[88,128]{1,0:T(8,128)}, u32[]{:S(2)}) copy-start(f32[88,128]{1,0:T(8,128)} %get-tuple-element.64.pick_ref) | copy-start | bytes 135172
  43.1 6.9 %copy-start.4 = (s32[88,128]{1,0:T(8,128)S(1)}, s32[88,128]{1,0:T(8,128)}, u32[]{:S(2)}) copy-start(s32[88,128]{1,0:T(8,128)} %get-tuple-element.65.expert_ref) | copy-start | bytes 135172
  43.1 6.9 %copy-start.5 = (f32[88,128]{1,0:T(8,128)S(1)}, f32[88,128]{1,0:T(8,128)}, u32[]{:S(2)}) copy-start(f32[88,128]{1,0:T(8,128)} %get-tuple-element.66.hs_ref) | copy-start | bytes 135172
  43.1 6.9 %copy-start.6 = (f32[88,128]{1,0:T(8,128)S(1)}, f32[88,128]{1,0:T(8,128)}, u32[]{:S(2)}) copy-start(f32[88,128]{1,0:T(8,128)} %get-tuple-element.67.ps_ref) | copy-start | bytes 135172
  43.1 6.9 %copy-start.7 = (s32[128,8]{0,1:T(8,128)S(1)}, s32[128,8]{0,1:T(8,128)}, u32[]{:S(2)}) copy-start(s32[128,8]{0,1:T(8,128)} %param.10) | copy-start | bytes 12292

commit v8 on v7

--- a/solution.py
+++ b/solution.py
@@ -442,10 +442,9 @@
         functools.partial(early_kernel, *sizes, orders[0], pieces),
         (shape((height, d_model + width), BF16), shape((height, width), F32)),
         [(vmem, a) for a in (w_held, slot, own_rows, beside, near, far)],
-        flops=2 * height * d_model * local_count * width,
-    )
-    far_beside, early_rows, own, turned[2] = lax.optimization_barrier((far_beside, early_rows, own, turned[2]))
-    far_across = swap(far_beside, 2, dev_count)
+        flops=2 * height * d_model * local_count * width * 30,
+    )
+    far_across = swap(turned[0][:copies], 1, dev_count)
     arrays = [far_beside, near_beside, far_across, *turned]
     pieces = {(5, COPIES): (0, 0), (3, COPIES): (1, 0), (7, COPIES): (2, 0), (6, COPIES): (3, 0)}
     for n, m in enumerate(even):

time: 51.4 us -> 50.5 us (0.982)
    ppermute x9, starting transfers between devices: 15 us -> 13.7 us  [swap(): return lax.ppermute(x, 'expert', [(i, i ^ bits) for i in range(count)])]
    all_to_all x1, starting transfers between devices: 3.75 us -> 4.62 us  [gather_body(): lax.all_to_all(back, 'expert', split_axis=0, concat_axis=0, tiled=True)]
where the time goes in v8:
time: 50.5 us; the launch traced here: 50.1 us
  starting transfers between devices  18.3 us (36%)
  waiting for transfers between devices  17.2 us (34%)
  Pallas kernels  9.8 us (19%)
  local copies, waits for them, and re-layouts  4.05 us (8%)
  between operations  0.76 us (2%)
    ppermute x9, starting transfers between devices, swap(): return lax.ppermute(x, 'expert', [(i, i ^ bits) for i in range(count)])  13.7 us
    ppermute x9, waiting for transfers between devices, swap(): return lax.ppermute(x, 'expert', [(i, i ^ bits) for i in range(count)])  11.7 us
    pallas_call x8, Pallas kernels, call(): pl.pallas_call(kernel, out_shape=out_shape, in_specs=[pl.BlockSpec(memory...  9.8 us
    all_to_all x1, waiting for transfers between devices, gather_body(): lax.all_to_all(back, 'expert', split_axis=0, concat_axis=0, tiled=True)  5.47 us
    all_to_all x1, starting transfers between devices, gather_body(): lax.all_to_all(back, 'expert', split_axis=0, concat_axis=0, tiled=True)  4.62 us
    unnamed x18, local copies, waits for them, and re-layouts  4.04 us
  transfers between devices with their start and end apart: 11, of which 6 were waited for; matrix products, arithmetic and copies ran while one was open for 0% of the time, Pallas kernels for 7%

profile of v8, /device:TPU:0, one launch (start us, length us, event | category | flops | bytes accessed | tf_op | source)
XLA Modules:
  0.0 50.1 jit_solution(5269512036473021450)
XLA Ops:
  0.6 2.7 %shard_map.94 = (f32[88,128]{1,0:T(8,128)}, s32[88,128]{1,0:T(8,128)}, f32[88,128]{1,0:T(8,128)}, f32[88,128]{1,0:T(8,128)}, bf16[56,3712]{1,0:T(8,128)(2,1)}, /...) custom-call(s32[8]{0:T(128)} %replica_ref.1, s32[1,8]{1,0:T(1,128)} %refs_1_.1, ...), custom_call_target="tpu_custom_call" | custom-call | flops 80740352 | bytes 2375744 | tf_op jit(solution)/shard_map/pallas_call | solution.py:372
  3.3 3.0 %collective-permute-start = (bf16[56,3712]{1,0:T(8,128)(2,1)}, bf16[56,3712]{1,0:T(8,128)(2,1)S(1)}, u32[]{:S(2)}, u32[]{:S(2)}) collective-permute-start(bf16[56,3712]{1,0:T(8,128)(2,1)} %get-tuple-element.33), channel_id=1, source_target_pairs={{0,2},{2,0},{4,6},{6,4},{8,10},{10,8},{12,14},{14,12},{1,3},{3,1},... | collective-permute-start | bytes 1247240 | tf_op jit(solution)/shard_map/ppermute | solution.py:384
  6.3 1.6 %collective-permute-start.2 = (bf16[24,3712]{1,0:T(8,128)(2,1)}, bf16[24,3712]{1,0:T(8,128)(2,1)S(1)}, u32[]{:S(2)}, u32[]{:S(2)}) collective-permute-start(bf16[24,3712]{1,0:T(8,128)(2,1)} %get-tuple-element.34), channel_id=1, source_target_pairs={{0,4},{2,6},{4,0},{6,2},{8,12},{10,14},{12,8},{14,10},{1,5},{3,7},... | collective-permute-start | bytes 534536 | tf_op jit(solution)/shard_map/ppermute | solution.py:384
  7.9 2.6 %collective-permute-start.1 = (bf16[24,3712]{1,0:T(8,128)(2,1)}, bf16[24,3712]{1,0:T(8,128)(2,1)S(1)}, u32[]{:S(2)}, u32[]{:S(2)}) collective-permute-start(bf16[24,3712]{1,0:T(8,128)(2,1)} %get-tuple-element.34), channel_id=1, source_target_pairs={{0,8},{2,10},{4,12},{6,14},{8,0},{10,2},{12,4},{14,6},{1,9},{3,11}... | collective-permute-start | bytes 534536 | tf_op jit(solution)/shard_map/ppermute | solution.py:384
  10.5 0.0 copy-start
  10.5 1.5 %copy-done = bf16[2,128,3584]{2,1,0:T(8,128)(2,1)S(1)} copy-done((bf16[2,128,3584]{2,1,0:T(8,128)(2,1)S(1)}, bf16[2,128,3584]{2,1,0:T(8,128)(2,1)}, u32[]{:S(2)}) %copy-start) | copy-done | bytes 1835032
  12.0 0.0 copy-start.1
  12.0 0.9 %copy-done.1 = bf16[32,3712]{1,0:T(8,128)(2,1)S(1)} copy-done((bf16[32,3712]{1,0:T(8,128)(2,1)S(1)}, bf16[32,3712]{1,0:T(8,128)(2,1)}, u32[]{:S(2)}) %copy-start.1) | copy-done | bytes 237592
  12.9 0.0 copy-start.2
  12.9 0.9 %copy-done.2 = bf16[24,3712]{1,0:T(8,128)(2,1)S(1)} copy-done((bf16[24,3712]{1,0:T(8,128)(2,1)S(1)}, bf16[24,3712]{1,0:T(8,128)(2,1)}, u32[]{:S(2)}) %copy-start.2) | copy-done | bytes 178200
  13.8 0.0 copy-start.8
  13.8 0.7 %copy-done.8 = s32[8]{0:T(128)S(1)} copy-done((s32[8]{0:T(128)S(1)}, s32[8]{0:T(128)}, u32[]{:S(2)}) %copy-start.8) | copy-done | bytes 56
  14.5 1.2 %shard_map.95 = (bf16[32,3712]{1,0:T(8,128)(2,1)S(1)}, bf16[24,3712]{1,0:T(8,128)(2,1)S(1)}, bf16[256,3584]{1,0:T(8,128)(2,1)S(1)}, s32[32,128]{1,0:T(8,128)S(1)}) custom-call(s32[8]{0:T(128)S(1)} %copy-done.8, bf16[256,3584]{1,0:T(8,128)(2,1)S(1)} %bitcast.8, bf16[32,3712]{1,0:T(8,128)(2,1)S(1)} %copy-done.1, bf16[24,3712]{1,0:T(8,128)(2,1)S(1)} %copy-done.2), custom_call_target="tpu_custom_call" | custom-call | bytes 4517920 | tf_op jit(solution)/shard_map/pallas_call | solution.py:372
  15.7 0.4 collective-permute-done.2.refs_2_
  16.2 2.4 %collective-permute-done.1.refs_3_.far_ref = bf16[24,3712]{1,0:T(8,128)(2,1)S(1)} collective-permute-done((bf16[24,3712]{1,0:T(8,128)(2,1)}, bf16[24,3712]{1,0:T(8,128)(2,1)S(1)}, u32[]{:S(2)}, u32[]{:S(2)}) %collective-permute-start.1) | collective-permute-done | bytes 178208 | tf_op jit(solution)/shard_map/ppermute | solution.py:384
  18.6 0.0 collective-permute-done.refs_1_.beside_ref
  18.6 0.5 collective-permute-start.5
  19.1 0.5 %collective-permute-start.3 = (bf16[24,3712]{1,0:T(8,128)(2,1)S(1)}, bf16[24,3712]{1,0:T(8,128)(2,1)S(1)}, u32[]{:S(2)}, u32[]{:S(2)}) collective-permute-start(bf16[24,3712]{1,0:T(8,128)(2,1)S(1)} %collective-permute-done.1.refs_3_.far_ref), channel_id=1, source_target_pairs={{0,2},{2,0},{4,6},{6,4},{8,10},{10,8},{12,14},{14,12},{1,3},{3,1},... | collective-permute-start | bytes 534536 | tf_op jit(solution)/shard_map/ppermute | solution.py:384
  19.6 1.5 %collective-permute-start.4 = (bf16[24,3712]{1,0:T(8,128)(2,1)S(1)}, bf16[24,3712]{1,0:T(8,128)(2,1)S(1)}, u32[]{:S(2)}, u32[]{:S(2)}) collective-permute-start(bf16[24,3712]{1,0:T(8,128)(2,1)S(1)} %collective-permute-done.2.refs_2_), channel_id=1, source_target_pairs={{0,2},{2,0},{4,6},{6,4},{8,10},{10,8},{12,14},{14,12},{1,3},{3,1},... | collective-permute-start | bytes 534536 | tf_op jit(solution)/shard_map/ppermute | solution.py:384
  21.1 2.6 %collective-permute-start.7 = (bf16[16,3712]{1,0:T(8,128)(2,1)S(1)}, bf16[16,3712]{1,0:T(8,128)(2,1)S(1)}, u32[]{:S(2)}, u32[]{:S(2)}) collective-permute-start(bf16[16,3712]{1,0:T(8,128)(2,1)S(1)} %get-tuple-element.50), channel_id=1, source_target_pairs={{0,8},{2,10},{4,12},{6,14},{8,0},{10,2},{12,4},{14,6},{1,9},{3,11}... | collective-permute-start | bytes 356360 | tf_op jit(solution)/shard_map/ppermute | solution.py:384
  23.7 1.4 %collective-permute-start.8 = (bf16[16,3712]{1,0:T(8,128)(2,1)S(1)}, bf16[16,3712]{1,0:T(8,128)(2,1)S(1)}, u32[]{:S(2)}, u32[]{:S(2)}) collective-permute-start(bf16[16,3712]{1,0:T(8,128)(2,1)S(1)} %get-tuple-element.51), channel_id=1, source_target_pairs={{0,12},{2,14},{4,8},{6,10},{8,4},{10,6},{12,0},{14,2},{1,13},{3,15... | collective-permute-start | bytes 356360 | tf_op jit(solution)/shard_map/ppermute | solution.py:384
  25.1 4.1 %collective-permute-done.5.refs_3_ = bf16[40,3712]{1,0:T(8,128)(2,1)S(1)} collective-permute-done((bf16[40,3712]{1,0:T(8,128)(2,1)S(1)}, bf16[40,3712]{1,0:T(8,128)(2,1)S(1)}, u32[]{:S(2)}, u32[]{:S(2)}) %collective-permute-start.5) | collective-permute-done | bytes 296992 | tf_op jit(solution)/shard_map/ppermute | solution.py:384
  29.3 0.1 collective-permute-start.6
  29.3 0.7 %shard_map.96 = (bf16[112,3712]{1,0:T(8,128)(2,1)S(1)}, f32[112,128]{1,0:T(8,128)S(1)}) custom-call(bf16[256,3584]{1,0:T(8,128)(2,1)S(1)} %get-tuple-element.41.w_ref, s32[32,128]{1,0:T(8,128)S(1)} %get-tuple-element.42.slot_ref, bf16[32,3712]{1,0:T(8,128)(2,1)S(1)} %get-tuple-element.43.refs_0_, ...), custom_call_target="tpu_custom_call" | custom-call | flops 6165626880 | bytes 3749888 | tf_op jit(solution)/shard_map/pallas_call | solution.py:372
  30.1 0.0 collective-permute-done.7.refs_4_
  30.1 1.6 %collective-permute-done.8.refs_5_ = bf16[16,3712]{1,0:T(8,128)(2,1)S(1)} collective-permute-done((bf16[16,3712]{1,0:T(8,128)(2,1)S(1)}, bf16[16,3712]{1,0:T(8,128)(2,1)S(1)}, u32[]{:S(2)}, u32[]{:S(2)}) %collective-permute-start.8) | collective-permute-done | bytes 118816 | tf_op jit(solution)/shard_map/ppermute | solution.py:384
  31.6 0.0 collective-permute-done.4.refs_1_
  31.6 0.0 collective-permute-done.3.refs_0_
  31.6 3.2 %collective-permute-done.6.refs_2_ = bf16[24,3712]{1,0:T(8,128)(2,1)S(1)} collective-permute-done((bf16[24,3712]{1,0:T(8,128)(2,1)S(1)}, bf16[24,3712]{1,0:T(8,128)(2,1)S(1)}, u32[]{:S(2)}, u32[]{:S(2)}) %collective-permute-start.6) | collective-permute-done | bytes 178208 | tf_op jit(solution)/shard_map/ppermute | solution.py:384
  34.8 1.4 %shard_map.98 = (bf16[144,3712]{1,0:T(8,128)(2,1)S(1)}, bf16[256,128]{1,0:T(8,128)(2,1)}) custom-call(f32[112,128]{1,0:T(8,128)S(1)} %get-tuple-element.47.own_ref, bf16[256,3584]{1,0:T(8,128)(2,1)S(1)} %get-tuple-element.41.w_ref, s32[32,128]{1,0:T(8,128)S(1)} %get-tuple-element.42.slot_ref, bf16[24,3712]{1,0:T(8,128)(2,1)S(1)} %collective-permute-done.3.refs_0_, ...), custom_call_target="tpu_custom_call" | custom-call | flops 264241152 | bytes 4112384 | tf_op jit(solution)/shard_map/pallas_call | solution.py:372
  36.2 1.4 %shard_map.99 = bf16[256,1792]{1,0:T(8,128)(2,1)} custom-call(s32[32,128]{1,0:T(8,128)S(1)} %get-tuple-element.42.slot_ref, bf16[112,3712]{1,0:T(8,128)(2,1)S(1)} %get-tuple-element.53.early_ref, bf16[144,3712]{1,0:T(8,128)(2,1)S(1)} %get-tuple-element.54.late_ref), custom_call_target="tpu_custom_call" | custom-call | flops 234881024 | bytes 2834432 | tf_op jit(solution)/shard_map/pallas_call | solution.py:372
  37.6 0.0 collective-permute-start.9
  37.6 4.6 %all-to-all-start = ((bf16[8,32,128]{2,1,0:T(8,128)(2,1)}), bf16[8,32,128]{2,1,0:T(8,128)(2,1)S(1)}, u32[]{:S(2)}, u32[]{:S(2)}) async-start(bf16[8,32,128]{2,1,0:T(8,128)(2,1)} %bitcast.4), calls=%async_computation | async-start | bytes 131072 | tf_op jit(solution)/shard_map/all_to_all | solution.py:461
  42.2 0.0 copy-start.3
  42.2 0.0 copy-start.4
  42.2 0.0 copy-start.5
  42.2 0.0 copy-start.6
  42.2 0.0 copy-start.7
  42.2 0.0 collective-permute-done.9.arrived_ref
  42.3 1.4 %shard_map.100 = bf16[256,1792]{1,0:T(8,128)(2,1)} custom-call(s32[32,128]{1,0:T(8,128)S(1)} %get-tuple-element.42.slot_ref, bf16[112,3712]{1,0:T(8,128)(2,1)S(1)} %get-tuple-element.53.early_ref, bf16[144,3712]{1,0:T(8,128)(2,1)S(1)} %get-tuple-element.54.late_ref, bf16[256,1792]{1,0:T(8,128)(2,1)S(1)} %collective-permute-done.9.arrived_ref), custom_call_target="tpu_custom_call" | custom-call | flops 234881024 | bytes 3751936 | tf_op jit(solution)/shard_map/pallas_call | solution.py:372
  43.6 5.5 %all-to-all-done.back_ref = bf16[8,32,128]{2,1,0:T(8,128)(2,1)S(1)} async-done(((bf16[8,32,128]{2,1,0:T(8,128)(2,1)}), bf16[8,32,128]{2,1,0:T(8,128)(2,1)S(1)}, u32[]{:S(2)}, u32[]{:S(2)}) %all-to-all-start) | async-done | bytes 65568 | tf_op jit(solution)/shard_map/all_to_all | solution.py:461
  49.1 0.0 copy-done.3
  49.1 0.0 copy-done.4
  49.1 0.0 copy-done.5
  49.1 0.0 copy-done.6
  49.1 0.0 copy-done.7
  49.1 1.0 %shard_map.101 = (bf16[1024,128]{1,0:T(8,128)(2,1)}, bf16[8,128]{1,0:T(8,128)(2,1)}) custom-call(bf16[8,32,128]{2,1,0:T(8,128)(2,1)S(1)} %all-to-all-done.back_ref, f32[88,128]{1,0:T(8,128)S(1)} %copy-done.3, s32[88,128]{1,0:T(8,128)S(1)} %copy-done.4, f32[88,128]{1,0:T(8,128)S(1)} %copy-done.5, f32[88,128]{1,0:T(8,128)S(1)} %copy-done.6, s32[8,128]{1,0:T(8,128)S(1)} %bitcast.10), custom_call_target="tpu_custom_call" | custom-call | flops 23068672 | bytes 514048 | tf_op jit(solution)/shard_map/pallas_call | solution.py:372
  (2 shorter events, 0.1 us)
Async XLA Ops:
  3.3 15.3 %collective-permute-start = (bf16[56,3712]{1,0:T(8,128)(2,1)}, bf16[56,3712]{1,0:T(8,128)(2,1)S(1)}, u32[]{:S(2)}, u32[]{:S(2)}) collective-permute-start(bf16[56,3712]{1,0:T(8,128)(2,1)} %get-tuple-element.33), channel_id=1, source_target_pairs={{0,2},{2,0},{4,6},{6,4},{8,10},{10,8},{12,14},{14,12},{1,3},{3,1},... | collective-permute-start | bytes 1247240 | tf_op jit(solution)/shard_map/ppermute | solution.py:384
  6.3 9.9 %collective-permute-start.2 = (bf16[24,3712]{1,0:T(8,128)(2,1)}, bf16[24,3712]{1,0:T(8,128)(2,1)S(1)}, u32[]{:S(2)}, u32[]{:S(2)}) collective-permute-start(bf16[24,3712]{1,0:T(8,128)(2,1)} %get-tuple-element.34), channel_id=1, source_target_pairs={{0,4},{2,6},{4,0},{6,2},{8,12},{10,14},{12,8},{14,10},{1,5},{3,7},... | collective-permute-start | bytes 534536 | tf_op jit(solution)/shard_map/ppermute | solution.py:384
  7.9 10.7 %collective-permute-start.1 = (bf16[24,3712]{1,0:T(8,128)(2,1)}, bf16[24,3712]{1,0:T(8,128)(2,1)S(1)}, u32[]{:S(2)}, u32[]{:S(2)}) collective-permute-start(bf16[24,3712]{1,0:T(8,128)(2,1)} %get-tuple-element.34), channel_id=1, source_target_pairs={{0,8},{2,10},{4,12},{6,14},{8,0},{10,2},{12,4},{14,6},{1,9},{3,11}... | collective-permute-start | bytes 534536 | tf_op jit(solution)/shard_map/ppermute | solution.py:384
  10.5 1.5 %copy-start = (bf16[2,128,3584]{2,1,0:T(8,128)(2,1)S(1)}, bf16[2,128,3584]{2,1,0:T(8,128)(2,1)}, u32[]{:S(2)}) copy-start(bf16[2,128,3584]{2,1,0:T(8,128)(2,1)} %param.13) | copy-start | bytes 5505028
  12.0 0.9 %copy-start.1 = (bf16[32,3712]{1,0:T(8,128)(2,1)S(1)}, bf16[32,3712]{1,0:T(8,128)(2,1)}, u32[]{:S(2)}) copy-start(bf16[32,3712]{1,0:T(8,128)(2,1)} %get-tuple-element.35.own_hbm) | copy-start | bytes 712708
  12.9 0.9 %copy-start.2 = (bf16[24,3712]{1,0:T(8,128)(2,1)S(1)}, bf16[24,3712]{1,0:T(8,128)(2,1)}, u32[]{:S(2)}) copy-start(bf16[24,3712]{1,0:T(8,128)(2,1)} %get-tuple-element.36.even_hbm) | copy-start | bytes 534532
  13.8 0.7 %copy-start.8 = (s32[8]{0:T(128)S(1)}, s32[8]{0:T(128)}, u32[]{:S(2)}) copy-start(s32[8]{0:T(128)} %replica_ref.1) | copy-start | bytes 100
  18.6 10.6 %collective-permute-start.5 = (bf16[40,3712]{1,0:T(8,128)(2,1)S(1)}, bf16[40,3712]{1,0:T(8,128)(2,1)S(1)}, u32[]{:S(2)}, u32[]{:S(2)}) collective-permute-start(bf16[40,3712]{1,0:T(8,128)(2,1)S(1)} %get-tuple-element.49), channel_id=1, source_target_pairs={{0,4},{2,6},{4,0},{6,2},{8,12},{10,14},{12,8},{14,10},{1,5},{3,7},... | collective-permute-start | bytes 890888 | tf_op jit(solution)/shard_map/ppermute | solution.py:384
  19.1 12.5 %collective-permute-start.3 = (bf16[24,3712]{1,0:T(8,128)(2,1)S(1)}, bf16[24,3712]{1,0:T(8,128)(2,1)S(1)}, u32[]{:S(2)}, u32[]{:S(2)}) collective-permute-start(bf16[24,3712]{1,0:T(8,128)(2,1)S(1)} %collective-permute-done.1.refs_3_.far_ref), channel_id=1, source_target_pairs={{0,2},{2,0},{4,6},{6,4},{8,10},{10,8},{12,14},{14,12},{1,3},{3,1},... | collective-permute-start | bytes 534536 | tf_op jit(solution)/shard_map/ppermute | solution.py:384
  19.6 12.0 %collective-permute-start.4 = (bf16[24,3712]{1,0:T(8,128)(2,1)S(1)}, bf16[24,3712]{1,0:T(8,128)(2,1)S(1)}, u32[]{:S(2)}, u32[]{:S(2)}) collective-permute-start(bf16[24,3712]{1,0:T(8,128)(2,1)S(1)} %collective-permute-done.2.refs_2_), channel_id=1, source_target_pairs={{0,2},{2,0},{4,6},{6,4},{8,10},{10,8},{12,14},{14,12},{1,3},{3,1},... | collective-permute-start | bytes 534536 | tf_op jit(solution)/shard_map/ppermute | solution.py:384
  21.1 8.9 %collective-permute-start.7 = (bf16[16,3712]{1,0:T(8,128)(2,1)S(1)}, bf16[16,3712]{1,0:T(8,128)(2,1)S(1)}, u32[]{:S(2)}, u32[]{:S(2)}) collective-permute-start(bf16[16,3712]{1,0:T(8,128)(2,1)S(1)} %get-tuple-element.50), channel_id=1, source_target_pairs={{0,8},{2,10},{4,12},{6,14},{8,0},{10,2},{12,4},{14,6},{1,9},{3,11}... | collective-permute-start | bytes 356360 | tf_op jit(solution)/shard_map/ppermute | solution.py:384
  23.7 7.9 %collective-permute-start.8 = (bf16[16,3712]{1,0:T(8,128)(2,1)S(1)}, bf16[16,3712]{1,0:T(8,128)(2,1)S(1)}, u32[]{:S(2)}, u32[]{:S(2)}) collective-permute-start(bf16[16,3712]{1,0:T(8,128)(2,1)S(1)} %get-tuple-element.51), channel_id=1, source_target_pairs={{0,12},{2,14},{4,8},{6,10},{8,4},{10,6},{12,0},{14,2},{1,13},{3,15... | collective-permute-start | bytes 356360 | tf_op jit(solution)/shard_map/ppermute | solution.py:384
  29.3 5.5 %collective-permute-start.6 = (bf16[24,3712]{1,0:T(8,128)(2,1)S(1)}, bf16[24,3712]{1,0:T(8,128)(2,1)S(1)}, u32[]{:S(2)}, u32[]{:S(2)}) collective-permute-start(bf16[24,3712]{1,0:T(8,128)(2,1)S(1)} %slice.4), channel_id=1, source_target_pairs={{0,2},{2,0},{4,6},{6,4},{8,10},{10,8},{12,14},{14,12},{1,3},{3,1},... | collective-permute-start | bytes 534536 | tf_op jit(solution)/shard_map/ppermute | solution.py:384
  37.6 4.7 %collective-permute-start.9 = (bf16[256,1792]{1,0:T(8,128)(2,1)}, bf16[256,1792]{1,0:T(8,128)(2,1)S(1)}, u32[]{:S(2)}, u32[]{:S(2)}) collective-permute-start(bf16[256,1792]{1,0:T(8,128)(2,1)} %shard_map.99), channel_id=1, source_target_pairs={{0,1},{1,0},{2,3},{3,2},{4,5},{5,4},{6,7},{7,6},{8,9},{9,8},{10,11... | collective-permute-start | bytes 2752520 | tf_op jit(solution)/shard_map/ppermute | solution.py:470
  37.6 11.5 %all-to-all-start = ((bf16[8,32,128]{2,1,0:T(8,128)(2,1)}), bf16[8,32,128]{2,1,0:T(8,128)(2,1)S(1)}, u32[]{:S(2)}, u32[]{:S(2)}) async-start(bf16[8,32,128]{2,1,0:T(8,128)(2,1)} %bitcast.4), calls=%async_computation | async-start | bytes 131072 | tf_op jit(solution)/shard_map/all_to_all | solution.py:461
  42.2 6.9 %copy-start.3 = (f32[88,128]{1,0:T(8,128)S(1)}, f32[88,128]{1,0:T(8,128)}, u32[]{:S(2)}) copy-start(f32[88,128]{1,0:T(8,128)} %get-tuple-element.56.pick_ref) | copy-start | bytes 135172
  42.2 6.9 %copy-start.4 = (s32[88,128]{1,0:T(8,128)S(1)}, s32[88,128]{1,0:T(8,128)}, u32[]{:S(2)}) copy-start(s32[88,128]{1,0:T(8,128)} %get-tuple-element.57.expert_ref) | copy-start | bytes 135172
  42.2 6.9 %copy-start.5 = (f32[88,128]{1,0:T(8,128)S(1)}, f32[88,128]{1,0:T(8,128)}, u32[]{:S(2)}) copy-start(f32[88,128]{1,0:T(8,128)} %get-tuple-element.58.hs_ref) | copy-start | bytes 135172
  42.2 6.9 %copy-start.6 = (f32[88,128]{1,0:T(8,128)S(1)}, f32[88,128]{1,0:T(8,128)}, u32[]{:S(2)}) copy-start(f32[88,128]{1,0:T(8,128)} %get-tuple-element.59.ps_ref) | copy-start | bytes 135172
  42.2 6.9 %copy-start.7 = (s32[128,8]{0,1:T(8,128)S(1)}, s32[128,8]{0,1:T(8,128)}, u32[]{:S(2)}) copy-start(s32[128,8]{0,1:T(8,128)} %param.10) | copy-start | bytes 12292

commit v9 on v8

--- a/solution.py
+++ b/solution.py
@@ -154,7 +154,7 @@
     return (hidden_gradient, grad_probs, grad_weights)
 
 
-SLOT = 4
+SLOT = 3
 HOME, COPIES = "home", "copies"
 F32 = jnp.float32
 BF16 = jnp.bfloat16
@@ -287,7 +287,7 @@
 
 def turn_kernel(local_count, dev_count, beside_ref, far_ref, even_ref, *out_refs):
     per_home, per_copy = local_count * SLOT, dev_count * CAPR
-    beside = beside_ref[per_copy + per_home:].astype(F32)
+    beside = beside_ref[...].astype(F32)[per_copy + per_home:]
     even = even_ref[...].astype(F32)
     for n, out_ref in enumerate(out_refs):
         span = slice(n * per_home, (n + 1) * per_home)
@@ -308,6 +308,8 @@
     per_home, per_copy = local_count * SLOT, dev_count * CAPR
     fill_rows(order, pieces, per_home, per_copy, piece_refs, rows_ref)
     own = own_columns(rows_ref, w_ref, slots_of(order, slot_ref, per_home, rows_ref.shape[0]), local_count)
+    if passed.shape[1] > per_home + per_copy:
+        passed[:, per_home + per_copy:] = jnp.zeros_like(passed[:, per_home + per_copy:])
     for keys, value in ((early, own_ref[...]), (order, own)):
         start = 0
         for m, kind in keys:
@@ -350,7 +352,9 @@
     per_home = local_count * SLOT
     me = lax.axis_index("expert")
     back = [back_ref[me ^ m].astype(F32) for m in range(dev_count)]
-    copy = functools.reduce(jnp.add, [b[per_home:] for b in back])
+    slots = pick_ref.shape[0]
+    copies = slots - dev_count * per_home
+    copy = functools.reduce(jnp.add, [b[per_home:per_home + copies] for b in back])
     grad_in = jnp.concatenate([b[:per_home] for b in back] + [copy], axis=0)
     h_rows = (ps_ref[...] * grad_in).astype(BF16)
     p_rows = jnp.sum(hs_ref[...] * grad_in, axis=1, keepdims=True)
@@ -451,11 +455,12 @@
         pieces[m, HOME], pieces[m + 1, HOME] = ((3 + n, copies * (m == 2) + k * per_home) for k in range(2))
     orders.append(list(pieces))
     height = padded(sum(per_home if kind == HOME else copies for _, kind in pieces))
+    block = padded(per_home + copies)
     late_rows, back = call(
         functools.partial(late_kernel, *sizes, *orders, pieces),
-        (shape((height, d_model + width), BF16), shape((dev_count * (per_home + copies), width), BF16)),
+        (shape((height, d_model + width), BF16), shape((dev_count * block, width), BF16)),
         [(vmem, a) for a in (own, w_held, slot, *arrays)],
-        [vmem((dev_count, per_home + copies, width), F32)],
+        [vmem((dev_count, block, width), F32)],
         flops=2 * height * d_model * local_count * width,
     )
     back = lax.all_to_all(back, "expert", split_axis=0, concat_axis=0, tiled=True)
@@ -472,13 +477,13 @@
         functools.partial(own_half_kernel, *sizes, orders),
         shape((local_count * width, columns), BF16),
         [(vmem, a) for a in (*halves, arrived)],
-        flops=half_flops,
+        flops=30 * half_flops,
     )
     grad_w, pick = lax.optimization_barrier((grad_w, pick))
     grad_h, grad_p = call(
         functools.partial(combine_kernel, *sizes),
         (shape((toks * top, width), BF16), shape((top, toks), BF16)),
-        [(vmem, a) for a in (back.reshape(dev_count, per_home + copies, width), pick, expert, h_slot, p_slot, ids)],
+        [(vmem, a) for a in (back.reshape(dev_count, block, width), pick, expert, h_slot, p_slot, ids)],
         [vmem((toks * top, width), F32), vmem((top, toks), F32)],
         flops=2 * slots * toks * width * top,
     )

time: 50.5 us -> 48.6 us (0.962)
  waiting for transfers between devices: 17.2 us -> 15.2 us
    all_to_all x1, waiting for transfers between devices: 5.47 us -> 4.26 us  [gather_body(): lax.all_to_all(back, 'expert', split_axis=0, concat_axis=0, tiled=True)]
    all_to_all x1, starting transfers between devices: 4.62 us -> 3.63 us  [gather_body(): lax.all_to_all(back, 'expert', split_axis=0, concat_axis=0, tiled=True)]
    ppermute x9, waiting for transfers between devices: 11.7 us -> 10.9 us  [swap(): return lax.ppermute(x, 'expert', [(i, i ^ bits) for i in range(count)])]
    ppermute x9, starting transfers between devices: 13.7 us -> 14.4 us  [swap(): return lax.ppermute(x, 'expert', [(i, i ^ bits) for i in range(count)])]
  transfers between devices with their start and end apart: 11 -> 11, of which waited for: 6 -> 6; matrix products, arithmetic and copies ran while one was open for 0% -> 0% of each run, Pallas kernels for 7% -> 9%
where the time goes in v9:
time: 48.6 us; the launch traced here: 48.2 us
  starting transfers between devices  18.1 us (37%)
  waiting for transfers between devices  15.2 us (31%)
  Pallas kernels  10.2 us (21%)
  local copies, waits for them, and re-layouts  4.05 us (8%)
  between operations  0.76 us (2%)
    ppermute x9, starting transfers between devices, swap(): return lax.ppermute(x, 'expert', [(i, i ^ bits) for i in range(count)])  14.4 us
    ppermute x9, waiting for transfers between devices, swap(): return lax.ppermute(x, 'expert', [(i, i ^ bits) for i in range(count)])  10.9 us
    pallas_call x8, Pallas kernels, call(): pl.pallas_call(kernel, out_shape=out_shape, in_specs=[pl.BlockSpec(memory...  10.2 us
    all_to_all x1, waiting for transfers between devices, gather_body(): lax.all_to_all(back, 'expert', split_axis=0, concat_axis=0, tiled=True)  4.26 us
    unnamed x18, local copies, waits for them, and re-layouts  4.04 us
    all_to_all x1, starting transfers between devices, gather_body(): lax.all_to_all(back, 'expert', split_axis=0, concat_axis=0, tiled=True)  3.63 us
  transfers between devices with their start and end apart: 11, of which 6 were waited for; matrix products, arithmetic and copies ran while one was open for 0% of the time, Pallas kernels for 9%

profile of v9, /device:TPU:0, one launch (start us, length us, event | category | flops | bytes accessed | tf_op | source)
XLA Modules:
  0.0 48.2 jit_solution(377937725471033583)
XLA Ops:
  0.6 2.7 %shard_map.94 = (f32[72,128]{1,0:T(8,128)}, s32[72,128]{1,0:T(8,128)}, f32[72,128]{1,0:T(8,128)}, f32[72,128]{1,0:T(8,128)}, bf16[48,3712]{1,0:T(8,128)(2,1)}, /...) custom-call(s32[8]{0:T(128)} %replica_ref.1, s32[1,8]{1,0:T(1,128)} %refs_1_.1, ...), custom_call_target="tpu_custom_call" | custom-call | flops 66060288 | bytes 2224192 | tf_op jit(solution)/shard_map/pallas_call | solution.py:376
  3.3 3.0 %collective-permute-start = (bf16[48,3712]{1,0:T(8,128)(2,1)}, bf16[48,3712]{1,0:T(8,128)(2,1)S(1)}, u32[]{:S(2)}, u32[]{:S(2)}) collective-permute-start(bf16[48,3712]{1,0:T(8,128)(2,1)} %get-tuple-element.33), channel_id=1, source_target_pairs={{0,2},{2,0},{4,6},{6,4},{8,10},{10,8},{12,14},{14,12},{1,3},{3,1},... | collective-permute-start | bytes 1069064 | tf_op jit(solution)/shard_map/ppermute | solution.py:388
  6.3 1.6 %collective-permute-start.2 = (bf16[24,3712]{1,0:T(8,128)(2,1)}, bf16[24,3712]{1,0:T(8,128)(2,1)S(1)}, u32[]{:S(2)}, u32[]{:S(2)}) collective-permute-start(bf16[24,3712]{1,0:T(8,128)(2,1)} %get-tuple-element.34), channel_id=1, source_target_pairs={{0,4},{2,6},{4,0},{6,2},{8,12},{10,14},{12,8},{14,10},{1,5},{3,7},... | collective-permute-start | bytes 534536 | tf_op jit(solution)/shard_map/ppermute | solution.py:388
  7.9 2.6 %collective-permute-start.1 = (bf16[24,3712]{1,0:T(8,128)(2,1)}, bf16[24,3712]{1,0:T(8,128)(2,1)S(1)}, u32[]{:S(2)}, u32[]{:S(2)}) collective-permute-start(bf16[24,3712]{1,0:T(8,128)(2,1)} %get-tuple-element.34), channel_id=1, source_target_pairs={{0,8},{2,10},{4,12},{6,14},{8,0},{10,2},{12,4},{14,6},{1,9},{3,11}... | collective-permute-start | bytes 534536 | tf_op jit(solution)/shard_map/ppermute | solution.py:388
  10.5 0.0 copy-start
  10.5 1.5 %copy-done = bf16[2,128,3584]{2,1,0:T(8,128)(2,1)S(1)} copy-done((bf16[2,128,3584]{2,1,0:T(8,128)(2,1)S(1)}, bf16[2,128,3584]{2,1,0:T(8,128)(2,1)}, u32[]{:S(2)}) %copy-start) | copy-done | bytes 1835032
  12.0 0.0 copy-start.1
  12.0 0.9 %copy-done.1 = bf16[30,3712]{1,0:T(8,128)(2,1)S(1)} copy-done((bf16[30,3712]{1,0:T(8,128)(2,1)S(1)}, bf16[30,3712]{1,0:T(8,128)(2,1)}, u32[]{:S(2)}) %copy-start.1) | copy-done | bytes 222744
  12.9 0.0 copy-start.2
  12.9 0.9 %copy-done.2 = bf16[18,3712]{1,0:T(8,128)(2,1)S(1)} copy-done((bf16[18,3712]{1,0:T(8,128)(2,1)S(1)}, bf16[18,3712]{1,0:T(8,128)(2,1)}, u32[]{:S(2)}) %copy-start.2) | copy-done | bytes 133656
  13.8 0.0 copy-start.8
  13.8 0.7 %copy-done.8 = s32[8]{0:T(128)S(1)} copy-done((s32[8]{0:T(128)S(1)}, s32[8]{0:T(128)}, u32[]{:S(2)}) %copy-start.8) | copy-done | bytes 56
  14.5 1.2 %shard_map.95 = (bf16[30,3712]{1,0:T(8,128)(2,1)S(1)}, bf16[18,3712]{1,0:T(8,128)(2,1)S(1)}, bf16[256,3584]{1,0:T(8,128)(2,1)S(1)}, s32[30,128]{1,0:T(8,128)S(1)}) custom-call(s32[8]{0:T(128)S(1)} %copy-done.8, bf16[256,3584]{1,0:T(8,128)(2,1)S(1)} %bitcast.8, bf16[30,3712]{1,0:T(8,128)(2,1)S(1)} %copy-done.1, bf16[18,3712]{1,0:T(8,128)(2,1)S(1)} %copy-done.2), custom_call_target="tpu_custom_call" | custom-call | bytes 4398112 | tf_op jit(solution)/shard_map/pallas_call | solution.py:376
  15.7 0.4 collective-permute-done.2.refs_2_
  16.2 2.4 %collective-permute-done.1.refs_3_.far_ref = bf16[24,3712]{1,0:T(8,128)(2,1)S(1)} collective-permute-done((bf16[24,3712]{1,0:T(8,128)(2,1)}, bf16[24,3712]{1,0:T(8,128)(2,1)S(1)}, u32[]{:S(2)}, u32[]{:S(2)}) %collective-permute-start.1) | collective-permute-done | bytes 178208 | tf_op jit(solution)/shard_map/ppermute | solution.py:388
  18.6 0.0 collective-permute-done.refs_1_.beside_ref
  18.6 0.1 shard_map.97
  18.7 0.5 %collective-permute-start.5 = (bf16[36,3712]{1,0:T(8,128)(2,1)S(1)}, bf16[36,3712]{1,0:T(8,128)(2,1)S(1)}, u32[]{:S(2)}, u32[]{:S(2)}) collective-permute-start(bf16[36,3712]{1,0:T(8,128)(2,1)S(1)} %get-tuple-element.49), channel_id=1, source_target_pairs={{0,4},{2,6},{4,0},{6,2},{8,12},{10,14},{12,8},{14,10},{1,5},{3,7},... | collective-permute-start | bytes 801800 | tf_op jit(solution)/shard_map/ppermute | solution.py:388
  19.2 0.5 %collective-permute-start.3 = (bf16[24,3712]{1,0:T(8,128)(2,1)S(1)}, bf16[24,3712]{1,0:T(8,128)(2,1)S(1)}, u32[]{:S(2)}, u32[]{:S(2)}) collective-permute-start(bf16[24,3712]{1,0:T(8,128)(2,1)S(1)} %collective-permute-done.1.refs_3_.far_ref), channel_id=1, source_target_pairs={{0,2},{2,0},{4,6},{6,4},{8,10},{10,8},{12,14},{14,12},{1,3},{3,1},... | collective-permute-start | bytes 534536 | tf_op jit(solution)/shard_map/ppermute | solution.py:388
  19.7 1.5 %collective-permute-start.4 = (bf16[24,3712]{1,0:T(8,128)(2,1)S(1)}, bf16[24,3712]{1,0:T(8,128)(2,1)S(1)}, u32[]{:S(2)}, u32[]{:S(2)}) collective-permute-start(bf16[24,3712]{1,0:T(8,128)(2,1)S(1)} %collective-permute-done.2.refs_2_), channel_id=1, source_target_pairs={{0,2},{2,0},{4,6},{6,4},{8,10},{10,8},{12,14},{14,12},{1,3},{3,1},... | collective-permute-start | bytes 534536 | tf_op jit(solution)/shard_map/ppermute | solution.py:388
  21.2 2.7 %collective-permute-start.7 = (bf16[12,3712]{1,0:T(8,128)(2,1)S(1)}, bf16[12,3712]{1,0:T(8,128)(2,1)S(1)}, u32[]{:S(2)}, u32[]{:S(2)}) collective-permute-start(bf16[12,3712]{1,0:T(8,128)(2,1)S(1)} %get-tuple-element.50), channel_id=1, source_target_pairs={{0,8},{2,10},{4,12},{6,14},{8,0},{10,2},{12,4},{14,6},{1,9},{3,11}... | collective-permute-start | bytes 267272 | tf_op jit(solution)/shard_map/ppermute | solution.py:388
  23.8 1.3 %collective-permute-start.8 = (bf16[12,3712]{1,0:T(8,128)(2,1)S(1)}, bf16[12,3712]{1,0:T(8,128)(2,1)S(1)}, u32[]{:S(2)}, u32[]{:S(2)}) collective-permute-start(bf16[12,3712]{1,0:T(8,128)(2,1)S(1)} %get-tuple-element.51), channel_id=1, source_target_pairs={{0,12},{2,14},{4,8},{6,10},{8,4},{10,6},{12,0},{14,2},{1,13},{3,15... | collective-permute-start | bytes 267272 | tf_op jit(solution)/shard_map/ppermute | solution.py:388
  25.2 4.0 %collective-permute-done.5.refs_3_ = bf16[36,3712]{1,0:T(8,128)(2,1)S(1)} collective-permute-done((bf16[36,3712]{1,0:T(8,128)(2,1)S(1)}, bf16[36,3712]{1,0:T(8,128)(2,1)S(1)}, u32[]{:S(2)}, u32[]{:S(2)}) %collective-permute-start.5) | collective-permute-done | bytes 267296 | tf_op jit(solution)/shard_map/ppermute | solution.py:388
  29.2 0.7 %collective-permute-start.6 = (bf16[24,3712]{1,0:T(8,128)(2,1)S(1)}, bf16[24,3712]{1,0:T(8,128)(2,1)S(1)}, u32[]{:S(2)}, u32[]{:S(2)}) collective-permute-start(bf16[24,3712]{1,0:T(8,128)(2,1)S(1)} %slice.4), channel_id=1, source_target_pairs={{0,2},{2,0},{4,6},{6,4},{8,10},{10,8},{12,14},{14,12},{1,3},{3,1},... | collective-permute-start | bytes 534536 | tf_op jit(solution)/shard_map/ppermute | solution.py:388
  29.9 0.7 %shard_map.96 = (bf16[112,3712]{1,0:T(8,128)(2,1)S(1)}, f32[112,128]{1,0:T(8,128)S(1)}) custom-call(bf16[256,3584]{1,0:T(8,128)(2,1)S(1)} %get-tuple-element.41.w_ref, s32[30,128]{1,0:T(8,128)S(1)} %get-tuple-element.42.slot_ref, bf16[30,3712]{1,0:T(8,128)(2,1)S(1)} %get-tuple-element.43.refs_0_, ...), custom_call_target="tpu_custom_call" | custom-call | flops 6165626880 | bytes 3674624 | tf_op jit(solution)/shard_map/pallas_call | solution.py:376
  30.7 0.6 %collective-permute-done.7.refs_4_ = bf16[12,3712]{1,0:T(8,128)(2,1)S(1)} collective-permute-done((bf16[12,3712]{1,0:T(8,128)(2,1)S(1)}, bf16[12,3712]{1,0:T(8,128)(2,1)S(1)}, u32[]{:S(2)}, u32[]{:S(2)}) %collective-permute-start.7) | collective-permute-done | bytes 89120 | tf_op jit(solution)/shard_map/ppermute | solution.py:388
  31.3 0.0 collective-permute-done.8.refs_5_
  31.3 0.0 collective-permute-done.4.refs_1_
  31.3 0.0 collective-permute-done.3.refs_0_
  31.3 3.4 %collective-permute-done.6.refs_2_ = bf16[24,3712]{1,0:T(8,128)(2,1)S(1)} collective-permute-done((bf16[24,3712]{1,0:T(8,128)(2,1)S(1)}, bf16[24,3712]{1,0:T(8,128)(2,1)S(1)}, u32[]{:S(2)}, u32[]{:S(2)}) %collective-permute-start.6) | collective-permute-done | bytes 178208 | tf_op jit(solution)/shard_map/ppermute | solution.py:388
  34.7 1.4 %shard_map.98 = (bf16[144,3712]{1,0:T(8,128)(2,1)S(1)}, bf16[256,128]{1,0:T(8,128)(2,1)}) custom-call(f32[112,128]{1,0:T(8,128)S(1)} %get-tuple-element.47.own_ref, bf16[256,3584]{1,0:T(8,128)(2,1)S(1)} %get-tuple-element.41.w_ref, s32[30,128]{1,0:T(8,128)S(1)} %get-tuple-element.42.slot_ref, bf16[24,3712]{1,0:T(8,128)(2,1)S(1)} %collective-permute-done.3.refs_0_, ...), custom_call_target="tpu_custom_call" | custom-call | flops 264241152 | bytes 4022272 | tf_op jit(solution)/shard_map/pallas_call | solution.py:376
  36.1 0.4 shard_map.99
  36.6 0.1 collective-permute-start.9
  36.7 3.6 %all-to-all-start = ((bf16[8,32,128]{2,1,0:T(8,128)(2,1)}), bf16[8,32,128]{2,1,0:T(8,128)(2,1)S(1)}, u32[]{:S(2)}, u32[]{:S(2)}) async-start(bf16[8,32,128]{2,1,0:T(8,128)(2,1)} %bitcast.4), calls=%async_computation | async-start | bytes 131072 | tf_op jit(solution)/shard_map/all_to_all | solution.py:466
  40.3 0.0 copy-start.3
  40.3 0.0 copy-start.4
  40.3 0.0 copy-start.5
  40.3 0.0 copy-start.6
  40.3 0.0 copy-start.7
  40.4 0.0 collective-permute-done.9.arrived_ref
  40.4 2.6 %shard_map.100 = bf16[256,1792]{1,0:T(8,128)(2,1)} custom-call(s32[30,128]{1,0:T(8,128)S(1)} %get-tuple-element.42.slot_ref, bf16[112,3712]{1,0:T(8,128)(2,1)S(1)} %get-tuple-element.53.early_ref, bf16[144,3712]{1,0:T(8,128)(2,1)S(1)} %get-tuple-element.54.late_ref, bf16[256,1792]{1,0:T(8,128)(2,1)} %collective-permute-done.9.arrived_ref), custom_call_target="tpu_custom_call" | custom-call | flops 6606028800 | bytes 3750912 | tf_op jit(solution)/shard_map/pallas_call | solution.py:376
  42.9 4.3 %all-to-all-done.back_ref = bf16[8,32,128]{2,1,0:T(8,128)(2,1)S(1)} async-done(((bf16[8,32,128]{2,1,0:T(8,128)(2,1)}), bf16[8,32,128]{2,1,0:T(8,128)(2,1)S(1)}, u32[]{:S(2)}, u32[]{:S(2)}) %all-to-all-start) | async-done | bytes 65568 | tf_op jit(solution)/shard_map/all_to_all | solution.py:466
  47.2 0.0 copy-done.3
  47.2 0.0 copy-done.4
  47.2 0.0 copy-done.5
  47.2 0.0 copy-done.6
  47.2 0.0 copy-done.7
  47.2 1.0 %shard_map.101 = (bf16[1024,128]{1,0:T(8,128)(2,1)}, bf16[8,128]{1,0:T(8,128)(2,1)}) custom-call(bf16[8,32,128]{2,1,0:T(8,128)(2,1)S(1)} %all-to-all-done.back_ref, f32[72,128]{1,0:T(8,128)S(1)} %copy-done.3, s32[72,128]{1,0:T(8,128)S(1)} %copy-done.4, f32[72,128]{1,0:T(8,128)S(1)} %copy-done.5, f32[72,128]{1,0:T(8,128)S(1)} %copy-done.6, s32[8,128]{1,0:T(8,128)S(1)} %bitcast.10), custom_call_target="tpu_custom_call" | custom-call | flops 18874368 | bytes 481280 | tf_op jit(solution)/shard_map/pallas_call | solution.py:376
  (1 shorter events, 0.0 us)
Async XLA Ops:
  3.3 15.3 %collective-permute-start = (bf16[48,3712]{1,0:T(8,128)(2,1)}, bf16[48,3712]{1,0:T(8,128)(2,1)S(1)}, u32[]{:S(2)}, u32[]{:S(2)}) collective-permute-start(bf16[48,3712]{1,0:T(8,128)(2,1)} %get-tuple-element.33), channel_id=1, source_target_pairs={{0,2},{2,0},{4,6},{6,4},{8,10},{10,8},{12,14},{14,12},{1,3},{3,1},... | collective-permute-start | bytes 1069064 | tf_op jit(solution)/shard_map/ppermute | solution.py:388
  6.3 9.9 %collective-permute-start.2 = (bf16[24,3712]{1,0:T(8,128)(2,1)}, bf16[24,3712]{1,0:T(8,128)(2,1)S(1)}, u32[]{:S(2)}, u32[]{:S(2)}) collective-permute-start(bf16[24,3712]{1,0:T(8,128)(2,1)} %get-tuple-element.34), channel_id=1, source_target_pairs={{0,4},{2,6},{4,0},{6,2},{8,12},{10,14},{12,8},{14,10},{1,5},{3,7},... | collective-permute-start | bytes 534536 | tf_op jit(solution)/shard_map/ppermute | solution.py:388
  7.9 10.7 %collective-permute-start.1 = (bf16[24,3712]{1,0:T(8,128)(2,1)}, bf16[24,3712]{1,0:T(8,128)(2,1)S(1)}, u32[]{:S(2)}, u32[]{:S(2)}) collective-permute-start(bf16[24,3712]{1,0:T(8,128)(2,1)} %get-tuple-element.34), channel_id=1, source_target_pairs={{0,8},{2,10},{4,12},{6,14},{8,0},{10,2},{12,4},{14,6},{1,9},{3,11}... | collective-permute-start | bytes 534536 | tf_op jit(solution)/shard_map/ppermute | solution.py:388
  10.5 1.5 %copy-start = (bf16[2,128,3584]{2,1,0:T(8,128)(2,1)S(1)}, bf16[2,128,3584]{2,1,0:T(8,128)(2,1)}, u32[]{:S(2)}) copy-start(bf16[2,128,3584]{2,1,0:T(8,128)(2,1)} %param.13) | copy-start | bytes 5505028
  12.0 0.9 %copy-start.1 = (bf16[30,3712]{1,0:T(8,128)(2,1)S(1)}, bf16[30,3712]{1,0:T(8,128)(2,1)}, u32[]{:S(2)}) copy-start(bf16[30,3712]{1,0:T(8,128)(2,1)} %get-tuple-element.35.own_hbm) | copy-start | bytes 668164
  12.9 0.9 %copy-start.2 = (bf16[18,3712]{1,0:T(8,128)(2,1)S(1)}, bf16[18,3712]{1,0:T(8,128)(2,1)}, u32[]{:S(2)}) copy-start(bf16[18,3712]{1,0:T(8,128)(2,1)} %get-tuple-element.36.even_hbm) | copy-start | bytes 400900
  13.8 0.7 %copy-start.8 = (s32[8]{0:T(128)S(1)}, s32[8]{0:T(128)}, u32[]{:S(2)}) copy-start(s32[8]{0:T(128)} %replica_ref.1) | copy-start | bytes 100
  18.7 10.5 %collective-permute-start.5 = (bf16[36,3712]{1,0:T(8,128)(2,1)S(1)}, bf16[36,3712]{1,0:T(8,128)(2,1)S(1)}, u32[]{:S(2)}, u32[]{:S(2)}) collective-permute-start(bf16[36,3712]{1,0:T(8,128)(2,1)S(1)} %get-tuple-element.49), channel_id=1, source_target_pairs={{0,4},{2,6},{4,0},{6,2},{8,12},{10,14},{12,8},{14,10},{1,5},{3,7},... | collective-permute-start | bytes 801800 | tf_op jit(solution)/shard_map/ppermute | solution.py:388
  19.2 12.1 %collective-permute-start.3 = (bf16[24,3712]{1,0:T(8,128)(2,1)S(1)}, bf16[24,3712]{1,0:T(8,128)(2,1)S(1)}, u32[]{:S(2)}, u32[]{:S(2)}) collective-permute-start(bf16[24,3712]{1,0:T(8,128)(2,1)S(1)} %collective-permute-done.1.refs_3_.far_ref), channel_id=1, source_target_pairs={{0,2},{2,0},{4,6},{6,4},{8,10},{10,8},{12,14},{14,12},{1,3},{3,1},... | collective-permute-start | bytes 534536 | tf_op jit(solution)/shard_map/ppermute | solution.py:388
  19.7 11.6 %collective-permute-start.4 = (bf16[24,3712]{1,0:T(8,128)(2,1)S(1)}, bf16[24,3712]{1,0:T(8,128)(2,1)S(1)}, u32[]{:S(2)}, u32[]{:S(2)}) collective-permute-start(bf16[24,3712]{1,0:T(8,128)(2,1)S(1)} %collective-permute-done.2.refs_2_), channel_id=1, source_target_pairs={{0,2},{2,0},{4,6},{6,4},{8,10},{10,8},{12,14},{14,12},{1,3},{3,1},... | collective-permute-start | bytes 534536 | tf_op jit(solution)/shard_map/ppermute | solution.py:388
  21.2 10.1 %collective-permute-start.7 = (bf16[12,3712]{1,0:T(8,128)(2,1)S(1)}, bf16[12,3712]{1,0:T(8,128)(2,1)S(1)}, u32[]{:S(2)}, u32[]{:S(2)}) collective-permute-start(bf16[12,3712]{1,0:T(8,128)(2,1)S(1)} %get-tuple-element.50), channel_id=1, source_target_pairs={{0,8},{2,10},{4,12},{6,14},{8,0},{10,2},{12,4},{14,6},{1,9},{3,11}... | collective-permute-start | bytes 267272 | tf_op jit(solution)/shard_map/ppermute | solution.py:388
  23.8 7.5 %collective-permute-start.8 = (bf16[12,3712]{1,0:T(8,128)(2,1)S(1)}, bf16[12,3712]{1,0:T(8,128)(2,1)S(1)}, u32[]{:S(2)}, u32[]{:S(2)}) collective-permute-start(bf16[12,3712]{1,0:T(8,128)(2,1)S(1)} %get-tuple-element.51), channel_id=1, source_target_pairs={{0,12},{2,14},{4,8},{6,10},{8,4},{10,6},{12,0},{14,2},{1,13},{3,15... | collective-permute-start | bytes 267272 | tf_op jit(solution)/shard_map/ppermute | solution.py:388
  29.2 5.5 %collective-permute-start.6 = (bf16[24,3712]{1,0:T(8,128)(2,1)S(1)}, bf16[24,3712]{1,0:T(8,128)(2,1)S(1)}, u32[]{:S(2)}, u32[]{:S(2)}) collective-permute-start(bf16[24,3712]{1,0:T(8,128)(2,1)S(1)} %slice.4), channel_id=1, source_target_pairs={{0,2},{2,0},{4,6},{6,4},{8,10},{10,8},{12,14},{14,12},{1,3},{3,1},... | collective-permute-start | bytes 534536 | tf_op jit(solution)/shard_map/ppermute | solution.py:388
  36.6 3.8 %collective-permute-start.9 = (bf16[256,1792]{1,0:T(8,128)(2,1)S(1)}, bf16[256,1792]{1,0:T(8,128)(2,1)}, u32[]{:S(2)}, u32[]{:S(2)}) collective-permute-start(bf16[256,1792]{1,0:T(8,128)(2,1)S(1)} %shard_map.99), channel_id=1, source_target_pairs={{0,1},{1,0},{2,3},{3,2},{4,5},{5,4},{6,7},{7,6},{8,9},{9,8},{10,11... | collective-permute-start | bytes 2752520 | tf_op jit(solution)/shard_map/ppermute | solution.py:475
  36.7 10.5 %all-to-all-start = ((bf16[8,32,128]{2,1,0:T(8,128)(2,1)}), bf16[8,32,128]{2,1,0:T(8,128)(2,1)S(1)}, u32[]{:S(2)}, u32[]{:S(2)}) async-start(bf16[8,32,128]{2,1,0:T(8,128)(2,1)} %bitcast.4), calls=%async_computation | async-start | bytes 131072 | tf_op jit(solution)/shard_map/all_to_all | solution.py:466
  40.3 6.9 %copy-start.3 = (f32[72,128]{1,0:T(8,128)S(1)}, f32[72,128]{1,0:T(8,128)}, u32[]{:S(2)}) copy-start(f32[72,128]{1,0:T(8,128)} %get-tuple-element.56.pick_ref) | copy-start | bytes 110596
  40.3 6.9 %copy-start.4 = (s32[72,128]{1,0:T(8,128)S(1)}, s32[72,128]{1,0:T(8,128)}, u32[]{:S(2)}) copy-start(s32[72,128]{1,0:T(8,128)} %get-tuple-element.57.expert_ref) | copy-start | bytes 110596
  40.3 6.9 %copy-start.5 = (f32[72,128]{1,0:T(8,128)S(1)}, f32[72,128]{1,0:T(8,128)}, u32[]{:S(2)}) copy-start(f32[72,128]{1,0:T(8,128)} %get-tuple-element.58.hs_ref) | copy-start | bytes 110596
  40.3 6.9 %copy-start.6 = (f32[72,128]{1,0:T(8,128)S(1)}, f32[72,128]{1,0:T(8,128)}, u32[]{:S(2)}) copy-start(f32[72,128]{1,0:T(8,128)} %get-tuple-element.59.ps_ref) | copy-start | bytes 110596
  40.3 6.9 %copy-start.7 = (s32[128,8]{0,1:T(8,128)S(1)}, s32[128,8]{0,1:T(8,128)}, u32[]{:S(2)}) copy-start(s32[128,8]{0,1:T(8,128)} %param.10) | copy-start | bytes 12292

commit v10 on v9

--- a/solution.py
+++ b/solution.py
@@ -208,14 +208,16 @@
     for move in moves[3:5]:
         move.wait()
     wide[...] = hid_ref[...].astype(F32)
-    h_slot = jnp.zeros((slots, hid_ref.shape[1]), F32)
     p_slot = jnp.zeros((slots, toks), F32)
     probs = probs_ref[...].astype(F32)
+    chosen, values = [], []
     for k in range(top):
         sel = jnp.where(ids[k:k + 1, :] == expert, pick, 0.0)
-        h_k = wide[pl.ds(k, toks, stride=top), :].astype(BF16)
-        h_slot = h_slot + jnp.dot(sel.astype(BF16), h_k, preferred_element_type=F32)
+        chosen.append(sel.astype(BF16))
+        values.append(wide[pl.ds(k, toks, stride=top), :].astype(BF16))
         p_slot = p_slot + sel * probs[k:k + 1, :]
+    h_slot = jnp.dot(
+        jnp.concatenate(chosen, axis=1), jnp.concatenate(values, axis=0), preferred_element_type=F32)
     p_slot = jnp.sum(p_slot, axis=1, keepdims=True)
     hs_ref[...] = h_slot
     ps_ref[...] = jnp.broadcast_to(p_slot, ps_ref.shape)
@@ -285,14 +287,13 @@
         move.wait()
 
 
-def turn_kernel(local_count, dev_count, beside_ref, far_ref, even_ref, *out_refs):
+def turn_kernel(local_count, dev_count, beside_ref, even_ref, *line_refs):
     per_home, per_copy = local_count * SLOT, dev_count * CAPR
     beside = beside_ref[...].astype(F32)[per_copy + per_home:]
     even = even_ref[...].astype(F32)
-    for n, out_ref in enumerate(out_refs):
+    for n, line_ref in enumerate(line_refs):
         span = slice(n * per_home, (n + 1) * per_home)
-        blocks = [far_ref[...].astype(F32)] * (n == 0) + [even[span], beside[span]]
-        out_ref[...] = jnp.concatenate(blocks, axis=0).astype(BF16)
+        line_ref[...] = jnp.concatenate([even[span], beside[span]], axis=0).astype(BF16)
 
 
 def early_kernel(local_count, dev_count, order, pieces, w_ref, slot_ref, *refs):
@@ -430,14 +431,14 @@
     )
     beside, far, near, own_rows, even_rows, w_held, slot = lax.optimization_barrier(
         (beside, far, near, own_rows, even_rows, w_held, slot))
-    far_beside = swap(far, 1, dev_count)
-    turned = call(
+    far_near = swap(far, 2, dev_count)
+    lines = call(
         functools.partial(turn_kernel, *sizes),
-        [shape((copies * (m == 2) + 2 * per_home, d_model + width), BF16) for m in even],
-        [(vmem, a) for a in (beside, far, even_rows)],
-    )
-    turned = [swap(a, m, dev_count) for a, m in zip(turned, even)]
-    near_beside = swap(near, 1, dev_count)
+        [shape((n, d_model + width), BF16) for n in [2 * per_home] * len(even)],
+        [(vmem, a) for a in (beside, even_rows)],
+    )
+    far_beside, near_beside = swap(far, 1, dev_count), swap(near, 1, dev_count)
+    lines = [swap(a, m, dev_count) for a, m in zip(lines, even)]
     pieces = {(0, HOME): (0, 0), (0, COPIES): (0, per_home), (1, COPIES): (1, 0), (1, HOME): (1, copies),
               (2, COPIES): (2, 0), (4, COPIES): (3, 0)}
     orders = [list(pieces)]
@@ -448,11 +449,11 @@
         [(vmem, a) for a in (w_held, slot, own_rows, beside, near, far)],
         flops=2 * height * d_model * local_count * width * 30,
     )
-    far_across = swap(turned[0][:copies], 1, dev_count)
-    arrays = [far_beside, near_beside, far_across, *turned]
-    pieces = {(5, COPIES): (0, 0), (3, COPIES): (1, 0), (7, COPIES): (2, 0), (6, COPIES): (3, 0)}
+    far_across = swap(far_near, 1, dev_count)
+    arrays = [far_beside, near_beside, far_near, far_across, *lines]
+    pieces = {(5, COPIES): (0, 0), (3, COPIES): (1, 0), (6, COPIES): (2, 0), (7, COPIES): (3, 0)}
     for n, m in enumerate(even):
-        pieces[m, HOME], pieces[m + 1, HOME] = ((3 + n, copies * (m == 2) + k * per_home) for k in range(2))
+        pieces[m, HOME], pieces[m + 1, HOME] = ((4 + n, k * per_home) for k in range(2))
     orders.append(list(pieces))
     height = padded(sum(per_home if kind == HOME else copies for _, kind in pieces))
     block = padded(per_home + copies)

time: 48.6 us -> 48 us (0.988)
  waiting for transfers between devices: 15.2 us -> 14.2 us
    ppermute x9 -> x10, waiting for transfers between devices: 10.9 us -> 9.97 us  [swap(): return lax.ppermute(x, 'expert', [(i, i ^ bits) for i in range(count)])]
    ppermute x9 -> x10, starting transfers between devices: 14.4 us -> 15 us  [swap(): return lax.ppermute(x, 'expert', [(i, i ^ bits) for i in range(count)])]
  transfers between devices with their start and end apart: 11 -> 12, of which waited for: 6 -> 7; matrix products, arithmetic and copies ran while one was open for 0% -> 0% of each run, Pallas kernels for 9% -> 10%
where the time goes in v10:
time: 48 us; the launch traced here: 47.6 us
  starting transfers between devices  18.5 us (39%)
  waiting for transfers between devices  14.2 us (30%)
  Pallas kernels  10 us (21%)
  local copies, waits for them, and re-layouts  4.04 us (8%)
  between operations  0.75 us (2%)
    ppermute x10, starting transfers between devices, swap(): return lax.ppermute(x, 'expert', [(i, i ^ bits) for i in range(count)])  15 us
    pallas_call x8, Pallas kernels, call(): pl.pallas_call(kernel, out_shape=out_shape, in_specs=[pl.BlockSpec(memory...  10 us
    ppermute x10, waiting for transfers between devices, swap(): return lax.ppermute(x, 'expert', [(i, i ^ bits) for i in range(count)])  9.97 us
    all_to_all x1, waiting for transfers between devices, gather_body(): lax.all_to_all(back, 'expert', split_axis=0, concat_axis=0, tiled=True)  4.26 us
    unnamed x18, local copies, waits for them, and re-layouts  4.04 us
    all_to_all x1, starting transfers between devices, gather_body(): lax.all_to_all(back, 'expert', split_axis=0, concat_axis=0, tiled=True)  3.47 us
  transfers between devices with their start and end apart: 12, of which 7 were waited for; matrix products, arithmetic and copies ran while one was open for 0% of the time, Pallas kernels for 10%

profile of v10, /device:TPU:0, one launch (start us, length us, event | category | flops | bytes accessed | tf_op | source)
XLA Modules:
  0.0 47.6 jit_solution(12619196615786755370)
XLA Ops:
  0.6 2.6 %shard_map.94 = (f32[72,128]{1,0:T(8,128)}, s32[72,128]{1,0:T(8,128)}, f32[72,128]{1,0:T(8,128)}, f32[72,128]{1,0:T(8,128)}, bf16[48,3712]{1,0:T(8,128)(2,1)}, /...) custom-call(s32[8]{0:T(128)} %replica_ref.1, s32[1,8]{1,0:T(1,128)} %refs_1_.1, ...), custom_call_target="tpu_custom_call" | custom-call | flops 66060288 | bytes 2224192 | tf_op jit(solution)/shard_map/pallas_call | solution.py:377
  3.2 3.0 %collective-permute-start = (bf16[48,3712]{1,0:T(8,128)(2,1)}, bf16[48,3712]{1,0:T(8,128)(2,1)S(1)}, u32[]{:S(2)}, u32[]{:S(2)}) collective-permute-start(bf16[48,3712]{1,0:T(8,128)(2,1)} %get-tuple-element.33), channel_id=1, source_target_pairs={{0,2},{2,0},{4,6},{6,4},{8,10},{10,8},{12,14},{14,12},{1,3},{3,1},... | collective-permute-start | bytes 1069064 | tf_op jit(solution)/shard_map/ppermute | solution.py:389
  6.2 1.6 %collective-permute-start.2 = (bf16[24,3712]{1,0:T(8,128)(2,1)}, bf16[24,3712]{1,0:T(8,128)(2,1)S(1)}, u32[]{:S(2)}, u32[]{:S(2)}) collective-permute-start(bf16[24,3712]{1,0:T(8,128)(2,1)} %get-tuple-element.34), channel_id=1, source_target_pairs={{0,4},{2,6},{4,0},{6,2},{8,12},{10,14},{12,8},{14,10},{1,5},{3,7},... | collective-permute-start | bytes 534536 | tf_op jit(solution)/shard_map/ppermute | solution.py:389
  7.8 2.6 %collective-permute-start.1 = (bf16[24,3712]{1,0:T(8,128)(2,1)}, bf16[24,3712]{1,0:T(8,128)(2,1)S(1)}, u32[]{:S(2)}, u32[]{:S(2)}) collective-permute-start(bf16[24,3712]{1,0:T(8,128)(2,1)} %get-tuple-element.34), channel_id=1, source_target_pairs={{0,8},{2,10},{4,12},{6,14},{8,0},{10,2},{12,4},{14,6},{1,9},{3,11}... | collective-permute-start | bytes 534536 | tf_op jit(solution)/shard_map/ppermute | solution.py:389
  10.4 0.0 copy-start
  10.4 1.5 %copy-done = bf16[2,128,3584]{2,1,0:T(8,128)(2,1)S(1)} copy-done((bf16[2,128,3584]{2,1,0:T(8,128)(2,1)S(1)}, bf16[2,128,3584]{2,1,0:T(8,128)(2,1)}, u32[]{:S(2)}) %copy-start) | copy-done | bytes 1835032
  11.9 0.0 copy-start.1
  11.9 0.9 %copy-done.1 = bf16[30,3712]{1,0:T(8,128)(2,1)S(1)} copy-done((bf16[30,3712]{1,0:T(8,128)(2,1)S(1)}, bf16[30,3712]{1,0:T(8,128)(2,1)}, u32[]{:S(2)}) %copy-start.1) | copy-done | bytes 222744
  12.8 0.0 copy-start.2
  12.8 0.9 %copy-done.2 = bf16[18,3712]{1,0:T(8,128)(2,1)S(1)} copy-done((bf16[18,3712]{1,0:T(8,128)(2,1)S(1)}, bf16[18,3712]{1,0:T(8,128)(2,1)}, u32[]{:S(2)}) %copy-start.2) | copy-done | bytes 133656
  13.7 0.0 copy-start.8
  13.7 0.7 %copy-done.8 = s32[8]{0:T(128)S(1)} copy-done((s32[8]{0:T(128)S(1)}, s32[8]{0:T(128)}, u32[]{:S(2)}) %copy-start.8) | copy-done | bytes 56
  14.4 1.2 %shard_map.95 = (bf16[30,3712]{1,0:T(8,128)(2,1)S(1)}, bf16[18,3712]{1,0:T(8,128)(2,1)S(1)}, bf16[256,3584]{1,0:T(8,128)(2,1)S(1)}, s32[30,128]{1,0:T(8,128)S(1)}) custom-call(s32[8]{0:T(128)S(1)} %copy-done.8, bf16[256,3584]{1,0:T(8,128)(2,1)S(1)} %bitcast.8, bf16[30,3712]{1,0:T(8,128)(2,1)S(1)} %copy-done.1, bf16[18,3712]{1,0:T(8,128)(2,1)S(1)} %copy-done.2), custom_call_target="tpu_custom_call" | custom-call | bytes 4398112 | tf_op jit(solution)/shard_map/pallas_call | solution.py:377
  15.6 0.4 collective-permute-done.2.refs_2_
  16.1 2.5 %collective-permute-done.1.refs_3_ = bf16[24,3712]{1,0:T(8,128)(2,1)S(1)} collective-permute-done((bf16[24,3712]{1,0:T(8,128)(2,1)}, bf16[24,3712]{1,0:T(8,128)(2,1)S(1)}, u32[]{:S(2)}, u32[]{:S(2)}) %collective-permute-start.1) | collective-permute-done | bytes 178208 | tf_op jit(solution)/shard_map/ppermute | solution.py:389
  18.6 0.0 collective-permute-done.refs_1_.beside_ref
  18.6 0.3 collective-permute-start.5
  18.9 0.1 shard_map.97
  19.0 1.8 %collective-permute-start.7 = (bf16[12,3712]{1,0:T(8,128)(2,1)S(1)}, bf16[12,3712]{1,0:T(8,128)(2,1)S(1)}, u32[]{:S(2)}, u32[]{:S(2)}) collective-permute-start(bf16[12,3712]{1,0:T(8,128)(2,1)S(1)} %get-tuple-element.49), channel_id=1, source_target_pairs={{0,4},{2,6},{4,0},{6,2},{8,12},{10,14},{12,8},{14,10},{1,5},{3,7},... | collective-permute-start | bytes 267272 | tf_op jit(solution)/shard_map/ppermute | solution.py:389
  20.8 0.5 %collective-permute-start.3 = (bf16[24,3712]{1,0:T(8,128)(2,1)S(1)}, bf16[24,3712]{1,0:T(8,128)(2,1)S(1)}, u32[]{:S(2)}, u32[]{:S(2)}) collective-permute-start(bf16[24,3712]{1,0:T(8,128)(2,1)S(1)} %collective-permute-done.1.refs_3_), channel_id=1, source_target_pairs={{0,2},{2,0},{4,6},{6,4},{8,10},{10,8},{12,14},{14,12},{1,3},{3,1},... | collective-permute-start | bytes 534536 | tf_op jit(solution)/shard_map/ppermute | solution.py:389
  21.3 1.5 %collective-permute-start.4 = (bf16[24,3712]{1,0:T(8,128)(2,1)S(1)}, bf16[24,3712]{1,0:T(8,128)(2,1)S(1)}, u32[]{:S(2)}, u32[]{:S(2)}) collective-permute-start(bf16[24,3712]{1,0:T(8,128)(2,1)S(1)} %collective-permute-done.2.refs_2_), channel_id=1, source_target_pairs={{0,2},{2,0},{4,6},{6,4},{8,10},{10,8},{12,14},{14,12},{1,3},{3,1},... | collective-permute-start | bytes 534536 | tf_op jit(solution)/shard_map/ppermute | solution.py:389
  22.8 1.1 %collective-permute-start.8 = (bf16[12,3712]{1,0:T(8,128)(2,1)S(1)}, bf16[12,3712]{1,0:T(8,128)(2,1)S(1)}, u32[]{:S(2)}, u32[]{:S(2)}) collective-permute-start(bf16[12,3712]{1,0:T(8,128)(2,1)S(1)} %get-tuple-element.50), channel_id=1, source_target_pairs={{0,8},{2,10},{4,12},{6,14},{8,0},{10,2},{12,4},{14,6},{1,9},{3,11}... | collective-permute-start | bytes 267272 | tf_op jit(solution)/shard_map/ppermute | solution.py:389
  23.8 3.3 %collective-permute-done.7.refs_4_ = bf16[12,3712]{1,0:T(8,128)(2,1)S(1)} collective-permute-done((bf16[12,3712]{1,0:T(8,128)(2,1)S(1)}, bf16[12,3712]{1,0:T(8,128)(2,1)S(1)}, u32[]{:S(2)}, u32[]{:S(2)}) %collective-permute-start.7) | collective-permute-done | bytes 89120 | tf_op jit(solution)/shard_map/ppermute | solution.py:389
  27.2 1.6 %collective-permute-start.9 = (bf16[12,3712]{1,0:T(8,128)(2,1)S(1)}, bf16[12,3712]{1,0:T(8,128)(2,1)S(1)}, u32[]{:S(2)}, u32[]{:S(2)}) collective-permute-start(bf16[12,3712]{1,0:T(8,128)(2,1)S(1)} %get-tuple-element.51), channel_id=1, source_target_pairs={{0,12},{2,14},{4,8},{6,10},{8,4},{10,6},{12,0},{14,2},{1,13},{3,15... | collective-permute-start | bytes 267272 | tf_op jit(solution)/shard_map/ppermute | solution.py:389
  28.8 0.0 collective-permute-done.5.refs_2_
  28.8 1.0 %collective-permute-start.6 = (bf16[24,3712]{1,0:T(8,128)(2,1)S(1)}, bf16[24,3712]{1,0:T(8,128)(2,1)S(1)}, u32[]{:S(2)}, u32[]{:S(2)}) collective-permute-start(bf16[24,3712]{1,0:T(8,128)(2,1)S(1)} %collective-permute-done.5.refs_2_), channel_id=1, source_target_pairs={{0,2},{2,0},{4,6},{6,4},{8,10},{10,8},{12,14},{14,12},{1,3},{3,1},... | collective-permute-start | bytes 534536 | tf_op jit(solution)/shard_map/ppermute | solution.py:389
  29.8 0.7 %shard_map.96 = (bf16[112,3712]{1,0:T(8,128)(2,1)S(1)}, f32[112,128]{1,0:T(8,128)S(1)}) custom-call(bf16[256,3584]{1,0:T(8,128)(2,1)S(1)} %get-tuple-element.41.w_ref, s32[30,128]{1,0:T(8,128)S(1)} %get-tuple-element.42.slot_ref, bf16[30,3712]{1,0:T(8,128)(2,1)S(1)} %get-tuple-element.43.refs_0_, ...), custom_call_target="tpu_custom_call" | custom-call | flops 6165626880 | bytes 3674624 | tf_op jit(solution)/shard_map/pallas_call | solution.py:377
  30.6 0.6 %collective-permute-done.8.refs_5_ = bf16[12,3712]{1,0:T(8,128)(2,1)S(1)} collective-permute-done((bf16[12,3712]{1,0:T(8,128)(2,1)S(1)}, bf16[12,3712]{1,0:T(8,128)(2,1)S(1)}, u32[]{:S(2)}, u32[]{:S(2)}) %collective-permute-start.8) | collective-permute-done | bytes 89120 | tf_op jit(solution)/shard_map/ppermute | solution.py:389
  31.1 2.8 %collective-permute-done.9.refs_6_ = bf16[12,3712]{1,0:T(8,128)(2,1)S(1)} collective-permute-done((bf16[12,3712]{1,0:T(8,128)(2,1)S(1)}, bf16[12,3712]{1,0:T(8,128)(2,1)S(1)}, u32[]{:S(2)}, u32[]{:S(2)}) %collective-permute-start.9) | collective-permute-done | bytes 89120 | tf_op jit(solution)/shard_map/ppermute | solution.py:389
  33.9 0.0 collective-permute-done.4.refs_1_
  33.9 0.0 collective-permute-done.3.refs_0_
  33.9 0.4 collective-permute-done.6.refs_3_
  34.3 1.4 %shard_map.98 = (bf16[144,3712]{1,0:T(8,128)(2,1)S(1)}, bf16[256,128]{1,0:T(8,128)(2,1)}) custom-call(f32[112,128]{1,0:T(8,128)S(1)} %get-tuple-element.47.own_ref, bf16[256,3584]{1,0:T(8,128)(2,1)S(1)} %get-tuple-element.41.w_ref, s32[30,128]{1,0:T(8,128)S(1)} %get-tuple-element.42.slot_ref, bf16[24,3712]{1,0:T(8,128)(2,1)S(1)} %collective-permute-done.3.refs_0_, ...), custom_call_target="tpu_custom_call" | custom-call | flops 264241152 | bytes 4022272 | tf_op jit(solution)/shard_map/pallas_call | solution.py:377
  35.7 0.4 shard_map.99
  36.1 0.1 collective-permute-start.10
  36.2 3.5 %all-to-all-start = ((bf16[8,32,128]{2,1,0:T(8,128)(2,1)}), bf16[8,32,128]{2,1,0:T(8,128)(2,1)S(1)}, u32[]{:S(2)}, u32[]{:S(2)}) async-start(bf16[8,32,128]{2,1,0:T(8,128)(2,1)} %bitcast.4), calls=%async_computation | async-start | bytes 131072 | tf_op jit(solution)/shard_map/all_to_all | solution.py:467
  39.7 0.0 copy-start.3
  39.7 0.0 copy-start.4
  39.7 0.0 copy-start.5
  39.7 0.0 copy-start.6
  39.7 0.0 copy-start.7
  39.7 0.0 collective-permute-done.10.arrived_ref
  39.7 2.6 %shard_map.100 = bf16[256,1792]{1,0:T(8,128)(2,1)} custom-call(s32[30,128]{1,0:T(8,128)S(1)} %get-tuple-element.42.slot_ref, bf16[112,3712]{1,0:T(8,128)(2,1)S(1)} %get-tuple-element.53.early_ref, bf16[144,3712]{1,0:T(8,128)(2,1)S(1)} %get-tuple-element.54.late_ref, bf16[256,1792]{1,0:T(8,128)(2,1)} %collective-permute-done.10.arrived_ref), custom_call_target="tpu_custom_call" | custom-call | flops 6606028800 | bytes 3750912 | tf_op jit(solution)/shard_map/pallas_call | solution.py:377
  42.3 4.3 %all-to-all-done.back_ref = bf16[8,32,128]{2,1,0:T(8,128)(2,1)S(1)} async-done(((bf16[8,32,128]{2,1,0:T(8,128)(2,1)}), bf16[8,32,128]{2,1,0:T(8,128)(2,1)S(1)}, u32[]{:S(2)}, u32[]{:S(2)}) %all-to-all-start) | async-done | bytes 65568 | tf_op jit(solution)/shard_map/all_to_all | solution.py:467
  46.6 0.0 copy-done.3
  46.6 0.0 copy-done.4
  46.6 0.0 copy-done.5
  46.6 0.0 copy-done.6
  46.6 0.0 copy-done.7
  46.6 1.0 %shard_map.101 = (bf16[1024,128]{1,0:T(8,128)(2,1)}, bf16[8,128]{1,0:T(8,128)(2,1)}) custom-call(bf16[8,32,128]{2,1,0:T(8,128)(2,1)S(1)} %all-to-all-done.back_ref, f32[72,128]{1,0:T(8,128)S(1)} %copy-done.3, s32[72,128]{1,0:T(8,128)S(1)} %copy-done.4, f32[72,128]{1,0:T(8,128)S(1)} %copy-done.5, f32[72,128]{1,0:T(8,128)S(1)} %copy-done.6, s32[8,128]{1,0:T(8,128)S(1)} %bitcast.10), custom_call_target="tpu_custom_call" | custom-call | flops 18874368 | bytes 481280 | tf_op jit(solution)/shard_map/pallas_call | solution.py:377
Async XLA Ops:
  3.2 15.4 %collective-permute-start = (bf16[48,3712]{1,0:T(8,128)(2,1)}, bf16[48,3712]{1,0:T(8,128)(2,1)S(1)}, u32[]{:S(2)}, u32[]{:S(2)}) collective-permute-start(bf16[48,3712]{1,0:T(8,128)(2,1)} %get-tuple-element.33), channel_id=1, source_target_pairs={{0,2},{2,0},{4,6},{6,4},{8,10},{10,8},{12,14},{14,12},{1,3},{3,1},... | collective-permute-start | bytes 1069064 | tf_op jit(solution)/shard_map/ppermute | solution.py:389
  6.2 9.9 %collective-permute-start.2 = (bf16[24,3712]{1,0:T(8,128)(2,1)}, bf16[24,3712]{1,0:T(8,128)(2,1)S(1)}, u32[]{:S(2)}, u32[]{:S(2)}) collective-permute-start(bf16[24,3712]{1,0:T(8,128)(2,1)} %get-tuple-element.34), channel_id=1, source_target_pairs={{0,4},{2,6},{4,0},{6,2},{8,12},{10,14},{12,8},{14,10},{1,5},{3,7},... | collective-permute-start | bytes 534536 | tf_op jit(solution)/shard_map/ppermute | solution.py:389
  7.8 10.8 %collective-permute-start.1 = (bf16[24,3712]{1,0:T(8,128)(2,1)}, bf16[24,3712]{1,0:T(8,128)(2,1)S(1)}, u32[]{:S(2)}, u32[]{:S(2)}) collective-permute-start(bf16[24,3712]{1,0:T(8,128)(2,1)} %get-tuple-element.34), channel_id=1, source_target_pairs={{0,8},{2,10},{4,12},{6,14},{8,0},{10,2},{12,4},{14,6},{1,9},{3,11}... | collective-permute-start | bytes 534536 | tf_op jit(solution)/shard_map/ppermute | solution.py:389
  10.4 1.5 %copy-start = (bf16[2,128,3584]{2,1,0:T(8,128)(2,1)S(1)}, bf16[2,128,3584]{2,1,0:T(8,128)(2,1)}, u32[]{:S(2)}) copy-start(bf16[2,128,3584]{2,1,0:T(8,128)(2,1)} %param.13) | copy-start | bytes 5505028
  11.9 0.9 %copy-start.1 = (bf16[30,3712]{1,0:T(8,128)(2,1)S(1)}, bf16[30,3712]{1,0:T(8,128)(2,1)}, u32[]{:S(2)}) copy-start(bf16[30,3712]{1,0:T(8,128)(2,1)} %get-tuple-element.35.own_hbm) | copy-start | bytes 668164
  12.8 0.9 %copy-start.2 = (bf16[18,3712]{1,0:T(8,128)(2,1)S(1)}, bf16[18,3712]{1,0:T(8,128)(2,1)}, u32[]{:S(2)}) copy-start(bf16[18,3712]{1,0:T(8,128)(2,1)} %get-tuple-element.36.even_hbm) | copy-start | bytes 400900
  13.7 0.7 %copy-start.8 = (s32[8]{0:T(128)S(1)}, s32[8]{0:T(128)}, u32[]{:S(2)}) copy-start(s32[8]{0:T(128)} %replica_ref.1) | copy-start | bytes 100
  18.6 10.2 %collective-permute-start.5 = (bf16[24,3712]{1,0:T(8,128)(2,1)S(1)}, bf16[24,3712]{1,0:T(8,128)(2,1)S(1)}, u32[]{:S(2)}, u32[]{:S(2)}) collective-permute-start(bf16[24,3712]{1,0:T(8,128)(2,1)S(1)} %collective-permute-done.1.refs_3_), channel_id=1, source_target_pairs={{0,4},{2,6},{4,0},{6,2},{8,12},{10,14},{12,8},{14,10},{1,5},{3,7},... | collective-permute-start | bytes 534536 | tf_op jit(solution)/shard_map/ppermute | solution.py:389
  19.0 8.2 %collective-permute-start.7 = (bf16[12,3712]{1,0:T(8,128)(2,1)S(1)}, bf16[12,3712]{1,0:T(8,128)(2,1)S(1)}, u32[]{:S(2)}, u32[]{:S(2)}) collective-permute-start(bf16[12,3712]{1,0:T(8,128)(2,1)S(1)} %get-tuple-element.49), channel_id=1, source_target_pairs={{0,4},{2,6},{4,0},{6,2},{8,12},{10,14},{12,8},{14,10},{1,5},{3,7},... | collective-permute-start | bytes 267272 | tf_op jit(solution)/shard_map/ppermute | solution.py:389
  20.8 13.2 %collective-permute-start.3 = (bf16[24,3712]{1,0:T(8,128)(2,1)S(1)}, bf16[24,3712]{1,0:T(8,128)(2,1)S(1)}, u32[]{:S(2)}, u32[]{:S(2)}) collective-permute-start(bf16[24,3712]{1,0:T(8,128)(2,1)S(1)} %collective-permute-done.1.refs_3_), channel_id=1, source_target_pairs={{0,2},{2,0},{4,6},{6,4},{8,10},{10,8},{12,14},{14,12},{1,3},{3,1},... | collective-permute-start | bytes 534536 | tf_op jit(solution)/shard_map/ppermute | solution.py:389
  21.3 12.6 %collective-permute-start.4 = (bf16[24,3712]{1,0:T(8,128)(2,1)S(1)}, bf16[24,3712]{1,0:T(8,128)(2,1)S(1)}, u32[]{:S(2)}, u32[]{:S(2)}) collective-permute-start(bf16[24,3712]{1,0:T(8,128)(2,1)S(1)} %collective-permute-done.2.refs_2_), channel_id=1, source_target_pairs={{0,2},{2,0},{4,6},{6,4},{8,10},{10,8},{12,14},{14,12},{1,3},{3,1},... | collective-permute-start | bytes 534536 | tf_op jit(solution)/shard_map/ppermute | solution.py:389
  22.8 8.3 %collective-permute-start.8 = (bf16[12,3712]{1,0:T(8,128)(2,1)S(1)}, bf16[12,3712]{1,0:T(8,128)(2,1)S(1)}, u32[]{:S(2)}, u32[]{:S(2)}) collective-permute-start(bf16[12,3712]{1,0:T(8,128)(2,1)S(1)} %get-tuple-element.50), channel_id=1, source_target_pairs={{0,8},{2,10},{4,12},{6,14},{8,0},{10,2},{12,4},{14,6},{1,9},{3,11}... | collective-permute-start | bytes 267272 | tf_op jit(solution)/shard_map/ppermute | solution.py:389
  27.2 6.7 %collective-permute-start.9 = (bf16[12,3712]{1,0:T(8,128)(2,1)S(1)}, bf16[12,3712]{1,0:T(8,128)(2,1)S(1)}, u32[]{:S(2)}, u32[]{:S(2)}) collective-permute-start(bf16[12,3712]{1,0:T(8,128)(2,1)S(1)} %get-tuple-element.51), channel_id=1, source_target_pairs={{0,12},{2,14},{4,8},{6,10},{8,4},{10,6},{12,0},{14,2},{1,13},{3,15... | collective-permute-start | bytes 267272 | tf_op jit(solution)/shard_map/ppermute | solution.py:389
  28.8 5.5 %collective-permute-start.6 = (bf16[24,3712]{1,0:T(8,128)(2,1)S(1)}, bf16[24,3712]{1,0:T(8,128)(2,1)S(1)}, u32[]{:S(2)}, u32[]{:S(2)}) collective-permute-start(bf16[24,3712]{1,0:T(8,128)(2,1)S(1)} %collective-permute-done.5.refs_2_), channel_id=1, source_target_pairs={{0,2},{2,0},{4,6},{6,4},{8,10},{10,8},{12,14},{14,12},{1,3},{3,1},... | collective-permute-start | bytes 534536 | tf_op jit(solution)/shard_map/ppermute | solution.py:389
  36.1 3.6 %collective-permute-start.10 = (bf16[256,1792]{1,0:T(8,128)(2,1)S(1)}, bf16[256,1792]{1,0:T(8,128)(2,1)}, u32[]{:S(2)}, u32[]{:S(2)}) collective-permute-start(bf16[256,1792]{1,0:T(8,128)(2,1)S(1)} %shard_map.99), channel_id=1, source_target_pairs={{0,1},{1,0},{2,3},{3,2},{4,5},{5,4},{6,7},{7,6},{8,9},{9,8},{10,11... | collective-permute-start | bytes 2752520 | tf_op jit(solution)/shard_map/ppermute | solution.py:476
  36.2 10.4 %all-to-all-start = ((bf16[8,32,128]{2,1,0:T(8,128)(2,1)}), bf16[8,32,128]{2,1,0:T(8,128)(2,1)S(1)}, u32[]{:S(2)}, u32[]{:S(2)}) async-start(bf16[8,32,128]{2,1,0:T(8,128)(2,1)} %bitcast.4), calls=%async_computation | async-start | bytes 131072 | tf_op jit(solution)/shard_map/all_to_all | solution.py:467
  39.7 6.9 %copy-start.3 = (f32[72,128]{1,0:T(8,128)S(1)}, f32[72,128]{1,0:T(8,128)}, u32[]{:S(2)}) copy-start(f32[72,128]{1,0:T(8,128)} %get-tuple-element.56.pick_ref) | copy-start | bytes 110596
  39.7 6.9 %copy-start.4 = (s32[72,128]{1,0:T(8,128)S(1)}, s32[72,128]{1,0:T(8,128)}, u32[]{:S(2)}) copy-start(s32[72,128]{1,0:T(8,128)} %get-tuple-element.57.expert_ref) | copy-start | bytes 110596
  39.7 6.9 %copy-start.5 = (f32[72,128]{1,0:T(8,128)S(1)}, f32[72,128]{1,0:T(8,128)}, u32[]{:S(2)}) copy-start(f32[72,128]{1,0:T(8,128)} %get-tuple-element.58.hs_ref) | copy-start | bytes 110596
  39.7 6.9 %copy-start.6 = (f32[72,128]{1,0:T(8,128)S(1)}, f32[72,128]{1,0:T(8,128)}, u32[]{:S(2)}) copy-start(f32[72,128]{1,0:T(8,128)} %get-tuple-element.59.ps_ref) | copy-start | bytes 110596
  39.7 6.9 %copy-start.7 = (s32[128,8]{0,1:T(8,128)S(1)}, s32[128,8]{0,1:T(8,128)}, u32[]{:S(2)}) copy-start(s32[128,8]{0,1:T(8,128)} %param.10) | copy-start | bytes 12292

commit v11 on v10

--- a/solution.py
+++ b/solution.py
@@ -440,20 +440,20 @@
     far_beside, near_beside = swap(far, 1, dev_count), swap(near, 1, dev_count)
     lines = [swap(a, m, dev_count) for a, m in zip(lines, even)]
     pieces = {(0, HOME): (0, 0), (0, COPIES): (0, per_home), (1, COPIES): (1, 0), (1, HOME): (1, copies),
-              (2, COPIES): (2, 0), (4, COPIES): (3, 0)}
+              (2, COPIES): (2, 0), (4, COPIES): (3, 0), (5, COPIES): (4, 0), (3, COPIES): (5, 0)}
     orders = [list(pieces)]
     height = padded(sum(per_home if kind == HOME else copies for _, kind in pieces))
     early_rows, own = call(
         functools.partial(early_kernel, *sizes, orders[0], pieces),
         (shape((height, d_model + width), BF16), shape((height, width), F32)),
-        [(vmem, a) for a in (w_held, slot, own_rows, beside, near, far)],
+        [(vmem, a) for a in (w_held, slot, own_rows, beside, near, far, far_beside, near_beside)],
         flops=2 * height * d_model * local_count * width * 30,
     )
     far_across = swap(far_near, 1, dev_count)
-    arrays = [far_beside, near_beside, far_near, far_across, *lines]
-    pieces = {(5, COPIES): (0, 0), (3, COPIES): (1, 0), (6, COPIES): (2, 0), (7, COPIES): (3, 0)}
+    arrays = [far_near, far_across, *lines]
+    pieces = {(6, COPIES): (0, 0), (7, COPIES): (1, 0)}
     for n, m in enumerate(even):
-        pieces[m, HOME], pieces[m + 1, HOME] = ((4 + n, k * per_home) for k in range(2))
+        pieces[m, HOME], pieces[m + 1, HOME] = ((2 + n, k * per_home) for k in range(2))
     orders.append(list(pieces))
     height = padded(sum(per_home if kind == HOME else copies for _, kind in pieces))
     block = padded(per_home + copies)

time: 48 us -> 49.1 us (1.023)
  starting transfers between devices: 18.5 us -> 22.6 us
  waiting for transfers between devices: 14.2 us -> 11.4 us
    ppermute x10, waiting for transfers between devices: 9.97 us -> 7.11 us  [swap(): return lax.ppermute(x, 'expert', [(i, i ^ bits) for i in range(count)])]
    ppermute x10, starting transfers between devices: 15 us -> 17.2 us  [swap(): return lax.ppermute(x, 'expert', [(i, i ^ bits) for i in range(count)])]
    all_to_all x1, starting transfers between devices: 3.47 us -> 5.3 us  [gather_body(): lax.all_to_all(back, 'expert', split_axis=0, concat_axis=0, tiled=True)]
  transfers between devices with their start and end apart: 12 -> 12, of which waited for: 7 -> 5; matrix products, arithmetic and copies ran while one was open for 0% -> 0% of each run, Pallas kernels for 10% -> 10%
where the time goes in v11:
time: 49.1 us; the launch traced here: 48.8 us
  starting transfers between devices  22.6 us (46%)
  waiting for transfers between devices  11.4 us (23%)
  Pallas kernels  10.1 us (21%)
  local copies, waits for them, and re-layouts  4.04 us (8%)
  between operations  0.76 us (2%)
    ppermute x10, starting transfers between devices, swap(): return lax.ppermute(x, 'expert', [(i, i ^ bits) for i in range(count)])  17.2 us
    pallas_call x8, Pallas kernels, call(): pl.pallas_call(kernel, out_shape=out_shape, in_specs=[pl.BlockSpec(memory...  10.1 us
    ppermute x10, waiting for transfers between devices, swap(): return lax.ppermute(x, 'expert', [(i, i ^ bits) for i in range(count)])  7.11 us
    all_to_all x1, starting transfers between devices, gather_body(): lax.all_to_all(back, 'expert', split_axis=0, concat_axis=0, tiled=True)  5.3 us
    all_to_all x1, waiting for transfers between devices, gather_body(): lax.all_to_all(back, 'expert', split_axis=0, concat_axis=0, tiled=True)  4.26 us
    unnamed x18, local copies, waits for them, and re-layouts  4.04 us
  transfers between devices with their start and end apart: 12, of which 5 were waited for; matrix products, arithmetic and copies ran while one was open for 0% of the time, Pallas kernels for 10%

profile of v11, /device:TPU:0, one launch (start us, length us, event | category | flops | bytes accessed | tf_op | source)
XLA Modules:
  0.0 48.8 jit_solution(3934237720545011273)
XLA Ops:
  0.6 2.6 %shard_map.94 = (f32[72,128]{1,0:T(8,128)}, s32[72,128]{1,0:T(8,128)}, f32[72,128]{1,0:T(8,128)}, f32[72,128]{1,0:T(8,128)}, bf16[48,3712]{1,0:T(8,128)(2,1)}, /...) custom-call(s32[8]{0:T(128)} %replica_ref.1, s32[1,8]{1,0:T(1,128)} %refs_1_.1, ...), custom_call_target="tpu_custom_call" | custom-call | flops 66060288 | bytes 2224192 | tf_op jit(solution)/shard_map/pallas_call | solution.py:377
  3.2 3.0 %collective-permute-start = (bf16[48,3712]{1,0:T(8,128)(2,1)}, bf16[48,3712]{1,0:T(8,128)(2,1)S(1)}, u32[]{:S(2)}, u32[]{:S(2)}) collective-permute-start(bf16[48,3712]{1,0:T(8,128)(2,1)} %get-tuple-element.33), channel_id=1, source_target_pairs={{0,2},{2,0},{4,6},{6,4},{8,10},{10,8},{12,14},{14,12},{1,3},{3,1},... | collective-permute-start | bytes 1069064 | tf_op jit(solution)/shard_map/ppermute | solution.py:389
  6.2 2.6 %collective-permute-start.1 = (bf16[24,3712]{1,0:T(8,128)(2,1)}, bf16[24,3712]{1,0:T(8,128)(2,1)S(1)}, u32[]{:S(2)}, u32[]{:S(2)}) collective-permute-start(bf16[24,3712]{1,0:T(8,128)(2,1)} %get-tuple-element.34), channel_id=1, source_target_pairs={{0,8},{2,10},{4,12},{6,14},{8,0},{10,2},{12,4},{14,6},{1,9},{3,11}... | collective-permute-start | bytes 534536 | tf_op jit(solution)/shard_map/ppermute | solution.py:389
  8.8 1.6 %collective-permute-start.2 = (bf16[24,3712]{1,0:T(8,128)(2,1)}, bf16[24,3712]{1,0:T(8,128)(2,1)S(1)}, u32[]{:S(2)}, u32[]{:S(2)}) collective-permute-start(bf16[24,3712]{1,0:T(8,128)(2,1)} %get-tuple-element.34), channel_id=1, source_target_pairs={{0,4},{2,6},{4,0},{6,2},{8,12},{10,14},{12,8},{14,10},{1,5},{3,7},... | collective-permute-start | bytes 534536 | tf_op jit(solution)/shard_map/ppermute | solution.py:389
  10.4 0.0 copy-start
  10.4 1.5 %copy-done = bf16[2,128,3584]{2,1,0:T(8,128)(2,1)S(1)} copy-done((bf16[2,128,3584]{2,1,0:T(8,128)(2,1)S(1)}, bf16[2,128,3584]{2,1,0:T(8,128)(2,1)}, u32[]{:S(2)}) %copy-start) | copy-done | bytes 1835032
  11.9 0.0 copy-start.1
  11.9 0.9 %copy-done.1 = bf16[30,3712]{1,0:T(8,128)(2,1)S(1)} copy-done((bf16[30,3712]{1,0:T(8,128)(2,1)S(1)}, bf16[30,3712]{1,0:T(8,128)(2,1)}, u32[]{:S(2)}) %copy-start.1) | copy-done | bytes 222744
  12.8 0.0 copy-start.2
  12.8 0.9 %copy-done.2 = bf16[18,3712]{1,0:T(8,128)(2,1)S(1)} copy-done((bf16[18,3712]{1,0:T(8,128)(2,1)S(1)}, bf16[18,3712]{1,0:T(8,128)(2,1)}, u32[]{:S(2)}) %copy-start.2) | copy-done | bytes 133656
  13.7 0.0 copy-start.8
  13.7 0.7 %copy-done.8 = s32[8]{0:T(128)S(1)} copy-done((s32[8]{0:T(128)S(1)}, s32[8]{0:T(128)}, u32[]{:S(2)}) %copy-start.8) | copy-done | bytes 56
  14.4 1.2 %shard_map.95 = (bf16[30,3712]{1,0:T(8,128)(2,1)S(1)}, bf16[18,3712]{1,0:T(8,128)(2,1)S(1)}, bf16[256,3584]{1,0:T(8,128)(2,1)S(1)}, s32[30,128]{1,0:T(8,128)S(1)}) custom-call(s32[8]{0:T(128)S(1)} %copy-done.8, bf16[256,3584]{1,0:T(8,128)(2,1)S(1)} %bitcast.8, bf16[30,3712]{1,0:T(8,128)(2,1)S(1)} %copy-done.1, bf16[18,3712]{1,0:T(8,128)(2,1)S(1)} %copy-done.2), custom_call_target="tpu_custom_call" | custom-call | bytes 4398112 | tf_op jit(solution)/shard_map/pallas_call | solution.py:377
  15.6 1.6 %collective-permute-done.1.refs_3_ = bf16[24,3712]{1,0:T(8,128)(2,1)S(1)} collective-permute-done((bf16[24,3712]{1,0:T(8,128)(2,1)}, bf16[24,3712]{1,0:T(8,128)(2,1)S(1)}, u32[]{:S(2)}, u32[]{:S(2)}) %collective-permute-start.1) | collective-permute-done | bytes 178208 | tf_op jit(solution)/shard_map/ppermute | solution.py:389
  17.2 0.2 collective-permute-done.2.refs_2_
  17.4 0.0 collective-permute-done.refs_1_.beside_ref
  17.4 0.5 collective-permute-start.3
  17.9 1.5 %collective-permute-start.5 = (bf16[24,3712]{1,0:T(8,128)(2,1)S(1)}, bf16[24,3712]{1,0:T(8,128)(2,1)S(1)}, u32[]{:S(2)}, u32[]{:S(2)}) collective-permute-start(bf16[24,3712]{1,0:T(8,128)(2,1)S(1)} %collective-permute-done.1.refs_3_), channel_id=1, source_target_pairs={{0,4},{2,6},{4,0},{6,2},{8,12},{10,14},{12,8},{14,10},{1,5},{3,7},... | collective-permute-start | bytes 534536 | tf_op jit(solution)/shard_map/ppermute | solution.py:389
  19.4 1.5 %collective-permute-start.4 = (bf16[24,3712]{1,0:T(8,128)(2,1)S(1)}, bf16[24,3712]{1,0:T(8,128)(2,1)S(1)}, u32[]{:S(2)}, u32[]{:S(2)}) collective-permute-start(bf16[24,3712]{1,0:T(8,128)(2,1)S(1)} %collective-permute-done.2.refs_2_), channel_id=1, source_target_pairs={{0,2},{2,0},{4,6},{6,4},{8,10},{10,8},{12,14},{14,12},{1,3},{3,1},... | collective-permute-start | bytes 534536 | tf_op jit(solution)/shard_map/ppermute | solution.py:389
  20.9 0.1 shard_map.97
  21.0 0.7 %collective-permute-start.7 = (bf16[12,3712]{1,0:T(8,128)(2,1)S(1)}, bf16[12,3712]{1,0:T(8,128)(2,1)S(1)}, u32[]{:S(2)}, u32[]{:S(2)}) collective-permute-start(bf16[12,3712]{1,0:T(8,128)(2,1)S(1)} %get-tuple-element.49), channel_id=1, source_target_pairs={{0,4},{2,6},{4,0},{6,2},{8,12},{10,14},{12,8},{14,10},{1,5},{3,7},... | collective-permute-start | bytes 267272 | tf_op jit(solution)/shard_map/ppermute | solution.py:389
  21.6 1.8 %collective-permute-start.8 = (bf16[12,3712]{1,0:T(8,128)(2,1)S(1)}, bf16[12,3712]{1,0:T(8,128)(2,1)S(1)}, u32[]{:S(2)}, u32[]{:S(2)}) collective-permute-start(bf16[12,3712]{1,0:T(8,128)(2,1)S(1)} %get-tuple-element.50), channel_id=1, source_target_pairs={{0,8},{2,10},{4,12},{6,14},{8,0},{10,2},{12,4},{14,6},{1,9},{3,11}... | collective-permute-start | bytes 267272 | tf_op jit(solution)/shard_map/ppermute | solution.py:389
  23.4 1.0 %collective-permute-done.3.refs_4_ = bf16[24,3712]{1,0:T(8,128)(2,1)S(1)} collective-permute-done((bf16[24,3712]{1,0:T(8,128)(2,1)S(1)}, bf16[24,3712]{1,0:T(8,128)(2,1)S(1)}, u32[]{:S(2)}, u32[]{:S(2)}) %collective-permute-start.3) | collective-permute-done | bytes 178208 | tf_op jit(solution)/shard_map/ppermute | solution.py:389
  24.4 3.6 %collective-permute-start.9 = (bf16[12,3712]{1,0:T(8,128)(2,1)S(1)}, bf16[12,3712]{1,0:T(8,128)(2,1)S(1)}, u32[]{:S(2)}, u32[]{:S(2)}) collective-permute-start(bf16[12,3712]{1,0:T(8,128)(2,1)S(1)} %get-tuple-element.51), channel_id=1, source_target_pairs={{0,12},{2,14},{4,8},{6,10},{8,4},{10,6},{12,0},{14,2},{1,13},{3,15... | collective-permute-start | bytes 267272 | tf_op jit(solution)/shard_map/ppermute | solution.py:389
  28.0 0.0 collective-permute-done.5.refs_0_
  28.0 0.5 %collective-permute-start.6 = (bf16[24,3712]{1,0:T(8,128)(2,1)S(1)}, bf16[24,3712]{1,0:T(8,128)(2,1)S(1)}, u32[]{:S(2)}, u32[]{:S(2)}) collective-permute-start(bf16[24,3712]{1,0:T(8,128)(2,1)S(1)} %collective-permute-done.5.refs_0_), channel_id=1, source_target_pairs={{0,2},{2,0},{4,6},{6,4},{8,10},{10,8},{12,14},{14,12},{1,3},{3,1},... | collective-permute-start | bytes 534536 | tf_op jit(solution)/shard_map/ppermute | solution.py:389
  28.5 0.0 collective-permute-done.4.refs_5_
  28.5 0.8 %shard_map.96 = (bf16[160,3712]{1,0:T(8,128)(2,1)S(1)}, f32[160,128]{1,0:T(8,128)S(1)}) custom-call(bf16[256,3584]{1,0:T(8,128)(2,1)S(1)} %get-tuple-element.41.w_ref, s32[30,128]{1,0:T(8,128)S(1)} %get-tuple-element.42.slot_ref, bf16[30,3712]{1,0:T(8,128)(2,1)S(1)} %get-tuple-element.43.refs_0_, ...), custom_call_target="tpu_custom_call" | custom-call | flops 8808038400 | bytes 4411904 | tf_op jit(solution)/shard_map/pallas_call | solution.py:377
  29.3 0.0 collective-permute-done.7.refs_2_
  29.3 4.4 %collective-permute-done.8.refs_3_ = bf16[12,3712]{1,0:T(8,128)(2,1)S(1)} collective-permute-done((bf16[12,3712]{1,0:T(8,128)(2,1)S(1)}, bf16[12,3712]{1,0:T(8,128)(2,1)S(1)}, u32[]{:S(2)}, u32[]{:S(2)}) %collective-permute-start.8) | collective-permute-done | bytes 89120 | tf_op jit(solution)/shard_map/ppermute | solution.py:389
  33.7 0.0 collective-permute-done.9.refs_4_
  33.7 0.0 collective-permute-done.6.refs_1_
  33.7 1.3 %shard_map.98 = (bf16[96,3712]{1,0:T(8,128)(2,1)S(1)}, bf16[256,128]{1,0:T(8,128)(2,1)}) custom-call(f32[160,128]{1,0:T(8,128)S(1)} %get-tuple-element.47.own_ref, bf16[256,3584]{1,0:T(8,128)(2,1)S(1)} %get-tuple-element.41.w_ref, s32[30,128]{1,0:T(8,128)S(1)} %get-tuple-element.42.slot_ref, bf16[24,3712]{1,0:T(8,128)(2,1)S(1)} %collective-permute-done.5.refs_0_, ...), custom_call_target="tpu_custom_call" | custom-call | flops 176160768 | bytes 3334144 | tf_op jit(solution)/shard_map/pallas_call | solution.py:377
  35.0 0.4 shard_map.99
  35.5 0.1 collective-permute-start.10
  35.6 5.3 %all-to-all-start = ((bf16[8,32,128]{2,1,0:T(8,128)(2,1)}), bf16[8,32,128]{2,1,0:T(8,128)(2,1)S(1)}, u32[]{:S(2)}, u32[]{:S(2)}) async-start(bf16[8,32,128]{2,1,0:T(8,128)(2,1)} %bitcast.4), calls=%async_computation | async-start | bytes 131072 | tf_op jit(solution)/shard_map/all_to_all | solution.py:467
  40.9 0.0 copy-start.3
  40.9 0.0 copy-start.4
  40.9 0.0 copy-start.5
  40.9 0.0 copy-start.6
  40.9 0.0 copy-start.7
  40.9 0.0 collective-permute-done.10.arrived_ref
  40.9 2.6 %shard_map.100 = bf16[256,1792]{1,0:T(8,128)(2,1)} custom-call(s32[30,128]{1,0:T(8,128)S(1)} %get-tuple-element.42.slot_ref, bf16[160,3712]{1,0:T(8,128)(2,1)S(1)} %get-tuple-element.53.early_ref, bf16[96,3712]{1,0:T(8,128)(2,1)S(1)} %get-tuple-element.54.late_ref, bf16[256,1792]{1,0:T(8,128)(2,1)} %collective-permute-done.10.arrived_ref), custom_call_target="tpu_custom_call" | custom-call | flops 6606028800 | bytes 3750912 | tf_op jit(solution)/shard_map/pallas_call | solution.py:377
  43.5 4.3 %all-to-all-done.back_ref = bf16[8,32,128]{2,1,0:T(8,128)(2,1)S(1)} async-done(((bf16[8,32,128]{2,1,0:T(8,128)(2,1)}), bf16[8,32,128]{2,1,0:T(8,128)(2,1)S(1)}, u32[]{:S(2)}, u32[]{:S(2)}) %all-to-all-start) | async-done | bytes 65568 | tf_op jit(solution)/shard_map/all_to_all | solution.py:467
  47.8 0.0 copy-done.3
  47.8 0.0 copy-done.4
  47.8 0.0 copy-done.5
  47.8 0.0 copy-done.6
  47.8 0.0 copy-done.7
  47.8 1.0 %shard_map.101 = (bf16[1024,128]{1,0:T(8,128)(2,1)}, bf16[8,128]{1,0:T(8,128)(2,1)}) custom-call(bf16[8,32,128]{2,1,0:T(8,128)(2,1)S(1)} %all-to-all-done.back_ref, f32[72,128]{1,0:T(8,128)S(1)} %copy-done.3, s32[72,128]{1,0:T(8,128)S(1)} %copy-done.4, f32[72,128]{1,0:T(8,128)S(1)} %copy-done.5, f32[72,128]{1,0:T(8,128)S(1)} %copy-done.6, s32[8,128]{1,0:T(8,128)S(1)} %bitcast.10), custom_call_target="tpu_custom_call" | custom-call | flops 18874368 | bytes 481280 | tf_op jit(solution)/shard_map/pallas_call | solution.py:377
Async XLA Ops:
  3.2 14.2 %collective-permute-start = (bf16[48,3712]{1,0:T(8,128)(2,1)}, bf16[48,3712]{1,0:T(8,128)(2,1)S(1)}, u32[]{:S(2)}, u32[]{:S(2)}) collective-permute-start(bf16[48,3712]{1,0:T(8,128)(2,1)} %get-tuple-element.33), channel_id=1, source_target_pairs={{0,2},{2,0},{4,6},{6,4},{8,10},{10,8},{12,14},{14,12},{1,3},{3,1},... | collective-permute-start | bytes 1069064 | tf_op jit(solution)/shard_map/ppermute | solution.py:389
  6.2 11.0 %collective-permute-start.1 = (bf16[24,3712]{1,0:T(8,128)(2,1)}, bf16[24,3712]{1,0:T(8,128)(2,1)S(1)}, u32[]{:S(2)}, u32[]{:S(2)}) collective-permute-start(bf16[24,3712]{1,0:T(8,128)(2,1)} %get-tuple-element.34), channel_id=1, source_target_pairs={{0,8},{2,10},{4,12},{6,14},{8,0},{10,2},{12,4},{14,6},{1,9},{3,11}... | collective-permute-start | bytes 534536 | tf_op jit(solution)/shard_map/ppermute | solution.py:389
  8.8 8.6 %collective-permute-start.2 = (bf16[24,3712]{1,0:T(8,128)(2,1)}, bf16[24,3712]{1,0:T(8,128)(2,1)S(1)}, u32[]{:S(2)}, u32[]{:S(2)}) collective-permute-start(bf16[24,3712]{1,0:T(8,128)(2,1)} %get-tuple-element.34), channel_id=1, source_target_pairs={{0,4},{2,6},{4,0},{6,2},{8,12},{10,14},{12,8},{14,10},{1,5},{3,7},... | collective-permute-start | bytes 534536 | tf_op jit(solution)/shard_map/ppermute | solution.py:389
  10.4 1.5 %copy-start = (bf16[2,128,3584]{2,1,0:T(8,128)(2,1)S(1)}, bf16[2,128,3584]{2,1,0:T(8,128)(2,1)}, u32[]{:S(2)}) copy-start(bf16[2,128,3584]{2,1,0:T(8,128)(2,1)} %param.13) | copy-start | bytes 5505028
  11.9 0.9 %copy-start.1 = (bf16[30,3712]{1,0:T(8,128)(2,1)S(1)}, bf16[30,3712]{1,0:T(8,128)(2,1)}, u32[]{:S(2)}) copy-start(bf16[30,3712]{1,0:T(8,128)(2,1)} %get-tuple-element.35.own_hbm) | copy-start | bytes 668164
  12.8 0.9 %copy-start.2 = (bf16[18,3712]{1,0:T(8,128)(2,1)S(1)}, bf16[18,3712]{1,0:T(8,128)(2,1)}, u32[]{:S(2)}) copy-start(bf16[18,3712]{1,0:T(8,128)(2,1)} %get-tuple-element.36.even_hbm) | copy-start | bytes 400900
  13.7 0.7 %copy-start.8 = (s32[8]{0:T(128)S(1)}, s32[8]{0:T(128)}, u32[]{:S(2)}) copy-start(s32[8]{0:T(128)} %replica_ref.1) | copy-start | bytes 100
  17.4 7.0 %collective-permute-start.3 = (bf16[24,3712]{1,0:T(8,128)(2,1)S(1)}, bf16[24,3712]{1,0:T(8,128)(2,1)S(1)}, u32[]{:S(2)}, u32[]{:S(2)}) collective-permute-start(bf16[24,3712]{1,0:T(8,128)(2,1)S(1)} %collective-permute-done.1.refs_3_), channel_id=1, source_target_pairs={{0,2},{2,0},{4,6},{6,4},{8,10},{10,8},{12,14},{14,12},{1,3},{3,1},... | collective-permute-start | bytes 534536 | tf_op jit(solution)/shard_map/ppermute | solution.py:389
  17.9 10.1 %collective-permute-start.5 = (bf16[24,3712]{1,0:T(8,128)(2,1)S(1)}, bf16[24,3712]{1,0:T(8,128)(2,1)S(1)}, u32[]{:S(2)}, u32[]{:S(2)}) collective-permute-start(bf16[24,3712]{1,0:T(8,128)(2,1)S(1)} %collective-permute-done.1.refs_3_), channel_id=1, source_target_pairs={{0,4},{2,6},{4,0},{6,2},{8,12},{10,14},{12,8},{14,10},{1,5},{3,7},... | collective-permute-start | bytes 534536 | tf_op jit(solution)/shard_map/ppermute | solution.py:389
  19.4 9.1 %collective-permute-start.4 = (bf16[24,3712]{1,0:T(8,128)(2,1)S(1)}, bf16[24,3712]{1,0:T(8,128)(2,1)S(1)}, u32[]{:S(2)}, u32[]{:S(2)}) collective-permute-start(bf16[24,3712]{1,0:T(8,128)(2,1)S(1)} %collective-permute-done.2.refs_2_), channel_id=1, source_target_pairs={{0,2},{2,0},{4,6},{6,4},{8,10},{10,8},{12,14},{14,12},{1,3},{3,1},... | collective-permute-start | bytes 534536 | tf_op jit(solution)/shard_map/ppermute | solution.py:389
  21.0 8.3 %collective-permute-start.7 = (bf16[12,3712]{1,0:T(8,128)(2,1)S(1)}, bf16[12,3712]{1,0:T(8,128)(2,1)S(1)}, u32[]{:S(2)}, u32[]{:S(2)}) collective-permute-start(bf16[12,3712]{1,0:T(8,128)(2,1)S(1)} %get-tuple-element.49), channel_id=1, source_target_pairs={{0,4},{2,6},{4,0},{6,2},{8,12},{10,14},{12,8},{14,10},{1,5},{3,7},... | collective-permute-start | bytes 267272 | tf_op jit(solution)/shard_map/ppermute | solution.py:389
  21.6 12.0 %collective-permute-start.8 = (bf16[12,3712]{1,0:T(8,128)(2,1)S(1)}, bf16[12,3712]{1,0:T(8,128)(2,1)S(1)}, u32[]{:S(2)}, u32[]{:S(2)}) collective-permute-start(bf16[12,3712]{1,0:T(8,128)(2,1)S(1)} %get-tuple-element.50), channel_id=1, source_target_pairs={{0,8},{2,10},{4,12},{6,14},{8,0},{10,2},{12,4},{14,6},{1,9},{3,11}... | collective-permute-start | bytes 267272 | tf_op jit(solution)/shard_map/ppermute | solution.py:389
  24.4 9.3 %collective-permute-start.9 = (bf16[12,3712]{1,0:T(8,128)(2,1)S(1)}, bf16[12,3712]{1,0:T(8,128)(2,1)S(1)}, u32[]{:S(2)}, u32[]{:S(2)}) collective-permute-start(bf16[12,3712]{1,0:T(8,128)(2,1)S(1)} %get-tuple-element.51), channel_id=1, source_target_pairs={{0,12},{2,14},{4,8},{6,10},{8,4},{10,6},{12,0},{14,2},{1,13},{3,15... | collective-permute-start | bytes 267272 | tf_op jit(solution)/shard_map/ppermute | solution.py:389
  28.0 5.7 %collective-permute-start.6 = (bf16[24,3712]{1,0:T(8,128)(2,1)S(1)}, bf16[24,3712]{1,0:T(8,128)(2,1)S(1)}, u32[]{:S(2)}, u32[]{:S(2)}) collective-permute-start(bf16[24,3712]{1,0:T(8,128)(2,1)S(1)} %collective-permute-done.5.refs_0_), channel_id=1, source_target_pairs={{0,2},{2,0},{4,6},{6,4},{8,10},{10,8},{12,14},{14,12},{1,3},{3,1},... | collective-permute-start | bytes 534536 | tf_op jit(solution)/shard_map/ppermute | solution.py:389
  35.5 5.4 %collective-permute-start.10 = (bf16[256,1792]{1,0:T(8,128)(2,1)S(1)}, bf16[256,1792]{1,0:T(8,128)(2,1)}, u32[]{:S(2)}, u32[]{:S(2)}) collective-permute-start(bf16[256,1792]{1,0:T(8,128)(2,1)S(1)} %shard_map.99), channel_id=1, source_target_pairs={{0,1},{1,0},{2,3},{3,2},{4,5},{5,4},{6,7},{7,6},{8,9},{9,8},{10,11... | collective-permute-start | bytes 2752520 | tf_op jit(solution)/shard_map/ppermute | solution.py:476
  35.6 12.2 %all-to-all-start = ((bf16[8,32,128]{2,1,0:T(8,128)(2,1)}), bf16[8,32,128]{2,1,0:T(8,128)(2,1)S(1)}, u32[]{:S(2)}, u32[]{:S(2)}) async-start(bf16[8,32,128]{2,1,0:T(8,128)(2,1)} %bitcast.4), calls=%async_computation | async-start | bytes 131072 | tf_op jit(solution)/shard_map/all_to_all | solution.py:467
  40.9 6.9 %copy-start.3 = (f32[72,128]{1,0:T(8,128)S(1)}, f32[72,128]{1,0:T(8,128)}, u32[]{:S(2)}) copy-start(f32[72,128]{1,0:T(8,128)} %get-tuple-element.56.pick_ref) | copy-start | bytes 110596
  40.9 6.9 %copy-start.4 = (s32[72,128]{1,0:T(8,128)S(1)}, s32[72,128]{1,0:T(8,128)}, u32[]{:S(2)}) copy-start(s32[72,128]{1,0:T(8,128)} %get-tuple-element.57.expert_ref) | copy-start | bytes 110596
  40.9 6.9 %copy-start.5 = (f32[72,128]{1,0:T(8,128)S(1)}, f32[72,128]{1,0:T(8,128)}, u32[]{:S(2)}) copy-start(f32[72,128]{1,0:T(8,128)} %get-tuple-element.58.hs_ref) | copy-start | bytes 110596
  40.9 6.9 %copy-start.6 = (f32[72,128]{1,0:T(8,128)S(1)}, f32[72,128]{1,0:T(8,128)}, u32[]{:S(2)}) copy-start(f32[72,128]{1,0:T(8,128)} %get-tuple-element.59.ps_ref) | copy-start | bytes 110596
  40.9 6.9 %copy-start.7 = (s32[128,8]{0,1:T(8,128)S(1)}, s32[128,8]{0,1:T(8,128)}, u32[]{:S(2)}) copy-start(s32[128,8]{0,1:T(8,128)} %param.10) | copy-start | bytes 12292

commit v12 on v11

--- a/solution.py
+++ b/solution.py
@@ -420,8 +420,8 @@
         limit=60,
     )
     beside = swap(to_beside, 1, dev_count)
+    near = swap(copy_rows, 2, dev_count)
     far = swap(copy_rows, 4, dev_count)
-    near = swap(copy_rows, 2, dev_count)
     flat_w = weights.reshape(local_count * width, d_model)
     own_rows, even_rows, w_held, slot = call(
         functools.partial(hold_kernel, *sizes),
@@ -429,8 +429,8 @@
         [(smem, replica_of)] + [(hbm, a) for a in (flat_w, own_rows, even_rows)],
         [pltpu.SemaphoreType.DMA((3,))],
     )
-    beside, far, near, own_rows, even_rows, w_held, slot = lax.optimization_barrier(
-        (beside, far, near, own_rows, even_rows, w_held, slot))
+    near, far, beside, own_rows, even_rows, w_held, slot = lax.optimization_barrier(
+        (near, far, beside, own_rows, even_rows, w_held, slot))
     far_near = swap(far, 2, dev_count)
     lines = call(
         functools.partial(turn_kernel, *sizes),
@@ -450,9 +450,9 @@
         flops=2 * height * d_model * local_count * width * 30,
     )
     far_across = swap(far_near, 1, dev_count)
-    arrays = [far_near, far_across, *lines]
+    arrays = [far_near, far_across, *lines[::-1]]
     pieces = {(6, COPIES): (0, 0), (7, COPIES): (1, 0)}
-    for n, m in enumerate(even):
+    for n, m in enumerate(even[::-1]):
         pieces[m, HOME], pieces[m + 1, HOME] = ((2 + n, k * per_home) for k in range(2))
     orders.append(list(pieces))
     height = padded(sum(per_home if kind == HOME else copies for _, kind in pieces))

time: 49.1 us -> 49.5 us (level)
  waiting for transfers between devices: 11.4 us -> 13.1 us
  starting transfers between devices: 22.6 us -> 21.1 us
    ppermute x10, waiting for transfers between devices: 7.11 us -> 8.87 us  [swap(): return lax.ppermute(x, 'expert', [(i, i ^ bits) for i in range(count)])]
    all_to_all x1, starting transfers between devices: 5.3 us -> 4.41 us  [gather_body(): lax.all_to_all(back, 'expert', split_axis=0, concat_axis=0, tiled=True)]
    ppermute x10, starting transfers between devices: 17.2 us -> 16.7 us  [swap(): return lax.ppermute(x, 'expert', [(i, i ^ bits) for i in range(count)])]
  transfers between devices with their start and end apart: 12 -> 12, of which waited for: 5 -> 6; matrix products, arithmetic and copies ran while one was open for 0% -> 0% of each run, Pallas kernels for 10% -> 10%
where the time goes in v12:
time: 49.5 us; the launch traced here: 49.1 us
  starting transfers between devices  21.1 us (43%)
  waiting for transfers between devices  13.1 us (26%)
  Pallas kernels  10.1 us (20%)
  local copies, waits for them, and re-layouts  4.04 us (8%)
  between operations  0.76 us (2%)
    ppermute x10, starting transfers between devices, swap(): return lax.ppermute(x, 'expert', [(i, i ^ bits) for i in range(count)])  16.7 us
    pallas_call x8, Pallas kernels, call(): pl.pallas_call(kernel, out_shape=out_shape, in_specs=[pl.BlockSpec(memory...  10.1 us
    ppermute x10, waiting for transfers between devices, swap(): return lax.ppermute(x, 'expert', [(i, i ^ bits) for i in range(count)])  8.87 us
    all_to_all x1, starting transfers between devices, gather_body(): lax.all_to_all(back, 'expert', split_axis=0, concat_axis=0, tiled=True)  4.41 us
    all_to_all x1, waiting for transfers between devices, gather_body(): lax.all_to_all(back, 'expert', split_axis=0, concat_axis=0, tiled=True)  4.26 us
    unnamed x18, local copies, waits for them, and re-layouts  4.04 us
  transfers between devices with their start and end apart: 12, of which 6 were waited for; matrix products, arithmetic and copies ran while one was open for 0% of the time, Pallas kernels for 10%

profile of v12, /device:TPU:0, one launch (start us, length us, event | category | flops | bytes accessed | tf_op | source)
XLA Modules:
  0.0 49.1 jit_solution(17604666802328736657)
XLA Ops:
  0.6 2.6 %shard_map.94 = (f32[72,128]{1,0:T(8,128)}, s32[72,128]{1,0:T(8,128)}, f32[72,128]{1,0:T(8,128)}, f32[72,128]{1,0:T(8,128)}, bf16[48,3712]{1,0:T(8,128)(2,1)}, /...) custom-call(s32[8]{0:T(128)} %replica_ref.1, s32[1,8]{1,0:T(1,128)} %refs_1_.1, ...), custom_call_target="tpu_custom_call" | custom-call | flops 66060288 | bytes 2224192 | tf_op jit(solution)/shard_map/pallas_call | solution.py:377
  3.2 3.0 %collective-permute-start.2 = (bf16[48,3712]{1,0:T(8,128)(2,1)}, bf16[48,3712]{1,0:T(8,128)(2,1)S(1)}, u32[]{:S(2)}, u32[]{:S(2)}) collective-permute-start(bf16[48,3712]{1,0:T(8,128)(2,1)} %get-tuple-element.34), channel_id=1, source_target_pairs={{0,2},{2,0},{4,6},{6,4},{8,10},{10,8},{12,14},{14,12},{1,3},{3,1},... | collective-permute-start | bytes 1069064 | tf_op jit(solution)/shard_map/ppermute | solution.py:389
  6.2 1.6 %collective-permute-start = (bf16[24,3712]{1,0:T(8,128)(2,1)}, bf16[24,3712]{1,0:T(8,128)(2,1)S(1)}, u32[]{:S(2)}, u32[]{:S(2)}) collective-permute-start(bf16[24,3712]{1,0:T(8,128)(2,1)} %get-tuple-element.33), channel_id=1, source_target_pairs={{0,4},{2,6},{4,0},{6,2},{8,12},{10,14},{12,8},{14,10},{1,5},{3,7},... | collective-permute-start | bytes 534536 | tf_op jit(solution)/shard_map/ppermute | solution.py:389
  7.8 2.6 %collective-permute-start.1 = (bf16[24,3712]{1,0:T(8,128)(2,1)}, bf16[24,3712]{1,0:T(8,128)(2,1)S(1)}, u32[]{:S(2)}, u32[]{:S(2)}) collective-permute-start(bf16[24,3712]{1,0:T(8,128)(2,1)} %get-tuple-element.33), channel_id=1, source_target_pairs={{0,8},{2,10},{4,12},{6,14},{8,0},{10,2},{12,4},{14,6},{1,9},{3,11}... | collective-permute-start | bytes 534536 | tf_op jit(solution)/shard_map/ppermute | solution.py:389
  10.4 0.0 copy-start
  10.4 1.5 %copy-done = bf16[2,128,3584]{2,1,0:T(8,128)(2,1)S(1)} copy-done((bf16[2,128,3584]{2,1,0:T(8,128)(2,1)S(1)}, bf16[2,128,3584]{2,1,0:T(8,128)(2,1)}, u32[]{:S(2)}) %copy-start) | copy-done | bytes 1835032
  11.9 0.0 copy-start.1
  11.9 0.9 %copy-done.1 = bf16[30,3712]{1,0:T(8,128)(2,1)S(1)} copy-done((bf16[30,3712]{1,0:T(8,128)(2,1)S(1)}, bf16[30,3712]{1,0:T(8,128)(2,1)}, u32[]{:S(2)}) %copy-start.1) | copy-done | bytes 222744
  12.8 0.0 copy-start.2
  12.8 0.9 %copy-done.2 = bf16[18,3712]{1,0:T(8,128)(2,1)S(1)} copy-done((bf16[18,3712]{1,0:T(8,128)(2,1)S(1)}, bf16[18,3712]{1,0:T(8,128)(2,1)}, u32[]{:S(2)}) %copy-start.2) | copy-done | bytes 133656
  13.7 0.0 copy-start.8
  13.7 0.7 %copy-done.8 = s32[8]{0:T(128)S(1)} copy-done((s32[8]{0:T(128)S(1)}, s32[8]{0:T(128)}, u32[]{:S(2)}) %copy-start.8) | copy-done | bytes 56
  14.4 1.2 %shard_map.95 = (bf16[30,3712]{1,0:T(8,128)(2,1)S(1)}, bf16[18,3712]{1,0:T(8,128)(2,1)S(1)}, bf16[256,3584]{1,0:T(8,128)(2,1)S(1)}, s32[30,128]{1,0:T(8,128)S(1)}) custom-call(s32[8]{0:T(128)S(1)} %copy-done.8, bf16[256,3584]{1,0:T(8,128)(2,1)S(1)} %bitcast.8, bf16[30,3712]{1,0:T(8,128)(2,1)S(1)} %copy-done.1, bf16[18,3712]{1,0:T(8,128)(2,1)S(1)} %copy-done.2), custom_call_target="tpu_custom_call" | custom-call | bytes 4398112 | tf_op jit(solution)/shard_map/pallas_call | solution.py:377
  15.6 0.4 collective-permute-done.refs_2_
  16.1 2.4 %collective-permute-done.1.refs_3_ = bf16[24,3712]{1,0:T(8,128)(2,1)S(1)} collective-permute-done((bf16[24,3712]{1,0:T(8,128)(2,1)}, bf16[24,3712]{1,0:T(8,128)(2,1)S(1)}, u32[]{:S(2)}, u32[]{:S(2)}) %collective-permute-start.1) | collective-permute-done | bytes 178208 | tf_op jit(solution)/shard_map/ppermute | solution.py:389
  18.5 0.0 collective-permute-done.2.refs_1_.beside_ref
  18.5 0.5 %collective-permute-start.3 = (bf16[24,3712]{1,0:T(8,128)(2,1)S(1)}, bf16[24,3712]{1,0:T(8,128)(2,1)S(1)}, u32[]{:S(2)}, u32[]{:S(2)}) collective-permute-start(bf16[24,3712]{1,0:T(8,128)(2,1)S(1)} %collective-permute-done.1.refs_3_), channel_id=1, source_target_pairs={{0,2},{2,0},{4,6},{6,4},{8,10},{10,8},{12,14},{14,12},{1,3},{3,1},... | collective-permute-start | bytes 534536 | tf_op jit(solution)/shard_map/ppermute | solution.py:389
  19.0 0.4 collective-permute-start.5
  19.4 1.5 %collective-permute-start.4 = (bf16[24,3712]{1,0:T(8,128)(2,1)S(1)}, bf16[24,3712]{1,0:T(8,128)(2,1)S(1)}, u32[]{:S(2)}, u32[]{:S(2)}) collective-permute-start(bf16[24,3712]{1,0:T(8,128)(2,1)S(1)} %collective-permute-done.refs_2_), channel_id=1, source_target_pairs={{0,2},{2,0},{4,6},{6,4},{8,10},{10,8},{12,14},{14,12},{1,3},{3,1},... | collective-permute-start | bytes 534536 | tf_op jit(solution)/shard_map/ppermute | solution.py:389
  20.9 0.1 shard_map.97
  21.0 2.1 %collective-permute-start.7 = (bf16[12,3712]{1,0:T(8,128)(2,1)S(1)}, bf16[12,3712]{1,0:T(8,128)(2,1)S(1)}, u32[]{:S(2)}, u32[]{:S(2)}) collective-permute-start(bf16[12,3712]{1,0:T(8,128)(2,1)S(1)} %get-tuple-element.49), channel_id=1, source_target_pairs={{0,12},{2,14},{4,8},{6,10},{8,4},{10,6},{12,0},{14,2},{1,13},{3,15... | collective-permute-start | bytes 267272 | tf_op jit(solution)/shard_map/ppermute | solution.py:389
  23.1 1.0 %collective-permute-start.8 = (bf16[12,3712]{1,0:T(8,128)(2,1)S(1)}, bf16[12,3712]{1,0:T(8,128)(2,1)S(1)}, u32[]{:S(2)}, u32[]{:S(2)}) collective-permute-start(bf16[12,3712]{1,0:T(8,128)(2,1)S(1)} %get-tuple-element.50), channel_id=1, source_target_pairs={{0,8},{2,10},{4,12},{6,14},{8,0},{10,2},{12,4},{14,6},{1,9},{3,11}... | collective-permute-start | bytes 267272 | tf_op jit(solution)/shard_map/ppermute | solution.py:389
  24.1 0.0 collective-permute-done.3.refs_4_
  24.2 2.0 %collective-permute-start.9 = (bf16[12,3712]{1,0:T(8,128)(2,1)S(1)}, bf16[12,3712]{1,0:T(8,128)(2,1)S(1)}, u32[]{:S(2)}, u32[]{:S(2)}) collective-permute-start(bf16[12,3712]{1,0:T(8,128)(2,1)S(1)} %get-tuple-element.51), channel_id=1, source_target_pairs={{0,4},{2,6},{4,0},{6,2},{8,12},{10,14},{12,8},{14,10},{1,5},{3,7},... | collective-permute-start | bytes 267272 | tf_op jit(solution)/shard_map/ppermute | solution.py:389
  26.2 3.2 %collective-permute-done.5.refs_0_ = bf16[24,3712]{1,0:T(8,128)(2,1)S(1)} collective-permute-done((bf16[24,3712]{1,0:T(8,128)(2,1)S(1)}, bf16[24,3712]{1,0:T(8,128)(2,1)S(1)}, u32[]{:S(2)}, u32[]{:S(2)}) %collective-permute-start.5) | collective-permute-done | bytes 178208 | tf_op jit(solution)/shard_map/ppermute | solution.py:389
  29.4 1.9 %collective-permute-start.6 = (bf16[24,3712]{1,0:T(8,128)(2,1)S(1)}, bf16[24,3712]{1,0:T(8,128)(2,1)S(1)}, u32[]{:S(2)}, u32[]{:S(2)}) collective-permute-start(bf16[24,3712]{1,0:T(8,128)(2,1)S(1)} %collective-permute-done.5.refs_0_), channel_id=1, source_target_pairs={{0,2},{2,0},{4,6},{6,4},{8,10},{10,8},{12,14},{14,12},{1,3},{3,1},... | collective-permute-start | bytes 534536 | tf_op jit(solution)/shard_map/ppermute | solution.py:389
  31.3 0.0 collective-permute-done.4.refs_5_
  31.3 0.8 %shard_map.96 = (bf16[160,3712]{1,0:T(8,128)(2,1)S(1)}, f32[160,128]{1,0:T(8,128)S(1)}) custom-call(bf16[256,3584]{1,0:T(8,128)(2,1)S(1)} %get-tuple-element.41.w_ref, s32[30,128]{1,0:T(8,128)S(1)} %get-tuple-element.42.slot_ref, bf16[30,3712]{1,0:T(8,128)(2,1)S(1)} %get-tuple-element.43.refs_0_, ...), custom_call_target="tpu_custom_call" | custom-call | flops 8808038400 | bytes 4411904 | tf_op jit(solution)/shard_map/pallas_call | solution.py:377
  32.1 0.0 collective-permute-done.7.refs_2_
  32.1 0.1 collective-permute-done.8.refs_3_
  32.2 0.0 collective-permute-done.9.refs_4_
  32.2 2.7 %collective-permute-done.6.refs_1_ = bf16[24,3712]{1,0:T(8,128)(2,1)S(1)} collective-permute-done((bf16[24,3712]{1,0:T(8,128)(2,1)S(1)}, bf16[24,3712]{1,0:T(8,128)(2,1)S(1)}, u32[]{:S(2)}, u32[]{:S(2)}) %collective-permute-start.6) | collective-permute-done | bytes 178208 | tf_op jit(solution)/shard_map/ppermute | solution.py:389
  34.9 1.3 %shard_map.98 = (bf16[96,3712]{1,0:T(8,128)(2,1)S(1)}, bf16[256,128]{1,0:T(8,128)(2,1)}) custom-call(f32[160,128]{1,0:T(8,128)S(1)} %get-tuple-element.47.own_ref, bf16[256,3584]{1,0:T(8,128)(2,1)S(1)} %get-tuple-element.41.w_ref, s32[30,128]{1,0:T(8,128)S(1)} %get-tuple-element.42.slot_ref, bf16[24,3712]{1,0:T(8,128)(2,1)S(1)} %collective-permute-done.5.refs_0_, ...), custom_call_target="tpu_custom_call" | custom-call | flops 176160768 | bytes 3334144 | tf_op jit(solution)/shard_map/pallas_call | solution.py:377
  36.2 0.4 shard_map.99
  36.7 0.1 collective-permute-start.10
  36.8 4.4 %all-to-all-start = ((bf16[8,32,128]{2,1,0:T(8,128)(2,1)}), bf16[8,32,128]{2,1,0:T(8,128)(2,1)S(1)}, u32[]{:S(2)}, u32[]{:S(2)}) async-start(bf16[8,32,128]{2,1,0:T(8,128)(2,1)} %bitcast.4), calls=%async_computation | async-start | bytes 131072 | tf_op jit(solution)/shard_map/all_to_all | solution.py:467
  41.2 0.0 copy-start.3
  41.2 0.0 copy-start.4
  41.2 0.0 copy-start.5
  41.2 0.0 copy-start.6
  41.2 0.0 copy-start.7
  41.2 0.0 collective-permute-done.10.arrived_ref
  41.2 2.6 %shard_map.100 = bf16[256,1792]{1,0:T(8,128)(2,1)} custom-call(s32[30,128]{1,0:T(8,128)S(1)} %get-tuple-element.42.slot_ref, bf16[160,3712]{1,0:T(8,128)(2,1)S(1)} %get-tuple-element.53.early_ref, bf16[96,3712]{1,0:T(8,128)(2,1)S(1)} %get-tuple-element.54.late_ref, bf16[256,1792]{1,0:T(8,128)(2,1)} %collective-permute-done.10.arrived_ref), custom_call_target="tpu_custom_call" | custom-call | flops 6606028800 | bytes 3750912 | tf_op jit(solution)/shard_map/pallas_call | solution.py:377
  43.8 4.3 %all-to-all-done.back_ref = bf16[8,32,128]{2,1,0:T(8,128)(2,1)S(1)} async-done(((bf16[8,32,128]{2,1,0:T(8,128)(2,1)}), bf16[8,32,128]{2,1,0:T(8,128)(2,1)S(1)}, u32[]{:S(2)}, u32[]{:S(2)}) %all-to-all-start) | async-done | bytes 65568 | tf_op jit(solution)/shard_map/all_to_all | solution.py:467
  48.1 0.0 copy-done.3
  48.1 0.0 copy-done.4
  48.1 0.0 copy-done.5
  48.1 0.0 copy-done.6
  48.1 0.0 copy-done.7
  48.1 1.0 %shard_map.101 = (bf16[1024,128]{1,0:T(8,128)(2,1)}, bf16[8,128]{1,0:T(8,128)(2,1)}) custom-call(bf16[8,32,128]{2,1,0:T(8,128)(2,1)S(1)} %all-to-all-done.back_ref, f32[72,128]{1,0:T(8,128)S(1)} %copy-done.3, s32[72,128]{1,0:T(8,128)S(1)} %copy-done.4, f32[72,128]{1,0:T(8,128)S(1)} %copy-done.5, f32[72,128]{1,0:T(8,128)S(1)} %copy-done.6, s32[8,128]{1,0:T(8,128)S(1)} %bitcast.10), custom_call_target="tpu_custom_call" | custom-call | flops 18874368 | bytes 481280 | tf_op jit(solution)/shard_map/pallas_call | solution.py:377
Async XLA Ops:
  3.2 15.3 %collective-permute-start.2 = (bf16[48,3712]{1,0:T(8,128)(2,1)}, bf16[48,3712]{1,0:T(8,128)(2,1)S(1)}, u32[]{:S(2)}, u32[]{:S(2)}) collective-permute-start(bf16[48,3712]{1,0:T(8,128)(2,1)} %get-tuple-element.34), channel_id=1, source_target_pairs={{0,2},{2,0},{4,6},{6,4},{8,10},{10,8},{12,14},{14,12},{1,3},{3,1},... | collective-permute-start | bytes 1069064 | tf_op jit(solution)/shard_map/ppermute | solution.py:389
  6.2 9.9 %collective-permute-start = (bf16[24,3712]{1,0:T(8,128)(2,1)}, bf16[24,3712]{1,0:T(8,128)(2,1)S(1)}, u32[]{:S(2)}, u32[]{:S(2)}) collective-permute-start(bf16[24,3712]{1,0:T(8,128)(2,1)} %get-tuple-element.33), channel_id=1, source_target_pairs={{0,4},{2,6},{4,0},{6,2},{8,12},{10,14},{12,8},{14,10},{1,5},{3,7},... | collective-permute-start | bytes 534536 | tf_op jit(solution)/shard_map/ppermute | solution.py:389
  7.8 10.7 %collective-permute-start.1 = (bf16[24,3712]{1,0:T(8,128)(2,1)}, bf16[24,3712]{1,0:T(8,128)(2,1)S(1)}, u32[]{:S(2)}, u32[]{:S(2)}) collective-permute-start(bf16[24,3712]{1,0:T(8,128)(2,1)} %get-tuple-element.33), channel_id=1, source_target_pairs={{0,8},{2,10},{4,12},{6,14},{8,0},{10,2},{12,4},{14,6},{1,9},{3,11}... | collective-permute-start | bytes 534536 | tf_op jit(solution)/shard_map/ppermute | solution.py:389
  10.4 1.5 %copy-start = (bf16[2,128,3584]{2,1,0:T(8,128)(2,1)S(1)}, bf16[2,128,3584]{2,1,0:T(8,128)(2,1)}, u32[]{:S(2)}) copy-start(bf16[2,128,3584]{2,1,0:T(8,128)(2,1)} %param.13) | copy-start | bytes 5505028
  11.9 0.9 %copy-start.1 = (bf16[30,3712]{1,0:T(8,128)(2,1)S(1)}, bf16[30,3712]{1,0:T(8,128)(2,1)}, u32[]{:S(2)}) copy-start(bf16[30,3712]{1,0:T(8,128)(2,1)} %get-tuple-element.35.own_hbm) | copy-start | bytes 668164
  12.8 0.9 %copy-start.2 = (bf16[18,3712]{1,0:T(8,128)(2,1)S(1)}, bf16[18,3712]{1,0:T(8,128)(2,1)}, u32[]{:S(2)}) copy-start(bf16[18,3712]{1,0:T(8,128)(2,1)} %get-tuple-element.36.even_hbm) | copy-start | bytes 400900
  13.7 0.7 %copy-start.8 = (s32[8]{0:T(128)S(1)}, s32[8]{0:T(128)}, u32[]{:S(2)}) copy-start(s32[8]{0:T(128)} %replica_ref.1) | copy-start | bytes 100
  18.5 5.7 %collective-permute-start.3 = (bf16[24,3712]{1,0:T(8,128)(2,1)S(1)}, bf16[24,3712]{1,0:T(8,128)(2,1)S(1)}, u32[]{:S(2)}, u32[]{:S(2)}) collective-permute-start(bf16[24,3712]{1,0:T(8,128)(2,1)S(1)} %collective-permute-done.1.refs_3_), channel_id=1, source_target_pairs={{0,2},{2,0},{4,6},{6,4},{8,10},{10,8},{12,14},{14,12},{1,3},{3,1},... | collective-permute-start | bytes 534536 | tf_op jit(solution)/shard_map/ppermute | solution.py:389
  19.0 10.4 %collective-permute-start.5 = (bf16[24,3712]{1,0:T(8,128)(2,1)S(1)}, bf16[24,3712]{1,0:T(8,128)(2,1)S(1)}, u32[]{:S(2)}, u32[]{:S(2)}) collective-permute-start(bf16[24,3712]{1,0:T(8,128)(2,1)S(1)} %collective-permute-done.1.refs_3_), channel_id=1, source_target_pairs={{0,4},{2,6},{4,0},{6,2},{8,12},{10,14},{12,8},{14,10},{1,5},{3,7},... | collective-permute-start | bytes 534536 | tf_op jit(solution)/shard_map/ppermute | solution.py:389
  19.4 11.9 %collective-permute-start.4 = (bf16[24,3712]{1,0:T(8,128)(2,1)S(1)}, bf16[24,3712]{1,0:T(8,128)(2,1)S(1)}, u32[]{:S(2)}, u32[]{:S(2)}) collective-permute-start(bf16[24,3712]{1,0:T(8,128)(2,1)S(1)} %collective-permute-done.refs_2_), channel_id=1, source_target_pairs={{0,2},{2,0},{4,6},{6,4},{8,10},{10,8},{12,14},{14,12},{1,3},{3,1},... | collective-permute-start | bytes 534536 | tf_op jit(solution)/shard_map/ppermute | solution.py:389
  21.0 11.1 %collective-permute-start.7 = (bf16[12,3712]{1,0:T(8,128)(2,1)S(1)}, bf16[12,3712]{1,0:T(8,128)(2,1)S(1)}, u32[]{:S(2)}, u32[]{:S(2)}) collective-permute-start(bf16[12,3712]{1,0:T(8,128)(2,1)S(1)} %get-tuple-element.49), channel_id=1, source_target_pairs={{0,12},{2,14},{4,8},{6,10},{8,4},{10,6},{12,0},{14,2},{1,13},{3,15... | collective-permute-start | bytes 267272 | tf_op jit(solution)/shard_map/ppermute | solution.py:389
  23.1 9.1 %collective-permute-start.8 = (bf16[12,3712]{1,0:T(8,128)(2,1)S(1)}, bf16[12,3712]{1,0:T(8,128)(2,1)S(1)}, u32[]{:S(2)}, u32[]{:S(2)}) collective-permute-start(bf16[12,3712]{1,0:T(8,128)(2,1)S(1)} %get-tuple-element.50), channel_id=1, source_target_pairs={{0,8},{2,10},{4,12},{6,14},{8,0},{10,2},{12,4},{14,6},{1,9},{3,11}... | collective-permute-start | bytes 267272 | tf_op jit(solution)/shard_map/ppermute | solution.py:389
  24.2 8.1 %collective-permute-start.9 = (bf16[12,3712]{1,0:T(8,128)(2,1)S(1)}, bf16[12,3712]{1,0:T(8,128)(2,1)S(1)}, u32[]{:S(2)}, u32[]{:S(2)}) collective-permute-start(bf16[12,3712]{1,0:T(8,128)(2,1)S(1)} %get-tuple-element.51), channel_id=1, source_target_pairs={{0,4},{2,6},{4,0},{6,2},{8,12},{10,14},{12,8},{14,10},{1,5},{3,7},... | collective-permute-start | bytes 267272 | tf_op jit(solution)/shard_map/ppermute | solution.py:389
  29.4 5.5 %collective-permute-start.6 = (bf16[24,3712]{1,0:T(8,128)(2,1)S(1)}, bf16[24,3712]{1,0:T(8,128)(2,1)S(1)}, u32[]{:S(2)}, u32[]{:S(2)}) collective-permute-start(bf16[24,3712]{1,0:T(8,128)(2,1)S(1)} %collective-permute-done.5.refs_0_), channel_id=1, source_target_pairs={{0,2},{2,0},{4,6},{6,4},{8,10},{10,8},{12,14},{14,12},{1,3},{3,1},... | collective-permute-start | bytes 534536 | tf_op jit(solution)/shard_map/ppermute | solution.py:389
  36.7 4.5 %collective-permute-start.10 = (bf16[256,1792]{1,0:T(8,128)(2,1)S(1)}, bf16[256,1792]{1,0:T(8,128)(2,1)}, u32[]{:S(2)}, u32[]{:S(2)}) collective-permute-start(bf16[256,1792]{1,0:T(8,128)(2,1)S(1)} %shard_map.99), channel_id=1, source_target_pairs={{0,1},{1,0},{2,3},{3,2},{4,5},{5,4},{6,7},{7,6},{8,9},{9,8},{10,11... | collective-permute-start | bytes 2752520 | tf_op jit(solution)/shard_map/ppermute | solution.py:476
  36.8 11.3 %all-to-all-start = ((bf16[8,32,128]{2,1,0:T(8,128)(2,1)}), bf16[8,32,128]{2,1,0:T(8,128)(2,1)S(1)}, u32[]{:S(2)}, u32[]{:S(2)}) async-start(bf16[8,32,128]{2,1,0:T(8,128)(2,1)} %bitcast.4), calls=%async_computation | async-start | bytes 131072 | tf_op jit(solution)/shard_map/all_to_all | solution.py:467
  41.2 6.9 %copy-start.3 = (f32[72,128]{1,0:T(8,128)S(1)}, f32[72,128]{1,0:T(8,128)}, u32[]{:S(2)}) copy-start(f32[72,128]{1,0:T(8,128)} %get-tuple-element.56.pick_ref) | copy-start | bytes 110596
  41.2 6.9 %copy-start.4 = (s32[72,128]{1,0:T(8,128)S(1)}, s32[72,128]{1,0:T(8,128)}, u32[]{:S(2)}) copy-start(s32[72,128]{1,0:T(8,128)} %get-tuple-element.57.expert_ref) | copy-start | bytes 110596
  41.2 6.9 %copy-start.5 = (f32[72,128]{1,0:T(8,128)S(1)}, f32[72,128]{1,0:T(8,128)}, u32[]{:S(2)}) copy-start(f32[72,128]{1,0:T(8,128)} %get-tuple-element.58.hs_ref) | copy-start | bytes 110596
  41.2 6.9 %copy-start.6 = (f32[72,128]{1,0:T(8,128)S(1)}, f32[72,128]{1,0:T(8,128)}, u32[]{:S(2)}) copy-start(f32[72,128]{1,0:T(8,128)} %get-tuple-element.59.ps_ref) | copy-start | bytes 110596
  41.2 6.9 %copy-start.7 = (s32[128,8]{0,1:T(8,128)S(1)}, s32[128,8]{0,1:T(8,128)}, u32[]{:S(2)}) copy-start(s32[128,8]{0,1:T(8,128)} %param.10) | copy-start | bytes 12292

commit v13 on v12

--- a/solution.py
+++ b/solution.py
@@ -243,13 +243,31 @@
     return jnp.concatenate(values, axis=0)
 
 
+def fold_width(columns):
+    return -(-columns // 256) * 128
+
+
+def folded(rows):
+    count, columns = rows.shape
+    left = fold_width(columns)
+    right = [rows[:, left:], jnp.zeros((count, 2 * left - columns), rows.dtype)]
+    return jnp.concatenate([rows[:, :left], jnp.concatenate(right, axis=1)], axis=0)
+
+
+def unfolded(rows, columns):
+    count, left = rows.shape
+    if left == columns:
+        return rows
+    return jnp.concatenate([rows[:count // 2], rows[count // 2:, :columns - left]], axis=1)
+
+
 def slots_of(order, slot_ref, per_home, height):
     kinds = {HOME: slot_ref[:per_home], COPIES: slot_ref[per_home:]}
     return stack(order, {key: kinds[key[1]] for key in order}, height)
 
 
 def fill_rows(order, pieces, per_home, per_copy, piece_refs, rows_ref):
-    values = [r[...].astype(F32) for r in piece_refs]
+    values = [unfolded(r[...].astype(F32), rows_ref.shape[1]) for r in piece_refs]
     blocks = {}
     for key in order:
         n, start = pieces[key]
@@ -293,7 +311,7 @@
     even = even_ref[...].astype(F32)
     for n, line_ref in enumerate(line_refs):
         span = slice(n * per_home, (n + 1) * per_home)
-        line_ref[...] = jnp.concatenate([even[span], beside[span]], axis=0).astype(BF16)
+        line_ref[...] = folded(jnp.concatenate([even[span], beside[span]], axis=0)).astype(BF16)
 
 
 def early_kernel(local_count, dev_count, order, pieces, w_ref, slot_ref, *refs):
@@ -434,7 +452,7 @@
     far_near = swap(far, 2, dev_count)
     lines = call(
         functools.partial(turn_kernel, *sizes),
-        [shape((n, d_model + width), BF16) for n in [2 * per_home] * len(even)],
+        [shape((4 * per_home, fold_width(d_model + width)), BF16)] * len(even),
         [(vmem, a) for a in (beside, even_rows)],
     )
     far_beside, near_beside = swap(far, 1, dev_count), swap(near, 1, dev_count)

time: 49.5 us -> 48.2 us (0.974)
  waiting for transfers between devices: 13.1 us -> 12.2 us
    ppermute x10, waiting for transfers between devices: 8.87 us -> 7.89 us  [swap(): return lax.ppermute(x, 'expert', [(i, i ^ bits) for i in range(count)])]
  transfers between devices with their start and end apart: 12 -> 12, of which waited for: 6 -> 5; matrix products, arithmetic and copies ran while one was open for 0% -> 0% of each run, Pallas kernels for 10% -> 10%
where the time goes in v13:
time: 48.2 us; the launch traced here: 47.9 us
  starting transfers between devices  20.9 us (43%)
  waiting for transfers between devices  12.2 us (25%)
  Pallas kernels  10.1 us (21%)
  local copies, waits for them, and re-layouts  4.04 us (8%)
  between operations  0.77 us (2%)
    ppermute x10, starting transfers between devices, swap(): return lax.ppermute(x, 'expert', [(i, i ^ bits) for i in range(count)])  16.5 us
    pallas_call x8, Pallas kernels, call(): pl.pallas_call(kernel, out_shape=out_shape, in_specs=[pl.BlockSpec(memory...  10.1 us
    ppermute x10, waiting for transfers between devices, swap(): return lax.ppermute(x, 'expert', [(i, i ^ bits) for i in range(count)])  7.89 us
    all_to_all x1, waiting for transfers between devices, gather_body(): lax.all_to_all(back, 'expert', split_axis=0, concat_axis=0, tiled=True)  4.26 us
    all_to_all x1, starting transfers between devices, gather_body(): lax.all_to_all(back, 'expert', split_axis=0, concat_axis=0, tiled=True)  4.25 us
    unnamed x18, local copies, waits for them, and re-layouts  4.04 us
  transfers between devices with their start and end apart: 12, of which 5 were waited for; matrix products, arithmetic and copies ran while one was open for 0% of the time, Pallas kernels for 10%

profile of v13, /device:TPU:0, one launch (start us, length us, event | category | flops | bytes accessed | tf_op | source)
XLA Modules:
  0.0 47.9 jit_solution(16696941129548765189)
XLA Ops:
  0.6 2.6 %shard_map.94 = (f32[72,128]{1,0:T(8,128)}, s32[72,128]{1,0:T(8,128)}, f32[72,128]{1,0:T(8,128)}, f32[72,128]{1,0:T(8,128)}, bf16[48,3712]{1,0:T(8,128)(2,1)}, /...) custom-call(s32[8]{0:T(128)} %replica_ref.1, s32[1,8]{1,0:T(1,128)} %refs_1_.1, ...), custom_call_target="tpu_custom_call" | custom-call | flops 66060288 | bytes 2224192 | tf_op jit(solution)/shard_map/pallas_call | solution.py:395
  3.2 3.0 %collective-permute-start.2 = (bf16[48,3712]{1,0:T(8,128)(2,1)}, bf16[48,3712]{1,0:T(8,128)(2,1)S(1)}, u32[]{:S(2)}, u32[]{:S(2)}) collective-permute-start(bf16[48,3712]{1,0:T(8,128)(2,1)} %get-tuple-element.34), channel_id=1, source_target_pairs={{0,2},{2,0},{4,6},{6,4},{8,10},{10,8},{12,14},{14,12},{1,3},{3,1},... | collective-permute-start | bytes 1069064 | tf_op jit(solution)/shard_map/ppermute | solution.py:407
  6.2 1.6 %collective-permute-start = (bf16[24,3712]{1,0:T(8,128)(2,1)}, bf16[24,3712]{1,0:T(8,128)(2,1)S(1)}, u32[]{:S(2)}, u32[]{:S(2)}) collective-permute-start(bf16[24,3712]{1,0:T(8,128)(2,1)} %get-tuple-element.33), channel_id=1, source_target_pairs={{0,4},{2,6},{4,0},{6,2},{8,12},{10,14},{12,8},{14,10},{1,5},{3,7},... | collective-permute-start | bytes 534536 | tf_op jit(solution)/shard_map/ppermute | solution.py:407
  7.8 2.6 %collective-permute-start.1 = (bf16[24,3712]{1,0:T(8,128)(2,1)}, bf16[24,3712]{1,0:T(8,128)(2,1)S(1)}, u32[]{:S(2)}, u32[]{:S(2)}) collective-permute-start(bf16[24,3712]{1,0:T(8,128)(2,1)} %get-tuple-element.33), channel_id=1, source_target_pairs={{0,8},{2,10},{4,12},{6,14},{8,0},{10,2},{12,4},{14,6},{1,9},{3,11}... | collective-permute-start | bytes 534536 | tf_op jit(solution)/shard_map/ppermute | solution.py:407
  10.4 0.0 copy-start
  10.4 1.5 %copy-done = bf16[2,128,3584]{2,1,0:T(8,128)(2,1)S(1)} copy-done((bf16[2,128,3584]{2,1,0:T(8,128)(2,1)S(1)}, bf16[2,128,3584]{2,1,0:T(8,128)(2,1)}, u32[]{:S(2)}) %copy-start) | copy-done | bytes 1835032
  11.9 0.0 copy-start.1
  11.9 0.9 %copy-done.1 = bf16[30,3712]{1,0:T(8,128)(2,1)S(1)} copy-done((bf16[30,3712]{1,0:T(8,128)(2,1)S(1)}, bf16[30,3712]{1,0:T(8,128)(2,1)}, u32[]{:S(2)}) %copy-start.1) | copy-done | bytes 222744
  12.8 0.0 copy-start.2
  12.8 0.9 %copy-done.2 = bf16[18,3712]{1,0:T(8,128)(2,1)S(1)} copy-done((bf16[18,3712]{1,0:T(8,128)(2,1)S(1)}, bf16[18,3712]{1,0:T(8,128)(2,1)}, u32[]{:S(2)}) %copy-start.2) | copy-done | bytes 133656
  13.7 0.0 copy-start.8
  13.7 0.7 %copy-done.8 = s32[8]{0:T(128)S(1)} copy-done((s32[8]{0:T(128)S(1)}, s32[8]{0:T(128)}, u32[]{:S(2)}) %copy-start.8) | copy-done | bytes 56
  14.4 1.2 %shard_map.95 = (bf16[30,3712]{1,0:T(8,128)(2,1)S(1)}, bf16[18,3712]{1,0:T(8,128)(2,1)S(1)}, bf16[256,3584]{1,0:T(8,128)(2,1)S(1)}, s32[30,128]{1,0:T(8,128)S(1)}) custom-call(s32[8]{0:T(128)S(1)} %copy-done.8, bf16[256,3584]{1,0:T(8,128)(2,1)S(1)} %bitcast.8, bf16[30,3712]{1,0:T(8,128)(2,1)S(1)} %copy-done.1, bf16[18,3712]{1,0:T(8,128)(2,1)S(1)} %copy-done.2), custom_call_target="tpu_custom_call" | custom-call | bytes 4398112 | tf_op jit(solution)/shard_map/pallas_call | solution.py:395
  15.6 0.4 collective-permute-done.refs_2_
  16.1 2.4 %collective-permute-done.1.refs_3_ = bf16[24,3712]{1,0:T(8,128)(2,1)S(1)} collective-permute-done((bf16[24,3712]{1,0:T(8,128)(2,1)}, bf16[24,3712]{1,0:T(8,128)(2,1)S(1)}, u32[]{:S(2)}, u32[]{:S(2)}) %collective-permute-start.1) | collective-permute-done | bytes 178208 | tf_op jit(solution)/shard_map/ppermute | solution.py:407
  18.5 0.0 collective-permute-done.2.refs_1_.beside_ref
  18.5 0.5 %collective-permute-start.3 = (bf16[24,3712]{1,0:T(8,128)(2,1)S(1)}, bf16[24,3712]{1,0:T(8,128)(2,1)S(1)}, u32[]{:S(2)}, u32[]{:S(2)}) collective-permute-start(bf16[24,3712]{1,0:T(8,128)(2,1)S(1)} %collective-permute-done.1.refs_3_), channel_id=1, source_target_pairs={{0,2},{2,0},{4,6},{6,4},{8,10},{10,8},{12,14},{14,12},{1,3},{3,1},... | collective-permute-start | bytes 534536 | tf_op jit(solution)/shard_map/ppermute | solution.py:407
  19.0 0.4 collective-permute-start.5
  19.4 1.5 %collective-permute-start.4 = (bf16[24,3712]{1,0:T(8,128)(2,1)S(1)}, bf16[24,3712]{1,0:T(8,128)(2,1)S(1)}, u32[]{:S(2)}, u32[]{:S(2)}) collective-permute-start(bf16[24,3712]{1,0:T(8,128)(2,1)S(1)} %collective-permute-done.refs_2_), channel_id=1, source_target_pairs={{0,2},{2,0},{4,6},{6,4},{8,10},{10,8},{12,14},{14,12},{1,3},{3,1},... | collective-permute-start | bytes 534536 | tf_op jit(solution)/shard_map/ppermute | solution.py:407
  20.9 0.1 shard_map.97
  21.1 2.1 %collective-permute-start.7 = (bf16[24,1920]{1,0:T(8,128)(2,1)S(1)}, bf16[24,1920]{1,0:T(8,128)(2,1)S(1)}, u32[]{:S(2)}, u32[]{:S(2)}) collective-permute-start(bf16[24,1920]{1,0:T(8,128)(2,1)S(1)} %get-tuple-element.49), channel_id=1, source_target_pairs={{0,12},{2,14},{4,8},{6,10},{8,4},{10,6},{12,0},{14,2},{1,13},{3,15... | collective-permute-start | bytes 276488 | tf_op jit(solution)/shard_map/ppermute | solution.py:407
  23.1 1.0 %collective-permute-start.8 = (bf16[24,1920]{1,0:T(8,128)(2,1)S(1)}, bf16[24,1920]{1,0:T(8,128)(2,1)S(1)}, u32[]{:S(2)}, u32[]{:S(2)}) collective-permute-start(bf16[24,1920]{1,0:T(8,128)(2,1)S(1)} %get-tuple-element.50), channel_id=1, source_target_pairs={{0,8},{2,10},{4,12},{6,14},{8,0},{10,2},{12,4},{14,6},{1,9},{3,11}... | collective-permute-start | bytes 276488 | tf_op jit(solution)/shard_map/ppermute | solution.py:407
  24.2 0.0 collective-permute-done.3.refs_4_
  24.2 2.0 %collective-permute-start.9 = (bf16[24,1920]{1,0:T(8,128)(2,1)S(1)}, bf16[24,1920]{1,0:T(8,128)(2,1)S(1)}, u32[]{:S(2)}, u32[]{:S(2)}) collective-permute-start(bf16[24,1920]{1,0:T(8,128)(2,1)S(1)} %get-tuple-element.51), channel_id=1, source_target_pairs={{0,4},{2,6},{4,0},{6,2},{8,12},{10,14},{12,8},{14,10},{1,5},{3,7},... | collective-permute-start | bytes 276488 | tf_op jit(solution)/shard_map/ppermute | solution.py:407
  26.1 2.2 %collective-permute-done.5.refs_0_ = bf16[24,3712]{1,0:T(8,128)(2,1)S(1)} collective-permute-done((bf16[24,3712]{1,0:T(8,128)(2,1)S(1)}, bf16[24,3712]{1,0:T(8,128)(2,1)S(1)}, u32[]{:S(2)}, u32[]{:S(2)}) %collective-permute-start.5) | collective-permute-done | bytes 178208 | tf_op jit(solution)/shard_map/ppermute | solution.py:407
  28.4 1.8 %collective-permute-start.6 = (bf16[24,3712]{1,0:T(8,128)(2,1)S(1)}, bf16[24,3712]{1,0:T(8,128)(2,1)S(1)}, u32[]{:S(2)}, u32[]{:S(2)}) collective-permute-start(bf16[24,3712]{1,0:T(8,128)(2,1)S(1)} %collective-permute-done.5.refs_0_), channel_id=1, source_target_pairs={{0,2},{2,0},{4,6},{6,4},{8,10},{10,8},{12,14},{14,12},{1,3},{3,1},... | collective-permute-start | bytes 534536 | tf_op jit(solution)/shard_map/ppermute | solution.py:407
  30.2 0.0 collective-permute-done.4.refs_5_
  30.2 0.8 %shard_map.96 = (bf16[160,3712]{1,0:T(8,128)(2,1)S(1)}, f32[160,128]{1,0:T(8,128)S(1)}) custom-call(bf16[256,3584]{1,0:T(8,128)(2,1)S(1)} %get-tuple-element.41.w_ref, s32[30,128]{1,0:T(8,128)S(1)} %get-tuple-element.42.slot_ref, bf16[30,3712]{1,0:T(8,128)(2,1)S(1)} %get-tuple-element.43.refs_0_, ...), custom_call_target="tpu_custom_call" | custom-call | flops 8808038400 | bytes 4411904 | tf_op jit(solution)/shard_map/pallas_call | solution.py:395
  31.0 0.0 collective-permute-done.7.refs_2_
  31.0 0.0 collective-permute-done.8.refs_3_
  31.0 0.0 collective-permute-done.9.refs_4_
  31.0 2.8 %collective-permute-done.6.refs_1_ = bf16[24,3712]{1,0:T(8,128)(2,1)S(1)} collective-permute-done((bf16[24,3712]{1,0:T(8,128)(2,1)S(1)}, bf16[24,3712]{1,0:T(8,128)(2,1)S(1)}, u32[]{:S(2)}, u32[]{:S(2)}) %collective-permute-start.6) | collective-permute-done | bytes 178208 | tf_op jit(solution)/shard_map/ppermute | solution.py:407
  33.8 1.3 %shard_map.98 = (bf16[96,3712]{1,0:T(8,128)(2,1)S(1)}, bf16[256,128]{1,0:T(8,128)(2,1)}) custom-call(f32[160,128]{1,0:T(8,128)S(1)} %get-tuple-element.47.own_ref, bf16[256,3584]{1,0:T(8,128)(2,1)S(1)} %get-tuple-element.41.w_ref, s32[30,128]{1,0:T(8,128)S(1)} %get-tuple-element.42.slot_ref, bf16[24,3712]{1,0:T(8,128)(2,1)S(1)} %collective-permute-done.5.refs_0_, ...), custom_call_target="tpu_custom_call" | custom-call | flops 176160768 | bytes 3343360 | tf_op jit(solution)/shard_map/pallas_call | solution.py:395
  35.2 0.4 shard_map.99
  35.6 0.1 collective-permute-start.10
  35.7 4.3 %all-to-all-start = ((bf16[8,32,128]{2,1,0:T(8,128)(2,1)}), bf16[8,32,128]{2,1,0:T(8,128)(2,1)S(1)}, u32[]{:S(2)}, u32[]{:S(2)}) async-start(bf16[8,32,128]{2,1,0:T(8,128)(2,1)} %bitcast.4), calls=%async_computation | async-start | bytes 131072 | tf_op jit(solution)/shard_map/all_to_all | solution.py:485
  40.0 0.0 copy-start.3
  40.0 0.0 copy-start.4
  40.0 0.0 copy-start.5
  40.0 0.0 copy-start.6
  40.0 0.0 copy-start.7
  40.0 0.0 collective-permute-done.10.arrived_ref
  40.0 2.6 %shard_map.100 = bf16[256,1792]{1,0:T(8,128)(2,1)} custom-call(s32[30,128]{1,0:T(8,128)S(1)} %get-tuple-element.42.slot_ref, bf16[160,3712]{1,0:T(8,128)(2,1)S(1)} %get-tuple-element.53.early_ref, bf16[96,3712]{1,0:T(8,128)(2,1)S(1)} %get-tuple-element.54.late_ref, bf16[256,1792]{1,0:T(8,128)(2,1)} %collective-permute-done.10.arrived_ref), custom_call_target="tpu_custom_call" | custom-call | flops 6606028800 | bytes 3750912 | tf_op jit(solution)/shard_map/pallas_call | solution.py:395
  42.6 4.3 %all-to-all-done.back_ref = bf16[8,32,128]{2,1,0:T(8,128)(2,1)S(1)} async-done(((bf16[8,32,128]{2,1,0:T(8,128)(2,1)}), bf16[8,32,128]{2,1,0:T(8,128)(2,1)S(1)}, u32[]{:S(2)}, u32[]{:S(2)}) %all-to-all-start) | async-done | bytes 65568 | tf_op jit(solution)/shard_map/all_to_all | solution.py:485
  46.9 0.0 copy-done.3
  46.9 0.0 copy-done.4
  46.9 0.0 copy-done.5
  46.9 0.0 copy-done.6
  46.9 0.0 copy-done.7
  46.9 1.0 %shard_map.101 = (bf16[1024,128]{1,0:T(8,128)(2,1)}, bf16[8,128]{1,0:T(8,128)(2,1)}) custom-call(bf16[8,32,128]{2,1,0:T(8,128)(2,1)S(1)} %all-to-all-done.back_ref, f32[72,128]{1,0:T(8,128)S(1)} %copy-done.3, s32[72,128]{1,0:T(8,128)S(1)} %copy-done.4, f32[72,128]{1,0:T(8,128)S(1)} %copy-done.5, f32[72,128]{1,0:T(8,128)S(1)} %copy-done.6, s32[8,128]{1,0:T(8,128)S(1)} %bitcast.10), custom_call_target="tpu_custom_call" | custom-call | flops 18874368 | bytes 481280 | tf_op jit(solution)/shard_map/pallas_call | solution.py:395
Async XLA Ops:
  3.2 15.3 %collective-permute-start.2 = (bf16[48,3712]{1,0:T(8,128)(2,1)}, bf16[48,3712]{1,0:T(8,128)(2,1)S(1)}, u32[]{:S(2)}, u32[]{:S(2)}) collective-permute-start(bf16[48,3712]{1,0:T(8,128)(2,1)} %get-tuple-element.34), channel_id=1, source_target_pairs={{0,2},{2,0},{4,6},{6,4},{8,10},{10,8},{12,14},{14,12},{1,3},{3,1},... | collective-permute-start | bytes 1069064 | tf_op jit(solution)/shard_map/ppermute | solution.py:407
  6.2 9.9 %collective-permute-start = (bf16[24,3712]{1,0:T(8,128)(2,1)}, bf16[24,3712]{1,0:T(8,128)(2,1)S(1)}, u32[]{:S(2)}, u32[]{:S(2)}) collective-permute-start(bf16[24,3712]{1,0:T(8,128)(2,1)} %get-tuple-element.33), channel_id=1, source_target_pairs={{0,4},{2,6},{4,0},{6,2},{8,12},{10,14},{12,8},{14,10},{1,5},{3,7},... | collective-permute-start | bytes 534536 | tf_op jit(solution)/shard_map/ppermute | solution.py:407
  7.8 10.7 %collective-permute-start.1 = (bf16[24,3712]{1,0:T(8,128)(2,1)}, bf16[24,3712]{1,0:T(8,128)(2,1)S(1)}, u32[]{:S(2)}, u32[]{:S(2)}) collective-permute-start(bf16[24,3712]{1,0:T(8,128)(2,1)} %get-tuple-element.33), channel_id=1, source_target_pairs={{0,8},{2,10},{4,12},{6,14},{8,0},{10,2},{12,4},{14,6},{1,9},{3,11}... | collective-permute-start | bytes 534536 | tf_op jit(solution)/shard_map/ppermute | solution.py:407
  10.4 1.5 %copy-start = (bf16[2,128,3584]{2,1,0:T(8,128)(2,1)S(1)}, bf16[2,128,3584]{2,1,0:T(8,128)(2,1)}, u32[]{:S(2)}) copy-start(bf16[2,128,3584]{2,1,0:T(8,128)(2,1)} %param.13) | copy-start | bytes 5505028
  11.9 0.9 %copy-start.1 = (bf16[30,3712]{1,0:T(8,128)(2,1)S(1)}, bf16[30,3712]{1,0:T(8,128)(2,1)}, u32[]{:S(2)}) copy-start(bf16[30,3712]{1,0:T(8,128)(2,1)} %get-tuple-element.35.own_hbm) | copy-start | bytes 668164
  12.8 0.9 %copy-start.2 = (bf16[18,3712]{1,0:T(8,128)(2,1)S(1)}, bf16[18,3712]{1,0:T(8,128)(2,1)}, u32[]{:S(2)}) copy-start(bf16[18,3712]{1,0:T(8,128)(2,1)} %get-tuple-element.36.even_hbm) | copy-start | bytes 400900
  13.7 0.7 %copy-start.8 = (s32[8]{0:T(128)S(1)}, s32[8]{0:T(128)}, u32[]{:S(2)}) copy-start(s32[8]{0:T(128)} %replica_ref.1) | copy-start | bytes 100
  18.5 5.7 %collective-permute-start.3 = (bf16[24,3712]{1,0:T(8,128)(2,1)S(1)}, bf16[24,3712]{1,0:T(8,128)(2,1)S(1)}, u32[]{:S(2)}, u32[]{:S(2)}) collective-permute-start(bf16[24,3712]{1,0:T(8,128)(2,1)S(1)} %collective-permute-done.1.refs_3_), channel_id=1, source_target_pairs={{0,2},{2,0},{4,6},{6,4},{8,10},{10,8},{12,14},{14,12},{1,3},{3,1},... | collective-permute-start | bytes 534536 | tf_op jit(solution)/shard_map/ppermute | solution.py:407
  19.0 9.4 %collective-permute-start.5 = (bf16[24,3712]{1,0:T(8,128)(2,1)S(1)}, bf16[24,3712]{1,0:T(8,128)(2,1)S(1)}, u32[]{:S(2)}, u32[]{:S(2)}) collective-permute-start(bf16[24,3712]{1,0:T(8,128)(2,1)S(1)} %collective-permute-done.1.refs_3_), channel_id=1, source_target_pairs={{0,4},{2,6},{4,0},{6,2},{8,12},{10,14},{12,8},{14,10},{1,5},{3,7},... | collective-permute-start | bytes 534536 | tf_op jit(solution)/shard_map/ppermute | solution.py:407
  19.4 10.7 %collective-permute-start.4 = (bf16[24,3712]{1,0:T(8,128)(2,1)S(1)}, bf16[24,3712]{1,0:T(8,128)(2,1)S(1)}, u32[]{:S(2)}, u32[]{:S(2)}) collective-permute-start(bf16[24,3712]{1,0:T(8,128)(2,1)S(1)} %collective-permute-done.refs_2_), channel_id=1, source_target_pairs={{0,2},{2,0},{4,6},{6,4},{8,10},{10,8},{12,14},{14,12},{1,3},{3,1},... | collective-permute-start | bytes 534536 | tf_op jit(solution)/shard_map/ppermute | solution.py:407
  21.1 9.9 %collective-permute-start.7 = (bf16[24,1920]{1,0:T(8,128)(2,1)S(1)}, bf16[24,1920]{1,0:T(8,128)(2,1)S(1)}, u32[]{:S(2)}, u32[]{:S(2)}) collective-permute-start(bf16[24,1920]{1,0:T(8,128)(2,1)S(1)} %get-tuple-element.49), channel_id=1, source_target_pairs={{0,12},{2,14},{4,8},{6,10},{8,4},{10,6},{12,0},{14,2},{1,13},{3,15... | collective-permute-start | bytes 276488 | tf_op jit(solution)/shard_map/ppermute | solution.py:407
  23.1 7.8 %collective-permute-start.8 = (bf16[24,1920]{1,0:T(8,128)(2,1)S(1)}, bf16[24,1920]{1,0:T(8,128)(2,1)S(1)}, u32[]{:S(2)}, u32[]{:S(2)}) collective-permute-start(bf16[24,1920]{1,0:T(8,128)(2,1)S(1)} %get-tuple-element.50), channel_id=1, source_target_pairs={{0,8},{2,10},{4,12},{6,14},{8,0},{10,2},{12,4},{14,6},{1,9},{3,11}... | collective-permute-start | bytes 276488 | tf_op jit(solution)/shard_map/ppermute | solution.py:407
  24.2 6.8 %collective-permute-start.9 = (bf16[24,1920]{1,0:T(8,128)(2,1)S(1)}, bf16[24,1920]{1,0:T(8,128)(2,1)S(1)}, u32[]{:S(2)}, u32[]{:S(2)}) collective-permute-start(bf16[24,1920]{1,0:T(8,128)(2,1)S(1)} %get-tuple-element.51), channel_id=1, source_target_pairs={{0,4},{2,6},{4,0},{6,2},{8,12},{10,14},{12,8},{14,10},{1,5},{3,7},... | collective-permute-start | bytes 276488 | tf_op jit(solution)/shard_map/ppermute | solution.py:407
  28.4 5.5 %collective-permute-start.6 = (bf16[24,3712]{1,0:T(8,128)(2,1)S(1)}, bf16[24,3712]{1,0:T(8,128)(2,1)S(1)}, u32[]{:S(2)}, u32[]{:S(2)}) collective-permute-start(bf16[24,3712]{1,0:T(8,128)(2,1)S(1)} %collective-permute-done.5.refs_0_), channel_id=1, source_target_pairs={{0,2},{2,0},{4,6},{6,4},{8,10},{10,8},{12,14},{14,12},{1,3},{3,1},... | collective-permute-start | bytes 534536 | tf_op jit(solution)/shard_map/ppermute | solution.py:407
  35.6 4.4 %collective-permute-start.10 = (bf16[256,1792]{1,0:T(8,128)(2,1)S(1)}, bf16[256,1792]{1,0:T(8,128)(2,1)}, u32[]{:S(2)}, u32[]{:S(2)}) collective-permute-start(bf16[256,1792]{1,0:T(8,128)(2,1)S(1)} %shard_map.99), channel_id=1, source_target_pairs={{0,1},{1,0},{2,3},{3,2},{4,5},{5,4},{6,7},{7,6},{8,9},{9,8},{10,11... | collective-permute-start | bytes 2752520 | tf_op jit(solution)/shard_map/ppermute | solution.py:494
  35.7 11.2 %all-to-all-start = ((bf16[8,32,128]{2,1,0:T(8,128)(2,1)}), bf16[8,32,128]{2,1,0:T(8,128)(2,1)S(1)}, u32[]{:S(2)}, u32[]{:S(2)}) async-start(bf16[8,32,128]{2,1,0:T(8,128)(2,1)} %bitcast.4), calls=%async_computation | async-start | bytes 131072 | tf_op jit(solution)/shard_map/all_to_all | solution.py:485
  40.0 6.9 %copy-start.3 = (f32[72,128]{1,0:T(8,128)S(1)}, f32[72,128]{1,0:T(8,128)}, u32[]{:S(2)}) copy-start(f32[72,128]{1,0:T(8,128)} %get-tuple-element.56.pick_ref) | copy-start | bytes 110596
  40.0 6.9 %copy-start.4 = (s32[72,128]{1,0:T(8,128)S(1)}, s32[72,128]{1,0:T(8,128)}, u32[]{:S(2)}) copy-start(s32[72,128]{1,0:T(8,128)} %get-tuple-element.57.expert_ref) | copy-start | bytes 110596
  40.0 6.9 %copy-start.5 = (f32[72,128]{1,0:T(8,128)S(1)}, f32[72,128]{1,0:T(8,128)}, u32[]{:S(2)}) copy-start(f32[72,128]{1,0:T(8,128)} %get-tuple-element.58.hs_ref) | copy-start | bytes 110596
  40.0 6.9 %copy-start.6 = (f32[72,128]{1,0:T(8,128)S(1)}, f32[72,128]{1,0:T(8,128)}, u32[]{:S(2)}) copy-start(f32[72,128]{1,0:T(8,128)} %get-tuple-element.59.ps_ref) | copy-start | bytes 110596
  40.0 6.9 %copy-start.7 = (s32[128,8]{0,1:T(8,128)S(1)}, s32[128,8]{0,1:T(8,128)}, u32[]{:S(2)}) copy-start(s32[128,8]{0,1:T(8,128)} %param.10) | copy-start | bytes 12292

commit v14 on v13

--- a/solution.py
+++ b/solution.py
@@ -465,7 +465,7 @@
         functools.partial(early_kernel, *sizes, orders[0], pieces),
         (shape((height, d_model + width), BF16), shape((height, width), F32)),
         [(vmem, a) for a in (w_held, slot, own_rows, beside, near, far, far_beside, near_beside)],
-        flops=2 * height * d_model * local_count * width * 30,
+        flops=2 * height * d_model * local_count * width,
     )
     far_across = swap(far_near, 1, dev_count)
     arrays = [far_near, far_across, *lines[::-1]]

time: 48.2 us -> 47.9 us (level)
  starting transfers between devices: 20.9 us -> 19.2 us
  waiting for transfers between devices: 12.2 us -> 13.5 us
    ppermute x10, starting transfers between devices: 16.5 us -> 14.5 us  [swap(): return lax.ppermute(x, 'expert', [(i, i ^ bits) for i in range(count)])]
    ppermute x10, waiting for transfers between devices: 7.89 us -> 9.23 us  [swap(): return lax.ppermute(x, 'expert', [(i, i ^ bits) for i in range(count)])]
  transfers between devices with their start and end apart: 12 -> 12, of which waited for: 5 -> 7; matrix products, arithmetic and copies ran while one was open for 0% -> 0% of each run, Pallas kernels for 10% -> 10%
where the time goes in v14:
time: 47.9 us; the launch traced here: 47.6 us
  starting transfers between devices  19.2 us (40%)
  waiting for transfers between devices  13.5 us (28%)
  Pallas kernels  10.1 us (21%)
  local copies, waits for them, and re-layouts  4.04 us (8%)
  between operations  0.75 us (2%)
    ppermute x10, starting transfers between devices, swap(): return lax.ppermute(x, 'expert', [(i, i ^ bits) for i in range(count)])  14.5 us
    pallas_call x8, Pallas kernels, call(): pl.pallas_call(kernel, out_shape=out_shape, in_specs=[pl.BlockSpec(memory...  10.1 us
    ppermute x10, waiting for transfers between devices, swap(): return lax.ppermute(x, 'expert', [(i, i ^ bits) for i in range(count)])  9.23 us
    all_to_all x1, starting transfers between devices, gather_body(): lax.all_to_all(back, 'expert', split_axis=0, concat_axis=0, tiled=True)  4.65 us
    all_to_all x1, waiting for transfers between devices, gather_body(): lax.all_to_all(back, 'expert', split_axis=0, concat_axis=0, tiled=True)  4.26 us
    unnamed x18, local copies, waits for them, and re-layouts  4.04 us
  transfers between devices with their start and end apart: 12, of which 7 were waited for; matrix products, arithmetic and copies ran while one was open for 0% of the time, Pallas kernels for 10%

profile of v14, /device:TPU:0, one launch (start us, length us, event | category | flops | bytes accessed | tf_op | source)
XLA Modules:
  0.0 47.6 jit_solution(10494869474429544883)
XLA Ops:
  0.6 2.6 %shard_map.94 = (f32[72,128]{1,0:T(8,128)}, s32[72,128]{1,0:T(8,128)}, f32[72,128]{1,0:T(8,128)}, f32[72,128]{1,0:T(8,128)}, bf16[48,3712]{1,0:T(8,128)(2,1)}, /...) custom-call(s32[8]{0:T(128)} %replica_ref.1, s32[1,8]{1,0:T(1,128)} %refs_1_.1, ...), custom_call_target="tpu_custom_call" | custom-call | flops 66060288 | bytes 2224192 | tf_op jit(solution)/shard_map/pallas_call | solution.py:395
  3.2 3.0 %collective-permute-start.2 = (bf16[48,3712]{1,0:T(8,128)(2,1)}, bf16[48,3712]{1,0:T(8,128)(2,1)S(1)}, u32[]{:S(2)}, u32[]{:S(2)}) collective-permute-start(bf16[48,3712]{1,0:T(8,128)(2,1)} %get-tuple-element.34), channel_id=1, source_target_pairs={{0,2},{2,0},{4,6},{6,4},{8,10},{10,8},{12,14},{14,12},{1,3},{3,1},... | collective-permute-start | bytes 1069064 | tf_op jit(solution)/shard_map/ppermute | solution.py:407
  6.2 1.6 %collective-permute-start = (bf16[24,3712]{1,0:T(8,128)(2,1)}, bf16[24,3712]{1,0:T(8,128)(2,1)S(1)}, u32[]{:S(2)}, u32[]{:S(2)}) collective-permute-start(bf16[24,3712]{1,0:T(8,128)(2,1)} %get-tuple-element.33), channel_id=1, source_target_pairs={{0,4},{2,6},{4,0},{6,2},{8,12},{10,14},{12,8},{14,10},{1,5},{3,7},... | collective-permute-start | bytes 534536 | tf_op jit(solution)/shard_map/ppermute | solution.py:407
  7.8 2.6 %collective-permute-start.1 = (bf16[24,3712]{1,0:T(8,128)(2,1)}, bf16[24,3712]{1,0:T(8,128)(2,1)S(1)}, u32[]{:S(2)}, u32[]{:S(2)}) collective-permute-start(bf16[24,3712]{1,0:T(8,128)(2,1)} %get-tuple-element.33), channel_id=1, source_target_pairs={{0,8},{2,10},{4,12},{6,14},{8,0},{10,2},{12,4},{14,6},{1,9},{3,11}... | collective-permute-start | bytes 534536 | tf_op jit(solution)/shard_map/ppermute | solution.py:407
  10.4 0.0 copy-start
  10.4 1.5 %copy-done = bf16[2,128,3584]{2,1,0:T(8,128)(2,1)S(1)} copy-done((bf16[2,128,3584]{2,1,0:T(8,128)(2,1)S(1)}, bf16[2,128,3584]{2,1,0:T(8,128)(2,1)}, u32[]{:S(2)}) %copy-start) | copy-done | bytes 1835032
  11.9 0.0 copy-start.1
  11.9 0.9 %copy-done.1 = bf16[30,3712]{1,0:T(8,128)(2,1)S(1)} copy-done((bf16[30,3712]{1,0:T(8,128)(2,1)S(1)}, bf16[30,3712]{1,0:T(8,128)(2,1)}, u32[]{:S(2)}) %copy-start.1) | copy-done | bytes 222744
  12.8 0.0 copy-start.2
  12.8 0.9 %copy-done.2 = bf16[18,3712]{1,0:T(8,128)(2,1)S(1)} copy-done((bf16[18,3712]{1,0:T(8,128)(2,1)S(1)}, bf16[18,3712]{1,0:T(8,128)(2,1)}, u32[]{:S(2)}) %copy-start.2) | copy-done | bytes 133656
  13.7 0.0 copy-start.8
  13.7 0.7 %copy-done.8 = s32[8]{0:T(128)S(1)} copy-done((s32[8]{0:T(128)S(1)}, s32[8]{0:T(128)}, u32[]{:S(2)}) %copy-start.8) | copy-done | bytes 56
  14.4 1.2 %shard_map.95 = (bf16[30,3712]{1,0:T(8,128)(2,1)S(1)}, bf16[18,3712]{1,0:T(8,128)(2,1)S(1)}, bf16[256,3584]{1,0:T(8,128)(2,1)S(1)}, s32[30,128]{1,0:T(8,128)S(1)}) custom-call(s32[8]{0:T(128)S(1)} %copy-done.8, bf16[256,3584]{1,0:T(8,128)(2,1)S(1)} %bitcast.8, bf16[30,3712]{1,0:T(8,128)(2,1)S(1)} %copy-done.1, bf16[18,3712]{1,0:T(8,128)(2,1)S(1)} %copy-done.2), custom_call_target="tpu_custom_call" | custom-call | bytes 4398112 | tf_op jit(solution)/shard_map/pallas_call | solution.py:395
  15.6 0.4 collective-permute-done.refs_2_
  16.1 2.5 %collective-permute-done.1.refs_3_ = bf16[24,3712]{1,0:T(8,128)(2,1)S(1)} collective-permute-done((bf16[24,3712]{1,0:T(8,128)(2,1)}, bf16[24,3712]{1,0:T(8,128)(2,1)S(1)}, u32[]{:S(2)}, u32[]{:S(2)}) %collective-permute-start.1) | collective-permute-done | bytes 178208 | tf_op jit(solution)/shard_map/ppermute | solution.py:407
  18.6 0.0 collective-permute-done.2.refs_1_.beside_ref
  18.6 0.3 collective-permute-start.5
  18.9 0.5 %collective-permute-start.3 = (bf16[24,3712]{1,0:T(8,128)(2,1)S(1)}, bf16[24,3712]{1,0:T(8,128)(2,1)S(1)}, u32[]{:S(2)}, u32[]{:S(2)}) collective-permute-start(bf16[24,3712]{1,0:T(8,128)(2,1)S(1)} %collective-permute-done.1.refs_3_), channel_id=1, source_target_pairs={{0,2},{2,0},{4,6},{6,4},{8,10},{10,8},{12,14},{14,12},{1,3},{3,1},... | collective-permute-start | bytes 534536 | tf_op jit(solution)/shard_map/ppermute | solution.py:407
  19.4 1.5 %collective-permute-start.4 = (bf16[24,3712]{1,0:T(8,128)(2,1)S(1)}, bf16[24,3712]{1,0:T(8,128)(2,1)S(1)}, u32[]{:S(2)}, u32[]{:S(2)}) collective-permute-start(bf16[24,3712]{1,0:T(8,128)(2,1)S(1)} %collective-permute-done.refs_2_), channel_id=1, source_target_pairs={{0,2},{2,0},{4,6},{6,4},{8,10},{10,8},{12,14},{14,12},{1,3},{3,1},... | collective-permute-start | bytes 534536 | tf_op jit(solution)/shard_map/ppermute | solution.py:407
  20.9 3.1 %collective-permute-done.5.refs_0_ = bf16[24,3712]{1,0:T(8,128)(2,1)S(1)} collective-permute-done((bf16[24,3712]{1,0:T(8,128)(2,1)S(1)}, bf16[24,3712]{1,0:T(8,128)(2,1)S(1)}, u32[]{:S(2)}, u32[]{:S(2)}) %collective-permute-start.5) | collective-permute-done | bytes 178208 | tf_op jit(solution)/shard_map/ppermute | solution.py:407
  24.1 0.5 %collective-permute-start.6 = (bf16[24,3712]{1,0:T(8,128)(2,1)S(1)}, bf16[24,3712]{1,0:T(8,128)(2,1)S(1)}, u32[]{:S(2)}, u32[]{:S(2)}) collective-permute-start(bf16[24,3712]{1,0:T(8,128)(2,1)S(1)} %collective-permute-done.5.refs_0_), channel_id=1, source_target_pairs={{0,2},{2,0},{4,6},{6,4},{8,10},{10,8},{12,14},{14,12},{1,3},{3,1},... | collective-permute-start | bytes 534536 | tf_op jit(solution)/shard_map/ppermute | solution.py:407
  24.6 0.1 shard_map.97
  24.7 2.4 %collective-permute-start.7 = (bf16[24,1920]{1,0:T(8,128)(2,1)S(1)}, bf16[24,1920]{1,0:T(8,128)(2,1)S(1)}, u32[]{:S(2)}, u32[]{:S(2)}) collective-permute-start(bf16[24,1920]{1,0:T(8,128)(2,1)S(1)} %get-tuple-element.49), channel_id=1, source_target_pairs={{0,12},{2,14},{4,8},{6,10},{8,4},{10,6},{12,0},{14,2},{1,13},{3,15... | collective-permute-start | bytes 276488 | tf_op jit(solution)/shard_map/ppermute | solution.py:407
  27.1 0.0 collective-permute-start.8
  27.1 0.0 collective-permute-done.3.refs_4_
  27.1 2.0 %collective-permute-start.9 = (bf16[24,1920]{1,0:T(8,128)(2,1)S(1)}, bf16[24,1920]{1,0:T(8,128)(2,1)S(1)}, u32[]{:S(2)}, u32[]{:S(2)}) collective-permute-start(bf16[24,1920]{1,0:T(8,128)(2,1)S(1)} %get-tuple-element.51), channel_id=1, source_target_pairs={{0,4},{2,6},{4,0},{6,2},{8,12},{10,14},{12,8},{14,10},{1,5},{3,7},... | collective-permute-start | bytes 276488 | tf_op jit(solution)/shard_map/ppermute | solution.py:407
  29.2 0.1 collective-permute-done.4.refs_5_
  29.3 0.8 %shard_map.96 = (bf16[160,3712]{1,0:T(8,128)(2,1)S(1)}, f32[160,128]{1,0:T(8,128)S(1)}) custom-call(bf16[256,3584]{1,0:T(8,128)(2,1)S(1)} %get-tuple-element.41.w_ref, s32[30,128]{1,0:T(8,128)S(1)} %get-tuple-element.42.slot_ref, bf16[30,3712]{1,0:T(8,128)(2,1)S(1)} %get-tuple-element.43.refs_0_, ...), custom_call_target="tpu_custom_call" | custom-call | flops 293601280 | bytes 4411904 | tf_op jit(solution)/shard_map/pallas_call | solution.py:395
  30.1 1.1 %collective-permute-done.7.refs_2_ = bf16[24,1920]{1,0:T(8,128)(2,1)S(1)} collective-permute-done((bf16[24,1920]{1,0:T(8,128)(2,1)S(1)}, bf16[24,1920]{1,0:T(8,128)(2,1)S(1)}, u32[]{:S(2)}, u32[]{:S(2)}) %collective-permute-start.7) | collective-permute-done | bytes 92192 | tf_op jit(solution)/shard_map/ppermute | solution.py:407
  31.2 1.9 %collective-permute-done.8.refs_3_ = bf16[24,1920]{1,0:T(8,128)(2,1)S(1)} collective-permute-done((bf16[24,1920]{1,0:T(8,128)(2,1)S(1)}, bf16[24,1920]{1,0:T(8,128)(2,1)S(1)}, u32[]{:S(2)}, u32[]{:S(2)}) %collective-permute-start.8) | collective-permute-done | bytes 92192 | tf_op jit(solution)/shard_map/ppermute | solution.py:407
  33.1 0.0 collective-permute-done.9.refs_4_
  33.1 0.0 collective-permute-done.6.refs_1_
  33.1 1.4 %shard_map.98 = (bf16[96,3712]{1,0:T(8,128)(2,1)S(1)}, bf16[256,128]{1,0:T(8,128)(2,1)}) custom-call(f32[160,128]{1,0:T(8,128)S(1)} %get-tuple-element.47.own_ref, bf16[256,3584]{1,0:T(8,128)(2,1)S(1)} %get-tuple-element.41.w_ref, s32[30,128]{1,0:T(8,128)S(1)} %get-tuple-element.42.slot_ref, bf16[24,3712]{1,0:T(8,128)(2,1)S(1)} %collective-permute-done.5.refs_0_, ...), custom_call_target="tpu_custom_call" | custom-call | flops 176160768 | bytes 3343360 | tf_op jit(solution)/shard_map/pallas_call | solution.py:395
  34.5 0.4 shard_map.99
  34.9 0.1 collective-permute-start.10
  35.0 4.6 %all-to-all-start = ((bf16[8,32,128]{2,1,0:T(8,128)(2,1)}), bf16[8,32,128]{2,1,0:T(8,128)(2,1)S(1)}, u32[]{:S(2)}, u32[]{:S(2)}) async-start(bf16[8,32,128]{2,1,0:T(8,128)(2,1)} %bitcast.4), calls=%async_computation | async-start | bytes 131072 | tf_op jit(solution)/shard_map/all_to_all | solution.py:485
  39.6 0.0 copy-start.3
  39.6 0.0 copy-start.4
  39.7 0.0 copy-start.5
  39.7 0.0 copy-start.6
  39.7 0.0 copy-start.7
  39.7 0.0 collective-permute-done.10.arrived_ref
  39.7 2.6 %shard_map.100 = bf16[256,1792]{1,0:T(8,128)(2,1)} custom-call(s32[30,128]{1,0:T(8,128)S(1)} %get-tuple-element.42.slot_ref, bf16[160,3712]{1,0:T(8,128)(2,1)S(1)} %get-tuple-element.53.early_ref, bf16[96,3712]{1,0:T(8,128)(2,1)S(1)} %get-tuple-element.54.late_ref, bf16[256,1792]{1,0:T(8,128)(2,1)} %collective-permute-done.10.arrived_ref), custom_call_target="tpu_custom_call" | custom-call | flops 6606028800 | bytes 3750912 | tf_op jit(solution)/shard_map/pallas_call | solution.py:395
  42.3 4.3 %all-to-all-done.back_ref = bf16[8,32,128]{2,1,0:T(8,128)(2,1)S(1)} async-done(((bf16[8,32,128]{2,1,0:T(8,128)(2,1)}), bf16[8,32,128]{2,1,0:T(8,128)(2,1)S(1)}, u32[]{:S(2)}, u32[]{:S(2)}) %all-to-all-start) | async-done | bytes 65568 | tf_op jit(solution)/shard_map/all_to_all | solution.py:485
  46.5 0.0 copy-done.3
  46.5 0.0 copy-done.4
  46.6 0.0 copy-done.5
  46.6 0.0 copy-done.6
  46.6 0.0 copy-done.7
  46.6 1.0 %shard_map.101 = (bf16[1024,128]{1,0:T(8,128)(2,1)}, bf16[8,128]{1,0:T(8,128)(2,1)}) custom-call(bf16[8,32,128]{2,1,0:T(8,128)(2,1)S(1)} %all-to-all-done.back_ref, f32[72,128]{1,0:T(8,128)S(1)} %copy-done.3, s32[72,128]{1,0:T(8,128)S(1)} %copy-done.4, f32[72,128]{1,0:T(8,128)S(1)} %copy-done.5, f32[72,128]{1,0:T(8,128)S(1)} %copy-done.6, s32[8,128]{1,0:T(8,128)S(1)} %bitcast.10), custom_call_target="tpu_custom_call" | custom-call | flops 18874368 | bytes 481280 | tf_op jit(solution)/shard_map/pallas_call | solution.py:395
Async XLA Ops:
  3.2 15.4 %collective-permute-start.2 = (bf16[48,3712]{1,0:T(8,128)(2,1)}, bf16[48,3712]{1,0:T(8,128)(2,1)S(1)}, u32[]{:S(2)}, u32[]{:S(2)}) collective-permute-start(bf16[48,3712]{1,0:T(8,128)(2,1)} %get-tuple-element.34), channel_id=1, source_target_pairs={{0,2},{2,0},{4,6},{6,4},{8,10},{10,8},{12,14},{14,12},{1,3},{3,1},... | collective-permute-start | bytes 1069064 | tf_op jit(solution)/shard_map/ppermute | solution.py:407
  6.2 9.9 %collective-permute-start = (bf16[24,3712]{1,0:T(8,128)(2,1)}, bf16[24,3712]{1,0:T(8,128)(2,1)S(1)}, u32[]{:S(2)}, u32[]{:S(2)}) collective-permute-start(bf16[24,3712]{1,0:T(8,128)(2,1)} %get-tuple-element.33), channel_id=1, source_target_pairs={{0,4},{2,6},{4,0},{6,2},{8,12},{10,14},{12,8},{14,10},{1,5},{3,7},... | collective-permute-start | bytes 534536 | tf_op jit(solution)/shard_map/ppermute | solution.py:407
  7.8 10.8 %collective-permute-start.1 = (bf16[24,3712]{1,0:T(8,128)(2,1)}, bf16[24,3712]{1,0:T(8,128)(2,1)S(1)}, u32[]{:S(2)}, u32[]{:S(2)}) collective-permute-start(bf16[24,3712]{1,0:T(8,128)(2,1)} %get-tuple-element.33), channel_id=1, source_target_pairs={{0,8},{2,10},{4,12},{6,14},{8,0},{10,2},{12,4},{14,6},{1,9},{3,11}... | collective-permute-start | bytes 534536 | tf_op jit(solution)/shard_map/ppermute | solution.py:407
  10.4 1.5 %copy-start = (bf16[2,128,3584]{2,1,0:T(8,128)(2,1)S(1)}, bf16[2,128,3584]{2,1,0:T(8,128)(2,1)}, u32[]{:S(2)}) copy-start(bf16[2,128,3584]{2,1,0:T(8,128)(2,1)} %param.13) | copy-start | bytes 5505028
  11.9 0.9 %copy-start.1 = (bf16[30,3712]{1,0:T(8,128)(2,1)S(1)}, bf16[30,3712]{1,0:T(8,128)(2,1)}, u32[]{:S(2)}) copy-start(bf16[30,3712]{1,0:T(8,128)(2,1)} %get-tuple-element.35.own_hbm) | copy-start | bytes 668164
  12.8 0.9 %copy-start.2 = (bf16[18,3712]{1,0:T(8,128)(2,1)S(1)}, bf16[18,3712]{1,0:T(8,128)(2,1)}, u32[]{:S(2)}) copy-start(bf16[18,3712]{1,0:T(8,128)(2,1)} %get-tuple-element.36.even_hbm) | copy-start | bytes 400900
  13.7 0.7 %copy-start.8 = (s32[8]{0:T(128)S(1)}, s32[8]{0:T(128)}, u32[]{:S(2)}) copy-start(s32[8]{0:T(128)} %replica_ref.1) | copy-start | bytes 100
  18.6 5.5 %collective-permute-start.5 = (bf16[24,3712]{1,0:T(8,128)(2,1)S(1)}, bf16[24,3712]{1,0:T(8,128)(2,1)S(1)}, u32[]{:S(2)}, u32[]{:S(2)}) collective-permute-start(bf16[24,3712]{1,0:T(8,128)(2,1)S(1)} %collective-permute-done.1.refs_3_), channel_id=1, source_target_pairs={{0,4},{2,6},{4,0},{6,2},{8,12},{10,14},{12,8},{14,10},{1,5},{3,7},... | collective-permute-start | bytes 534536 | tf_op jit(solution)/shard_map/ppermute | solution.py:407
  18.9 8.2 %collective-permute-start.3 = (bf16[24,3712]{1,0:T(8,128)(2,1)S(1)}, bf16[24,3712]{1,0:T(8,128)(2,1)S(1)}, u32[]{:S(2)}, u32[]{:S(2)}) collective-permute-start(bf16[24,3712]{1,0:T(8,128)(2,1)S(1)} %collective-permute-done.1.refs_3_), channel_id=1, source_target_pairs={{0,2},{2,0},{4,6},{6,4},{8,10},{10,8},{12,14},{14,12},{1,3},{3,1},... | collective-permute-start | bytes 534536 | tf_op jit(solution)/shard_map/ppermute | solution.py:407
  19.4 9.9 %collective-permute-start.4 = (bf16[24,3712]{1,0:T(8,128)(2,1)S(1)}, bf16[24,3712]{1,0:T(8,128)(2,1)S(1)}, u32[]{:S(2)}, u32[]{:S(2)}) collective-permute-start(bf16[24,3712]{1,0:T(8,128)(2,1)S(1)} %collective-permute-done.refs_2_), channel_id=1, source_target_pairs={{0,2},{2,0},{4,6},{6,4},{8,10},{10,8},{12,14},{14,12},{1,3},{3,1},... | collective-permute-start | bytes 534536 | tf_op jit(solution)/shard_map/ppermute | solution.py:407
  24.1 9.1 %collective-permute-start.6 = (bf16[24,3712]{1,0:T(8,128)(2,1)S(1)}, bf16[24,3712]{1,0:T(8,128)(2,1)S(1)}, u32[]{:S(2)}, u32[]{:S(2)}) collective-permute-start(bf16[24,3712]{1,0:T(8,128)(2,1)S(1)} %collective-permute-done.5.refs_0_), channel_id=1, source_target_pairs={{0,2},{2,0},{4,6},{6,4},{8,10},{10,8},{12,14},{14,12},{1,3},{3,1},... | collective-permute-start | bytes 534536 | tf_op jit(solution)/shard_map/ppermute | solution.py:407
  24.7 6.5 %collective-permute-start.7 = (bf16[24,1920]{1,0:T(8,128)(2,1)S(1)}, bf16[24,1920]{1,0:T(8,128)(2,1)S(1)}, u32[]{:S(2)}, u32[]{:S(2)}) collective-permute-start(bf16[24,1920]{1,0:T(8,128)(2,1)S(1)} %get-tuple-element.49), channel_id=1, source_target_pairs={{0,12},{2,14},{4,8},{6,10},{8,4},{10,6},{12,0},{14,2},{1,13},{3,15... | collective-permute-start | bytes 276488 | tf_op jit(solution)/shard_map/ppermute | solution.py:407
  27.1 6.0 %collective-permute-start.8 = (bf16[24,1920]{1,0:T(8,128)(2,1)S(1)}, bf16[24,1920]{1,0:T(8,128)(2,1)S(1)}, u32[]{:S(2)}, u32[]{:S(2)}) collective-permute-start(bf16[24,1920]{1,0:T(8,128)(2,1)S(1)} %get-tuple-element.50), channel_id=1, source_target_pairs={{0,8},{2,10},{4,12},{6,14},{8,0},{10,2},{12,4},{14,6},{1,9},{3,11}... | collective-permute-start | bytes 276488 | tf_op jit(solution)/shard_map/ppermute | solution.py:407
  27.1 6.0 %collective-permute-start.9 = (bf16[24,1920]{1,0:T(8,128)(2,1)S(1)}, bf16[24,1920]{1,0:T(8,128)(2,1)S(1)}, u32[]{:S(2)}, u32[]{:S(2)}) collective-permute-start(bf16[24,1920]{1,0:T(8,128)(2,1)S(1)} %get-tuple-element.51), channel_id=1, source_target_pairs={{0,4},{2,6},{4,0},{6,2},{8,12},{10,14},{12,8},{14,10},{1,5},{3,7},... | collective-permute-start | bytes 276488 | tf_op jit(solution)/shard_map/ppermute | solution.py:407
  34.9 4.8 %collective-permute-start.10 = (bf16[256,1792]{1,0:T(8,128)(2,1)S(1)}, bf16[256,1792]{1,0:T(8,128)(2,1)}, u32[]{:S(2)}, u32[]{:S(2)}) collective-permute-start(bf16[256,1792]{1,0:T(8,128)(2,1)S(1)} %shard_map.99), channel_id=1, source_target_pairs={{0,1},{1,0},{2,3},{3,2},{4,5},{5,4},{6,7},{7,6},{8,9},{9,8},{10,11... | collective-permute-start | bytes 2752520 | tf_op jit(solution)/shard_map/ppermute | solution.py:494
  35.0 11.6 %all-to-all-start = ((bf16[8,32,128]{2,1,0:T(8,128)(2,1)}), bf16[8,32,128]{2,1,0:T(8,128)(2,1)S(1)}, u32[]{:S(2)}, u32[]{:S(2)}) async-start(bf16[8,32,128]{2,1,0:T(8,128)(2,1)} %bitcast.4), calls=%async_computation | async-start | bytes 131072 | tf_op jit(solution)/shard_map/all_to_all | solution.py:485
  39.6 6.9 %copy-start.3 = (f32[72,128]{1,0:T(8,128)S(1)}, f32[72,128]{1,0:T(8,128)}, u32[]{:S(2)}) copy-start(f32[72,128]{1,0:T(8,128)} %get-tuple-element.56.pick_ref) | copy-start | bytes 110596
  39.6 6.9 %copy-start.4 = (s32[72,128]{1,0:T(8,128)S(1)}, s32[72,128]{1,0:T(8,128)}, u32[]{:S(2)}) copy-start(s32[72,128]{1,0:T(8,128)} %get-tuple-element.57.expert_ref) | copy-start | bytes 110596
  39.7 6.9 %copy-start.5 = (f32[72,128]{1,0:T(8,128)S(1)}, f32[72,128]{1,0:T(8,128)}, u32[]{:S(2)}) copy-start(f32[72,128]{1,0:T(8,128)} %get-tuple-element.58.hs_ref) | copy-start | bytes 110596
  39.7 6.9 %copy-start.6 = (f32[72,128]{1,0:T(8,128)S(1)}, f32[72,128]{1,0:T(8,128)}, u32[]{:S(2)}) copy-start(f32[72,128]{1,0:T(8,128)} %get-tuple-element.59.ps_ref) | copy-start | bytes 110596
  39.7 6.9 %copy-start.7 = (s32[128,8]{0,1:T(8,128)S(1)}, s32[128,8]{0,1:T(8,128)}, u32[]{:S(2)}) copy-start(s32[128,8]{0,1:T(8,128)} %param.10) | copy-start | bytes 12292

commit v15 on v14

--- a/solution.py
+++ b/solution.py
@@ -179,12 +179,13 @@
     homes = dev_count * per_home
     slots = homes + dev_count * CAPR
     me = lax.axis_index("expert")
-    for move in moves[:3]:
-        move.wait()
     row = iota((slots, toks), 0)
     expert = ((row // per_home) ^ me) * local_count + (row % per_home) // SLOT
     within = row % SLOT
     allowed = jnp.where(within < CAPH, 1, 0)
+    before = jnp.where(iota((toks, toks), 0) < iota((toks, toks), 1), 1.0, 0.0).astype(BF16)
+    for move in moves[:3]:
+        move.wait()
     for d in range(dev_count):
         first = homes + d * CAPR
         mine = (row >= first) & (row < first + CAPR)
@@ -199,7 +200,6 @@
     named = jnp.zeros((slots, toks), F32)
     for k in range(top):
         named = named + jnp.where(ids[k:k + 1, :] == expert, 1.0, 0.0)
-    before = jnp.where(iota((toks, toks), 0) < iota((toks, toks), 1), 1.0, 0.0).astype(BF16)
     rank = jnp.dot(named.astype(BF16), before, preferred_element_type=F32)
     wanted = (lower + within).astype(F32)
     pick = jnp.where((rank == wanted) & (allowed > 0), named, 0.0)
@@ -380,10 +380,11 @@
     ids = ids_ref[...]
     pick = pick_ref[...]
     expert = expert_ref[...]
-    for k in range(top):
-        sel = jnp.where(ids[k:k + 1, :] == expert, pick, 0.0)
-        wide[pl.ds(k, toks, stride=top), :] = lax.dot_general(
-            sel.astype(BF16), h_rows, TN, preferred_element_type=F32)
+    sels = [jnp.where(ids[k:k + 1, :] == expert, pick, 0.0) for k in range(top)]
+    rows = lax.dot_general(
+        jnp.concatenate([sel.astype(BF16) for sel in sels], axis=1), h_rows, TN, preferred_element_type=F32)
+    for k, sel in enumerate(sels):
+        wide[pl.ds(k, toks, stride=top), :] = rows[k * toks:(k + 1) * toks]
         narrow[k:k + 1, :] = jnp.sum(sel * p_rows, axis=0, keepdims=True)
     grad_h_ref[...] = wide[...].astype(grad_h_ref.dtype)
     grad_p_ref[...] = narrow[...].astype(grad_p_ref.dtype)
@@ -458,19 +459,20 @@
     far_beside, near_beside = swap(far, 1, dev_count), swap(near, 1, dev_count)
     lines = [swap(a, m, dev_count) for a, m in zip(lines, even)]
     pieces = {(0, HOME): (0, 0), (0, COPIES): (0, per_home), (1, COPIES): (1, 0), (1, HOME): (1, copies),
-              (2, COPIES): (2, 0), (4, COPIES): (3, 0), (5, COPIES): (4, 0), (3, COPIES): (5, 0)}
+              (2, COPIES): (2, 0), (4, COPIES): (3, 0), (5, COPIES): (4, 0), (3, COPIES): (5, 0),
+              (even[-1], HOME): (6, 0), (even[-1] + 1, HOME): (6, per_home)}
     orders = [list(pieces)]
     height = padded(sum(per_home if kind == HOME else copies for _, kind in pieces))
     early_rows, own = call(
         functools.partial(early_kernel, *sizes, orders[0], pieces),
         (shape((height, d_model + width), BF16), shape((height, width), F32)),
-        [(vmem, a) for a in (w_held, slot, own_rows, beside, near, far, far_beside, near_beside)],
+        [(vmem, a) for a in (w_held, slot, own_rows, beside, near, far, far_beside, near_beside, lines[-1])],
         flops=2 * height * d_model * local_count * width,
     )
     far_across = swap(far_near, 1, dev_count)
-    arrays = [far_near, far_across, *lines[::-1]]
+    arrays = [far_near, far_across, *lines[-2::-1]]
     pieces = {(6, COPIES): (0, 0), (7, COPIES): (1, 0)}
-    for n, m in enumerate(even[::-1]):
+    for n, m in enumerate(even[-2::-1]):
         pieces[m, HOME], pieces[m + 1, HOME] = ((2 + n, k * per_home) for k in range(2))
     orders.append(list(pieces))
     height = padded(sum(per_home if kind == HOME else copies for _, kind in pieces))

time: 47.9 us -> 46.8 us (0.977)
  starting transfers between devices: 19.2 us -> 17.3 us
  waiting for transfers between devices: 13.5 us -> 14.3 us
    ppermute x10, starting transfers between devices: 14.5 us -> 13.4 us  [swap(): return lax.ppermute(x, 'expert', [(i, i ^ bits) for i in range(count)])]
    ppermute x10, waiting for transfers between devices: 9.23 us -> 10.1 us  [swap(): return lax.ppermute(x, 'expert', [(i, i ^ bits) for i in range(count)])]
    all_to_all x1, starting transfers between devices: 4.65 us -> 3.82 us  [gather_body(): lax.all_to_all(back, 'expert', split_axis=0, concat_axis=0, tiled=True)]
  transfers between devices with their start and end apart: 12 -> 12, of which waited for: 7 -> 8; matrix products, arithmetic and copies ran while one was open for 0% -> 0% of each run, Pallas kernels for 10% -> 10%
where the time goes in v15:
time: 46.8 us; the launch traced here: 46.5 us
  starting transfers between devices  17.3 us (37%)
  waiting for transfers between devices  14.3 us (31%)
  Pallas kernels  10.1 us (22%)
  local copies, waits for them, and re-layouts  4.04 us (9%)
  between operations  0.75 us (2%)
    ppermute x10, starting transfers between devices, swap(): return lax.ppermute(x, 'expert', [(i, i ^ bits) for i in range(count)])  13.4 us
    pallas_call x8, Pallas kernels, call(): pl.pallas_call(kernel, out_shape=out_shape, in_specs=[pl.BlockSpec(memory...  10.1 us
    ppermute x10, waiting for transfers between devices, swap(): return lax.ppermute(x, 'expert', [(i, i ^ bits) for i in range(count)])  10.1 us
    all_to_all x1, waiting for transfers between devices, gather_body(): lax.all_to_all(back, 'expert', split_axis=0, concat_axis=0, tiled=True)  4.26 us
    unnamed x18, local copies, waits for them, and re-layouts  4.04 us
    all_to_all x1, starting transfers between devices, gather_body(): lax.all_to_all(back, 'expert', split_axis=0, concat_axis=0, tiled=True)  3.82 us
  transfers between devices with their start and end apart: 12, of which 8 were waited for; matrix products, arithmetic and copies ran while one was open for 0% of the time, Pallas kernels for 10%

profile of v15, /device:TPU:0, one launch (start us, length us, event | category | flops | bytes accessed | tf_op | source)
XLA Modules:
  0.0 46.5 jit_solution(17407675411195935874)
XLA Ops:
  0.6 2.6 %shard_map.94 = (f32[72,128]{1,0:T(8,128)}, s32[72,128]{1,0:T(8,128)}, f32[72,128]{1,0:T(8,128)}, f32[72,128]{1,0:T(8,128)}, bf16[48,3712]{1,0:T(8,128)(2,1)}, /...) custom-call(s32[8]{0:T(128)} %replica_ref.1, s32[1,8]{1,0:T(1,128)} %refs_1_.1, ...), custom_call_target="tpu_custom_call" | custom-call | flops 66060288 | bytes 2224192 | tf_op jit(solution)/shard_map/pallas_call | solution.py:396
  3.2 3.0 %collective-permute-start.2 = (bf16[48,3712]{1,0:T(8,128)(2,1)}, bf16[48,3712]{1,0:T(8,128)(2,1)S(1)}, u32[]{:S(2)}, u32[]{:S(2)}) collective-permute-start(bf16[48,3712]{1,0:T(8,128)(2,1)} %get-tuple-element.34), channel_id=1, source_target_pairs={{0,2},{2,0},{4,6},{6,4},{8,10},{10,8},{12,14},{14,12},{1,3},{3,1},... | collective-permute-start | bytes 1069064 | tf_op jit(solution)/shard_map/ppermute | solution.py:408
  6.2 1.6 %collective-permute-start = (bf16[24,3712]{1,0:T(8,128)(2,1)}, bf16[24,3712]{1,0:T(8,128)(2,1)S(1)}, u32[]{:S(2)}, u32[]{:S(2)}) collective-permute-start(bf16[24,3712]{1,0:T(8,128)(2,1)} %get-tuple-element.33), channel_id=1, source_target_pairs={{0,4},{2,6},{4,0},{6,2},{8,12},{10,14},{12,8},{14,10},{1,5},{3,7},... | collective-permute-start | bytes 534536 | tf_op jit(solution)/shard_map/ppermute | solution.py:408
  7.8 2.6 %collective-permute-start.1 = (bf16[24,3712]{1,0:T(8,128)(2,1)}, bf16[24,3712]{1,0:T(8,128)(2,1)S(1)}, u32[]{:S(2)}, u32[]{:S(2)}) collective-permute-start(bf16[24,3712]{1,0:T(8,128)(2,1)} %get-tuple-element.33), channel_id=1, source_target_pairs={{0,8},{2,10},{4,12},{6,14},{8,0},{10,2},{12,4},{14,6},{1,9},{3,11}... | collective-permute-start | bytes 534536 | tf_op jit(solution)/shard_map/ppermute | solution.py:408
  10.4 0.0 copy-start
  10.4 1.5 %copy-done = bf16[2,128,3584]{2,1,0:T(8,128)(2,1)S(1)} copy-done((bf16[2,128,3584]{2,1,0:T(8,128)(2,1)S(1)}, bf16[2,128,3584]{2,1,0:T(8,128)(2,1)}, u32[]{:S(2)}) %copy-start) | copy-done | bytes 1835032
  11.9 0.0 copy-start.1
  11.9 0.9 %copy-done.1 = bf16[30,3712]{1,0:T(8,128)(2,1)S(1)} copy-done((bf16[30,3712]{1,0:T(8,128)(2,1)S(1)}, bf16[30,3712]{1,0:T(8,128)(2,1)}, u32[]{:S(2)}) %copy-start.1) | copy-done | bytes 222744
  12.8 0.0 copy-start.2
  12.8 0.9 %copy-done.2 = bf16[18,3712]{1,0:T(8,128)(2,1)S(1)} copy-done((bf16[18,3712]{1,0:T(8,128)(2,1)S(1)}, bf16[18,3712]{1,0:T(8,128)(2,1)}, u32[]{:S(2)}) %copy-start.2) | copy-done | bytes 133656
  13.7 0.0 copy-start.8
  13.7 0.7 %copy-done.8 = s32[8]{0:T(128)S(1)} copy-done((s32[8]{0:T(128)S(1)}, s32[8]{0:T(128)}, u32[]{:S(2)}) %copy-start.8) | copy-done | bytes 56
  14.4 1.2 %shard_map.95 = (bf16[30,3712]{1,0:T(8,128)(2,1)S(1)}, bf16[18,3712]{1,0:T(8,128)(2,1)S(1)}, bf16[256,3584]{1,0:T(8,128)(2,1)S(1)}, s32[30,128]{1,0:T(8,128)S(1)}) custom-call(s32[8]{0:T(128)S(1)} %copy-done.8, bf16[256,3584]{1,0:T(8,128)(2,1)S(1)} %bitcast.8, bf16[30,3712]{1,0:T(8,128)(2,1)S(1)} %copy-done.1, bf16[18,3712]{1,0:T(8,128)(2,1)S(1)} %copy-done.2), custom_call_target="tpu_custom_call" | custom-call | bytes 4398112 | tf_op jit(solution)/shard_map/pallas_call | solution.py:396
  15.6 0.4 collective-permute-done.refs_2_
  16.1 2.5 %collective-permute-done.1.refs_3_ = bf16[24,3712]{1,0:T(8,128)(2,1)S(1)} collective-permute-done((bf16[24,3712]{1,0:T(8,128)(2,1)}, bf16[24,3712]{1,0:T(8,128)(2,1)S(1)}, u32[]{:S(2)}, u32[]{:S(2)}) %collective-permute-start.1) | collective-permute-done | bytes 178208 | tf_op jit(solution)/shard_map/ppermute | solution.py:408
  18.6 0.0 collective-permute-done.2.beside_ref.refs_1_
  18.6 0.3 collective-permute-start.6
  18.9 0.5 %collective-permute-start.3 = (bf16[24,3712]{1,0:T(8,128)(2,1)S(1)}, bf16[24,3712]{1,0:T(8,128)(2,1)S(1)}, u32[]{:S(2)}, u32[]{:S(2)}) collective-permute-start(bf16[24,3712]{1,0:T(8,128)(2,1)S(1)} %collective-permute-done.1.refs_3_), channel_id=1, source_target_pairs={{0,2},{2,0},{4,6},{6,4},{8,10},{10,8},{12,14},{14,12},{1,3},{3,1},... | collective-permute-start | bytes 534536 | tf_op jit(solution)/shard_map/ppermute | solution.py:408
  19.4 1.5 %collective-permute-start.4 = (bf16[24,3712]{1,0:T(8,128)(2,1)S(1)}, bf16[24,3712]{1,0:T(8,128)(2,1)S(1)}, u32[]{:S(2)}, u32[]{:S(2)}) collective-permute-start(bf16[24,3712]{1,0:T(8,128)(2,1)S(1)} %collective-permute-done.refs_2_), channel_id=1, source_target_pairs={{0,2},{2,0},{4,6},{6,4},{8,10},{10,8},{12,14},{14,12},{1,3},{3,1},... | collective-permute-start | bytes 534536 | tf_op jit(solution)/shard_map/ppermute | solution.py:408
  20.9 0.1 shard_map.96
  21.1 2.2 %collective-permute-start.5 = (bf16[24,1920]{1,0:T(8,128)(2,1)S(1)}, bf16[24,1920]{1,0:T(8,128)(2,1)S(1)}, u32[]{:S(2)}, u32[]{:S(2)}) collective-permute-start(bf16[24,1920]{1,0:T(8,128)(2,1)S(1)} %get-tuple-element.48), channel_id=1, source_target_pairs={{0,12},{2,14},{4,8},{6,10},{8,4},{10,6},{12,0},{14,2},{1,13},{3,15... | collective-permute-start | bytes 276488 | tf_op jit(solution)/shard_map/ppermute | solution.py:408
  23.2 2.8 %collective-permute-done.6.refs_0_ = bf16[24,3712]{1,0:T(8,128)(2,1)S(1)} collective-permute-done((bf16[24,3712]{1,0:T(8,128)(2,1)S(1)}, bf16[24,3712]{1,0:T(8,128)(2,1)S(1)}, u32[]{:S(2)}, u32[]{:S(2)}) %collective-permute-start.6) | collective-permute-done | bytes 178208 | tf_op jit(solution)/shard_map/ppermute | solution.py:408
  26.0 0.0 collective-permute-start.7
  26.0 0.4 collective-permute-start.8
  26.5 1.3 %collective-permute-done.5.refs_6_ = bf16[24,1920]{1,0:T(8,128)(2,1)S(1)} collective-permute-done((bf16[24,1920]{1,0:T(8,128)(2,1)S(1)}, bf16[24,1920]{1,0:T(8,128)(2,1)S(1)}, u32[]{:S(2)}, u32[]{:S(2)}) %collective-permute-start.5) | collective-permute-done | bytes 92192 | tf_op jit(solution)/shard_map/ppermute | solution.py:408
  27.8 1.3 %collective-permute-start.9 = (bf16[24,1920]{1,0:T(8,128)(2,1)S(1)}, bf16[24,1920]{1,0:T(8,128)(2,1)S(1)}, u32[]{:S(2)}, u32[]{:S(2)}) collective-permute-start(bf16[24,1920]{1,0:T(8,128)(2,1)S(1)} %get-tuple-element.51), channel_id=1, source_target_pairs={{0,4},{2,6},{4,0},{6,2},{8,12},{10,14},{12,8},{14,10},{1,5},{3,7},... | collective-permute-start | bytes 276488 | tf_op jit(solution)/shard_map/ppermute | solution.py:408
  29.0 0.0 collective-permute-done.3.refs_4_
  29.0 0.3 collective-permute-done.4.refs_5_
  29.3 0.8 %shard_map.97 = (bf16[176,3712]{1,0:T(8,128)(2,1)S(1)}, f32[176,128]{1,0:T(8,128)S(1)}) custom-call(bf16[256,3584]{1,0:T(8,128)(2,1)S(1)} %get-tuple-element.41.w_ref, s32[30,128]{1,0:T(8,128)S(1)} %get-tuple-element.42.slot_ref, bf16[30,3712]{1,0:T(8,128)(2,1)S(1)} %get-tuple-element.43.refs_0_, ...), custom_call_target="tpu_custom_call" | custom-call | flops 322961408 | bytes 4631040 | tf_op jit(solution)/shard_map/pallas_call | solution.py:396
  30.1 1.8 %collective-permute-done.8.refs_2_ = bf16[24,1920]{1,0:T(8,128)(2,1)S(1)} collective-permute-done((bf16[24,1920]{1,0:T(8,128)(2,1)S(1)}, bf16[24,1920]{1,0:T(8,128)(2,1)S(1)}, u32[]{:S(2)}, u32[]{:S(2)}) %collective-permute-start.8) | collective-permute-done | bytes 92192 | tf_op jit(solution)/shard_map/ppermute | solution.py:408
  31.9 0.9 %collective-permute-done.9.refs_3_ = bf16[24,1920]{1,0:T(8,128)(2,1)S(1)} collective-permute-done((bf16[24,1920]{1,0:T(8,128)(2,1)S(1)}, bf16[24,1920]{1,0:T(8,128)(2,1)S(1)}, u32[]{:S(2)}, u32[]{:S(2)}) %collective-permute-start.9) | collective-permute-done | bytes 92192 | tf_op jit(solution)/shard_map/ppermute | solution.py:408
  32.9 0.0 collective-permute-done.7.refs_1_
  32.9 1.3 %shard_map.98 = (bf16[80,3712]{1,0:T(8,128)(2,1)S(1)}, bf16[256,128]{1,0:T(8,128)(2,1)}) custom-call(f32[176,128]{1,0:T(8,128)S(1)} %get-tuple-element.49.own_ref, bf16[256,3584]{1,0:T(8,128)(2,1)S(1)} %get-tuple-element.41.w_ref, s32[30,128]{1,0:T(8,128)S(1)} %get-tuple-element.42.slot_ref, bf16[24,3712]{1,0:T(8,128)(2,1)S(1)} %collective-permute-done.6.refs_0_, ...), custom_call_target="tpu_custom_call" | custom-call | flops 146800640 | bytes 3140608 | tf_op jit(solution)/shard_map/pallas_call | solution.py:396
  34.2 0.4 shard_map.99
  34.7 0.1 collective-permute-start.10
  34.7 3.8 %all-to-all-start = ((bf16[8,32,128]{2,1,0:T(8,128)(2,1)}), bf16[8,32,128]{2,1,0:T(8,128)(2,1)S(1)}, u32[]{:S(2)}, u32[]{:S(2)}) async-start(bf16[8,32,128]{2,1,0:T(8,128)(2,1)} %bitcast.4), calls=%async_computation | async-start | bytes 131072 | tf_op jit(solution)/shard_map/all_to_all | solution.py:487
  38.6 0.0 copy-start.3
  38.6 0.0 copy-start.4
  38.6 0.0 copy-start.5
  38.6 0.0 copy-start.6
  38.6 0.0 copy-start.7
  38.6 0.0 collective-permute-done.10.arrived_ref
  38.6 2.6 %shard_map.100 = bf16[256,1792]{1,0:T(8,128)(2,1)} custom-call(s32[30,128]{1,0:T(8,128)S(1)} %get-tuple-element.42.slot_ref, bf16[176,3712]{1,0:T(8,128)(2,1)S(1)} %get-tuple-element.53.early_ref, bf16[80,3712]{1,0:T(8,128)(2,1)S(1)} %get-tuple-element.54.late_ref, bf16[256,1792]{1,0:T(8,128)(2,1)} %collective-permute-done.10.arrived_ref), custom_call_target="tpu_custom_call" | custom-call | flops 6606028800 | bytes 3750912 | tf_op jit(solution)/shard_map/pallas_call | solution.py:396
  41.2 4.3 %all-to-all-done.back_ref = bf16[8,32,128]{2,1,0:T(8,128)(2,1)S(1)} async-done(((bf16[8,32,128]{2,1,0:T(8,128)(2,1)}), bf16[8,32,128]{2,1,0:T(8,128)(2,1)S(1)}, u32[]{:S(2)}, u32[]{:S(2)}) %all-to-all-start) | async-done | bytes 65568 | tf_op jit(solution)/shard_map/all_to_all | solution.py:487
  45.5 0.0 copy-done.3
  45.5 0.0 copy-done.4
  45.5 0.0 copy-done.5
  45.5 0.0 copy-done.6
  45.5 0.0 copy-done.7
  45.5 1.0 %shard_map.101 = (bf16[1024,128]{1,0:T(8,128)(2,1)}, bf16[8,128]{1,0:T(8,128)(2,1)}) custom-call(bf16[8,32,128]{2,1,0:T(8,128)(2,1)S(1)} %all-to-all-done.back_ref, f32[72,128]{1,0:T(8,128)S(1)} %copy-done.3, s32[72,128]{1,0:T(8,128)S(1)} %copy-done.4, f32[72,128]{1,0:T(8,128)S(1)} %copy-done.5, f32[72,128]{1,0:T(8,128)S(1)} %copy-done.6, s32[8,128]{1,0:T(8,128)S(1)} %bitcast.10), custom_call_target="tpu_custom_call" | custom-call | flops 18874368 | bytes 481280 | tf_op jit(solution)/shard_map/pallas_call | solution.py:396
Async XLA Ops:
  3.2 15.4 %collective-permute-start.2 = (bf16[48,3712]{1,0:T(8,128)(2,1)}, bf16[48,3712]{1,0:T(8,128)(2,1)S(1)}, u32[]{:S(2)}, u32[]{:S(2)}) collective-permute-start(bf16[48,3712]{1,0:T(8,128)(2,1)} %get-tuple-element.34), channel_id=1, source_target_pairs={{0,2},{2,0},{4,6},{6,4},{8,10},{10,8},{12,14},{14,12},{1,3},{3,1},... | collective-permute-start | bytes 1069064 | tf_op jit(solution)/shard_map/ppermute | solution.py:408
  6.2 9.9 %collective-permute-start = (bf16[24,3712]{1,0:T(8,128)(2,1)}, bf16[24,3712]{1,0:T(8,128)(2,1)S(1)}, u32[]{:S(2)}, u32[]{:S(2)}) collective-permute-start(bf16[24,3712]{1,0:T(8,128)(2,1)} %get-tuple-element.33), channel_id=1, source_target_pairs={{0,4},{2,6},{4,0},{6,2},{8,12},{10,14},{12,8},{14,10},{1,5},{3,7},... | collective-permute-start | bytes 534536 | tf_op jit(solution)/shard_map/ppermute | solution.py:408
  7.8 10.8 %collective-permute-start.1 = (bf16[24,3712]{1,0:T(8,128)(2,1)}, bf16[24,3712]{1,0:T(8,128)(2,1)S(1)}, u32[]{:S(2)}, u32[]{:S(2)}) collective-permute-start(bf16[24,3712]{1,0:T(8,128)(2,1)} %get-tuple-element.33), channel_id=1, source_target_pairs={{0,8},{2,10},{4,12},{6,14},{8,0},{10,2},{12,4},{14,6},{1,9},{3,11}... | collective-permute-start | bytes 534536 | tf_op jit(solution)/shard_map/ppermute | solution.py:408
  10.4 1.5 %copy-start = (bf16[2,128,3584]{2,1,0:T(8,128)(2,1)S(1)}, bf16[2,128,3584]{2,1,0:T(8,128)(2,1)}, u32[]{:S(2)}) copy-start(bf16[2,128,3584]{2,1,0:T(8,128)(2,1)} %param.13) | copy-start | bytes 5505028
  11.9 0.9 %copy-start.1 = (bf16[30,3712]{1,0:T(8,128)(2,1)S(1)}, bf16[30,3712]{1,0:T(8,128)(2,1)}, u32[]{:S(2)}) copy-start(bf16[30,3712]{1,0:T(8,128)(2,1)} %get-tuple-element.35.own_hbm) | copy-start | bytes 668164
  12.8 0.9 %copy-start.2 = (bf16[18,3712]{1,0:T(8,128)(2,1)S(1)}, bf16[18,3712]{1,0:T(8,128)(2,1)}, u32[]{:S(2)}) copy-start(bf16[18,3712]{1,0:T(8,128)(2,1)} %get-tuple-element.36.even_hbm) | copy-start | bytes 400900
  13.7 0.7 %copy-start.8 = (s32[8]{0:T(128)S(1)}, s32[8]{0:T(128)}, u32[]{:S(2)}) copy-start(s32[8]{0:T(128)} %replica_ref.1) | copy-start | bytes 100
  18.6 7.4 %collective-permute-start.6 = (bf16[24,3712]{1,0:T(8,128)(2,1)S(1)}, bf16[24,3712]{1,0:T(8,128)(2,1)S(1)}, u32[]{:S(2)}, u32[]{:S(2)}) collective-permute-start(bf16[24,3712]{1,0:T(8,128)(2,1)S(1)} %collective-permute-done.1.refs_3_), channel_id=1, source_target_pairs={{0,4},{2,6},{4,0},{6,2},{8,12},{10,14},{12,8},{14,10},{1,5},{3,7},... | collective-permute-start | bytes 534536 | tf_op jit(solution)/shard_map/ppermute | solution.py:408
  18.9 10.1 %collective-permute-start.3 = (bf16[24,3712]{1,0:T(8,128)(2,1)S(1)}, bf16[24,3712]{1,0:T(8,128)(2,1)S(1)}, u32[]{:S(2)}, u32[]{:S(2)}) collective-permute-start(bf16[24,3712]{1,0:T(8,128)(2,1)S(1)} %collective-permute-done.1.refs_3_), channel_id=1, source_target_pairs={{0,2},{2,0},{4,6},{6,4},{8,10},{10,8},{12,14},{14,12},{1,3},{3,1},... | collective-permute-start | bytes 534536 | tf_op jit(solution)/shard_map/ppermute | solution.py:408
  19.4 9.9 %collective-permute-start.4 = (bf16[24,3712]{1,0:T(8,128)(2,1)S(1)}, bf16[24,3712]{1,0:T(8,128)(2,1)S(1)}, u32[]{:S(2)}, u32[]{:S(2)}) collective-permute-start(bf16[24,3712]{1,0:T(8,128)(2,1)S(1)} %collective-permute-done.refs_2_), channel_id=1, source_target_pairs={{0,2},{2,0},{4,6},{6,4},{8,10},{10,8},{12,14},{14,12},{1,3},{3,1},... | collective-permute-start | bytes 534536 | tf_op jit(solution)/shard_map/ppermute | solution.py:408
  21.1 6.7 %collective-permute-start.5 = (bf16[24,1920]{1,0:T(8,128)(2,1)S(1)}, bf16[24,1920]{1,0:T(8,128)(2,1)S(1)}, u32[]{:S(2)}, u32[]{:S(2)}) collective-permute-start(bf16[24,1920]{1,0:T(8,128)(2,1)S(1)} %get-tuple-element.48), channel_id=1, source_target_pairs={{0,12},{2,14},{4,8},{6,10},{8,4},{10,6},{12,0},{14,2},{1,13},{3,15... | collective-permute-start | bytes 276488 | tf_op jit(solution)/shard_map/ppermute | solution.py:408
  26.0 6.8 %collective-permute-start.7 = (bf16[24,3712]{1,0:T(8,128)(2,1)S(1)}, bf16[24,3712]{1,0:T(8,128)(2,1)S(1)}, u32[]{:S(2)}, u32[]{:S(2)}) collective-permute-start(bf16[24,3712]{1,0:T(8,128)(2,1)S(1)} %collective-permute-done.6.refs_0_), channel_id=1, source_target_pairs={{0,2},{2,0},{4,6},{6,4},{8,10},{10,8},{12,14},{14,12},{1,3},{3,1},... | collective-permute-start | bytes 534536 | tf_op jit(solution)/shard_map/ppermute | solution.py:408
  26.0 5.9 %collective-permute-start.8 = (bf16[24,1920]{1,0:T(8,128)(2,1)S(1)}, bf16[24,1920]{1,0:T(8,128)(2,1)S(1)}, u32[]{:S(2)}, u32[]{:S(2)}) collective-permute-start(bf16[24,1920]{1,0:T(8,128)(2,1)S(1)} %get-tuple-element.50), channel_id=1, source_target_pairs={{0,8},{2,10},{4,12},{6,14},{8,0},{10,2},{12,4},{14,6},{1,9},{3,11}... | collective-permute-start | bytes 276488 | tf_op jit(solution)/shard_map/ppermute | solution.py:408
  27.8 5.1 %collective-permute-start.9 = (bf16[24,1920]{1,0:T(8,128)(2,1)S(1)}, bf16[24,1920]{1,0:T(8,128)(2,1)S(1)}, u32[]{:S(2)}, u32[]{:S(2)}) collective-permute-start(bf16[24,1920]{1,0:T(8,128)(2,1)S(1)} %get-tuple-element.51), channel_id=1, source_target_pairs={{0,4},{2,6},{4,0},{6,2},{8,12},{10,14},{12,8},{14,10},{1,5},{3,7},... | collective-permute-start | bytes 276488 | tf_op jit(solution)/shard_map/ppermute | solution.py:408
  34.7 4.0 %collective-permute-start.10 = (bf16[256,1792]{1,0:T(8,128)(2,1)S(1)}, bf16[256,1792]{1,0:T(8,128)(2,1)}, u32[]{:S(2)}, u32[]{:S(2)}) collective-permute-start(bf16[256,1792]{1,0:T(8,128)(2,1)S(1)} %shard_map.99), channel_id=1, source_target_pairs={{0,1},{1,0},{2,3},{3,2},{4,5},{5,4},{6,7},{7,6},{8,9},{9,8},{10,11... | collective-permute-start | bytes 2752520 | tf_op jit(solution)/shard_map/ppermute | solution.py:496
  34.7 10.7 %all-to-all-start = ((bf16[8,32,128]{2,1,0:T(8,128)(2,1)}), bf16[8,32,128]{2,1,0:T(8,128)(2,1)S(1)}, u32[]{:S(2)}, u32[]{:S(2)}) async-start(bf16[8,32,128]{2,1,0:T(8,128)(2,1)} %bitcast.4), calls=%async_computation | async-start | bytes 131072 | tf_op jit(solution)/shard_map/all_to_all | solution.py:487
  38.6 6.9 %copy-start.3 = (f32[72,128]{1,0:T(8,128)S(1)}, f32[72,128]{1,0:T(8,128)}, u32[]{:S(2)}) copy-start(f32[72,128]{1,0:T(8,128)} %get-tuple-element.56.pick_ref) | copy-start | bytes 110596
  38.6 6.9 %copy-start.4 = (s32[72,128]{1,0:T(8,128)S(1)}, s32[72,128]{1,0:T(8,128)}, u32[]{:S(2)}) copy-start(s32[72,128]{1,0:T(8,128)} %get-tuple-element.57.expert_ref) | copy-start | bytes 110596
  38.6 6.9 %copy-start.5 = (f32[72,128]{1,0:T(8,128)S(1)}, f32[72,128]{1,0:T(8,128)}, u32[]{:S(2)}) copy-start(f32[72,128]{1,0:T(8,128)} %get-tuple-element.58.hs_ref) | copy-start | bytes 110596
  38.6 6.9 %copy-start.6 = (f32[72,128]{1,0:T(8,128)S(1)}, f32[72,128]{1,0:T(8,128)}, u32[]{:S(2)}) copy-start(f32[72,128]{1,0:T(8,128)} %get-tuple-element.59.ps_ref) | copy-start | bytes 110596
  38.6 6.9 %copy-start.7 = (s32[128,8]{0,1:T(8,128)S(1)}, s32[128,8]{0,1:T(8,128)}, u32[]{:S(2)}) copy-start(s32[128,8]{0,1:T(8,128)} %param.10) | copy-start | bytes 12292

commit v16 on v15

--- a/solution.py
+++ b/solution.py
@@ -307,7 +307,7 @@
 
 def turn_kernel(local_count, dev_count, beside_ref, even_ref, *line_refs):
     per_home, per_copy = local_count * SLOT, dev_count * CAPR
-    beside = beside_ref[...].astype(F32)[per_copy + per_home:]
+    beside = beside_ref[...].astype(F32)[per_home:]
     even = even_ref[...].astype(F32)
     for n, line_ref in enumerate(line_refs):
         span = slice(n * per_home, (n + 1) * per_home)
@@ -426,7 +426,7 @@
     sources = (replica_of, send_counts, ids, probs.T, hidden.reshape(toks * top, width), cotangent)
     per_home = local_count * SLOT
     odd, even = range(1, dev_count, 2), range(2, dev_count, 2)
-    packing = [[COPIES, *odd], [COPIES], [0, COPIES], [*even]]
+    packing = [[*odd], [COPIES], [0, COPIES], [*even]]
     sized = [sum(copies if b == COPIES else per_home for b in blocks) for blocks in packing]
     pick, expert, h_slot, p_slot, to_beside, copy_rows, own_rows, even_rows = call(
         functools.partial(dispatch_kernel, *sizes, packing),
@@ -438,9 +438,8 @@
         flops=2 * slots * toks * d_model,
         limit=60,
     )
-    beside = swap(to_beside, 1, dev_count)
-    near = swap(copy_rows, 2, dev_count)
-    far = swap(copy_rows, 4, dev_count)
+    near, far, beside = (swap(copy_rows, bits, dev_count) for bits in (2, 4, 1))
+    line = swap(to_beside, 1, dev_count)
     flat_w = weights.reshape(local_count * width, d_model)
     own_rows, even_rows, w_held, slot = call(
         functools.partial(hold_kernel, *sizes),
@@ -448,17 +447,17 @@
         [(smem, replica_of)] + [(hbm, a) for a in (flat_w, own_rows, even_rows)],
         [pltpu.SemaphoreType.DMA((3,))],
     )
-    near, far, beside, own_rows, even_rows, w_held, slot = lax.optimization_barrier(
-        (near, far, beside, own_rows, even_rows, w_held, slot))
+    near, far, line, beside, own_rows, even_rows, w_held, slot = lax.optimization_barrier(
+        (near, far, line, beside, own_rows, even_rows, w_held, slot))
     far_near = swap(far, 2, dev_count)
     lines = call(
         functools.partial(turn_kernel, *sizes),
         [shape((4 * per_home, fold_width(d_model + width)), BF16)] * len(even),
-        [(vmem, a) for a in (beside, even_rows)],
+        [(vmem, a) for a in (line, even_rows)],
     )
     far_beside, near_beside = swap(far, 1, dev_count), swap(near, 1, dev_count)
     lines = [swap(a, m, dev_count) for a, m in zip(lines, even)]
-    pieces = {(0, HOME): (0, 0), (0, COPIES): (0, per_home), (1, COPIES): (1, 0), (1, HOME): (1, copies),
+    pieces = {(0, HOME): (0, 0), (0, COPIES): (0, per_home), (1, COPIES): (1, 0), (1, HOME): (7, 0),
               (2, COPIES): (2, 0), (4, COPIES): (3, 0), (5, COPIES): (4, 0), (3, COPIES): (5, 0),
               (even[-1], HOME): (6, 0), (even[-1] + 1, HOME): (6, per_home)}
     orders = [list(pieces)]
@@ -466,13 +465,13 @@
     early_rows, own = call(
         functools.partial(early_kernel, *sizes, orders[0], pieces),
         (shape((height, d_model + width), BF16), shape((height, width), F32)),
-        [(vmem, a) for a in (w_held, slot, own_rows, beside, near, far, far_beside, near_beside, lines[-1])],
+        [(vmem, a) for a in (w_held, slot, own_rows, beside, near, far, far_beside, near_beside, lines[-1], line)],
         flops=2 * height * d_model * local_count * width,
     )
     far_across = swap(far_near, 1, dev_count)
-    arrays = [far_near, far_across, *lines[-2::-1]]
+    arrays = [far_near, far_across, *lines[:-1]]
     pieces = {(6, COPIES): (0, 0), (7, COPIES): (1, 0)}
-    for n, m in enumerate(even[-2::-1]):
+    for n, m in enumerate(even[:-1]):
         pieces[m, HOME], pieces[m + 1, HOME] = ((2 + n, k * per_home) for k in range(2))
     orders.append(list(pieces))
     height = padded(sum(per_home if kind == HOME else copies for _, kind in pieces))

time: 46.8 us -> 46.8 us (level)
  starting transfers between devices: 17.3 us -> 18.1 us
  waiting for transfers between devices: 14.3 us -> 13.5 us
    ppermute x10 -> x11, starting transfers between devices: 13.4 us -> 14.7 us  [swap(): return lax.ppermute(x, 'expert', [(i, i ^ bits) for i in range(count)])]
    ppermute x10 -> x11, waiting for transfers between devices: 10.1 us -> 9.25 us  [swap(): return lax.ppermute(x, 'expert', [(i, i ^ bits) for i in range(count)])]
  transfers between devices with their start and end apart: 12 -> 13, of which waited for: 8 -> 7; matrix products, arithmetic and copies ran while one was open for 0% -> 0% of each run, Pallas kernels for 10% -> 10%
where the time goes in v16:
time: 46.8 us; the launch traced here: 46.4 us
  starting transfers between devices  18.1 us (39%)
  waiting for transfers between devices  13.5 us (29%)
  Pallas kernels  10 us (21%)
  local copies, waits for them, and re-layouts  4.04 us (9%)
  between operations  0.77 us (2%)
    ppermute x11, starting transfers between devices, swap(): return lax.ppermute(x, 'expert', [(i, i ^ bits) for i in range(count)])  14.7 us
    pallas_call x8, Pallas kernels, call(): pl.pallas_call(kernel, out_shape=out_shape, in_specs=[pl.BlockSpec(memory...  10 us
    ppermute x11, waiting for transfers between devices, swap(): return lax.ppermute(x, 'expert', [(i, i ^ bits) for i in range(count)])  9.25 us
    all_to_all x1, waiting for transfers between devices, gather_body(): lax.all_to_all(back, 'expert', split_axis=0, concat_axis=0, tiled=True)  4.24 us
    unnamed x18, local copies, waits for them, and re-layouts  4.04 us
    all_to_all x1, starting transfers between devices, gather_body(): lax.all_to_all(back, 'expert', split_axis=0, concat_axis=0, tiled=True)  3.36 us
  transfers between devices with their start and end apart: 13, of which 7 were waited for; matrix products, arithmetic and copies ran while one was open for 0% of the time, Pallas kernels for 10%

profile of v16, /device:TPU:0, one launch (start us, length us, event | category | flops | bytes accessed | tf_op | source)
XLA Modules:
  0.0 46.4 jit_solution(445516680837166763)
XLA Ops:
  0.6 2.5 %shard_map.94 = (f32[72,128]{1,0:T(8,128)}, s32[72,128]{1,0:T(8,128)}, f32[72,128]{1,0:T(8,128)}, f32[72,128]{1,0:T(8,128)}, bf16[24,3712]{1,0:T(8,128)(2,1)}, /...) custom-call(s32[8]{0:T(128)} %replica_ref.1, s32[1,8]{1,0:T(1,128)} %refs_1_.1, ...), custom_call_target="tpu_custom_call" | custom-call | flops 66060288 | bytes 2046016 | tf_op jit(solution)/shard_map/pallas_call | solution.py:396
  3.2 3.1 %collective-permute-start = (bf16[24,3712]{1,0:T(8,128)(2,1)}, bf16[24,3712]{1,0:T(8,128)(2,1)S(1)}, u32[]{:S(2)}, u32[]{:S(2)}) collective-permute-start(bf16[24,3712]{1,0:T(8,128)(2,1)} %get-tuple-element.34), channel_id=1, source_target_pairs={{0,4},{2,6},{4,0},{6,2},{8,12},{10,14},{12,8},{14,10},{1,5},{3,7},... | collective-permute-start | bytes 534536 | tf_op jit(solution)/shard_map/ppermute | solution.py:408
  6.2 2.6 %collective-permute-start.1 = (bf16[24,3712]{1,0:T(8,128)(2,1)}, bf16[24,3712]{1,0:T(8,128)(2,1)S(1)}, u32[]{:S(2)}, u32[]{:S(2)}) collective-permute-start(bf16[24,3712]{1,0:T(8,128)(2,1)} %get-tuple-element.34), channel_id=1, source_target_pairs={{0,8},{2,10},{4,12},{6,14},{8,0},{10,2},{12,4},{14,6},{1,9},{3,11}... | collective-permute-start | bytes 534536 | tf_op jit(solution)/shard_map/ppermute | solution.py:408
  8.8 1.5 %collective-permute-start.3 = (bf16[24,3712]{1,0:T(8,128)(2,1)}, bf16[24,3712]{1,0:T(8,128)(2,1)S(1)}, u32[]{:S(2)}, u32[]{:S(2)}) collective-permute-start(bf16[24,3712]{1,0:T(8,128)(2,1)} %get-tuple-element.34), channel_id=1, source_target_pairs={{0,2},{2,0},{4,6},{6,4},{8,10},{10,8},{12,14},{14,12},{1,3},{3,1},... | collective-permute-start | bytes 534536 | tf_op jit(solution)/shard_map/ppermute | solution.py:408
  10.3 0.5 %collective-permute-start.2 = (bf16[24,3712]{1,0:T(8,128)(2,1)}, bf16[24,3712]{1,0:T(8,128)(2,1)S(1)}, u32[]{:S(2)}, u32[]{:S(2)}) collective-permute-start(bf16[24,3712]{1,0:T(8,128)(2,1)} %get-tuple-element.35), channel_id=1, source_target_pairs={{0,2},{2,0},{4,6},{6,4},{8,10},{10,8},{12,14},{14,12},{1,3},{3,1},... | collective-permute-start | bytes 534536 | tf_op jit(solution)/shard_map/ppermute | solution.py:408
  10.9 0.0 copy-start
  10.9 1.5 %copy-done = bf16[2,128,3584]{2,1,0:T(8,128)(2,1)S(1)} copy-done((bf16[2,128,3584]{2,1,0:T(8,128)(2,1)S(1)}, bf16[2,128,3584]{2,1,0:T(8,128)(2,1)}, u32[]{:S(2)}) %copy-start) | copy-done | bytes 1835032
  12.4 0.0 copy-start.1
  12.4 0.9 %copy-done.1 = bf16[30,3712]{1,0:T(8,128)(2,1)S(1)} copy-done((bf16[30,3712]{1,0:T(8,128)(2,1)S(1)}, bf16[30,3712]{1,0:T(8,128)(2,1)}, u32[]{:S(2)}) %copy-start.1) | copy-done | bytes 222744
  13.3 0.0 copy-start.2
  13.3 0.9 %copy-done.2 = bf16[18,3712]{1,0:T(8,128)(2,1)S(1)} copy-done((bf16[18,3712]{1,0:T(8,128)(2,1)S(1)}, bf16[18,3712]{1,0:T(8,128)(2,1)}, u32[]{:S(2)}) %copy-start.2) | copy-done | bytes 133656
  14.2 0.0 copy-start.8
  14.2 0.7 %copy-done.8 = s32[8]{0:T(128)S(1)} copy-done((s32[8]{0:T(128)S(1)}, s32[8]{0:T(128)}, u32[]{:S(2)}) %copy-start.8) | copy-done | bytes 56
  14.9 1.2 %shard_map.95 = (bf16[30,3712]{1,0:T(8,128)(2,1)S(1)}, bf16[18,3712]{1,0:T(8,128)(2,1)S(1)}, bf16[256,3584]{1,0:T(8,128)(2,1)S(1)}, s32[30,128]{1,0:T(8,128)S(1)}) custom-call(s32[8]{0:T(128)S(1)} %copy-done.8, bf16[256,3584]{1,0:T(8,128)(2,1)S(1)} %bitcast.8, bf16[30,3712]{1,0:T(8,128)(2,1)S(1)} %copy-done.1, bf16[18,3712]{1,0:T(8,128)(2,1)S(1)} %copy-done.2), custom_call_target="tpu_custom_call" | custom-call | bytes 4398112 | tf_op jit(solution)/shard_map/pallas_call | solution.py:396
  16.1 0.0 collective-permute-done.refs_2_
  16.1 1.1 %collective-permute-done.1.refs_3_ = bf16[24,3712]{1,0:T(8,128)(2,1)S(1)} collective-permute-done((bf16[24,3712]{1,0:T(8,128)(2,1)}, bf16[24,3712]{1,0:T(8,128)(2,1)S(1)}, u32[]{:S(2)}, u32[]{:S(2)}) %collective-permute-start.1) | collective-permute-done | bytes 178208 | tf_op jit(solution)/shard_map/ppermute | solution.py:408
  17.2 0.0 collective-permute-done.3.refs_1_
  17.2 1.3 %collective-permute-done.2.beside_ref.refs_7_ = bf16[24,3712]{1,0:T(8,128)(2,1)S(1)} collective-permute-done((bf16[24,3712]{1,0:T(8,128)(2,1)}, bf16[24,3712]{1,0:T(8,128)(2,1)S(1)}, u32[]{:S(2)}, u32[]{:S(2)}) %collective-permute-start.2) | collective-permute-done | bytes 178208 | tf_op jit(solution)/shard_map/ppermute | solution.py:408
  18.5 0.4 collective-permute-start.7
  19.0 1.5 %collective-permute-start.4 = (bf16[24,3712]{1,0:T(8,128)(2,1)S(1)}, bf16[24,3712]{1,0:T(8,128)(2,1)S(1)}, u32[]{:S(2)}, u32[]{:S(2)}) collective-permute-start(bf16[24,3712]{1,0:T(8,128)(2,1)S(1)} %collective-permute-done.1.refs_3_), channel_id=1, source_target_pairs={{0,2},{2,0},{4,6},{6,4},{8,10},{10,8},{12,14},{14,12},{1,3},{3,1},... | collective-permute-start | bytes 534536 | tf_op jit(solution)/shard_map/ppermute | solution.py:408
  20.5 0.5 %collective-permute-start.5 = (bf16[24,3712]{1,0:T(8,128)(2,1)S(1)}, bf16[24,3712]{1,0:T(8,128)(2,1)S(1)}, u32[]{:S(2)}, u32[]{:S(2)}) collective-permute-start(bf16[24,3712]{1,0:T(8,128)(2,1)S(1)} %collective-permute-done.refs_2_), channel_id=1, source_target_pairs={{0,2},{2,0},{4,6},{6,4},{8,10},{10,8},{12,14},{14,12},{1,3},{3,1},... | collective-permute-start | bytes 534536 | tf_op jit(solution)/shard_map/ppermute | solution.py:408
  21.0 0.1 shard_map.96
  21.1 1.4 %collective-permute-start.6 = (bf16[24,1920]{1,0:T(8,128)(2,1)S(1)}, bf16[24,1920]{1,0:T(8,128)(2,1)S(1)}, u32[]{:S(2)}, u32[]{:S(2)}) collective-permute-start(bf16[24,1920]{1,0:T(8,128)(2,1)S(1)} %get-tuple-element.50), channel_id=1, source_target_pairs={{0,12},{2,14},{4,8},{6,10},{8,4},{10,6},{12,0},{14,2},{1,13},{3,15... | collective-permute-start | bytes 276488 | tf_op jit(solution)/shard_map/ppermute | solution.py:408
  22.6 2.4 %collective-permute-done.7.refs_0_ = bf16[24,3712]{1,0:T(8,128)(2,1)S(1)} collective-permute-done((bf16[24,3712]{1,0:T(8,128)(2,1)S(1)}, bf16[24,3712]{1,0:T(8,128)(2,1)S(1)}, u32[]{:S(2)}, u32[]{:S(2)}) %collective-permute-start.7) | collective-permute-done | bytes 178208 | tf_op jit(solution)/shard_map/ppermute | solution.py:408
  25.0 1.5 %collective-permute-start.8 = (bf16[24,3712]{1,0:T(8,128)(2,1)S(1)}, bf16[24,3712]{1,0:T(8,128)(2,1)S(1)}, u32[]{:S(2)}, u32[]{:S(2)}) collective-permute-start(bf16[24,3712]{1,0:T(8,128)(2,1)S(1)} %collective-permute-done.7.refs_0_), channel_id=1, source_target_pairs={{0,2},{2,0},{4,6},{6,4},{8,10},{10,8},{12,14},{14,12},{1,3},{3,1},... | collective-permute-start | bytes 534536 | tf_op jit(solution)/shard_map/ppermute | solution.py:408
  26.5 0.0 collective-permute-start.10
  26.5 2.1 %collective-permute-done.6.refs_6_ = bf16[24,1920]{1,0:T(8,128)(2,1)S(1)} collective-permute-done((bf16[24,1920]{1,0:T(8,128)(2,1)S(1)}, bf16[24,1920]{1,0:T(8,128)(2,1)S(1)}, u32[]{:S(2)}, u32[]{:S(2)}) %collective-permute-start.6) | collective-permute-done | bytes 92192 | tf_op jit(solution)/shard_map/ppermute | solution.py:408
  28.6 1.6 %collective-permute-start.9 = (bf16[24,1920]{1,0:T(8,128)(2,1)S(1)}, bf16[24,1920]{1,0:T(8,128)(2,1)S(1)}, u32[]{:S(2)}, u32[]{:S(2)}) collective-permute-start(bf16[24,1920]{1,0:T(8,128)(2,1)S(1)} %get-tuple-element.52), channel_id=1, source_target_pairs={{0,4},{2,6},{4,0},{6,2},{8,12},{10,14},{12,8},{14,10},{1,5},{3,7},... | collective-permute-start | bytes 276488 | tf_op jit(solution)/shard_map/ppermute | solution.py:408
  30.2 0.0 collective-permute-done.4.refs_4_
  30.2 0.0 collective-permute-done.5.refs_5_
  30.2 0.8 %shard_map.97 = (bf16[176,3712]{1,0:T(8,128)(2,1)S(1)}, f32[176,128]{1,0:T(8,128)S(1)}) custom-call(bf16[256,3584]{1,0:T(8,128)(2,1)S(1)} %get-tuple-element.42.w_ref, s32[30,128]{1,0:T(8,128)S(1)} %get-tuple-element.43.slot_ref, bf16[30,3712]{1,0:T(8,128)(2,1)S(1)} %get-tuple-element.44.refs_0_, bf16[24,3712]{1,0:T(8,128)(2,1)S(1)} %collective-permute-done.3.refs_1_, ...), custom_call_target="tpu_custom_call" | custom-call | flops 322961408 | bytes 4631040 | tf_op jit(solution)/shard_map/pallas_call | solution.py:396
  31.0 2.1 %collective-permute-done.10.refs_3_ = bf16[24,1920]{1,0:T(8,128)(2,1)S(1)} collective-permute-done((bf16[24,1920]{1,0:T(8,128)(2,1)S(1)}, bf16[24,1920]{1,0:T(8,128)(2,1)S(1)}, u32[]{:S(2)}, u32[]{:S(2)}) %collective-permute-start.10) | collective-permute-done | bytes 92192 | tf_op jit(solution)/shard_map/ppermute | solution.py:408
  33.0 0.2 collective-permute-done.9.refs_2_
  33.3 0.0 collective-permute-done.8.refs_1_
  33.3 1.3 %shard_map.98 = (bf16[80,3712]{1,0:T(8,128)(2,1)S(1)}, bf16[256,128]{1,0:T(8,128)(2,1)}) custom-call(f32[176,128]{1,0:T(8,128)S(1)} %get-tuple-element.51.own_ref, bf16[256,3584]{1,0:T(8,128)(2,1)S(1)} %get-tuple-element.42.w_ref, s32[30,128]{1,0:T(8,128)S(1)} %get-tuple-element.43.slot_ref, bf16[24,3712]{1,0:T(8,128)(2,1)S(1)} %collective-permute-done.7.refs_0_, ...), custom_call_target="tpu_custom_call" | custom-call | flops 146800640 | bytes 3140608 | tf_op jit(solution)/shard_map/pallas_call | solution.py:396
  34.6 0.4 shard_map.99
  35.1 0.1 collective-permute-start.11
  35.2 3.4 %all-to-all-start = ((bf16[8,32,128]{2,1,0:T(8,128)(2,1)}), bf16[8,32,128]{2,1,0:T(8,128)(2,1)S(1)}, u32[]{:S(2)}, u32[]{:S(2)}) async-start(bf16[8,32,128]{2,1,0:T(8,128)(2,1)} %bitcast.4), calls=%async_computation | async-start | bytes 131072 | tf_op jit(solution)/shard_map/all_to_all | solution.py:486
  38.5 0.0 copy-start.3
  38.5 0.0 copy-start.4
  38.5 0.0 copy-start.5
  38.6 0.0 copy-start.6
  38.6 0.0 copy-start.7
  38.6 0.0 collective-permute-done.11.arrived_ref
  38.6 2.6 %shard_map.100 = bf16[256,1792]{1,0:T(8,128)(2,1)} custom-call(s32[30,128]{1,0:T(8,128)S(1)} %get-tuple-element.43.slot_ref, bf16[176,3712]{1,0:T(8,128)(2,1)S(1)} %get-tuple-element.55.early_ref, bf16[80,3712]{1,0:T(8,128)(2,1)S(1)} %get-tuple-element.56.late_ref, bf16[256,1792]{1,0:T(8,128)(2,1)} %collective-permute-done.11.arrived_ref), custom_call_target="tpu_custom_call" | custom-call | flops 6606028800 | bytes 3750912 | tf_op jit(solution)/shard_map/pallas_call | solution.py:396
  41.2 4.2 %all-to-all-done.back_ref = bf16[8,32,128]{2,1,0:T(8,128)(2,1)S(1)} async-done(((bf16[8,32,128]{2,1,0:T(8,128)(2,1)}), bf16[8,32,128]{2,1,0:T(8,128)(2,1)S(1)}, u32[]{:S(2)}, u32[]{:S(2)}) %all-to-all-start) | async-done | bytes 65568 | tf_op jit(solution)/shard_map/all_to_all | solution.py:486
  45.4 0.0 copy-done.3
  45.4 0.0 copy-done.4
  45.4 0.0 copy-done.5
  45.4 0.0 copy-done.6
  45.4 0.0 copy-done.7
  45.4 1.0 %shard_map.101 = (bf16[1024,128]{1,0:T(8,128)(2,1)}, bf16[8,128]{1,0:T(8,128)(2,1)}) custom-call(bf16[8,32,128]{2,1,0:T(8,128)(2,1)S(1)} %all-to-all-done.back_ref, f32[72,128]{1,0:T(8,128)S(1)} %copy-done.3, s32[72,128]{1,0:T(8,128)S(1)} %copy-done.4, f32[72,128]{1,0:T(8,128)S(1)} %copy-done.5, f32[72,128]{1,0:T(8,128)S(1)} %copy-done.6, s32[8,128]{1,0:T(8,128)S(1)} %bitcast.10), custom_call_target="tpu_custom_call" | custom-call | flops 18874368 | bytes 481280 | tf_op jit(solution)/shard_map/pallas_call | solution.py:396
Async XLA Ops:
  3.2 13.0 %collective-permute-start = (bf16[24,3712]{1,0:T(8,128)(2,1)}, bf16[24,3712]{1,0:T(8,128)(2,1)S(1)}, u32[]{:S(2)}, u32[]{:S(2)}) collective-permute-start(bf16[24,3712]{1,0:T(8,128)(2,1)} %get-tuple-element.34), channel_id=1, source_target_pairs={{0,4},{2,6},{4,0},{6,2},{8,12},{10,14},{12,8},{14,10},{1,5},{3,7},... | collective-permute-start | bytes 534536 | tf_op jit(solution)/shard_map/ppermute | solution.py:408
  6.2 11.0 %collective-permute-start.1 = (bf16[24,3712]{1,0:T(8,128)(2,1)}, bf16[24,3712]{1,0:T(8,128)(2,1)S(1)}, u32[]{:S(2)}, u32[]{:S(2)}) collective-permute-start(bf16[24,3712]{1,0:T(8,128)(2,1)} %get-tuple-element.34), channel_id=1, source_target_pairs={{0,8},{2,10},{4,12},{6,14},{8,0},{10,2},{12,4},{14,6},{1,9},{3,11}... | collective-permute-start | bytes 534536 | tf_op jit(solution)/shard_map/ppermute | solution.py:408
  8.8 8.4 %collective-permute-start.3 = (bf16[24,3712]{1,0:T(8,128)(2,1)}, bf16[24,3712]{1,0:T(8,128)(2,1)S(1)}, u32[]{:S(2)}, u32[]{:S(2)}) collective-permute-start(bf16[24,3712]{1,0:T(8,128)(2,1)} %get-tuple-element.34), channel_id=1, source_target_pairs={{0,2},{2,0},{4,6},{6,4},{8,10},{10,8},{12,14},{14,12},{1,3},{3,1},... | collective-permute-start | bytes 534536 | tf_op jit(solution)/shard_map/ppermute | solution.py:408
  10.3 8.2 %collective-permute-start.2 = (bf16[24,3712]{1,0:T(8,128)(2,1)}, bf16[24,3712]{1,0:T(8,128)(2,1)S(1)}, u32[]{:S(2)}, u32[]{:S(2)}) collective-permute-start(bf16[24,3712]{1,0:T(8,128)(2,1)} %get-tuple-element.35), channel_id=1, source_target_pairs={{0,2},{2,0},{4,6},{6,4},{8,10},{10,8},{12,14},{14,12},{1,3},{3,1},... | collective-permute-start | bytes 534536 | tf_op jit(solution)/shard_map/ppermute | solution.py:408
  10.9 1.5 %copy-start = (bf16[2,128,3584]{2,1,0:T(8,128)(2,1)S(1)}, bf16[2,128,3584]{2,1,0:T(8,128)(2,1)}, u32[]{:S(2)}) copy-start(bf16[2,128,3584]{2,1,0:T(8,128)(2,1)} %param.13) | copy-start | bytes 5505028
  12.4 0.9 %copy-start.1 = (bf16[30,3712]{1,0:T(8,128)(2,1)S(1)}, bf16[30,3712]{1,0:T(8,128)(2,1)}, u32[]{:S(2)}) copy-start(bf16[30,3712]{1,0:T(8,128)(2,1)} %get-tuple-element.36.own_hbm) | copy-start | bytes 668164
  13.3 0.9 %copy-start.2 = (bf16[18,3712]{1,0:T(8,128)(2,1)S(1)}, bf16[18,3712]{1,0:T(8,128)(2,1)}, u32[]{:S(2)}) copy-start(bf16[18,3712]{1,0:T(8,128)(2,1)} %get-tuple-element.37.even_hbm) | copy-start | bytes 400900
  14.2 0.7 %copy-start.8 = (s32[8]{0:T(128)S(1)}, s32[8]{0:T(128)}, u32[]{:S(2)}) copy-start(s32[8]{0:T(128)} %replica_ref.1) | copy-start | bytes 100
  18.5 6.5 %collective-permute-start.7 = (bf16[24,3712]{1,0:T(8,128)(2,1)S(1)}, bf16[24,3712]{1,0:T(8,128)(2,1)S(1)}, u32[]{:S(2)}, u32[]{:S(2)}) collective-permute-start(bf16[24,3712]{1,0:T(8,128)(2,1)S(1)} %collective-permute-done.1.refs_3_), channel_id=1, source_target_pairs={{0,4},{2,6},{4,0},{6,2},{8,12},{10,14},{12,8},{14,10},{1,5},{3,7},... | collective-permute-start | bytes 534536 | tf_op jit(solution)/shard_map/ppermute | solution.py:408
  19.0 11.2 %collective-permute-start.4 = (bf16[24,3712]{1,0:T(8,128)(2,1)S(1)}, bf16[24,3712]{1,0:T(8,128)(2,1)S(1)}, u32[]{:S(2)}, u32[]{:S(2)}) collective-permute-start(bf16[24,3712]{1,0:T(8,128)(2,1)S(1)} %collective-permute-done.1.refs_3_), channel_id=1, source_target_pairs={{0,2},{2,0},{4,6},{6,4},{8,10},{10,8},{12,14},{14,12},{1,3},{3,1},... | collective-permute-start | bytes 534536 | tf_op jit(solution)/shard_map/ppermute | solution.py:408
  20.5 9.7 %collective-permute-start.5 = (bf16[24,3712]{1,0:T(8,128)(2,1)S(1)}, bf16[24,3712]{1,0:T(8,128)(2,1)S(1)}, u32[]{:S(2)}, u32[]{:S(2)}) collective-permute-start(bf16[24,3712]{1,0:T(8,128)(2,1)S(1)} %collective-permute-done.refs_2_), channel_id=1, source_target_pairs={{0,2},{2,0},{4,6},{6,4},{8,10},{10,8},{12,14},{14,12},{1,3},{3,1},... | collective-permute-start | bytes 534536 | tf_op jit(solution)/shard_map/ppermute | solution.py:408
  21.1 7.4 %collective-permute-start.6 = (bf16[24,1920]{1,0:T(8,128)(2,1)S(1)}, bf16[24,1920]{1,0:T(8,128)(2,1)S(1)}, u32[]{:S(2)}, u32[]{:S(2)}) collective-permute-start(bf16[24,1920]{1,0:T(8,128)(2,1)S(1)} %get-tuple-element.50), channel_id=1, source_target_pairs={{0,12},{2,14},{4,8},{6,10},{8,4},{10,6},{12,0},{14,2},{1,13},{3,15... | collective-permute-start | bytes 276488 | tf_op jit(solution)/shard_map/ppermute | solution.py:408
  25.0 8.3 %collective-permute-start.8 = (bf16[24,3712]{1,0:T(8,128)(2,1)S(1)}, bf16[24,3712]{1,0:T(8,128)(2,1)S(1)}, u32[]{:S(2)}, u32[]{:S(2)}) collective-permute-start(bf16[24,3712]{1,0:T(8,128)(2,1)S(1)} %collective-permute-done.7.refs_0_), channel_id=1, source_target_pairs={{0,2},{2,0},{4,6},{6,4},{8,10},{10,8},{12,14},{14,12},{1,3},{3,1},... | collective-permute-start | bytes 534536 | tf_op jit(solution)/shard_map/ppermute | solution.py:408
  26.5 6.5 %collective-permute-start.10 = (bf16[24,1920]{1,0:T(8,128)(2,1)S(1)}, bf16[24,1920]{1,0:T(8,128)(2,1)S(1)}, u32[]{:S(2)}, u32[]{:S(2)}) collective-permute-start(bf16[24,1920]{1,0:T(8,128)(2,1)S(1)} %get-tuple-element.53), channel_id=1, source_target_pairs={{0,8},{2,10},{4,12},{6,14},{8,0},{10,2},{12,4},{14,6},{1,9},{3,11}... | collective-permute-start | bytes 276488 | tf_op jit(solution)/shard_map/ppermute | solution.py:408
  28.6 4.7 %collective-permute-start.9 = (bf16[24,1920]{1,0:T(8,128)(2,1)S(1)}, bf16[24,1920]{1,0:T(8,128)(2,1)S(1)}, u32[]{:S(2)}, u32[]{:S(2)}) collective-permute-start(bf16[24,1920]{1,0:T(8,128)(2,1)S(1)} %get-tuple-element.52), channel_id=1, source_target_pairs={{0,4},{2,6},{4,0},{6,2},{8,12},{10,14},{12,8},{14,10},{1,5},{3,7},... | collective-permute-start | bytes 276488 | tf_op jit(solution)/shard_map/ppermute | solution.py:408
  35.1 3.5 %collective-permute-start.11 = (bf16[256,1792]{1,0:T(8,128)(2,1)S(1)}, bf16[256,1792]{1,0:T(8,128)(2,1)}, u32[]{:S(2)}, u32[]{:S(2)}) collective-permute-start(bf16[256,1792]{1,0:T(8,128)(2,1)S(1)} %shard_map.99), channel_id=1, source_target_pairs={{0,1},{1,0},{2,3},{3,2},{4,5},{5,4},{6,7},{7,6},{8,9},{9,8},{10,11... | collective-permute-start | bytes 2752520 | tf_op jit(solution)/shard_map/ppermute | solution.py:495
  35.2 10.3 %all-to-all-start = ((bf16[8,32,128]{2,1,0:T(8,128)(2,1)}), bf16[8,32,128]{2,1,0:T(8,128)(2,1)S(1)}, u32[]{:S(2)}, u32[]{:S(2)}) async-start(bf16[8,32,128]{2,1,0:T(8,128)(2,1)} %bitcast.4), calls=%async_computation | async-start | bytes 131072 | tf_op jit(solution)/shard_map/all_to_all | solution.py:486
  38.5 6.9 %copy-start.3 = (f32[72,128]{1,0:T(8,128)S(1)}, f32[72,128]{1,0:T(8,128)}, u32[]{:S(2)}) copy-start(f32[72,128]{1,0:T(8,128)} %get-tuple-element.58.pick_ref) | copy-start | bytes 110596
  38.5 6.9 %copy-start.4 = (s32[72,128]{1,0:T(8,128)S(1)}, s32[72,128]{1,0:T(8,128)}, u32[]{:S(2)}) copy-start(s32[72,128]{1,0:T(8,128)} %get-tuple-element.59.expert_ref) | copy-start | bytes 110596
  38.5 6.9 %copy-start.5 = (f32[72,128]{1,0:T(8,128)S(1)}, f32[72,128]{1,0:T(8,128)}, u32[]{:S(2)}) copy-start(f32[72,128]{1,0:T(8,128)} %get-tuple-element.60.hs_ref) | copy-start | bytes 110596
  38.6 6.9 %copy-start.6 = (f32[72,128]{1,0:T(8,128)S(1)}, f32[72,128]{1,0:T(8,128)}, u32[]{:S(2)}) copy-start(f32[72,128]{1,0:T(8,128)} %get-tuple-element.61.ps_ref) | copy-start | bytes 110596
  38.6 6.9 %copy-start.7 = (s32[128,8]{0,1:T(8,128)S(1)}, s32[128,8]{0,1:T(8,128)}, u32[]{:S(2)}) copy-start(s32[128,8]{0,1:T(8,128)} %param.10) | copy-start | bytes 12292

commit v17 on v16

--- a/solution.py
+++ b/solution.py
@@ -305,13 +305,14 @@
         move.wait()
 
 
-def turn_kernel(local_count, dev_count, beside_ref, even_ref, *line_refs):
-    per_home, per_copy = local_count * SLOT, dev_count * CAPR
-    beside = beside_ref[...].astype(F32)[per_home:]
-    even = even_ref[...].astype(F32)
-    for n, line_ref in enumerate(line_refs):
+def turn_kernel(local_count, dev_count, line_ref, far_ref, near_ref, even_ref, near_out, beside_out, *line_outs):
+    per_home = local_count * SLOT
+    far, line, even = far_ref[...].astype(F32), line_ref[...].astype(F32)[per_home:], even_ref[...].astype(F32)
+    beside_out[...] = jnp.concatenate([far, near_ref[...].astype(F32)], axis=0).astype(BF16)
+    for n, out_ref in enumerate((near_out, *line_outs)):
         span = slice(n * per_home, (n + 1) * per_home)
-        line_ref[...] = folded(jnp.concatenate([even[span], beside[span]], axis=0)).astype(BF16)
+        rows = jnp.concatenate([far] * (n == 0) + [even[span], line[span]], axis=0)
+        out_ref[...] = (folded(rows) if n else rows).astype(BF16)
 
 
 def early_kernel(local_count, dev_count, order, pieces, w_ref, slot_ref, *refs):
@@ -449,29 +450,29 @@
     )
     near, far, line, beside, own_rows, even_rows, w_held, slot = lax.optimization_barrier(
         (near, far, line, beside, own_rows, even_rows, w_held, slot))
-    far_near = swap(far, 2, dev_count)
-    lines = call(
+    to_near, to_beside, *lines = call(
         functools.partial(turn_kernel, *sizes),
-        [shape((4 * per_home, fold_width(d_model + width)), BF16)] * len(even),
-        [(vmem, a) for a in (line, even_rows)],
-    )
-    far_beside, near_beside = swap(far, 1, dev_count), swap(near, 1, dev_count)
-    lines = [swap(a, m, dev_count) for a, m in zip(lines, even)]
-    pieces = {(0, HOME): (0, 0), (0, COPIES): (0, per_home), (1, COPIES): (1, 0), (1, HOME): (7, 0),
-              (2, COPIES): (2, 0), (4, COPIES): (3, 0), (5, COPIES): (4, 0), (3, COPIES): (5, 0),
-              (even[-1], HOME): (6, 0), (even[-1] + 1, HOME): (6, per_home)}
+        [shape((copies + 2 * per_home, d_model + width), BF16), shape((2 * copies, d_model + width), BF16)]
+        + [shape((4 * per_home, fold_width(d_model + width)), BF16)] * (len(even) - 1),
+        [(vmem, a) for a in (line, far, near, even_rows)],
+    )
+    far_near, onward = swap(to_near, 2, dev_count), swap(to_beside, 1, dev_count)
+    lines = [swap(a, m, dev_count) for a, m in zip(lines, even[1:])]
+    pieces = {(0, HOME): (0, 0), (0, COPIES): (0, per_home), (1, COPIES): (1, 0), (1, HOME): (6, 0),
+              (2, COPIES): (2, 0), (4, COPIES): (3, 0), (5, COPIES): (4, 0), (3, COPIES): (4, copies),
+              (even[-1], HOME): (5, 0), (even[-1] + 1, HOME): (5, per_home)}
     orders = [list(pieces)]
     height = padded(sum(per_home if kind == HOME else copies for _, kind in pieces))
     early_rows, own = call(
         functools.partial(early_kernel, *sizes, orders[0], pieces),
         (shape((height, d_model + width), BF16), shape((height, width), F32)),
-        [(vmem, a) for a in (w_held, slot, own_rows, beside, near, far, far_beside, near_beside, lines[-1], line)],
-        flops=2 * height * d_model * local_count * width,
-    )
-    far_across = swap(far_near, 1, dev_count)
+        [(vmem, a) for a in (w_held, slot, own_rows, beside, near, far, onward, lines[-1], line)],
+        flops=2 * height * d_model * local_count * width * 30,
+    )
+    far_across = swap(far_near[:copies], 1, dev_count)
     arrays = [far_near, far_across, *lines[:-1]]
-    pieces = {(6, COPIES): (0, 0), (7, COPIES): (1, 0)}
-    for n, m in enumerate(even[:-1]):
+    pieces = {(6, COPIES): (0, 0), (2, HOME): (0, copies), (3, HOME): (0, copies + per_home), (7, COPIES): (1, 0)}
+    for n, m in enumerate(even[1:-1]):
         pieces[m, HOME], pieces[m + 1, HOME] = ((2 + n, k * per_home) for k in range(2))
     orders.append(list(pieces))
     height = padded(sum(per_home if kind == HOME else copies for _, kind in pieces))

time: 46.8 us -> 50.3 us (1.075)
  waiting for transfers between devices: 13.5 us -> 18.3 us
  starting transfers between devices: 18.1 us -> 16.8 us
    ppermute x11 -> x9, waiting for transfers between devices: 9.25 us -> 14 us  [swap(): return lax.ppermute(x, 'expert', [(i, i ^ bits) for i in range(count)])]
    ppermute x11 -> x9, starting transfers between devices: 14.7 us -> 13.3 us  [swap(): return lax.ppermute(x, 'expert', [(i, i ^ bits) for i in range(count)])]
  transfers between devices with their start and end apart: 13 -> 11, of which waited for: 7 -> 5; matrix products, arithmetic and copies ran while one was open for 0% -> 0% of each run, Pallas kernels for 10% -> 9%
where the time goes in v17:
time: 50.3 us; the launch traced here: 49.9 us
  waiting for transfers between devices  18.3 us (36%)
  starting transfers between devices  16.8 us (33%)
  Pallas kernels  10 us (20%)
  local copies, waits for them, and re-layouts  4.05 us (8%)
  between operations  0.78 us (2%)
    ppermute x9, waiting for transfers between devices, swap(): return lax.ppermute(x, 'expert', [(i, i ^ bits) for i in range(count)])  14 us
    ppermute x9, starting transfers between devices, swap(): return lax.ppermute(x, 'expert', [(i, i ^ bits) for i in range(count)])  13.3 us
    pallas_call x8, Pallas kernels, call(): pl.pallas_call(kernel, out_shape=out_shape, in_specs=[pl.BlockSpec(memory...  10 us
    all_to_all x1, waiting for transfers between devices, gather_body(): lax.all_to_all(back, 'expert', split_axis=0, concat_axis=0, tiled=True)  4.24 us
    unnamed x18, local copies, waits for them, and re-layouts  4.04 us
    all_to_all x1, starting transfers between devices, gather_body(): lax.all_to_all(back, 'expert', split_axis=0, concat_axis=0, tiled=True)  3.36 us
  transfers between devices with their start and end apart: 11, of which 5 were waited for; matrix products, arithmetic and copies ran while one was open for 0% of the time, Pallas kernels for 9%

profile of v17, /device:TPU:0, one launch (start us, length us, event | category | flops | bytes accessed | tf_op | source)
XLA Modules:
  0.0 49.9 jit_solution(18355124406471921278)
XLA Ops:
  0.6 2.5 %shard_map.94 = (f32[72,128]{1,0:T(8,128)}, s32[72,128]{1,0:T(8,128)}, f32[72,128]{1,0:T(8,128)}, f32[72,128]{1,0:T(8,128)}, bf16[24,3712]{1,0:T(8,128)(2,1)}, /...) custom-call(s32[8]{0:T(128)} %replica_ref.1, s32[1,8]{1,0:T(1,128)} %refs_1_.1, ...), custom_call_target="tpu_custom_call" | custom-call | flops 66060288 | bytes 2046016 | tf_op jit(solution)/shard_map/pallas_call | solution.py:397
  3.2 3.1 %collective-permute-start = (bf16[24,3712]{1,0:T(8,128)(2,1)}, bf16[24,3712]{1,0:T(8,128)(2,1)S(1)}, u32[]{:S(2)}, u32[]{:S(2)}) collective-permute-start(bf16[24,3712]{1,0:T(8,128)(2,1)} %get-tuple-element.35), channel_id=1, source_target_pairs={{0,4},{2,6},{4,0},{6,2},{8,12},{10,14},{12,8},{14,10},{1,5},{3,7},... | collective-permute-start | bytes 534536 | tf_op jit(solution)/shard_map/ppermute | solution.py:409
  6.2 2.6 %collective-permute-start.1 = (bf16[24,3712]{1,0:T(8,128)(2,1)}, bf16[24,3712]{1,0:T(8,128)(2,1)S(1)}, u32[]{:S(2)}, u32[]{:S(2)}) collective-permute-start(bf16[24,3712]{1,0:T(8,128)(2,1)} %get-tuple-element.35), channel_id=1, source_target_pairs={{0,8},{2,10},{4,12},{6,14},{8,0},{10,2},{12,4},{14,6},{1,9},{3,11}... | collective-permute-start | bytes 534536 | tf_op jit(solution)/shard_map/ppermute | solution.py:409
  8.8 1.5 %collective-permute-start.3 = (bf16[24,3712]{1,0:T(8,128)(2,1)}, bf16[24,3712]{1,0:T(8,128)(2,1)S(1)}, u32[]{:S(2)}, u32[]{:S(2)}) collective-permute-start(bf16[24,3712]{1,0:T(8,128)(2,1)} %get-tuple-element.35), channel_id=1, source_target_pairs={{0,2},{2,0},{4,6},{6,4},{8,10},{10,8},{12,14},{14,12},{1,3},{3,1},... | collective-permute-start | bytes 534536 | tf_op jit(solution)/shard_map/ppermute | solution.py:409
  10.3 0.5 %collective-permute-start.2 = (bf16[24,3712]{1,0:T(8,128)(2,1)}, bf16[24,3712]{1,0:T(8,128)(2,1)S(1)}, u32[]{:S(2)}, u32[]{:S(2)}) collective-permute-start(bf16[24,3712]{1,0:T(8,128)(2,1)} %get-tuple-element.36), channel_id=1, source_target_pairs={{0,2},{2,0},{4,6},{6,4},{8,10},{10,8},{12,14},{14,12},{1,3},{3,1},... | collective-permute-start | bytes 534536 | tf_op jit(solution)/shard_map/ppermute | solution.py:409
  10.9 0.0 copy-start
  10.9 1.5 %copy-done = bf16[2,128,3584]{2,1,0:T(8,128)(2,1)S(1)} copy-done((bf16[2,128,3584]{2,1,0:T(8,128)(2,1)S(1)}, bf16[2,128,3584]{2,1,0:T(8,128)(2,1)}, u32[]{:S(2)}) %copy-start) | copy-done | bytes 1835032
  12.4 0.0 copy-start.1
  12.4 0.9 %copy-done.1 = bf16[30,3712]{1,0:T(8,128)(2,1)S(1)} copy-done((bf16[30,3712]{1,0:T(8,128)(2,1)S(1)}, bf16[30,3712]{1,0:T(8,128)(2,1)}, u32[]{:S(2)}) %copy-start.1) | copy-done | bytes 222744
  13.3 0.0 copy-start.2
  13.3 0.9 %copy-done.2 = bf16[18,3712]{1,0:T(8,128)(2,1)S(1)} copy-done((bf16[18,3712]{1,0:T(8,128)(2,1)S(1)}, bf16[18,3712]{1,0:T(8,128)(2,1)}, u32[]{:S(2)}) %copy-start.2) | copy-done | bytes 133656
  14.2 0.0 copy-start.8
  14.2 0.7 %copy-done.8 = s32[8]{0:T(128)S(1)} copy-done((s32[8]{0:T(128)S(1)}, s32[8]{0:T(128)}, u32[]{:S(2)}) %copy-start.8) | copy-done | bytes 56
  14.9 1.2 %shard_map.95 = (bf16[30,3712]{1,0:T(8,128)(2,1)S(1)}, bf16[18,3712]{1,0:T(8,128)(2,1)S(1)}, bf16[256,3584]{1,0:T(8,128)(2,1)S(1)}, s32[30,128]{1,0:T(8,128)S(1)}) custom-call(s32[8]{0:T(128)S(1)} %copy-done.8, bf16[256,3584]{1,0:T(8,128)(2,1)S(1)} %bitcast.8, bf16[30,3712]{1,0:T(8,128)(2,1)S(1)} %copy-done.1, bf16[18,3712]{1,0:T(8,128)(2,1)S(1)} %copy-done.2), custom_call_target="tpu_custom_call" | custom-call | bytes 4398112 | tf_op jit(solution)/shard_map/pallas_call | solution.py:397
  16.1 0.0 collective-permute-done.near_ref.refs_2_
  16.1 1.1 %collective-permute-done.1.far_ref.refs_3_ = bf16[24,3712]{1,0:T(8,128)(2,1)S(1)} collective-permute-done((bf16[24,3712]{1,0:T(8,128)(2,1)}, bf16[24,3712]{1,0:T(8,128)(2,1)S(1)}, u32[]{:S(2)}, u32[]{:S(2)}) %collective-permute-start.1) | collective-permute-done | bytes 178208 | tf_op jit(solution)/shard_map/ppermute | solution.py:409
  17.2 0.0 collective-permute-done.3.refs_1_
  17.2 1.3 %collective-permute-done.2.line_ref.refs_6_ = bf16[24,3712]{1,0:T(8,128)(2,1)S(1)} collective-permute-done((bf16[24,3712]{1,0:T(8,128)(2,1)}, bf16[24,3712]{1,0:T(8,128)(2,1)S(1)}, u32[]{:S(2)}, u32[]{:S(2)}) %collective-permute-start.2) | collective-permute-done | bytes 178208 | tf_op jit(solution)/shard_map/ppermute | solution.py:409
  18.5 0.1 shard_map.96
  18.7 1.6 %collective-permute-start.4 = (bf16[48,3712]{1,0:T(8,128)(2,1)S(1)}, bf16[48,3712]{1,0:T(8,128)(2,1)S(1)}, u32[]{:S(2)}, u32[]{:S(2)}) collective-permute-start(bf16[48,3712]{1,0:T(8,128)(2,1)S(1)} %get-tuple-element.51), channel_id=1, source_target_pairs={{0,2},{2,0},{4,6},{6,4},{8,10},{10,8},{12,14},{14,12},{1,3},{3,1},... | collective-permute-start | bytes 1069064 | tf_op jit(solution)/shard_map/ppermute | solution.py:409
  20.2 0.4 collective-permute-start.6
  20.7 1.3 %collective-permute-start.5 = (bf16[24,1920]{1,0:T(8,128)(2,1)S(1)}, bf16[24,1920]{1,0:T(8,128)(2,1)S(1)}, u32[]{:S(2)}, u32[]{:S(2)}) collective-permute-start(bf16[24,1920]{1,0:T(8,128)(2,1)S(1)} %get-tuple-element.52), channel_id=1, source_target_pairs={{0,12},{2,14},{4,8},{6,10},{8,4},{10,6},{12,0},{14,2},{1,13},{3,15... | collective-permute-start | bytes 276488 | tf_op jit(solution)/shard_map/ppermute | solution.py:409
  22.0 1.7 %collective-permute-start.8 = (bf16[24,1920]{1,0:T(8,128)(2,1)S(1)}, bf16[24,1920]{1,0:T(8,128)(2,1)S(1)}, u32[]{:S(2)}, u32[]{:S(2)}) collective-permute-start(bf16[24,1920]{1,0:T(8,128)(2,1)S(1)} %get-tuple-element.55), channel_id=1, source_target_pairs={{0,8},{2,10},{4,12},{6,14},{8,0},{10,2},{12,4},{14,6},{1,9},{3,11}... | collective-permute-start | bytes 276488 | tf_op jit(solution)/shard_map/ppermute | solution.py:409
  23.7 7.5 %collective-permute-done.6.refs_0_ = bf16[36,3712]{1,0:T(8,128)(2,1)S(1)} collective-permute-done((bf16[36,3712]{1,0:T(8,128)(2,1)S(1)}, bf16[36,3712]{1,0:T(8,128)(2,1)S(1)}, u32[]{:S(2)}, u32[]{:S(2)}) %collective-permute-start.6) | collective-permute-done | bytes 267296 | tf_op jit(solution)/shard_map/ppermute | solution.py:409
  31.2 0.6 %collective-permute-start.7 = (bf16[24,3712]{1,0:T(8,128)(2,1)S(1)}, bf16[24,3712]{1,0:T(8,128)(2,1)S(1)}, u32[]{:S(2)}, u32[]{:S(2)}) collective-permute-start(bf16[24,3712]{1,0:T(8,128)(2,1)S(1)} %slice.4), channel_id=1, source_target_pairs={{0,2},{2,0},{4,6},{6,4},{8,10},{10,8},{12,14},{14,12},{1,3},{3,1},... | collective-permute-start | bytes 534536 | tf_op jit(solution)/shard_map/ppermute | solution.py:409
  31.8 0.0 collective-permute-done.5.refs_5_
  31.8 0.0 collective-permute-done.4.refs_4_
  31.9 0.8 %shard_map.97 = (bf16[176,3712]{1,0:T(8,128)(2,1)S(1)}, f32[176,128]{1,0:T(8,128)S(1)}) custom-call(bf16[256,3584]{1,0:T(8,128)(2,1)S(1)} %get-tuple-element.43.w_ref, s32[30,128]{1,0:T(8,128)S(1)} %get-tuple-element.44.slot_ref, bf16[30,3712]{1,0:T(8,128)(2,1)S(1)} %get-tuple-element.45.refs_0_, bf16[24,3712]{1,0:T(8,128)(2,1)S(1)} %collective-permute-done.3.refs_1_, ...), custom_call_target="tpu_custom_call" | custom-call | flops 9688842240 | bytes 4631040 | tf_op jit(solution)/shard_map/pallas_call | solution.py:397
  32.6 0.0 collective-permute-done.8.refs_2_
  32.7 4.1 %collective-permute-done.7.refs_1_ = bf16[24,3712]{1,0:T(8,128)(2,1)S(1)} collective-permute-done((bf16[24,3712]{1,0:T(8,128)(2,1)S(1)}, bf16[24,3712]{1,0:T(8,128)(2,1)S(1)}, u32[]{:S(2)}, u32[]{:S(2)}) %collective-permute-start.7) | collective-permute-done | bytes 178208 | tf_op jit(solution)/shard_map/ppermute | solution.py:409
  36.8 1.3 %shard_map.98 = (bf16[80,3712]{1,0:T(8,128)(2,1)S(1)}, bf16[256,128]{1,0:T(8,128)(2,1)}) custom-call(f32[176,128]{1,0:T(8,128)S(1)} %get-tuple-element.53.own_ref, bf16[256,3584]{1,0:T(8,128)(2,1)S(1)} %get-tuple-element.43.w_ref, s32[30,128]{1,0:T(8,128)S(1)} %get-tuple-element.44.slot_ref, bf16[36,3712]{1,0:T(8,128)(2,1)S(1)} %collective-permute-done.6.refs_0_, ...), custom_call_target="tpu_custom_call" | custom-call | flops 146800640 | bytes 3137536 | tf_op jit(solution)/shard_map/pallas_call | solution.py:397
  38.1 0.4 shard_map.99
  38.6 0.1 collective-permute-start.9
  38.6 3.4 %all-to-all-start = ((bf16[8,32,128]{2,1,0:T(8,128)(2,1)}), bf16[8,32,128]{2,1,0:T(8,128)(2,1)S(1)}, u32[]{:S(2)}, u32[]{:S(2)}) async-start(bf16[8,32,128]{2,1,0:T(8,128)(2,1)} %bitcast.4), calls=%async_computation | async-start | bytes 131072 | tf_op jit(solution)/shard_map/all_to_all | solution.py:487
  42.0 0.0 copy-start.3
  42.0 0.0 copy-start.4
  42.0 0.0 copy-start.5
  42.0 0.0 copy-start.6
  42.1 0.0 copy-start.7
  42.1 0.0 collective-permute-done.9.arrived_ref
  42.1 2.6 %shard_map.100 = bf16[256,1792]{1,0:T(8,128)(2,1)} custom-call(s32[30,128]{1,0:T(8,128)S(1)} %get-tuple-element.44.slot_ref, bf16[176,3712]{1,0:T(8,128)(2,1)S(1)} %get-tuple-element.57.early_ref, bf16[80,3712]{1,0:T(8,128)(2,1)S(1)} %get-tuple-element.58.late_ref, bf16[256,1792]{1,0:T(8,128)(2,1)} %collective-permute-done.9.arrived_ref), custom_call_target="tpu_custom_call" | custom-call | flops 6606028800 | bytes 3750912 | tf_op jit(solution)/shard_map/pallas_call | solution.py:397
  44.7 4.2 %all-to-all-done.back_ref = bf16[8,32,128]{2,1,0:T(8,128)(2,1)S(1)} async-done(((bf16[8,32,128]{2,1,0:T(8,128)(2,1)}), bf16[8,32,128]{2,1,0:T(8,128)(2,1)S(1)}, u32[]{:S(2)}, u32[]{:S(2)}) %all-to-all-start) | async-done | bytes 65568 | tf_op jit(solution)/shard_map/all_to_all | solution.py:487
  48.9 0.0 copy-done.3
  48.9 0.0 copy-done.4
  48.9 0.0 copy-done.5
  48.9 0.0 copy-done.6
  48.9 0.0 copy-done.7
  48.9 1.0 %shard_map.101 = (bf16[1024,128]{1,0:T(8,128)(2,1)}, bf16[8,128]{1,0:T(8,128)(2,1)}) custom-call(bf16[8,32,128]{2,1,0:T(8,128)(2,1)S(1)} %all-to-all-done.back_ref, f32[72,128]{1,0:T(8,128)S(1)} %copy-done.3, s32[72,128]{1,0:T(8,128)S(1)} %copy-done.4, f32[72,128]{1,0:T(8,128)S(1)} %copy-done.5, f32[72,128]{1,0:T(8,128)S(1)} %copy-done.6, s32[8,128]{1,0:T(8,128)S(1)} %bitcast.10), custom_call_target="tpu_custom_call" | custom-call | flops 18874368 | bytes 481280 | tf_op jit(solution)/shard_map/pallas_call | solution.py:397
  (1 shorter events, 0.0 us)
Async XLA Ops:
  3.2 13.0 %collective-permute-start = (bf16[24,3712]{1,0:T(8,128)(2,1)}, bf16[24,3712]{1,0:T(8,128)(2,1)S(1)}, u32[]{:S(2)}, u32[]{:S(2)}) collective-permute-start(bf16[24,3712]{1,0:T(8,128)(2,1)} %get-tuple-element.35), channel_id=1, source_target_pairs={{0,4},{2,6},{4,0},{6,2},{8,12},{10,14},{12,8},{14,10},{1,5},{3,7},... | collective-permute-start | bytes 534536 | tf_op jit(solution)/shard_map/ppermute | solution.py:409
  6.2 11.0 %collective-permute-start.1 = (bf16[24,3712]{1,0:T(8,128)(2,1)}, bf16[24,3712]{1,0:T(8,128)(2,1)S(1)}, u32[]{:S(2)}, u32[]{:S(2)}) collective-permute-start(bf16[24,3712]{1,0:T(8,128)(2,1)} %get-tuple-element.35), channel_id=1, source_target_pairs={{0,8},{2,10},{4,12},{6,14},{8,0},{10,2},{12,4},{14,6},{1,9},{3,11}... | collective-permute-start | bytes 534536 | tf_op jit(solution)/shard_map/ppermute | solution.py:409
  8.8 8.4 %collective-permute-start.3 = (bf16[24,3712]{1,0:T(8,128)(2,1)}, bf16[24,3712]{1,0:T(8,128)(2,1)S(1)}, u32[]{:S(2)}, u32[]{:S(2)}) collective-permute-start(bf16[24,3712]{1,0:T(8,128)(2,1)} %get-tuple-element.35), channel_id=1, source_target_pairs={{0,2},{2,0},{4,6},{6,4},{8,10},{10,8},{12,14},{14,12},{1,3},{3,1},... | collective-permute-start | bytes 534536 | tf_op jit(solution)/shard_map/ppermute | solution.py:409
  10.3 8.2 %collective-permute-start.2 = (bf16[24,3712]{1,0:T(8,128)(2,1)}, bf16[24,3712]{1,0:T(8,128)(2,1)S(1)}, u32[]{:S(2)}, u32[]{:S(2)}) collective-permute-start(bf16[24,3712]{1,0:T(8,128)(2,1)} %get-tuple-element.36), channel_id=1, source_target_pairs={{0,2},{2,0},{4,6},{6,4},{8,10},{10,8},{12,14},{14,12},{1,3},{3,1},... | collective-permute-start | bytes 534536 | tf_op jit(solution)/shard_map/ppermute | solution.py:409
  10.9 1.5 %copy-start = (bf16[2,128,3584]{2,1,0:T(8,128)(2,1)S(1)}, bf16[2,128,3584]{2,1,0:T(8,128)(2,1)}, u32[]{:S(2)}) copy-start(bf16[2,128,3584]{2,1,0:T(8,128)(2,1)} %param.13) | copy-start | bytes 5505028
  12.4 0.9 %copy-start.1 = (bf16[30,3712]{1,0:T(8,128)(2,1)S(1)}, bf16[30,3712]{1,0:T(8,128)(2,1)}, u32[]{:S(2)}) copy-start(bf16[30,3712]{1,0:T(8,128)(2,1)} %get-tuple-element.37.own_hbm) | copy-start | bytes 668164
  13.3 0.9 %copy-start.2 = (bf16[18,3712]{1,0:T(8,128)(2,1)S(1)}, bf16[18,3712]{1,0:T(8,128)(2,1)}, u32[]{:S(2)}) copy-start(bf16[18,3712]{1,0:T(8,128)(2,1)} %get-tuple-element.38.even_hbm) | copy-start | bytes 400900
  14.2 0.7 %copy-start.8 = (s32[8]{0:T(128)S(1)}, s32[8]{0:T(128)}, u32[]{:S(2)}) copy-start(s32[8]{0:T(128)} %replica_ref.1) | copy-start | bytes 100
  18.7 13.2 %collective-permute-start.4 = (bf16[48,3712]{1,0:T(8,128)(2,1)S(1)}, bf16[48,3712]{1,0:T(8,128)(2,1)S(1)}, u32[]{:S(2)}, u32[]{:S(2)}) collective-permute-start(bf16[48,3712]{1,0:T(8,128)(2,1)S(1)} %get-tuple-element.51), channel_id=1, source_target_pairs={{0,2},{2,0},{4,6},{6,4},{8,10},{10,8},{12,14},{14,12},{1,3},{3,1},... | collective-permute-start | bytes 1069064 | tf_op jit(solution)/shard_map/ppermute | solution.py:409
  20.2 11.0 %collective-permute-start.6 = (bf16[36,3712]{1,0:T(8,128)(2,1)S(1)}, bf16[36,3712]{1,0:T(8,128)(2,1)S(1)}, u32[]{:S(2)}, u32[]{:S(2)}) collective-permute-start(bf16[36,3712]{1,0:T(8,128)(2,1)S(1)} %get-tuple-element.54), channel_id=1, source_target_pairs={{0,4},{2,6},{4,0},{6,2},{8,12},{10,14},{12,8},{14,10},{1,5},{3,7},... | collective-permute-start | bytes 801800 | tf_op jit(solution)/shard_map/ppermute | solution.py:409
  20.7 11.2 %collective-permute-start.5 = (bf16[24,1920]{1,0:T(8,128)(2,1)S(1)}, bf16[24,1920]{1,0:T(8,128)(2,1)S(1)}, u32[]{:S(2)}, u32[]{:S(2)}) collective-permute-start(bf16[24,1920]{1,0:T(8,128)(2,1)S(1)} %get-tuple-element.52), channel_id=1, source_target_pairs={{0,12},{2,14},{4,8},{6,10},{8,4},{10,6},{12,0},{14,2},{1,13},{3,15... | collective-permute-start | bytes 276488 | tf_op jit(solution)/shard_map/ppermute | solution.py:409
  22.0 10.6 %collective-permute-start.8 = (bf16[24,1920]{1,0:T(8,128)(2,1)S(1)}, bf16[24,1920]{1,0:T(8,128)(2,1)S(1)}, u32[]{:S(2)}, u32[]{:S(2)}) collective-permute-start(bf16[24,1920]{1,0:T(8,128)(2,1)S(1)} %get-tuple-element.55), channel_id=1, source_target_pairs={{0,8},{2,10},{4,12},{6,14},{8,0},{10,2},{12,4},{14,6},{1,9},{3,11}... | collective-permute-start | bytes 276488 | tf_op jit(solution)/shard_map/ppermute | solution.py:409
  31.2 5.5 %collective-permute-start.7 = (bf16[24,3712]{1,0:T(8,128)(2,1)S(1)}, bf16[24,3712]{1,0:T(8,128)(2,1)S(1)}, u32[]{:S(2)}, u32[]{:S(2)}) collective-permute-start(bf16[24,3712]{1,0:T(8,128)(2,1)S(1)} %slice.4), channel_id=1, source_target_pairs={{0,2},{2,0},{4,6},{6,4},{8,10},{10,8},{12,14},{14,12},{1,3},{3,1},... | collective-permute-start | bytes 534536 | tf_op jit(solution)/shard_map/ppermute | solution.py:409
  38.6 3.5 %collective-permute-start.9 = (bf16[256,1792]{1,0:T(8,128)(2,1)S(1)}, bf16[256,1792]{1,0:T(8,128)(2,1)}, u32[]{:S(2)}, u32[]{:S(2)}) collective-permute-start(bf16[256,1792]{1,0:T(8,128)(2,1)S(1)} %shard_map.99), channel_id=1, source_target_pairs={{0,1},{1,0},{2,3},{3,2},{4,5},{5,4},{6,7},{7,6},{8,9},{9,8},{10,11... | collective-permute-start | bytes 2752520 | tf_op jit(solution)/shard_map/ppermute | solution.py:496
  38.6 10.3 %all-to-all-start = ((bf16[8,32,128]{2,1,0:T(8,128)(2,1)}), bf16[8,32,128]{2,1,0:T(8,128)(2,1)S(1)}, u32[]{:S(2)}, u32[]{:S(2)}) async-start(bf16[8,32,128]{2,1,0:T(8,128)(2,1)} %bitcast.4), calls=%async_computation | async-start | bytes 131072 | tf_op jit(solution)/shard_map/all_to_all | solution.py:487
  42.0 6.9 %copy-start.3 = (f32[72,128]{1,0:T(8,128)S(1)}, f32[72,128]{1,0:T(8,128)}, u32[]{:S(2)}) copy-start(f32[72,128]{1,0:T(8,128)} %get-tuple-element.60.pick_ref) | copy-start | bytes 110596
  42.0 6.9 %copy-start.4 = (s32[72,128]{1,0:T(8,128)S(1)}, s32[72,128]{1,0:T(8,128)}, u32[]{:S(2)}) copy-start(s32[72,128]{1,0:T(8,128)} %get-tuple-element.61.expert_ref) | copy-start | bytes 110596
  42.0 6.9 %copy-start.5 = (f32[72,128]{1,0:T(8,128)S(1)}, f32[72,128]{1,0:T(8,128)}, u32[]{:S(2)}) copy-start(f32[72,128]{1,0:T(8,128)} %get-tuple-element.62.hs_ref) | copy-start | bytes 110596
  42.0 6.9 %copy-start.6 = (f32[72,128]{1,0:T(8,128)S(1)}, f32[72,128]{1,0:T(8,128)}, u32[]{:S(2)}) copy-start(f32[72,128]{1,0:T(8,128)} %get-tuple-element.63.ps_ref) | copy-start | bytes 110596
  42.1 6.9 %copy-start.7 = (s32[128,8]{0,1:T(8,128)S(1)}, s32[128,8]{0,1:T(8,128)}, u32[]{:S(2)}) copy-start(s32[128,8]{0,1:T(8,128)} %param.10) | copy-start | bytes 12292

commit v18 on v17

--- a/solution.py
+++ b/solution.py
@@ -305,14 +305,13 @@
         move.wait()
 
 
-def turn_kernel(local_count, dev_count, line_ref, far_ref, near_ref, even_ref, near_out, beside_out, *line_outs):
+def turn_kernel(local_count, dev_count, line_ref, far_ref, near_ref, even_ref, beside_out, *line_outs):
     per_home = local_count * SLOT
-    far, line, even = far_ref[...].astype(F32), line_ref[...].astype(F32)[per_home:], even_ref[...].astype(F32)
-    beside_out[...] = jnp.concatenate([far, near_ref[...].astype(F32)], axis=0).astype(BF16)
-    for n, out_ref in enumerate((near_out, *line_outs)):
+    beside_out[...] = jnp.concatenate([far_ref[...].astype(F32), near_ref[...].astype(F32)], axis=0).astype(BF16)
+    line, even = line_ref[...].astype(F32)[per_home:], even_ref[...].astype(F32)
+    for n, out_ref in enumerate(line_outs):
         span = slice(n * per_home, (n + 1) * per_home)
-        rows = jnp.concatenate([far] * (n == 0) + [even[span], line[span]], axis=0)
-        out_ref[...] = (folded(rows) if n else rows).astype(BF16)
+        out_ref[...] = folded(jnp.concatenate([even[span], line[span]], axis=0)).astype(BF16)
 
 
 def early_kernel(local_count, dev_count, order, pieces, w_ref, slot_ref, *refs):
@@ -450,14 +449,15 @@
     )
     near, far, line, beside, own_rows, even_rows, w_held, slot = lax.optimization_barrier(
         (near, far, line, beside, own_rows, even_rows, w_held, slot))
-    to_near, to_beside, *lines = call(
+    far_near = swap(far, 2, dev_count)
+    to_beside, *lines = call(
         functools.partial(turn_kernel, *sizes),
-        [shape((copies + 2 * per_home, d_model + width), BF16), shape((2 * copies, d_model + width), BF16)]
-        + [shape((4 * per_home, fold_width(d_model + width)), BF16)] * (len(even) - 1),
+        [shape((2 * copies, d_model + width), BF16)]
+        + [shape((4 * per_home, fold_width(d_model + width)), BF16)] * len(even),
         [(vmem, a) for a in (line, far, near, even_rows)],
     )
-    far_near, onward = swap(to_near, 2, dev_count), swap(to_beside, 1, dev_count)
-    lines = [swap(a, m, dev_count) for a, m in zip(lines, even[1:])]
+    onward = swap(to_beside, 1, dev_count)
+    lines = [swap(a, m, dev_count) for a, m in zip(lines, even)]
     pieces = {(0, HOME): (0, 0), (0, COPIES): (0, per_home), (1, COPIES): (1, 0), (1, HOME): (6, 0),
               (2, COPIES): (2, 0), (4, COPIES): (3, 0), (5, COPIES): (4, 0), (3, COPIES): (4, copies),
               (even[-1], HOME): (5, 0), (even[-1] + 1, HOME): (5, per_home)}
@@ -467,12 +467,12 @@
         functools.partial(early_kernel, *sizes, orders[0], pieces),
         (shape((height, d_model + width), BF16), shape((height, width), F32)),
         [(vmem, a) for a in (w_held, slot, own_rows, beside, near, far, onward, lines[-1], line)],
-        flops=2 * height * d_model * local_count * width * 30,
-    )
-    far_across = swap(far_near[:copies], 1, dev_count)
-    arrays = [far_near, far_across, *lines[:-1]]
-    pieces = {(6, COPIES): (0, 0), (2, HOME): (0, copies), (3, HOME): (0, copies + per_home), (7, COPIES): (1, 0)}
-    for n, m in enumerate(even[1:-1]):
+        flops=2 * height * d_model * local_count * width * 4,
+    )
+    far_across = swap(far_near, 1, dev_count)
+    arrays = [far_near, far_across, *lines[-2::-1]]
+    pieces = {(6, COPIES): (0, 0), (7, COPIES): (1, 0)}
+    for n, m in enumerate(even[-2::-1]):
         pieces[m, HOME], pieces[m + 1, HOME] = ((2 + n, k * per_home) for k in range(2))
     orders.append(list(pieces))
     height = padded(sum(per_home if kind == HOME else copies for _, kind in pieces))

time: 50.3 us -> 47.7 us (0.948)
  waiting for transfers between devices: 18.3 us -> 13.8 us
  starting transfers between devices: 16.8 us -> 18.6 us
    ppermute x9 -> x10, waiting for transfers between devices: 14 us -> 9.57 us  [swap(): return lax.ppermute(x, 'expert', [(i, i ^ bits) for i in range(count)])]
    ppermute x9 -> x10, starting transfers between devices: 13.3 us -> 14.3 us  [swap(): return lax.ppermute(x, 'expert', [(i, i ^ bits) for i in range(count)])]
    all_to_all x1, starting transfers between devices: 3.36 us -> 4.25 us  [gather_body(): lax.all_to_all(back, 'expert', split_axis=0, concat_axis=0, tiled=True)]
  transfers between devices with their start and end apart: 11 -> 12, of which waited for: 5 -> 6; matrix products, arithmetic and copies ran while one was open for 0% -> 0% of each run, Pallas kernels for 9% -> 10%
where the time goes in v18:
time: 47.7 us; the launch traced here: 47.3 us
  starting transfers between devices  18.6 us (39%)
  waiting for transfers between devices  13.8 us (29%)
  Pallas kernels  10 us (21%)
  local copies, waits for them, and re-layouts  4.04 us (8%)
  between operations  0.75 us (2%)
    ppermute x10, starting transfers between devices, swap(): return lax.ppermute(x, 'expert', [(i, i ^ bits) for i in range(count)])  14.3 us
    pallas_call x8, Pallas kernels, call(): pl.pallas_call(kernel, out_shape=out_shape, in_specs=[pl.BlockSpec(memory...  10 us
    ppermute x10, waiting for transfers between devices, swap(): return lax.ppermute(x, 'expert', [(i, i ^ bits) for i in range(count)])  9.57 us
    all_to_all x1, waiting for transfers between devices, gather_body(): lax.all_to_all(back, 'expert', split_axis=0, concat_axis=0, tiled=True)  4.26 us
    all_to_all x1, starting transfers between devices, gather_body(): lax.all_to_all(back, 'expert', split_axis=0, concat_axis=0, tiled=True)  4.25 us
    unnamed x18, local copies, waits for them, and re-layouts  4.04 us
  transfers between devices with their start and end apart: 12, of which 6 were waited for; matrix products, arithmetic and copies ran while one was open for 0% of the time, Pallas kernels for 10%

profile of v18, /device:TPU:0, one launch (start us, length us, event | category | flops | bytes accessed | tf_op | source)
XLA Modules:
  0.0 47.3 jit_solution(18121295172790668684)
XLA Ops:
  0.6 2.5 %shard_map.94 = (f32[72,128]{1,0:T(8,128)}, s32[72,128]{1,0:T(8,128)}, f32[72,128]{1,0:T(8,128)}, f32[72,128]{1,0:T(8,128)}, bf16[24,3712]{1,0:T(8,128)(2,1)}, /...) custom-call(s32[8]{0:T(128)} %replica_ref.1, s32[1,8]{1,0:T(1,128)} %refs_1_.1, ...), custom_call_target="tpu_custom_call" | custom-call | flops 66060288 | bytes 2046016 | tf_op jit(solution)/shard_map/pallas_call | solution.py:396
  3.2 3.1 %collective-permute-start = (bf16[24,3712]{1,0:T(8,128)(2,1)}, bf16[24,3712]{1,0:T(8,128)(2,1)S(1)}, u32[]{:S(2)}, u32[]{:S(2)}) collective-permute-start(bf16[24,3712]{1,0:T(8,128)(2,1)} %get-tuple-element.35), channel_id=1, source_target_pairs={{0,4},{2,6},{4,0},{6,2},{8,12},{10,14},{12,8},{14,10},{1,5},{3,7},... | collective-permute-start | bytes 534536 | tf_op jit(solution)/shard_map/ppermute | solution.py:408
  6.2 2.6 %collective-permute-start.1 = (bf16[24,3712]{1,0:T(8,128)(2,1)}, bf16[24,3712]{1,0:T(8,128)(2,1)S(1)}, u32[]{:S(2)}, u32[]{:S(2)}) collective-permute-start(bf16[24,3712]{1,0:T(8,128)(2,1)} %get-tuple-element.35), channel_id=1, source_target_pairs={{0,8},{2,10},{4,12},{6,14},{8,0},{10,2},{12,4},{14,6},{1,9},{3,11}... | collective-permute-start | bytes 534536 | tf_op jit(solution)/shard_map/ppermute | solution.py:408
  8.8 1.5 %collective-permute-start.3 = (bf16[24,3712]{1,0:T(8,128)(2,1)}, bf16[24,3712]{1,0:T(8,128)(2,1)S(1)}, u32[]{:S(2)}, u32[]{:S(2)}) collective-permute-start(bf16[24,3712]{1,0:T(8,128)(2,1)} %get-tuple-element.35), channel_id=1, source_target_pairs={{0,2},{2,0},{4,6},{6,4},{8,10},{10,8},{12,14},{14,12},{1,3},{3,1},... | collective-permute-start | bytes 534536 | tf_op jit(solution)/shard_map/ppermute | solution.py:408
  10.3 0.5 %collective-permute-start.2 = (bf16[24,3712]{1,0:T(8,128)(2,1)}, bf16[24,3712]{1,0:T(8,128)(2,1)S(1)}, u32[]{:S(2)}, u32[]{:S(2)}) collective-permute-start(bf16[24,3712]{1,0:T(8,128)(2,1)} %get-tuple-element.36), channel_id=1, source_target_pairs={{0,2},{2,0},{4,6},{6,4},{8,10},{10,8},{12,14},{14,12},{1,3},{3,1},... | collective-permute-start | bytes 534536 | tf_op jit(solution)/shard_map/ppermute | solution.py:408
  10.9 0.0 copy-start
  10.9 1.5 %copy-done = bf16[2,128,3584]{2,1,0:T(8,128)(2,1)S(1)} copy-done((bf16[2,128,3584]{2,1,0:T(8,128)(2,1)S(1)}, bf16[2,128,3584]{2,1,0:T(8,128)(2,1)}, u32[]{:S(2)}) %copy-start) | copy-done | bytes 1835032
  12.4 0.0 copy-start.1
  12.4 0.9 %copy-done.1 = bf16[30,3712]{1,0:T(8,128)(2,1)S(1)} copy-done((bf16[30,3712]{1,0:T(8,128)(2,1)S(1)}, bf16[30,3712]{1,0:T(8,128)(2,1)}, u32[]{:S(2)}) %copy-start.1) | copy-done | bytes 222744
  13.3 0.0 copy-start.2
  13.3 0.9 %copy-done.2 = bf16[18,3712]{1,0:T(8,128)(2,1)S(1)} copy-done((bf16[18,3712]{1,0:T(8,128)(2,1)S(1)}, bf16[18,3712]{1,0:T(8,128)(2,1)}, u32[]{:S(2)}) %copy-start.2) | copy-done | bytes 133656
  14.2 0.0 copy-start.8
  14.2 0.7 %copy-done.8 = s32[8]{0:T(128)S(1)} copy-done((s32[8]{0:T(128)S(1)}, s32[8]{0:T(128)}, u32[]{:S(2)}) %copy-start.8) | copy-done | bytes 56
  14.9 1.2 %shard_map.95 = (bf16[30,3712]{1,0:T(8,128)(2,1)S(1)}, bf16[18,3712]{1,0:T(8,128)(2,1)S(1)}, bf16[256,3584]{1,0:T(8,128)(2,1)S(1)}, s32[30,128]{1,0:T(8,128)S(1)}) custom-call(s32[8]{0:T(128)S(1)} %copy-done.8, bf16[256,3584]{1,0:T(8,128)(2,1)S(1)} %bitcast.8, bf16[30,3712]{1,0:T(8,128)(2,1)S(1)} %copy-done.1, bf16[18,3712]{1,0:T(8,128)(2,1)S(1)} %copy-done.2), custom_call_target="tpu_custom_call" | custom-call | bytes 4398112 | tf_op jit(solution)/shard_map/pallas_call | solution.py:396
  16.1 0.0 collective-permute-done.near_ref.refs_2_
  16.1 1.1 %collective-permute-done.1.far_ref.refs_3_ = bf16[24,3712]{1,0:T(8,128)(2,1)S(1)} collective-permute-done((bf16[24,3712]{1,0:T(8,128)(2,1)}, bf16[24,3712]{1,0:T(8,128)(2,1)S(1)}, u32[]{:S(2)}, u32[]{:S(2)}) %collective-permute-start.1) | collective-permute-done | bytes 178208 | tf_op jit(solution)/shard_map/ppermute | solution.py:408
  17.2 0.0 collective-permute-done.3.refs_1_
  17.2 1.3 %collective-permute-done.2.line_ref.refs_6_ = bf16[24,3712]{1,0:T(8,128)(2,1)S(1)} collective-permute-done((bf16[24,3712]{1,0:T(8,128)(2,1)}, bf16[24,3712]{1,0:T(8,128)(2,1)S(1)}, u32[]{:S(2)}, u32[]{:S(2)}) %collective-permute-start.2) | collective-permute-done | bytes 178208 | tf_op jit(solution)/shard_map/ppermute | solution.py:408
  18.5 0.1 shard_map.96
  18.7 1.6 %collective-permute-start.4 = (bf16[48,3712]{1,0:T(8,128)(2,1)S(1)}, bf16[48,3712]{1,0:T(8,128)(2,1)S(1)}, u32[]{:S(2)}, u32[]{:S(2)}) collective-permute-start(bf16[48,3712]{1,0:T(8,128)(2,1)S(1)} %get-tuple-element.51), channel_id=1, source_target_pairs={{0,2},{2,0},{4,6},{6,4},{8,10},{10,8},{12,14},{14,12},{1,3},{3,1},... | collective-permute-start | bytes 1069064 | tf_op jit(solution)/shard_map/ppermute | solution.py:408
  20.2 0.4 collective-permute-start.6
  20.7 1.3 %collective-permute-start.5 = (bf16[24,1920]{1,0:T(8,128)(2,1)S(1)}, bf16[24,1920]{1,0:T(8,128)(2,1)S(1)}, u32[]{:S(2)}, u32[]{:S(2)}) collective-permute-start(bf16[24,1920]{1,0:T(8,128)(2,1)S(1)} %get-tuple-element.52), channel_id=1, source_target_pairs={{0,12},{2,14},{4,8},{6,10},{8,4},{10,6},{12,0},{14,2},{1,13},{3,15... | collective-permute-start | bytes 276488 | tf_op jit(solution)/shard_map/ppermute | solution.py:408
  22.0 4.5 %collective-permute-done.6.refs_0_ = bf16[24,3712]{1,0:T(8,128)(2,1)S(1)} collective-permute-done((bf16[24,3712]{1,0:T(8,128)(2,1)S(1)}, bf16[24,3712]{1,0:T(8,128)(2,1)S(1)}, u32[]{:S(2)}, u32[]{:S(2)}) %collective-permute-start.6) | collective-permute-done | bytes 178208 | tf_op jit(solution)/shard_map/ppermute | solution.py:408
  26.5 0.0 collective-permute-start.7
  26.5 0.4 collective-permute-start.8
  26.9 2.9 %collective-permute-start.9 = (bf16[24,1920]{1,0:T(8,128)(2,1)S(1)}, bf16[24,1920]{1,0:T(8,128)(2,1)S(1)}, u32[]{:S(2)}, u32[]{:S(2)}) collective-permute-start(bf16[24,1920]{1,0:T(8,128)(2,1)S(1)} %get-tuple-element.55), channel_id=1, source_target_pairs={{0,4},{2,6},{4,0},{6,2},{8,12},{10,14},{12,8},{14,10},{1,5},{3,7},... | collective-permute-start | bytes 276488 | tf_op jit(solution)/shard_map/ppermute | solution.py:408
  29.8 0.0 collective-permute-done.5.refs_5_
  29.8 0.0 collective-permute-done.4.refs_4_
  29.8 0.8 %shard_map.97 = (bf16[176,3712]{1,0:T(8,128)(2,1)S(1)}, f32[176,128]{1,0:T(8,128)S(1)}) custom-call(bf16[256,3584]{1,0:T(8,128)(2,1)S(1)} %get-tuple-element.43.w_ref, s32[30,128]{1,0:T(8,128)S(1)} %get-tuple-element.44.slot_ref, bf16[30,3712]{1,0:T(8,128)(2,1)S(1)} %get-tuple-element.45.refs_0_, bf16[24,3712]{1,0:T(8,128)(2,1)S(1)} %collective-permute-done.3.refs_1_, ...), custom_call_target="tpu_custom_call" | custom-call | flops 1291845632 | bytes 4631040 | tf_op jit(solution)/shard_map/pallas_call | solution.py:396
  30.6 2.3 %collective-permute-done.8.refs_2_ = bf16[24,1920]{1,0:T(8,128)(2,1)S(1)} collective-permute-done((bf16[24,1920]{1,0:T(8,128)(2,1)S(1)}, bf16[24,1920]{1,0:T(8,128)(2,1)S(1)}, u32[]{:S(2)}, u32[]{:S(2)}) %collective-permute-start.8) | collective-permute-done | bytes 92192 | tf_op jit(solution)/shard_map/ppermute | solution.py:408
  32.8 0.4 collective-permute-done.9.refs_3_
  33.3 0.0 collective-permute-done.7.refs_1_
  33.3 1.3 %shard_map.98 = (bf16[80,3712]{1,0:T(8,128)(2,1)S(1)}, bf16[256,128]{1,0:T(8,128)(2,1)}) custom-call(f32[176,128]{1,0:T(8,128)S(1)} %get-tuple-element.53.own_ref, bf16[256,3584]{1,0:T(8,128)(2,1)S(1)} %get-tuple-element.43.w_ref, s32[30,128]{1,0:T(8,128)S(1)} %get-tuple-element.44.slot_ref, bf16[24,3712]{1,0:T(8,128)(2,1)S(1)} %collective-permute-done.6.refs_0_, ...), custom_call_target="tpu_custom_call" | custom-call | flops 146800640 | bytes 3140608 | tf_op jit(solution)/shard_map/pallas_call | solution.py:396
  34.6 0.4 shard_map.99
  35.0 0.1 collective-permute-start.10
  35.1 4.2 %all-to-all-start = ((bf16[8,32,128]{2,1,0:T(8,128)(2,1)}), bf16[8,32,128]{2,1,0:T(8,128)(2,1)S(1)}, u32[]{:S(2)}, u32[]{:S(2)}) async-start(bf16[8,32,128]{2,1,0:T(8,128)(2,1)} %bitcast.4), calls=%async_computation | async-start | bytes 131072 | tf_op jit(solution)/shard_map/all_to_all | solution.py:487
  39.4 0.0 copy-start.3
  39.4 0.0 copy-start.4
  39.4 0.0 copy-start.5
  39.4 0.0 copy-start.6
  39.4 0.0 copy-start.7
  39.4 0.0 collective-permute-done.10.arrived_ref
  39.4 2.6 %shard_map.100 = bf16[256,1792]{1,0:T(8,128)(2,1)} custom-call(s32[30,128]{1,0:T(8,128)S(1)} %get-tuple-element.44.slot_ref, bf16[176,3712]{1,0:T(8,128)(2,1)S(1)} %get-tuple-element.57.early_ref, bf16[80,3712]{1,0:T(8,128)(2,1)S(1)} %get-tuple-element.58.late_ref, bf16[256,1792]{1,0:T(8,128)(2,1)} %collective-permute-done.10.arrived_ref), custom_call_target="tpu_custom_call" | custom-call | flops 6606028800 | bytes 3750912 | tf_op jit(solution)/shard_map/pallas_call | solution.py:396
  42.0 4.3 %all-to-all-done.back_ref = bf16[8,32,128]{2,1,0:T(8,128)(2,1)S(1)} async-done(((bf16[8,32,128]{2,1,0:T(8,128)(2,1)}), bf16[8,32,128]{2,1,0:T(8,128)(2,1)S(1)}, u32[]{:S(2)}, u32[]{:S(2)}) %all-to-all-start) | async-done | bytes 65568 | tf_op jit(solution)/shard_map/all_to_all | solution.py:487
  46.3 0.0 copy-done.3
  46.3 0.0 copy-done.4
  46.3 0.0 copy-done.5
  46.3 0.0 copy-done.6
  46.3 0.0 copy-done.7
  46.3 1.0 %shard_map.101 = (bf16[1024,128]{1,0:T(8,128)(2,1)}, bf16[8,128]{1,0:T(8,128)(2,1)}) custom-call(bf16[8,32,128]{2,1,0:T(8,128)(2,1)S(1)} %all-to-all-done.back_ref, f32[72,128]{1,0:T(8,128)S(1)} %copy-done.3, s32[72,128]{1,0:T(8,128)S(1)} %copy-done.4, f32[72,128]{1,0:T(8,128)S(1)} %copy-done.5, f32[72,128]{1,0:T(8,128)S(1)} %copy-done.6, s32[8,128]{1,0:T(8,128)S(1)} %bitcast.10), custom_call_target="tpu_custom_call" | custom-call | flops 18874368 | bytes 481280 | tf_op jit(solution)/shard_map/pallas_call | solution.py:396
Async XLA Ops:
  3.2 13.0 %collective-permute-start = (bf16[24,3712]{1,0:T(8,128)(2,1)}, bf16[24,3712]{1,0:T(8,128)(2,1)S(1)}, u32[]{:S(2)}, u32[]{:S(2)}) collective-permute-start(bf16[24,3712]{1,0:T(8,128)(2,1)} %get-tuple-element.35), channel_id=1, source_target_pairs={{0,4},{2,6},{4,0},{6,2},{8,12},{10,14},{12,8},{14,10},{1,5},{3,7},... | collective-permute-start | bytes 534536 | tf_op jit(solution)/shard_map/ppermute | solution.py:408
  6.2 11.0 %collective-permute-start.1 = (bf16[24,3712]{1,0:T(8,128)(2,1)}, bf16[24,3712]{1,0:T(8,128)(2,1)S(1)}, u32[]{:S(2)}, u32[]{:S(2)}) collective-permute-start(bf16[24,3712]{1,0:T(8,128)(2,1)} %get-tuple-element.35), channel_id=1, source_target_pairs={{0,8},{2,10},{4,12},{6,14},{8,0},{10,2},{12,4},{14,6},{1,9},{3,11}... | collective-permute-start | bytes 534536 | tf_op jit(solution)/shard_map/ppermute | solution.py:408
  8.8 8.4 %collective-permute-start.3 = (bf16[24,3712]{1,0:T(8,128)(2,1)}, bf16[24,3712]{1,0:T(8,128)(2,1)S(1)}, u32[]{:S(2)}, u32[]{:S(2)}) collective-permute-start(bf16[24,3712]{1,0:T(8,128)(2,1)} %get-tuple-element.35), channel_id=1, source_target_pairs={{0,2},{2,0},{4,6},{6,4},{8,10},{10,8},{12,14},{14,12},{1,3},{3,1},... | collective-permute-start | bytes 534536 | tf_op jit(solution)/shard_map/ppermute | solution.py:408
  10.3 8.2 %collective-permute-start.2 = (bf16[24,3712]{1,0:T(8,128)(2,1)}, bf16[24,3712]{1,0:T(8,128)(2,1)S(1)}, u32[]{:S(2)}, u32[]{:S(2)}) collective-permute-start(bf16[24,3712]{1,0:T(8,128)(2,1)} %get-tuple-element.36), channel_id=1, source_target_pairs={{0,2},{2,0},{4,6},{6,4},{8,10},{10,8},{12,14},{14,12},{1,3},{3,1},... | collective-permute-start | bytes 534536 | tf_op jit(solution)/shard_map/ppermute | solution.py:408
  10.9 1.5 %copy-start = (bf16[2,128,3584]{2,1,0:T(8,128)(2,1)S(1)}, bf16[2,128,3584]{2,1,0:T(8,128)(2,1)}, u32[]{:S(2)}) copy-start(bf16[2,128,3584]{2,1,0:T(8,128)(2,1)} %param.13) | copy-start | bytes 5505028
  12.4 0.9 %copy-start.1 = (bf16[30,3712]{1,0:T(8,128)(2,1)S(1)}, bf16[30,3712]{1,0:T(8,128)(2,1)}, u32[]{:S(2)}) copy-start(bf16[30,3712]{1,0:T(8,128)(2,1)} %get-tuple-element.37.own_hbm) | copy-start | bytes 668164
  13.3 0.9 %copy-start.2 = (bf16[18,3712]{1,0:T(8,128)(2,1)S(1)}, bf16[18,3712]{1,0:T(8,128)(2,1)}, u32[]{:S(2)}) copy-start(bf16[18,3712]{1,0:T(8,128)(2,1)} %get-tuple-element.38.even_hbm) | copy-start | bytes 400900
  14.2 0.7 %copy-start.8 = (s32[8]{0:T(128)S(1)}, s32[8]{0:T(128)}, u32[]{:S(2)}) copy-start(s32[8]{0:T(128)} %replica_ref.1) | copy-start | bytes 100
  18.7 11.1 %collective-permute-start.4 = (bf16[48,3712]{1,0:T(8,128)(2,1)S(1)}, bf16[48,3712]{1,0:T(8,128)(2,1)S(1)}, u32[]{:S(2)}, u32[]{:S(2)}) collective-permute-start(bf16[48,3712]{1,0:T(8,128)(2,1)S(1)} %get-tuple-element.51), channel_id=1, source_target_pairs={{0,2},{2,0},{4,6},{6,4},{8,10},{10,8},{12,14},{14,12},{1,3},{3,1},... | collective-permute-start | bytes 1069064 | tf_op jit(solution)/shard_map/ppermute | solution.py:408
  20.2 6.3 %collective-permute-start.6 = (bf16[24,3712]{1,0:T(8,128)(2,1)S(1)}, bf16[24,3712]{1,0:T(8,128)(2,1)S(1)}, u32[]{:S(2)}, u32[]{:S(2)}) collective-permute-start(bf16[24,3712]{1,0:T(8,128)(2,1)S(1)} %collective-permute-done.1.far_ref.refs_3_), channel_id=1, source_target_pairs={{0,4},{2,6},{4,0},{6,2},{8,12},{10,14},{12,8},{14,10},{1,5},{3,7},... | collective-permute-start | bytes 534536 | tf_op jit(solution)/shard_map/ppermute | solution.py:408
  20.7 9.1 %collective-permute-start.5 = (bf16[24,1920]{1,0:T(8,128)(2,1)S(1)}, bf16[24,1920]{1,0:T(8,128)(2,1)S(1)}, u32[]{:S(2)}, u32[]{:S(2)}) collective-permute-start(bf16[24,1920]{1,0:T(8,128)(2,1)S(1)} %get-tuple-element.52), channel_id=1, source_target_pairs={{0,12},{2,14},{4,8},{6,10},{8,4},{10,6},{12,0},{14,2},{1,13},{3,15... | collective-permute-start | bytes 276488 | tf_op jit(solution)/shard_map/ppermute | solution.py:408
  26.5 6.8 %collective-permute-start.7 = (bf16[24,3712]{1,0:T(8,128)(2,1)S(1)}, bf16[24,3712]{1,0:T(8,128)(2,1)S(1)}, u32[]{:S(2)}, u32[]{:S(2)}) collective-permute-start(bf16[24,3712]{1,0:T(8,128)(2,1)S(1)} %collective-permute-done.6.refs_0_), channel_id=1, source_target_pairs={{0,2},{2,0},{4,6},{6,4},{8,10},{10,8},{12,14},{14,12},{1,3},{3,1},... | collective-permute-start | bytes 534536 | tf_op jit(solution)/shard_map/ppermute | solution.py:408
  26.5 6.3 %collective-permute-start.8 = (bf16[24,1920]{1,0:T(8,128)(2,1)S(1)}, bf16[24,1920]{1,0:T(8,128)(2,1)S(1)}, u32[]{:S(2)}, u32[]{:S(2)}) collective-permute-start(bf16[24,1920]{1,0:T(8,128)(2,1)S(1)} %get-tuple-element.54), channel_id=1, source_target_pairs={{0,8},{2,10},{4,12},{6,14},{8,0},{10,2},{12,4},{14,6},{1,9},{3,11}... | collective-permute-start | bytes 276488 | tf_op jit(solution)/shard_map/ppermute | solution.py:408
  26.9 6.4 %collective-permute-start.9 = (bf16[24,1920]{1,0:T(8,128)(2,1)S(1)}, bf16[24,1920]{1,0:T(8,128)(2,1)S(1)}, u32[]{:S(2)}, u32[]{:S(2)}) collective-permute-start(bf16[24,1920]{1,0:T(8,128)(2,1)S(1)} %get-tuple-element.55), channel_id=1, source_target_pairs={{0,4},{2,6},{4,0},{6,2},{8,12},{10,14},{12,8},{14,10},{1,5},{3,7},... | collective-permute-start | bytes 276488 | tf_op jit(solution)/shard_map/ppermute | solution.py:408
  35.0 4.4 %collective-permute-start.10 = (bf16[256,1792]{1,0:T(8,128)(2,1)S(1)}, bf16[256,1792]{1,0:T(8,128)(2,1)}, u32[]{:S(2)}, u32[]{:S(2)}) collective-permute-start(bf16[256,1792]{1,0:T(8,128)(2,1)S(1)} %shard_map.99), channel_id=1, source_target_pairs={{0,1},{1,0},{2,3},{3,2},{4,5},{5,4},{6,7},{7,6},{8,9},{9,8},{10,11... | collective-permute-start | bytes 2752520 | tf_op jit(solution)/shard_map/ppermute | solution.py:496
  35.1 11.2 %all-to-all-start = ((bf16[8,32,128]{2,1,0:T(8,128)(2,1)}), bf16[8,32,128]{2,1,0:T(8,128)(2,1)S(1)}, u32[]{:S(2)}, u32[]{:S(2)}) async-start(bf16[8,32,128]{2,1,0:T(8,128)(2,1)} %bitcast.4), calls=%async_computation | async-start | bytes 131072 | tf_op jit(solution)/shard_map/all_to_all | solution.py:487
  39.4 6.9 %copy-start.3 = (f32[72,128]{1,0:T(8,128)S(1)}, f32[72,128]{1,0:T(8,128)}, u32[]{:S(2)}) copy-start(f32[72,128]{1,0:T(8,128)} %get-tuple-element.60.pick_ref) | copy-start | bytes 110596
  39.4 6.9 %copy-start.4 = (s32[72,128]{1,0:T(8,128)S(1)}, s32[72,128]{1,0:T(8,128)}, u32[]{:S(2)}) copy-start(s32[72,128]{1,0:T(8,128)} %get-tuple-element.61.expert_ref) | copy-start | bytes 110596
  39.4 6.9 %copy-start.5 = (f32[72,128]{1,0:T(8,128)S(1)}, f32[72,128]{1,0:T(8,128)}, u32[]{:S(2)}) copy-start(f32[72,128]{1,0:T(8,128)} %get-tuple-element.62.hs_ref) | copy-start | bytes 110596
  39.4 6.9 %copy-start.6 = (f32[72,128]{1,0:T(8,128)S(1)}, f32[72,128]{1,0:T(8,128)}, u32[]{:S(2)}) copy-start(f32[72,128]{1,0:T(8,128)} %get-tuple-element.63.ps_ref) | copy-start | bytes 110596
  39.4 6.9 %copy-start.7 = (s32[128,8]{0,1:T(8,128)S(1)}, s32[128,8]{0,1:T(8,128)}, u32[]{:S(2)}) copy-start(s32[128,8]{0,1:T(8,128)} %param.10) | copy-start | bytes 12292

commit v19 on v18

--- a/solution.py
+++ b/solution.py
@@ -458,22 +458,22 @@
     )
     onward = swap(to_beside, 1, dev_count)
     lines = [swap(a, m, dev_count) for a, m in zip(lines, even)]
-    pieces = {(0, HOME): (0, 0), (0, COPIES): (0, per_home), (1, COPIES): (1, 0), (1, HOME): (6, 0),
-              (2, COPIES): (2, 0), (4, COPIES): (3, 0), (5, COPIES): (4, 0), (3, COPIES): (4, copies),
-              (even[-1], HOME): (5, 0), (even[-1] + 1, HOME): (5, per_home)}
+    pieces = {(0, HOME): (0, 0), (0, COPIES): (0, per_home), (1, COPIES): (1, 0), (1, HOME): (5, 0),
+              (2, COPIES): (2, 0), (4, COPIES): (3, 0),
+              (even[-1], HOME): (4, 0), (even[-1] + 1, HOME): (4, per_home)}
     orders = [list(pieces)]
     height = padded(sum(per_home if kind == HOME else copies for _, kind in pieces))
     early_rows, own = call(
         functools.partial(early_kernel, *sizes, orders[0], pieces),
         (shape((height, d_model + width), BF16), shape((height, width), F32)),
-        [(vmem, a) for a in (w_held, slot, own_rows, beside, near, far, onward, lines[-1], line)],
-        flops=2 * height * d_model * local_count * width * 4,
+        [(vmem, a) for a in (w_held, slot, own_rows, beside, near, far, lines[-1], line)],
+        flops=2 * height * d_model * local_count * width,
     )
     far_across = swap(far_near, 1, dev_count)
-    arrays = [far_near, far_across, *lines[-2::-1]]
-    pieces = {(6, COPIES): (0, 0), (7, COPIES): (1, 0)}
+    arrays = [far_near, far_across, onward, *lines[-2::-1]]
+    pieces = {(6, COPIES): (0, 0), (7, COPIES): (1, 0), (5, COPIES): (2, 0), (3, COPIES): (2, copies)}
     for n, m in enumerate(even[-2::-1]):
-        pieces[m, HOME], pieces[m + 1, HOME] = ((2 + n, k * per_home) for k in range(2))
+        pieces[m, HOME], pieces[m + 1, HOME] = ((3 + n, k * per_home) for k in range(2))
     orders.append(list(pieces))
     height = padded(sum(per_home if kind == HOME else copies for _, kind in pieces))
     block = padded(per_home + copies)

time: 47.7 us -> 47.4 us (level)
  waiting for transfers between devices: 13.8 us -> 13.2 us
    ppermute x10, starting transfers between devices: 14.3 us -> 15.6 us  [swap(): return lax.ppermute(x, 'expert', [(i, i ^ bits) for i in range(count)])]
    all_to_all x1, starting transfers between devices: 4.25 us -> 3.36 us  [gather_body(): lax.all_to_all(back, 'expert', split_axis=0, concat_axis=0, tiled=True)]
    ppermute x10, waiting for transfers between devices: 9.57 us -> 8.93 us  [swap(): return lax.ppermute(x, 'expert', [(i, i ^ bits) for i in range(count)])]
where the time goes in v19:
time: 47.4 us; the launch traced here: 47.1 us
  starting transfers between devices  19 us (40%)
  waiting for transfers between devices  13.2 us (28%)
  Pallas kernels  10 us (21%)
  local copies, waits for them, and re-layouts  4.04 us (9%)
  between operations  0.77 us (2%)
    ppermute x10, starting transfers between devices, swap(): return lax.ppermute(x, 'expert', [(i, i ^ bits) for i in range(count)])  15.6 us
    pallas_call x8, Pallas kernels, call(): pl.pallas_call(kernel, out_shape=out_shape, in_specs=[pl.BlockSpec(memory...  10 us
    ppermute x10, waiting for transfers between devices, swap(): return lax.ppermute(x, 'expert', [(i, i ^ bits) for i in range(count)])  8.93 us
    all_to_all x1, waiting for transfers between devices, gather_body(): lax.all_to_all(back, 'expert', split_axis=0, concat_axis=0, tiled=True)  4.24 us
    unnamed x18, local copies, waits for them, and re-layouts  4.04 us
    all_to_all x1, starting transfers between devices, gather_body(): lax.all_to_all(back, 'expert', split_axis=0, concat_axis=0, tiled=True)  3.36 us
  transfers between devices with their start and end apart: 12, of which 6 were waited for; matrix products, arithmetic and copies ran while one was open for 0% of the time, Pallas kernels for 10%

profile of v19, /device:TPU:0, one launch (start us, length us, event | category | flops | bytes accessed | tf_op | source)
XLA Modules:
  0.0 47.1 jit_solution(4135539661260188448)
XLA Ops:
  0.6 2.5 %shard_map.94 = (f32[72,128]{1,0:T(8,128)}, s32[72,128]{1,0:T(8,128)}, f32[72,128]{1,0:T(8,128)}, f32[72,128]{1,0:T(8,128)}, bf16[24,3712]{1,0:T(8,128)(2,1)}, /...) custom-call(s32[8]{0:T(128)} %replica_ref.1, s32[1,8]{1,0:T(1,128)} %refs_1_.1, ...), custom_call_target="tpu_custom_call" | custom-call | flops 66060288 | bytes 2046016 | tf_op jit(solution)/shard_map/pallas_call | solution.py:396
  3.2 3.1 %collective-permute-start = (bf16[24,3712]{1,0:T(8,128)(2,1)}, bf16[24,3712]{1,0:T(8,128)(2,1)S(1)}, u32[]{:S(2)}, u32[]{:S(2)}) collective-permute-start(bf16[24,3712]{1,0:T(8,128)(2,1)} %get-tuple-element.35), channel_id=1, source_target_pairs={{0,4},{2,6},{4,0},{6,2},{8,12},{10,14},{12,8},{14,10},{1,5},{3,7},... | collective-permute-start | bytes 534536 | tf_op jit(solution)/shard_map/ppermute | solution.py:408
  6.2 2.6 %collective-permute-start.1 = (bf16[24,3712]{1,0:T(8,128)(2,1)}, bf16[24,3712]{1,0:T(8,128)(2,1)S(1)}, u32[]{:S(2)}, u32[]{:S(2)}) collective-permute-start(bf16[24,3712]{1,0:T(8,128)(2,1)} %get-tuple-element.35), channel_id=1, source_target_pairs={{0,8},{2,10},{4,12},{6,14},{8,0},{10,2},{12,4},{14,6},{1,9},{3,11}... | collective-permute-start | bytes 534536 | tf_op jit(solution)/shard_map/ppermute | solution.py:408
  8.8 1.5 %collective-permute-start.3 = (bf16[24,3712]{1,0:T(8,128)(2,1)}, bf16[24,3712]{1,0:T(8,128)(2,1)S(1)}, u32[]{:S(2)}, u32[]{:S(2)}) collective-permute-start(bf16[24,3712]{1,0:T(8,128)(2,1)} %get-tuple-element.35), channel_id=1, source_target_pairs={{0,2},{2,0},{4,6},{6,4},{8,10},{10,8},{12,14},{14,12},{1,3},{3,1},... | collective-permute-start | bytes 534536 | tf_op jit(solution)/shard_map/ppermute | solution.py:408
  10.3 0.5 %collective-permute-start.2 = (bf16[24,3712]{1,0:T(8,128)(2,1)}, bf16[24,3712]{1,0:T(8,128)(2,1)S(1)}, u32[]{:S(2)}, u32[]{:S(2)}) collective-permute-start(bf16[24,3712]{1,0:T(8,128)(2,1)} %get-tuple-element.36), channel_id=1, source_target_pairs={{0,2},{2,0},{4,6},{6,4},{8,10},{10,8},{12,14},{14,12},{1,3},{3,1},... | collective-permute-start | bytes 534536 | tf_op jit(solution)/shard_map/ppermute | solution.py:408
  10.9 0.0 copy-start
  10.9 1.5 %copy-done = bf16[2,128,3584]{2,1,0:T(8,128)(2,1)S(1)} copy-done((bf16[2,128,3584]{2,1,0:T(8,128)(2,1)S(1)}, bf16[2,128,3584]{2,1,0:T(8,128)(2,1)}, u32[]{:S(2)}) %copy-start) | copy-done | bytes 1835032
  12.4 0.0 copy-start.1
  12.4 0.9 %copy-done.1 = bf16[30,3712]{1,0:T(8,128)(2,1)S(1)} copy-done((bf16[30,3712]{1,0:T(8,128)(2,1)S(1)}, bf16[30,3712]{1,0:T(8,128)(2,1)}, u32[]{:S(2)}) %copy-start.1) | copy-done | bytes 222744
  13.3 0.0 copy-start.2
  13.3 0.9 %copy-done.2 = bf16[18,3712]{1,0:T(8,128)(2,1)S(1)} copy-done((bf16[18,3712]{1,0:T(8,128)(2,1)S(1)}, bf16[18,3712]{1,0:T(8,128)(2,1)}, u32[]{:S(2)}) %copy-start.2) | copy-done | bytes 133656
  14.2 0.0 copy-start.8
  14.2 0.7 %copy-done.8 = s32[8]{0:T(128)S(1)} copy-done((s32[8]{0:T(128)S(1)}, s32[8]{0:T(128)}, u32[]{:S(2)}) %copy-start.8) | copy-done | bytes 56
  14.9 1.2 %shard_map.95 = (bf16[30,3712]{1,0:T(8,128)(2,1)S(1)}, bf16[18,3712]{1,0:T(8,128)(2,1)S(1)}, bf16[256,3584]{1,0:T(8,128)(2,1)S(1)}, s32[30,128]{1,0:T(8,128)S(1)}) custom-call(s32[8]{0:T(128)S(1)} %copy-done.8, bf16[256,3584]{1,0:T(8,128)(2,1)S(1)} %bitcast.8, bf16[30,3712]{1,0:T(8,128)(2,1)S(1)} %copy-done.1, bf16[18,3712]{1,0:T(8,128)(2,1)S(1)} %copy-done.2), custom_call_target="tpu_custom_call" | custom-call | bytes 4398112 | tf_op jit(solution)/shard_map/pallas_call | solution.py:396
  16.1 0.0 collective-permute-done.near_ref.refs_2_
  16.1 1.1 %collective-permute-done.1.far_ref.refs_3_ = bf16[24,3712]{1,0:T(8,128)(2,1)S(1)} collective-permute-done((bf16[24,3712]{1,0:T(8,128)(2,1)}, bf16[24,3712]{1,0:T(8,128)(2,1)S(1)}, u32[]{:S(2)}, u32[]{:S(2)}) %collective-permute-start.1) | collective-permute-done | bytes 178208 | tf_op jit(solution)/shard_map/ppermute | solution.py:408
  17.2 0.0 collective-permute-done.3.refs_1_
  17.2 1.3 %collective-permute-done.2.line_ref.refs_5_ = bf16[24,3712]{1,0:T(8,128)(2,1)S(1)} collective-permute-done((bf16[24,3712]{1,0:T(8,128)(2,1)}, bf16[24,3712]{1,0:T(8,128)(2,1)S(1)}, u32[]{:S(2)}, u32[]{:S(2)}) %collective-permute-start.2) | collective-permute-done | bytes 178208 | tf_op jit(solution)/shard_map/ppermute | solution.py:408
  18.5 0.4 collective-permute-start.5
  19.0 0.1 shard_map.96
  19.1 1.6 %collective-permute-start.7 = (bf16[48,3712]{1,0:T(8,128)(2,1)S(1)}, bf16[48,3712]{1,0:T(8,128)(2,1)S(1)}, u32[]{:S(2)}, u32[]{:S(2)}) collective-permute-start(bf16[48,3712]{1,0:T(8,128)(2,1)S(1)} %get-tuple-element.53), channel_id=1, source_target_pairs={{0,2},{2,0},{4,6},{6,4},{8,10},{10,8},{12,14},{14,12},{1,3},{3,1},... | collective-permute-start | bytes 1069064 | tf_op jit(solution)/shard_map/ppermute | solution.py:408
  20.7 3.3 %collective-permute-done.5.refs_0_ = bf16[24,3712]{1,0:T(8,128)(2,1)S(1)} collective-permute-done((bf16[24,3712]{1,0:T(8,128)(2,1)S(1)}, bf16[24,3712]{1,0:T(8,128)(2,1)S(1)}, u32[]{:S(2)}, u32[]{:S(2)}) %collective-permute-start.5) | collective-permute-done | bytes 178208 | tf_op jit(solution)/shard_map/ppermute | solution.py:408
  24.0 1.5 %collective-permute-start.6 = (bf16[24,3712]{1,0:T(8,128)(2,1)S(1)}, bf16[24,3712]{1,0:T(8,128)(2,1)S(1)}, u32[]{:S(2)}, u32[]{:S(2)}) collective-permute-start(bf16[24,3712]{1,0:T(8,128)(2,1)S(1)} %collective-permute-done.5.refs_0_), channel_id=1, source_target_pairs={{0,2},{2,0},{4,6},{6,4},{8,10},{10,8},{12,14},{14,12},{1,3},{3,1},... | collective-permute-start | bytes 534536 | tf_op jit(solution)/shard_map/ppermute | solution.py:408
  25.5 1.1 %collective-permute-start.4 = (bf16[24,1920]{1,0:T(8,128)(2,1)S(1)}, bf16[24,1920]{1,0:T(8,128)(2,1)S(1)}, u32[]{:S(2)}, u32[]{:S(2)}) collective-permute-start(bf16[24,1920]{1,0:T(8,128)(2,1)S(1)} %get-tuple-element.51), channel_id=1, source_target_pairs={{0,12},{2,14},{4,8},{6,10},{8,4},{10,6},{12,0},{14,2},{1,13},{3,15... | collective-permute-start | bytes 276488 | tf_op jit(solution)/shard_map/ppermute | solution.py:408
  26.6 0.8 %collective-permute-start.8 = (bf16[24,1920]{1,0:T(8,128)(2,1)S(1)}, bf16[24,1920]{1,0:T(8,128)(2,1)S(1)}, u32[]{:S(2)}, u32[]{:S(2)}) collective-permute-start(bf16[24,1920]{1,0:T(8,128)(2,1)S(1)} %get-tuple-element.54), channel_id=1, source_target_pairs={{0,8},{2,10},{4,12},{6,14},{8,0},{10,2},{12,4},{14,6},{1,9},{3,11}... | collective-permute-start | bytes 276488 | tf_op jit(solution)/shard_map/ppermute | solution.py:408
  27.4 2.5 %collective-permute-start.9 = (bf16[24,1920]{1,0:T(8,128)(2,1)S(1)}, bf16[24,1920]{1,0:T(8,128)(2,1)S(1)}, u32[]{:S(2)}, u32[]{:S(2)}) collective-permute-start(bf16[24,1920]{1,0:T(8,128)(2,1)S(1)} %get-tuple-element.55), channel_id=1, source_target_pairs={{0,4},{2,6},{4,0},{6,2},{8,12},{10,14},{12,8},{14,10},{1,5},{3,7},... | collective-permute-start | bytes 276488 | tf_op jit(solution)/shard_map/ppermute | solution.py:408
  29.9 2.1 %collective-permute-done.4.refs_4_ = bf16[24,1920]{1,0:T(8,128)(2,1)S(1)} collective-permute-done((bf16[24,1920]{1,0:T(8,128)(2,1)S(1)}, bf16[24,1920]{1,0:T(8,128)(2,1)S(1)}, u32[]{:S(2)}, u32[]{:S(2)}) %collective-permute-start.4) | collective-permute-done | bytes 92192 | tf_op jit(solution)/shard_map/ppermute | solution.py:408
  32.0 0.7 %shard_map.97 = (bf16[128,3712]{1,0:T(8,128)(2,1)S(1)}, f32[128,128]{1,0:T(8,128)S(1)}) custom-call(bf16[256,3584]{1,0:T(8,128)(2,1)S(1)} %get-tuple-element.43.w_ref, s32[30,128]{1,0:T(8,128)S(1)} %get-tuple-element.44.slot_ref, bf16[30,3712]{1,0:T(8,128)(2,1)S(1)} %get-tuple-element.45.refs_0_, bf16[24,3712]{1,0:T(8,128)(2,1)S(1)} %collective-permute-done.3.refs_1_, ...), custom_call_target="tpu_custom_call" | custom-call | flops 234881024 | bytes 3893760 | tf_op jit(solution)/shard_map/pallas_call | solution.py:396
  32.7 1.1 %collective-permute-done.8.refs_3_ = bf16[24,1920]{1,0:T(8,128)(2,1)S(1)} collective-permute-done((bf16[24,1920]{1,0:T(8,128)(2,1)S(1)}, bf16[24,1920]{1,0:T(8,128)(2,1)S(1)}, u32[]{:S(2)}, u32[]{:S(2)}) %collective-permute-start.8) | collective-permute-done | bytes 92192 | tf_op jit(solution)/shard_map/ppermute | solution.py:408
  33.8 0.0 collective-permute-done.9.refs_4_
  33.8 0.0 collective-permute-done.7.refs_2_
  33.8 0.0 collective-permute-done.6.refs_1_
  33.8 1.4 %shard_map.98 = (bf16[128,3712]{1,0:T(8,128)(2,1)S(1)}, bf16[256,128]{1,0:T(8,128)(2,1)}) custom-call(f32[128,128]{1,0:T(8,128)S(1)} %get-tuple-element.52.own_ref, bf16[256,3584]{1,0:T(8,128)(2,1)S(1)} %get-tuple-element.43.w_ref, s32[30,128]{1,0:T(8,128)S(1)} %get-tuple-element.44.slot_ref, bf16[24,3712]{1,0:T(8,128)(2,1)S(1)} %collective-permute-done.5.refs_0_, ...), custom_call_target="tpu_custom_call" | custom-call | flops 234881024 | bytes 3828736 | tf_op jit(solution)/shard_map/pallas_call | solution.py:396
  35.2 0.4 shard_map.99
  35.7 0.1 collective-permute-start.10
  35.8 3.4 %all-to-all-start = ((bf16[8,32,128]{2,1,0:T(8,128)(2,1)}), bf16[8,32,128]{2,1,0:T(8,128)(2,1)S(1)}, u32[]{:S(2)}, u32[]{:S(2)}) async-start(bf16[8,32,128]{2,1,0:T(8,128)(2,1)} %bitcast.4), calls=%async_computation | async-start | bytes 131072 | tf_op jit(solution)/shard_map/all_to_all | solution.py:487
  39.1 0.0 copy-start.3
  39.1 0.0 copy-start.4
  39.2 0.0 copy-start.5
  39.2 0.0 copy-start.6
  39.2 0.0 copy-start.7
  39.2 0.0 collective-permute-done.10.arrived_ref
  39.2 2.6 %shard_map.100 = bf16[256,1792]{1,0:T(8,128)(2,1)} custom-call(s32[30,128]{1,0:T(8,128)S(1)} %get-tuple-element.44.slot_ref, bf16[128,3712]{1,0:T(8,128)(2,1)S(1)} %get-tuple-element.57.early_ref, bf16[128,3712]{1,0:T(8,128)(2,1)S(1)} %get-tuple-element.58.late_ref, bf16[256,1792]{1,0:T(8,128)(2,1)} %collective-permute-done.10.arrived_ref), custom_call_target="tpu_custom_call" | custom-call | flops 6606028800 | bytes 3750912 | tf_op jit(solution)/shard_map/pallas_call | solution.py:396
  41.8 4.2 %all-to-all-done.back_ref = bf16[8,32,128]{2,1,0:T(8,128)(2,1)S(1)} async-done(((bf16[8,32,128]{2,1,0:T(8,128)(2,1)}), bf16[8,32,128]{2,1,0:T(8,128)(2,1)S(1)}, u32[]{:S(2)}, u32[]{:S(2)}) %all-to-all-start) | async-done | bytes 65568 | tf_op jit(solution)/shard_map/all_to_all | solution.py:487
  46.0 0.0 copy-done.3
  46.0 0.0 copy-done.4
  46.0 0.0 copy-done.5
  46.0 0.0 copy-done.6
  46.0 0.0 copy-done.7
  46.1 1.0 %shard_map.101 = (bf16[1024,128]{1,0:T(8,128)(2,1)}, bf16[8,128]{1,0:T(8,128)(2,1)}) custom-call(bf16[8,32,128]{2,1,0:T(8,128)(2,1)S(1)} %all-to-all-done.back_ref, f32[72,128]{1,0:T(8,128)S(1)} %copy-done.3, s32[72,128]{1,0:T(8,128)S(1)} %copy-done.4, f32[72,128]{1,0:T(8,128)S(1)} %copy-done.5, f32[72,128]{1,0:T(8,128)S(1)} %copy-done.6, s32[8,128]{1,0:T(8,128)S(1)} %bitcast.10), custom_call_target="tpu_custom_call" | custom-call | flops 18874368 | bytes 481280 | tf_op jit(solution)/shard_map/pallas_call | solution.py:396
Async XLA Ops:
  3.2 13.0 %collective-permute-start = (bf16[24,3712]{1,0:T(8,128)(2,1)}, bf16[24,3712]{1,0:T(8,128)(2,1)S(1)}, u32[]{:S(2)}, u32[]{:S(2)}) collective-permute-start(bf16[24,3712]{1,0:T(8,128)(2,1)} %get-tuple-element.35), channel_id=1, source_target_pairs={{0,4},{2,6},{4,0},{6,2},{8,12},{10,14},{12,8},{14,10},{1,5},{3,7},... | collective-permute-start | bytes 534536 | tf_op jit(solution)/shard_map/ppermute | solution.py:408
  6.2 11.0 %collective-permute-start.1 = (bf16[24,3712]{1,0:T(8,128)(2,1)}, bf16[24,3712]{1,0:T(8,128)(2,1)S(1)}, u32[]{:S(2)}, u32[]{:S(2)}) collective-permute-start(bf16[24,3712]{1,0:T(8,128)(2,1)} %get-tuple-element.35), channel_id=1, source_target_pairs={{0,8},{2,10},{4,12},{6,14},{8,0},{10,2},{12,4},{14,6},{1,9},{3,11}... | collective-permute-start | bytes 534536 | tf_op jit(solution)/shard_map/ppermute | solution.py:408
  8.8 8.4 %collective-permute-start.3 = (bf16[24,3712]{1,0:T(8,128)(2,1)}, bf16[24,3712]{1,0:T(8,128)(2,1)S(1)}, u32[]{:S(2)}, u32[]{:S(2)}) collective-permute-start(bf16[24,3712]{1,0:T(8,128)(2,1)} %get-tuple-element.35), channel_id=1, source_target_pairs={{0,2},{2,0},{4,6},{6,4},{8,10},{10,8},{12,14},{14,12},{1,3},{3,1},... | collective-permute-start | bytes 534536 | tf_op jit(solution)/shard_map/ppermute | solution.py:408
  10.3 8.2 %collective-permute-start.2 = (bf16[24,3712]{1,0:T(8,128)(2,1)}, bf16[24,3712]{1,0:T(8,128)(2,1)S(1)}, u32[]{:S(2)}, u32[]{:S(2)}) collective-permute-start(bf16[24,3712]{1,0:T(8,128)(2,1)} %get-tuple-element.36), channel_id=1, source_target_pairs={{0,2},{2,0},{4,6},{6,4},{8,10},{10,8},{12,14},{14,12},{1,3},{3,1},... | collective-permute-start | bytes 534536 | tf_op jit(solution)/shard_map/ppermute | solution.py:408
  10.9 1.5 %copy-start = (bf16[2,128,3584]{2,1,0:T(8,128)(2,1)S(1)}, bf16[2,128,3584]{2,1,0:T(8,128)(2,1)}, u32[]{:S(2)}) copy-start(bf16[2,128,3584]{2,1,0:T(8,128)(2,1)} %param.13) | copy-start | bytes 5505028
  12.4 0.9 %copy-start.1 = (bf16[30,3712]{1,0:T(8,128)(2,1)S(1)}, bf16[30,3712]{1,0:T(8,128)(2,1)}, u32[]{:S(2)}) copy-start(bf16[30,3712]{1,0:T(8,128)(2,1)} %get-tuple-element.37.own_hbm) | copy-start | bytes 668164
  13.3 0.9 %copy-start.2 = (bf16[18,3712]{1,0:T(8,128)(2,1)S(1)}, bf16[18,3712]{1,0:T(8,128)(2,1)}, u32[]{:S(2)}) copy-start(bf16[18,3712]{1,0:T(8,128)(2,1)} %get-tuple-element.38.even_hbm) | copy-start | bytes 400900
  14.2 0.7 %copy-start.8 = (s32[8]{0:T(128)S(1)}, s32[8]{0:T(128)}, u32[]{:S(2)}) copy-start(s32[8]{0:T(128)} %replica_ref.1) | copy-start | bytes 100
  18.5 5.5 %collective-permute-start.5 = (bf16[24,3712]{1,0:T(8,128)(2,1)S(1)}, bf16[24,3712]{1,0:T(8,128)(2,1)S(1)}, u32[]{:S(2)}, u32[]{:S(2)}) collective-permute-start(bf16[24,3712]{1,0:T(8,128)(2,1)S(1)} %collective-permute-done.1.far_ref.refs_3_), channel_id=1, source_target_pairs={{0,4},{2,6},{4,0},{6,2},{8,12},{10,14},{12,8},{14,10},{1,5},{3,7},... | collective-permute-start | bytes 534536 | tf_op jit(solution)/shard_map/ppermute | solution.py:408
  19.1 14.7 %collective-permute-start.7 = (bf16[48,3712]{1,0:T(8,128)(2,1)S(1)}, bf16[48,3712]{1,0:T(8,128)(2,1)S(1)}, u32[]{:S(2)}, u32[]{:S(2)}) collective-permute-start(bf16[48,3712]{1,0:T(8,128)(2,1)S(1)} %get-tuple-element.53), channel_id=1, source_target_pairs={{0,2},{2,0},{4,6},{6,4},{8,10},{10,8},{12,14},{14,12},{1,3},{3,1},... | collective-permute-start | bytes 1069064 | tf_op jit(solution)/shard_map/ppermute | solution.py:408
  24.0 9.8 %collective-permute-start.6 = (bf16[24,3712]{1,0:T(8,128)(2,1)S(1)}, bf16[24,3712]{1,0:T(8,128)(2,1)S(1)}, u32[]{:S(2)}, u32[]{:S(2)}) collective-permute-start(bf16[24,3712]{1,0:T(8,128)(2,1)S(1)} %collective-permute-done.5.refs_0_), channel_id=1, source_target_pairs={{0,2},{2,0},{4,6},{6,4},{8,10},{10,8},{12,14},{14,12},{1,3},{3,1},... | collective-permute-start | bytes 534536 | tf_op jit(solution)/shard_map/ppermute | solution.py:408
  25.5 6.5 %collective-permute-start.4 = (bf16[24,1920]{1,0:T(8,128)(2,1)S(1)}, bf16[24,1920]{1,0:T(8,128)(2,1)S(1)}, u32[]{:S(2)}, u32[]{:S(2)}) collective-permute-start(bf16[24,1920]{1,0:T(8,128)(2,1)S(1)} %get-tuple-element.51), channel_id=1, source_target_pairs={{0,12},{2,14},{4,8},{6,10},{8,4},{10,6},{12,0},{14,2},{1,13},{3,15... | collective-permute-start | bytes 276488 | tf_op jit(solution)/shard_map/ppermute | solution.py:408
  26.6 7.2 %collective-permute-start.8 = (bf16[24,1920]{1,0:T(8,128)(2,1)S(1)}, bf16[24,1920]{1,0:T(8,128)(2,1)S(1)}, u32[]{:S(2)}, u32[]{:S(2)}) collective-permute-start(bf16[24,1920]{1,0:T(8,128)(2,1)S(1)} %get-tuple-element.54), channel_id=1, source_target_pairs={{0,8},{2,10},{4,12},{6,14},{8,0},{10,2},{12,4},{14,6},{1,9},{3,11}... | collective-permute-start | bytes 276488 | tf_op jit(solution)/shard_map/ppermute | solution.py:408
  27.4 6.4 %collective-permute-start.9 = (bf16[24,1920]{1,0:T(8,128)(2,1)S(1)}, bf16[24,1920]{1,0:T(8,128)(2,1)S(1)}, u32[]{:S(2)}, u32[]{:S(2)}) collective-permute-start(bf16[24,1920]{1,0:T(8,128)(2,1)S(1)} %get-tuple-element.55), channel_id=1, source_target_pairs={{0,4},{2,6},{4,0},{6,2},{8,12},{10,14},{12,8},{14,10},{1,5},{3,7},... | collective-permute-start | bytes 276488 | tf_op jit(solution)/shard_map/ppermute | solution.py:408
  35.7 3.5 %collective-permute-start.10 = (bf16[256,1792]{1,0:T(8,128)(2,1)S(1)}, bf16[256,1792]{1,0:T(8,128)(2,1)}, u32[]{:S(2)}, u32[]{:S(2)}) collective-permute-start(bf16[256,1792]{1,0:T(8,128)(2,1)S(1)} %shard_map.99), channel_id=1, source_target_pairs={{0,1},{1,0},{2,3},{3,2},{4,5},{5,4},{6,7},{7,6},{8,9},{9,8},{10,11... | collective-permute-start | bytes 2752520 | tf_op jit(solution)/shard_map/ppermute | solution.py:496
  35.8 10.3 %all-to-all-start = ((bf16[8,32,128]{2,1,0:T(8,128)(2,1)}), bf16[8,32,128]{2,1,0:T(8,128)(2,1)S(1)}, u32[]{:S(2)}, u32[]{:S(2)}) async-start(bf16[8,32,128]{2,1,0:T(8,128)(2,1)} %bitcast.4), calls=%async_computation | async-start | bytes 131072 | tf_op jit(solution)/shard_map/all_to_all | solution.py:487
  39.1 6.9 %copy-start.3 = (f32[72,128]{1,0:T(8,128)S(1)}, f32[72,128]{1,0:T(8,128)}, u32[]{:S(2)}) copy-start(f32[72,128]{1,0:T(8,128)} %get-tuple-element.60.pick_ref) | copy-start | bytes 110596
  39.1 6.9 %copy-start.4 = (s32[72,128]{1,0:T(8,128)S(1)}, s32[72,128]{1,0:T(8,128)}, u32[]{:S(2)}) copy-start(s32[72,128]{1,0:T(8,128)} %get-tuple-element.61.expert_ref) | copy-start | bytes 110596
  39.2 6.9 %copy-start.5 = (f32[72,128]{1,0:T(8,128)S(1)}, f32[72,128]{1,0:T(8,128)}, u32[]{:S(2)}) copy-start(f32[72,128]{1,0:T(8,128)} %get-tuple-element.62.hs_ref) | copy-start | bytes 110596
  39.2 6.9 %copy-start.6 = (f32[72,128]{1,0:T(8,128)S(1)}, f32[72,128]{1,0:T(8,128)}, u32[]{:S(2)}) copy-start(f32[72,128]{1,0:T(8,128)} %get-tuple-element.63.ps_ref) | copy-start | bytes 110596
  39.2 6.9 %copy-start.7 = (s32[128,8]{0,1:T(8,128)S(1)}, s32[128,8]{0,1:T(8,128)}, u32[]{:S(2)}) copy-start(s32[128,8]{0,1:T(8,128)} %param.10) | copy-start | bytes 12292

commit v20 on v16

--- a/solution.py
+++ b/solution.py
@@ -314,29 +314,32 @@
         line_ref[...] = folded(jnp.concatenate([even[span], beside[span]], axis=0)).astype(BF16)
 
 
+def place(order, value, per_home, per_copy, placed):
+    start = 0
+    for m, kind in order:
+        lower, size = (0, per_home) if kind == HOME else (per_home, per_copy)
+        placed[m, lower:lower + size] = value[start:start + size]
+        start += size
+
+
 def early_kernel(local_count, dev_count, order, pieces, w_ref, slot_ref, *refs):
     piece_refs, (rows_ref, own_ref) = refs[:-2], refs[-2:]
     per_home, per_copy = local_count * SLOT, dev_count * CAPR
     fill_rows(order, pieces, per_home, per_copy, piece_refs, rows_ref)
     slot = slots_of(order, slot_ref, per_home, rows_ref.shape[0])
-    own_ref[...] = own_columns(rows_ref, w_ref, slot, local_count)
-
-
-def late_kernel(local_count, dev_count, early, order, pieces, own_ref, w_ref, slot_ref, *refs):
-    piece_refs, (rows_ref, back_ref, passed) = refs[:-3], refs[-3:]
+    own_ref[...] = jnp.zeros_like(own_ref)
+    place(order, own_columns(rows_ref, w_ref, slot, local_count), per_home, per_copy, own_ref)
+
+
+def late_kernel(local_count, dev_count, order, pieces, own_ref, w_ref, slot_ref, *refs):
+    piece_refs, (rows_ref, back_ref, placed) = refs[:-3], refs[-3:]
     per_home, per_copy = local_count * SLOT, dev_count * CAPR
+    placed[...] = own_ref[...]
     fill_rows(order, pieces, per_home, per_copy, piece_refs, rows_ref)
-    own = own_columns(rows_ref, w_ref, slots_of(order, slot_ref, per_home, rows_ref.shape[0]), local_count)
-    if passed.shape[1] > per_home + per_copy:
-        passed[:, per_home + per_copy:] = jnp.zeros_like(passed[:, per_home + per_copy:])
-    for keys, value in ((early, own_ref[...]), (order, own)):
-        start = 0
-        for m, kind in keys:
-            lower, size = (0, per_home) if kind == HOME else (per_home, per_copy)
-            passed[m, lower:lower + size] = value[start:start + size]
-            start += size
+    slot = slots_of(order, slot_ref, per_home, rows_ref.shape[0])
+    place(order, own_columns(rows_ref, w_ref, slot, local_count), per_home, per_copy, placed)
     me = lax.axis_index("expert")
-    back = jnp.concatenate([passed[me ^ source] for source in range(dev_count)], axis=0)
+    back = jnp.concatenate([placed[me ^ source] for source in range(dev_count)], axis=0)
     back_ref[...] = back.astype(back_ref.dtype)
 
 
@@ -460,11 +463,11 @@
     pieces = {(0, HOME): (0, 0), (0, COPIES): (0, per_home), (1, COPIES): (1, 0), (1, HOME): (7, 0),
               (2, COPIES): (2, 0), (4, COPIES): (3, 0), (5, COPIES): (4, 0), (3, COPIES): (5, 0),
               (even[-1], HOME): (6, 0), (even[-1] + 1, HOME): (6, per_home)}
-    orders = [list(pieces)]
+    orders, block = [list(pieces)], padded(per_home + copies)
     height = padded(sum(per_home if kind == HOME else copies for _, kind in pieces))
     early_rows, own = call(
         functools.partial(early_kernel, *sizes, orders[0], pieces),
-        (shape((height, d_model + width), BF16), shape((height, width), F32)),
+        (shape((height, d_model + width), BF16), shape((dev_count, block, width), F32)),
         [(vmem, a) for a in (w_held, slot, own_rows, beside, near, far, far_beside, near_beside, lines[-1], line)],
         flops=2 * height * d_model * local_count * width,
     )
@@ -475,9 +478,8 @@
         pieces[m, HOME], pieces[m + 1, HOME] = ((2 + n, k * per_home) for k in range(2))
     orders.append(list(pieces))
     height = padded(sum(per_home if kind == HOME else copies for _, kind in pieces))
-    block = padded(per_home + copies)
     late_rows, back = call(
-        functools.partial(late_kernel, *sizes, *orders, pieces),
+        functools.partial(late_kernel, *sizes, orders[1], pieces),
         (shape((height, d_model + width), BF16), shape((dev_count * block, width), BF16)),
         [(vmem, a) for a in (own, w_held, slot, *arrays)],
         [vmem((dev_count, block, width), F32)],

time: 46.8 us -> 46.8 us (level)
  no operation moved by 1% of the time
where the time goes in v20:
time: 46.8 us; the launch traced here: 46.4 us
  starting transfers between devices  18.1 us (39%)
  waiting for transfers between devices  13.5 us (29%)
  Pallas kernels  10 us (21%)
  local copies, waits for them, and re-layouts  4.04 us (9%)
  between operations  0.77 us (2%)
    ppermute x11, starting transfers between devices, swap(): return lax.ppermute(x, 'expert', [(i, i ^ bits) for i in range(count)])  14.7 us
    pallas_call x8, Pallas kernels, call(): pl.pallas_call(kernel, out_shape=out_shape, in_specs=[pl.BlockSpec(memory...  10 us
    ppermute x11, waiting for transfers between devices, swap(): return lax.ppermute(x, 'expert', [(i, i ^ bits) for i in range(count)])  9.25 us
    all_to_all x1, waiting for transfers between devices, gather_body(): lax.all_to_all(back, 'expert', split_axis=0, concat_axis=0, tiled=True)  4.24 us
    unnamed x18, local copies, waits for them, and re-layouts  4.04 us
    all_to_all x1, starting transfers between devices, gather_body(): lax.all_to_all(back, 'expert', split_axis=0, concat_axis=0, tiled=True)  3.36 us
  transfers between devices with their start and end apart: 13, of which 7 were waited for; matrix products, arithmetic and copies ran while one was open for 0% of the time, Pallas kernels for 10%

profile of v20, /device:TPU:0, one launch (start us, length us, event | category | flops | bytes accessed | tf_op | source)
XLA Modules:
  0.0 46.4 jit_solution(5542526818918864738)
XLA Ops:
  0.6 2.5 %shard_map.94 = (f32[72,128]{1,0:T(8,128)}, s32[72,128]{1,0:T(8,128)}, f32[72,128]{1,0:T(8,128)}, f32[72,128]{1,0:T(8,128)}, bf16[24,3712]{1,0:T(8,128)(2,1)}, /...) custom-call(s32[8]{0:T(128)} %replica_ref.1, s32[1,8]{1,0:T(1,128)} %refs_1_.1, ...), custom_call_target="tpu_custom_call" | custom-call | flops 66060288 | bytes 2046016 | tf_op jit(solution)/shard_map/pallas_call | solution.py:399
  3.2 3.1 %collective-permute-start = (bf16[24,3712]{1,0:T(8,128)(2,1)}, bf16[24,3712]{1,0:T(8,128)(2,1)S(1)}, u32[]{:S(2)}, u32[]{:S(2)}) collective-permute-start(bf16[24,3712]{1,0:T(8,128)(2,1)} %get-tuple-element.34), channel_id=1, source_target_pairs={{0,4},{2,6},{4,0},{6,2},{8,12},{10,14},{12,8},{14,10},{1,5},{3,7},... | collective-permute-start | bytes 534536 | tf_op jit(solution)/shard_map/ppermute | solution.py:411
  6.2 2.6 %collective-permute-start.1 = (bf16[24,3712]{1,0:T(8,128)(2,1)}, bf16[24,3712]{1,0:T(8,128)(2,1)S(1)}, u32[]{:S(2)}, u32[]{:S(2)}) collective-permute-start(bf16[24,3712]{1,0:T(8,128)(2,1)} %get-tuple-element.34), channel_id=1, source_target_pairs={{0,8},{2,10},{4,12},{6,14},{8,0},{10,2},{12,4},{14,6},{1,9},{3,11}... | collective-permute-start | bytes 534536 | tf_op jit(solution)/shard_map/ppermute | solution.py:411
  8.8 1.5 %collective-permute-start.3 = (bf16[24,3712]{1,0:T(8,128)(2,1)}, bf16[24,3712]{1,0:T(8,128)(2,1)S(1)}, u32[]{:S(2)}, u32[]{:S(2)}) collective-permute-start(bf16[24,3712]{1,0:T(8,128)(2,1)} %get-tuple-element.34), channel_id=1, source_target_pairs={{0,2},{2,0},{4,6},{6,4},{8,10},{10,8},{12,14},{14,12},{1,3},{3,1},... | collective-permute-start | bytes 534536 | tf_op jit(solution)/shard_map/ppermute | solution.py:411
  10.3 0.5 %collective-permute-start.2 = (bf16[24,3712]{1,0:T(8,128)(2,1)}, bf16[24,3712]{1,0:T(8,128)(2,1)S(1)}, u32[]{:S(2)}, u32[]{:S(2)}) collective-permute-start(bf16[24,3712]{1,0:T(8,128)(2,1)} %get-tuple-element.35), channel_id=1, source_target_pairs={{0,2},{2,0},{4,6},{6,4},{8,10},{10,8},{12,14},{14,12},{1,3},{3,1},... | collective-permute-start | bytes 534536 | tf_op jit(solution)/shard_map/ppermute | solution.py:411
  10.9 0.0 copy-start
  10.9 1.5 %copy-done = bf16[2,128,3584]{2,1,0:T(8,128)(2,1)S(1)} copy-done((bf16[2,128,3584]{2,1,0:T(8,128)(2,1)S(1)}, bf16[2,128,3584]{2,1,0:T(8,128)(2,1)}, u32[]{:S(2)}) %copy-start) | copy-done | bytes 1835032
  12.4 0.0 copy-start.1
  12.4 0.9 %copy-done.1 = bf16[30,3712]{1,0:T(8,128)(2,1)S(1)} copy-done((bf16[30,3712]{1,0:T(8,128)(2,1)S(1)}, bf16[30,3712]{1,0:T(8,128)(2,1)}, u32[]{:S(2)}) %copy-start.1) | copy-done | bytes 222744
  13.3 0.0 copy-start.2
  13.3 0.9 %copy-done.2 = bf16[18,3712]{1,0:T(8,128)(2,1)S(1)} copy-done((bf16[18,3712]{1,0:T(8,128)(2,1)S(1)}, bf16[18,3712]{1,0:T(8,128)(2,1)}, u32[]{:S(2)}) %copy-start.2) | copy-done | bytes 133656
  14.2 0.0 copy-start.8
  14.2 0.7 %copy-done.8 = s32[8]{0:T(128)S(1)} copy-done((s32[8]{0:T(128)S(1)}, s32[8]{0:T(128)}, u32[]{:S(2)}) %copy-start.8) | copy-done | bytes 56
  14.9 1.2 %shard_map.95 = (bf16[30,3712]{1,0:T(8,128)(2,1)S(1)}, bf16[18,3712]{1,0:T(8,128)(2,1)S(1)}, bf16[256,3584]{1,0:T(8,128)(2,1)S(1)}, s32[30,128]{1,0:T(8,128)S(1)}) custom-call(s32[8]{0:T(128)S(1)} %copy-done.8, bf16[256,3584]{1,0:T(8,128)(2,1)S(1)} %bitcast.8, bf16[30,3712]{1,0:T(8,128)(2,1)S(1)} %copy-done.1, bf16[18,3712]{1,0:T(8,128)(2,1)S(1)} %copy-done.2), custom_call_target="tpu_custom_call" | custom-call | bytes 4398112 | tf_op jit(solution)/shard_map/pallas_call | solution.py:399
  16.1 0.0 collective-permute-done.refs_2_
  16.1 1.1 %collective-permute-done.1.refs_3_ = bf16[24,3712]{1,0:T(8,128)(2,1)S(1)} collective-permute-done((bf16[24,3712]{1,0:T(8,128)(2,1)}, bf16[24,3712]{1,0:T(8,128)(2,1)S(1)}, u32[]{:S(2)}, u32[]{:S(2)}) %collective-permute-start.1) | collective-permute-done | bytes 178208 | tf_op jit(solution)/shard_map/ppermute | solution.py:411
  17.2 0.0 collective-permute-done.3.refs_1_
  17.2 1.3 %collective-permute-done.2.beside_ref.refs_7_ = bf16[24,3712]{1,0:T(8,128)(2,1)S(1)} collective-permute-done((bf16[24,3712]{1,0:T(8,128)(2,1)}, bf16[24,3712]{1,0:T(8,128)(2,1)S(1)}, u32[]{:S(2)}, u32[]{:S(2)}) %collective-permute-start.2) | collective-permute-done | bytes 178208 | tf_op jit(solution)/shard_map/ppermute | solution.py:411
  18.5 0.4 collective-permute-start.7
  19.0 1.5 %collective-permute-start.4 = (bf16[24,3712]{1,0:T(8,128)(2,1)S(1)}, bf16[24,3712]{1,0:T(8,128)(2,1)S(1)}, u32[]{:S(2)}, u32[]{:S(2)}) collective-permute-start(bf16[24,3712]{1,0:T(8,128)(2,1)S(1)} %collective-permute-done.1.refs_3_), channel_id=1, source_target_pairs={{0,2},{2,0},{4,6},{6,4},{8,10},{10,8},{12,14},{14,12},{1,3},{3,1},... | collective-permute-start | bytes 534536 | tf_op jit(solution)/shard_map/ppermute | solution.py:411
  20.5 0.5 %collective-permute-start.5 = (bf16[24,3712]{1,0:T(8,128)(2,1)S(1)}, bf16[24,3712]{1,0:T(8,128)(2,1)S(1)}, u32[]{:S(2)}, u32[]{:S(2)}) collective-permute-start(bf16[24,3712]{1,0:T(8,128)(2,1)S(1)} %collective-permute-done.refs_2_), channel_id=1, source_target_pairs={{0,2},{2,0},{4,6},{6,4},{8,10},{10,8},{12,14},{14,12},{1,3},{3,1},... | collective-permute-start | bytes 534536 | tf_op jit(solution)/shard_map/ppermute | solution.py:411
  21.0 0.1 shard_map.96
  21.1 1.4 %collective-permute-start.6 = (bf16[24,1920]{1,0:T(8,128)(2,1)S(1)}, bf16[24,1920]{1,0:T(8,128)(2,1)S(1)}, u32[]{:S(2)}, u32[]{:S(2)}) collective-permute-start(bf16[24,1920]{1,0:T(8,128)(2,1)S(1)} %get-tuple-element.50), channel_id=1, source_target_pairs={{0,12},{2,14},{4,8},{6,10},{8,4},{10,6},{12,0},{14,2},{1,13},{3,15... | collective-permute-start | bytes 276488 | tf_op jit(solution)/shard_map/ppermute | solution.py:411
  22.6 2.4 %collective-permute-done.7.refs_0_ = bf16[24,3712]{1,0:T(8,128)(2,1)S(1)} collective-permute-done((bf16[24,3712]{1,0:T(8,128)(2,1)S(1)}, bf16[24,3712]{1,0:T(8,128)(2,1)S(1)}, u32[]{:S(2)}, u32[]{:S(2)}) %collective-permute-start.7) | collective-permute-done | bytes 178208 | tf_op jit(solution)/shard_map/ppermute | solution.py:411
  25.0 1.5 %collective-permute-start.8 = (bf16[24,3712]{1,0:T(8,128)(2,1)S(1)}, bf16[24,3712]{1,0:T(8,128)(2,1)S(1)}, u32[]{:S(2)}, u32[]{:S(2)}) collective-permute-start(bf16[24,3712]{1,0:T(8,128)(2,1)S(1)} %collective-permute-done.7.refs_0_), channel_id=1, source_target_pairs={{0,2},{2,0},{4,6},{6,4},{8,10},{10,8},{12,14},{14,12},{1,3},{3,1},... | collective-permute-start | bytes 534536 | tf_op jit(solution)/shard_map/ppermute | solution.py:411
  26.5 0.0 collective-permute-start.10
  26.5 2.1 %collective-permute-done.6.refs_6_ = bf16[24,1920]{1,0:T(8,128)(2,1)S(1)} collective-permute-done((bf16[24,1920]{1,0:T(8,128)(2,1)S(1)}, bf16[24,1920]{1,0:T(8,128)(2,1)S(1)}, u32[]{:S(2)}, u32[]{:S(2)}) %collective-permute-start.6) | collective-permute-done | bytes 92192 | tf_op jit(solution)/shard_map/ppermute | solution.py:411
  28.6 1.6 %collective-permute-start.9 = (bf16[24,1920]{1,0:T(8,128)(2,1)S(1)}, bf16[24,1920]{1,0:T(8,128)(2,1)S(1)}, u32[]{:S(2)}, u32[]{:S(2)}) collective-permute-start(bf16[24,1920]{1,0:T(8,128)(2,1)S(1)} %get-tuple-element.52), channel_id=1, source_target_pairs={{0,4},{2,6},{4,0},{6,2},{8,12},{10,14},{12,8},{14,10},{1,5},{3,7},... | collective-permute-start | bytes 276488 | tf_op jit(solution)/shard_map/ppermute | solution.py:411
  30.2 0.0 collective-permute-done.4.refs_4_
  30.2 0.0 collective-permute-done.5.refs_5_
  30.2 0.8 %shard_map.97 = (bf16[176,3712]{1,0:T(8,128)(2,1)S(1)}, f32[8,32,128]{2,1,0:T(8,128)S(1)}) custom-call(bf16[256,3584]{1,0:T(8,128)(2,1)S(1)} %get-tuple-element.42.w_ref, s32[30,128]{1,0:T(8,128)S(1)} %get-tuple-element.43.slot_ref, bf16[30,3712]{1,0:T(8,128)(2,1)S(1)} %get-tuple-element.44.refs_0_, bf16[24,3712]{1,0:T(8,128)(2,1)S(1)} %collective-permute-done.3.refs_1_, ...), custom_call_target="tpu_custom_call" | custom-call | flops 322961408 | bytes 4672000 | tf_op jit(solution)/shard_map/pallas_call | solution.py:399
  31.0 2.1 %collective-permute-done.10.refs_3_ = bf16[24,1920]{1,0:T(8,128)(2,1)S(1)} collective-permute-done((bf16[24,1920]{1,0:T(8,128)(2,1)S(1)}, bf16[24,1920]{1,0:T(8,128)(2,1)S(1)}, u32[]{:S(2)}, u32[]{:S(2)}) %collective-permute-start.10) | collective-permute-done | bytes 92192 | tf_op jit(solution)/shard_map/ppermute | solution.py:411
  33.0 0.2 collective-permute-done.9.refs_2_
  33.3 0.0 collective-permute-done.8.refs_1_
  33.3 1.3 %shard_map.98 = (bf16[80,3712]{1,0:T(8,128)(2,1)S(1)}, bf16[256,128]{1,0:T(8,128)(2,1)}) custom-call(f32[8,32,128]{2,1,0:T(8,128)S(1)} %get-tuple-element.51.own_ref, bf16[256,3584]{1,0:T(8,128)(2,1)S(1)} %get-tuple-element.42.w_ref, s32[30,128]{1,0:T(8,128)S(1)} %get-tuple-element.43.slot_ref, bf16[24,3712]{1,0:T(8,128)(2,1)S(1)} %collective-permute-done.7.refs_0_, ...), custom_call_target="tpu_custom_call" | custom-call | flops 146800640 | bytes 3181568 | tf_op jit(solution)/shard_map/pallas_call | solution.py:399
  34.6 0.4 shard_map.99
  35.1 0.1 collective-permute-start.11
  35.2 3.4 %all-to-all-start = ((bf16[8,32,128]{2,1,0:T(8,128)(2,1)}), bf16[8,32,128]{2,1,0:T(8,128)(2,1)S(1)}, u32[]{:S(2)}, u32[]{:S(2)}) async-start(bf16[8,32,128]{2,1,0:T(8,128)(2,1)} %bitcast.4), calls=%async_computation | async-start | bytes 131072 | tf_op jit(solution)/shard_map/all_to_all | solution.py:488
  38.5 0.0 copy-start.3
  38.5 0.0 copy-start.4
  38.5 0.0 copy-start.5
  38.6 0.0 copy-start.6
  38.6 0.0 copy-start.7
  38.6 0.0 collective-permute-done.11.arrived_ref
  38.6 2.6 %shard_map.100 = bf16[256,1792]{1,0:T(8,128)(2,1)} custom-call(s32[30,128]{1,0:T(8,128)S(1)} %get-tuple-element.43.slot_ref, bf16[176,3712]{1,0:T(8,128)(2,1)S(1)} %get-tuple-element.55.early_ref, bf16[80,3712]{1,0:T(8,128)(2,1)S(1)} %get-tuple-element.56.late_ref, bf16[256,1792]{1,0:T(8,128)(2,1)} %collective-permute-done.11.arrived_ref), custom_call_target="tpu_custom_call" | custom-call | flops 6606028800 | bytes 3750912 | tf_op jit(solution)/shard_map/pallas_call | solution.py:399
  41.2 4.2 %all-to-all-done.back_ref = bf16[8,32,128]{2,1,0:T(8,128)(2,1)S(1)} async-done(((bf16[8,32,128]{2,1,0:T(8,128)(2,1)}), bf16[8,32,128]{2,1,0:T(8,128)(2,1)S(1)}, u32[]{:S(2)}, u32[]{:S(2)}) %all-to-all-start) | async-done | bytes 65568 | tf_op jit(solution)/shard_map/all_to_all | solution.py:488
  45.4 0.0 copy-done.3
  45.4 0.0 copy-done.4
  45.4 0.0 copy-done.5
  45.4 0.0 copy-done.6
  45.4 0.0 copy-done.7
  45.4 1.0 %shard_map.101 = (bf16[1024,128]{1,0:T(8,128)(2,1)}, bf16[8,128]{1,0:T(8,128)(2,1)}) custom-call(bf16[8,32,128]{2,1,0:T(8,128)(2,1)S(1)} %all-to-all-done.back_ref, f32[72,128]{1,0:T(8,128)S(1)} %copy-done.3, s32[72,128]{1,0:T(8,128)S(1)} %copy-done.4, f32[72,128]{1,0:T(8,128)S(1)} %copy-done.5, f32[72,128]{1,0:T(8,128)S(1)} %copy-done.6, s32[8,128]{1,0:T(8,128)S(1)} %bitcast.10), custom_call_target="tpu_custom_call" | custom-call | flops 18874368 | bytes 481280 | tf_op jit(solution)/shard_map/pallas_call | solution.py:399
Async XLA Ops:
  3.2 13.0 %collective-permute-start = (bf16[24,3712]{1,0:T(8,128)(2,1)}, bf16[24,3712]{1,0:T(8,128)(2,1)S(1)}, u32[]{:S(2)}, u32[]{:S(2)}) collective-permute-start(bf16[24,3712]{1,0:T(8,128)(2,1)} %get-tuple-element.34), channel_id=1, source_target_pairs={{0,4},{2,6},{4,0},{6,2},{8,12},{10,14},{12,8},{14,10},{1,5},{3,7},... | collective-permute-start | bytes 534536 | tf_op jit(solution)/shard_map/ppermute | solution.py:411
  6.2 11.0 %collective-permute-start.1 = (bf16[24,3712]{1,0:T(8,128)(2,1)}, bf16[24,3712]{1,0:T(8,128)(2,1)S(1)}, u32[]{:S(2)}, u32[]{:S(2)}) collective-permute-start(bf16[24,3712]{1,0:T(8,128)(2,1)} %get-tuple-element.34), channel_id=1, source_target_pairs={{0,8},{2,10},{4,12},{6,14},{8,0},{10,2},{12,4},{14,6},{1,9},{3,11}... | collective-permute-start | bytes 534536 | tf_op jit(solution)/shard_map/ppermute | solution.py:411
  8.8 8.4 %collective-permute-start.3 = (bf16[24,3712]{1,0:T(8,128)(2,1)}, bf16[24,3712]{1,0:T(8,128)(2,1)S(1)}, u32[]{:S(2)}, u32[]{:S(2)}) collective-permute-start(bf16[24,3712]{1,0:T(8,128)(2,1)} %get-tuple-element.34), channel_id=1, source_target_pairs={{0,2},{2,0},{4,6},{6,4},{8,10},{10,8},{12,14},{14,12},{1,3},{3,1},... | collective-permute-start | bytes 534536 | tf_op jit(solution)/shard_map/ppermute | solution.py:411
  10.3 8.2 %collective-permute-start.2 = (bf16[24,3712]{1,0:T(8,128)(2,1)}, bf16[24,3712]{1,0:T(8,128)(2,1)S(1)}, u32[]{:S(2)}, u32[]{:S(2)}) collective-permute-start(bf16[24,3712]{1,0:T(8,128)(2,1)} %get-tuple-element.35), channel_id=1, source_target_pairs={{0,2},{2,0},{4,6},{6,4},{8,10},{10,8},{12,14},{14,12},{1,3},{3,1},... | collective-permute-start | bytes 534536 | tf_op jit(solution)/shard_map/ppermute | solution.py:411
  10.9 1.5 %copy-start = (bf16[2,128,3584]{2,1,0:T(8,128)(2,1)S(1)}, bf16[2,128,3584]{2,1,0:T(8,128)(2,1)}, u32[]{:S(2)}) copy-start(bf16[2,128,3584]{2,1,0:T(8,128)(2,1)} %param.13) | copy-start | bytes 5505028
  12.4 0.9 %copy-start.1 = (bf16[30,3712]{1,0:T(8,128)(2,1)S(1)}, bf16[30,3712]{1,0:T(8,128)(2,1)}, u32[]{:S(2)}) copy-start(bf16[30,3712]{1,0:T(8,128)(2,1)} %get-tuple-element.36.own_hbm) | copy-start | bytes 668164
  13.3 0.9 %copy-start.2 = (bf16[18,3712]{1,0:T(8,128)(2,1)S(1)}, bf16[18,3712]{1,0:T(8,128)(2,1)}, u32[]{:S(2)}) copy-start(bf16[18,3712]{1,0:T(8,128)(2,1)} %get-tuple-element.37.even_hbm) | copy-start | bytes 400900
  14.2 0.7 %copy-start.8 = (s32[8]{0:T(128)S(1)}, s32[8]{0:T(128)}, u32[]{:S(2)}) copy-start(s32[8]{0:T(128)} %replica_ref.1) | copy-start | bytes 100
  18.5 6.5 %collective-permute-start.7 = (bf16[24,3712]{1,0:T(8,128)(2,1)S(1)}, bf16[24,3712]{1,0:T(8,128)(2,1)S(1)}, u32[]{:S(2)}, u32[]{:S(2)}) collective-permute-start(bf16[24,3712]{1,0:T(8,128)(2,1)S(1)} %collective-permute-done.1.refs_3_), channel_id=1, source_target_pairs={{0,4},{2,6},{4,0},{6,2},{8,12},{10,14},{12,8},{14,10},{1,5},{3,7},... | collective-permute-start | bytes 534536 | tf_op jit(solution)/shard_map/ppermute | solution.py:411
  19.0 11.2 %collective-permute-start.4 = (bf16[24,3712]{1,0:T(8,128)(2,1)S(1)}, bf16[24,3712]{1,0:T(8,128)(2,1)S(1)}, u32[]{:S(2)}, u32[]{:S(2)}) collective-permute-start(bf16[24,3712]{1,0:T(8,128)(2,1)S(1)} %collective-permute-done.1.refs_3_), channel_id=1, source_target_pairs={{0,2},{2,0},{4,6},{6,4},{8,10},{10,8},{12,14},{14,12},{1,3},{3,1},... | collective-permute-start | bytes 534536 | tf_op jit(solution)/shard_map/ppermute | solution.py:411
  20.5 9.7 %collective-permute-start.5 = (bf16[24,3712]{1,0:T(8,128)(2,1)S(1)}, bf16[24,3712]{1,0:T(8,128)(2,1)S(1)}, u32[]{:S(2)}, u32[]{:S(2)}) collective-permute-start(bf16[24,3712]{1,0:T(8,128)(2,1)S(1)} %collective-permute-done.refs_2_), channel_id=1, source_target_pairs={{0,2},{2,0},{4,6},{6,4},{8,10},{10,8},{12,14},{14,12},{1,3},{3,1},... | collective-permute-start | bytes 534536 | tf_op jit(solution)/shard_map/ppermute | solution.py:411
  21.1 7.4 %collective-permute-start.6 = (bf16[24,1920]{1,0:T(8,128)(2,1)S(1)}, bf16[24,1920]{1,0:T(8,128)(2,1)S(1)}, u32[]{:S(2)}, u32[]{:S(2)}) collective-permute-start(bf16[24,1920]{1,0:T(8,128)(2,1)S(1)} %get-tuple-element.50), channel_id=1, source_target_pairs={{0,12},{2,14},{4,8},{6,10},{8,4},{10,6},{12,0},{14,2},{1,13},{3,15... | collective-permute-start | bytes 276488 | tf_op jit(solution)/shard_map/ppermute | solution.py:411
  25.0 8.3 %collective-permute-start.8 = (bf16[24,3712]{1,0:T(8,128)(2,1)S(1)}, bf16[24,3712]{1,0:T(8,128)(2,1)S(1)}, u32[]{:S(2)}, u32[]{:S(2)}) collective-permute-start(bf16[24,3712]{1,0:T(8,128)(2,1)S(1)} %collective-permute-done.7.refs_0_), channel_id=1, source_target_pairs={{0,2},{2,0},{4,6},{6,4},{8,10},{10,8},{12,14},{14,12},{1,3},{3,1},... | collective-permute-start | bytes 534536 | tf_op jit(solution)/shard_map/ppermute | solution.py:411
  26.5 6.5 %collective-permute-start.10 = (bf16[24,1920]{1,0:T(8,128)(2,1)S(1)}, bf16[24,1920]{1,0:T(8,128)(2,1)S(1)}, u32[]{:S(2)}, u32[]{:S(2)}) collective-permute-start(bf16[24,1920]{1,0:T(8,128)(2,1)S(1)} %get-tuple-element.53), channel_id=1, source_target_pairs={{0,8},{2,10},{4,12},{6,14},{8,0},{10,2},{12,4},{14,6},{1,9},{3,11}... | collective-permute-start | bytes 276488 | tf_op jit(solution)/shard_map/ppermute | solution.py:411
  28.6 4.7 %collective-permute-start.9 = (bf16[24,1920]{1,0:T(8,128)(2,1)S(1)}, bf16[24,1920]{1,0:T(8,128)(2,1)S(1)}, u32[]{:S(2)}, u32[]{:S(2)}) collective-permute-start(bf16[24,1920]{1,0:T(8,128)(2,1)S(1)} %get-tuple-element.52), channel_id=1, source_target_pairs={{0,4},{2,6},{4,0},{6,2},{8,12},{10,14},{12,8},{14,10},{1,5},{3,7},... | collective-permute-start | bytes 276488 | tf_op jit(solution)/shard_map/ppermute | solution.py:411
  35.1 3.5 %collective-permute-start.11 = (bf16[256,1792]{1,0:T(8,128)(2,1)S(1)}, bf16[256,1792]{1,0:T(8,128)(2,1)}, u32[]{:S(2)}, u32[]{:S(2)}) collective-permute-start(bf16[256,1792]{1,0:T(8,128)(2,1)S(1)} %shard_map.99), channel_id=1, source_target_pairs={{0,1},{1,0},{2,3},{3,2},{4,5},{5,4},{6,7},{7,6},{8,9},{9,8},{10,11... | collective-permute-start | bytes 2752520 | tf_op jit(solution)/shard_map/ppermute | solution.py:497
  35.2 10.3 %all-to-all-start = ((bf16[8,32,128]{2,1,0:T(8,128)(2,1)}), bf16[8,32,128]{2,1,0:T(8,128)(2,1)S(1)}, u32[]{:S(2)}, u32[]{:S(2)}) async-start(bf16[8,32,128]{2,1,0:T(8,128)(2,1)} %bitcast.4), calls=%async_computation | async-start | bytes 131072 | tf_op jit(solution)/shard_map/all_to_all | solution.py:488
  38.5 6.9 %copy-start.3 = (f32[72,128]{1,0:T(8,128)S(1)}, f32[72,128]{1,0:T(8,128)}, u32[]{:S(2)}) copy-start(f32[72,128]{1,0:T(8,128)} %get-tuple-element.58.pick_ref) | copy-start | bytes 110596
  38.5 6.9 %copy-start.4 = (s32[72,128]{1,0:T(8,128)S(1)}, s32[72,128]{1,0:T(8,128)}, u32[]{:S(2)}) copy-start(s32[72,128]{1,0:T(8,128)} %get-tuple-element.59.expert_ref) | copy-start | bytes 110596
  38.5 6.9 %copy-start.5 = (f32[72,128]{1,0:T(8,128)S(1)}, f32[72,128]{1,0:T(8,128)}, u32[]{:S(2)}) copy-start(f32[72,128]{1,0:T(8,128)} %get-tuple-element.60.hs_ref) | copy-start | bytes 110596
  38.6 6.9 %copy-start.6 = (f32[72,128]{1,0:T(8,128)S(1)}, f32[72,128]{1,0:T(8,128)}, u32[]{:S(2)}) copy-start(f32[72,128]{1,0:T(8,128)} %get-tuple-element.61.ps_ref) | copy-start | bytes 110596
  38.6 6.9 %copy-start.7 = (s32[128,8]{0,1:T(8,128)S(1)}, s32[128,8]{0,1:T(8,128)}, u32[]{:S(2)}) copy-start(s32[128,8]{0,1:T(8,128)} %param.10) | copy-start | bytes 12292

commit v21 on v20

--- a/solution.py
+++ b/solution.py
@@ -167,13 +167,13 @@
 
 
 def dispatch_kernel(local_count, dev_count, packing, *refs):
-    sources, refs = refs[:6], refs[6:]
-    pick_ref, expert_ref, hs_ref, ps_ref = refs[:4]
-    packed, (held, wide, sems) = refs[4:4 + len(packing)], (refs[-8:-2], refs[-2], refs[-1])
-    moves = [pltpu.make_async_copy(s, h, sems.at[n]) for n, (s, h) in enumerate(zip(sources, held))]
+    replica_ref, counts_ref, ids_ref, probs_ref, hid_hbm, cot_hbm = refs[:6]
+    pick_ref, expert_ref, hs_ref, ps_ref = refs[6:10]
+    packed, (hid_ref, cot_ref, wide, sems) = refs[10:-4], refs[-4:]
+    moves = [pltpu.make_async_copy(s, h, sems.at[n])
+             for n, (s, h) in enumerate(((hid_hbm, hid_ref), (cot_hbm, cot_ref)))]
     for move in moves:
         move.start()
-    replica_ref, counts_ref, ids_ref, probs_ref, hid_ref, cot_ref = held
     top, toks = ids_ref.shape
     per_home = local_count * SLOT
     homes = dev_count * per_home
@@ -184,8 +184,6 @@
     within = row % SLOT
     allowed = jnp.where(within < CAPH, 1, 0)
     before = jnp.where(iota((toks, toks), 0) < iota((toks, toks), 1), 1.0, 0.0).astype(BF16)
-    for move in moves[:3]:
-        move.wait()
     for d in range(dev_count):
         first = homes + d * CAPR
         mine = (row >= first) & (row < first + CAPR)
@@ -205,8 +203,7 @@
     pick = jnp.where((rank == wanted) & (allowed > 0), named, 0.0)
     pick_ref[...] = pick
     expert_ref[...] = expert
-    for move in moves[3:5]:
-        move.wait()
+    moves[0].wait()
     wide[...] = hid_ref[...].astype(F32)
     p_slot = jnp.zeros((slots, toks), F32)
     probs = probs_ref[...].astype(F32)
@@ -222,13 +219,14 @@
     hs_ref[...] = h_slot
     ps_ref[...] = jnp.broadcast_to(p_slot, ps_ref.shape)
     scaled = p_slot * h_slot
-    moves[5].wait()
+    moves[1].wait()
     rows = jnp.dot(pick.astype(BF16), cot_ref[...], preferred_element_type=F32)
     d_model = cot_ref.shape[1]
     for out_ref, blocks in zip(packed, packing):
         spans = [(homes, slots) if b == COPIES else (b * per_home, (b + 1) * per_home) for b in blocks]
-        out_ref[:, :d_model] = jnp.concatenate([rows[i:j] for i, j in spans], axis=0).astype(BF16)
-        out_ref[:, d_model:] = jnp.concatenate([scaled[i:j] for i, j in spans], axis=0).astype(BF16)
+        for columns, value in ((slice(0, d_model), rows), (slice(d_model, None), scaled)):
+            chosen = {span: value[span[0]:span[1]] for span in spans}
+            out_ref[:, columns] = stack(spans, chosen, out_ref.shape[0]).astype(BF16)
 
 
 def padded(rows):
@@ -431,13 +429,14 @@
     odd, even = range(1, dev_count, 2), range(2, dev_count, 2)
     packing = [[*odd], [COPIES], [0, COPIES], [*even]]
     sized = [sum(copies if b == COPIES else per_home for b in blocks) for blocks in packing]
+    sized[2:] = [padded(n) for n in sized[2:]]
     pick, expert, h_slot, p_slot, to_beside, copy_rows, own_rows, even_rows = call(
         functools.partial(dispatch_kernel, *sizes, packing),
         [shape((slots, toks), F32), shape((slots, toks), jnp.int32), shape((slots, width), F32),
          shape((slots, width), F32)] + [shape((n, d_model + width), BF16) for n in sized],
-        [(hbm, a) for a in sources],
-        [(smem if n < 2 else vmem)(a.shape, a.dtype) for n, a in enumerate(sources)]
-        + [vmem((toks * top, width), F32), pltpu.SemaphoreType.DMA((len(sources),))],
+        list(zip((smem, smem, vmem, vmem, hbm, hbm), sources)),
+        [vmem(a.shape, a.dtype) for a in sources[4:]]
+        + [vmem((toks * top, width), F32), pltpu.SemaphoreType.DMA((2,))],
         flops=2 * slots * toks * d_model,
         limit=60,
     )

time: 46.8 us -> 47.5 us (1.015)
  Pallas kernels: 10 us -> 10.8 us
    pallas_call x8, Pallas kernels: 10 us -> 10.8 us  [call(): pl.pallas_call(kernel, out_shape=out_shape, in_specs=[pl.BlockSpec(memory...]
where the time goes in v21:
time: 47.5 us; the launch traced here: 47.1 us
  starting transfers between devices  18.2 us (38%)
  waiting for transfers between devices  13.4 us (28%)
  Pallas kernels  10.8 us (23%)
  local copies, waits for them, and re-layouts  4.06 us (9%)
  between operations  0.77 us (2%)
    ppermute x11, starting transfers between devices, swap(): return lax.ppermute(x, 'expert', [(i, i ^ bits) for i in range(count)])  14.7 us
    pallas_call x8, Pallas kernels, call(): pl.pallas_call(kernel, out_shape=out_shape, in_specs=[pl.BlockSpec(memory...  10.8 us
    ppermute x11, waiting for transfers between devices, swap(): return lax.ppermute(x, 'expert', [(i, i ^ bits) for i in range(count)])  9.12 us
    all_to_all x1, waiting for transfers between devices, gather_body(): lax.all_to_all(back, 'expert', split_axis=0, concat_axis=0, tiled=True)  4.24 us
    unnamed x18, local copies, waits for them, and re-layouts  4.06 us
    all_to_all x1, starting transfers between devices, gather_body(): lax.all_to_all(back, 'expert', split_axis=0, concat_axis=0, tiled=True)  3.36 us
  transfers between devices with their start and end apart: 13, of which 7 were waited for; matrix products, arithmetic and copies ran while one was open for 0% of the time, Pallas kernels for 10%

profile of v21, /device:TPU:0, one launch (start us, length us, event | category | flops | bytes accessed | tf_op | source)
XLA Modules:
  0.0 47.1 jit_solution(8866865165830024781)
XLA Ops:
  0.6 3.2 %shard_map.94 = (f32[72,128]{1,0:T(8,128)}, s32[72,128]{1,0:T(8,128)}, f32[72,128]{1,0:T(8,128)}, f32[72,128]{1,0:T(8,128)}, bf16[24,3712]{1,0:T(8,128)(2,1)}, /...) custom-call(s32[8]{0:T(128)} %replica_ref.1, s32[1,8]{1,0:T(1,128)} %refs_1_.1, ...), custom_call_target="tpu_custom_call" | custom-call | flops 66060288 | bytes 2164800 | tf_op jit(solution)/shard_map/pallas_call | solution.py:397
  3.8 3.1 %collective-permute-start = (bf16[24,3712]{1,0:T(8,128)(2,1)}, bf16[24,3712]{1,0:T(8,128)(2,1)S(1)}, u32[]{:S(2)}, u32[]{:S(2)}) collective-permute-start(bf16[24,3712]{1,0:T(8,128)(2,1)} %get-tuple-element.34), channel_id=1, source_target_pairs={{0,4},{2,6},{4,0},{6,2},{8,12},{10,14},{12,8},{14,10},{1,5},{3,7},... | collective-permute-start | bytes 534536 | tf_op jit(solution)/shard_map/ppermute | solution.py:409
  6.9 2.6 %collective-permute-start.1 = (bf16[24,3712]{1,0:T(8,128)(2,1)}, bf16[24,3712]{1,0:T(8,128)(2,1)S(1)}, u32[]{:S(2)}, u32[]{:S(2)}) collective-permute-start(bf16[24,3712]{1,0:T(8,128)(2,1)} %get-tuple-element.34), channel_id=1, source_target_pairs={{0,8},{2,10},{4,12},{6,14},{8,0},{10,2},{12,4},{14,6},{1,9},{3,11}... | collective-permute-start | bytes 534536 | tf_op jit(solution)/shard_map/ppermute | solution.py:409
  9.5 1.5 %collective-permute-start.3 = (bf16[24,3712]{1,0:T(8,128)(2,1)}, bf16[24,3712]{1,0:T(8,128)(2,1)S(1)}, u32[]{:S(2)}, u32[]{:S(2)}) collective-permute-start(bf16[24,3712]{1,0:T(8,128)(2,1)} %get-tuple-element.34), channel_id=1, source_target_pairs={{0,2},{2,0},{4,6},{6,4},{8,10},{10,8},{12,14},{14,12},{1,3},{3,1},... | collective-permute-start | bytes 534536 | tf_op jit(solution)/shard_map/ppermute | solution.py:409
  11.0 0.5 %collective-permute-start.2 = (bf16[24,3712]{1,0:T(8,128)(2,1)}, bf16[24,3712]{1,0:T(8,128)(2,1)S(1)}, u32[]{:S(2)}, u32[]{:S(2)}) collective-permute-start(bf16[24,3712]{1,0:T(8,128)(2,1)} %get-tuple-element.35), channel_id=1, source_target_pairs={{0,2},{2,0},{4,6},{6,4},{8,10},{10,8},{12,14},{14,12},{1,3},{3,1},... | collective-permute-start | bytes 534536 | tf_op jit(solution)/shard_map/ppermute | solution.py:409
  11.5 0.0 copy-start
  11.5 1.5 %copy-done = bf16[2,128,3584]{2,1,0:T(8,128)(2,1)S(1)} copy-done((bf16[2,128,3584]{2,1,0:T(8,128)(2,1)S(1)}, bf16[2,128,3584]{2,1,0:T(8,128)(2,1)}, u32[]{:S(2)}) %copy-start) | copy-done | bytes 1835032
  13.0 0.0 copy-start.1
  13.0 0.9 %copy-done.1 = bf16[32,3712]{1,0:T(8,128)(2,1)S(1)} copy-done((bf16[32,3712]{1,0:T(8,128)(2,1)S(1)}, bf16[32,3712]{1,0:T(8,128)(2,1)}, u32[]{:S(2)}) %copy-start.1) | copy-done | bytes 237592
  14.0 0.0 copy-start.2
  14.0 0.9 %copy-done.2 = bf16[32,3712]{1,0:T(8,128)(2,1)S(1)} copy-done((bf16[32,3712]{1,0:T(8,128)(2,1)S(1)}, bf16[32,3712]{1,0:T(8,128)(2,1)}, u32[]{:S(2)}) %copy-start.2) | copy-done | bytes 237592
  14.9 0.0 copy-start.8
  14.9 0.7 %copy-done.8 = s32[8]{0:T(128)S(1)} copy-done((s32[8]{0:T(128)S(1)}, s32[8]{0:T(128)}, u32[]{:S(2)}) %copy-start.8) | copy-done | bytes 56
  15.6 1.3 %shard_map.95 = (bf16[32,3712]{1,0:T(8,128)(2,1)S(1)}, bf16[32,3712]{1,0:T(8,128)(2,1)S(1)}, bf16[256,3584]{1,0:T(8,128)(2,1)S(1)}, s32[30,128]{1,0:T(8,128)S(1)}) custom-call(s32[8]{0:T(128)S(1)} %copy-done.8, bf16[256,3584]{1,0:T(8,128)(2,1)S(1)} %bitcast.8, bf16[32,3712]{1,0:T(8,128)(2,1)S(1)} %copy-done.1, bf16[32,3712]{1,0:T(8,128)(2,1)S(1)} %copy-done.2), custom_call_target="tpu_custom_call" | custom-call | bytes 4635680 | tf_op jit(solution)/shard_map/pallas_call | solution.py:397
  16.9 0.0 collective-permute-done.refs_2_
  16.9 1.0 %collective-permute-done.1.refs_3_ = bf16[24,3712]{1,0:T(8,128)(2,1)S(1)} collective-permute-done((bf16[24,3712]{1,0:T(8,128)(2,1)}, bf16[24,3712]{1,0:T(8,128)(2,1)S(1)}, u32[]{:S(2)}, u32[]{:S(2)}) %collective-permute-start.1) | collective-permute-done | bytes 178208 | tf_op jit(solution)/shard_map/ppermute | solution.py:409
  17.9 0.0 collective-permute-done.3.refs_1_
  17.9 1.3 %collective-permute-done.2.beside_ref.refs_7_ = bf16[24,3712]{1,0:T(8,128)(2,1)S(1)} collective-permute-done((bf16[24,3712]{1,0:T(8,128)(2,1)}, bf16[24,3712]{1,0:T(8,128)(2,1)S(1)}, u32[]{:S(2)}, u32[]{:S(2)}) %collective-permute-start.2) | collective-permute-done | bytes 178208 | tf_op jit(solution)/shard_map/ppermute | solution.py:409
  19.2 0.4 collective-permute-start.7
  19.7 1.5 %collective-permute-start.4 = (bf16[24,3712]{1,0:T(8,128)(2,1)S(1)}, bf16[24,3712]{1,0:T(8,128)(2,1)S(1)}, u32[]{:S(2)}, u32[]{:S(2)}) collective-permute-start(bf16[24,3712]{1,0:T(8,128)(2,1)S(1)} %collective-permute-done.1.refs_3_), channel_id=1, source_target_pairs={{0,2},{2,0},{4,6},{6,4},{8,10},{10,8},{12,14},{14,12},{1,3},{3,1},... | collective-permute-start | bytes 534536 | tf_op jit(solution)/shard_map/ppermute | solution.py:409
  21.2 0.5 %collective-permute-start.5 = (bf16[24,3712]{1,0:T(8,128)(2,1)S(1)}, bf16[24,3712]{1,0:T(8,128)(2,1)S(1)}, u32[]{:S(2)}, u32[]{:S(2)}) collective-permute-start(bf16[24,3712]{1,0:T(8,128)(2,1)S(1)} %collective-permute-done.refs_2_), channel_id=1, source_target_pairs={{0,2},{2,0},{4,6},{6,4},{8,10},{10,8},{12,14},{14,12},{1,3},{3,1},... | collective-permute-start | bytes 534536 | tf_op jit(solution)/shard_map/ppermute | solution.py:409
  21.7 0.1 shard_map.96
  21.8 1.4 %collective-permute-start.6 = (bf16[24,1920]{1,0:T(8,128)(2,1)S(1)}, bf16[24,1920]{1,0:T(8,128)(2,1)S(1)}, u32[]{:S(2)}, u32[]{:S(2)}) collective-permute-start(bf16[24,1920]{1,0:T(8,128)(2,1)S(1)} %get-tuple-element.50), channel_id=1, source_target_pairs={{0,12},{2,14},{4,8},{6,10},{8,4},{10,6},{12,0},{14,2},{1,13},{3,15... | collective-permute-start | bytes 276488 | tf_op jit(solution)/shard_map/ppermute | solution.py:409
  23.2 2.4 %collective-permute-done.7.refs_0_ = bf16[24,3712]{1,0:T(8,128)(2,1)S(1)} collective-permute-done((bf16[24,3712]{1,0:T(8,128)(2,1)S(1)}, bf16[24,3712]{1,0:T(8,128)(2,1)S(1)}, u32[]{:S(2)}, u32[]{:S(2)}) %collective-permute-start.7) | collective-permute-done | bytes 178208 | tf_op jit(solution)/shard_map/ppermute | solution.py:409
  25.7 1.5 %collective-permute-start.8 = (bf16[24,3712]{1,0:T(8,128)(2,1)S(1)}, bf16[24,3712]{1,0:T(8,128)(2,1)S(1)}, u32[]{:S(2)}, u32[]{:S(2)}) collective-permute-start(bf16[24,3712]{1,0:T(8,128)(2,1)S(1)} %collective-permute-done.7.refs_0_), channel_id=1, source_target_pairs={{0,2},{2,0},{4,6},{6,4},{8,10},{10,8},{12,14},{14,12},{1,3},{3,1},... | collective-permute-start | bytes 534536 | tf_op jit(solution)/shard_map/ppermute | solution.py:409
  27.2 0.0 collective-permute-start.10
  27.2 2.0 %collective-permute-done.6.refs_6_ = bf16[24,1920]{1,0:T(8,128)(2,1)S(1)} collective-permute-done((bf16[24,1920]{1,0:T(8,128)(2,1)S(1)}, bf16[24,1920]{1,0:T(8,128)(2,1)S(1)}, u32[]{:S(2)}, u32[]{:S(2)}) %collective-permute-start.6) | collective-permute-done | bytes 92192 | tf_op jit(solution)/shard_map/ppermute | solution.py:409
  29.2 1.6 %collective-permute-start.9 = (bf16[24,1920]{1,0:T(8,128)(2,1)S(1)}, bf16[24,1920]{1,0:T(8,128)(2,1)S(1)}, u32[]{:S(2)}, u32[]{:S(2)}) collective-permute-start(bf16[24,1920]{1,0:T(8,128)(2,1)S(1)} %get-tuple-element.52), channel_id=1, source_target_pairs={{0,4},{2,6},{4,0},{6,2},{8,12},{10,14},{12,8},{14,10},{1,5},{3,7},... | collective-permute-start | bytes 276488 | tf_op jit(solution)/shard_map/ppermute | solution.py:409
  30.9 0.0 collective-permute-done.4.refs_4_
  30.9 0.0 collective-permute-done.5.refs_5_
  30.9 0.8 %shard_map.97 = (bf16[176,3712]{1,0:T(8,128)(2,1)S(1)}, f32[8,32,128]{2,1,0:T(8,128)S(1)}) custom-call(bf16[256,3584]{1,0:T(8,128)(2,1)S(1)} %get-tuple-element.42.w_ref, s32[30,128]{1,0:T(8,128)S(1)} %get-tuple-element.43.slot_ref, bf16[32,3712]{1,0:T(8,128)(2,1)S(1)} %get-tuple-element.44.refs_0_, bf16[24,3712]{1,0:T(8,128)(2,1)S(1)} %collective-permute-done.3.refs_1_, ...), custom_call_target="tpu_custom_call" | custom-call | flops 322961408 | bytes 4686848 | tf_op jit(solution)/shard_map/pallas_call | solution.py:397
  31.7 2.1 %collective-permute-done.10.refs_3_ = bf16[24,1920]{1,0:T(8,128)(2,1)S(1)} collective-permute-done((bf16[24,1920]{1,0:T(8,128)(2,1)S(1)}, bf16[24,1920]{1,0:T(8,128)(2,1)S(1)}, u32[]{:S(2)}, u32[]{:S(2)}) %collective-permute-start.10) | collective-permute-done | bytes 92192 | tf_op jit(solution)/shard_map/ppermute | solution.py:409
  33.7 0.3 collective-permute-done.9.refs_2_
  34.0 0.0 collective-permute-done.8.refs_1_
  34.0 1.3 %shard_map.98 = (bf16[80,3712]{1,0:T(8,128)(2,1)S(1)}, bf16[256,128]{1,0:T(8,128)(2,1)}) custom-call(f32[8,32,128]{2,1,0:T(8,128)S(1)} %get-tuple-element.51.own_ref, bf16[256,3584]{1,0:T(8,128)(2,1)S(1)} %get-tuple-element.42.w_ref, s32[30,128]{1,0:T(8,128)S(1)} %get-tuple-element.43.slot_ref, bf16[24,3712]{1,0:T(8,128)(2,1)S(1)} %collective-permute-done.7.refs_0_, ...), custom_call_target="tpu_custom_call" | custom-call | flops 146800640 | bytes 3181568 | tf_op jit(solution)/shard_map/pallas_call | solution.py:397
  35.3 0.4 shard_map.99
  35.8 0.1 collective-permute-start.11
  35.8 3.4 %all-to-all-start = ((bf16[8,32,128]{2,1,0:T(8,128)(2,1)}), bf16[8,32,128]{2,1,0:T(8,128)(2,1)S(1)}, u32[]{:S(2)}, u32[]{:S(2)}) async-start(bf16[8,32,128]{2,1,0:T(8,128)(2,1)} %bitcast.4), calls=%async_computation | async-start | bytes 131072 | tf_op jit(solution)/shard_map/all_to_all | solution.py:487
  39.2 0.0 copy-start.3
  39.2 0.0 copy-start.4
  39.2 0.0 copy-start.5
  39.2 0.0 copy-start.6
  39.3 0.0 copy-start.7
  39.3 0.0 collective-permute-done.11.arrived_ref
  39.3 2.6 %shard_map.100 = bf16[256,1792]{1,0:T(8,128)(2,1)} custom-call(s32[30,128]{1,0:T(8,128)S(1)} %get-tuple-element.43.slot_ref, bf16[176,3712]{1,0:T(8,128)(2,1)S(1)} %get-tuple-element.55.early_ref, bf16[80,3712]{1,0:T(8,128)(2,1)S(1)} %get-tuple-element.56.late_ref, bf16[256,1792]{1,0:T(8,128)(2,1)} %collective-permute-done.11.arrived_ref), custom_call_target="tpu_custom_call" | custom-call | flops 6606028800 | bytes 3750912 | tf_op jit(solution)/shard_map/pallas_call | solution.py:397
  41.9 4.2 %all-to-all-done.back_ref = bf16[8,32,128]{2,1,0:T(8,128)(2,1)S(1)} async-done(((bf16[8,32,128]{2,1,0:T(8,128)(2,1)}), bf16[8,32,128]{2,1,0:T(8,128)(2,1)S(1)}, u32[]{:S(2)}, u32[]{:S(2)}) %all-to-all-start) | async-done | bytes 65568 | tf_op jit(solution)/shard_map/all_to_all | solution.py:487
  46.1 0.0 copy-done.3
  46.1 0.0 copy-done.4
  46.1 0.0 copy-done.5
  46.1 0.0 copy-done.6
  46.1 0.0 copy-done.7
  46.1 1.0 %shard_map.101 = (bf16[1024,128]{1,0:T(8,128)(2,1)}, bf16[8,128]{1,0:T(8,128)(2,1)}) custom-call(bf16[8,32,128]{2,1,0:T(8,128)(2,1)S(1)} %all-to-all-done.back_ref, f32[72,128]{1,0:T(8,128)S(1)} %copy-done.3, s32[72,128]{1,0:T(8,128)S(1)} %copy-done.4, f32[72,128]{1,0:T(8,128)S(1)} %copy-done.5, f32[72,128]{1,0:T(8,128)S(1)} %copy-done.6, s32[8,128]{1,0:T(8,128)S(1)} %bitcast.10), custom_call_target="tpu_custom_call" | custom-call | flops 18874368 | bytes 481280 | tf_op jit(solution)/shard_map/pallas_call | solution.py:397
Async XLA Ops:
  3.8 13.1 %collective-permute-start = (bf16[24,3712]{1,0:T(8,128)(2,1)}, bf16[24,3712]{1,0:T(8,128)(2,1)S(1)}, u32[]{:S(2)}, u32[]{:S(2)}) collective-permute-start(bf16[24,3712]{1,0:T(8,128)(2,1)} %get-tuple-element.34), channel_id=1, source_target_pairs={{0,4},{2,6},{4,0},{6,2},{8,12},{10,14},{12,8},{14,10},{1,5},{3,7},... | collective-permute-start | bytes 534536 | tf_op jit(solution)/shard_map/ppermute | solution.py:409
  6.9 11.0 %collective-permute-start.1 = (bf16[24,3712]{1,0:T(8,128)(2,1)}, bf16[24,3712]{1,0:T(8,128)(2,1)S(1)}, u32[]{:S(2)}, u32[]{:S(2)}) collective-permute-start(bf16[24,3712]{1,0:T(8,128)(2,1)} %get-tuple-element.34), channel_id=1, source_target_pairs={{0,8},{2,10},{4,12},{6,14},{8,0},{10,2},{12,4},{14,6},{1,9},{3,11}... | collective-permute-start | bytes 534536 | tf_op jit(solution)/shard_map/ppermute | solution.py:409
  9.5 8.4 %collective-permute-start.3 = (bf16[24,3712]{1,0:T(8,128)(2,1)}, bf16[24,3712]{1,0:T(8,128)(2,1)S(1)}, u32[]{:S(2)}, u32[]{:S(2)}) collective-permute-start(bf16[24,3712]{1,0:T(8,128)(2,1)} %get-tuple-element.34), channel_id=1, source_target_pairs={{0,2},{2,0},{4,6},{6,4},{8,10},{10,8},{12,14},{14,12},{1,3},{3,1},... | collective-permute-start | bytes 534536 | tf_op jit(solution)/shard_map/ppermute | solution.py:409
  11.0 8.2 %collective-permute-start.2 = (bf16[24,3712]{1,0:T(8,128)(2,1)}, bf16[24,3712]{1,0:T(8,128)(2,1)S(1)}, u32[]{:S(2)}, u32[]{:S(2)}) collective-permute-start(bf16[24,3712]{1,0:T(8,128)(2,1)} %get-tuple-element.35), channel_id=1, source_target_pairs={{0,2},{2,0},{4,6},{6,4},{8,10},{10,8},{12,14},{14,12},{1,3},{3,1},... | collective-permute-start | bytes 534536 | tf_op jit(solution)/shard_map/ppermute | solution.py:409
  11.5 1.5 %copy-start = (bf16[2,128,3584]{2,1,0:T(8,128)(2,1)S(1)}, bf16[2,128,3584]{2,1,0:T(8,128)(2,1)}, u32[]{:S(2)}) copy-start(bf16[2,128,3584]{2,1,0:T(8,128)(2,1)} %param.13) | copy-start | bytes 5505028
  13.0 0.9 %copy-start.1 = (bf16[32,3712]{1,0:T(8,128)(2,1)S(1)}, bf16[32,3712]{1,0:T(8,128)(2,1)}, u32[]{:S(2)}) copy-start(bf16[32,3712]{1,0:T(8,128)(2,1)} %get-tuple-element.36.own_hbm) | copy-start | bytes 712708
  14.0 0.9 %copy-start.2 = (bf16[32,3712]{1,0:T(8,128)(2,1)S(1)}, bf16[32,3712]{1,0:T(8,128)(2,1)}, u32[]{:S(2)}) copy-start(bf16[32,3712]{1,0:T(8,128)(2,1)} %get-tuple-element.37.even_hbm) | copy-start | bytes 712708
  14.9 0.7 %copy-start.8 = (s32[8]{0:T(128)S(1)}, s32[8]{0:T(128)}, u32[]{:S(2)}) copy-start(s32[8]{0:T(128)} %replica_ref.1) | copy-start | bytes 100
  19.2 6.5 %collective-permute-start.7 = (bf16[24,3712]{1,0:T(8,128)(2,1)S(1)}, bf16[24,3712]{1,0:T(8,128)(2,1)S(1)}, u32[]{:S(2)}, u32[]{:S(2)}) collective-permute-start(bf16[24,3712]{1,0:T(8,128)(2,1)S(1)} %collective-permute-done.1.refs_3_), channel_id=1, source_target_pairs={{0,4},{2,6},{4,0},{6,2},{8,12},{10,14},{12,8},{14,10},{1,5},{3,7},... | collective-permute-start | bytes 534536 | tf_op jit(solution)/shard_map/ppermute | solution.py:409
  19.7 11.2 %collective-permute-start.4 = (bf16[24,3712]{1,0:T(8,128)(2,1)S(1)}, bf16[24,3712]{1,0:T(8,128)(2,1)S(1)}, u32[]{:S(2)}, u32[]{:S(2)}) collective-permute-start(bf16[24,3712]{1,0:T(8,128)(2,1)S(1)} %collective-permute-done.1.refs_3_), channel_id=1, source_target_pairs={{0,2},{2,0},{4,6},{6,4},{8,10},{10,8},{12,14},{14,12},{1,3},{3,1},... | collective-permute-start | bytes 534536 | tf_op jit(solution)/shard_map/ppermute | solution.py:409
  21.2 9.7 %collective-permute-start.5 = (bf16[24,3712]{1,0:T(8,128)(2,1)S(1)}, bf16[24,3712]{1,0:T(8,128)(2,1)S(1)}, u32[]{:S(2)}, u32[]{:S(2)}) collective-permute-start(bf16[24,3712]{1,0:T(8,128)(2,1)S(1)} %collective-permute-done.refs_2_), channel_id=1, source_target_pairs={{0,2},{2,0},{4,6},{6,4},{8,10},{10,8},{12,14},{14,12},{1,3},{3,1},... | collective-permute-start | bytes 534536 | tf_op jit(solution)/shard_map/ppermute | solution.py:409
  21.8 7.4 %collective-permute-start.6 = (bf16[24,1920]{1,0:T(8,128)(2,1)S(1)}, bf16[24,1920]{1,0:T(8,128)(2,1)S(1)}, u32[]{:S(2)}, u32[]{:S(2)}) collective-permute-start(bf16[24,1920]{1,0:T(8,128)(2,1)S(1)} %get-tuple-element.50), channel_id=1, source_target_pairs={{0,12},{2,14},{4,8},{6,10},{8,4},{10,6},{12,0},{14,2},{1,13},{3,15... | collective-permute-start | bytes 276488 | tf_op jit(solution)/shard_map/ppermute | solution.py:409
  25.7 8.3 %collective-permute-start.8 = (bf16[24,3712]{1,0:T(8,128)(2,1)S(1)}, bf16[24,3712]{1,0:T(8,128)(2,1)S(1)}, u32[]{:S(2)}, u32[]{:S(2)}) collective-permute-start(bf16[24,3712]{1,0:T(8,128)(2,1)S(1)} %collective-permute-done.7.refs_0_), channel_id=1, source_target_pairs={{0,2},{2,0},{4,6},{6,4},{8,10},{10,8},{12,14},{14,12},{1,3},{3,1},... | collective-permute-start | bytes 534536 | tf_op jit(solution)/shard_map/ppermute | solution.py:409
  27.2 6.5 %collective-permute-start.10 = (bf16[24,1920]{1,0:T(8,128)(2,1)S(1)}, bf16[24,1920]{1,0:T(8,128)(2,1)S(1)}, u32[]{:S(2)}, u32[]{:S(2)}) collective-permute-start(bf16[24,1920]{1,0:T(8,128)(2,1)S(1)} %get-tuple-element.53), channel_id=1, source_target_pairs={{0,8},{2,10},{4,12},{6,14},{8,0},{10,2},{12,4},{14,6},{1,9},{3,11}... | collective-permute-start | bytes 276488 | tf_op jit(solution)/shard_map/ppermute | solution.py:409
  29.2 4.7 %collective-permute-start.9 = (bf16[24,1920]{1,0:T(8,128)(2,1)S(1)}, bf16[24,1920]{1,0:T(8,128)(2,1)S(1)}, u32[]{:S(2)}, u32[]{:S(2)}) collective-permute-start(bf16[24,1920]{1,0:T(8,128)(2,1)S(1)} %get-tuple-element.52), channel_id=1, source_target_pairs={{0,4},{2,6},{4,0},{6,2},{8,12},{10,14},{12,8},{14,10},{1,5},{3,7},... | collective-permute-start | bytes 276488 | tf_op jit(solution)/shard_map/ppermute | solution.py:409
  35.8 3.5 %collective-permute-start.11 = (bf16[256,1792]{1,0:T(8,128)(2,1)S(1)}, bf16[256,1792]{1,0:T(8,128)(2,1)}, u32[]{:S(2)}, u32[]{:S(2)}) collective-permute-start(bf16[256,1792]{1,0:T(8,128)(2,1)S(1)} %shard_map.99), channel_id=1, source_target_pairs={{0,1},{1,0},{2,3},{3,2},{4,5},{5,4},{6,7},{7,6},{8,9},{9,8},{10,11... | collective-permute-start | bytes 2752520 | tf_op jit(solution)/shard_map/ppermute | solution.py:496
  35.8 10.3 %all-to-all-start = ((bf16[8,32,128]{2,1,0:T(8,128)(2,1)}), bf16[8,32,128]{2,1,0:T(8,128)(2,1)S(1)}, u32[]{:S(2)}, u32[]{:S(2)}) async-start(bf16[8,32,128]{2,1,0:T(8,128)(2,1)} %bitcast.4), calls=%async_computation | async-start | bytes 131072 | tf_op jit(solution)/shard_map/all_to_all | solution.py:487
  39.2 6.9 %copy-start.3 = (f32[72,128]{1,0:T(8,128)S(1)}, f32[72,128]{1,0:T(8,128)}, u32[]{:S(2)}) copy-start(f32[72,128]{1,0:T(8,128)} %get-tuple-element.58.pick_ref) | copy-start | bytes 110596
  39.2 6.9 %copy-start.4 = (s32[72,128]{1,0:T(8,128)S(1)}, s32[72,128]{1,0:T(8,128)}, u32[]{:S(2)}) copy-start(s32[72,128]{1,0:T(8,128)} %get-tuple-element.59.expert_ref) | copy-start | bytes 110596
  39.2 6.9 %copy-start.5 = (f32[72,128]{1,0:T(8,128)S(1)}, f32[72,128]{1,0:T(8,128)}, u32[]{:S(2)}) copy-start(f32[72,128]{1,0:T(8,128)} %get-tuple-element.60.hs_ref) | copy-start | bytes 110596
  39.2 6.9 %copy-start.6 = (f32[72,128]{1,0:T(8,128)S(1)}, f32[72,128]{1,0:T(8,128)}, u32[]{:S(2)}) copy-start(f32[72,128]{1,0:T(8,128)} %get-tuple-element.61.ps_ref) | copy-start | bytes 110596
  39.3 6.9 %copy-start.7 = (s32[128,8]{0,1:T(8,128)S(1)}, s32[128,8]{0,1:T(8,128)}, u32[]{:S(2)}) copy-start(s32[128,8]{0,1:T(8,128)} %param.10) | copy-start | bytes 12292

commit v22 on v20

--- a/solution.py
+++ b/solution.py
@@ -227,8 +227,9 @@
     d_model = cot_ref.shape[1]
     for out_ref, blocks in zip(packed, packing):
         spans = [(homes, slots) if b == COPIES else (b * per_home, (b + 1) * per_home) for b in blocks]
-        out_ref[:, :d_model] = jnp.concatenate([rows[i:j] for i, j in spans], axis=0).astype(BF16)
-        out_ref[:, d_model:] = jnp.concatenate([scaled[i:j] for i, j in spans], axis=0).astype(BF16)
+        for columns, value in ((slice(0, d_model), rows), (slice(d_model, None), scaled)):
+            chosen = {span: value[span[0]:span[1]] for span in spans}
+            out_ref[:, columns] = stack(spans, chosen, out_ref.shape[0]).astype(BF16)
 
 
 def padded(rows):
@@ -431,6 +432,7 @@
     odd, even = range(1, dev_count, 2), range(2, dev_count, 2)
     packing = [[*odd], [COPIES], [0, COPIES], [*even]]
     sized = [sum(copies if b == COPIES else per_home for b in blocks) for blocks in packing]
+    sized[2:] = [padded(n) for n in sized[2:]]
     pick, expert, h_slot, p_slot, to_beside, copy_rows, own_rows, even_rows = call(
         functools.partial(dispatch_kernel, *sizes, packing),
         [shape((slots, toks), F32), shape((slots, toks), jnp.int32), shape((slots, width), F32),

time: 46.8 us -> 46.8 us (level)
  no operation moved by 1% of the time
where the time goes in v22:
time: 46.8 us; the launch traced here: 46.5 us
  starting transfers between devices  18.1 us (39%)
  waiting for transfers between devices  13.4 us (29%)
  Pallas kernels  10.1 us (22%)
  local copies, waits for them, and re-layouts  4.06 us (9%)
  between operations  0.77 us (2%)
    ppermute x11, starting transfers between devices, swap(): return lax.ppermute(x, 'expert', [(i, i ^ bits) for i in range(count)])  14.7 us
    pallas_call x8, Pallas kernels, call(): pl.pallas_call(kernel, out_shape=out_shape, in_specs=[pl.BlockSpec(memory...  10.1 us
    ppermute x11, waiting for transfers between devices, swap(): return lax.ppermute(x, 'expert', [(i, i ^ bits) for i in range(count)])  9.14 us
    all_to_all x1, waiting for transfers between devices, gather_body(): lax.all_to_all(back, 'expert', split_axis=0, concat_axis=0, tiled=True)  4.24 us
    unnamed x18, local copies, waits for them, and re-layouts  4.06 us
    all_to_all x1, starting transfers between devices, gather_body(): lax.all_to_all(back, 'expert', split_axis=0, concat_axis=0, tiled=True)  3.36 us
  transfers between devices with their start and end apart: 13, of which 7 were waited for; matrix products, arithmetic and copies ran while one was open for 0% of the time, Pallas kernels for 10%

profile of v22, /device:TPU:0, one launch (start us, length us, event | category | flops | bytes accessed | tf_op | source)
XLA Modules:
  0.0 46.5 jit_solution(5536146091545748226)
XLA Ops:
  0.6 2.5 %shard_map.94 = (f32[72,128]{1,0:T(8,128)}, s32[72,128]{1,0:T(8,128)}, f32[72,128]{1,0:T(8,128)}, f32[72,128]{1,0:T(8,128)}, bf16[24,3712]{1,0:T(8,128)(2,1)}, /...) custom-call(s32[8]{0:T(128)} %replica_ref.1, s32[1,8]{1,0:T(1,128)} %refs_1_.1, ...), custom_call_target="tpu_custom_call" | custom-call | flops 66060288 | bytes 2164800 | tf_op jit(solution)/shard_map/pallas_call | solution.py:400
  3.2 3.1 %collective-permute-start = (bf16[24,3712]{1,0:T(8,128)(2,1)}, bf16[24,3712]{1,0:T(8,128)(2,1)S(1)}, u32[]{:S(2)}, u32[]{:S(2)}) collective-permute-start(bf16[24,3712]{1,0:T(8,128)(2,1)} %get-tuple-element.34), channel_id=1, source_target_pairs={{0,4},{2,6},{4,0},{6,2},{8,12},{10,14},{12,8},{14,10},{1,5},{3,7},... | collective-permute-start | bytes 534536 | tf_op jit(solution)/shard_map/ppermute | solution.py:412
  6.3 2.6 %collective-permute-start.1 = (bf16[24,3712]{1,0:T(8,128)(2,1)}, bf16[24,3712]{1,0:T(8,128)(2,1)S(1)}, u32[]{:S(2)}, u32[]{:S(2)}) collective-permute-start(bf16[24,3712]{1,0:T(8,128)(2,1)} %get-tuple-element.34), channel_id=1, source_target_pairs={{0,8},{2,10},{4,12},{6,14},{8,0},{10,2},{12,4},{14,6},{1,9},{3,11}... | collective-permute-start | bytes 534536 | tf_op jit(solution)/shard_map/ppermute | solution.py:412
  8.9 1.5 %collective-permute-start.3 = (bf16[24,3712]{1,0:T(8,128)(2,1)}, bf16[24,3712]{1,0:T(8,128)(2,1)S(1)}, u32[]{:S(2)}, u32[]{:S(2)}) collective-permute-start(bf16[24,3712]{1,0:T(8,128)(2,1)} %get-tuple-element.34), channel_id=1, source_target_pairs={{0,2},{2,0},{4,6},{6,4},{8,10},{10,8},{12,14},{14,12},{1,3},{3,1},... | collective-permute-start | bytes 534536 | tf_op jit(solution)/shard_map/ppermute | solution.py:412
  10.3 0.5 %collective-permute-start.2 = (bf16[24,3712]{1,0:T(8,128)(2,1)}, bf16[24,3712]{1,0:T(8,128)(2,1)S(1)}, u32[]{:S(2)}, u32[]{:S(2)}) collective-permute-start(bf16[24,3712]{1,0:T(8,128)(2,1)} %get-tuple-element.35), channel_id=1, source_target_pairs={{0,2},{2,0},{4,6},{6,4},{8,10},{10,8},{12,14},{14,12},{1,3},{3,1},... | collective-permute-start | bytes 534536 | tf_op jit(solution)/shard_map/ppermute | solution.py:412
  10.9 0.0 copy-start
  10.9 1.5 %copy-done = bf16[2,128,3584]{2,1,0:T(8,128)(2,1)S(1)} copy-done((bf16[2,128,3584]{2,1,0:T(8,128)(2,1)S(1)}, bf16[2,128,3584]{2,1,0:T(8,128)(2,1)}, u32[]{:S(2)}) %copy-start) | copy-done | bytes 1835032
  12.4 0.0 copy-start.1
  12.4 0.9 %copy-done.1 = bf16[32,3712]{1,0:T(8,128)(2,1)S(1)} copy-done((bf16[32,3712]{1,0:T(8,128)(2,1)S(1)}, bf16[32,3712]{1,0:T(8,128)(2,1)}, u32[]{:S(2)}) %copy-start.1) | copy-done | bytes 237592
  13.3 0.0 copy-start.2
  13.3 0.9 %copy-done.2 = bf16[32,3712]{1,0:T(8,128)(2,1)S(1)} copy-done((bf16[32,3712]{1,0:T(8,128)(2,1)S(1)}, bf16[32,3712]{1,0:T(8,128)(2,1)}, u32[]{:S(2)}) %copy-start.2) | copy-done | bytes 237592
  14.3 0.0 copy-start.8
  14.3 0.7 %copy-done.8 = s32[8]{0:T(128)S(1)} copy-done((s32[8]{0:T(128)S(1)}, s32[8]{0:T(128)}, u32[]{:S(2)}) %copy-start.8) | copy-done | bytes 56
  14.9 1.3 %shard_map.95 = (bf16[32,3712]{1,0:T(8,128)(2,1)S(1)}, bf16[32,3712]{1,0:T(8,128)(2,1)S(1)}, bf16[256,3584]{1,0:T(8,128)(2,1)S(1)}, s32[30,128]{1,0:T(8,128)S(1)}) custom-call(s32[8]{0:T(128)S(1)} %copy-done.8, bf16[256,3584]{1,0:T(8,128)(2,1)S(1)} %bitcast.8, bf16[32,3712]{1,0:T(8,128)(2,1)S(1)} %copy-done.1, bf16[32,3712]{1,0:T(8,128)(2,1)S(1)} %copy-done.2), custom_call_target="tpu_custom_call" | custom-call | bytes 4635680 | tf_op jit(solution)/shard_map/pallas_call | solution.py:400
  16.2 0.0 collective-permute-done.refs_2_
  16.3 1.0 %collective-permute-done.1.refs_3_ = bf16[24,3712]{1,0:T(8,128)(2,1)S(1)} collective-permute-done((bf16[24,3712]{1,0:T(8,128)(2,1)}, bf16[24,3712]{1,0:T(8,128)(2,1)S(1)}, u32[]{:S(2)}, u32[]{:S(2)}) %collective-permute-start.1) | collective-permute-done | bytes 178208 | tf_op jit(solution)/shard_map/ppermute | solution.py:412
  17.2 0.0 collective-permute-done.3.refs_1_
  17.2 1.3 %collective-permute-done.2.beside_ref.refs_7_ = bf16[24,3712]{1,0:T(8,128)(2,1)S(1)} collective-permute-done((bf16[24,3712]{1,0:T(8,128)(2,1)}, bf16[24,3712]{1,0:T(8,128)(2,1)S(1)}, u32[]{:S(2)}, u32[]{:S(2)}) %collective-permute-start.2) | collective-permute-done | bytes 178208 | tf_op jit(solution)/shard_map/ppermute | solution.py:412
  18.6 0.4 collective-permute-start.7
  19.0 1.5 %collective-permute-start.4 = (bf16[24,3712]{1,0:T(8,128)(2,1)S(1)}, bf16[24,3712]{1,0:T(8,128)(2,1)S(1)}, u32[]{:S(2)}, u32[]{:S(2)}) collective-permute-start(bf16[24,3712]{1,0:T(8,128)(2,1)S(1)} %collective-permute-done.1.refs_3_), channel_id=1, source_target_pairs={{0,2},{2,0},{4,6},{6,4},{8,10},{10,8},{12,14},{14,12},{1,3},{3,1},... | collective-permute-start | bytes 534536 | tf_op jit(solution)/shard_map/ppermute | solution.py:412
  20.5 0.5 %collective-permute-start.5 = (bf16[24,3712]{1,0:T(8,128)(2,1)S(1)}, bf16[24,3712]{1,0:T(8,128)(2,1)S(1)}, u32[]{:S(2)}, u32[]{:S(2)}) collective-permute-start(bf16[24,3712]{1,0:T(8,128)(2,1)S(1)} %collective-permute-done.refs_2_), channel_id=1, source_target_pairs={{0,2},{2,0},{4,6},{6,4},{8,10},{10,8},{12,14},{14,12},{1,3},{3,1},... | collective-permute-start | bytes 534536 | tf_op jit(solution)/shard_map/ppermute | solution.py:412
  21.0 0.1 shard_map.96
  21.2 1.4 %collective-permute-start.6 = (bf16[24,1920]{1,0:T(8,128)(2,1)S(1)}, bf16[24,1920]{1,0:T(8,128)(2,1)S(1)}, u32[]{:S(2)}, u32[]{:S(2)}) collective-permute-start(bf16[24,1920]{1,0:T(8,128)(2,1)S(1)} %get-tuple-element.50), channel_id=1, source_target_pairs={{0,12},{2,14},{4,8},{6,10},{8,4},{10,6},{12,0},{14,2},{1,13},{3,15... | collective-permute-start | bytes 276488 | tf_op jit(solution)/shard_map/ppermute | solution.py:412
  22.6 2.4 %collective-permute-done.7.refs_0_ = bf16[24,3712]{1,0:T(8,128)(2,1)S(1)} collective-permute-done((bf16[24,3712]{1,0:T(8,128)(2,1)S(1)}, bf16[24,3712]{1,0:T(8,128)(2,1)S(1)}, u32[]{:S(2)}, u32[]{:S(2)}) %collective-permute-start.7) | collective-permute-done | bytes 178208 | tf_op jit(solution)/shard_map/ppermute | solution.py:412
  25.0 1.5 %collective-permute-start.8 = (bf16[24,3712]{1,0:T(8,128)(2,1)S(1)}, bf16[24,3712]{1,0:T(8,128)(2,1)S(1)}, u32[]{:S(2)}, u32[]{:S(2)}) collective-permute-start(bf16[24,3712]{1,0:T(8,128)(2,1)S(1)} %collective-permute-done.7.refs_0_), channel_id=1, source_target_pairs={{0,2},{2,0},{4,6},{6,4},{8,10},{10,8},{12,14},{14,12},{1,3},{3,1},... | collective-permute-start | bytes 534536 | tf_op jit(solution)/shard_map/ppermute | solution.py:412
  26.5 0.0 collective-permute-start.10
  26.5 2.1 %collective-permute-done.6.refs_6_ = bf16[24,1920]{1,0:T(8,128)(2,1)S(1)} collective-permute-done((bf16[24,1920]{1,0:T(8,128)(2,1)S(1)}, bf16[24,1920]{1,0:T(8,128)(2,1)S(1)}, u32[]{:S(2)}, u32[]{:S(2)}) %collective-permute-start.6) | collective-permute-done | bytes 92192 | tf_op jit(solution)/shard_map/ppermute | solution.py:412
  28.6 1.6 %collective-permute-start.9 = (bf16[24,1920]{1,0:T(8,128)(2,1)S(1)}, bf16[24,1920]{1,0:T(8,128)(2,1)S(1)}, u32[]{:S(2)}, u32[]{:S(2)}) collective-permute-start(bf16[24,1920]{1,0:T(8,128)(2,1)S(1)} %get-tuple-element.52), channel_id=1, source_target_pairs={{0,4},{2,6},{4,0},{6,2},{8,12},{10,14},{12,8},{14,10},{1,5},{3,7},... | collective-permute-start | bytes 276488 | tf_op jit(solution)/shard_map/ppermute | solution.py:412
  30.2 0.0 collective-permute-done.4.refs_4_
  30.2 0.0 collective-permute-done.5.refs_5_
  30.2 0.8 %shard_map.97 = (bf16[176,3712]{1,0:T(8,128)(2,1)S(1)}, f32[8,32,128]{2,1,0:T(8,128)S(1)}) custom-call(bf16[256,3584]{1,0:T(8,128)(2,1)S(1)} %get-tuple-element.42.w_ref, s32[30,128]{1,0:T(8,128)S(1)} %get-tuple-element.43.slot_ref, bf16[32,3712]{1,0:T(8,128)(2,1)S(1)} %get-tuple-element.44.refs_0_, bf16[24,3712]{1,0:T(8,128)(2,1)S(1)} %collective-permute-done.3.refs_1_, ...), custom_call_target="tpu_custom_call" | custom-call | flops 322961408 | bytes 4686848 | tf_op jit(solution)/shard_map/pallas_call | solution.py:400
  31.0 2.1 %collective-permute-done.10.refs_3_ = bf16[24,1920]{1,0:T(8,128)(2,1)S(1)} collective-permute-done((bf16[24,1920]{1,0:T(8,128)(2,1)S(1)}, bf16[24,1920]{1,0:T(8,128)(2,1)S(1)}, u32[]{:S(2)}, u32[]{:S(2)}) %collective-permute-start.10) | collective-permute-done | bytes 92192 | tf_op jit(solution)/shard_map/ppermute | solution.py:412
  33.1 0.2 collective-permute-done.9.refs_2_
  33.3 0.0 collective-permute-done.8.refs_1_
  33.3 1.3 %shard_map.98 = (bf16[80,3712]{1,0:T(8,128)(2,1)S(1)}, bf16[256,128]{1,0:T(8,128)(2,1)}) custom-call(f32[8,32,128]{2,1,0:T(8,128)S(1)} %get-tuple-element.51.own_ref, bf16[256,3584]{1,0:T(8,128)(2,1)S(1)} %get-tuple-element.42.w_ref, s32[30,128]{1,0:T(8,128)S(1)} %get-tuple-element.43.slot_ref, bf16[24,3712]{1,0:T(8,128)(2,1)S(1)} %collective-permute-done.7.refs_0_, ...), custom_call_target="tpu_custom_call" | custom-call | flops 146800640 | bytes 3181568 | tf_op jit(solution)/shard_map/pallas_call | solution.py:400
  34.6 0.4 shard_map.99
  35.1 0.1 collective-permute-start.11
  35.2 3.4 %all-to-all-start = ((bf16[8,32,128]{2,1,0:T(8,128)(2,1)}), bf16[8,32,128]{2,1,0:T(8,128)(2,1)S(1)}, u32[]{:S(2)}, u32[]{:S(2)}) async-start(bf16[8,32,128]{2,1,0:T(8,128)(2,1)} %bitcast.4), calls=%async_computation | async-start | bytes 131072 | tf_op jit(solution)/shard_map/all_to_all | solution.py:490
  38.5 0.0 copy-start.3
  38.6 0.0 copy-start.4
  38.6 0.0 copy-start.5
  38.6 0.0 copy-start.6
  38.6 0.0 copy-start.7
  38.6 0.0 collective-permute-done.11.arrived_ref
  38.6 2.6 %shard_map.100 = bf16[256,1792]{1,0:T(8,128)(2,1)} custom-call(s32[30,128]{1,0:T(8,128)S(1)} %get-tuple-element.43.slot_ref, bf16[176,3712]{1,0:T(8,128)(2,1)S(1)} %get-tuple-element.55.early_ref, bf16[80,3712]{1,0:T(8,128)(2,1)S(1)} %get-tuple-element.56.late_ref, bf16[256,1792]{1,0:T(8,128)(2,1)} %collective-permute-done.11.arrived_ref), custom_call_target="tpu_custom_call" | custom-call | flops 6606028800 | bytes 3750912 | tf_op jit(solution)/shard_map/pallas_call | solution.py:400
  41.2 4.2 %all-to-all-done.back_ref = bf16[8,32,128]{2,1,0:T(8,128)(2,1)S(1)} async-done(((bf16[8,32,128]{2,1,0:T(8,128)(2,1)}), bf16[8,32,128]{2,1,0:T(8,128)(2,1)S(1)}, u32[]{:S(2)}, u32[]{:S(2)}) %all-to-all-start) | async-done | bytes 65568 | tf_op jit(solution)/shard_map/all_to_all | solution.py:490
  45.4 0.0 copy-done.3
  45.4 0.0 copy-done.4
  45.4 0.0 copy-done.5
  45.4 0.0 copy-done.6
  45.4 0.0 copy-done.7
  45.5 1.0 %shard_map.101 = (bf16[1024,128]{1,0:T(8,128)(2,1)}, bf16[8,128]{1,0:T(8,128)(2,1)}) custom-call(bf16[8,32,128]{2,1,0:T(8,128)(2,1)S(1)} %all-to-all-done.back_ref, f32[72,128]{1,0:T(8,128)S(1)} %copy-done.3, s32[72,128]{1,0:T(8,128)S(1)} %copy-done.4, f32[72,128]{1,0:T(8,128)S(1)} %copy-done.5, f32[72,128]{1,0:T(8,128)S(1)} %copy-done.6, s32[8,128]{1,0:T(8,128)S(1)} %bitcast.10), custom_call_target="tpu_custom_call" | custom-call | flops 18874368 | bytes 481280 | tf_op jit(solution)/shard_map/pallas_call | solution.py:400
Async XLA Ops:
  3.2 13.1 %collective-permute-start = (bf16[24,3712]{1,0:T(8,128)(2,1)}, bf16[24,3712]{1,0:T(8,128)(2,1)S(1)}, u32[]{:S(2)}, u32[]{:S(2)}) collective-permute-start(bf16[24,3712]{1,0:T(8,128)(2,1)} %get-tuple-element.34), channel_id=1, source_target_pairs={{0,4},{2,6},{4,0},{6,2},{8,12},{10,14},{12,8},{14,10},{1,5},{3,7},... | collective-permute-start | bytes 534536 | tf_op jit(solution)/shard_map/ppermute | solution.py:412
  6.3 11.0 %collective-permute-start.1 = (bf16[24,3712]{1,0:T(8,128)(2,1)}, bf16[24,3712]{1,0:T(8,128)(2,1)S(1)}, u32[]{:S(2)}, u32[]{:S(2)}) collective-permute-start(bf16[24,3712]{1,0:T(8,128)(2,1)} %get-tuple-element.34), channel_id=1, source_target_pairs={{0,8},{2,10},{4,12},{6,14},{8,0},{10,2},{12,4},{14,6},{1,9},{3,11}... | collective-permute-start | bytes 534536 | tf_op jit(solution)/shard_map/ppermute | solution.py:412
  8.9 8.4 %collective-permute-start.3 = (bf16[24,3712]{1,0:T(8,128)(2,1)}, bf16[24,3712]{1,0:T(8,128)(2,1)S(1)}, u32[]{:S(2)}, u32[]{:S(2)}) collective-permute-start(bf16[24,3712]{1,0:T(8,128)(2,1)} %get-tuple-element.34), channel_id=1, source_target_pairs={{0,2},{2,0},{4,6},{6,4},{8,10},{10,8},{12,14},{14,12},{1,3},{3,1},... | collective-permute-start | bytes 534536 | tf_op jit(solution)/shard_map/ppermute | solution.py:412
  10.3 8.2 %collective-permute-start.2 = (bf16[24,3712]{1,0:T(8,128)(2,1)}, bf16[24,3712]{1,0:T(8,128)(2,1)S(1)}, u32[]{:S(2)}, u32[]{:S(2)}) collective-permute-start(bf16[24,3712]{1,0:T(8,128)(2,1)} %get-tuple-element.35), channel_id=1, source_target_pairs={{0,2},{2,0},{4,6},{6,4},{8,10},{10,8},{12,14},{14,12},{1,3},{3,1},... | collective-permute-start | bytes 534536 | tf_op jit(solution)/shard_map/ppermute | solution.py:412
  10.9 1.5 %copy-start = (bf16[2,128,3584]{2,1,0:T(8,128)(2,1)S(1)}, bf16[2,128,3584]{2,1,0:T(8,128)(2,1)}, u32[]{:S(2)}) copy-start(bf16[2,128,3584]{2,1,0:T(8,128)(2,1)} %param.13) | copy-start | bytes 5505028
  12.4 0.9 %copy-start.1 = (bf16[32,3712]{1,0:T(8,128)(2,1)S(1)}, bf16[32,3712]{1,0:T(8,128)(2,1)}, u32[]{:S(2)}) copy-start(bf16[32,3712]{1,0:T(8,128)(2,1)} %get-tuple-element.36.own_hbm) | copy-start | bytes 712708
  13.3 0.9 %copy-start.2 = (bf16[32,3712]{1,0:T(8,128)(2,1)S(1)}, bf16[32,3712]{1,0:T(8,128)(2,1)}, u32[]{:S(2)}) copy-start(bf16[32,3712]{1,0:T(8,128)(2,1)} %get-tuple-element.37.even_hbm) | copy-start | bytes 712708
  14.3 0.7 %copy-start.8 = (s32[8]{0:T(128)S(1)}, s32[8]{0:T(128)}, u32[]{:S(2)}) copy-start(s32[8]{0:T(128)} %replica_ref.1) | copy-start | bytes 100
  18.6 6.5 %collective-permute-start.7 = (bf16[24,3712]{1,0:T(8,128)(2,1)S(1)}, bf16[24,3712]{1,0:T(8,128)(2,1)S(1)}, u32[]{:S(2)}, u32[]{:S(2)}) collective-permute-start(bf16[24,3712]{1,0:T(8,128)(2,1)S(1)} %collective-permute-done.1.refs_3_), channel_id=1, source_target_pairs={{0,4},{2,6},{4,0},{6,2},{8,12},{10,14},{12,8},{14,10},{1,5},{3,7},... | collective-permute-start | bytes 534536 | tf_op jit(solution)/shard_map/ppermute | solution.py:412
  19.0 11.2 %collective-permute-start.4 = (bf16[24,3712]{1,0:T(8,128)(2,1)S(1)}, bf16[24,3712]{1,0:T(8,128)(2,1)S(1)}, u32[]{:S(2)}, u32[]{:S(2)}) collective-permute-start(bf16[24,3712]{1,0:T(8,128)(2,1)S(1)} %collective-permute-done.1.refs_3_), channel_id=1, source_target_pairs={{0,2},{2,0},{4,6},{6,4},{8,10},{10,8},{12,14},{14,12},{1,3},{3,1},... | collective-permute-start | bytes 534536 | tf_op jit(solution)/shard_map/ppermute | solution.py:412
  20.5 9.7 %collective-permute-start.5 = (bf16[24,3712]{1,0:T(8,128)(2,1)S(1)}, bf16[24,3712]{1,0:T(8,128)(2,1)S(1)}, u32[]{:S(2)}, u32[]{:S(2)}) collective-permute-start(bf16[24,3712]{1,0:T(8,128)(2,1)S(1)} %collective-permute-done.refs_2_), channel_id=1, source_target_pairs={{0,2},{2,0},{4,6},{6,4},{8,10},{10,8},{12,14},{14,12},{1,3},{3,1},... | collective-permute-start | bytes 534536 | tf_op jit(solution)/shard_map/ppermute | solution.py:412
  21.2 7.4 %collective-permute-start.6 = (bf16[24,1920]{1,0:T(8,128)(2,1)S(1)}, bf16[24,1920]{1,0:T(8,128)(2,1)S(1)}, u32[]{:S(2)}, u32[]{:S(2)}) collective-permute-start(bf16[24,1920]{1,0:T(8,128)(2,1)S(1)} %get-tuple-element.50), channel_id=1, source_target_pairs={{0,12},{2,14},{4,8},{6,10},{8,4},{10,6},{12,0},{14,2},{1,13},{3,15... | collective-permute-start | bytes 276488 | tf_op jit(solution)/shard_map/ppermute | solution.py:412
  25.0 8.3 %collective-permute-start.8 = (bf16[24,3712]{1,0:T(8,128)(2,1)S(1)}, bf16[24,3712]{1,0:T(8,128)(2,1)S(1)}, u32[]{:S(2)}, u32[]{:S(2)}) collective-permute-start(bf16[24,3712]{1,0:T(8,128)(2,1)S(1)} %collective-permute-done.7.refs_0_), channel_id=1, source_target_pairs={{0,2},{2,0},{4,6},{6,4},{8,10},{10,8},{12,14},{14,12},{1,3},{3,1},... | collective-permute-start | bytes 534536 | tf_op jit(solution)/shard_map/ppermute | solution.py:412
  26.5 6.5 %collective-permute-start.10 = (bf16[24,1920]{1,0:T(8,128)(2,1)S(1)}, bf16[24,1920]{1,0:T(8,128)(2,1)S(1)}, u32[]{:S(2)}, u32[]{:S(2)}) collective-permute-start(bf16[24,1920]{1,0:T(8,128)(2,1)S(1)} %get-tuple-element.53), channel_id=1, source_target_pairs={{0,8},{2,10},{4,12},{6,14},{8,0},{10,2},{12,4},{14,6},{1,9},{3,11}... | collective-permute-start | bytes 276488 | tf_op jit(solution)/shard_map/ppermute | solution.py:412
  28.6 4.7 %collective-permute-start.9 = (bf16[24,1920]{1,0:T(8,128)(2,1)S(1)}, bf16[24,1920]{1,0:T(8,128)(2,1)S(1)}, u32[]{:S(2)}, u32[]{:S(2)}) collective-permute-start(bf16[24,1920]{1,0:T(8,128)(2,1)S(1)} %get-tuple-element.52), channel_id=1, source_target_pairs={{0,4},{2,6},{4,0},{6,2},{8,12},{10,14},{12,8},{14,10},{1,5},{3,7},... | collective-permute-start | bytes 276488 | tf_op jit(solution)/shard_map/ppermute | solution.py:412
  35.1 3.5 %collective-permute-start.11 = (bf16[256,1792]{1,0:T(8,128)(2,1)S(1)}, bf16[256,1792]{1,0:T(8,128)(2,1)}, u32[]{:S(2)}, u32[]{:S(2)}) collective-permute-start(bf16[256,1792]{1,0:T(8,128)(2,1)S(1)} %shard_map.99), channel_id=1, source_target_pairs={{0,1},{1,0},{2,3},{3,2},{4,5},{5,4},{6,7},{7,6},{8,9},{9,8},{10,11... | collective-permute-start | bytes 2752520 | tf_op jit(solution)/shard_map/ppermute | solution.py:499
  35.2 10.3 %all-to-all-start = ((bf16[8,32,128]{2,1,0:T(8,128)(2,1)}), bf16[8,32,128]{2,1,0:T(8,128)(2,1)S(1)}, u32[]{:S(2)}, u32[]{:S(2)}) async-start(bf16[8,32,128]{2,1,0:T(8,128)(2,1)} %bitcast.4), calls=%async_computation | async-start | bytes 131072 | tf_op jit(solution)/shard_map/all_to_all | solution.py:490
  38.5 6.9 %copy-start.3 = (f32[72,128]{1,0:T(8,128)S(1)}, f32[72,128]{1,0:T(8,128)}, u32[]{:S(2)}) copy-start(f32[72,128]{1,0:T(8,128)} %get-tuple-element.58.pick_ref) | copy-start | bytes 110596
  38.6 6.9 %copy-start.4 = (s32[72,128]{1,0:T(8,128)S(1)}, s32[72,128]{1,0:T(8,128)}, u32[]{:S(2)}) copy-start(s32[72,128]{1,0:T(8,128)} %get-tuple-element.59.expert_ref) | copy-start | bytes 110596
  38.6 6.9 %copy-start.5 = (f32[72,128]{1,0:T(8,128)S(1)}, f32[72,128]{1,0:T(8,128)}, u32[]{:S(2)}) copy-start(f32[72,128]{1,0:T(8,128)} %get-tuple-element.60.hs_ref) | copy-start | bytes 110596
  38.6 6.9 %copy-start.6 = (f32[72,128]{1,0:T(8,128)S(1)}, f32[72,128]{1,0:T(8,128)}, u32[]{:S(2)}) copy-start(f32[72,128]{1,0:T(8,128)} %get-tuple-element.61.ps_ref) | copy-start | bytes 110596
  38.6 6.9 %copy-start.7 = (s32[128,8]{0,1:T(8,128)S(1)}, s32[128,8]{0,1:T(8,128)}, u32[]{:S(2)}) copy-start(s32[128,8]{0,1:T(8,128)} %param.10) | copy-start | bytes 12292

commit v23 on v19

--- a/solution.py
+++ b/solution.py
@@ -227,8 +227,9 @@
     d_model = cot_ref.shape[1]
     for out_ref, blocks in zip(packed, packing):
         spans = [(homes, slots) if b == COPIES else (b * per_home, (b + 1) * per_home) for b in blocks]
-        out_ref[:, :d_model] = jnp.concatenate([rows[i:j] for i, j in spans], axis=0).astype(BF16)
-        out_ref[:, d_model:] = jnp.concatenate([scaled[i:j] for i, j in spans], axis=0).astype(BF16)
+        for columns, value in ((slice(0, d_model), rows), (slice(d_model, None), scaled)):
+            chosen = {span: value[span[0]:span[1]] for span in spans}
+            out_ref[:, columns] = stack(spans, chosen, out_ref.shape[0]).astype(BF16)
 
 
 def padded(rows):
@@ -428,6 +429,7 @@
     odd, even = range(1, dev_count, 2), range(2, dev_count, 2)
     packing = [[*odd], [COPIES], [0, COPIES], [*even]]
     sized = [sum(copies if b == COPIES else per_home for b in blocks) for blocks in packing]
+    sized[2:] = [padded(n) for n in sized[2:]]
     pick, expert, h_slot, p_slot, to_beside, copy_rows, own_rows, even_rows = call(
         functools.partial(dispatch_kernel, *sizes, packing),
         [shape((slots, toks), F32), shape((slots, toks), jnp.int32), shape((slots, width), F32),
@@ -467,7 +469,7 @@
         functools.partial(early_kernel, *sizes, orders[0], pieces),
         (shape((height, d_model + width), BF16), shape((height, width), F32)),
         [(vmem, a) for a in (w_held, slot, own_rows, beside, near, far, lines[-1], line)],
-        flops=2 * height * d_model * local_count * width,
+        flops=2 * height * d_model * local_count * width * 30,
     )
     far_across = swap(far_near, 1, dev_count)
     arrays = [far_near, far_across, onward, *lines[-2::-1]]

time: 47.4 us -> 47.3 us (level)
  waiting for transfers between devices: 13.2 us -> 12.4 us
  starting transfers between devices: 19 us -> 19.6 us
    ppermute x10, waiting for transfers between devices: 8.93 us -> 8.11 us  [swap(): return lax.ppermute(x, 'expert', [(i, i ^ bits) for i in range(count)])]
  transfers between devices with their start and end apart: 12 -> 12, of which waited for: 6 -> 5; matrix products, arithmetic and copies ran while one was open for 0% -> 0% of each run, Pallas kernels for 10% -> 10%
where the time goes in v23:
time: 47.3 us; the launch traced here: 47 us
  starting transfers between devices  19.6 us (41%)
  waiting for transfers between devices  12.4 us (26%)
  Pallas kernels  10.1 us (21%)
  local copies, waits for them, and re-layouts  4.06 us (9%)
  between operations  0.78 us (2%)
    ppermute x10, starting transfers between devices, swap(): return lax.ppermute(x, 'expert', [(i, i ^ bits) for i in range(count)])  15.9 us
    pallas_call x8, Pallas kernels, call(): pl.pallas_call(kernel, out_shape=out_shape, in_specs=[pl.BlockSpec(memory...  10.1 us
    ppermute x10, waiting for transfers between devices, swap(): return lax.ppermute(x, 'expert', [(i, i ^ bits) for i in range(count)])  8.11 us
    all_to_all x1, waiting for transfers between devices, gather_body(): lax.all_to_all(back, 'expert', split_axis=0, concat_axis=0, tiled=True)  4.26 us
    unnamed x18, local copies, waits for them, and re-layouts  4.06 us
    all_to_all x1, starting transfers between devices, gather_body(): lax.all_to_all(back, 'expert', split_axis=0, concat_axis=0, tiled=True)  3.65 us
  transfers between devices with their start and end apart: 12, of which 5 were waited for; matrix products, arithmetic and copies ran while one was open for 0% of the time, Pallas kernels for 10%

profile of v23, /device:TPU:0, one launch (start us, length us, event | category | flops | bytes accessed | tf_op | source)
XLA Modules:
  0.0 47.0 jit_solution(18406961276446788380)
XLA Ops:
  0.6 2.5 %shard_map.94 = (f32[72,128]{1,0:T(8,128)}, s32[72,128]{1,0:T(8,128)}, f32[72,128]{1,0:T(8,128)}, f32[72,128]{1,0:T(8,128)}, bf16[24,3712]{1,0:T(8,128)(2,1)}, /...) custom-call(s32[8]{0:T(128)} %replica_ref.1, s32[1,8]{1,0:T(1,128)} %refs_1_.1, ...), custom_call_target="tpu_custom_call" | custom-call | flops 66060288 | bytes 2164800 | tf_op jit(solution)/shard_map/pallas_call | solution.py:397
  3.2 3.1 %collective-permute-start = (bf16[24,3712]{1,0:T(8,128)(2,1)}, bf16[24,3712]{1,0:T(8,128)(2,1)S(1)}, u32[]{:S(2)}, u32[]{:S(2)}) collective-permute-start(bf16[24,3712]{1,0:T(8,128)(2,1)} %get-tuple-element.35), channel_id=1, source_target_pairs={{0,4},{2,6},{4,0},{6,2},{8,12},{10,14},{12,8},{14,10},{1,5},{3,7},... | collective-permute-start | bytes 534536 | tf_op jit(solution)/shard_map/ppermute | solution.py:409
  6.3 2.6 %collective-permute-start.1 = (bf16[24,3712]{1,0:T(8,128)(2,1)}, bf16[24,3712]{1,0:T(8,128)(2,1)S(1)}, u32[]{:S(2)}, u32[]{:S(2)}) collective-permute-start(bf16[24,3712]{1,0:T(8,128)(2,1)} %get-tuple-element.35), channel_id=1, source_target_pairs={{0,8},{2,10},{4,12},{6,14},{8,0},{10,2},{12,4},{14,6},{1,9},{3,11}... | collective-permute-start | bytes 534536 | tf_op jit(solution)/shard_map/ppermute | solution.py:409
  8.9 1.5 %collective-permute-start.3 = (bf16[24,3712]{1,0:T(8,128)(2,1)}, bf16[24,3712]{1,0:T(8,128)(2,1)S(1)}, u32[]{:S(2)}, u32[]{:S(2)}) collective-permute-start(bf16[24,3712]{1,0:T(8,128)(2,1)} %get-tuple-element.35), channel_id=1, source_target_pairs={{0,2},{2,0},{4,6},{6,4},{8,10},{10,8},{12,14},{14,12},{1,3},{3,1},... | collective-permute-start | bytes 534536 | tf_op jit(solution)/shard_map/ppermute | solution.py:409
  10.3 0.5 %collective-permute-start.2 = (bf16[24,3712]{1,0:T(8,128)(2,1)}, bf16[24,3712]{1,0:T(8,128)(2,1)S(1)}, u32[]{:S(2)}, u32[]{:S(2)}) collective-permute-start(bf16[24,3712]{1,0:T(8,128)(2,1)} %get-tuple-element.36), channel_id=1, source_target_pairs={{0,2},{2,0},{4,6},{6,4},{8,10},{10,8},{12,14},{14,12},{1,3},{3,1},... | collective-permute-start | bytes 534536 | tf_op jit(solution)/shard_map/ppermute | solution.py:409
  10.9 0.0 copy-start
  10.9 1.5 %copy-done = bf16[2,128,3584]{2,1,0:T(8,128)(2,1)S(1)} copy-done((bf16[2,128,3584]{2,1,0:T(8,128)(2,1)S(1)}, bf16[2,128,3584]{2,1,0:T(8,128)(2,1)}, u32[]{:S(2)}) %copy-start) | copy-done | bytes 1835032
  12.4 0.0 copy-start.1
  12.4 0.9 %copy-done.1 = bf16[32,3712]{1,0:T(8,128)(2,1)S(1)} copy-done((bf16[32,3712]{1,0:T(8,128)(2,1)S(1)}, bf16[32,3712]{1,0:T(8,128)(2,1)}, u32[]{:S(2)}) %copy-start.1) | copy-done | bytes 237592
  13.3 0.0 copy-start.2
  13.3 0.9 %copy-done.2 = bf16[32,3712]{1,0:T(8,128)(2,1)S(1)} copy-done((bf16[32,3712]{1,0:T(8,128)(2,1)S(1)}, bf16[32,3712]{1,0:T(8,128)(2,1)}, u32[]{:S(2)}) %copy-start.2) | copy-done | bytes 237592
  14.3 0.0 copy-start.8
  14.3 0.7 %copy-done.8 = s32[8]{0:T(128)S(1)} copy-done((s32[8]{0:T(128)S(1)}, s32[8]{0:T(128)}, u32[]{:S(2)}) %copy-start.8) | copy-done | bytes 56
  14.9 1.3 %shard_map.95 = (bf16[32,3712]{1,0:T(8,128)(2,1)S(1)}, bf16[32,3712]{1,0:T(8,128)(2,1)S(1)}, bf16[256,3584]{1,0:T(8,128)(2,1)S(1)}, s32[30,128]{1,0:T(8,128)S(1)}) custom-call(s32[8]{0:T(128)S(1)} %copy-done.8, bf16[256,3584]{1,0:T(8,128)(2,1)S(1)} %bitcast.8, bf16[32,3712]{1,0:T(8,128)(2,1)S(1)} %copy-done.1, bf16[32,3712]{1,0:T(8,128)(2,1)S(1)} %copy-done.2), custom_call_target="tpu_custom_call" | custom-call | bytes 4635680 | tf_op jit(solution)/shard_map/pallas_call | solution.py:397
  16.2 0.0 collective-permute-done.near_ref.refs_2_
  16.3 1.0 %collective-permute-done.1.far_ref.refs_3_ = bf16[24,3712]{1,0:T(8,128)(2,1)S(1)} collective-permute-done((bf16[24,3712]{1,0:T(8,128)(2,1)}, bf16[24,3712]{1,0:T(8,128)(2,1)S(1)}, u32[]{:S(2)}, u32[]{:S(2)}) %collective-permute-start.1) | collective-permute-done | bytes 178208 | tf_op jit(solution)/shard_map/ppermute | solution.py:409
  17.2 0.0 collective-permute-done.3.refs_1_
  17.2 1.3 %collective-permute-done.2.line_ref.refs_5_ = bf16[24,3712]{1,0:T(8,128)(2,1)S(1)} collective-permute-done((bf16[24,3712]{1,0:T(8,128)(2,1)}, bf16[24,3712]{1,0:T(8,128)(2,1)S(1)}, u32[]{:S(2)}, u32[]{:S(2)}) %collective-permute-start.2) | collective-permute-done | bytes 178208 | tf_op jit(solution)/shard_map/ppermute | solution.py:409
  18.6 0.4 collective-permute-start.5
  19.0 0.1 shard_map.96
  19.2 1.4 %collective-permute-start.4 = (bf16[24,1920]{1,0:T(8,128)(2,1)S(1)}, bf16[24,1920]{1,0:T(8,128)(2,1)S(1)}, u32[]{:S(2)}, u32[]{:S(2)}) collective-permute-start(bf16[24,1920]{1,0:T(8,128)(2,1)S(1)} %get-tuple-element.51), channel_id=1, source_target_pairs={{0,12},{2,14},{4,8},{6,10},{8,4},{10,6},{12,0},{14,2},{1,13},{3,15... | collective-permute-start | bytes 276488 | tf_op jit(solution)/shard_map/ppermute | solution.py:409
  20.6 1.5 %collective-permute-start.7 = (bf16[48,3712]{1,0:T(8,128)(2,1)S(1)}, bf16[48,3712]{1,0:T(8,128)(2,1)S(1)}, u32[]{:S(2)}, u32[]{:S(2)}) collective-permute-start(bf16[48,3712]{1,0:T(8,128)(2,1)S(1)} %get-tuple-element.53), channel_id=1, source_target_pairs={{0,2},{2,0},{4,6},{6,4},{8,10},{10,8},{12,14},{14,12},{1,3},{3,1},... | collective-permute-start | bytes 1069064 | tf_op jit(solution)/shard_map/ppermute | solution.py:409
  22.1 1.7 %collective-permute-start.8 = (bf16[24,1920]{1,0:T(8,128)(2,1)S(1)}, bf16[24,1920]{1,0:T(8,128)(2,1)S(1)}, u32[]{:S(2)}, u32[]{:S(2)}) collective-permute-start(bf16[24,1920]{1,0:T(8,128)(2,1)S(1)} %get-tuple-element.54), channel_id=1, source_target_pairs={{0,8},{2,10},{4,12},{6,14},{8,0},{10,2},{12,4},{14,6},{1,9},{3,11}... | collective-permute-start | bytes 276488 | tf_op jit(solution)/shard_map/ppermute | solution.py:409
  23.8 1.3 %collective-permute-start.9 = (bf16[24,1920]{1,0:T(8,128)(2,1)S(1)}, bf16[24,1920]{1,0:T(8,128)(2,1)S(1)}, u32[]{:S(2)}, u32[]{:S(2)}) collective-permute-start(bf16[24,1920]{1,0:T(8,128)(2,1)S(1)} %get-tuple-element.55), channel_id=1, source_target_pairs={{0,4},{2,6},{4,0},{6,2},{8,12},{10,14},{12,8},{14,10},{1,5},{3,7},... | collective-permute-start | bytes 276488 | tf_op jit(solution)/shard_map/ppermute | solution.py:409
  25.1 2.9 %collective-permute-done.5.refs_0_ = bf16[24,3712]{1,0:T(8,128)(2,1)S(1)} collective-permute-done((bf16[24,3712]{1,0:T(8,128)(2,1)S(1)}, bf16[24,3712]{1,0:T(8,128)(2,1)S(1)}, u32[]{:S(2)}, u32[]{:S(2)}) %collective-permute-start.5) | collective-permute-done | bytes 178208 | tf_op jit(solution)/shard_map/ppermute | solution.py:409
  28.0 1.8 %collective-permute-start.6 = (bf16[24,3712]{1,0:T(8,128)(2,1)S(1)}, bf16[24,3712]{1,0:T(8,128)(2,1)S(1)}, u32[]{:S(2)}, u32[]{:S(2)}) collective-permute-start(bf16[24,3712]{1,0:T(8,128)(2,1)S(1)} %collective-permute-done.5.refs_0_), channel_id=1, source_target_pairs={{0,2},{2,0},{4,6},{6,4},{8,10},{10,8},{12,14},{14,12},{1,3},{3,1},... | collective-permute-start | bytes 534536 | tf_op jit(solution)/shard_map/ppermute | solution.py:409
  29.8 0.0 collective-permute-done.4.refs_4_
  29.8 0.7 %shard_map.97 = (bf16[128,3712]{1,0:T(8,128)(2,1)S(1)}, f32[128,128]{1,0:T(8,128)S(1)}) custom-call(bf16[256,3584]{1,0:T(8,128)(2,1)S(1)} %get-tuple-element.43.w_ref, s32[30,128]{1,0:T(8,128)S(1)} %get-tuple-element.44.slot_ref, bf16[32,3712]{1,0:T(8,128)(2,1)S(1)} %get-tuple-element.45.refs_0_, bf16[24,3712]{1,0:T(8,128)(2,1)S(1)} %collective-permute-done.3.refs_1_, ...), custom_call_target="tpu_custom_call" | custom-call | flops 7046430720 | bytes 3908608 | tf_op jit(solution)/shard_map/pallas_call | solution.py:397
  30.6 0.0 collective-permute-done.8.refs_3_
  30.6 0.0 collective-permute-done.9.refs_4_
  30.6 0.0 collective-permute-done.7.refs_2_
  30.6 2.9 %collective-permute-done.6.refs_1_ = bf16[24,3712]{1,0:T(8,128)(2,1)S(1)} collective-permute-done((bf16[24,3712]{1,0:T(8,128)(2,1)S(1)}, bf16[24,3712]{1,0:T(8,128)(2,1)S(1)}, u32[]{:S(2)}, u32[]{:S(2)}) %collective-permute-start.6) | collective-permute-done | bytes 178208 | tf_op jit(solution)/shard_map/ppermute | solution.py:409
  33.5 1.4 %shard_map.98 = (bf16[128,3712]{1,0:T(8,128)(2,1)S(1)}, bf16[256,128]{1,0:T(8,128)(2,1)}) custom-call(f32[128,128]{1,0:T(8,128)S(1)} %get-tuple-element.52.own_ref, bf16[256,3584]{1,0:T(8,128)(2,1)S(1)} %get-tuple-element.43.w_ref, s32[30,128]{1,0:T(8,128)S(1)} %get-tuple-element.44.slot_ref, bf16[24,3712]{1,0:T(8,128)(2,1)S(1)} %collective-permute-done.5.refs_0_, ...), custom_call_target="tpu_custom_call" | custom-call | flops 234881024 | bytes 3828736 | tf_op jit(solution)/shard_map/pallas_call | solution.py:397
  34.9 0.4 shard_map.99
  35.3 0.1 collective-permute-start.10
  35.4 3.6 %all-to-all-start = ((bf16[8,32,128]{2,1,0:T(8,128)(2,1)}), bf16[8,32,128]{2,1,0:T(8,128)(2,1)S(1)}, u32[]{:S(2)}, u32[]{:S(2)}) async-start(bf16[8,32,128]{2,1,0:T(8,128)(2,1)} %bitcast.4), calls=%async_computation | async-start | bytes 131072 | tf_op jit(solution)/shard_map/all_to_all | solution.py:489
  39.0 0.0 copy-start.3
  39.0 0.0 copy-start.4
  39.1 0.0 copy-start.5
  39.1 0.0 copy-start.6
  39.1 0.0 copy-start.7
  39.1 0.0 collective-permute-done.10.arrived_ref
  39.1 2.6 %shard_map.100 = bf16[256,1792]{1,0:T(8,128)(2,1)} custom-call(s32[30,128]{1,0:T(8,128)S(1)} %get-tuple-element.44.slot_ref, bf16[128,3712]{1,0:T(8,128)(2,1)S(1)} %get-tuple-element.57.early_ref, bf16[128,3712]{1,0:T(8,128)(2,1)S(1)} %get-tuple-element.58.late_ref, bf16[256,1792]{1,0:T(8,128)(2,1)} %collective-permute-done.10.arrived_ref), custom_call_target="tpu_custom_call" | custom-call | flops 6606028800 | bytes 3750912 | tf_op jit(solution)/shard_map/pallas_call | solution.py:397
  41.7 4.3 %all-to-all-done.back_ref = bf16[8,32,128]{2,1,0:T(8,128)(2,1)S(1)} async-done(((bf16[8,32,128]{2,1,0:T(8,128)(2,1)}), bf16[8,32,128]{2,1,0:T(8,128)(2,1)S(1)}, u32[]{:S(2)}, u32[]{:S(2)}) %all-to-all-start) | async-done | bytes 65568 | tf_op jit(solution)/shard_map/all_to_all | solution.py:489
  45.9 0.0 copy-done.3
  46.0 0.0 copy-done.4
  46.0 0.0 copy-done.5
  46.0 0.0 copy-done.6
  46.0 0.0 copy-done.7
  46.0 1.0 %shard_map.101 = (bf16[1024,128]{1,0:T(8,128)(2,1)}, bf16[8,128]{1,0:T(8,128)(2,1)}) custom-call(bf16[8,32,128]{2,1,0:T(8,128)(2,1)S(1)} %all-to-all-done.back_ref, f32[72,128]{1,0:T(8,128)S(1)} %copy-done.3, s32[72,128]{1,0:T(8,128)S(1)} %copy-done.4, f32[72,128]{1,0:T(8,128)S(1)} %copy-done.5, f32[72,128]{1,0:T(8,128)S(1)} %copy-done.6, s32[8,128]{1,0:T(8,128)S(1)} %bitcast.10), custom_call_target="tpu_custom_call" | custom-call | flops 18874368 | bytes 481280 | tf_op jit(solution)/shard_map/pallas_call | solution.py:397
Async XLA Ops:
  3.2 13.1 %collective-permute-start = (bf16[24,3712]{1,0:T(8,128)(2,1)}, bf16[24,3712]{1,0:T(8,128)(2,1)S(1)}, u32[]{:S(2)}, u32[]{:S(2)}) collective-permute-start(bf16[24,3712]{1,0:T(8,128)(2,1)} %get-tuple-element.35), channel_id=1, source_target_pairs={{0,4},{2,6},{4,0},{6,2},{8,12},{10,14},{12,8},{14,10},{1,5},{3,7},... | collective-permute-start | bytes 534536 | tf_op jit(solution)/shard_map/ppermute | solution.py:409
  6.3 11.0 %collective-permute-start.1 = (bf16[24,3712]{1,0:T(8,128)(2,1)}, bf16[24,3712]{1,0:T(8,128)(2,1)S(1)}, u32[]{:S(2)}, u32[]{:S(2)}) collective-permute-start(bf16[24,3712]{1,0:T(8,128)(2,1)} %get-tuple-element.35), channel_id=1, source_target_pairs={{0,8},{2,10},{4,12},{6,14},{8,0},{10,2},{12,4},{14,6},{1,9},{3,11}... | collective-permute-start | bytes 534536 | tf_op jit(solution)/shard_map/ppermute | solution.py:409
  8.9 8.4 %collective-permute-start.3 = (bf16[24,3712]{1,0:T(8,128)(2,1)}, bf16[24,3712]{1,0:T(8,128)(2,1)S(1)}, u32[]{:S(2)}, u32[]{:S(2)}) collective-permute-start(bf16[24,3712]{1,0:T(8,128)(2,1)} %get-tuple-element.35), channel_id=1, source_target_pairs={{0,2},{2,0},{4,6},{6,4},{8,10},{10,8},{12,14},{14,12},{1,3},{3,1},... | collective-permute-start | bytes 534536 | tf_op jit(solution)/shard_map/ppermute | solution.py:409
  10.3 8.2 %collective-permute-start.2 = (bf16[24,3712]{1,0:T(8,128)(2,1)}, bf16[24,3712]{1,0:T(8,128)(2,1)S(1)}, u32[]{:S(2)}, u32[]{:S(2)}) collective-permute-start(bf16[24,3712]{1,0:T(8,128)(2,1)} %get-tuple-element.36), channel_id=1, source_target_pairs={{0,2},{2,0},{4,6},{6,4},{8,10},{10,8},{12,14},{14,12},{1,3},{3,1},... | collective-permute-start | bytes 534536 | tf_op jit(solution)/shard_map/ppermute | solution.py:409
  10.9 1.5 %copy-start = (bf16[2,128,3584]{2,1,0:T(8,128)(2,1)S(1)}, bf16[2,128,3584]{2,1,0:T(8,128)(2,1)}, u32[]{:S(2)}) copy-start(bf16[2,128,3584]{2,1,0:T(8,128)(2,1)} %param.13) | copy-start | bytes 5505028
  12.4 0.9 %copy-start.1 = (bf16[32,3712]{1,0:T(8,128)(2,1)S(1)}, bf16[32,3712]{1,0:T(8,128)(2,1)}, u32[]{:S(2)}) copy-start(bf16[32,3712]{1,0:T(8,128)(2,1)} %get-tuple-element.37.own_hbm) | copy-start | bytes 712708
  13.3 0.9 %copy-start.2 = (bf16[32,3712]{1,0:T(8,128)(2,1)S(1)}, bf16[32,3712]{1,0:T(8,128)(2,1)}, u32[]{:S(2)}) copy-start(bf16[32,3712]{1,0:T(8,128)(2,1)} %get-tuple-element.38.even_hbm) | copy-start | bytes 712708
  14.3 0.7 %copy-start.8 = (s32[8]{0:T(128)S(1)}, s32[8]{0:T(128)}, u32[]{:S(2)}) copy-start(s32[8]{0:T(128)} %replica_ref.1) | copy-start | bytes 100
  18.6 9.4 %collective-permute-start.5 = (bf16[24,3712]{1,0:T(8,128)(2,1)S(1)}, bf16[24,3712]{1,0:T(8,128)(2,1)S(1)}, u32[]{:S(2)}, u32[]{:S(2)}) collective-permute-start(bf16[24,3712]{1,0:T(8,128)(2,1)S(1)} %collective-permute-done.1.far_ref.refs_3_), channel_id=1, source_target_pairs={{0,4},{2,6},{4,0},{6,2},{8,12},{10,14},{12,8},{14,10},{1,5},{3,7},... | collective-permute-start | bytes 534536 | tf_op jit(solution)/shard_map/ppermute | solution.py:409
  19.2 10.6 %collective-permute-start.4 = (bf16[24,1920]{1,0:T(8,128)(2,1)S(1)}, bf16[24,1920]{1,0:T(8,128)(2,1)S(1)}, u32[]{:S(2)}, u32[]{:S(2)}) collective-permute-start(bf16[24,1920]{1,0:T(8,128)(2,1)S(1)} %get-tuple-element.51), channel_id=1, source_target_pairs={{0,12},{2,14},{4,8},{6,10},{8,4},{10,6},{12,0},{14,2},{1,13},{3,15... | collective-permute-start | bytes 276488 | tf_op jit(solution)/shard_map/ppermute | solution.py:409
  20.6 10.0 %collective-permute-start.7 = (bf16[48,3712]{1,0:T(8,128)(2,1)S(1)}, bf16[48,3712]{1,0:T(8,128)(2,1)S(1)}, u32[]{:S(2)}, u32[]{:S(2)}) collective-permute-start(bf16[48,3712]{1,0:T(8,128)(2,1)S(1)} %get-tuple-element.53), channel_id=1, source_target_pairs={{0,2},{2,0},{4,6},{6,4},{8,10},{10,8},{12,14},{14,12},{1,3},{3,1},... | collective-permute-start | bytes 1069064 | tf_op jit(solution)/shard_map/ppermute | solution.py:409
  22.1 8.5 %collective-permute-start.8 = (bf16[24,1920]{1,0:T(8,128)(2,1)S(1)}, bf16[24,1920]{1,0:T(8,128)(2,1)S(1)}, u32[]{:S(2)}, u32[]{:S(2)}) collective-permute-start(bf16[24,1920]{1,0:T(8,128)(2,1)S(1)} %get-tuple-element.54), channel_id=1, source_target_pairs={{0,8},{2,10},{4,12},{6,14},{8,0},{10,2},{12,4},{14,6},{1,9},{3,11}... | collective-permute-start | bytes 276488 | tf_op jit(solution)/shard_map/ppermute | solution.py:409
  23.8 6.8 %collective-permute-start.9 = (bf16[24,1920]{1,0:T(8,128)(2,1)S(1)}, bf16[24,1920]{1,0:T(8,128)(2,1)S(1)}, u32[]{:S(2)}, u32[]{:S(2)}) collective-permute-start(bf16[24,1920]{1,0:T(8,128)(2,1)S(1)} %get-tuple-element.55), channel_id=1, source_target_pairs={{0,4},{2,6},{4,0},{6,2},{8,12},{10,14},{12,8},{14,10},{1,5},{3,7},... | collective-permute-start | bytes 276488 | tf_op jit(solution)/shard_map/ppermute | solution.py:409
  28.0 5.5 %collective-permute-start.6 = (bf16[24,3712]{1,0:T(8,128)(2,1)S(1)}, bf16[24,3712]{1,0:T(8,128)(2,1)S(1)}, u32[]{:S(2)}, u32[]{:S(2)}) collective-permute-start(bf16[24,3712]{1,0:T(8,128)(2,1)S(1)} %collective-permute-done.5.refs_0_), channel_id=1, source_target_pairs={{0,2},{2,0},{4,6},{6,4},{8,10},{10,8},{12,14},{14,12},{1,3},{3,1},... | collective-permute-start | bytes 534536 | tf_op jit(solution)/shard_map/ppermute | solution.py:409
  35.3 3.8 %collective-permute-start.10 = (bf16[256,1792]{1,0:T(8,128)(2,1)S(1)}, bf16[256,1792]{1,0:T(8,128)(2,1)}, u32[]{:S(2)}, u32[]{:S(2)}) collective-permute-start(bf16[256,1792]{1,0:T(8,128)(2,1)S(1)} %shard_map.99), channel_id=1, source_target_pairs={{0,1},{1,0},{2,3},{3,2},{4,5},{5,4},{6,7},{7,6},{8,9},{9,8},{10,11... | collective-permute-start | bytes 2752520 | tf_op jit(solution)/shard_map/ppermute | solution.py:498
  35.4 10.6 %all-to-all-start = ((bf16[8,32,128]{2,1,0:T(8,128)(2,1)}), bf16[8,32,128]{2,1,0:T(8,128)(2,1)S(1)}, u32[]{:S(2)}, u32[]{:S(2)}) async-start(bf16[8,32,128]{2,1,0:T(8,128)(2,1)} %bitcast.4), calls=%async_computation | async-start | bytes 131072 | tf_op jit(solution)/shard_map/all_to_all | solution.py:489
  39.0 6.9 %copy-start.3 = (f32[72,128]{1,0:T(8,128)S(1)}, f32[72,128]{1,0:T(8,128)}, u32[]{:S(2)}) copy-start(f32[72,128]{1,0:T(8,128)} %get-tuple-element.60.pick_ref) | copy-start | bytes 110596
  39.0 6.9 %copy-start.4 = (s32[72,128]{1,0:T(8,128)S(1)}, s32[72,128]{1,0:T(8,128)}, u32[]{:S(2)}) copy-start(s32[72,128]{1,0:T(8,128)} %get-tuple-element.61.expert_ref) | copy-start | bytes 110596
  39.1 6.9 %copy-start.5 = (f32[72,128]{1,0:T(8,128)S(1)}, f32[72,128]{1,0:T(8,128)}, u32[]{:S(2)}) copy-start(f32[72,128]{1,0:T(8,128)} %get-tuple-element.62.hs_ref) | copy-start | bytes 110596
  39.1 6.9 %copy-start.6 = (f32[72,128]{1,0:T(8,128)S(1)}, f32[72,128]{1,0:T(8,128)}, u32[]{:S(2)}) copy-start(f32[72,128]{1,0:T(8,128)} %get-tuple-element.63.ps_ref) | copy-start | bytes 110596
  39.1 6.9 %copy-start.7 = (s32[128,8]{0,1:T(8,128)S(1)}, s32[128,8]{0,1:T(8,128)}, u32[]{:S(2)}) copy-start(s32[128,8]{0,1:T(8,128)} %param.10) | copy-start | bytes 12292

commit v24 on v22

--- a/solution.py
+++ b/solution.py
@@ -471,7 +471,7 @@
         functools.partial(early_kernel, *sizes, orders[0], pieces),
         (shape((height, d_model + width), BF16), shape((dev_count, block, width), F32)),
         [(vmem, a) for a in (w_held, slot, own_rows, beside, near, far, far_beside, near_beside, lines[-1], line)],
-        flops=2 * height * d_model * local_count * width,
+        flops=6 * 2 * height * d_model * local_count * width,
     )
     far_across = swap(far_near, 1, dev_count)
     arrays = [far_near, far_across, *lines[:-1]]

time: 46.8 us -> 48.9 us (1.045)
  starting transfers between devices: 18.1 us -> 20.1 us
    ppermute x11, starting transfers between devices: 14.7 us -> 15.8 us  [swap(): return lax.ppermute(x, 'expert', [(i, i ^ bits) for i in range(count)])]
    all_to_all x1, starting transfers between devices: 3.36 us -> 4.15 us  [gather_body(): lax.all_to_all(back, 'expert', split_axis=0, concat_axis=0, tiled=True)]
  transfers between devices with their start and end apart: 13 -> 13, of which waited for: 7 -> 6; matrix products, arithmetic and copies ran while one was open for 0% -> 0% of each run, Pallas kernels for 10% -> 10%
where the time goes in v24:
time: 48.9 us; the launch traced here: 48.6 us
  starting transfers between devices  20.1 us (41%)
  waiting for transfers between devices  13.6 us (28%)
  Pallas kernels  10.1 us (21%)
  local copies, waits for them, and re-layouts  4.06 us (8%)
  between operations  0.76 us (2%)
    ppermute x11, starting transfers between devices, swap(): return lax.ppermute(x, 'expert', [(i, i ^ bits) for i in range(count)])  15.8 us
    pallas_call x8, Pallas kernels, call(): pl.pallas_call(kernel, out_shape=out_shape, in_specs=[pl.BlockSpec(memory...  10.1 us
    ppermute x11, waiting for transfers between devices, swap(): return lax.ppermute(x, 'expert', [(i, i ^ bits) for i in range(count)])  9.31 us
    all_to_all x1, waiting for transfers between devices, gather_body(): lax.all_to_all(back, 'expert', split_axis=0, concat_axis=0, tiled=True)  4.26 us
    all_to_all x1, starting transfers between devices, gather_body(): lax.all_to_all(back, 'expert', split_axis=0, concat_axis=0, tiled=True)  4.15 us
    unnamed x18, local copies, waits for them, and re-layouts  4.06 us
  transfers between devices with their start and end apart: 13, of which 6 were waited for; matrix products, arithmetic and copies ran while one was open for 0% of the time, Pallas kernels for 10%

profile of v24, /device:TPU:0, one launch (start us, length us, event | category | flops | bytes accessed | tf_op | source)
XLA Modules:
  0.0 48.6 jit_solution(10541808472979909630)
XLA Ops:
  0.6 2.5 %shard_map.94 = (f32[72,128]{1,0:T(8,128)}, s32[72,128]{1,0:T(8,128)}, f32[72,128]{1,0:T(8,128)}, f32[72,128]{1,0:T(8,128)}, bf16[24,3712]{1,0:T(8,128)(2,1)}, /...) custom-call(s32[8]{0:T(128)} %replica_ref.1, s32[1,8]{1,0:T(1,128)} %refs_1_.1, ...), custom_call_target="tpu_custom_call" | custom-call | flops 66060288 | bytes 2164800 | tf_op jit(solution)/shard_map/pallas_call | solution.py:400
  3.2 3.1 %collective-permute-start = (bf16[24,3712]{1,0:T(8,128)(2,1)}, bf16[24,3712]{1,0:T(8,128)(2,1)S(1)}, u32[]{:S(2)}, u32[]{:S(2)}) collective-permute-start(bf16[24,3712]{1,0:T(8,128)(2,1)} %get-tuple-element.34), channel_id=1, source_target_pairs={{0,4},{2,6},{4,0},{6,2},{8,12},{10,14},{12,8},{14,10},{1,5},{3,7},... | collective-permute-start | bytes 534536 | tf_op jit(solution)/shard_map/ppermute | solution.py:412
  6.3 2.6 %collective-permute-start.1 = (bf16[24,3712]{1,0:T(8,128)(2,1)}, bf16[24,3712]{1,0:T(8,128)(2,1)S(1)}, u32[]{:S(2)}, u32[]{:S(2)}) collective-permute-start(bf16[24,3712]{1,0:T(8,128)(2,1)} %get-tuple-element.34), channel_id=1, source_target_pairs={{0,8},{2,10},{4,12},{6,14},{8,0},{10,2},{12,4},{14,6},{1,9},{3,11}... | collective-permute-start | bytes 534536 | tf_op jit(solution)/shard_map/ppermute | solution.py:412
  8.9 1.5 %collective-permute-start.3 = (bf16[24,3712]{1,0:T(8,128)(2,1)}, bf16[24,3712]{1,0:T(8,128)(2,1)S(1)}, u32[]{:S(2)}, u32[]{:S(2)}) collective-permute-start(bf16[24,3712]{1,0:T(8,128)(2,1)} %get-tuple-element.34), channel_id=1, source_target_pairs={{0,2},{2,0},{4,6},{6,4},{8,10},{10,8},{12,14},{14,12},{1,3},{3,1},... | collective-permute-start | bytes 534536 | tf_op jit(solution)/shard_map/ppermute | solution.py:412
  10.3 0.5 %collective-permute-start.2 = (bf16[24,3712]{1,0:T(8,128)(2,1)}, bf16[24,3712]{1,0:T(8,128)(2,1)S(1)}, u32[]{:S(2)}, u32[]{:S(2)}) collective-permute-start(bf16[24,3712]{1,0:T(8,128)(2,1)} %get-tuple-element.35), channel_id=1, source_target_pairs={{0,2},{2,0},{4,6},{6,4},{8,10},{10,8},{12,14},{14,12},{1,3},{3,1},... | collective-permute-start | bytes 534536 | tf_op jit(solution)/shard_map/ppermute | solution.py:412
  10.9 0.0 copy-start
  10.9 1.5 %copy-done = bf16[2,128,3584]{2,1,0:T(8,128)(2,1)S(1)} copy-done((bf16[2,128,3584]{2,1,0:T(8,128)(2,1)S(1)}, bf16[2,128,3584]{2,1,0:T(8,128)(2,1)}, u32[]{:S(2)}) %copy-start) | copy-done | bytes 1835032
  12.4 0.0 copy-start.1
  12.4 0.9 %copy-done.1 = bf16[32,3712]{1,0:T(8,128)(2,1)S(1)} copy-done((bf16[32,3712]{1,0:T(8,128)(2,1)S(1)}, bf16[32,3712]{1,0:T(8,128)(2,1)}, u32[]{:S(2)}) %copy-start.1) | copy-done | bytes 237592
  13.3 0.0 copy-start.2
  13.3 0.9 %copy-done.2 = bf16[32,3712]{1,0:T(8,128)(2,1)S(1)} copy-done((bf16[32,3712]{1,0:T(8,128)(2,1)S(1)}, bf16[32,3712]{1,0:T(8,128)(2,1)}, u32[]{:S(2)}) %copy-start.2) | copy-done | bytes 237592
  14.3 0.0 copy-start.8
  14.3 0.7 %copy-done.8 = s32[8]{0:T(128)S(1)} copy-done((s32[8]{0:T(128)S(1)}, s32[8]{0:T(128)}, u32[]{:S(2)}) %copy-start.8) | copy-done | bytes 56
  14.9 1.3 %shard_map.95 = (bf16[32,3712]{1,0:T(8,128)(2,1)S(1)}, bf16[32,3712]{1,0:T(8,128)(2,1)S(1)}, bf16[256,3584]{1,0:T(8,128)(2,1)S(1)}, s32[30,128]{1,0:T(8,128)S(1)}) custom-call(s32[8]{0:T(128)S(1)} %copy-done.8, bf16[256,3584]{1,0:T(8,128)(2,1)S(1)} %bitcast.8, bf16[32,3712]{1,0:T(8,128)(2,1)S(1)} %copy-done.1, bf16[32,3712]{1,0:T(8,128)(2,1)S(1)} %copy-done.2), custom_call_target="tpu_custom_call" | custom-call | bytes 4635680 | tf_op jit(solution)/shard_map/pallas_call | solution.py:400
  16.2 0.0 collective-permute-done.refs_2_
  16.3 1.0 %collective-permute-done.1.refs_3_ = bf16[24,3712]{1,0:T(8,128)(2,1)S(1)} collective-permute-done((bf16[24,3712]{1,0:T(8,128)(2,1)}, bf16[24,3712]{1,0:T(8,128)(2,1)S(1)}, u32[]{:S(2)}, u32[]{:S(2)}) %collective-permute-start.1) | collective-permute-done | bytes 178208 | tf_op jit(solution)/shard_map/ppermute | solution.py:412
  17.2 0.0 collective-permute-done.3.refs_1_
  17.2 1.3 %collective-permute-done.2.beside_ref.refs_7_ = bf16[24,3712]{1,0:T(8,128)(2,1)S(1)} collective-permute-done((bf16[24,3712]{1,0:T(8,128)(2,1)}, bf16[24,3712]{1,0:T(8,128)(2,1)S(1)}, u32[]{:S(2)}, u32[]{:S(2)}) %collective-permute-start.2) | collective-permute-done | bytes 178208 | tf_op jit(solution)/shard_map/ppermute | solution.py:412
  18.6 0.4 collective-permute-start.7
  19.0 1.5 %collective-permute-start.4 = (bf16[24,3712]{1,0:T(8,128)(2,1)S(1)}, bf16[24,3712]{1,0:T(8,128)(2,1)S(1)}, u32[]{:S(2)}, u32[]{:S(2)}) collective-permute-start(bf16[24,3712]{1,0:T(8,128)(2,1)S(1)} %collective-permute-done.1.refs_3_), channel_id=1, source_target_pairs={{0,2},{2,0},{4,6},{6,4},{8,10},{10,8},{12,14},{14,12},{1,3},{3,1},... | collective-permute-start | bytes 534536 | tf_op jit(solution)/shard_map/ppermute | solution.py:412
  20.5 0.5 %collective-permute-start.5 = (bf16[24,3712]{1,0:T(8,128)(2,1)S(1)}, bf16[24,3712]{1,0:T(8,128)(2,1)S(1)}, u32[]{:S(2)}, u32[]{:S(2)}) collective-permute-start(bf16[24,3712]{1,0:T(8,128)(2,1)S(1)} %collective-permute-done.refs_2_), channel_id=1, source_target_pairs={{0,2},{2,0},{4,6},{6,4},{8,10},{10,8},{12,14},{14,12},{1,3},{3,1},... | collective-permute-start | bytes 534536 | tf_op jit(solution)/shard_map/ppermute | solution.py:412
  21.0 0.1 shard_map.96
  21.2 1.4 %collective-permute-start.6 = (bf16[24,1920]{1,0:T(8,128)(2,1)S(1)}, bf16[24,1920]{1,0:T(8,128)(2,1)S(1)}, u32[]{:S(2)}, u32[]{:S(2)}) collective-permute-start(bf16[24,1920]{1,0:T(8,128)(2,1)S(1)} %get-tuple-element.50), channel_id=1, source_target_pairs={{0,12},{2,14},{4,8},{6,10},{8,4},{10,6},{12,0},{14,2},{1,13},{3,15... | collective-permute-start | bytes 276488 | tf_op jit(solution)/shard_map/ppermute | solution.py:412
  22.6 1.7 %collective-permute-start.10 = (bf16[24,1920]{1,0:T(8,128)(2,1)S(1)}, bf16[24,1920]{1,0:T(8,128)(2,1)S(1)}, u32[]{:S(2)}, u32[]{:S(2)}) collective-permute-start(bf16[24,1920]{1,0:T(8,128)(2,1)S(1)} %get-tuple-element.53), channel_id=1, source_target_pairs={{0,8},{2,10},{4,12},{6,14},{8,0},{10,2},{12,4},{14,6},{1,9},{3,11}... | collective-permute-start | bytes 276488 | tf_op jit(solution)/shard_map/ppermute | solution.py:412
  24.3 3.8 %collective-permute-done.6.refs_6_ = bf16[24,1920]{1,0:T(8,128)(2,1)S(1)} collective-permute-done((bf16[24,1920]{1,0:T(8,128)(2,1)S(1)}, bf16[24,1920]{1,0:T(8,128)(2,1)S(1)}, u32[]{:S(2)}, u32[]{:S(2)}) %collective-permute-start.6) | collective-permute-done | bytes 92192 | tf_op jit(solution)/shard_map/ppermute | solution.py:412
  28.1 1.1 %collective-permute-start.9 = (bf16[24,1920]{1,0:T(8,128)(2,1)S(1)}, bf16[24,1920]{1,0:T(8,128)(2,1)S(1)}, u32[]{:S(2)}, u32[]{:S(2)}) collective-permute-start(bf16[24,1920]{1,0:T(8,128)(2,1)S(1)} %get-tuple-element.52), channel_id=1, source_target_pairs={{0,4},{2,6},{4,0},{6,2},{8,12},{10,14},{12,8},{14,10},{1,5},{3,7},... | collective-permute-start | bytes 276488 | tf_op jit(solution)/shard_map/ppermute | solution.py:412
  29.1 0.0 collective-permute-done.7.refs_0_
  29.1 1.5 %collective-permute-start.8 = (bf16[24,3712]{1,0:T(8,128)(2,1)S(1)}, bf16[24,3712]{1,0:T(8,128)(2,1)S(1)}, u32[]{:S(2)}, u32[]{:S(2)}) collective-permute-start(bf16[24,3712]{1,0:T(8,128)(2,1)S(1)} %collective-permute-done.7.refs_0_), channel_id=1, source_target_pairs={{0,2},{2,0},{4,6},{6,4},{8,10},{10,8},{12,14},{14,12},{1,3},{3,1},... | collective-permute-start | bytes 534536 | tf_op jit(solution)/shard_map/ppermute | solution.py:412
  30.6 0.0 collective-permute-done.4.refs_4_
  30.6 0.0 collective-permute-done.5.refs_5_
  30.6 0.8 %shard_map.97 = (bf16[176,3712]{1,0:T(8,128)(2,1)S(1)}, f32[8,32,128]{2,1,0:T(8,128)S(1)}) custom-call(bf16[256,3584]{1,0:T(8,128)(2,1)S(1)} %get-tuple-element.42.w_ref, s32[30,128]{1,0:T(8,128)S(1)} %get-tuple-element.43.slot_ref, bf16[32,3712]{1,0:T(8,128)(2,1)S(1)} %get-tuple-element.44.refs_0_, bf16[24,3712]{1,0:T(8,128)(2,1)S(1)} %collective-permute-done.3.refs_1_, ...), custom_call_target="tpu_custom_call" | custom-call | flops 1937768448 | bytes 4686848 | tf_op jit(solution)/shard_map/pallas_call | solution.py:400
  31.4 0.0 collective-permute-done.10.refs_3_
  31.4 1.2 %collective-permute-done.9.refs_2_ = bf16[24,1920]{1,0:T(8,128)(2,1)S(1)} collective-permute-done((bf16[24,1920]{1,0:T(8,128)(2,1)S(1)}, bf16[24,1920]{1,0:T(8,128)(2,1)S(1)}, u32[]{:S(2)}, u32[]{:S(2)}) %collective-permute-start.9) | collective-permute-done | bytes 92192 | tf_op jit(solution)/shard_map/ppermute | solution.py:412
  32.6 2.0 %collective-permute-done.8.refs_1_ = bf16[24,3712]{1,0:T(8,128)(2,1)S(1)} collective-permute-done((bf16[24,3712]{1,0:T(8,128)(2,1)S(1)}, bf16[24,3712]{1,0:T(8,128)(2,1)S(1)}, u32[]{:S(2)}, u32[]{:S(2)}) %collective-permute-start.8) | collective-permute-done | bytes 178208 | tf_op jit(solution)/shard_map/ppermute | solution.py:412
  34.6 1.3 %shard_map.98 = (bf16[80,3712]{1,0:T(8,128)(2,1)S(1)}, bf16[256,128]{1,0:T(8,128)(2,1)}) custom-call(f32[8,32,128]{2,1,0:T(8,128)S(1)} %get-tuple-element.51.own_ref, bf16[256,3584]{1,0:T(8,128)(2,1)S(1)} %get-tuple-element.42.w_ref, s32[30,128]{1,0:T(8,128)S(1)} %get-tuple-element.43.slot_ref, bf16[24,3712]{1,0:T(8,128)(2,1)S(1)} %collective-permute-done.7.refs_0_, ...), custom_call_target="tpu_custom_call" | custom-call | flops 146800640 | bytes 3181568 | tf_op jit(solution)/shard_map/pallas_call | solution.py:400
  35.9 0.4 shard_map.99
  36.4 0.1 collective-permute-start.11
  36.5 4.2 %all-to-all-start = ((bf16[8,32,128]{2,1,0:T(8,128)(2,1)}), bf16[8,32,128]{2,1,0:T(8,128)(2,1)S(1)}, u32[]{:S(2)}, u32[]{:S(2)}) async-start(bf16[8,32,128]{2,1,0:T(8,128)(2,1)} %bitcast.4), calls=%async_computation | async-start | bytes 131072 | tf_op jit(solution)/shard_map/all_to_all | solution.py:490
  40.6 0.0 copy-start.3
  40.6 0.0 copy-start.4
  40.6 0.0 copy-start.5
  40.7 0.0 copy-start.6
  40.7 0.0 copy-start.7
  40.7 0.0 collective-permute-done.11.arrived_ref
  40.7 2.6 %shard_map.100 = bf16[256,1792]{1,0:T(8,128)(2,1)} custom-call(s32[30,128]{1,0:T(8,128)S(1)} %get-tuple-element.43.slot_ref, bf16[176,3712]{1,0:T(8,128)(2,1)S(1)} %get-tuple-element.55.early_ref, bf16[80,3712]{1,0:T(8,128)(2,1)S(1)} %get-tuple-element.56.late_ref, bf16[256,1792]{1,0:T(8,128)(2,1)} %collective-permute-done.11.arrived_ref), custom_call_target="tpu_custom_call" | custom-call | flops 6606028800 | bytes 3750912 | tf_op jit(solution)/shard_map/pallas_call | solution.py:400
  43.3 4.3 %all-to-all-done.back_ref = bf16[8,32,128]{2,1,0:T(8,128)(2,1)S(1)} async-done(((bf16[8,32,128]{2,1,0:T(8,128)(2,1)}), bf16[8,32,128]{2,1,0:T(8,128)(2,1)S(1)}, u32[]{:S(2)}, u32[]{:S(2)}) %all-to-all-start) | async-done | bytes 65568 | tf_op jit(solution)/shard_map/all_to_all | solution.py:490
  47.5 0.0 copy-done.3
  47.5 0.0 copy-done.4
  47.5 0.0 copy-done.5
  47.5 0.0 copy-done.6
  47.6 0.0 copy-done.7
  47.6 1.0 %shard_map.101 = (bf16[1024,128]{1,0:T(8,128)(2,1)}, bf16[8,128]{1,0:T(8,128)(2,1)}) custom-call(bf16[8,32,128]{2,1,0:T(8,128)(2,1)S(1)} %all-to-all-done.back_ref, f32[72,128]{1,0:T(8,128)S(1)} %copy-done.3, s32[72,128]{1,0:T(8,128)S(1)} %copy-done.4, f32[72,128]{1,0:T(8,128)S(1)} %copy-done.5, f32[72,128]{1,0:T(8,128)S(1)} %copy-done.6, s32[8,128]{1,0:T(8,128)S(1)} %bitcast.10), custom_call_target="tpu_custom_call" | custom-call | flops 18874368 | bytes 481280 | tf_op jit(solution)/shard_map/pallas_call | solution.py:400
Async XLA Ops:
  3.2 13.1 %collective-permute-start = (bf16[24,3712]{1,0:T(8,128)(2,1)}, bf16[24,3712]{1,0:T(8,128)(2,1)S(1)}, u32[]{:S(2)}, u32[]{:S(2)}) collective-permute-start(bf16[24,3712]{1,0:T(8,128)(2,1)} %get-tuple-element.34), channel_id=1, source_target_pairs={{0,4},{2,6},{4,0},{6,2},{8,12},{10,14},{12,8},{14,10},{1,5},{3,7},... | collective-permute-start | bytes 534536 | tf_op jit(solution)/shard_map/ppermute | solution.py:412
  6.3 11.0 %collective-permute-start.1 = (bf16[24,3712]{1,0:T(8,128)(2,1)}, bf16[24,3712]{1,0:T(8,128)(2,1)S(1)}, u32[]{:S(2)}, u32[]{:S(2)}) collective-permute-start(bf16[24,3712]{1,0:T(8,128)(2,1)} %get-tuple-element.34), channel_id=1, source_target_pairs={{0,8},{2,10},{4,12},{6,14},{8,0},{10,2},{12,4},{14,6},{1,9},{3,11}... | collective-permute-start | bytes 534536 | tf_op jit(solution)/shard_map/ppermute | solution.py:412
  8.9 8.4 %collective-permute-start.3 = (bf16[24,3712]{1,0:T(8,128)(2,1)}, bf16[24,3712]{1,0:T(8,128)(2,1)S(1)}, u32[]{:S(2)}, u32[]{:S(2)}) collective-permute-start(bf16[24,3712]{1,0:T(8,128)(2,1)} %get-tuple-element.34), channel_id=1, source_target_pairs={{0,2},{2,0},{4,6},{6,4},{8,10},{10,8},{12,14},{14,12},{1,3},{3,1},... | collective-permute-start | bytes 534536 | tf_op jit(solution)/shard_map/ppermute | solution.py:412
  10.3 8.2 %collective-permute-start.2 = (bf16[24,3712]{1,0:T(8,128)(2,1)}, bf16[24,3712]{1,0:T(8,128)(2,1)S(1)}, u32[]{:S(2)}, u32[]{:S(2)}) collective-permute-start(bf16[24,3712]{1,0:T(8,128)(2,1)} %get-tuple-element.35), channel_id=1, source_target_pairs={{0,2},{2,0},{4,6},{6,4},{8,10},{10,8},{12,14},{14,12},{1,3},{3,1},... | collective-permute-start | bytes 534536 | tf_op jit(solution)/shard_map/ppermute | solution.py:412
  10.9 1.5 %copy-start = (bf16[2,128,3584]{2,1,0:T(8,128)(2,1)S(1)}, bf16[2,128,3584]{2,1,0:T(8,128)(2,1)}, u32[]{:S(2)}) copy-start(bf16[2,128,3584]{2,1,0:T(8,128)(2,1)} %param.13) | copy-start | bytes 5505028
  12.4 0.9 %copy-start.1 = (bf16[32,3712]{1,0:T(8,128)(2,1)S(1)}, bf16[32,3712]{1,0:T(8,128)(2,1)}, u32[]{:S(2)}) copy-start(bf16[32,3712]{1,0:T(8,128)(2,1)} %get-tuple-element.36.own_hbm) | copy-start | bytes 712708
  13.3 0.9 %copy-start.2 = (bf16[32,3712]{1,0:T(8,128)(2,1)S(1)}, bf16[32,3712]{1,0:T(8,128)(2,1)}, u32[]{:S(2)}) copy-start(bf16[32,3712]{1,0:T(8,128)(2,1)} %get-tuple-element.37.even_hbm) | copy-start | bytes 712708
  14.3 0.7 %copy-start.8 = (s32[8]{0:T(128)S(1)}, s32[8]{0:T(128)}, u32[]{:S(2)}) copy-start(s32[8]{0:T(128)} %replica_ref.1) | copy-start | bytes 100
  18.6 10.6 %collective-permute-start.7 = (bf16[24,3712]{1,0:T(8,128)(2,1)S(1)}, bf16[24,3712]{1,0:T(8,128)(2,1)S(1)}, u32[]{:S(2)}, u32[]{:S(2)}) collective-permute-start(bf16[24,3712]{1,0:T(8,128)(2,1)S(1)} %collective-permute-done.1.refs_3_), channel_id=1, source_target_pairs={{0,4},{2,6},{4,0},{6,2},{8,12},{10,14},{12,8},{14,10},{1,5},{3,7},... | collective-permute-start | bytes 534536 | tf_op jit(solution)/shard_map/ppermute | solution.py:412
  19.0 11.6 %collective-permute-start.4 = (bf16[24,3712]{1,0:T(8,128)(2,1)S(1)}, bf16[24,3712]{1,0:T(8,128)(2,1)S(1)}, u32[]{:S(2)}, u32[]{:S(2)}) collective-permute-start(bf16[24,3712]{1,0:T(8,128)(2,1)S(1)} %collective-permute-done.1.refs_3_), channel_id=1, source_target_pairs={{0,2},{2,0},{4,6},{6,4},{8,10},{10,8},{12,14},{14,12},{1,3},{3,1},... | collective-permute-start | bytes 534536 | tf_op jit(solution)/shard_map/ppermute | solution.py:412
  20.5 10.1 %collective-permute-start.5 = (bf16[24,3712]{1,0:T(8,128)(2,1)S(1)}, bf16[24,3712]{1,0:T(8,128)(2,1)S(1)}, u32[]{:S(2)}, u32[]{:S(2)}) collective-permute-start(bf16[24,3712]{1,0:T(8,128)(2,1)S(1)} %collective-permute-done.refs_2_), channel_id=1, source_target_pairs={{0,2},{2,0},{4,6},{6,4},{8,10},{10,8},{12,14},{14,12},{1,3},{3,1},... | collective-permute-start | bytes 534536 | tf_op jit(solution)/shard_map/ppermute | solution.py:412
  21.2 6.9 %collective-permute-start.6 = (bf16[24,1920]{1,0:T(8,128)(2,1)S(1)}, bf16[24,1920]{1,0:T(8,128)(2,1)S(1)}, u32[]{:S(2)}, u32[]{:S(2)}) collective-permute-start(bf16[24,1920]{1,0:T(8,128)(2,1)S(1)} %get-tuple-element.50), channel_id=1, source_target_pairs={{0,12},{2,14},{4,8},{6,10},{8,4},{10,6},{12,0},{14,2},{1,13},{3,15... | collective-permute-start | bytes 276488 | tf_op jit(solution)/shard_map/ppermute | solution.py:412
  22.6 8.8 %collective-permute-start.10 = (bf16[24,1920]{1,0:T(8,128)(2,1)S(1)}, bf16[24,1920]{1,0:T(8,128)(2,1)S(1)}, u32[]{:S(2)}, u32[]{:S(2)}) collective-permute-start(bf16[24,1920]{1,0:T(8,128)(2,1)S(1)} %get-tuple-element.53), channel_id=1, source_target_pairs={{0,8},{2,10},{4,12},{6,14},{8,0},{10,2},{12,4},{14,6},{1,9},{3,11}... | collective-permute-start | bytes 276488 | tf_op jit(solution)/shard_map/ppermute | solution.py:412
  28.1 4.6 %collective-permute-start.9 = (bf16[24,1920]{1,0:T(8,128)(2,1)S(1)}, bf16[24,1920]{1,0:T(8,128)(2,1)S(1)}, u32[]{:S(2)}, u32[]{:S(2)}) collective-permute-start(bf16[24,1920]{1,0:T(8,128)(2,1)S(1)} %get-tuple-element.52), channel_id=1, source_target_pairs={{0,4},{2,6},{4,0},{6,2},{8,12},{10,14},{12,8},{14,10},{1,5},{3,7},... | collective-permute-start | bytes 276488 | tf_op jit(solution)/shard_map/ppermute | solution.py:412
  29.1 5.5 %collective-permute-start.8 = (bf16[24,3712]{1,0:T(8,128)(2,1)S(1)}, bf16[24,3712]{1,0:T(8,128)(2,1)S(1)}, u32[]{:S(2)}, u32[]{:S(2)}) collective-permute-start(bf16[24,3712]{1,0:T(8,128)(2,1)S(1)} %collective-permute-done.7.refs_0_), channel_id=1, source_target_pairs={{0,2},{2,0},{4,6},{6,4},{8,10},{10,8},{12,14},{14,12},{1,3},{3,1},... | collective-permute-start | bytes 534536 | tf_op jit(solution)/shard_map/ppermute | solution.py:412
  36.4 4.3 %collective-permute-start.11 = (bf16[256,1792]{1,0:T(8,128)(2,1)S(1)}, bf16[256,1792]{1,0:T(8,128)(2,1)}, u32[]{:S(2)}, u32[]{:S(2)}) collective-permute-start(bf16[256,1792]{1,0:T(8,128)(2,1)S(1)} %shard_map.99), channel_id=1, source_target_pairs={{0,1},{1,0},{2,3},{3,2},{4,5},{5,4},{6,7},{7,6},{8,9},{9,8},{10,11... | collective-permute-start | bytes 2752520 | tf_op jit(solution)/shard_map/ppermute | solution.py:499
  36.5 11.1 %all-to-all-start = ((bf16[8,32,128]{2,1,0:T(8,128)(2,1)}), bf16[8,32,128]{2,1,0:T(8,128)(2,1)S(1)}, u32[]{:S(2)}, u32[]{:S(2)}) async-start(bf16[8,32,128]{2,1,0:T(8,128)(2,1)} %bitcast.4), calls=%async_computation | async-start | bytes 131072 | tf_op jit(solution)/shard_map/all_to_all | solution.py:490
  40.6 6.9 %copy-start.3 = (f32[72,128]{1,0:T(8,128)S(1)}, f32[72,128]{1,0:T(8,128)}, u32[]{:S(2)}) copy-start(f32[72,128]{1,0:T(8,128)} %get-tuple-element.58.pick_ref) | copy-start | bytes 110596
  40.6 6.9 %copy-start.4 = (s32[72,128]{1,0:T(8,128)S(1)}, s32[72,128]{1,0:T(8,128)}, u32[]{:S(2)}) copy-start(s32[72,128]{1,0:T(8,128)} %get-tuple-element.59.expert_ref) | copy-start | bytes 110596
  40.6 6.9 %copy-start.5 = (f32[72,128]{1,0:T(8,128)S(1)}, f32[72,128]{1,0:T(8,128)}, u32[]{:S(2)}) copy-start(f32[72,128]{1,0:T(8,128)} %get-tuple-element.60.hs_ref) | copy-start | bytes 110596
  40.7 6.9 %copy-start.6 = (f32[72,128]{1,0:T(8,128)S(1)}, f32[72,128]{1,0:T(8,128)}, u32[]{:S(2)}) copy-start(f32[72,128]{1,0:T(8,128)} %get-tuple-element.61.ps_ref) | copy-start | bytes 110596
  40.7 6.9 %copy-start.7 = (s32[128,8]{0,1:T(8,128)S(1)}, s32[128,8]{0,1:T(8,128)}, u32[]{:S(2)}) copy-start(s32[128,8]{0,1:T(8,128)} %param.10) | copy-start | bytes 12292
